TPU v7x, 32 devices: a whole 2x2x4 slice. The times are simulated.
32 devices in a mesh: seq: 8 (over z, x), head: 4 (over y, core).
Axes of the slice: x: 2, y: 2, z: 4, core: 2. Of those that a mesh axis runs over, the one named last changes fastest.
Arguments:
- queries: bfloat16 [4096, 4096], P(('seq', 'head')), may hold values from -6 to 6
- keys: bfloat16 [4096, 4096], P(('seq', 'head')), may hold values from -6 to 6
- values: bfloat16 [4096, 4096], P(('seq', 'head')), may hold values from -128 to 128
- out_grad: bfloat16 [4096, 4096], P(('seq', 'head')), may hold values from -16 to 16
- doc_lengths: int32 [8], replicated, may hold values from 1 to 2048, 4096 in all
Outputs:
- attn_out: bfloat16 [4096, 4096], P(('seq', 'head'))
- grad_queries: bfloat16 [4096, 4096], P(('seq', 'head'))
- grad_keys: bfloat16 [4096, 4096], P(('seq', 'head'))
- grad_values: bfloat16 [4096, 4096], P(('seq', 'head'))
Inputs may be any that keep to these rules, and one draw needn't show every extreme that they name: `doc_lengths`: the lengths sum to 4096; the longest is exactly 2048.
All inputs are finite; a program needn't handle non-finite values.
Results may differ from a plain program's by a relative error of at most 0.011.
Values may be sent and summed in bfloat16 or wider, within the bound.
No kernel may reach another device: no remote copies, remote signals or barrier semaphores. Data moves between devices by JAX's collectives and lax.ppermute only.
A program may use at most 128 MiB of HBM per device.

v0:
```python
import jax
import jax.numpy as jnp
from jax import lax
from jax.sharding import PartitionSpec as P

DH = 128


def from_behind(array, axis, by):
    devices = lax.axis_size(axis)
    pairs = [(i, i + by) for i in range(devices) if 0 <= i + by < devices]
    return lax.ppermute(array, axis, pairs)


def feature(array):
    wide = array.astype(jnp.float32)
    return jnp.where(wide > 0, wide + 1.0, jnp.exp(jnp.minimum(wide, 0.0)))


def slope(array):
    wide = array.astype(jnp.float32)
    return jnp.where(wide > 0, 1.0, jnp.exp(jnp.minimum(wide, 0.0)))


def doc_index(doc_ends, where):
    return jnp.sum((jnp.asarray(where)[..., None] >= doc_ends).astype(jnp.int32), axis=-1)


def forward_hops(summary, doc_ends, block_index, block_len):
    rounds = (lax.axis_size("seq") - 1).bit_length()
    current = from_behind(summary, "seq", 1)
    for depth_bit in range(rounds):
        stride = 1 << depth_bit
        arriving = from_behind(current, "seq", stride)
        boundary = doc_index(doc_ends, block_index * block_len - 1) != doc_index(
            doc_ends, (block_index - stride) * block_len - 1
        )
        current = current + jnp.where(boundary, 0.0, arriving)
    return current


def backward_hops(summary, doc_ends, block_index, block_len):
    rounds = (lax.axis_size("seq") - 1).bit_length()
    current = from_behind(summary.astype(jnp.bfloat16), "seq", -1).astype(summary.dtype)
    for depth_bit in range(rounds):
        stride = 1 << depth_bit
        arriving = from_behind(current.astype(jnp.bfloat16), "seq", -stride).astype(current.dtype)
        boundary = doc_index(doc_ends, (block_index + 1) * block_len) != doc_index(
            doc_ends, (block_index + 1 + stride) * block_len
        )
        current = current + jnp.where(boundary, 0.0, arriving)
    return current


def local(queries, keys, values, out_grad, doc_lengths):
    shared = (
        lax.all_to_all(queries, "head", split_axis=1, concat_axis=0, tiled=True),
        lax.all_to_all(keys, "head", split_axis=1, concat_axis=0, tiled=True),
        lax.all_to_all(values, "head", split_axis=1, concat_axis=0, tiled=True),
        lax.all_to_all(out_grad, "head", split_axis=1, concat_axis=0, tiled=True),
    )
    block_len = shared[0].shape[0]
    head_count = shared[0].shape[1] // DH
    query_rows = shared[0].reshape(block_len, head_count, DH)
    key_rows = shared[1].reshape(block_len, head_count, DH)
    value_rows = shared[2].reshape(block_len, head_count, DH)
    grad_rows = shared[3].reshape(block_len, head_count, DH)
    block_index = lax.axis_index("seq")
    doc_ends = jnp.cumsum(doc_lengths)
    block_start = block_index * block_len
    within = jnp.arange(block_len, dtype=jnp.int32)
    doc_of = doc_index(doc_ends, block_start + within)
    doc_first = doc_of[0]
    doc_last = doc_of[block_len - 1]
    before = doc_index(doc_ends, block_start - 1)
    doc_after = doc_index(doc_ends, block_start + block_len)
    visible = (within[:, None] >= within[None, :]) & (doc_of[:, None] == doc_of[None, :])
    head_rows = (doc_of == doc_first)[:, None, None]
    tail_rows = (doc_of == doc_last)[:, None, None]
    tile_rows = 256
    tile_count = block_len // tile_rows
    feat_query = feature(query_rows).astype(jnp.bfloat16)
    feat_key = feature(key_rows).astype(jnp.bfloat16)
    zero_bf = jnp.zeros((), jnp.bfloat16)
    tail_state = jnp.einsum(
        "shd,she->hde",
        jnp.where(tail_rows, feat_key, zero_bf),
        value_rows,
        preferred_element_type=jnp.float32,
    )
    carried = forward_hops(tail_state, doc_ends, block_index, block_len)
    incoming = jnp.where(doc_first == before, carried, 0.0).astype(jnp.bfloat16)
    score_tiles = []
    normed_tiles = []
    grad_att_tiles = []
    for tile in range(tile_count):
        first = tile * tile_rows
        last = first + tile_rows
        query_tile = feat_query[first:last]
        tile_scores = jnp.einsum(
            "thd,shd->hts", query_tile, feat_key[:last], preferred_element_type=jnp.float32
        )
        tile_scores = jnp.where(visible[first:last, :last][None], tile_scores, 0.0).astype(
            jnp.bfloat16
        )
        attended = jnp.einsum(
            "hts,she->the", tile_scores, value_rows[:last], preferred_element_type=jnp.float32
        )
        attended = attended + jnp.where(
            head_rows[first:last],
            jnp.einsum("thd,hde->the", query_tile, incoming, preferred_element_type=jnp.float32),
            0.0,
        )
        inv_rms = lax.rsqrt(jnp.mean(attended * attended, axis=-1, keepdims=True) + 1e-05)
        normed = attended * inv_rms
        grad_out = grad_rows[first:last].astype(jnp.float32)
        grad_att_tile = (
            (grad_out - normed * jnp.mean(grad_out * normed, axis=-1, keepdims=True)) * inv_rms
        ).astype(jnp.bfloat16)
        score_tiles.append(tile_scores)
        normed_tiles.append(normed.astype(jnp.bfloat16))
        grad_att_tiles.append(grad_att_tile)
    out_block = jnp.concatenate(normed_tiles, axis=0).reshape(block_len, head_count * DH)
    grad_att = jnp.concatenate(grad_att_tiles, axis=0)
    attn_out = lax.all_to_all(out_block, "head", split_axis=0, concat_axis=1, tiled=True)
    head_sum = jnp.einsum(
        "thd,the->hde",
        jnp.where(head_rows, feat_query, zero_bf),
        grad_att,
        preferred_element_type=jnp.float32,
    )
    future = backward_hops(head_sum, doc_ends, block_index, block_len)
    outgoing = jnp.where(doc_last == doc_after, future, 0.0).astype(jnp.bfloat16)
    grad_fk = jnp.zeros((block_len, head_count, DH), jnp.float32)
    grad_fv = jnp.zeros((block_len, head_count, DH), jnp.float32)
    grad_fq_tiles = []
    for tile in range(tile_count):
        first = tile * tile_rows
        last = first + tile_rows
        grad_tile = grad_att_tiles[tile]
        tile_grads = jnp.einsum(
            "the,she->hts", grad_tile, value_rows[:last], preferred_element_type=jnp.float32
        )
        tile_grads = jnp.where(visible[first:last, :last][None], tile_grads, 0.0).astype(
            jnp.bfloat16
        )
        grad_fq_tile = jnp.einsum(
            "hts,shd->thd", tile_grads, feat_key[:last], preferred_element_type=jnp.float32
        )
        grad_fq_tile = grad_fq_tile + jnp.where(
            head_rows[first:last],
            jnp.einsum("the,hde->thd", grad_tile, incoming, preferred_element_type=jnp.float32),
            0.0,
        )
        grad_fq_tiles.append(grad_fq_tile)
        grad_fk = grad_fk.at[:last].add(
            jnp.einsum(
                "hts,thd->shd",
                tile_grads,
                feat_query[first:last],
                preferred_element_type=jnp.float32,
            )
        )
        grad_fv = grad_fv.at[:last].add(
            jnp.einsum(
                "hts,the->she", score_tiles[tile], grad_tile, preferred_element_type=jnp.float32
            )
        )
    grad_fq = jnp.concatenate(grad_fq_tiles, axis=0)
    grad_fk = grad_fk + jnp.where(
        tail_rows,
        jnp.einsum("she,hde->shd", value_rows, outgoing, preferred_element_type=jnp.float32),
        0.0,
    )
    grad_fv = grad_fv + jnp.where(
        tail_rows,
        jnp.einsum("shd,hde->she", feat_key, outgoing, preferred_element_type=jnp.float32),
        0.0,
    )
    grad_query = (
        (grad_fq * slope(query_rows)).astype(jnp.bfloat16).reshape(block_len, head_count * DH)
    )
    grad_key = (grad_fk * slope(key_rows)).astype(jnp.bfloat16).reshape(block_len, head_count * DH)
    grad_value = grad_fv.astype(jnp.bfloat16).reshape(block_len, head_count * DH)
    grad_queries, grad_keys, grad_values = (
        lax.all_to_all(grad_query, "head", split_axis=0, concat_axis=1, tiled=True),
        lax.all_to_all(grad_key, "head", split_axis=0, concat_axis=1, tiled=True),
        lax.all_to_all(grad_value, "head", split_axis=0, concat_axis=1, tiled=True),
    )
    return (attn_out, grad_queries, grad_keys, grad_values)


def solution(mesh):
    placed = (
        P(("seq", "head"), None),
        P(("seq", "head"), None),
        P(("seq", "head"), None),
        P(("seq", "head"), None),
        P(),
    )
    return jax.shard_map(
        local,
        mesh=mesh,
        in_specs=placed,
        out_specs=(
            P(("seq", "head"), None),
            P(("seq", "head"), None),
            P(("seq", "head"), None),
            P(("seq", "head"), None),
        ),
        check_vma=False,
    )
```

profile of v0, /device:TPU:0, one launch (start us, length us, event | category | flops | bytes accessed | tf_op | source)
XLA Modules:
  0.0 259.1 jit_solution(10583568102197396025)
XLA Ops:
  0.6 2.4 copy.285
  3.0 4.2 %all-to-all-start.1 = ((bf16[128,4,1024]{2,0,1:T(8,128)(2,1)}), bf16[128,4,1024]{2,0,1:T(8,128)(2,1)S(1)}, u32[]{:S(2)}, u32[]{:S(2)}) async-start(bf16[128,4,1024]{2,0,1:T(8,128)(2,1)} %bitcast.156), calls=%async_computation.1 | async-start | bytes 2097152 | tf_op jit(solution)/shard_map/all_to_all | solution.py:58
  8.3 13.4 %all-to-all-done.1 = bf16[128,4,1024]{2,0,1:T(8,128)(2,1)S(1)} async-done(((bf16[128,4,1024]{2,0,1:T(8,128)(2,1)}), bf16[128,4,1024]{2,0,1:T(8,128)(2,1)S(1)}, u32[]{:S(2)}, u32[]{:S(2)}) %all-to-all-start.1) | async-done | bytes 1048608 | tf_op jit(solution)/shard_map/all_to_all | solution.py:58
  21.7 3.5 %all-to-all-start.2 = ((bf16[128,4,1024]{2,0,1:T(8,128)(2,1)}), bf16[128,4,1024]{2,0,1:T(8,128)(2,1)S(1)}, u32[]{:S(2)}, u32[]{:S(2)}) async-start(bf16[128,4,1024]{2,0,1:T(8,128)(2,1)} %bitcast.155), calls=%async_computation.2 | async-start | bytes 2097152 | tf_op jit(solution)/shard_map/all_to_all | solution.py:59
  40.4 4.3 %all-to-all-start.4 = ((bf16[128,4,1024]{2,0,1:T(8,128)(2,1)}), bf16[128,4,1024]{2,0,1:T(8,128)(2,1)}, u32[]{:S(2)}, u32[]{:S(2)}) async-start(bf16[128,4,1024]{2,0,1:T(8,128)(2,1)} %bitcast.154), calls=%async_computation.4 | async-start | bytes 2097152 | tf_op jit(solution)/shard_map/all_to_all | solution.py:60
  44.6 1.3 broadcast_compare_fusion.1
  47.2 2.3 fusion.10
  49.7 9.5 %all-to-all-done.4 = bf16[128,4,1024]{2,0,1:T(8,128)(2,1)} async-done(((bf16[128,4,1024]{2,0,1:T(8,128)(2,1)}), bf16[128,4,1024]{2,0,1:T(8,128)(2,1)}, u32[]{:S(2)}, u32[]{:S(2)}) %all-to-all-start.4) | async-done | bytes 1048608 | tf_op jit(solution)/shard_map/all_to_all | solution.py:60
  59.2 3.5 %all-to-all-start = ((bf16[128,4,1024]{2,0,1:T(8,128)(2,1)}), bf16[128,4,1024]{2,0,1:T(8,128)(2,1)S(1)}, u32[]{:S(2)}, u32[]{:S(2)}) async-start(bf16[128,4,1024]{2,0,1:T(8,128)(2,1)} %bitcast.178), calls=%async_computation | async-start | bytes 2097152 | tf_op jit(solution)/shard_map/all_to_all | solution.py:57
  62.7 1.8 broadcast_select_fusion
  64.5 1.4 fusion.26
  65.9 4.9 %collective-permute-start = (f32[8,128,128]{2,1,0:T(8,128)}, f32[8,128,128]{2,1,0:T(8,128)}, u32[]{:S(2)}, u32[]{:S(2)}) collective-permute-start(f32[8,128,128]{2,1,0:T(8,128)} %fusion.26), channel_id=1, source_target_pairs={{0,4},{4,8},{8,12},{12,16},{16,20},{20,24},{24,28},{1,5},{5,9},{9,... | collective-permute-start | bytes 1572872 | tf_op jit(solution)/shard_map/ppermute | solution.py:12
  70.7 1.4 slice_convert_fusion.1
  74.5 2.6 %all-to-all-done = bf16[128,4,1024]{2,0,1:T(8,128)(2,1)S(1)} async-done(((bf16[128,4,1024]{2,0,1:T(8,128)(2,1)}), bf16[128,4,1024]{2,0,1:T(8,128)(2,1)S(1)}, u32[]{:S(2)}, u32[]{:S(2)}) %all-to-all-start) | async-done | bytes 1048608 | tf_op jit(solution)/shard_map/all_to_all | solution.py:57
  77.7 1.2 copy.251
  78.9 3.1 %collective-permute-done = f32[8,128,128]{2,1,0:T(8,128)} collective-permute-done((f32[8,128,128]{2,1,0:T(8,128)}, f32[8,128,128]{2,1,0:T(8,128)}, u32[]{:S(2)}, u32[]{:S(2)}) %collective-permute-start) | collective-permute-done | bytes 524320 | tf_op jit(solution)/shard_map/ppermute | solution.py:12
  82.0 5.2 %collective-permute-start.1 = (f32[8,128,128]{2,1,0:T(8,128)}, f32[8,128,128]{2,1,0:T(8,128)}, u32[]{:S(2)}, u32[]{:S(2)}) collective-permute-start(f32[8,128,128]{2,1,0:T(8,128)} %collective-permute-done), channel_id=1, source_target_pairs={{0,4},{4,8},{8,12},{12,16},{16,20},{20,24},{24,28},{1,5},{5,9},{9,... | collective-permute-start | bytes 1572872 | tf_op jit(solution)/shard_map/ppermute | solution.py:12
  88.6 1.2 copy.212
  89.8 3.4 %copy.252 = f32[64,8,8,128]{3,2,1,0:T(8,128)} copy(f32[64,8,8,128]{3,1,2,0:T(8,128)} %bitcast.169) | data formatting | bytes 4194304
  93.2 3.1 %copy.237 = f32[512,8,128]{0,2,1:T(8,128)} copy(f32[512,8,128]{2,1,0:T(8,128)} %bitcast.171) | data formatting | bytes 4194304 | tf_op jit(solution)/shard_map/jit(_where)/select_n | solution.py:22
  97.5 1.7 select_convert_fusion.3
  99.3 1.3 select_add_fusion.3
  100.6 4.5 %collective-permute-start.2 = (f32[8,128,128]{2,1,0:T(8,128)S(1)}, f32[8,128,128]{2,1,0:T(8,128)S(1)}, u32[]{:S(2)}, u32[]{:S(2)}) collective-permute-start(f32[8,128,128]{2,1,0:T(8,128)S(1)} %select_add_fusion.3), channel_id=1, source_target_pairs={{0,8},{4,12},{8,16},{12,20},{16,24},{20,28},{1,9},{5,13},{9,17},{1... | collective-permute-start | bytes 1572872 | tf_op jit(solution)/shard_map/ppermute | solution.py:12
  106.5 8.7 %collective-permute-done.2 = f32[8,128,128]{2,1,0:T(8,128)S(1)} collective-permute-done((f32[8,128,128]{2,1,0:T(8,128)S(1)}, f32[8,128,128]{2,1,0:T(8,128)S(1)}, u32[]{:S(2)}, u32[]{:S(2)}) %collective-permute-start.2) | collective-permute-done | bytes 524320 | tf_op jit(solution)/shard_map/ppermute | solution.py:12
  115.3 5.8 %collective-permute-start.3 = (f32[8,128,128]{2,1,0:T(8,128)S(1)}, f32[8,128,128]{2,1,0:T(8,128)S(1)}, u32[]{:S(2)}, u32[]{:S(2)}) collective-permute-start(f32[8,128,128]{2,1,0:T(8,128)S(1)} %select_add_fusion.2), channel_id=1, source_target_pairs={{0,16},{4,20},{8,24},{12,28},{1,17},{5,21},{9,25},{13,29},{2,18},{... | collective-permute-start | bytes 1572872 | tf_op jit(solution)/shard_map/ppermute | solution.py:12
  121.0 1.8 bitcast_select_fusion
  123.6 6.5 %collective-permute-done.3 = f32[8,128,128]{2,1,0:T(8,128)S(1)} collective-permute-done((f32[8,128,128]{2,1,0:T(8,128)S(1)}, f32[8,128,128]{2,1,0:T(8,128)S(1)}, u32[]{:S(2)}, u32[]{:S(2)}) %collective-permute-start.3) | collective-permute-done | bytes 524320 | tf_op jit(solution)/shard_map/ppermute | solution.py:12
  132.7 1.5 multiply_convert_fusion
  134.3 1.4 select_convert_fusion.2
  135.7 2.1 select_convert_fusion
  137.9 1.2 convolution_convert_fusion
  139.1 1.6 copy.192
  140.8 2.3 all_to_all.105
  143.1 4.2 %all-to-all-start.3 = ((bf16[4,128,1024]{2,1,0:T(8,128)(2,1)}), bf16[4,128,1024]{2,1,0:T(8,128)(2,1)}, u32[]{:S(2)}, u32[]{:S(2)}) async-start(bf16[4,128,1024]{2,1,0:T(8,128)(2,1)} %all_to_all.105), calls=%async_computation.3 | async-start | bytes 2097152 | tf_op jit(solution)/shard_map/all_to_all | solution.py:125
  147.3 1.4 collective-permute-start.4
  148.8 1.8 fusion.56
  150.6 1.3 fusion.15
  153.6 1.3 fusion.17
  154.9 2.6 %copy.201 = f32[256,8,128]{0,2,1:T(8,128)} copy(f32[256,8,128]{2,0,1:T(8,128)} %fusion.15) | data formatting | bytes 2097152 | tf_op jit(solution)/shard_map/add | solution.py:150
  157.5 2.5 copy.208
  160.0 3.2 %pad_maximum_fusion = f32[512,1024]{0,1:T(8,128)} fusion(f32[256,1024]{0,1:T(8,128)} %bitcast.182, f32[256,1024]{0,1:T(8,128)} %bitcast.181), kind=kLoop, calls=%fused_computation.19 | loop fusion | flops 524288 | bytes 4194304 | tf_op jit(solution)/shard_map/concatenate | solution.py:169
  163.2 3.0 %copy.236 = f32[512,1024]{1,0:T(8,128)} copy(f32[512,1024]{0,1:T(8,128)} %pad_maximum_fusion) | data formatting | bytes 4194304 | tf_op jit(solution)/shard_map/concatenate | solution.py:169
  166.2 1.4 collective-permute-start.5
  167.6 3.6 %fusion.58 = f32[8,128,512]{2,1,0:T(8,128)} fusion(bf16[256,8,128]{2,0,1:T(8,128)(2,1)} %copy-done.18, bf16[8,256,512]{2,1,0:T(8,128)(2,1)} %copy-done.9), kind=kOutput, calls=%fused_computation.123 | convolution fusion | flops 268435456 | bytes 4718592 | tf_op jit(solution)/shard_map/hts,the->she/dot_general | solution.py:165
  171.3 7.9 %collective-permute-done.5 = bf16[8,128,128]{2,1,0:T(8,128)(2,1)S(1)} collective-permute-done((bf16[8,128,128]{2,1,0:T(8,128)(2,1)}, bf16[8,128,128]{2,1,0:T(8,128)(2,1)S(1)}, u32[]{:S(2)}, u32[]{:S(2)}) %collective-permute-start.5) | collective-permute-done | bytes 262176 | tf_op jit(solution)/shard_map/ppermute | solution.py:12
  180.2 1.3 collective-permute-start.6
  181.6 1.5 fusion.6
  183.1 16.4 %collective-permute-done.6 = bf16[8,128,128]{2,1,0:T(8,128)(2,1)S(1)} collective-permute-done((bf16[8,128,128]{2,1,0:T(8,128)(2,1)S(1)}, bf16[8,128,128]{2,1,0:T(8,128)(2,1)S(1)}, u32[]{:S(2)}, u32[]{:S(2)}) %collective-permute-start.6) | collective-permute-done | bytes 262176 | tf_op jit(solution)/shard_map/ppermute | solution.py:12
  199.5 1.2 fusion.40
  200.7 1.4 collective-permute-start.7
  202.1 4.6 %all-to-all-start.5 = ((bf16[4,128,1024]{2,1,0:T(8,128)(2,1)}), bf16[4,128,1024]{2,1,0:T(8,128)(2,1)}, u32[]{:S(2)}, u32[]{:S(2)}) async-start(bf16[4,128,1024]{2,1,0:T(8,128)(2,1)} %fusion.6), calls=%async_computation.5 | async-start | bytes 2097152 | tf_op jit(solution)/shard_map/all_to_all | solution.py:186
  207.1 9.5 %collective-permute-done.7 = bf16[8,128,128]{2,1,0:T(8,128)(2,1)} collective-permute-done((bf16[8,128,128]{2,1,0:T(8,128)(2,1)S(1)}, bf16[8,128,128]{2,1,0:T(8,128)(2,1)}, u32[]{:S(2)}, u32[]{:S(2)}) %collective-permute-start.7) | collective-permute-done | bytes 262176 | tf_op jit(solution)/shard_map/ppermute | solution.py:12
  216.6 1.2 select_convert_fusion.4
  219.9 1.2 all-to-all-done.5
  221.1 4.2 %all-to-all-start.7 = ((bf16[4,128,1024]{1,2,0:T(8,128)(2,1)}), bf16[4,128,1024]{1,2,0:T(8,128)(2,1)}, u32[]{:S(2)}, u32[]{:S(2)}) async-start(bf16[4,128,1024]{1,2,0:T(8,128)(2,1)} %copy.221), calls=%async_computation.7 | async-start | bytes 2097152 | tf_op jit(solution)/shard_map/all_to_all | solution.py:188
  225.3 1.5 convolution_bitcast_fusion.2
  230.8 9.0 %all-to-all-done.7 = bf16[4,128,1024]{1,2,0:T(8,128)(2,1)} async-done(((bf16[4,128,1024]{1,2,0:T(8,128)(2,1)}), bf16[4,128,1024]{1,2,0:T(8,128)(2,1)}, u32[]{:S(2)}, u32[]{:S(2)}) %all-to-all-start.7) | async-done | bytes 1048608 | tf_op jit(solution)/shard_map/all_to_all | solution.py:188
  239.8 3.5 %all-to-all-start.6 = ((bf16[4,128,1024]{1,2,0:T(8,128)(2,1)}), bf16[4,128,1024]{1,2,0:T(8,128)(2,1)S(1)}, u32[]{:S(2)}, u32[]{:S(2)}) async-start(bf16[4,128,1024]{1,2,0:T(8,128)(2,1)} %copy.216), calls=%async_computation.6 | async-start | bytes 2097152 | tf_op jit(solution)/shard_map/all_to_all | solution.py:187
  243.4 1.6 copy.193
  245.0 1.3 copy.222
  246.3 2.3 copy.242
  248.6 2.3 copy.224
  250.8 6.9 %all-to-all-done.6 = bf16[4,128,1024]{1,2,0:T(8,128)(2,1)S(1)} async-done(((bf16[4,128,1024]{1,2,0:T(8,128)(2,1)}), bf16[4,128,1024]{1,2,0:T(8,128)(2,1)S(1)}, u32[]{:S(2)}, u32[]{:S(2)}) %all-to-all-start.6) | async-done | bytes 1048608 | tf_op jit(solution)/shard_map/all_to_all | solution.py:187
  257.8 1.3 copy.223
  (120 shorter events, 26.7 us)
Async XLA Ops:
  0.6 6.6 %copy-start.27 = (bf16[128,4096]{1,0:T(8,128)(2,1)S(1)}, bf16[128,4096]{1,0:T(8,128)(2,1)}, u32[]{:S(2)}) copy-start(bf16[128,4096]{1,0:T(8,128)(2,1)} %param.19) | copy-start | bytes 3145732
  3.0 18.7 %all-to-all-start.1 = ((bf16[128,4,1024]{2,0,1:T(8,128)(2,1)}), bf16[128,4,1024]{2,0,1:T(8,128)(2,1)S(1)}, u32[]{:S(2)}, u32[]{:S(2)}) async-start(bf16[128,4,1024]{2,0,1:T(8,128)(2,1)} %bitcast.156), calls=%async_computation.1 | async-start | bytes 2097152 | tf_op jit(solution)/shard_map/all_to_all | solution.py:58
  7.3 18.0 %copy-start.32 = (s32[8]{0:T(128)S(1)}, s32[8]{0:T(128)}, u32[]{:S(2)}) copy-start(s32[8]{0:T(128)} %param.21) | copy-start | bytes 100
  7.3 29.2 %copy-start.28 = (bf16[128,4096]{1,0:T(8,128)(2,1)S(1)}, bf16[128,4096]{1,0:T(8,128)(2,1)}, u32[]{:S(2)}) copy-start(bf16[128,4096]{1,0:T(8,128)(2,1)} %param.17) | copy-start | bytes 3145732
  21.7 18.6 %all-to-all-start.2 = ((bf16[128,4,1024]{2,0,1:T(8,128)(2,1)}), bf16[128,4,1024]{2,0,1:T(8,128)(2,1)S(1)}, u32[]{:S(2)}, u32[]{:S(2)}) async-start(bf16[128,4,1024]{2,0,1:T(8,128)(2,1)} %bitcast.155), calls=%async_computation.2 | async-start | bytes 2097152 | tf_op jit(solution)/shard_map/all_to_all | solution.py:59
  25.8 79.8 %copy-start.30 = (pred[256,512]{1,0:T(8,128)(4,1)}, pred[256,512]{1,0:T(8,128)(4,1)S(1)}, u32[]{:S(2)}) copy-start(pred[256,512]{1,0:T(8,128)(4,1)S(1)} %slice.160) | copy-start | bytes 393220
  36.4 1.6 copy-start.29
  40.4 18.8 %all-to-all-start.4 = ((bf16[128,4,1024]{2,0,1:T(8,128)(2,1)}), bf16[128,4,1024]{2,0,1:T(8,128)(2,1)}, u32[]{:S(2)}, u32[]{:S(2)}) async-start(bf16[128,4,1024]{2,0,1:T(8,128)(2,1)} %bitcast.154), calls=%async_computation.4 | async-start | bytes 2097152 | tf_op jit(solution)/shard_map/all_to_all | solution.py:60
  47.2 17.3 %copy-start.2 = (bf16[64,8,8,128]{3,2,1,0:T(8,128)(2,1)}, bf16[64,8,8,128]{3,2,1,0:T(8,128)(2,1)S(1)}, u32[]{:S(2)}) copy-start(bf16[64,8,8,128]{3,2,1,0:T(8,128)(2,1)S(1)} %copy.247) | copy-start | bytes 3145732
  59.2 18.0 %all-to-all-start = ((bf16[128,4,1024]{2,0,1:T(8,128)(2,1)}), bf16[128,4,1024]{2,0,1:T(8,128)(2,1)S(1)}, u32[]{:S(2)}, u32[]{:S(2)}) async-start(bf16[128,4,1024]{2,0,1:T(8,128)(2,1)} %bitcast.178), calls=%async_computation | async-start | bytes 2097152 | tf_op jit(solution)/shard_map/all_to_all | solution.py:57
  65.9 16.2 %collective-permute-start = (f32[8,128,128]{2,1,0:T(8,128)}, f32[8,128,128]{2,1,0:T(8,128)}, u32[]{:S(2)}, u32[]{:S(2)}) collective-permute-start(f32[8,128,128]{2,1,0:T(8,128)} %fusion.26), channel_id=1, source_target_pairs={{0,4},{4,8},{8,12},{12,16},{16,20},{20,24},{24,28},{1,5},{5,9},{9,... | collective-permute-start | bytes 1572872 | tf_op jit(solution)/shard_map/ppermute | solution.py:12
  82.0 17.2 %collective-permute-start.1 = (f32[8,128,128]{2,1,0:T(8,128)}, f32[8,128,128]{2,1,0:T(8,128)}, u32[]{:S(2)}, u32[]{:S(2)}) collective-permute-start(f32[8,128,128]{2,1,0:T(8,128)} %collective-permute-done), channel_id=1, source_target_pairs={{0,4},{4,8},{8,12},{12,16},{16,20},{20,24},{24,28},{1,5},{5,9},{9,... | collective-permute-start | bytes 1572872 | tf_op jit(solution)/shard_map/ppermute | solution.py:12
  93.2 3.1 %copy-start.21 = (bf16[4,128,1024]{2,1,0:T(8,128)(2,1)S(1)}, bf16[4,128,1024]{2,1,0:T(8,128)(2,1)}, u32[]{:S(2)}) copy-start(bf16[4,128,1024]{2,1,0:T(8,128)(2,1)} %get-tuple-element.96) | copy-start | bytes 3145732
  97.5 7.6 %copy-start.24 = (bf16[32,8,8,128]{3,2,1,0:T(8,128)(2,1)S(1)}, bf16[32,8,8,128]{3,2,1,0:T(8,128)(2,1)}, u32[]{:S(2)}) copy-start(bf16[32,8,8,128]{3,2,1,0:T(8,128)(2,1)} %copy.245) | copy-start | bytes 1572868
  99.3 6.3 %copy-start.13 = (bf16[256,8,128]{0,2,1:T(8,128)(2,1)S(1)}, bf16[256,8,128]{0,2,1:T(8,128)(2,1)}, u32[]{:S(2)}) copy-start(bf16[256,8,128]{0,2,1:T(8,128)(2,1)} %copy.212) | copy-start | bytes 1572868
  100.6 14.6 %collective-permute-start.2 = (f32[8,128,128]{2,1,0:T(8,128)S(1)}, f32[8,128,128]{2,1,0:T(8,128)S(1)}, u32[]{:S(2)}, u32[]{:S(2)}) collective-permute-start(f32[8,128,128]{2,1,0:T(8,128)S(1)} %select_add_fusion.3), channel_id=1, source_target_pairs={{0,8},{4,12},{8,16},{12,20},{16,24},{20,28},{1,9},{5,13},{9,17},{1... | collective-permute-start | bytes 1572872 | tf_op jit(solution)/shard_map/ppermute | solution.py:12
  105.6 15.4 %copy-start.20 = (bf16[64,8,8,128]{3,2,1,0:T(8,128)(2,1)S(1)}, bf16[64,8,8,128]{3,2,1,0:T(8,128)(2,1)}, u32[]{:S(2)}) copy-start(bf16[64,8,8,128]{3,2,1,0:T(8,128)(2,1)} %copy.251) | copy-start | bytes 3145732
  106.5 17.1 %copy-start.9 = (bf16[8,256,512]{2,1,0:T(8,128)(2,1)}, bf16[8,256,512]{2,1,0:T(8,128)(2,1)S(1)}, u32[]{:S(2)}) copy-start(bf16[8,256,512]{2,1,0:T(8,128)(2,1)S(1)} %select_convert_fusion.1) | copy-start | bytes 6291460
  106.5 16.3 %copy-start.3 = (bf16[64,8,8,128]{3,2,1,0:T(8,128)(2,1)S(1)}, bf16[64,8,8,128]{3,2,1,0:T(8,128)(2,1)}, u32[]{:S(2)}) copy-start(bf16[64,8,8,128]{3,2,1,0:T(8,128)(2,1)} %copy-done.2) | copy-start | bytes 3145732
  115.3 14.8 %collective-permute-start.3 = (f32[8,128,128]{2,1,0:T(8,128)S(1)}, f32[8,128,128]{2,1,0:T(8,128)S(1)}, u32[]{:S(2)}, u32[]{:S(2)}) collective-permute-start(f32[8,128,128]{2,1,0:T(8,128)S(1)} %select_add_fusion.2), channel_id=1, source_target_pairs={{0,16},{4,20},{8,24},{12,28},{1,17},{5,21},{9,25},{13,29},{2,18},{... | collective-permute-start | bytes 1572872 | tf_op jit(solution)/shard_map/ppermute | solution.py:12
  122.8 7.3 %copy-start.5 = (bf16[256,8,128]{0,2,1:T(8,128)(2,1)S(1)}, bf16[256,8,128]{0,2,1:T(8,128)(2,1)}, u32[]{:S(2)}) copy-start(bf16[256,8,128]{0,2,1:T(8,128)(2,1)} %copy.211) | copy-start | bytes 1572868
  123.6 7.2 %copy-start = (f32[32,8,8,128]{3,2,1,0:T(8,128)S(1)}, f32[32,8,8,128]{3,2,1,0:T(8,128)}, u32[]{:S(2)}) copy-start(f32[32,8,8,128]{3,2,1,0:T(8,128)} %copy.249) | copy-start | bytes 3145732
  130.8 1.3 copy-start.1
  134.3 3.6 %copy-start.15 = (bf16[256,8,128]{2,0,1:T(8,128)(2,1)}, bf16[256,8,128]{2,0,1:T(8,128)(2,1)S(1)}, u32[]{:S(2)}) copy-start(bf16[256,8,128]{2,0,1:T(8,128)(2,1)S(1)} %get-tuple-element.113) | copy-start | bytes 1572868
  134.3 3.6 %copy-start.18 = (bf16[256,8,128]{2,0,1:T(8,128)(2,1)}, bf16[256,8,128]{2,0,1:T(8,128)(2,1)S(1)}, u32[]{:S(2)}) copy-start(bf16[256,8,128]{2,0,1:T(8,128)(2,1)S(1)} %get-tuple-element.91) | copy-start | bytes 1572868
  134.3 1.5 copy-start.31
  143.1 59.0 %all-to-all-start.3 = ((bf16[4,128,1024]{2,1,0:T(8,128)(2,1)}), bf16[4,128,1024]{2,1,0:T(8,128)(2,1)}, u32[]{:S(2)}, u32[]{:S(2)}) async-start(bf16[4,128,1024]{2,1,0:T(8,128)(2,1)} %all_to_all.105), calls=%async_computation.3 | async-start | bytes 2097152 | tf_op jit(solution)/shard_map/all_to_all | solution.py:125
  147.3 3.3 %copy-start.16 = (bf16[256,8,128]{2,0,1:T(8,128)(2,1)S(1)}, bf16[256,8,128]{2,0,1:T(8,128)(2,1)}, u32[]{:S(2)}) copy-start(bf16[256,8,128]{2,0,1:T(8,128)(2,1)} %copy-done.15) | copy-start | bytes 1572868
  147.3 18.8 %collective-permute-start.4 = (bf16[8,128,128]{2,1,0:T(8,128)(2,1)}, bf16[8,128,128]{2,1,0:T(8,128)(2,1)}, u32[]{:S(2)}, u32[]{:S(2)}) collective-permute-start(bf16[8,128,128]{2,1,0:T(8,128)(2,1)} %convolution_convert_fusion), channel_id=1, source_target_pairs={{4,0},{8,4},{12,8},{16,12},{20,16},{24,20},{28,24},{5,1},{9,5},{13... | collective-permute-start | bytes 786440 | tf_op jit(solution)/shard_map/ppermute | solution.py:12
  150.6 2.0 copy-start.7
  152.6 1.0 copy-start.19
  166.2 15.4 %copy-start.11 = (f32[512,1024]{1,0:T(8,128)S(1)}, f32[512,1024]{1,0:T(8,128)}, u32[]{:S(2)}) copy-start(f32[512,1024]{1,0:T(8,128)} %copy.236) | copy-start | bytes 6291460
  166.2 12.9 %collective-permute-start.5 = (bf16[8,128,128]{2,1,0:T(8,128)(2,1)}, bf16[8,128,128]{2,1,0:T(8,128)(2,1)S(1)}, u32[]{:S(2)}, u32[]{:S(2)}) collective-permute-start(bf16[8,128,128]{2,1,0:T(8,128)(2,1)} %collective-permute-done.4), channel_id=1, source_target_pairs={{4,0},{8,4},{12,8},{16,12},{20,16},{24,20},{28,24},{5,1},{9,5},{13... | collective-permute-start | bytes 786440 | tf_op jit(solution)/shard_map/ppermute | solution.py:12
  179.1 20.4 %copy-start.22 = (bf16[8,128,128]{2,1,0:T(8,128)(2,1)}, bf16[8,128,128]{2,1,0:T(8,128)(2,1)S(1)}, u32[]{:S(2)}) copy-start(bf16[8,128,128]{2,1,0:T(8,128)(2,1)S(1)} %collective-permute-done.5) | copy-start | bytes 786436
  180.2 19.2 %collective-permute-start.6 = (bf16[8,128,128]{2,1,0:T(8,128)(2,1)S(1)}, bf16[8,128,128]{2,1,0:T(8,128)(2,1)S(1)}, u32[]{:S(2)}, u32[]{:S(2)}) collective-permute-start(bf16[8,128,128]{2,1,0:T(8,128)(2,1)S(1)} %fusion.37), channel_id=1, source_target_pairs={{8,0},{12,4},{16,8},{20,12},{24,16},{28,20},{9,1},{13,5},{17,9},{2... | collective-permute-start | bytes 786440 | tf_op jit(solution)/shard_map/ppermute | solution.py:12
  183.1 23.7 %copy-start.17 = (bf16[256,8,128]{2,0,1:T(8,128)(2,1)S(1)}, bf16[256,8,128]{2,0,1:T(8,128)(2,1)}, u32[]{:S(2)}) copy-start(bf16[256,8,128]{2,0,1:T(8,128)(2,1)} %copy-done.15) | copy-start | bytes 1572868
  199.5 1.2 copy-start.25
  200.7 15.9 %copy-start.23 = (bf16[8,128,128]{2,1,0:T(8,128)(2,1)S(1)}, bf16[8,128,128]{2,1,0:T(8,128)(2,1)}, u32[]{:S(2)}) copy-start(bf16[8,128,128]{2,1,0:T(8,128)(2,1)} %copy-done.22) | copy-start | bytes 786436
  200.7 15.9 %collective-permute-start.7 = (bf16[8,128,128]{2,1,0:T(8,128)(2,1)S(1)}, bf16[8,128,128]{2,1,0:T(8,128)(2,1)}, u32[]{:S(2)}, u32[]{:S(2)}) collective-permute-start(bf16[8,128,128]{2,1,0:T(8,128)(2,1)S(1)} %fusion.40), channel_id=1, source_target_pairs={{16,0},{20,4},{24,8},{28,12},{17,1},{21,5},{25,9},{29,13},{18,2},{... | collective-permute-start | bytes 786440 | tf_op jit(solution)/shard_map/ppermute | solution.py:12
  202.1 14.5 %copy-start.26 = (bf16[8,128,128]{2,1,0:T(8,128)(2,1)S(1)}, bf16[8,128,128]{2,1,0:T(8,128)(2,1)}, u32[]{:S(2)}) copy-start(bf16[8,128,128]{2,1,0:T(8,128)(2,1)} %copy-done.25) | copy-start | bytes 786436
  202.1 18.9 %all-to-all-start.5 = ((bf16[4,128,1024]{2,1,0:T(8,128)(2,1)}), bf16[4,128,1024]{2,1,0:T(8,128)(2,1)}, u32[]{:S(2)}, u32[]{:S(2)}) async-start(bf16[4,128,1024]{2,1,0:T(8,128)(2,1)} %fusion.6), calls=%async_computation.5 | async-start | bytes 2097152 | tf_op jit(solution)/shard_map/all_to_all | solution.py:186
  206.8 11.1 %copy-start.10 = (f32[8,128,512]{2,1,0:T(8,128)S(1)}, f32[8,128,512]{2,1,0:T(8,128)}, u32[]{:S(2)}) copy-start(f32[8,128,512]{2,1,0:T(8,128)} %fusion.58) | copy-start | bytes 6291460
  218.7 6.6 %copy-start.6 = (bf16[256,8,128]{0,2,1:T(8,128)(2,1)S(1)}, bf16[256,8,128]{0,2,1:T(8,128)(2,1)}, u32[]{:S(2)}) copy-start(bf16[256,8,128]{0,2,1:T(8,128)(2,1)} %copy.211) | copy-start | bytes 1572868
  219.9 7.0 %copy-start.8 = (bf16[8,256,512]{2,1,0:T(8,128)(2,1)S(1)}, bf16[8,256,512]{2,1,0:T(8,128)(2,1)}, u32[]{:S(2)}) copy-start(bf16[8,256,512]{2,1,0:T(8,128)(2,1)} %select_convert_fusion) | copy-start | bytes 6291460
  219.9 7.0 %copy-start.14 = (bf16[256,8,128]{0,2,1:T(8,128)(2,1)S(1)}, bf16[256,8,128]{0,2,1:T(8,128)(2,1)}, u32[]{:S(2)}) copy-start(bf16[256,8,128]{0,2,1:T(8,128)(2,1)} %copy.212) | copy-start | bytes 1572868
  221.1 18.8 %all-to-all-start.7 = ((bf16[4,128,1024]{1,2,0:T(8,128)(2,1)}), bf16[4,128,1024]{1,2,0:T(8,128)(2,1)}, u32[]{:S(2)}, u32[]{:S(2)}) async-start(bf16[4,128,1024]{1,2,0:T(8,128)(2,1)} %copy.221), calls=%async_computation.7 | async-start | bytes 2097152 | tf_op jit(solution)/shard_map/all_to_all | solution.py:188
  226.9 1.2 copy-start.4
  226.9 1.9 copy-start.12
  239.8 18.0 %all-to-all-start.6 = ((bf16[4,128,1024]{1,2,0:T(8,128)(2,1)}), bf16[4,128,1024]{1,2,0:T(8,128)(2,1)S(1)}, u32[]{:S(2)}, u32[]{:S(2)}) async-start(bf16[4,128,1024]{1,2,0:T(8,128)(2,1)} %copy.216), calls=%async_computation.6 | async-start | bytes 2097152 | tf_op jit(solution)/shard_map/all_to_all | solution.py:187
where the time goes:
time: 262 us; the launch traced here: 259 us
  waiting for transfers between devices  94.6 us (36%)
  starting transfers between devices  58.1 us (22%)
  local copies, waits for them, and re-layouts  48.2 us (18%)
  matrix products  23.4 us (9%)
  other arithmetic  23 us (9%)
  between operations  11.8 us (5%)
    ppermute x8, waiting for transfers between devices, from_behind(): return lax.ppermute(array, axis, pairs)  52 us
    ppermute x8, starting transfers between devices, from_behind(): return lax.ppermute(array, axis, pairs)  25.9 us
    unnamed x79, local copies, waits for them, and re-layouts  16.6 us
    all_to_all x1, waiting for transfers between devices, local(): lax.all_to_all(keys, 'head', split_axis=1, concat_axis=0, tiled=True)  13.4 us
    all_to_all x1, waiting for transfers between devices, local(): lax.all_to_all(out_grad, 'head', split_axis=1, concat_axis=0, tiled=True)  9.47 us
    all_to_all x1, waiting for transfers between devices, local(): lax.all_to_all(grad_value, 'head', split_axis=0, concat_axis=1, tiled=True)  9 us
    all_to_all x1, waiting for transfers between devices, local(): lax.all_to_all(grad_key, 'head', split_axis=0, concat_axis=1, tiled=True)  6.94 us
  transfers between devices with their start and end apart: 16, of which 12 were waited for; matrix products, arithmetic and copies ran while one was open for 28% of the time, Pallas kernels for 0%

commit v1 on v0

v1 whole, which is shorter than its diff:
```python
import functools

import jax
import jax.numpy as jnp
from jax import lax
from jax.experimental import pallas as pl
from jax.experimental.pallas import tpu as pltpu
from jax.sharding import Mesh, PartitionSpec as P

DH = 128
F32 = jnp.float32
BF16 = jnp.bfloat16
NN = (((1,), (0,)), ((), ()))
NT = (((1,), (1,)), ((), ()))
TN = (((0,), (0,)), ((), ()))
LAYER = ("x", "head")


def mul(a, b, dims):
    return lax.dot_general(a, b, dims, preferred_element_type=F32)


def feature(wide):
    return jnp.where(wide > 0, wide + 1.0, jnp.exp(jnp.minimum(wide, 0.0)))


def slope(wide):
    return jnp.where(wide > 0, 1.0, jnp.exp(jnp.minimum(wide, 0.0)))


def doc_ends(lens):
    ends, total = [], 0
    for j in range(lens.shape[0]):
        total = total + lens[j]
        ends.append(total)
    return ends


def doc_at(ends, where):
    found = 0
    for end in ends:
        found = found + jnp.where(where >= end, 1, 0)
    return found


def rows_of(ends, first, count):
    at = first + lax.broadcasted_iota(jnp.int32, (count, 1), 0)
    return doc_at(ends, at)


def columns_of(ends, first, count):
    at = first + lax.broadcasted_iota(jnp.int32, (1, count), 1)
    return doc_at(ends, at)


def visible(ends, first, count):
    later = lax.broadcasted_iota(jnp.int32, (count, count), 0)
    earlier = lax.broadcasted_iota(jnp.int32, (count, count), 1)
    return (later >= earlier) & (
        rows_of(ends, first, count) == columns_of(ends, first, count)
    )


def head_mask(ends, first, count):
    return rows_of(ends, first, count) == doc_at(ends, first)


def tail_mask(ends, first, count):
    return rows_of(ends, first, count) == doc_at(ends, first + count - 1)


def cols(h):
    return slice(h * DH, (h + 1) * DH)


def tail_kernel(lens, place, k, v, out):
    count = k.shape[0]
    tail = tail_mask(doc_ends(lens), place[0] * count, count)
    for h in range(out.shape[0]):
        fk = jnp.where(tail, feature(k[:, cols(h)].astype(F32)), 0.0).astype(BF16)
        out[h] = mul(fk, v[:, cols(h)], TN).astype(BF16)


def local_kernel(lens, place, q, k, v, scores, part):
    count = q.shape[0]
    seen = visible(doc_ends(lens), place[0] * count, count)
    for h in range(scores.shape[0]):
        fq = feature(q[:, cols(h)].astype(F32)).astype(BF16)
        fk = feature(k[:, cols(h)].astype(F32)).astype(BF16)
        s = jnp.where(seen, mul(fq, fk, NT), 0.0).astype(BF16)
        scores[h] = s
        part[:, cols(h)] = mul(s, v[:, cols(h)], NN)


def norm_kernel(lens, place, q, g, part, incoming, out, grad_att, state):
    count = q.shape[0]
    head = head_mask(doc_ends(lens), place[0] * count, count)
    for h in range(state.shape[0]):
        fq = jnp.where(head, feature(q[:, cols(h)].astype(F32)), 0.0).astype(BF16)
        att = part[:, cols(h)] + mul(fq, incoming[h], NN)
        inv = lax.rsqrt(jnp.mean(att * att, axis=-1, keepdims=True) + 1e-05)
        normed = att * inv
        out[:, cols(h)] = normed.astype(BF16)
        go = g[:, cols(h)].astype(F32)
        ga = (go - normed * jnp.mean(go * normed, axis=-1, keepdims=True)) * inv
        ga = ga.astype(BF16)
        grad_att[:, cols(h)] = ga
        state[h] = mul(fq, ga, TN).astype(BF16)


def inner_kernel(lens, place, q, k, v, grad_att, incoming, scores, gq, gk, gv):
    count = q.shape[0]
    ends = doc_ends(lens)
    first = place[0] * count
    seen = visible(ends, first, count)
    head = head_mask(ends, first, count)
    for h in range(scores.shape[0]):
        wide = q[:, cols(h)].astype(F32)
        fq = feature(wide).astype(BF16)
        fk = feature(k[:, cols(h)].astype(F32)).astype(BF16)
        ga = grad_att[:, cols(h)]
        gs = jnp.where(seen, mul(ga, v[:, cols(h)], NT), 0.0).astype(BF16)
        total = mul(gs, fk, NN) + jnp.where(head, mul(ga, incoming[h], NT), 0.0)
        gq[:, cols(h)] = (total * slope(wide)).astype(BF16)
        gk[:, cols(h)] = mul(gs, fq, TN)
        gv[:, cols(h)] = mul(scores[h], ga, TN)


def last_kernel(lens, place, k, v, gk_part, gv_part, outgoing, gk, gv):
    count = k.shape[0]
    tail = tail_mask(doc_ends(lens), place[0] * count, count)
    for h in range(outgoing.shape[0]):
        wide = k[:, cols(h)].astype(F32)
        fk = jnp.where(tail, feature(wide), 0.0).astype(BF16)
        vt = jnp.where(tail, v[:, cols(h)].astype(F32), 0.0).astype(BF16)
        gk[:, cols(h)] = (
            (gk_part[:, cols(h)] + mul(vt, outgoing[h], NT)) * slope(wide)
        ).astype(BF16)
        gv[:, cols(h)] = (gv_part[:, cols(h)] + mul(fk, outgoing[h], NN)).astype(BF16)


def same(a, b):
    return jnp.where(a == b, 1.0, 0.0).astype(F32)


def total_kernel(forward, count, lens, place, held, total):
    members = held.shape[0]
    ends = doc_ends(lens)
    layer = place[1] * (members * count)
    carry = None
    for step in range(members):
        i = step if forward else members - 1 - step
        mine = held[i, 0].astype(F32)
        edge = layer + ((i + 1) * count - 1 if forward else i * count)
        here = doc_at(ends, edge)
        if carry is not None:
            mine = mine + carry * same(here, previous)
        carry, previous = mine, here
    total[0] = carry.astype(BF16)


def prefix_kernel(forward, count, lens, place, held, *rest):
    others, out = rest[:-1], rest[-1]
    members = held.shape[0]
    span = members * count
    ends = doc_ends(lens)
    layer = place[1] * span
    sign = -1 if forward else 1
    previous = doc_at(ends, layer - 1 if forward else layer + span)
    carry = None
    for s, other in enumerate(others):
        far = layer + sign * s * span
        there = doc_at(ends, far - 1 if forward else far + span)
        term = other[0].astype(F32) * same(there, previous)
        carry = term if carry is None else carry + term
    for step in range(members):
        i = step if forward else members - 1 - step
        near, far = layer + i * count, layer + (i + 1) * count - 1
        if not forward:
            near, far = far, near
        if carry is None:
            out[i, 0] = jnp.zeros(out.shape[2:], BF16)
        else:
            out[i, 0] = (carry * same(doc_at(ends, near), previous)).astype(BF16)
        if step < members - 1:
            here = doc_at(ends, far)
            mine = held[i, 0].astype(F32)
            if carry is not None:
                mine = mine + carry * same(here, previous)
            carry, previous = mine, here


SMEM = pl.BlockSpec(memory_space=pltpu.SMEM)
PARAMS = pltpu.CompilerParams(
    dimension_semantics=("arbitrary",), vmem_limit_bytes=48 * 1024 * 1024
)


def local(queries, keys, values, out_grad, doc_lengths):
    count, width = queries.shape
    heads = width // DH
    layers = lax.axis_size("z")
    members = lax.axis_size("x") * lax.axis_size("head")
    owned = heads // members
    place = jnp.stack(
        [lax.axis_index(("z", "x", "head")), lax.axis_index("z")]
    ).astype(jnp.int32)
    block_heads = 4
    steps = heads // block_heads
    tokens = pl.BlockSpec((count, block_heads * DH), lambda i: (0, i))
    states = pl.BlockSpec((block_heads, DH, DH), lambda i: (i, 0, 0))
    tiles = pl.BlockSpec((block_heads, count, count), lambda i: (i, 0, 0))
    token_bf = jax.ShapeDtypeStruct((count, width), BF16)
    token_f32 = jax.ShapeDtypeStruct((count, width), F32)
    state_bf = jax.ShapeDtypeStruct((heads, DH, DH), BF16)
    tile_bf = jax.ShapeDtypeStruct((heads, count, count), BF16)

    def run(kernel, ins, outs, shapes, args, products, name):
        return pl.pallas_call(
            kernel,
            grid=(steps,),
            in_specs=[SMEM, SMEM] + ins,
            out_specs=outs,
            out_shape=shapes,
            compiler_params=PARAMS,
            cost_estimate=pl.CostEstimate(
                flops=2 * products * heads * count * DH * DH,
                bytes_accessed=2 * (len(ins) + len(outs)) * count * width,
                transcendentals=count * width,
            ),
            name=name,
        )(doc_lengths, place, *args)

    def combine(kernel, args, many, forward, name):
        group = pl.BlockSpec((members, 1, DH, DH), lambda i: (0, i, 0, 0))
        single = pl.BlockSpec((1, DH, DH), lambda i: (i, 0, 0))
        return pl.pallas_call(
            functools.partial(kernel, forward, count),
            grid=(owned,),
            in_specs=[SMEM, SMEM, group] + [single] * (len(args) - 1),
            out_specs=group if many else single,
            out_shape=jax.ShapeDtypeStruct(
                ((members,) if many else ()) + (owned, DH, DH), BF16
            ),
            compiler_params=PARAMS,
            cost_estimate=pl.CostEstimate(
                flops=4 * heads * DH * DH,
                bytes_accessed=4 * heads * DH * DH,
                transcendentals=0,
            ),
            name=name,
        )(doc_lengths, place, *args)

    def scan(state, forward, name):
        held = lax.all_to_all(state, LAYER, split_axis=0, concat_axis=0, tiled=True)
        held = held.reshape(members, owned, DH, DH)
        others = []
        if layers > 1:
            total = combine(total_kernel, (held,), False, forward, name + "_total")
            for s in range(1, min(layers - 1, -(-layers // 2)) + 1):
                pairs = [(i, i + s) if forward else (i + s, i) for i in range(layers - s)]
                others.append(lax.ppermute(total, "z", pairs))
        sums = combine(prefix_kernel, (held, *others), True, forward, name + "_prefix")
        return lax.all_to_all(
            sums.reshape(heads, DH, DH), LAYER, split_axis=0, concat_axis=0, tiled=True
        )

    (tail,) = run(tail_kernel, [tokens] * 2, [states], [state_bf], (keys, values), 1, "tail")
    incoming = scan(tail, True, "carried")
    scores, part = run(
        local_kernel,
        [tokens] * 3,
        [tiles, tokens],
        [tile_bf, token_f32],
        (queries, keys, values),
        2,
        "within",
    )
    attn_out, grad_att, head_state = run(
        norm_kernel,
        [tokens, tokens, tokens, states],
        [tokens, tokens, states],
        [token_bf, token_bf, state_bf],
        (queries, out_grad, part, incoming),
        2,
        "normed",
    )
    outgoing = scan(head_state, False, "future")
    grad_queries, gk_part, gv_part = run(
        inner_kernel,
        [tokens] * 4 + [states, tiles],
        [tokens] * 3,
        [token_bf, token_f32, token_f32],
        (queries, keys, values, grad_att, incoming, scores),
        5,
        "grads_within",
    )
    grad_keys, grad_values = run(
        last_kernel,
        [tokens] * 4 + [states],
        [tokens] * 2,
        [token_bf, token_bf],
        (keys, values, gk_part, gv_part, outgoing),
        2,
        "grads_last",
    )
    return attn_out, grad_queries, grad_keys, grad_values


def solution(mesh):
    n_seq, n_head = mesh.shape["seq"], mesh.shape["head"]
    inner = 2 if n_seq % 2 == 0 else 1
    fine = Mesh(mesh.devices.reshape(n_seq // inner, inner, n_head), ("z", "x", "head"))
    rows = P(("z", "x", "head"), None)
    return jax.shard_map(
        local,
        mesh=fine,
        in_specs=(rows, rows, rows, rows, P()),
        out_specs=(rows, rows, rows, rows),
        check_vma=False,
    )
```

time: 262 us -> 132 us (0.50)
  waiting for transfers between devices: 94.6 us -> 22.6 us
  Pallas kernels: 0 us -> 40.9 us
  starting transfers between devices: 58.1 us -> 19.3 us
  local copies, waits for them, and re-layouts: 48.2 us -> 10.1 us
  blocking collectives: 0 us -> 36.7 us
  matrix products: 23.4 us -> 0 us
  other arithmetic: 23 us -> 0.08 us
  between operations: 11.8 us -> 0.82 us
    pallas_call x0 -> x9, Pallas kernels: none -> 40.9 us  [the longest x5 35.8 us: run(): pl.pallas_call(kernel, grid=(steps,), in_specs=[SMEM, SMEM] + ins, out_sp...]
    ppermute x8 -> x4, waiting for transfers between devices: 52 us -> 14 us  [scan(): others.append(lax.ppermute(total, 'z', pairs))]
    all_to_all x0 -> x2, blocking collectives: none -> 36.7 us  [scan(): held = lax.all_to_all(state, LAYER, split_axis=0, concat_axis=0, tiled=True)]
    all_to_all x8 -> x2, waiting for transfers between devices: 42.6 us -> 8.67 us  [scan(): lax.all_to_all(sums.reshape(heads, DH, DH), LAYER, split_axis=0, concat_a...]
    all_to_all x8 -> x2, starting transfers between devices: 32.2 us -> 8.5 us  [scan(): lax.all_to_all(sums.reshape(heads, DH, DH), LAYER, split_axis=0, concat_a...]
    dot_general x20 -> x0, matrix products: 23.4 us -> none  [the longest x2 3.99 us: local(): jnp.einsum('hts,the->she', score_tiles[tile], grad_tile, preferred_elemen...]
    ppermute x8 -> x4, starting transfers between devices: 25.9 us -> 10.8 us  [scan(): others.append(lax.ppermute(total, 'z', pairs))]
    all_to_all x11 -> x0, local copies, waits for them, and re-layouts: 14.5 us -> none  [the longest x2 3.91 us: local(): lax.all_to_all(out_block, 'head', split_axis=0, concat_axis=1, tiled=True)]
  transfers between devices with their start and end apart: 16 -> 6, of which waited for: 12 -> 4; matrix products, arithmetic and copies ran while one was open for 28% -> 0% of each run, Pallas kernels for 0% -> 14%
where the time goes in v1:
time: 132 us; the launch traced here: 131 us
  Pallas kernels  40.9 us (31%)
  blocking collectives  36.7 us (28%)
  waiting for transfers between devices  22.6 us (17%)
  starting transfers between devices  19.3 us (15%)
  local copies, waits for them, and re-layouts  10.1 us (8%)
    all_to_all x2, blocking collectives, scan(): held = lax.all_to_all(state, LAYER, split_axis=0, concat_axis=0, tiled=True)  36.7 us
    pallas_call x5, Pallas kernels, run(): pl.pallas_call(kernel, grid=(steps,), in_specs=[SMEM, SMEM] + ins, out_sp...  35.8 us
    ppermute x4, waiting for transfers between devices, scan(): others.append(lax.ppermute(total, 'z', pairs))  14 us
    ppermute x4, starting transfers between devices, scan(): others.append(lax.ppermute(total, 'z', pairs))  10.8 us
    unnamed x28, local copies, waits for them, and re-layouts  10.1 us
    all_to_all x2, waiting for transfers between devices, scan(): lax.all_to_all(sums.reshape(heads, DH, DH), LAYER, split_axis=0, concat_a...  8.67 us
    all_to_all x2, starting transfers between devices, scan(): lax.all_to_all(sums.reshape(heads, DH, DH), LAYER, split_axis=0, concat_a...  8.5 us
    pallas_call x4, Pallas kernels, combine(): pl.pallas_call(functools.partial(kernel, forward, count), grid=(owned,),...  5.17 us
  transfers between devices with their start and end apart: 6, of which 4 were waited for; matrix products, arithmetic and copies ran while one was open for 0% of the time, Pallas kernels for 14%

profile of v1, /device:TPU:0, one launch (start us, length us, event | category | flops | bytes accessed | tf_op | source)
XLA Modules:
  0.0 130.6 jit_solution(2449587646075922837)
XLA Ops:
  0.6 0.1 pad_add_fusion.place
  0.7 0.0 copy-start
  0.7 1.2 copy-done
  1.9 0.0 copy-start.2
  1.9 1.2 copy-done.2
  3.2 0.0 copy-start.12
  3.2 0.7 copy-done.12
  3.8 0.0 copy-start.13
  3.8 3.3 %tail.1 = bf16[32,128,128]{2,1,0:T(8,128)(2,1)S(1)} custom-call(s32[8]{0:T(128)S(1)} %copy-done.12, s32[2]{0:T(128)S(1)} %pad_add_fusion.place, bf16[128,4096]{1,0:T(8,128)(2,1)S(1)} %copy-done, bf16[128,4096]{1,0:T(8,128)(2,1)S(1)} %copy-done.2), custom_call_target="tpu_custom_call" | custom-call | flops 134217728 | bytes 3145728 | tf_op jit(solution)/shard_map/tail/pallas_call | solution.py:219
  7.1 19.6 %all_to_all.20 = bf16[32,128,128]{2,1,0:T(8,128)(2,1)S(1)} all-to-all(bf16[32,128,128]{2,1,0:T(8,128)(2,1)S(1)} %tail.1), channel_id=1, replica_groups=mesh['z'=4,'x'=2,'head'=4] {'x','head'}, dimensions={0} | all-to-all | bytes 2097152 | tf_op jit(solution)/shard_map/all_to_all | solution.py:255
  26.7 0.0 copy-done.13
  26.7 1.1 carried_total.1
  27.8 0.0 copy-start.1
  27.8 0.0 copy-start.3
  27.9 0.0 copy-start.4
  27.9 4.8 %collective-permute-start.1 = (bf16[4,128,128]{2,1,0:T(8,128)(2,1)S(1)}, bf16[4,128,128]{2,1,0:T(8,128)(2,1)S(1)}, u32[]{:S(2)}, u32[]{:S(2)}) collective-permute-start(bf16[4,128,128]{2,1,0:T(8,128)(2,1)S(1)} %carried_total.1), channel_id=1, source_target_pairs={{0,16},{8,24},{1,17},{9,25},{2,18},{10,26},{3,19},{11,27},{4,20},{... | collective-permute-start | bytes 393224 | tf_op jit(solution)/shard_map/ppermute | solution.py:262
  32.6 3.5 %collective-permute-start = (bf16[4,128,128]{2,1,0:T(8,128)(2,1)S(1)}, bf16[4,128,128]{2,1,0:T(8,128)(2,1)S(1)}, u32[]{:S(2)}, u32[]{:S(2)}) collective-permute-start(bf16[4,128,128]{2,1,0:T(8,128)(2,1)S(1)} %carried_total.1), channel_id=1, source_target_pairs={{0,8},{8,16},{16,24},{1,9},{9,17},{17,25},{2,10},{10,18},{18,26},{... | collective-permute-start | bytes 393224 | tf_op jit(solution)/shard_map/ppermute | solution.py:262
  36.1 0.0 collective-permute-done.1.rest_1_
  36.1 2.5 %collective-permute-done.rest_0_ = bf16[4,128,128]{2,1,0:T(8,128)(2,1)S(1)} collective-permute-done((bf16[4,128,128]{2,1,0:T(8,128)(2,1)S(1)}, bf16[4,128,128]{2,1,0:T(8,128)(2,1)S(1)}, u32[]{:S(2)}, u32[]{:S(2)}) %collective-permute-start) | collective-permute-done | bytes 131104 | tf_op jit(solution)/shard_map/ppermute | solution.py:262
  38.6 1.5 %carried_prefix.1 = bf16[8,4,128,128]{3,2,1,0:T(8,128)(2,1)S(1)} custom-call(s32[8]{0:T(128)S(1)} %copy-done.13, s32[2]{0:T(128)S(1)} %pad_add_fusion.place, bf16[8,4,128,128]{3,2,1,0:T(8,128)(2,1)S(1)} %bitcast.7, bf16[4,128,128]{2,1,0:T(8,128)(2,1)S(1)} %collective-permute-done.rest_0_, bf16[4,128,128]{2,1,0:T(8,128)(2,1)S(1)} %collective-permute-done.1.rest_1_), custom_call_target="tpu_custom_call" | custom-call | flops 2097152 | bytes 2097152 | tf_op jit(solution)/shard_map/carried_prefix/pallas_call | solution.py:237
  40.1 0.0 copy-start.6
  40.1 1.0 copy-done.6
  41.1 4.2 %all-to-all-start.1 = ((bf16[32,128,128]{2,1,0:T(8,128)(2,1)}), bf16[32,128,128]{2,1,0:T(8,128)(2,1)}, u32[]{:S(2)}, u32[]{:S(2)}) async-start(bf16[32,128,128]{2,1,0:T(8,128)(2,1)} %bitcast.11), calls=%async_computation.1 | async-start | bytes 2097152 | tf_op jit(solution)/shard_map/all_to_all | solution.py:264
  45.3 0.0 copy-done.1
  45.3 0.0 copy-done.3
  45.3 0.0 copy-done.4
  45.4 7.6 %within.1 = (bf16[32,128,128]{2,1,0:T(8,128)(2,1)S(1)}, f32[128,4096]{1,0:T(8,128)}) custom-call(s32[8]{0:T(128)S(1)} %copy-done.13, s32[2]{0:T(128)S(1)} %pad_add_fusion.place, bf16[128,4096]{1,0:T(8,128)(2,1)S(1)} %copy-done.4, bf16[128,4096]{1,0:T(8,128)(2,1)S(1)} %copy-done.1, bf16[128,4096]{1,0:T(8,128)(2,1)S(1)} %copy-done.3), custom_call_target="tpu_custom_call" | custom-call | flops 268435456 | bytes 5242880 | tf_op jit(solution)/shard_map/within/pallas_call | solution.py:219
  53.0 0.0 copy-start.9
  53.0 1.0 copy-done.9
  53.9 5.8 %all-to-all-done.1.incoming = bf16[32,128,128]{2,1,0:T(8,128)(2,1)} async-done(((bf16[32,128,128]{2,1,0:T(8,128)(2,1)}), bf16[32,128,128]{2,1,0:T(8,128)(2,1)}, u32[]{:S(2)}, u32[]{:S(2)}) %all-to-all-start.1) | async-done | bytes 1048608 | tf_op jit(solution)/shard_map/all_to_all | solution.py:264
  59.8 0.0 copy-start.8
  59.8 1.2 copy-done.8
  61.0 7.6 %normed.1 = (bf16[128,4096]{1,0:T(8,128)(2,1)}, bf16[128,4096]{1,0:T(8,128)(2,1)S(1)}, bf16[32,128,128]{2,1,0:T(8,128)(2,1)S(1)}) custom-call(s32[8]{0:T(128)S(1)} %copy-done.13, s32[2]{0:T(128)S(1)} %pad_add_fusion.place, bf16[128,4096]{1,0:T(8,128)(2,1)S(1)} %copy-done.4, bf16[128,4096]{1,0:T(8,128)(2,1)S(1)} %copy-done.8, ...), custom_call_target="tpu_custom_call" | custom-call | flops 268435456 | bytes 7340032 | tf_op jit(solution)/shard_map/normed/pallas_call | solution.py:219
  68.6 0.0 copy-start.10
  68.6 17.1 %all_to_all.21 = bf16[32,128,128]{2,1,0:T(8,128)(2,1)S(1)} all-to-all(bf16[32,128,128]{2,1,0:T(8,128)(2,1)S(1)} %get-tuple-element.21), channel_id=1, replica_groups=mesh['z'=4,'x'=2,'head'=4] {'x','head'}, dimensions={0} | all-to-all | bytes 2097152 | tf_op jit(solution)/shard_map/all_to_all | solution.py:255
  85.7 1.1 future_total.1
  86.9 1.3 collective-permute-start.3
  88.2 1.3 collective-permute-start.2
  89.5 11.5 %collective-permute-done.3.rest_1_ = bf16[4,128,128]{2,1,0:T(8,128)(2,1)S(1)} collective-permute-done((bf16[4,128,128]{2,1,0:T(8,128)(2,1)S(1)}, bf16[4,128,128]{2,1,0:T(8,128)(2,1)S(1)}, u32[]{:S(2)}, u32[]{:S(2)}) %collective-permute-start.3) | collective-permute-done | bytes 131104 | tf_op jit(solution)/shard_map/ppermute | solution.py:262
  101.0 0.0 copy-done.10
  101.0 0.0 collective-permute-done.2.rest_0_
  101.0 1.5 %future_prefix.1 = bf16[8,4,128,128]{3,2,1,0:T(8,128)(2,1)S(1)} custom-call(s32[8]{0:T(128)S(1)} %copy-done.13, s32[2]{0:T(128)S(1)} %pad_add_fusion.place, bf16[8,4,128,128]{3,2,1,0:T(8,128)(2,1)S(1)} %bitcast.9, bf16[4,128,128]{2,1,0:T(8,128)(2,1)S(1)} %collective-permute-done.2.rest_0_, bf16[4,128,128]{2,1,0:T(8,128)(2,1)S(1)} %collective-permute-done.3.rest_1_), custom_call_target="tpu_custom_call" | custom-call | flops 2097152 | bytes 2097152 | tf_op jit(solution)/shard_map/future_prefix/pallas_call | solution.py:237
  102.4 0.0 copy-start.5
  102.4 1.0 copy-done.5
  103.4 4.2 %all-to-all-start.3 = ((bf16[32,128,128]{2,1,0:T(8,128)(2,1)}), bf16[32,128,128]{2,1,0:T(8,128)(2,1)}, u32[]{:S(2)}, u32[]{:S(2)}) async-start(bf16[32,128,128]{2,1,0:T(8,128)(2,1)} %bitcast.10), calls=%async_computation.3 | async-start | bytes 2097152 | tf_op jit(solution)/shard_map/all_to_all | solution.py:264
  107.7 0.0 copy-start.11
  107.7 1.2 copy-done.11
  108.9 10.4 %grads_within.1 = (bf16[128,4096]{1,0:T(8,128)(2,1)}, f32[128,4096]{1,0:T(8,128)}, f32[128,4096]{1,0:T(8,128)}) custom-call(s32[8]{0:T(128)S(1)} %copy-done.13, s32[2]{0:T(128)S(1)} %pad_add_fusion.place, bf16[128,4096]{1,0:T(8,128)(2,1)S(1)} %copy-done.4, bf16[128,4096]{1,0:T(8,128)(2,1)S(1)} %copy-done.1, bf16[128,4096]{1,0:T(8,128)(2,1)S(1)} %copy-done.3, ...), custom_call_target="tpu_custom_call" | custom-call | flops 671088640 | bytes 9437184 | tf_op jit(solution)/shard_map/grads_within/pallas_call | solution.py:219
  119.3 2.8 %all-to-all-done.3.outgoing = bf16[32,128,128]{2,1,0:T(8,128)(2,1)} async-done(((bf16[32,128,128]{2,1,0:T(8,128)(2,1)}), bf16[32,128,128]{2,1,0:T(8,128)(2,1)}, u32[]{:S(2)}, u32[]{:S(2)}) %all-to-all-start.3) | async-done | bytes 1048608 | tf_op jit(solution)/shard_map/all_to_all | solution.py:264
  122.1 0.0 copy-start.7
  122.1 1.6 %copy-done.7 = f32[128,4096]{1,0:T(8,128)S(1)} copy-done((f32[128,4096]{1,0:T(8,128)S(1)}, f32[128,4096]{1,0:T(8,128)}, u32[]{:S(2)}) %copy-start.7) | copy-done | bytes 2097176
  123.7 6.9 %grads_last.1 = (bf16[128,4096]{1,0:T(8,128)(2,1)}, bf16[128,4096]{1,0:T(8,128)(2,1)}) custom-call(s32[8]{0:T(128)S(1)} %copy-done.13, s32[2]{0:T(128)S(1)} %pad_add_fusion.place, bf16[128,4096]{1,0:T(8,128)(2,1)S(1)} %copy-done.1, bf16[128,4096]{1,0:T(8,128)(2,1)S(1)} %copy-done.3, f32[128,4096]{1,0:T(8,128)S(1)} %copy-done.7, ...), custom_call_target="tpu_custom_call" | custom-call | flops 268435456 | bytes 7340032 | tf_op jit(solution)/shard_map/grads_last/pallas_call | solution.py:219
Async XLA Ops:
  0.7 1.2 copy-start
  1.9 1.2 copy-start.2
  3.2 0.7 copy-start.12
  3.8 22.9 %copy-start.13 = (s32[8]{0:T(128)S(1)}, s32[8]{0:T(128)}, u32[]{:S(2)}) copy-start(s32[8]{0:T(128)} %lens.17) | copy-start | bytes 100
  27.8 17.5 %copy-start.1 = (bf16[128,4096]{1,0:T(8,128)(2,1)S(1)}, bf16[128,4096]{1,0:T(8,128)(2,1)}, u32[]{:S(2)}) copy-start(bf16[128,4096]{1,0:T(8,128)(2,1)} %k.7) | copy-start | bytes 3145732
  27.8 17.5 %copy-start.3 = (bf16[128,4096]{1,0:T(8,128)(2,1)S(1)}, bf16[128,4096]{1,0:T(8,128)(2,1)}, u32[]{:S(2)}) copy-start(bf16[128,4096]{1,0:T(8,128)(2,1)} %v.7) | copy-start | bytes 3145732
  27.9 17.5 %copy-start.4 = (bf16[128,4096]{1,0:T(8,128)(2,1)S(1)}, bf16[128,4096]{1,0:T(8,128)(2,1)}, u32[]{:S(2)}) copy-start(bf16[128,4096]{1,0:T(8,128)(2,1)} %q.5) | copy-start | bytes 3145732
  27.9 8.3 %collective-permute-start.1 = (bf16[4,128,128]{2,1,0:T(8,128)(2,1)S(1)}, bf16[4,128,128]{2,1,0:T(8,128)(2,1)S(1)}, u32[]{:S(2)}, u32[]{:S(2)}) collective-permute-start(bf16[4,128,128]{2,1,0:T(8,128)(2,1)S(1)} %carried_total.1), channel_id=1, source_target_pairs={{0,16},{8,24},{1,17},{9,25},{2,18},{10,26},{3,19},{11,27},{4,20},{... | collective-permute-start | bytes 393224 | tf_op jit(solution)/shard_map/ppermute | solution.py:262
  32.6 6.0 %collective-permute-start = (bf16[4,128,128]{2,1,0:T(8,128)(2,1)S(1)}, bf16[4,128,128]{2,1,0:T(8,128)(2,1)S(1)}, u32[]{:S(2)}, u32[]{:S(2)}) collective-permute-start(bf16[4,128,128]{2,1,0:T(8,128)(2,1)S(1)} %carried_total.1), channel_id=1, source_target_pairs={{0,8},{8,16},{16,24},{1,9},{9,17},{17,25},{2,10},{10,18},{18,26},{... | collective-permute-start | bytes 393224 | tf_op jit(solution)/shard_map/ppermute | solution.py:262
  40.1 1.0 copy-start.6
  41.1 18.7 %all-to-all-start.1 = ((bf16[32,128,128]{2,1,0:T(8,128)(2,1)}), bf16[32,128,128]{2,1,0:T(8,128)(2,1)}, u32[]{:S(2)}, u32[]{:S(2)}) async-start(bf16[32,128,128]{2,1,0:T(8,128)(2,1)} %bitcast.11), calls=%async_computation.1 | async-start | bytes 2097152 | tf_op jit(solution)/shard_map/all_to_all | solution.py:264
  53.0 1.0 copy-start.9
  59.8 1.2 copy-start.8
  68.6 32.4 %copy-start.10 = (bf16[128,4096]{1,0:T(8,128)(2,1)}, bf16[128,4096]{1,0:T(8,128)(2,1)S(1)}, u32[]{:S(2)}) copy-start(bf16[128,4096]{1,0:T(8,128)(2,1)S(1)} %get-tuple-element.16.grad_att) | copy-start | bytes 3145732
  86.9 14.1 %collective-permute-start.3 = (bf16[4,128,128]{2,1,0:T(8,128)(2,1)S(1)}, bf16[4,128,128]{2,1,0:T(8,128)(2,1)S(1)}, u32[]{:S(2)}, u32[]{:S(2)}) collective-permute-start(bf16[4,128,128]{2,1,0:T(8,128)(2,1)S(1)} %future_total.1), channel_id=1, source_target_pairs={{16,0},{24,8},{17,1},{25,9},{18,2},{26,10},{19,3},{27,11},{20,4},{... | collective-permute-start | bytes 393224 | tf_op jit(solution)/shard_map/ppermute | solution.py:262
  88.2 12.8 %collective-permute-start.2 = (bf16[4,128,128]{2,1,0:T(8,128)(2,1)S(1)}, bf16[4,128,128]{2,1,0:T(8,128)(2,1)S(1)}, u32[]{:S(2)}, u32[]{:S(2)}) collective-permute-start(bf16[4,128,128]{2,1,0:T(8,128)(2,1)S(1)} %future_total.1), channel_id=1, source_target_pairs={{8,0},{16,8},{24,16},{9,1},{17,9},{25,17},{10,2},{18,10},{26,18},{... | collective-permute-start | bytes 393224 | tf_op jit(solution)/shard_map/ppermute | solution.py:262
  102.4 1.0 copy-start.5
  103.4 18.7 %all-to-all-start.3 = ((bf16[32,128,128]{2,1,0:T(8,128)(2,1)}), bf16[32,128,128]{2,1,0:T(8,128)(2,1)}, u32[]{:S(2)}, u32[]{:S(2)}) async-start(bf16[32,128,128]{2,1,0:T(8,128)(2,1)} %bitcast.10), calls=%async_computation.3 | async-start | bytes 2097152 | tf_op jit(solution)/shard_map/all_to_all | solution.py:264
  107.7 1.2 copy-start.11
  122.1 1.6 %copy-start.7 = (f32[128,4096]{1,0:T(8,128)S(1)}, f32[128,4096]{1,0:T(8,128)}, u32[]{:S(2)}) copy-start(f32[128,4096]{1,0:T(8,128)} %get-tuple-element.19.gk_part) | copy-start | bytes 6291460

commit v2 on v1

v2 whole, which is shorter than its diff:
```python
import functools

import jax
import jax.numpy as jnp
from jax import lax
from jax.experimental import pallas as pl
from jax.experimental.pallas import tpu as pltpu
from jax.sharding import Mesh, PartitionSpec as P

DH = 128
F32 = jnp.float32
BF16 = jnp.bfloat16
NN = (((1,), (0,)), ((), ()))
NT = (((1,), (1,)), ((), ()))
TN = (((0,), (0,)), ((), ()))
LAYER = ("x", "head")


def mul(a, b, dims):
    return lax.dot_general(a, b, dims, preferred_element_type=F32)


def feature(wide):
    return jnp.where(wide > 0, wide + 1.0, jnp.exp(jnp.minimum(wide, 0.0)))


def slope(wide):
    return jnp.where(wide > 0, 1.0, jnp.exp(jnp.minimum(wide, 0.0)))


def doc_ends(info):
    ends, total = [], 0
    for j in range(2, info.shape[0]):
        total = total + info[j]
        ends.append(total)
    return ends


def doc_at(ends, where):
    found = 0
    for end in ends:
        found = found + jnp.where(where >= end, 1, 0)
    return found


def rows_of(ends, first, count):
    at = first + lax.broadcasted_iota(jnp.int32, (count, 1), 0)
    return doc_at(ends, at)


def columns_of(ends, first, count):
    at = first + lax.broadcasted_iota(jnp.int32, (1, count), 1)
    return doc_at(ends, at)


def visible(ends, first, count):
    later = lax.broadcasted_iota(jnp.int32, (count, count), 0)
    earlier = lax.broadcasted_iota(jnp.int32, (count, count), 1)
    return (later >= earlier) & (
        rows_of(ends, first, count) == columns_of(ends, first, count)
    )


def head_mask(ends, first, count):
    return rows_of(ends, first, count) == doc_at(ends, first)


def tail_mask(ends, first, count):
    return rows_of(ends, first, count) == doc_at(ends, first + count - 1)


def cols(h):
    return slice(h * DH, (h + 1) * DH)


def bunches(heads, size=4):
    return [range(h, min(h + size, heads)) for h in range(0, heads, size)]


def halves(wide):
    high = wide.astype(BF16)
    return jnp.concatenate([high, (wide - high.astype(F32)).astype(BF16)], axis=1)


def row_mean(wide, weights):
    return mul(halves(wide), weights, NN)


def tail_kernel(info, k, v, out):
    count = k.shape[0]
    tail = tail_mask(doc_ends(info), info[0] * count, count)
    for hs in bunches(out.shape[0]):
        fks = [
            jnp.where(tail, feature(k[:, cols(h)].astype(F32)), 0.0).astype(BF16) for h in hs
        ]
        sums = [mul(fk, v[:, cols(h)], TN).astype(BF16) for h, fk in zip(hs, fks)]
        for h, value in zip(hs, sums):
            out[h] = value


def local_kernel(info, q, k, v, scores, part, head_fq, turned):
    count = q.shape[0]
    ends = doc_ends(info)
    first = info[0] * count
    seen = visible(ends, first, count)
    head = head_mask(ends, first, count)
    for hs in bunches(scores.shape[0]):
        wides = [feature(q[:, cols(h)].astype(F32)) for h in hs]
        fks = [feature(k[:, cols(h)].astype(F32)).astype(BF16) for h in hs]
        kept = [
            jnp.where(seen, mul(wide.astype(BF16), fk, NT), 0.0).astype(BF16)
            for wide, fk in zip(wides, fks)
        ]
        parts = [mul(s, v[:, cols(h)], NN) for h, s in zip(hs, kept)]
        heads = [jnp.where(head, wide, 0.0) for wide in wides]
        for h, s, p, f in zip(hs, kept, parts, heads):
            scores[h] = s
            part[:, cols(h)] = p
            head_fq[:, cols(h)] = f.astype(BF16)
            turned[h] = f.T.astype(BF16)


def norm_kernel(info, head_fq, turned, g, part, incoming, out, grad_att, state):
    weights = jnp.full((2 * DH, DH), 1.0 / DH, BF16)
    for hs in bunches(state.shape[0]):
        atts = [part[:, cols(h)] + mul(head_fq[:, cols(h)], incoming[h], NN) for h in hs]
        invs = [lax.rsqrt(row_mean(att * att, weights) + 1e-05) for att in atts]
        norms = [att * inv for att, inv in zip(atts, invs)]
        gos = [g[:, cols(h)].astype(F32) for h in hs]
        means = [row_mean(go * normed, weights) for go, normed in zip(gos, norms)]
        gas = [
            ((go - normed * m) * inv).astype(BF16)
            for go, normed, m, inv in zip(gos, norms, means, invs)
        ]
        sums = [mul(turned[h], ga, NN).astype(BF16) for h, ga in zip(hs, gas)]
        for h, normed, ga, value in zip(hs, norms, gas, sums):
            out[:, cols(h)] = normed.astype(BF16)
            grad_att[:, cols(h)] = ga
            state[h] = value


def inner_kernel(info, q, k, v, grad_att, incoming, scores, gq, gk, gv):
    count = q.shape[0]
    ends = doc_ends(info)
    first = info[0] * count
    seen = visible(ends, first, count)
    head = head_mask(ends, first, count)
    for hs in bunches(scores.shape[0]):
        wides = [q[:, cols(h)].astype(F32) for h in hs]
        fqs = [feature(wide).astype(BF16) for wide in wides]
        fks = [feature(k[:, cols(h)].astype(F32)).astype(BF16) for h in hs]
        gas = [grad_att[:, cols(h)] for h in hs]
        gss = [
            jnp.where(seen, mul(ga, v[:, cols(h)], NT), 0.0).astype(BF16)
            for h, ga in zip(hs, gas)
        ]
        totals = [
            mul(gs, fk, NN) + jnp.where(head, mul(ga, incoming[h], NT), 0.0)
            for h, gs, fk, ga in zip(hs, gss, fks, gas)
        ]
        gks = [mul(gs, fq, TN) for gs, fq in zip(gss, fqs)]
        gvs = [mul(scores[h], ga, TN) for h, ga in zip(hs, gas)]
        for h, total, wide, a, b in zip(hs, totals, wides, gks, gvs):
            gq[:, cols(h)] = (total * slope(wide)).astype(BF16)
            gk[:, cols(h)] = a
            gv[:, cols(h)] = b


def last_kernel(info, k, v, gk_part, gv_part, outgoing, gk, gv):
    count = k.shape[0]
    tail = tail_mask(doc_ends(info), info[0] * count, count)
    for hs in bunches(outgoing.shape[0]):
        wides = [k[:, cols(h)].astype(F32) for h in hs]
        fks = [jnp.where(tail, feature(wide), 0.0).astype(BF16) for wide in wides]
        vts = [jnp.where(tail, v[:, cols(h)].astype(F32), 0.0).astype(BF16) for h in hs]
        gks = [gk_part[:, cols(h)] + mul(vt, outgoing[h], NT) for h, vt in zip(hs, vts)]
        gvs = [gv_part[:, cols(h)] + mul(fk, outgoing[h], NN) for h, fk in zip(hs, fks)]
        for h, a, wide, b in zip(hs, gks, wides, gvs):
            gk[:, cols(h)] = (a * slope(wide)).astype(BF16)
            gv[:, cols(h)] = b.astype(BF16)


def same(a, b):
    return jnp.where(a == b, 1.0, 0.0).astype(F32)


def total_kernel(forward, count, info, held, total):
    members = held.shape[0]
    ends = doc_ends(info)
    layer = info[1] * (members * count)
    carry = None
    for step in range(members):
        i = step if forward else members - 1 - step
        mine = held[i].astype(F32)
        edge = layer + ((i + 1) * count - 1 if forward else i * count)
        here = doc_at(ends, edge)
        if carry is not None:
            mine = mine + carry * same(here, previous)
        carry, previous = mine, here
    total[...] = carry.astype(BF16)


def prefix_kernel(forward, count, info, held, *rest):
    others, out = rest[:-1], rest[-1]
    members = held.shape[0]
    span = members * count
    ends = doc_ends(info)
    layer = info[1] * span
    sign = -1 if forward else 1
    previous = doc_at(ends, layer - 1 if forward else layer + span)
    carry = None
    for s, other in enumerate(others):
        far = layer + sign * s * span
        there = doc_at(ends, far - 1 if forward else far + span)
        term = other[...].astype(F32) * same(there, previous)
        carry = term if carry is None else carry + term
    for step in range(members):
        i = step if forward else members - 1 - step
        near, far = layer + i * count, layer + (i + 1) * count - 1
        if not forward:
            near, far = far, near
        if carry is None:
            out[i] = jnp.zeros(out.shape[1:], BF16)
        else:
            out[i] = (carry * same(doc_at(ends, near), previous)).astype(BF16)
        if step < members - 1:
            here = doc_at(ends, far)
            mine = held[i].astype(F32)
            if carry is not None:
                mine = mine + carry * same(here, previous)
            carry, previous = mine, here


SMEM = pl.BlockSpec(memory_space=pltpu.SMEM)
PARAMS = pltpu.CompilerParams(dimension_semantics=("arbitrary",))


def local(queries, keys, values, out_grad, doc_lengths):
    count, width = queries.shape
    heads = width // DH
    layers = lax.axis_size("z")
    members = lax.axis_size("x") * lax.axis_size("head")
    owned = heads // members
    place = jnp.stack([lax.axis_index(("z", "x", "head")), lax.axis_index("z")])
    info = jnp.concatenate([place.astype(jnp.int32), doc_lengths])
    block_heads = 8 if heads % 8 == 0 else 1
    steps = heads // block_heads
    tokens = pl.BlockSpec((count, block_heads * DH), lambda i: (0, i))
    states = pl.BlockSpec((block_heads, DH, DH), lambda i: (i, 0, 0))
    tiles = pl.BlockSpec((block_heads, count, count), lambda i: (i, 0, 0))
    token_bf = jax.ShapeDtypeStruct((count, width), BF16)
    token_f32 = jax.ShapeDtypeStruct((count, width), F32)
    state_bf = jax.ShapeDtypeStruct((heads, DH, DH), BF16)
    tile_bf = jax.ShapeDtypeStruct((heads, count, count), BF16)

    def run(kernel, ins, outs, shapes, args, products, name):
        return pl.pallas_call(
            kernel,
            grid=(steps,),
            in_specs=[SMEM] + ins,
            out_specs=outs,
            out_shape=shapes,
            compiler_params=PARAMS,
            cost_estimate=pl.CostEstimate(
                flops=2 * products * heads * count * DH * DH,
                bytes_accessed=2 * (len(ins) + len(outs)) * count * width,
                transcendentals=count * width,
            ),
            name=name,
        )(info, *args)

    def combine(kernel, args, many, forward, name):
        group = pl.BlockSpec((members, None, DH, DH), lambda i: (0, i, 0, 0))
        single = pl.BlockSpec((None, DH, DH), lambda i: (i, 0, 0))
        return pl.pallas_call(
            functools.partial(kernel, forward, count),
            grid=(owned,),
            in_specs=[SMEM, group] + [single] * (len(args) - 1),
            out_specs=group if many else single,
            out_shape=jax.ShapeDtypeStruct(
                ((members,) if many else ()) + (owned, DH, DH), BF16
            ),
            compiler_params=PARAMS,
            cost_estimate=pl.CostEstimate(
                flops=4 * heads * DH * DH,
                bytes_accessed=4 * heads * DH * DH,
                transcendentals=0,
            ),
            name=name,
        )(info, *args)

    def scan(state, forward, name):
        held = lax.all_to_all(state, LAYER, split_axis=0, concat_axis=0, tiled=True)
        held = held.reshape(members, owned, DH, DH)
        others = []
        if layers > 1:
            total = combine(total_kernel, (held,), False, forward, name + "_total")
            for s in range(1, min(layers - 1, -(-layers // 2)) + 1):
                pairs = [(i, i + s) if forward else (i + s, i) for i in range(layers - s)]
                others.append(lax.ppermute(total, "z", pairs))
        sums = combine(prefix_kernel, (held, *others), True, forward, name + "_prefix")
        return lax.all_to_all(
            sums.reshape(heads, DH, DH), LAYER, split_axis=0, concat_axis=0, tiled=True
        )

    (tail,) = run(tail_kernel, [tokens] * 2, [states], [state_bf], (keys, values), 1, "tail")
    incoming = scan(tail, True, "carried")
    turned_bf = jax.ShapeDtypeStruct((heads, DH, count), BF16)
    turns = pl.BlockSpec((block_heads, DH, count), lambda i: (i, 0, 0))
    scores, part, head_fq, turned = run(
        local_kernel,
        [tokens] * 3,
        [tiles, tokens, tokens, turns],
        [tile_bf, token_f32, token_bf, turned_bf],
        (queries, keys, values),
        2,
        "within",
    )
    attn_out, grad_att, head_state = run(
        norm_kernel,
        [tokens, turns, tokens, tokens, states],
        [tokens, tokens, states],
        [token_bf, token_bf, state_bf],
        (head_fq, turned, out_grad, part, incoming),
        2,
        "normed",
    )
    outgoing = scan(head_state, False, "future")
    grad_queries, gk_part, gv_part = run(
        inner_kernel,
        [tokens] * 4 + [states, tiles],
        [tokens] * 3,
        [token_bf, token_f32, token_f32],
        (queries, keys, values, grad_att, incoming, scores),
        5,
        "grads_within",
    )
    grad_keys, grad_values = run(
        last_kernel,
        [tokens] * 4 + [states],
        [tokens] * 2,
        [token_bf, token_bf],
        (keys, values, gk_part, gv_part, outgoing),
        2,
        "grads_last",
    )
    return attn_out, grad_queries, grad_keys, grad_values


def solution(mesh):
    n_seq, n_head = mesh.shape["seq"], mesh.shape["head"]
    inner = next(n for n in (4, 2, 1) if n_seq % n == 0)
    fine = Mesh(mesh.devices.reshape(n_seq // inner, inner, n_head), ("z", "x", "head"))
    rows = P(("z", "x", "head"), None)
    return jax.shard_map(
        local,
        mesh=fine,
        in_specs=(rows, rows, rows, rows, P()),
        out_specs=(rows, rows, rows, rows),
        check_vma=False,
    )
```

time: 132 us -> 130 us (0.985)
  local copies, waits for them, and re-layouts: 10.1 us -> 3.18 us
  blocking collectives: 36.7 us -> 43.1 us
  starting transfers between devices: 19.3 us -> 13.1 us
  waiting for transfers between devices: 22.6 us -> 28.8 us
  Pallas kernels: 40.9 us -> 38.5 us
    all_to_all x2, waiting for transfers between devices: 8.67 us -> 20 us  [scan(): lax.all_to_all(sums.reshape(heads, DH, DH), LAYER, split_axis=0, concat_a...]
    unnamed x28 -> x8, local copies, waits for them, and re-layouts: 10.1 us -> 3.18 us
    all_to_all x2, blocking collectives: 36.7 us -> 43.1 us  [scan(): held = lax.all_to_all(state, LAYER, split_axis=0, concat_axis=0, tiled=True)]
    pallas_call x5, Pallas kernels: 35.8 us -> 29.5 us  [run(): pl.pallas_call(kernel, grid=(steps,), in_specs=[SMEM] + ins, out_specs=ou...]
    ppermute x4 -> x2, waiting for transfers between devices: 14 us -> 8.82 us  [scan(): others.append(lax.ppermute(total, 'z', pairs))]
    ppermute x4 -> x2, starting transfers between devices: 10.8 us -> 5.76 us  [scan(): others.append(lax.ppermute(total, 'z', pairs))]
    pallas_call x4, Pallas kernels: 5.17 us -> 9.08 us  [combine(): pl.pallas_call(functools.partial(kernel, forward, count), grid=(owned,),...]
    concatenate x0 -> x1, other arithmetic: none -> 1.32 us  [local(): info = jnp.concatenate([place.astype(jnp.int32), doc_lengths])]
  transfers between devices with their start and end apart: 6 -> 4, of which waited for: 4 -> 4; matrix products, arithmetic and copies ran while one was open for 0% -> 0% of each run, Pallas kernels for 14% -> 10%
where the time goes in v2:
time: 130 us; the launch traced here: 129 us
  blocking collectives  43.1 us (33%)
  Pallas kernels  38.5 us (30%)
  waiting for transfers between devices  28.8 us (22%)
  starting transfers between devices  13.1 us (10%)
  local copies, waits for them, and re-layouts  3.18 us (2%)
  other arithmetic  1.32 us (1%)
    all_to_all x2, blocking collectives, scan(): held = lax.all_to_all(state, LAYER, split_axis=0, concat_axis=0, tiled=True)  43.1 us
    pallas_call x5, Pallas kernels, run(): pl.pallas_call(kernel, grid=(steps,), in_specs=[SMEM] + ins, out_specs=ou...  29.5 us
    all_to_all x2, waiting for transfers between devices, scan(): lax.all_to_all(sums.reshape(heads, DH, DH), LAYER, split_axis=0, concat_a...  20 us
    pallas_call x4, Pallas kernels, combine(): pl.pallas_call(functools.partial(kernel, forward, count), grid=(owned,),...  9.08 us
    ppermute x2, waiting for transfers between devices, scan(): others.append(lax.ppermute(total, 'z', pairs))  8.82 us
    all_to_all x2, starting transfers between devices, scan(): lax.all_to_all(sums.reshape(heads, DH, DH), LAYER, split_axis=0, concat_a...  7.31 us
    ppermute x2, starting transfers between devices, scan(): others.append(lax.ppermute(total, 'z', pairs))  5.76 us
    unnamed x8, local copies, waits for them, and re-layouts  3.18 us
  transfers between devices with their start and end apart: 4, of which 4 were waited for; matrix products, arithmetic and copies ran while one was open for 0% of the time, Pallas kernels for 10%

profile of v2, /device:TPU:0, one launch (start us, length us, event | category | flops | bytes accessed | tf_op | source)
XLA Modules:
  0.0 128.6 jit_solution(8175783568473159758)
XLA Ops:
  0.6 1.3 %pad_add_fusion.info = s32[10]{0:T(128)} fusion(s32[8]{0:T(128)} %param.9, s32[1]{0:T(128)} %bitcast.1, s32[1]{0:T(128)} %bitcast), kind=kLoop, calls=%fused_computation | loop fusion | flops 20 | bytes 80 | tf_op jit(solution)/shard_map/concatenate | solution.py:245
  2.0 4.3 %tail.1 = bf16[32,128,128]{2,1,0:T(8,128)(2,1)} custom-call(s32[10]{0:T(128)} %pad_add_fusion.info, bf16[128,4096]{1,0:T(8,128)(2,1)} %k.7, bf16[128,4096]{1,0:T(8,128)(2,1)} %v.7), custom_call_target="tpu_custom_call" | custom-call | flops 134217728 | bytes 3145728 | tf_op jit(solution)/shard_map/tail/pallas_call | solution.py:257
  6.3 22.6 %all_to_all.20 = bf16[32,128,128]{2,1,0:T(8,128)(2,1)} all-to-all(bf16[32,128,128]{2,1,0:T(8,128)(2,1)} %tail.1), channel_id=1, replica_groups=mesh['z'=2,'x'=4,'head'=4] {'x','head'}, dimensions={0} | all-to-all | bytes 2097152 | tf_op jit(solution)/shard_map/all_to_all | solution.py:293
  28.9 2.0 %carried_total.1 = bf16[2,128,128]{2,1,0:T(8,128)(2,1)} custom-call(s32[10]{0:T(128)} %pad_add_fusion.info, bf16[16,2,128,128]{3,2,1,0:T(8,128)(2,1)} %bitcast.6), custom_call_target="tpu_custom_call" | custom-call | flops 2097152 | bytes 2097152 | tf_op jit(solution)/shard_map/carried_total/pallas_call | solution.py:275
  30.9 4.5 %collective-permute-start = (bf16[2,128,128]{2,1,0:T(8,128)(2,1)}, bf16[2,128,128]{2,1,0:T(8,128)(2,1)S(1)}, u32[]{:S(2)}, u32[]{:S(2)}) collective-permute-start(bf16[2,128,128]{2,1,0:T(8,128)(2,1)} %carried_total.1), channel_id=1, source_target_pairs={{0,16},{1,17},{2,18},{3,19},{4,20},{5,21},{6,22},{7,23},{8,24},{9,... | collective-permute-start | bytes 196616 | tf_op jit(solution)/shard_map/ppermute | solution.py:300
  35.4 2.2 %collective-permute-done.rest_0_ = bf16[2,128,128]{2,1,0:T(8,128)(2,1)S(1)} collective-permute-done((bf16[2,128,128]{2,1,0:T(8,128)(2,1)}, bf16[2,128,128]{2,1,0:T(8,128)(2,1)S(1)}, u32[]{:S(2)}, u32[]{:S(2)}) %collective-permute-start) | collective-permute-done | bytes 65568 | tf_op jit(solution)/shard_map/ppermute | solution.py:300
  37.6 0.0 copy-start.2
  37.6 0.6 copy-done.2
  38.2 2.5 %carried_prefix.1 = bf16[16,2,128,128]{3,2,1,0:T(8,128)(2,1)} custom-call(s32[10]{0:T(128)} %pad_add_fusion.info, bf16[16,2,128,128]{3,2,1,0:T(8,128)(2,1)} %bitcast.7, bf16[2,128,128]{2,1,0:T(8,128)(2,1)} %copy-done.2), custom_call_target="tpu_custom_call" | custom-call | flops 2097152 | bytes 2097152 | tf_op jit(solution)/shard_map/carried_prefix/pallas_call | solution.py:275
  40.7 3.7 %all-to-all-start.1 = ((bf16[32,128,128]{2,1,0:T(8,128)(2,1)}), bf16[32,128,128]{2,1,0:T(8,128)(2,1)S(1)}, u32[]{:S(2)}, u32[]{:S(2)}) async-start(bf16[32,128,128]{2,1,0:T(8,128)(2,1)} %bitcast.11), calls=%async_computation.1 | async-start | bytes 2097152 | tf_op jit(solution)/shard_map/all_to_all | solution.py:302
  44.4 5.6 %within.1 = (bf16[32,128,128]{2,1,0:T(8,128)(2,1)}, f32[128,4096]{1,0:T(8,128)}, bf16[128,4096]{1,0:T(8,128)(2,1)}, bf16[32,128,128]{2,1,0:T(8,128)(2,1)}) custom-call(s32[10]{0:T(128)} %pad_add_fusion.info, bf16[128,4096]{1,0:T(8,128)(2,1)} %q.3, bf16[128,4096]{1,0:T(8,128)(2,1)} %k.7, bf16[128,4096]{1,0:T(8,128)(2,1)} %v.7), custom_call_target="tpu_custom_call" | custom-call | flops 268435456 | bytes 7340032 | tf_op jit(solution)/shard_map/within/pallas_call | solution.py:257
  49.9 10.6 %all-to-all-done.1.incoming = bf16[32,128,128]{2,1,0:T(8,128)(2,1)S(1)} async-done(((bf16[32,128,128]{2,1,0:T(8,128)(2,1)}), bf16[32,128,128]{2,1,0:T(8,128)(2,1)S(1)}, u32[]{:S(2)}, u32[]{:S(2)}) %all-to-all-start.1) | async-done | bytes 1048608 | tf_op jit(solution)/shard_map/all_to_all | solution.py:302
  60.6 0.0 copy-start
  60.6 1.0 copy-done
  61.5 7.2 %normed.1 = (bf16[128,4096]{1,0:T(8,128)(2,1)}, bf16[128,4096]{1,0:T(8,128)(2,1)}, bf16[32,128,128]{2,1,0:T(8,128)(2,1)}) custom-call(s32[10]{0:T(128)} %pad_add_fusion.info, bf16[128,4096]{1,0:T(8,128)(2,1)} %get-tuple-element.16.head_fq, bf16[32,128,128]{2,1,0:T(8,128)(2,1)} %get-tuple-element.17.turned, bf16[128,4096]{1,0:T(8,128)(2,1)} %g.1, ...), custom_call_target="tpu_custom_call" | custom-call | flops 268435456 | bytes 8388608 | tf_op jit(solution)/shard_map/normed/pallas_call | solution.py:257
  68.8 20.5 %all_to_all.21 = bf16[32,128,128]{2,1,0:T(8,128)(2,1)} all-to-all(bf16[32,128,128]{2,1,0:T(8,128)(2,1)} %get-tuple-element.25), channel_id=1, replica_groups=mesh['z'=2,'x'=4,'head'=4] {'x','head'}, dimensions={0} | all-to-all | bytes 2097152 | tf_op jit(solution)/shard_map/all_to_all | solution.py:293
  89.3 2.0 %future_total.1 = bf16[2,128,128]{2,1,0:T(8,128)(2,1)} custom-call(s32[10]{0:T(128)} %pad_add_fusion.info, bf16[16,2,128,128]{3,2,1,0:T(8,128)(2,1)} %bitcast.8), custom_call_target="tpu_custom_call" | custom-call | flops 2097152 | bytes 2097152 | tf_op jit(solution)/shard_map/future_total/pallas_call | solution.py:275
  91.3 1.3 collective-permute-start.1
  92.6 6.6 %collective-permute-done.1.rest_0_ = bf16[2,128,128]{2,1,0:T(8,128)(2,1)S(1)} collective-permute-done((bf16[2,128,128]{2,1,0:T(8,128)(2,1)}, bf16[2,128,128]{2,1,0:T(8,128)(2,1)S(1)}, u32[]{:S(2)}, u32[]{:S(2)}) %collective-permute-start.1) | collective-permute-done | bytes 65568 | tf_op jit(solution)/shard_map/ppermute | solution.py:300
  99.2 0.0 copy-start.3
  99.2 0.6 copy-done.3
  99.8 2.5 %future_prefix.1 = bf16[16,2,128,128]{3,2,1,0:T(8,128)(2,1)} custom-call(s32[10]{0:T(128)} %pad_add_fusion.info, bf16[16,2,128,128]{3,2,1,0:T(8,128)(2,1)} %bitcast.9, bf16[2,128,128]{2,1,0:T(8,128)(2,1)} %copy-done.3), custom_call_target="tpu_custom_call" | custom-call | flops 2097152 | bytes 2097152 | tf_op jit(solution)/shard_map/future_prefix/pallas_call | solution.py:275
  102.3 3.7 %all-to-all-start.3 = ((bf16[32,128,128]{2,1,0:T(8,128)(2,1)}), bf16[32,128,128]{2,1,0:T(8,128)(2,1)S(1)}, u32[]{:S(2)}, u32[]{:S(2)}) async-start(bf16[32,128,128]{2,1,0:T(8,128)(2,1)} %bitcast.10), calls=%async_computation.3 | async-start | bytes 2097152 | tf_op jit(solution)/shard_map/all_to_all | solution.py:302
  106.0 6.9 %grads_within.1 = (bf16[128,4096]{1,0:T(8,128)(2,1)}, f32[128,4096]{1,0:T(8,128)}, f32[128,4096]{1,0:T(8,128)}) custom-call(s32[10]{0:T(128)} %pad_add_fusion.info, bf16[128,4096]{1,0:T(8,128)(2,1)} %q.3, bf16[128,4096]{1,0:T(8,128)(2,1)} %k.7, bf16[128,4096]{1,0:T(8,128)(2,1)} %v.7, bf16[128,4096]{1,0:T(8,128)(2,1)} %get-tuple-element.20.grad_att, ...), custom_call_target="tpu_custom_call" | custom-call | flops 671088640 | bytes 9437184 | tf_op jit(solution)/shard_map/grads_within/pallas_call | solution.py:257
  112.9 9.3 %all-to-all-done.3.outgoing = bf16[32,128,128]{2,1,0:T(8,128)(2,1)S(1)} async-done(((bf16[32,128,128]{2,1,0:T(8,128)(2,1)}), bf16[32,128,128]{2,1,0:T(8,128)(2,1)S(1)}, u32[]{:S(2)}, u32[]{:S(2)}) %all-to-all-start.3) | async-done | bytes 1048608 | tf_op jit(solution)/shard_map/all_to_all | solution.py:302
  122.2 0.0 copy-start.1
  122.2 1.0 copy-done.1
  123.2 5.5 %grads_last.1 = (bf16[128,4096]{1,0:T(8,128)(2,1)}, bf16[128,4096]{1,0:T(8,128)(2,1)}) custom-call(s32[10]{0:T(128)} %pad_add_fusion.info, bf16[128,4096]{1,0:T(8,128)(2,1)} %k.7, bf16[128,4096]{1,0:T(8,128)(2,1)} %v.7, f32[128,4096]{1,0:T(8,128)} %get-tuple-element.23.gk_part, f32[128,4096]{1,0:T(8,128)} %get-tuple-element.24.gv_part, ...), custom_call_target="tpu_custom_call" | custom-call | flops 268435456 | bytes 7340032 | tf_op jit(solution)/shard_map/grads_last/pallas_call | solution.py:257
Async XLA Ops:
  30.9 6.7 %collective-permute-start = (bf16[2,128,128]{2,1,0:T(8,128)(2,1)}, bf16[2,128,128]{2,1,0:T(8,128)(2,1)S(1)}, u32[]{:S(2)}, u32[]{:S(2)}) collective-permute-start(bf16[2,128,128]{2,1,0:T(8,128)(2,1)} %carried_total.1), channel_id=1, source_target_pairs={{0,16},{1,17},{2,18},{3,19},{4,20},{5,21},{6,22},{7,23},{8,24},{9,... | collective-permute-start | bytes 196616 | tf_op jit(solution)/shard_map/ppermute | solution.py:300
  37.6 0.6 copy-start.2
  40.7 19.9 %all-to-all-start.1 = ((bf16[32,128,128]{2,1,0:T(8,128)(2,1)}), bf16[32,128,128]{2,1,0:T(8,128)(2,1)S(1)}, u32[]{:S(2)}, u32[]{:S(2)}) async-start(bf16[32,128,128]{2,1,0:T(8,128)(2,1)} %bitcast.11), calls=%async_computation.1 | async-start | bytes 2097152 | tf_op jit(solution)/shard_map/all_to_all | solution.py:302
  60.6 1.0 copy-start
  91.3 7.9 %collective-permute-start.1 = (bf16[2,128,128]{2,1,0:T(8,128)(2,1)}, bf16[2,128,128]{2,1,0:T(8,128)(2,1)S(1)}, u32[]{:S(2)}, u32[]{:S(2)}) collective-permute-start(bf16[2,128,128]{2,1,0:T(8,128)(2,1)} %future_total.1), channel_id=1, source_target_pairs={{16,0},{17,1},{18,2},{19,3},{20,4},{21,5},{22,6},{23,7},{24,8},{25... | collective-permute-start | bytes 196616 | tf_op jit(solution)/shard_map/ppermute | solution.py:300
  99.2 0.6 copy-start.3
  102.3 19.9 %all-to-all-start.3 = ((bf16[32,128,128]{2,1,0:T(8,128)(2,1)}), bf16[32,128,128]{2,1,0:T(8,128)(2,1)S(1)}, u32[]{:S(2)}, u32[]{:S(2)}) async-start(bf16[32,128,128]{2,1,0:T(8,128)(2,1)} %bitcast.10), calls=%async_computation.3 | async-start | bytes 2097152 | tf_op jit(solution)/shard_map/all_to_all | solution.py:302
  122.2 1.0 copy-start.1

commit v3 on v2

--- a/solution.py
+++ b/solution.py
@@ -28,10 +28,10 @@
     return jnp.where(wide > 0, 1.0, jnp.exp(jnp.minimum(wide, 0.0)))
 
 
-def doc_ends(info):
+def doc_ends(lens):
     ends, total = [], 0
-    for j in range(2, info.shape[0]):
-        total = total + info[j]
+    for j in range(lens.shape[0]):
+        total = total + lens[j]
         ends.append(total)
     return ends
 
@@ -77,18 +77,13 @@
     return [range(h, min(h + size, heads)) for h in range(0, heads, size)]
 
 
-def halves(wide):
-    high = wide.astype(BF16)
-    return jnp.concatenate([high, (wide - high.astype(F32)).astype(BF16)], axis=1)
-
-
 def row_mean(wide, weights):
-    return mul(halves(wide), weights, NN)
-
-
-def tail_kernel(info, k, v, out):
+    return mul(wide.astype(BF16), weights, NN)
+
+
+def tail_kernel(lens, place, k, v, out):
     count = k.shape[0]
-    tail = tail_mask(doc_ends(info), info[0] * count, count)
+    tail = tail_mask(doc_ends(lens), place[0] * count, count)
     for hs in bunches(out.shape[0]):
         fks = [
             jnp.where(tail, feature(k[:, cols(h)].astype(F32)), 0.0).astype(BF16) for h in hs
@@ -98,10 +93,10 @@
             out[h] = value
 
 
-def local_kernel(info, q, k, v, scores, part, head_fq, turned):
+def local_kernel(lens, place, q, k, v, scores, part, head_fq, turned):
     count = q.shape[0]
-    ends = doc_ends(info)
-    first = info[0] * count
+    ends = doc_ends(lens)
+    first = place[0] * count
     seen = visible(ends, first, count)
     head = head_mask(ends, first, count)
     for hs in bunches(scores.shape[0]):
@@ -120,8 +115,8 @@
             turned[h] = f.T.astype(BF16)
 
 
-def norm_kernel(info, head_fq, turned, g, part, incoming, out, grad_att, state):
-    weights = jnp.full((2 * DH, DH), 1.0 / DH, BF16)
+def norm_kernel(lens, place, head_fq, turned, g, part, incoming, out, grad_att, state):
+    weights = jnp.full((DH, DH), 1.0 / DH, BF16)
     for hs in bunches(state.shape[0]):
         atts = [part[:, cols(h)] + mul(head_fq[:, cols(h)], incoming[h], NN) for h in hs]
         invs = [lax.rsqrt(row_mean(att * att, weights) + 1e-05) for att in atts]
@@ -139,10 +134,10 @@
             state[h] = value
 
 
-def inner_kernel(info, q, k, v, grad_att, incoming, scores, gq, gk, gv):
+def inner_kernel(lens, place, q, k, v, grad_att, incoming, scores, gq, gk, gv):
     count = q.shape[0]
-    ends = doc_ends(info)
-    first = info[0] * count
+    ends = doc_ends(lens)
+    first = place[0] * count
     seen = visible(ends, first, count)
     head = head_mask(ends, first, count)
     for hs in bunches(scores.shape[0]):
@@ -166,9 +161,9 @@
             gv[:, cols(h)] = b
 
 
-def last_kernel(info, k, v, gk_part, gv_part, outgoing, gk, gv):
+def last_kernel(lens, place, k, v, gk_part, gv_part, outgoing, gk, gv):
     count = k.shape[0]
-    tail = tail_mask(doc_ends(info), info[0] * count, count)
+    tail = tail_mask(doc_ends(lens), place[0] * count, count)
     for hs in bunches(outgoing.shape[0]):
         wides = [k[:, cols(h)].astype(F32) for h in hs]
         fks = [jnp.where(tail, feature(wide), 0.0).astype(BF16) for wide in wides]
@@ -184,10 +179,10 @@
     return jnp.where(a == b, 1.0, 0.0).astype(F32)
 
 
-def total_kernel(forward, count, info, held, total):
+def total_kernel(forward, count, lens, place, held, total):
     members = held.shape[0]
-    ends = doc_ends(info)
-    layer = info[1] * (members * count)
+    ends = doc_ends(lens)
+    layer = place[1] * (members * count)
     carry = None
     for step in range(members):
         i = step if forward else members - 1 - step
@@ -200,12 +195,12 @@
     total[...] = carry.astype(BF16)
 
 
-def prefix_kernel(forward, count, info, held, *rest):
+def prefix_kernel(forward, count, lens, place, held, *rest):
     others, out = rest[:-1], rest[-1]
     members = held.shape[0]
     span = members * count
-    ends = doc_ends(info)
-    layer = info[1] * span
+    ends = doc_ends(lens)
+    layer = place[1] * span
     sign = -1 if forward else 1
     previous = doc_at(ends, layer - 1 if forward else layer + span)
     carry = None
@@ -232,7 +227,12 @@
 
 
 SMEM = pl.BlockSpec(memory_space=pltpu.SMEM)
-PARAMS = pltpu.CompilerParams(dimension_semantics=("arbitrary",))
+SMALL = pltpu.CompilerParams(
+    dimension_semantics=("arbitrary",), vmem_limit_bytes=16 * 1024 * 1024
+)
+LARGE = pltpu.CompilerParams(
+    dimension_semantics=("arbitrary",), vmem_limit_bytes=60 * 1024 * 1024
+)
 
 
 def local(queries, keys, values, out_grad, doc_lengths):
@@ -241,8 +241,9 @@
     layers = lax.axis_size("z")
     members = lax.axis_size("x") * lax.axis_size("head")
     owned = heads // members
-    place = jnp.stack([lax.axis_index(("z", "x", "head")), lax.axis_index("z")])
-    info = jnp.concatenate([place.astype(jnp.int32), doc_lengths])
+    place = jnp.stack(
+        [lax.axis_index(("z", "x", "head")), lax.axis_index("z")]
+    ).astype(jnp.int32)
     block_heads = 8 if heads % 8 == 0 else 1
     steps = heads // block_heads
     tokens = pl.BlockSpec((count, block_heads * DH), lambda i: (0, i))
@@ -253,21 +254,21 @@
     state_bf = jax.ShapeDtypeStruct((heads, DH, DH), BF16)
     tile_bf = jax.ShapeDtypeStruct((heads, count, count), BF16)
 
-    def run(kernel, ins, outs, shapes, args, products, name):
+    def run(kernel, ins, outs, shapes, args, products, name, params=SMALL):
         return pl.pallas_call(
             kernel,
             grid=(steps,),
-            in_specs=[SMEM] + ins,
+            in_specs=[SMEM, SMEM] + ins,
             out_specs=outs,
             out_shape=shapes,
-            compiler_params=PARAMS,
+            compiler_params=params,
             cost_estimate=pl.CostEstimate(
                 flops=2 * products * heads * count * DH * DH,
                 bytes_accessed=2 * (len(ins) + len(outs)) * count * width,
                 transcendentals=count * width,
             ),
             name=name,
-        )(info, *args)
+        )(doc_lengths, place, *args)
 
     def combine(kernel, args, many, forward, name):
         group = pl.BlockSpec((members, None, DH, DH), lambda i: (0, i, 0, 0))
@@ -275,19 +276,19 @@
         return pl.pallas_call(
             functools.partial(kernel, forward, count),
             grid=(owned,),
-            in_specs=[SMEM, group] + [single] * (len(args) - 1),
+            in_specs=[SMEM, SMEM, group] + [single] * (len(args) - 1),
             out_specs=group if many else single,
             out_shape=jax.ShapeDtypeStruct(
                 ((members,) if many else ()) + (owned, DH, DH), BF16
             ),
-            compiler_params=PARAMS,
+            compiler_params=SMALL,
             cost_estimate=pl.CostEstimate(
                 flops=4 * heads * DH * DH,
                 bytes_accessed=4 * heads * DH * DH,
                 transcendentals=0,
             ),
             name=name,
-        )(info, *args)
+        )(doc_lengths, place, *args)
 
     def scan(state, forward, name):
         held = lax.all_to_all(state, LAYER, split_axis=0, concat_axis=0, tiled=True)
@@ -303,7 +304,7 @@
             sums.reshape(heads, DH, DH), LAYER, split_axis=0, concat_axis=0, tiled=True
         )
 
-    (tail,) = run(tail_kernel, [tokens] * 2, [states], [state_bf], (keys, values), 1, "tail")
+    (tail,) = run(tail_kernel, [tokens] * 2, [states], [state_bf], (keys, values), 1, "tail", LARGE)
     incoming = scan(tail, True, "carried")
     turned_bf = jax.ShapeDtypeStruct((heads, DH, count), BF16)
     turns = pl.BlockSpec((block_heads, DH, count), lambda i: (i, 0, 0))
@@ -349,7 +350,7 @@
 
 def solution(mesh):
     n_seq, n_head = mesh.shape["seq"], mesh.shape["head"]
-    inner = next(n for n in (4, 2, 1) if n_seq % n == 0)
+    inner = next(n for n in (2, 1) if n_seq % n == 0)
     fine = Mesh(mesh.devices.reshape(n_seq // inner, inner, n_head), ("z", "x", "head"))
     rows = P(("z", "x", "head"), None)
     return jax.shard_map(

time: 130 us -> 131 us (level)
  local copies, waits for them, and re-layouts: 3.18 us -> 22.3 us
  Pallas kernels: 38.5 us -> 28.1 us
  waiting for transfers between devices: 28.8 us -> 22.5 us
  blocking collectives: 43.1 us -> 36.9 us
  starting transfers between devices: 13.1 us -> 18.5 us
    unnamed x8 -> x46, local copies, waits for them, and re-layouts: 3.18 us -> 22.3 us
    all_to_all x2, waiting for transfers between devices: 20 us -> 8.54 us  [scan(): lax.all_to_all(sums.reshape(heads, DH, DH), LAYER, split_axis=0, concat_a...]
    pallas_call x5, Pallas kernels: 29.5 us -> 22.9 us  [run(): pl.pallas_call(kernel, grid=(steps,), in_specs=[SMEM, SMEM] + ins, out_sp...]
    all_to_all x2, blocking collectives: 43.1 us -> 36.9 us  [scan(): held = lax.all_to_all(state, LAYER, split_axis=0, concat_axis=0, tiled=True)]
    ppermute x2 -> x4, waiting for transfers between devices: 8.82 us -> 14 us  [scan(): others.append(lax.ppermute(total, 'z', pairs))]
    ppermute x2 -> x4, starting transfers between devices: 5.76 us -> 10.7 us  [scan(): others.append(lax.ppermute(total, 'z', pairs))]
    pallas_call x4, Pallas kernels: 9.08 us -> 5.17 us  [combine(): pl.pallas_call(functools.partial(kernel, forward, count), grid=(owned,),...]
    concatenate x1 -> x0, other arithmetic: 1.32 us -> none  [local(): info = jnp.concatenate([place.astype(jnp.int32), doc_lengths])]
  transfers between devices with their start and end apart: 4 -> 6, of which waited for: 4 -> 4; matrix products, arithmetic and copies ran while one was open for 0% -> 0% of each run, Pallas kernels for 10% -> 6%
where the time goes in v3:
time: 131 us; the launch traced here: 130 us
  blocking collectives  36.9 us (28%)
  Pallas kernels  28.1 us (21%)
  waiting for transfers between devices  22.5 us (17%)
  local copies, waits for them, and re-layouts  22.3 us (17%)
  starting transfers between devices  18.5 us (14%)
    all_to_all x2, blocking collectives, scan(): held = lax.all_to_all(state, LAYER, split_axis=0, concat_axis=0, tiled=True)  36.9 us
    pallas_call x5, Pallas kernels, run(): pl.pallas_call(kernel, grid=(steps,), in_specs=[SMEM, SMEM] + ins, out_sp...  22.9 us
    unnamed x46, local copies, waits for them, and re-layouts  22.3 us
    ppermute x4, waiting for transfers between devices, scan(): others.append(lax.ppermute(total, 'z', pairs))  14 us
    ppermute x4, starting transfers between devices, scan(): others.append(lax.ppermute(total, 'z', pairs))  10.7 us
    all_to_all x2, waiting for transfers between devices, scan(): lax.all_to_all(sums.reshape(heads, DH, DH), LAYER, split_axis=0, concat_a...  8.54 us
    all_to_all x2, starting transfers between devices, scan(): lax.all_to_all(sums.reshape(heads, DH, DH), LAYER, split_axis=0, concat_a...  7.81 us
    pallas_call x4, Pallas kernels, combine(): pl.pallas_call(functools.partial(kernel, forward, count), grid=(owned,),...  5.17 us
  transfers between devices with their start and end apart: 6, of which 4 were waited for; matrix products, arithmetic and copies ran while one was open for 0% of the time, Pallas kernels for 6%

profile of v3, /device:TPU:0, one launch (start us, length us, event | category | flops | bytes accessed | tf_op | source)
XLA Modules:
  0.0 129.6 jit_solution(15601590583192029617)
XLA Ops:
  0.6 0.6 pad_add_fusion.place
  1.2 0.0 copy-start.21
  1.2 0.0 copy-start.22
  1.2 4.4 %tail.1 = bf16[32,128,128]{2,1,0:T(8,128)(2,1)} custom-call(s32[8]{0:T(128)} %lens.17, s32[2]{0:T(128)} %pad_add_fusion.place, bf16[128,4096]{1,0:T(8,128)(2,1)} %k.7, bf16[128,4096]{1,0:T(8,128)(2,1)} %v.7), custom_call_target="tpu_custom_call" | custom-call | flops 134217728 | bytes 3145728 | tf_op jit(solution)/shard_map/tail/pallas_call | solution.py:258
  5.6 19.8 %all_to_all.20 = bf16[32,128,128]{2,1,0:T(8,128)(2,1)S(1)} all-to-all(bf16[32,128,128]{2,1,0:T(8,128)(2,1)} %tail.1), channel_id=1, replica_groups=mesh['z'=4,'x'=2,'head'=4] {'x','head'}, dimensions={0} | all-to-all | bytes 2097152 | tf_op jit(solution)/shard_map/all_to_all | solution.py:294
  25.3 0.0 copy-done.21
  25.4 0.0 copy-done.22
  25.4 1.1 carried_total.1
  26.5 0.0 copy-start
  26.5 0.0 copy-start.1
  26.5 4.6 %collective-permute-start.1 = (bf16[4,128,128]{2,1,0:T(8,128)(2,1)S(1)}, bf16[4,128,128]{2,1,0:T(8,128)(2,1)S(1)}, u32[]{:S(2)}, u32[]{:S(2)}) collective-permute-start(bf16[4,128,128]{2,1,0:T(8,128)(2,1)S(1)} %carried_total.1), channel_id=1, source_target_pairs={{0,16},{8,24},{1,17},{9,25},{2,18},{10,26},{3,19},{11,27},{4,20},{... | collective-permute-start | bytes 393224 | tf_op jit(solution)/shard_map/ppermute | solution.py:301
  31.2 3.5 %collective-permute-start = (bf16[4,128,128]{2,1,0:T(8,128)(2,1)S(1)}, bf16[4,128,128]{2,1,0:T(8,128)(2,1)S(1)}, u32[]{:S(2)}, u32[]{:S(2)}) collective-permute-start(bf16[4,128,128]{2,1,0:T(8,128)(2,1)S(1)} %carried_total.1), channel_id=1, source_target_pairs={{0,8},{8,16},{16,24},{1,9},{9,17},{17,25},{2,10},{10,18},{18,26},{... | collective-permute-start | bytes 393224 | tf_op jit(solution)/shard_map/ppermute | solution.py:301
  34.6 0.0 collective-permute-done.1.rest_1_
  34.7 2.5 %collective-permute-done.rest_0_ = bf16[4,128,128]{2,1,0:T(8,128)(2,1)S(1)} collective-permute-done((bf16[4,128,128]{2,1,0:T(8,128)(2,1)S(1)}, bf16[4,128,128]{2,1,0:T(8,128)(2,1)S(1)}, u32[]{:S(2)}, u32[]{:S(2)}) %collective-permute-start) | collective-permute-done | bytes 131104 | tf_op jit(solution)/shard_map/ppermute | solution.py:301
  37.1 1.5 %carried_prefix.1 = bf16[8,4,128,128]{3,2,1,0:T(8,128)(2,1)S(1)} custom-call(s32[8]{0:T(128)S(1)} %copy-done.21, s32[2]{0:T(128)S(1)} %copy-done.22, bf16[8,4,128,128]{3,2,1,0:T(8,128)(2,1)S(1)} %bitcast.7, bf16[4,128,128]{2,1,0:T(8,128)(2,1)S(1)} %collective-permute-done.rest_0_, bf16[4,128,128]{2,1,0:T(8,128)(2,1)S(1)} %collective-permute-done.1.rest_1_), custom_call_target="tpu_custom_call" | custom-call | flops 2097152 | bytes 2097152 | tf_op jit(solution)/shard_map/carried_prefix/pallas_call | solution.py:276
  38.6 0.0 copy-start.3
  38.6 1.0 copy-done.3
  39.6 3.6 %all-to-all-start.1 = ((bf16[32,128,128]{2,1,0:T(8,128)(2,1)}), bf16[32,128,128]{2,1,0:T(8,128)(2,1)S(1)}, u32[]{:S(2)}, u32[]{:S(2)}) async-start(bf16[32,128,128]{2,1,0:T(8,128)(2,1)} %bitcast.11), calls=%async_computation.1 | async-start | bytes 2097152 | tf_op jit(solution)/shard_map/all_to_all | solution.py:303
  43.1 0.0 copy-done
  43.2 0.0 copy-done.1
  43.2 0.0 copy-start.4
  43.2 1.2 copy-done.4
  44.4 3.3 %within.1 = (bf16[32,128,128]{2,1,0:T(8,128)(2,1)S(1)}, f32[128,4096]{1,0:T(8,128)S(1)}, bf16[128,4096]{1,0:T(8,128)(2,1)S(1)}, bf16[32,128,128]{2,1,0:T(8,128)(2,1)S(1)}) custom-call(s32[8]{0:T(128)S(1)} %copy-done.21, s32[2]{0:T(128)S(1)} %copy-done.22, bf16[128,4096]{1,0:T(8,128)(2,1)S(1)} %copy-done.4, bf16[128,4096]{1,0:T(8,128)(2,1)S(1)} %copy-done, ...), custom_call_target="tpu_custom_call" | custom-call | flops 268435456 | bytes 7340032 | tf_op jit(solution)/shard_map/within/pallas_call | solution.py:258
  47.7 0.0 copy-start.6
  47.7 1.3 %copy-done.6 = f32[128,4096]{1,0:T(8,128)} copy-done((f32[128,4096]{1,0:T(8,128)}, f32[128,4096]{1,0:T(8,128)S(1)}, u32[]{:S(2)}) %copy-start.6) | copy-done | bytes 2097176
  49.1 0.0 copy-start.13
  49.1 1.0 copy-done.13
  50.1 0.0 copy-start.17
  50.1 1.0 copy-done.17
  51.0 0.0 copy-start.19
  51.0 1.0 copy-done.19
  52.0 5.5 %all-to-all-done.1.incoming = bf16[32,128,128]{2,1,0:T(8,128)(2,1)S(1)} async-done(((bf16[32,128,128]{2,1,0:T(8,128)(2,1)}), bf16[32,128,128]{2,1,0:T(8,128)(2,1)S(1)}, u32[]{:S(2)}, u32[]{:S(2)}) %all-to-all-start.1) | async-done | bytes 1048608 | tf_op jit(solution)/shard_map/all_to_all | solution.py:303
  57.5 0.0 copy-start.7
  57.5 1.6 %copy-done.7 = f32[128,4096]{1,0:T(8,128)S(1)} copy-done((f32[128,4096]{1,0:T(8,128)S(1)}, f32[128,4096]{1,0:T(8,128)}, u32[]{:S(2)}) %copy-start.7) | copy-done | bytes 2097176
  59.1 0.0 copy-start.12
  59.1 1.2 copy-done.12
  60.3 1.2 copy-done.18
  61.6 0.0 copy-start.20
  61.6 1.2 copy-done.20
  62.8 5.6 %normed.1 = (bf16[128,4096]{1,0:T(8,128)(2,1)}, bf16[128,4096]{1,0:T(8,128)(2,1)S(1)}, bf16[32,128,128]{2,1,0:T(8,128)(2,1)S(1)}) custom-call(s32[8]{0:T(128)S(1)} %copy-done.21, s32[2]{0:T(128)S(1)} %copy-done.22, bf16[128,4096]{1,0:T(8,128)(2,1)S(1)} %copy-done.18, bf16[32,128,128]{2,1,0:T(8,128)(2,1)S(1)} %copy-done.20, bf16[128,4096]{1,0:T(8,128)(2,1)S(1)} %copy-done.12, ...), custom_call_target="tpu_custom_call" | custom-call | flops 268435456 | bytes 8388608 | tf_op jit(solution)/shard_map/normed/pallas_call | solution.py:258
  68.4 0.0 copy-start.15
  68.4 17.1 %all_to_all.21 = bf16[32,128,128]{2,1,0:T(8,128)(2,1)S(1)} all-to-all(bf16[32,128,128]{2,1,0:T(8,128)(2,1)S(1)} %get-tuple-element.25), channel_id=1, replica_groups=mesh['z'=4,'x'=2,'head'=4] {'x','head'}, dimensions={0} | all-to-all | bytes 2097152 | tf_op jit(solution)/shard_map/all_to_all | solution.py:294
  85.6 1.1 future_total.1
  86.7 1.3 collective-permute-start.3
  88.0 1.3 collective-permute-start.2
  89.3 11.5 %collective-permute-done.3.rest_1_ = bf16[4,128,128]{2,1,0:T(8,128)(2,1)S(1)} collective-permute-done((bf16[4,128,128]{2,1,0:T(8,128)(2,1)S(1)}, bf16[4,128,128]{2,1,0:T(8,128)(2,1)S(1)}, u32[]{:S(2)}, u32[]{:S(2)}) %collective-permute-start.3) | collective-permute-done | bytes 131104 | tf_op jit(solution)/shard_map/ppermute | solution.py:301
  100.8 0.0 collective-permute-done.2.rest_0_
  100.8 1.5 %future_prefix.1 = bf16[8,4,128,128]{3,2,1,0:T(8,128)(2,1)S(1)} custom-call(s32[8]{0:T(128)S(1)} %copy-done.21, s32[2]{0:T(128)S(1)} %copy-done.22, bf16[8,4,128,128]{3,2,1,0:T(8,128)(2,1)S(1)} %bitcast.9, bf16[4,128,128]{2,1,0:T(8,128)(2,1)S(1)} %collective-permute-done.2.rest_0_, bf16[4,128,128]{2,1,0:T(8,128)(2,1)S(1)} %collective-permute-done.3.rest_1_), custom_call_target="tpu_custom_call" | custom-call | flops 2097152 | bytes 2097152 | tf_op jit(solution)/shard_map/future_prefix/pallas_call | solution.py:276
  102.3 0.0 copy-done.15
  102.3 0.0 copy-start.2
  102.3 1.0 copy-done.2
  103.2 4.2 %all-to-all-start.3 = ((bf16[32,128,128]{2,1,0:T(8,128)(2,1)}), bf16[32,128,128]{2,1,0:T(8,128)(2,1)}, u32[]{:S(2)}, u32[]{:S(2)}) async-start(bf16[32,128,128]{2,1,0:T(8,128)(2,1)} %bitcast.10), calls=%async_computation.3 | async-start | bytes 2097152 | tf_op jit(solution)/shard_map/all_to_all | solution.py:303
  107.5 0.0 copy-start.5
  107.5 1.2 copy-done.5
  108.7 0.0 copy-start.14
  108.7 1.2 copy-done.14
  110.0 1.2 copy-done.16
  111.2 5.1 %grads_within.1 = (bf16[128,4096]{1,0:T(8,128)(2,1)}, f32[128,4096]{1,0:T(8,128)S(1)}, f32[128,4096]{1,0:T(8,128)S(1)}) custom-call(s32[8]{0:T(128)S(1)} %copy-done.21, s32[2]{0:T(128)S(1)} %copy-done.22, bf16[128,4096]{1,0:T(8,128)(2,1)S(1)} %copy-done.5, bf16[128,4096]{1,0:T(8,128)(2,1)S(1)} %copy-done, bf16[128,4096]{1,0:T(8,128)(2,1)S(1)} %copy-done.1, ...), custom_call_target="tpu_custom_call" | custom-call | flops 671088640 | bytes 9437184 | tf_op jit(solution)/shard_map/grads_within/pallas_call | solution.py:258
  116.3 1.3 %copy-done.8 = f32[128,4096]{1,0:T(8,128)} copy-done((f32[128,4096]{1,0:T(8,128)}, f32[128,4096]{1,0:T(8,128)S(1)}, u32[]{:S(2)}) %copy-start.8) | copy-done | bytes 2097176
  117.6 1.3 %copy-done.10 = f32[128,4096]{1,0:T(8,128)} copy-done((f32[128,4096]{1,0:T(8,128)}, f32[128,4096]{1,0:T(8,128)S(1)}, u32[]{:S(2)}) %copy-start.10) | copy-done | bytes 2097176
  118.9 3.0 %all-to-all-done.3.outgoing = bf16[32,128,128]{2,1,0:T(8,128)(2,1)} async-done(((bf16[32,128,128]{2,1,0:T(8,128)(2,1)}), bf16[32,128,128]{2,1,0:T(8,128)(2,1)}, u32[]{:S(2)}, u32[]{:S(2)}) %all-to-all-start.3) | async-done | bytes 1048608 | tf_op jit(solution)/shard_map/all_to_all | solution.py:303
  122.0 1.6 %copy-done.9 = f32[128,4096]{1,0:T(8,128)S(1)} copy-done((f32[128,4096]{1,0:T(8,128)S(1)}, f32[128,4096]{1,0:T(8,128)}, u32[]{:S(2)}) %copy-start.9) | copy-done | bytes 2097176
  123.6 1.6 %copy-done.11 = f32[128,4096]{1,0:T(8,128)S(1)} copy-done((f32[128,4096]{1,0:T(8,128)S(1)}, f32[128,4096]{1,0:T(8,128)}, u32[]{:S(2)}) %copy-start.11) | copy-done | bytes 2097176
  125.1 4.5 %grads_last.1 = (bf16[128,4096]{1,0:T(8,128)(2,1)}, bf16[128,4096]{1,0:T(8,128)(2,1)}) custom-call(s32[8]{0:T(128)S(1)} %copy-done.21, s32[2]{0:T(128)S(1)} %copy-done.22, bf16[128,4096]{1,0:T(8,128)(2,1)S(1)} %copy-done, bf16[128,4096]{1,0:T(8,128)(2,1)S(1)} %copy-done.1, f32[128,4096]{1,0:T(8,128)S(1)} %copy-done.9, f32[128,4096]{1,0:T(8,128)S(1)} %copy-done.11, ...), custom_call_target="tpu_custom_call" | custom-call | flops 268435456 | bytes 7340032 | tf_op jit(solution)/shard_map/grads_last/pallas_call | solution.py:258
  (6 shorter events, 0.0 us)
Async XLA Ops:
  1.2 24.1 %copy-start.21 = (s32[8]{0:T(128)S(1)}, s32[8]{0:T(128)}, u32[]{:S(2)}) copy-start(s32[8]{0:T(128)} %lens.17) | copy-start | bytes 100
  1.2 24.1 %copy-start.22 = (s32[2]{0:T(128)S(1)}, s32[2]{0:T(128)}, u32[]{:S(2)}) copy-start(s32[2]{0:T(128)} %pad_add_fusion.place) | copy-start | bytes 28
  26.5 16.7 %copy-start = (bf16[128,4096]{1,0:T(8,128)(2,1)S(1)}, bf16[128,4096]{1,0:T(8,128)(2,1)}, u32[]{:S(2)}) copy-start(bf16[128,4096]{1,0:T(8,128)(2,1)} %k.7) | copy-start | bytes 3145732
  26.5 16.7 %copy-start.1 = (bf16[128,4096]{1,0:T(8,128)(2,1)S(1)}, bf16[128,4096]{1,0:T(8,128)(2,1)}, u32[]{:S(2)}) copy-start(bf16[128,4096]{1,0:T(8,128)(2,1)} %v.7) | copy-start | bytes 3145732
  26.5 8.1 %collective-permute-start.1 = (bf16[4,128,128]{2,1,0:T(8,128)(2,1)S(1)}, bf16[4,128,128]{2,1,0:T(8,128)(2,1)S(1)}, u32[]{:S(2)}, u32[]{:S(2)}) collective-permute-start(bf16[4,128,128]{2,1,0:T(8,128)(2,1)S(1)} %carried_total.1), channel_id=1, source_target_pairs={{0,16},{8,24},{1,17},{9,25},{2,18},{10,26},{3,19},{11,27},{4,20},{... | collective-permute-start | bytes 393224 | tf_op jit(solution)/shard_map/ppermute | solution.py:301
  31.2 6.0 %collective-permute-start = (bf16[4,128,128]{2,1,0:T(8,128)(2,1)S(1)}, bf16[4,128,128]{2,1,0:T(8,128)(2,1)S(1)}, u32[]{:S(2)}, u32[]{:S(2)}) collective-permute-start(bf16[4,128,128]{2,1,0:T(8,128)(2,1)S(1)} %carried_total.1), channel_id=1, source_target_pairs={{0,8},{8,16},{16,24},{1,9},{9,17},{17,25},{2,10},{10,18},{18,26},{... | collective-permute-start | bytes 393224 | tf_op jit(solution)/shard_map/ppermute | solution.py:301
  38.6 1.0 copy-start.3
  39.6 17.9 %all-to-all-start.1 = ((bf16[32,128,128]{2,1,0:T(8,128)(2,1)}), bf16[32,128,128]{2,1,0:T(8,128)(2,1)S(1)}, u32[]{:S(2)}, u32[]{:S(2)}) async-start(bf16[32,128,128]{2,1,0:T(8,128)(2,1)} %bitcast.11), calls=%async_computation.1 | async-start | bytes 2097152 | tf_op jit(solution)/shard_map/all_to_all | solution.py:303
  43.2 1.2 copy-start.4
  47.7 1.4 %copy-start.6 = (f32[128,4096]{1,0:T(8,128)}, f32[128,4096]{1,0:T(8,128)S(1)}, u32[]{:S(2)}) copy-start(f32[128,4096]{1,0:T(8,128)S(1)} %get-tuple-element.18.part) | copy-start | bytes 6291460
  49.1 1.0 copy-start.13
  50.1 1.0 copy-start.17
  51.0 1.0 copy-start.19
  57.5 1.6 %copy-start.7 = (f32[128,4096]{1,0:T(8,128)S(1)}, f32[128,4096]{1,0:T(8,128)}, u32[]{:S(2)}) copy-start(f32[128,4096]{1,0:T(8,128)} %copy-done.6) | copy-start | bytes 6291460
  59.1 1.2 copy-start.12
  60.3 1.2 copy-start.18
  61.6 1.2 copy-start.20
  68.4 33.8 %copy-start.15 = (bf16[128,4096]{1,0:T(8,128)(2,1)}, bf16[128,4096]{1,0:T(8,128)(2,1)S(1)}, u32[]{:S(2)}) copy-start(bf16[128,4096]{1,0:T(8,128)(2,1)S(1)} %get-tuple-element.20.grad_att) | copy-start | bytes 3145732
  86.7 14.1 %collective-permute-start.3 = (bf16[4,128,128]{2,1,0:T(8,128)(2,1)S(1)}, bf16[4,128,128]{2,1,0:T(8,128)(2,1)S(1)}, u32[]{:S(2)}, u32[]{:S(2)}) collective-permute-start(bf16[4,128,128]{2,1,0:T(8,128)(2,1)S(1)} %future_total.1), channel_id=1, source_target_pairs={{16,0},{24,8},{17,1},{25,9},{18,2},{26,10},{19,3},{27,11},{20,4},{... | collective-permute-start | bytes 393224 | tf_op jit(solution)/shard_map/ppermute | solution.py:301
  88.0 12.8 %collective-permute-start.2 = (bf16[4,128,128]{2,1,0:T(8,128)(2,1)S(1)}, bf16[4,128,128]{2,1,0:T(8,128)(2,1)S(1)}, u32[]{:S(2)}, u32[]{:S(2)}) collective-permute-start(bf16[4,128,128]{2,1,0:T(8,128)(2,1)S(1)} %future_total.1), channel_id=1, source_target_pairs={{8,0},{16,8},{24,16},{9,1},{17,9},{25,17},{10,2},{18,10},{26,18},{... | collective-permute-start | bytes 393224 | tf_op jit(solution)/shard_map/ppermute | solution.py:301
  102.3 1.0 copy-start.2
  103.2 18.7 %all-to-all-start.3 = ((bf16[32,128,128]{2,1,0:T(8,128)(2,1)}), bf16[32,128,128]{2,1,0:T(8,128)(2,1)}, u32[]{:S(2)}, u32[]{:S(2)}) async-start(bf16[32,128,128]{2,1,0:T(8,128)(2,1)} %bitcast.10), calls=%async_computation.3 | async-start | bytes 2097152 | tf_op jit(solution)/shard_map/all_to_all | solution.py:303
  107.5 1.2 copy-start.5
  108.7 1.2 copy-start.14
  110.0 1.2 copy-start.16
  116.2 1.4 %copy-start.8 = (f32[128,4096]{1,0:T(8,128)}, f32[128,4096]{1,0:T(8,128)S(1)}, u32[]{:S(2)}) copy-start(f32[128,4096]{1,0:T(8,128)S(1)} %get-tuple-element.23.gk_part) | copy-start | bytes 6291460
  117.6 1.3 %copy-start.10 = (f32[128,4096]{1,0:T(8,128)}, f32[128,4096]{1,0:T(8,128)S(1)}, u32[]{:S(2)}) copy-start(f32[128,4096]{1,0:T(8,128)S(1)} %get-tuple-element.24.gv_part) | copy-start | bytes 6291460
  122.0 1.6 %copy-start.9 = (f32[128,4096]{1,0:T(8,128)S(1)}, f32[128,4096]{1,0:T(8,128)}, u32[]{:S(2)}) copy-start(f32[128,4096]{1,0:T(8,128)} %copy-done.8) | copy-start | bytes 6291460
  123.5 1.6 %copy-start.11 = (f32[128,4096]{1,0:T(8,128)S(1)}, f32[128,4096]{1,0:T(8,128)}, u32[]{:S(2)}) copy-start(f32[128,4096]{1,0:T(8,128)} %copy-done.10) | copy-start | bytes 6291460

commit v4 on v3

--- a/solution.py
+++ b/solution.py
@@ -73,12 +73,13 @@
     return slice(h * DH, (h + 1) * DH)
 
 
-def bunches(heads, size=4):
+def bunches(heads, size=8):
     return [range(h, min(h + size, heads)) for h in range(0, heads, size)]
 
 
-def row_mean(wide, weights):
-    return mul(wide.astype(BF16), weights, NN)
+def halves(wide):
+    high = wide.astype(BF16)
+    return jnp.concatenate([high, (wide - high.astype(F32)).astype(BF16)], axis=1)
 
 
 def tail_kernel(lens, place, k, v, out):
@@ -116,15 +117,19 @@
 
 
 def norm_kernel(lens, place, head_fq, turned, g, part, incoming, out, grad_att, state):
-    weights = jnp.full((DH, DH), 1.0 / DH, BF16)
+    count = g.shape[0]
+    weights = jnp.full((2 * DH, DH), 1.0 / DH, BF16)
     for hs in bunches(state.shape[0]):
         atts = [part[:, cols(h)] + mul(head_fq[:, cols(h)], incoming[h], NN) for h in hs]
-        invs = [lax.rsqrt(row_mean(att * att, weights) + 1e-05) for att in atts]
+        gos = [g[:, cols(h)].astype(F32) for h in hs]
+        means = [
+            mul(jnp.concatenate([halves(att * att), halves(go * att)], axis=0), weights, NN)
+            for att, go in zip(atts, gos)
+        ]
+        invs = [lax.rsqrt(m[:count] + 1e-05) for m in means]
         norms = [att * inv for att, inv in zip(atts, invs)]
-        gos = [g[:, cols(h)].astype(F32) for h in hs]
-        means = [row_mean(go * normed, weights) for go, normed in zip(gos, norms)]
         gas = [
-            ((go - normed * m) * inv).astype(BF16)
+            ((go - normed * (m[count:] * inv)) * inv).astype(BF16)
             for go, normed, m, inv in zip(gos, norms, means, invs)
         ]
         sums = [mul(turned[h], ga, NN).astype(BF16) for h, ga in zip(hs, gas)]
@@ -228,7 +233,7 @@
 
 SMEM = pl.BlockSpec(memory_space=pltpu.SMEM)
 SMALL = pltpu.CompilerParams(
-    dimension_semantics=("arbitrary",), vmem_limit_bytes=16 * 1024 * 1024
+    dimension_semantics=("arbitrary",), vmem_limit_bytes=24 * 1024 * 1024
 )
 LARGE = pltpu.CompilerParams(
     dimension_semantics=("arbitrary",), vmem_limit_bytes=60 * 1024 * 1024
@@ -249,12 +254,16 @@
     tokens = pl.BlockSpec((count, block_heads * DH), lambda i: (0, i))
     states = pl.BlockSpec((block_heads, DH, DH), lambda i: (i, 0, 0))
     tiles = pl.BlockSpec((block_heads, count, count), lambda i: (i, 0, 0))
-    token_bf = jax.ShapeDtypeStruct((count, width), BF16)
-    token_f32 = jax.ShapeDtypeStruct((count, width), F32)
+    token_bf = pltpu.HBM((count, width), BF16)
+    token_f32 = pltpu.HBM((count, width), F32)
     state_bf = jax.ShapeDtypeStruct((heads, DH, DH), BF16)
-    tile_bf = jax.ShapeDtypeStruct((heads, count, count), BF16)
+    tile_bf = pltpu.HBM((heads, count, count), BF16)
 
     def run(kernel, ins, outs, shapes, args, products, name, params=SMALL):
+        args = [
+            arg if spec is states else pltpu.with_memory_space_constraint(arg, pltpu.HBM)
+            for spec, arg in zip(ins, args)
+        ]
         return pl.pallas_call(
             kernel,
             grid=(steps,),
@@ -278,8 +287,10 @@
             grid=(owned,),
             in_specs=[SMEM, SMEM, group] + [single] * (len(args) - 1),
             out_specs=group if many else single,
-            out_shape=jax.ShapeDtypeStruct(
-                ((members,) if many else ()) + (owned, DH, DH), BF16
+            out_shape=(
+                pltpu.HBM((members, owned, DH, DH), BF16)
+                if many
+                else jax.ShapeDtypeStruct((owned, DH, DH), BF16)
             ),
             compiler_params=SMALL,
             cost_estimate=pl.CostEstimate(
@@ -306,7 +317,7 @@
 
     (tail,) = run(tail_kernel, [tokens] * 2, [states], [state_bf], (keys, values), 1, "tail", LARGE)
     incoming = scan(tail, True, "carried")
-    turned_bf = jax.ShapeDtypeStruct((heads, DH, count), BF16)
+    turned_bf = pltpu.HBM((heads, DH, count), BF16)
     turns = pl.BlockSpec((block_heads, DH, count), lambda i: (i, 0, 0))
     scores, part, head_fq, turned = run(
         local_kernel,

time: 131 us -> 122 us (0.931)
  local copies, waits for them, and re-layouts: 22.3 us -> 0.01 us
  waiting for transfers between devices: 22.5 us -> 30.6 us
  Pallas kernels: 28.1 us -> 34.8 us
    unnamed x46 -> x4, local copies, waits for them, and re-layouts: 22.3 us -> 0.01 us
    all_to_all x2, waiting for transfers between devices: 8.54 us -> 16.6 us  [scan(): lax.all_to_all(sums.reshape(heads, DH, DH), LAYER, split_axis=0, concat_a...]
    pallas_call x5, Pallas kernels: 22.9 us -> 27.4 us  [run(): pl.pallas_call(kernel, grid=(steps,), in_specs=[SMEM, SMEM] + ins, out_sp...]
    pallas_call x4, Pallas kernels: 5.17 us -> 7.41 us  [combine(): pl.pallas_call(functools.partial(kernel, forward, count), grid=(owned,),...]
  transfers between devices with their start and end apart: 6 -> 6, of which waited for: 4 -> 4; matrix products, arithmetic and copies ran while one was open for 0% -> 0% of each run, Pallas kernels for 6% -> 10%
where the time goes in v4:
time: 122 us; the launch traced here: 121 us
  blocking collectives  36.9 us (30%)
  Pallas kernels  34.8 us (29%)
  waiting for transfers between devices  30.6 us (25%)
  starting transfers between devices  17.7 us (15%)
    all_to_all x2, blocking collectives, scan(): held = lax.all_to_all(state, LAYER, split_axis=0, concat_axis=0, tiled=True)  36.9 us
    pallas_call x5, Pallas kernels, run(): pl.pallas_call(kernel, grid=(steps,), in_specs=[SMEM, SMEM] + ins, out_sp...  27.4 us
    all_to_all x2, waiting for transfers between devices, scan(): lax.all_to_all(sums.reshape(heads, DH, DH), LAYER, split_axis=0, concat_a...  16.6 us
    ppermute x4, waiting for transfers between devices, scan(): others.append(lax.ppermute(total, 'z', pairs))  14 us
    ppermute x4, starting transfers between devices, scan(): others.append(lax.ppermute(total, 'z', pairs))  10.6 us
    pallas_call x4, Pallas kernels, combine(): pl.pallas_call(functools.partial(kernel, forward, count), grid=(owned,),...  7.41 us
    all_to_all x2, starting transfers between devices, scan(): lax.all_to_all(sums.reshape(heads, DH, DH), LAYER, split_axis=0, concat_a...  7.12 us
  transfers between devices with their start and end apart: 6, of which 4 were waited for; matrix products, arithmetic and copies ran while one was open for 0% of the time, Pallas kernels for 10%

profile of v4, /device:TPU:0, one launch (start us, length us, event | category | flops | bytes accessed | tf_op | source)
XLA Modules:
  0.0 121.3 jit_solution(8672179662793206581)
XLA Ops:
  0.6 0.6 pad_add_fusion.place
  1.2 0.0 copy-start
  1.2 0.0 copy-start.1
  1.2 4.4 %tail.1 = bf16[32,128,128]{2,1,0:T(8,128)(2,1)} custom-call(s32[8]{0:T(128)} %lens.17, s32[2]{0:T(128)} %pad_add_fusion.place, bf16[128,4096]{1,0:T(8,128)(2,1)} %k.7, bf16[128,4096]{1,0:T(8,128)(2,1)} %v.7), custom_call_target="tpu_custom_call" | custom-call | flops 134217728 | bytes 3145728 | tf_op jit(solution)/shard_map/tail/pallas_call | solution.py:267
  5.6 19.8 %all_to_all.20 = bf16[32,128,128]{2,1,0:T(8,128)(2,1)S(1)} all-to-all(bf16[32,128,128]{2,1,0:T(8,128)(2,1)} %tail.1), channel_id=1, replica_groups=mesh['z'=4,'x'=2,'head'=4] {'x','head'}, dimensions={0} | all-to-all | bytes 2097152 | tf_op jit(solution)/shard_map/all_to_all | solution.py:305
  25.3 0.0 copy-done
  25.4 0.0 copy-done.1
  25.4 1.1 carried_total.1
  26.5 4.5 %collective-permute-start.1 = (bf16[4,128,128]{2,1,0:T(8,128)(2,1)S(1)}, bf16[4,128,128]{2,1,0:T(8,128)(2,1)S(1)}, u32[]{:S(2)}, u32[]{:S(2)}) collective-permute-start(bf16[4,128,128]{2,1,0:T(8,128)(2,1)S(1)} %carried_total.1), channel_id=1, source_target_pairs={{0,16},{8,24},{1,17},{9,25},{2,18},{10,26},{3,19},{11,27},{4,20},{... | collective-permute-start | bytes 393224 | tf_op jit(solution)/shard_map/ppermute | solution.py:312
  31.0 3.5 %collective-permute-start = (bf16[4,128,128]{2,1,0:T(8,128)(2,1)S(1)}, bf16[4,128,128]{2,1,0:T(8,128)(2,1)S(1)}, u32[]{:S(2)}, u32[]{:S(2)}) collective-permute-start(bf16[4,128,128]{2,1,0:T(8,128)(2,1)S(1)} %carried_total.1), channel_id=1, source_target_pairs={{0,8},{8,16},{16,24},{1,9},{9,17},{17,25},{2,10},{10,18},{18,26},{... | collective-permute-start | bytes 393224 | tf_op jit(solution)/shard_map/ppermute | solution.py:312
  34.5 0.0 collective-permute-done.1.rest_1_
  34.5 2.5 %collective-permute-done.rest_0_ = bf16[4,128,128]{2,1,0:T(8,128)(2,1)S(1)} collective-permute-done((bf16[4,128,128]{2,1,0:T(8,128)(2,1)S(1)}, bf16[4,128,128]{2,1,0:T(8,128)(2,1)S(1)}, u32[]{:S(2)}, u32[]{:S(2)}) %collective-permute-start) | collective-permute-done | bytes 131104 | tf_op jit(solution)/shard_map/ppermute | solution.py:312
  37.0 2.6 %carried_prefix.1 = bf16[8,4,128,128]{3,2,1,0:T(8,128)(2,1)} custom-call(s32[8]{0:T(128)S(1)} %copy-done, s32[2]{0:T(128)S(1)} %copy-done.1, bf16[8,4,128,128]{3,2,1,0:T(8,128)(2,1)S(1)} %bitcast.7, bf16[4,128,128]{2,1,0:T(8,128)(2,1)S(1)} %collective-permute-done.rest_0_, bf16[4,128,128]{2,1,0:T(8,128)(2,1)S(1)} %collective-permute-done.1.rest_1_), custom_call_target="tpu_custom_call" | custom-call | flops 2097152 | bytes 2097152 | tf_op jit(solution)/shard_map/carried_prefix/pallas_call | solution.py:285
  39.6 3.6 %all-to-all-start.1 = ((bf16[32,128,128]{2,1,0:T(8,128)(2,1)}), bf16[32,128,128]{2,1,0:T(8,128)(2,1)S(1)}, u32[]{:S(2)}, u32[]{:S(2)}) async-start(bf16[32,128,128]{2,1,0:T(8,128)(2,1)} %bitcast.11), calls=%async_computation.1 | async-start | bytes 2097152 | tf_op jit(solution)/shard_map/all_to_all | solution.py:314
  43.1 5.6 %within.1 = (bf16[32,128,128]{2,1,0:T(8,128)(2,1)}, f32[128,4096]{1,0:T(8,128)}, bf16[128,4096]{1,0:T(8,128)(2,1)}, bf16[32,128,128]{2,1,0:T(8,128)(2,1)}) custom-call(s32[8]{0:T(128)S(1)} %copy-done, s32[2]{0:T(128)S(1)} %copy-done.1, bf16[128,4096]{1,0:T(8,128)(2,1)} %q.3, bf16[128,4096]{1,0:T(8,128)(2,1)} %k.7, bf16[128,4096]{1,0:T(8,128)(2,1)} %v.7), custom_call_target="tpu_custom_call" | custom-call | flops 268435456 | bytes 7340032 | tf_op jit(solution)/shard_map/within/pallas_call | solution.py:267
  48.7 8.8 %all-to-all-done.1.incoming = bf16[32,128,128]{2,1,0:T(8,128)(2,1)S(1)} async-done(((bf16[32,128,128]{2,1,0:T(8,128)(2,1)}), bf16[32,128,128]{2,1,0:T(8,128)(2,1)S(1)}, u32[]{:S(2)}, u32[]{:S(2)}) %all-to-all-start.1) | async-done | bytes 1048608 | tf_op jit(solution)/shard_map/all_to_all | solution.py:314
  57.5 5.7 %normed.1 = (bf16[128,4096]{1,0:T(8,128)(2,1)}, bf16[128,4096]{1,0:T(8,128)(2,1)}, bf16[32,128,128]{2,1,0:T(8,128)(2,1)S(1)}) custom-call(s32[8]{0:T(128)S(1)} %copy-done, s32[2]{0:T(128)S(1)} %copy-done.1, bf16[128,4096]{1,0:T(8,128)(2,1)} %get-tuple-element.16.head_fq, bf16[32,128,128]{2,1,0:T(8,128)(2,1)} %get-tuple-element.17.turned, ...), custom_call_target="tpu_custom_call" | custom-call | flops 268435456 | bytes 8388608 | tf_op jit(solution)/shard_map/normed/pallas_call | solution.py:267
  63.2 17.1 %all_to_all.21 = bf16[32,128,128]{2,1,0:T(8,128)(2,1)S(1)} all-to-all(bf16[32,128,128]{2,1,0:T(8,128)(2,1)S(1)} %get-tuple-element.25), channel_id=1, replica_groups=mesh['z'=4,'x'=2,'head'=4] {'x','head'}, dimensions={0} | all-to-all | bytes 2097152 | tf_op jit(solution)/shard_map/all_to_all | solution.py:305
  80.3 1.1 future_total.1
  81.4 1.3 %collective-permute-start.3 = (bf16[4,128,128]{2,1,0:T(8,128)(2,1)S(1)}, bf16[4,128,128]{2,1,0:T(8,128)(2,1)S(1)}, u32[]{:S(2)}, u32[]{:S(2)}) collective-permute-start(bf16[4,128,128]{2,1,0:T(8,128)(2,1)S(1)} %future_total.1), channel_id=1, source_target_pairs={{16,0},{24,8},{17,1},{25,9},{18,2},{26,10},{19,3},{27,11},{20,4},{... | collective-permute-start | bytes 393224 | tf_op jit(solution)/shard_map/ppermute | solution.py:312
  82.7 1.3 %collective-permute-start.2 = (bf16[4,128,128]{2,1,0:T(8,128)(2,1)S(1)}, bf16[4,128,128]{2,1,0:T(8,128)(2,1)S(1)}, u32[]{:S(2)}, u32[]{:S(2)}) collective-permute-start(bf16[4,128,128]{2,1,0:T(8,128)(2,1)S(1)} %future_total.1), channel_id=1, source_target_pairs={{8,0},{16,8},{24,16},{9,1},{17,9},{25,17},{10,2},{18,10},{26,18},{... | collective-permute-start | bytes 393224 | tf_op jit(solution)/shard_map/ppermute | solution.py:312
  84.0 11.5 %collective-permute-done.3.rest_1_ = bf16[4,128,128]{2,1,0:T(8,128)(2,1)S(1)} collective-permute-done((bf16[4,128,128]{2,1,0:T(8,128)(2,1)S(1)}, bf16[4,128,128]{2,1,0:T(8,128)(2,1)S(1)}, u32[]{:S(2)}, u32[]{:S(2)}) %collective-permute-start.3) | collective-permute-done | bytes 131104 | tf_op jit(solution)/shard_map/ppermute | solution.py:312
  95.5 0.0 collective-permute-done.2.rest_0_
  95.5 2.6 %future_prefix.1 = bf16[8,4,128,128]{3,2,1,0:T(8,128)(2,1)} custom-call(s32[8]{0:T(128)S(1)} %copy-done, s32[2]{0:T(128)S(1)} %copy-done.1, bf16[8,4,128,128]{3,2,1,0:T(8,128)(2,1)S(1)} %bitcast.9, bf16[4,128,128]{2,1,0:T(8,128)(2,1)S(1)} %collective-permute-done.2.rest_0_, bf16[4,128,128]{2,1,0:T(8,128)(2,1)S(1)} %collective-permute-done.3.rest_1_), custom_call_target="tpu_custom_call" | custom-call | flops 2097152 | bytes 2097152 | tf_op jit(solution)/shard_map/future_prefix/pallas_call | solution.py:285
  98.1 3.6 %all-to-all-start.3 = ((bf16[32,128,128]{2,1,0:T(8,128)(2,1)}), bf16[32,128,128]{2,1,0:T(8,128)(2,1)S(1)}, u32[]{:S(2)}, u32[]{:S(2)}) async-start(bf16[32,128,128]{2,1,0:T(8,128)(2,1)} %bitcast.10), calls=%async_computation.3 | async-start | bytes 2097152 | tf_op jit(solution)/shard_map/all_to_all | solution.py:314
  101.7 6.6 %grads_within.1 = (bf16[128,4096]{1,0:T(8,128)(2,1)}, f32[128,4096]{1,0:T(8,128)}, f32[128,4096]{1,0:T(8,128)}) custom-call(s32[8]{0:T(128)S(1)} %copy-done, s32[2]{0:T(128)S(1)} %copy-done.1, bf16[128,4096]{1,0:T(8,128)(2,1)} %q.3, bf16[128,4096]{1,0:T(8,128)(2,1)} %k.7, bf16[128,4096]{1,0:T(8,128)(2,1)} %v.7, ...), custom_call_target="tpu_custom_call" | custom-call | flops 671088640 | bytes 9437184 | tf_op jit(solution)/shard_map/grads_within/pallas_call | solution.py:267
  108.2 7.8 %all-to-all-done.3.outgoing = bf16[32,128,128]{2,1,0:T(8,128)(2,1)S(1)} async-done(((bf16[32,128,128]{2,1,0:T(8,128)(2,1)}), bf16[32,128,128]{2,1,0:T(8,128)(2,1)S(1)}, u32[]{:S(2)}, u32[]{:S(2)}) %all-to-all-start.3) | async-done | bytes 1048608 | tf_op jit(solution)/shard_map/all_to_all | solution.py:314
  116.1 5.3 %grads_last.1 = (bf16[128,4096]{1,0:T(8,128)(2,1)}, bf16[128,4096]{1,0:T(8,128)(2,1)}) custom-call(s32[8]{0:T(128)S(1)} %copy-done, s32[2]{0:T(128)S(1)} %copy-done.1, bf16[128,4096]{1,0:T(8,128)(2,1)} %k.7, bf16[128,4096]{1,0:T(8,128)(2,1)} %v.7, f32[128,4096]{1,0:T(8,128)} %get-tuple-element.23.gk_part, f32[128,4096]{1,0:T(8,128)} %get-tuple-element.24.gv_part, ...), custom_call_target="tpu_custom_call" | custom-call | flops 268435456 | bytes 7340032 | tf_op jit(solution)/shard_map/grads_last/pallas_call | solution.py:267
Async XLA Ops:
  1.2 24.1 %copy-start = (s32[8]{0:T(128)S(1)}, s32[8]{0:T(128)}, u32[]{:S(2)}) copy-start(s32[8]{0:T(128)} %lens.17) | copy-start | bytes 100
  1.2 24.1 %copy-start.1 = (s32[2]{0:T(128)S(1)}, s32[2]{0:T(128)}, u32[]{:S(2)}) copy-start(s32[2]{0:T(128)} %pad_add_fusion.place) | copy-start | bytes 28
  26.5 8.0 %collective-permute-start.1 = (bf16[4,128,128]{2,1,0:T(8,128)(2,1)S(1)}, bf16[4,128,128]{2,1,0:T(8,128)(2,1)S(1)}, u32[]{:S(2)}, u32[]{:S(2)}) collective-permute-start(bf16[4,128,128]{2,1,0:T(8,128)(2,1)S(1)} %carried_total.1), channel_id=1, source_target_pairs={{0,16},{8,24},{1,17},{9,25},{2,18},{10,26},{3,19},{11,27},{4,20},{... | collective-permute-start | bytes 393224 | tf_op jit(solution)/shard_map/ppermute | solution.py:312
  31.0 6.0 %collective-permute-start = (bf16[4,128,128]{2,1,0:T(8,128)(2,1)S(1)}, bf16[4,128,128]{2,1,0:T(8,128)(2,1)S(1)}, u32[]{:S(2)}, u32[]{:S(2)}) collective-permute-start(bf16[4,128,128]{2,1,0:T(8,128)(2,1)S(1)} %carried_total.1), channel_id=1, source_target_pairs={{0,8},{8,16},{16,24},{1,9},{9,17},{17,25},{2,10},{10,18},{18,26},{... | collective-permute-start | bytes 393224 | tf_op jit(solution)/shard_map/ppermute | solution.py:312
  39.6 17.9 %all-to-all-start.1 = ((bf16[32,128,128]{2,1,0:T(8,128)(2,1)}), bf16[32,128,128]{2,1,0:T(8,128)(2,1)S(1)}, u32[]{:S(2)}, u32[]{:S(2)}) async-start(bf16[32,128,128]{2,1,0:T(8,128)(2,1)} %bitcast.11), calls=%async_computation.1 | async-start | bytes 2097152 | tf_op jit(solution)/shard_map/all_to_all | solution.py:314
  81.4 14.1 %collective-permute-start.3 = (bf16[4,128,128]{2,1,0:T(8,128)(2,1)S(1)}, bf16[4,128,128]{2,1,0:T(8,128)(2,1)S(1)}, u32[]{:S(2)}, u32[]{:S(2)}) collective-permute-start(bf16[4,128,128]{2,1,0:T(8,128)(2,1)S(1)} %future_total.1), channel_id=1, source_target_pairs={{16,0},{24,8},{17,1},{25,9},{18,2},{26,10},{19,3},{27,11},{20,4},{... | collective-permute-start | bytes 393224 | tf_op jit(solution)/shard_map/ppermute | solution.py:312
  82.7 12.8 %collective-permute-start.2 = (bf16[4,128,128]{2,1,0:T(8,128)(2,1)S(1)}, bf16[4,128,128]{2,1,0:T(8,128)(2,1)S(1)}, u32[]{:S(2)}, u32[]{:S(2)}) collective-permute-start(bf16[4,128,128]{2,1,0:T(8,128)(2,1)S(1)} %future_total.1), channel_id=1, source_target_pairs={{8,0},{16,8},{24,16},{9,1},{17,9},{25,17},{10,2},{18,10},{26,18},{... | collective-permute-start | bytes 393224 | tf_op jit(solution)/shard_map/ppermute | solution.py:312
  98.1 17.9 %all-to-all-start.3 = ((bf16[32,128,128]{2,1,0:T(8,128)(2,1)}), bf16[32,128,128]{2,1,0:T(8,128)(2,1)S(1)}, u32[]{:S(2)}, u32[]{:S(2)}) async-start(bf16[32,128,128]{2,1,0:T(8,128)(2,1)} %bitcast.10), calls=%async_computation.3 | async-start | bytes 2097152 | tf_op jit(solution)/shard_map/all_to_all | solution.py:314

commit v5 on v4

v5 whole, which is shorter than its diff:
```python
import functools

import jax
import jax.numpy as jnp
from jax import lax
from jax.experimental import pallas as pl
from jax.experimental.pallas import tpu as pltpu
from jax.sharding import Mesh, PartitionSpec as P

DH = 128
F32 = jnp.float32
BF16 = jnp.bfloat16
NN = (((1,), (0,)), ((), ()))
NT = (((1,), (1,)), ((), ()))
TN = (((0,), (0,)), ((), ()))
LAYER = ("x", "head")


def mul(a, b, dims):
    return lax.dot_general(a, b, dims, preferred_element_type=F32)


def feature(wide):
    return jnp.where(wide > 0, wide + 1.0, jnp.exp(jnp.minimum(wide, 0.0)))


def slope(wide):
    return jnp.where(wide > 0, 1.0, jnp.exp(jnp.minimum(wide, 0.0)))


def doc_ends(lens):
    ends, total = [], 0
    for j in range(lens.shape[0]):
        total = total + lens[j]
        ends.append(total)
    return ends


def doc_at(ends, where):
    found = 0
    for end in ends:
        found = found + jnp.where(where >= end, 1, 0)
    return found


def rows_of(ends, first, count):
    at = first + lax.broadcasted_iota(jnp.int32, (count, 1), 0)
    return doc_at(ends, at)


def columns_of(ends, first, count):
    at = first + lax.broadcasted_iota(jnp.int32, (1, count), 1)
    return doc_at(ends, at)


def visible(ends, first, count):
    later = lax.broadcasted_iota(jnp.int32, (count, count), 0)
    earlier = lax.broadcasted_iota(jnp.int32, (count, count), 1)
    return (later >= earlier) & (
        rows_of(ends, first, count) == columns_of(ends, first, count)
    )


def head_mask(ends, first, count):
    return rows_of(ends, first, count) == doc_at(ends, first)


def tail_mask(ends, first, count):
    return rows_of(ends, first, count) == doc_at(ends, first + count - 1)


def cols(h):
    return slice(h * DH, (h + 1) * DH)


def bunches(heads, size=8):
    return [range(h, min(h + size, heads)) for h in range(0, heads, size)]


def halves(wide):
    high = wide.astype(BF16)
    return jnp.concatenate([high, (wide - high.astype(F32)).astype(BF16)], axis=1)


def slot(place, n, owned):
    return pl.ds(((place[2] ^ n) >> 1) * owned, owned)


def tail_kernel(ns, lens, place, k, v, *rest):
    outs, kept = rest[:-1], rest[-1]
    count = k.shape[0]
    heads = k.shape[1] // DH
    step = pl.program_id(0)
    tail = tail_mask(doc_ends(lens), place[0] * count, count)
    for hs in bunches(heads):
        fks = [
            jnp.where(tail, feature(k[:, cols(h)].astype(F32)), 0.0).astype(BF16) for h in hs
        ]
        sums = [mul(fk, v[:, cols(h)], TN).astype(BF16) for h, fk in zip(hs, fks)]
        for h, value in zip(hs, sums):
            kept[step * heads + h] = value

    @pl.when(step == pl.num_programs(0) - 1)
    def _():
        for n, out in zip(ns, outs):
            out[...] = kept[slot(place, n, out.shape[0])]


def local_kernel(lens, place, q, k, v, scores, part, head_fq, turned):
    count = q.shape[0]
    ends = doc_ends(lens)
    first = place[0] * count
    seen = visible(ends, first, count)
    head = head_mask(ends, first, count)
    for hs in bunches(scores.shape[0]):
        wides = [feature(q[:, cols(h)].astype(F32)) for h in hs]
        fks = [feature(k[:, cols(h)].astype(F32)).astype(BF16) for h in hs]
        kept = [
            jnp.where(seen, mul(wide.astype(BF16), fk, NT), 0.0).astype(BF16)
            for wide, fk in zip(wides, fks)
        ]
        parts = [mul(s, v[:, cols(h)], NN) for h, s in zip(hs, kept)]
        heads = [jnp.where(head, wide, 0.0) for wide in wides]
        for h, s, p, f in zip(hs, kept, parts, heads):
            scores[h] = s
            part[:, cols(h)] = p
            head_fq[:, cols(h)] = f.astype(BF16)
            turned[h] = f.T.astype(BF16)


def norm_kernel(ns, filled, lens, place, head_fq, turned, g, part, *rest):
    size = len(ns)
    incoming, rest = rest[:size], rest[size + filled :]
    out, grad_att, outs, (came, kept) = rest[0], rest[1], rest[2:-2], rest[-2:]
    count = g.shape[0]
    heads = turned.shape[0]
    step = pl.program_id(0)

    @pl.when(step == 0)
    def _():
        for n, state in zip(ns, incoming):
            came[slot(place, n, state.shape[0])] = state[...]

    weights = jnp.full((2 * DH, DH), 1.0 / DH, BF16)
    for hs in bunches(heads):
        atts = [
            part[:, cols(h)] + mul(head_fq[:, cols(h)], came[step * heads + h], NN) for h in hs
        ]
        gos = [g[:, cols(h)].astype(F32) for h in hs]
        means = [
            mul(jnp.concatenate([halves(att * att), halves(go * att)], axis=0), weights, NN)
            for att, go in zip(atts, gos)
        ]
        invs = [lax.rsqrt(m[:count] + 1e-05) for m in means]
        norms = [att * inv for att, inv in zip(atts, invs)]
        gas = [
            ((go - normed * (m[count:] * inv)) * inv).astype(BF16)
            for go, normed, m, inv in zip(gos, norms, means, invs)
        ]
        sums = [mul(turned[h], ga, NN).astype(BF16) for h, ga in zip(hs, gas)]
        for h, normed, ga, value in zip(hs, norms, gas, sums):
            out[:, cols(h)] = normed.astype(BF16)
            grad_att[:, cols(h)] = ga
            kept[step * heads + h] = value

    @pl.when(step == pl.num_programs(0) - 1)
    def _():
        for n, state in zip(ns, outs):
            state[...] = kept[slot(place, n, state.shape[0])]


def inner_kernel(lens, place, q, k, v, grad_att, scores, *rest):
    states, (gq, gk, gv, came) = rest[:-4], rest[-4:]
    count = q.shape[0]
    heads = scores.shape[0]
    step = pl.program_id(0)

    @pl.when(step == 0)
    def _():
        for n, state in enumerate(states):
            owned = state.shape[0]
            owner = place[2] ^ n
            turn = (owner & 1) * (len(states) // 2) + (owner >> 1)
            came[pl.ds(turn * owned, owned)] = state[...]

    ends = doc_ends(lens)
    first = place[0] * count
    seen = visible(ends, first, count)
    head = head_mask(ends, first, count)
    for hs in bunches(scores.shape[0]):
        wides = [q[:, cols(h)].astype(F32) for h in hs]
        fqs = [feature(wide).astype(BF16) for wide in wides]
        fks = [feature(k[:, cols(h)].astype(F32)).astype(BF16) for h in hs]
        gas = [grad_att[:, cols(h)] for h in hs]
        gss = [
            jnp.where(seen, mul(ga, v[:, cols(h)], NT), 0.0).astype(BF16)
            for h, ga in zip(hs, gas)
        ]
        totals = [
            mul(gs, fk, NN) + jnp.where(head, mul(ga, came[step * heads + h], NT), 0.0)
            for h, gs, fk, ga in zip(hs, gss, fks, gas)
        ]
        gks = [mul(gs, fq, TN) for gs, fq in zip(gss, fqs)]
        gvs = [mul(scores[h], ga, TN) for h, ga in zip(hs, gas)]
        for h, total, wide, a, b in zip(hs, totals, wides, gks, gvs):
            gq[:, cols(h)] = (total * slope(wide)).astype(BF16)
            gk[:, cols(h)] = a
            gv[:, cols(h)] = b


def last_kernel(ns, filled, lens, place, k, v, gk_part, gv_part, *rest):
    size = len(ns)
    outgoing, (gk, gv, came) = rest[:size], rest[size + filled :]
    count = k.shape[0]
    heads = k.shape[1] // DH
    step = pl.program_id(0)

    @pl.when(step == 0)
    def _():
        for n, state in zip(ns, outgoing):
            came[slot(place, n, state.shape[0])] = state[...]

    tail = tail_mask(doc_ends(lens), place[0] * count, count)
    for hs in bunches(heads):
        wides = [k[:, cols(h)].astype(F32) for h in hs]
        fks = [jnp.where(tail, feature(wide), 0.0).astype(BF16) for wide in wides]
        vts = [jnp.where(tail, v[:, cols(h)].astype(F32), 0.0).astype(BF16) for h in hs]
        gks = [gk_part[:, cols(h)] + mul(vt, came[step * heads + h], NT) for h, vt in zip(hs, vts)]
        gvs = [gv_part[:, cols(h)] + mul(fk, came[step * heads + h], NN) for h, fk in zip(hs, fks)]
        for h, a, wide, b in zip(hs, gks, wides, gvs):
            gk[:, cols(h)] = (a * slope(wide)).astype(BF16)
            gv[:, cols(h)] = b.astype(BF16)


def same(a, b):
    return jnp.where(a == b, 1.0, 0.0).astype(F32)


def total_kernel(forward, count, lens, place, *rest):
    states, total, held = rest[:-2], rest[-2], rest[-1]
    members = len(states)
    for n, state in enumerate(states):
        held[place[2] ^ n] = state[...]
    ends = doc_ends(lens)
    layer = place[1] * (members * count)
    carry = None
    for step in range(members):
        i = step if forward else members - 1 - step
        mine = held[i].astype(F32)
        edge = layer + ((i + 1) * count - 1 if forward else i * count)
        here = doc_at(ends, edge)
        if carry is not None:
            mine = mine + carry * same(here, previous)
        carry, previous = mine, here
    total[...] = carry.astype(BF16)


def prefix_kernel(forward, count, members, lens, place, *rest):
    states, outs, (held, sums) = rest[:members], rest[-members - 2 : -2], rest[-2:]
    others = rest[members : -members - 2]
    for n, state in enumerate(states):
        held[place[2] ^ n] = state[...]
    span = members * count
    ends = doc_ends(lens)
    layer = place[1] * span
    sign = -1 if forward else 1
    previous = doc_at(ends, layer - 1 if forward else layer + span)
    carry = None
    for s, other in enumerate(others):
        far = layer + sign * s * span
        there = doc_at(ends, far - 1 if forward else far + span)
        term = other[...].astype(F32) * same(there, previous)
        carry = term if carry is None else carry + term
    for step in range(members):
        i = step if forward else members - 1 - step
        near, far = layer + i * count, layer + (i + 1) * count - 1
        if not forward:
            near, far = far, near
        if carry is None:
            sums[i] = jnp.zeros(sums.shape[1:], BF16)
        else:
            sums[i] = (carry * same(doc_at(ends, near), previous)).astype(BF16)
        if step < members - 1:
            here = doc_at(ends, far)
            mine = held[i].astype(F32)
            if carry is not None:
                mine = mine + carry * same(here, previous)
            carry, previous = mine, here
    for n, out in enumerate(outs):
        out[...] = sums[place[2] ^ n]


SMALL = pltpu.CompilerParams(
    dimension_semantics=("arbitrary",), vmem_limit_bytes=24 * 1024 * 1024
)
LARGE = pltpu.CompilerParams(
    dimension_semantics=("arbitrary",), vmem_limit_bytes=60 * 1024 * 1024
)


def local(queries, keys, values, out_grad, doc_lengths):
    count, width = queries.shape
    heads = width // DH
    layers = lax.axis_size("z")
    members = lax.axis_size("x") * lax.axis_size("head")
    owned = heads // members
    half = heads // 2
    reach = range(1, min(layers - 1, -(-layers // 2)) + 1)
    place = jnp.stack(
        [lax.axis_index(("z", "x", "head")), lax.axis_index("z"), lax.axis_index(LAYER)]
    ).astype(jnp.int32)
    same_core = [n for n in reversed(range(members)) if n % 2 == 0]
    other_core = [n for n in reversed(range(members)) if n % 2 == 1]
    step_heads = max(n for n in (8, 4, 2, 1) if half % n == 0)
    steps = half // step_heads

    def held_in_hbm(arg):
        return pltpu.with_memory_space_constraint(arg, pltpu.HBM)

    def at(parity):
        if parity is None:
            return lambda i, lens, place: i
        return lambda i, lens, place: ((place[2] & 1) ^ parity) * steps + i

    def tokens(parity):
        block = at(parity)
        return pl.BlockSpec((count, step_heads * DH), lambda *a: (0, block(*a)))

    def tiles(parity, rows, columns):
        block = at(parity)
        return pl.BlockSpec((step_heads, rows, columns), lambda *a: (block(*a), 0, 0))

    whole = pl.BlockSpec((owned, DH, DH), lambda *a: (0, 0, 0))
    untouched = pl.BlockSpec(memory_space=pl.ANY)
    token_bf = pltpu.HBM((count, width), BF16)
    token_f32 = pltpu.HBM((count, width), F32)
    tile_bf = pltpu.HBM((heads, count, count), BF16)
    turned_bf = pltpu.HBM((heads, DH, count), BF16)
    owned_bf = jax.ShapeDtypeStruct((owned, DH, DH), BF16)

    def run(kernel, grid, ins, outs, shapes, scratch, args, cost, name, params=SMALL, aliases={}):
        args = [
            arg if arg.shape == (owned, DH, DH) else held_in_hbm(arg) for arg in args
        ]
        flops, moved, exps = cost
        return pl.pallas_call(
            kernel,
            grid_spec=pltpu.PrefetchScalarGridSpec(
                num_scalar_prefetch=2,
                grid=(grid,),
                in_specs=ins,
                out_specs=outs,
                scratch_shapes=scratch,
            ),
            out_shape=shapes,
            input_output_aliases=aliases,
            compiler_params=params,
            cost_estimate=pl.CostEstimate(
                flops=flops, bytes_accessed=moved, transcendentals=exps
            ),
            name=name,
        )(doc_lengths, place, *args)

    product = 2 * half * count * DH * DH
    array = half * count * DH * 2
    half_states = pltpu.VMEM((half, DH, DH), BF16)
    all_states = pltpu.VMEM((heads, DH, DH), BF16)

    def exchange(states):
        pairs = {n: [(i, i ^ n) for i in range(members)] for n in states}
        return {
            n: state if n == 0 else lax.ppermute(state, LAYER, pairs[n])
            for n, state in states.items()
        }

    def scan(states, forward, name):
        block = 2 if owned % 2 == 0 else 1
        single = pl.BlockSpec((block, DH, DH), lambda i, *a: (i, 0, 0))
        buffer = pltpu.VMEM((members, block, DH, DH), BF16)
        came = exchange(states)
        came = [came[n] for n in range(members)]
        cost = (4 * heads * DH * DH, 4 * heads * DH * DH, 0)
        others = []
        if layers > 1:
            (total,) = run(
                functools.partial(total_kernel, forward, count),
                owned // block,
                [single] * members,
                [single],
                [owned_bf],
                [buffer],
                came,
                cost,
                name + "_total",
            )
            for s in reach:
                pairs = [(i, i + s) if forward else (i + s, i) for i in range(layers - s)]
                others.append(lax.ppermute(total, "z", pairs))
        sums = run(
            functools.partial(prefix_kernel, forward, count, members),
            owned // block,
            [single] * (members + len(others)),
            [single] * members,
            [owned_bf] * members,
            [buffer, buffer],
            came + others,
            cost,
            name + "_prefix",
        )
        return exchange({n: sums[n] for n in same_core + other_core})

    groups = ((0, same_core), (1, other_core))
    tail = {}
    for parity, ns in groups:
        outs = run(
            functools.partial(tail_kernel, ns),
            steps,
            [tokens(parity)] * 2,
            [whole] * len(ns),
            [owned_bf] * len(ns),
            [half_states],
            (keys, values),
            (product, 3 * array, half * count * DH),
            f"tail_{parity}",
            LARGE,
        )
        tail.update(zip(ns, outs))
    incoming = scan(tail, True, "carried")
    scores, part, head_fq, turned = run(
        local_kernel,
        2 * steps,
        [tokens(None)] * 3,
        [tiles(None, count, count), tokens(None), tokens(None), tiles(None, DH, count)],
        [tile_bf, token_f32, token_bf, turned_bf],
        [],
        (queries, keys, values),
        (4 * product, 16 * array, 4 * half * count * DH),
        "within",
    )
    head_state, made = {}, ()
    for parity, ns in groups:
        outs = run(
            functools.partial(norm_kernel, ns, len(made)),
            steps,
            [tokens(parity), tiles(parity, DH, count), tokens(parity), tokens(parity)]
            + [whole] * len(ns)
            + [untouched] * len(made),
            [tokens(parity)] * 2 + [whole] * len(ns),
            [token_bf] * 2 + [owned_bf] * len(ns),
            [half_states, half_states],
            (head_fq, turned, out_grad, part, *[incoming[n] for n in ns], *made),
            (4 * product, 9 * array, half * count * DH),
            f"normed_{parity}",
            aliases={6 + len(ns) + j: j for j in range(len(made))},
        )
        made = tuple(outs[:2])
        head_state.update(zip(ns, outs[2:]))
    attn_out, grad_att = made
    outgoing = scan(head_state, False, "future")
    grad_queries, gk_part, gv_part = run(
        inner_kernel,
        2 * steps,
        [tokens(None)] * 4 + [tiles(None, count, count)] + [whole] * members,
        [tokens(None)] * 3,
        [token_bf, token_f32, token_f32],
        [all_states],
        (queries, keys, values, grad_att, scores, *[incoming[n] for n in range(members)]),
        (10 * product, 22 * array, 4 * half * count * DH),
        "grads_within",
    )
    made = ()
    for parity, ns in groups:
        made = tuple(
            run(
                functools.partial(last_kernel, ns, len(made)),
                steps,
                [tokens(parity)] * 4 + [whole] * len(ns) + [untouched] * len(made),
                [tokens(parity)] * 2,
                [token_bf] * 2,
                [half_states],
                (keys, values, gk_part, gv_part, *[outgoing[n] for n in ns], *made),
                (2 * product, 9 * array, half * count * DH),
                f"grads_last_{parity}",
                aliases={6 + len(ns) + j: j for j in range(len(made))},
            )
        )
    return attn_out, grad_queries, *made


def solution(mesh):
    n_seq, n_head = mesh.shape["seq"], mesh.shape["head"]
    inner = 2 if n_seq % 2 == 0 else 1
    fine = Mesh(mesh.devices.reshape(n_seq // inner, inner, n_head), ("z", "x", "head"))
    rows = P(("z", "x", "head"), None)
    return jax.shard_map(
        local,
        mesh=fine,
        in_specs=(rows, rows, rows, rows, P()),
        out_specs=(rows, rows, rows, rows),
        check_vma=False,
    )
```

time: 122 us -> 116 us (0.951); the launches traced: 121 us -> 113 us
  blocking collectives: 36.9 us -> 0 us
  starting transfers between devices: 17.7 us -> 38.2 us
  Pallas kernels: 34.8 us -> 39.9 us
  waiting for transfers between devices: 30.6 us -> 32.9 us
    all_to_all x2 -> x0, blocking collectives: 36.9 us -> none  [scan(): held = lax.all_to_all(state, LAYER, split_axis=0, concat_axis=0, tiled=True)]
    ppermute x0 -> x28, starting transfers between devices: none -> 27.5 us  [exchange(): lax.ppermute(state, LAYER, pairs[n])]
    ppermute x0 -> x28, waiting for transfers between devices: none -> 18.1 us  [exchange(): lax.ppermute(state, LAYER, pairs[n])]
    all_to_all x2 -> x0, waiting for transfers between devices: 16.6 us -> none  [scan(): lax.all_to_all(sums.reshape(heads, DH, DH), LAYER, split_axis=0, concat_a...]
    all_to_all x2 -> x0, starting transfers between devices: 7.12 us -> none  [scan(): lax.all_to_all(sums.reshape(heads, DH, DH), LAYER, split_axis=0, concat_a...]
    pallas_call x9 -> x12, Pallas kernels: 34.8 us -> 39.9 us  [run(): pl.pallas_call(kernel, grid_spec=pltpu.PrefetchScalarGridSpec(num_scalar_...]
  transfers between devices with their start and end apart: 6 -> 32, of which waited for: 4 -> 12; matrix products, arithmetic and copies ran while one was open for 0% -> 0% of each run, Pallas kernels for 10% -> 22%
where the time goes in v5:
time: 116 us; the launch traced here: 113 us
  Pallas kernels  39.9 us (34%)
  starting transfers between devices  38.2 us (33%)
  waiting for transfers between devices  32.9 us (28%)
    pallas_call x12, Pallas kernels, run(): pl.pallas_call(kernel, grid_spec=pltpu.PrefetchScalarGridSpec(num_scalar_...  39.9 us
    ppermute x28, starting transfers between devices, exchange(): lax.ppermute(state, LAYER, pairs[n])  27.5 us
    ppermute x28, waiting for transfers between devices, exchange(): lax.ppermute(state, LAYER, pairs[n])  18.1 us
    ppermute x4, waiting for transfers between devices, scan(): others.append(lax.ppermute(total, 'z', pairs))  14.8 us
    ppermute x4, starting transfers between devices, scan(): others.append(lax.ppermute(total, 'z', pairs))  10.7 us
  transfers between devices with their start and end apart: 32, of which 12 were waited for; matrix products, arithmetic and copies ran while one was open for 0% of the time, Pallas kernels for 22%

profile of v5, /device:TPU:0, one launch (start us, length us, event | category | flops | bytes accessed | tf_op | source)
XLA Modules:
  0.0 113.4 jit_solution(12363280706683504580)
XLA Ops:
  0.6 0.7 pad_add_fusion.place
  1.3 3.5 %tail_1.1 = (bf16[4,128,128]{2,1,0:T(8,128)(2,1)}, bf16[4,128,128]{2,1,0:T(8,128)(2,1)}, bf16[4,128,128]{2,1,0:T(8,128)(2,1)}, bf16[4,128,128]{2,1,0:T(8,128)(2,1)}) custom-call(s32[8]{0:T(128)} %lens.23, s32[3]{0:T(128)} %pad_add_fusion.place, bf16[128,4096]{1,0:T(8,128)(2,1)} %k.11, bf16[128,4096]{1,0:T(8,128)(2,1)} %v.11), custom_call_target="tpu_custom_call" | custom-call | flops 67108864 | bytes 1572864 | tf_op jit(solution)/shard_map/tail_1/pallas_call | solution.py:346
  4.8 0.5 collective-permute-start
  5.3 2.6 %collective-permute-start.2 = (bf16[4,128,128]{2,1,0:T(8,128)(2,1)}, bf16[4,128,128]{2,1,0:T(8,128)(2,1)S(1)}, u32[]{:S(2)}, u32[]{:S(2)}) collective-permute-start(bf16[4,128,128]{2,1,0:T(8,128)(2,1)} %get-tuple-element.57), channel_id=1, source_target_pairs={{0,3},{1,2},{2,1},{3,0},{4,7},{5,6},{6,5},{7,4},{8,11},{9,10},{10,... | collective-permute-start | bytes 393224 | tf_op jit(solution)/shard_map/ppermute | solution.py:372
  7.9 1.1 collective-permute-start.4
  9.0 0.0 collective-permute-start.6
  9.1 3.4 %tail_0.1 = (bf16[4,128,128]{2,1,0:T(8,128)(2,1)}, bf16[4,128,128]{2,1,0:T(8,128)(2,1)}, bf16[4,128,128]{2,1,0:T(8,128)(2,1)}, bf16[4,128,128]{2,1,0:T(8,128)(2,1)}) custom-call(s32[8]{0:T(128)} %lens.23, s32[3]{0:T(128)} %pad_add_fusion.place, bf16[128,4096]{1,0:T(8,128)(2,1)} %k.11, bf16[128,4096]{1,0:T(8,128)(2,1)} %v.11), custom_call_target="tpu_custom_call" | custom-call | flops 67108864 | bytes 1572864 | tf_op jit(solution)/shard_map/tail_0/pallas_call | solution.py:346
  12.5 2.1 %collective-permute-start.1 = (bf16[4,128,128]{2,1,0:T(8,128)(2,1)}, bf16[4,128,128]{2,1,0:T(8,128)(2,1)S(1)}, u32[]{:S(2)}, u32[]{:S(2)}) collective-permute-start(bf16[4,128,128]{2,1,0:T(8,128)(2,1)} %get-tuple-element.56), channel_id=1, source_target_pairs={{0,2},{1,3},{2,0},{3,1},{4,6},{5,7},{6,4},{7,5},{8,10},{9,11},{10,... | collective-permute-start | bytes 393224 | tf_op jit(solution)/shard_map/ppermute | solution.py:372
  14.5 0.0 collective-permute-done.rest_1_
  14.5 1.5 %collective-permute-start.3 = (bf16[4,128,128]{2,1,0:T(8,128)(2,1)}, bf16[4,128,128]{2,1,0:T(8,128)(2,1)S(1)}, u32[]{:S(2)}, u32[]{:S(2)}) collective-permute-start(bf16[4,128,128]{2,1,0:T(8,128)(2,1)} %get-tuple-element.58), channel_id=1, source_target_pairs={{0,4},{1,5},{2,6},{3,7},{4,0},{5,1},{6,2},{7,3},{8,12},{9,13},{10,... | collective-permute-start | bytes 393224 | tf_op jit(solution)/shard_map/ppermute | solution.py:372
  16.0 0.0 collective-permute-done.2.rest_3_
  16.0 0.0 collective-permute-start.5
  16.0 0.0 collective-permute-done.4.rest_5_
  16.0 0.0 collective-permute-done.6.rest_7_
  16.1 3.4 %collective-permute-done.1.rest_2_ = bf16[4,128,128]{2,1,0:T(8,128)(2,1)S(1)} collective-permute-done((bf16[4,128,128]{2,1,0:T(8,128)(2,1)}, bf16[4,128,128]{2,1,0:T(8,128)(2,1)S(1)}, u32[]{:S(2)}, u32[]{:S(2)}) %collective-permute-start.1) | collective-permute-done | bytes 131104 | tf_op jit(solution)/shard_map/ppermute | solution.py:372
  19.4 1.7 %collective-permute-done.3.rest_4_ = bf16[4,128,128]{2,1,0:T(8,128)(2,1)S(1)} collective-permute-done((bf16[4,128,128]{2,1,0:T(8,128)(2,1)}, bf16[4,128,128]{2,1,0:T(8,128)(2,1)S(1)}, u32[]{:S(2)}, u32[]{:S(2)}) %collective-permute-start.3) | collective-permute-done | bytes 131104 | tf_op jit(solution)/shard_map/ppermute | solution.py:372
  21.1 1.4 %collective-permute-done.5.rest_6_ = bf16[4,128,128]{2,1,0:T(8,128)(2,1)S(1)} collective-permute-done((bf16[4,128,128]{2,1,0:T(8,128)(2,1)}, bf16[4,128,128]{2,1,0:T(8,128)(2,1)S(1)}, u32[]{:S(2)}, u32[]{:S(2)}) %collective-permute-start.5) | collective-permute-done | bytes 131104 | tf_op jit(solution)/shard_map/ppermute | solution.py:372
  22.5 0.9 copy-done
  23.4 0.9 carried_total.1
  24.3 4.6 %collective-permute-start.8 = (bf16[4,128,128]{2,1,0:T(8,128)(2,1)S(1)}, bf16[4,128,128]{2,1,0:T(8,128)(2,1)S(1)}, u32[]{:S(2)}, u32[]{:S(2)}) collective-permute-start(bf16[4,128,128]{2,1,0:T(8,128)(2,1)S(1)} %carried_total.1), channel_id=1, source_target_pairs={{0,16},{8,24},{1,17},{9,25},{2,18},{10,26},{3,19},{11,27},{4,20},{... | collective-permute-start | bytes 393224 | tf_op jit(solution)/shard_map/ppermute | solution.py:398
  28.9 3.5 %collective-permute-start.7 = (bf16[4,128,128]{2,1,0:T(8,128)(2,1)S(1)}, bf16[4,128,128]{2,1,0:T(8,128)(2,1)S(1)}, u32[]{:S(2)}, u32[]{:S(2)}) collective-permute-start(bf16[4,128,128]{2,1,0:T(8,128)(2,1)S(1)} %carried_total.1), channel_id=1, source_target_pairs={{0,8},{8,16},{16,24},{1,9},{9,17},{17,25},{2,10},{10,18},{18,26},{... | collective-permute-start | bytes 393224 | tf_op jit(solution)/shard_map/ppermute | solution.py:398
  32.4 2.5 %collective-permute-done.7.rest_8_ = bf16[4,128,128]{2,1,0:T(8,128)(2,1)S(1)} collective-permute-done((bf16[4,128,128]{2,1,0:T(8,128)(2,1)S(1)}, bf16[4,128,128]{2,1,0:T(8,128)(2,1)S(1)}, u32[]{:S(2)}, u32[]{:S(2)}) %collective-permute-start.7) | collective-permute-done | bytes 131104 | tf_op jit(solution)/shard_map/ppermute | solution.py:398
  34.9 1.1 carried_prefix.1
  36.0 2.5 %collective-permute-start.13 = (bf16[4,128,128]{2,1,0:T(8,128)(2,1)S(1)}, bf16[4,128,128]{2,1,0:T(8,128)(2,1)S(1)}, u32[]{:S(2)}, u32[]{:S(2)}) collective-permute-start(bf16[4,128,128]{2,1,0:T(8,128)(2,1)S(1)} %get-tuple-element.66), channel_id=1, source_target_pairs={{0,6},{1,7},{2,4},{3,5},{4,2},{5,3},{6,0},{7,1},{8,14},{9,15},{10,... | collective-permute-start | bytes 393224 | tf_op jit(solution)/shard_map/ppermute | solution.py:372
  38.5 0.5 collective-permute-start.14
  39.0 0.5 collective-permute-start.15
  39.6 0.0 collective-permute-start.9
  39.6 2.7 %collective-permute-start.10 = (bf16[4,128,128]{2,1,0:T(8,128)(2,1)S(1)}, bf16[4,128,128]{2,1,0:T(8,128)(2,1)S(1)}, u32[]{:S(2)}, u32[]{:S(2)}) collective-permute-start(bf16[4,128,128]{2,1,0:T(8,128)(2,1)S(1)} %get-tuple-element.63), channel_id=1, source_target_pairs={{0,5},{1,4},{2,7},{3,6},{4,1},{5,0},{6,3},{7,2},{8,13},{9,12},{10,... | collective-permute-start | bytes 393224 | tf_op jit(solution)/shard_map/ppermute | solution.py:372
  42.3 0.0 collective-permute-done.13.rest_0_.rest_6_
  42.3 0.0 collective-permute-start.11
  42.3 1.2 %collective-permute-done.14.rest_1_.rest_4_ = bf16[4,128,128]{2,1,0:T(8,128)(2,1)S(1)} collective-permute-done((bf16[4,128,128]{2,1,0:T(8,128)(2,1)S(1)}, bf16[4,128,128]{2,1,0:T(8,128)(2,1)S(1)}, u32[]{:S(2)}, u32[]{:S(2)}) %collective-permute-start.14) | collective-permute-done | bytes 131104 | tf_op jit(solution)/shard_map/ppermute | solution.py:372
  43.5 0.1 collective-permute-start.12
  43.6 6.1 %within.1 = (bf16[32,128,128]{2,1,0:T(8,128)(2,1)}, f32[128,4096]{1,0:T(8,128)}, bf16[128,4096]{1,0:T(8,128)(2,1)}, bf16[32,128,128]{2,1,0:T(8,128)(2,1)}) custom-call(s32[8]{0:T(128)S(1)} %copy-done.2, s32[3]{0:T(128)S(1)} %copy-done.1, bf16[128,4096]{1,0:T(8,128)(2,1)} %q.3, bf16[128,4096]{1,0:T(8,128)(2,1)} %k.11, bf16[128,4096]{1,0:T(8,128)(2,1)} %v.11), custom_call_target="tpu_custom_call" | custom-call | flops 268435456 | bytes 8388608 | tf_op jit(solution)/shard_map/within/pallas_call | solution.py:346
  49.7 4.3 %normed_0.1 = (bf16[128,4096]{1,0:T(8,128)(2,1)}, bf16[128,4096]{1,0:T(8,128)(2,1)}, bf16[4,128,128]{2,1,0:T(8,128)(2,1)S(1)}, bf16[4,128,128]{2,1,0:T(8,128)(2,...) custom-call(s32[8]{0:T(128)S(1)} %copy-done.2, s32[3]{0:T(128)S(1)} %copy-done.1, ...), custom_call_target="tpu_custom_call" | custom-call | flops 268435456 | bytes 4718592 | tf_op jit(solution)/shard_map/normed_0/pallas_call | solution.py:346
  54.0 0.0 collective-permute-done.11.rest_2_.rest_3_
  54.0 4.3 %normed_1.1 = (bf16[128,4096]{1,0:T(8,128)(2,1)}, bf16[128,4096]{1,0:T(8,128)(2,1)}, bf16[4,128,128]{2,1,0:T(8,128)(2,1)S(1)}, bf16[4,128,128]{2,1,0:T(8,128)(2,...) custom-call(s32[8]{0:T(128)S(1)} %copy-done.2, ...), custom_call_target="tpu_custom_call", output_to_operand_aliasing={{0}: (10, {}), {1}: (11, {})} | custom-call | flops 268435456 | bytes 4718592 | tf_op jit(solution)/shard_map/normed_1/pallas_call | solution.py:346
  58.3 0.4 collective-permute-start.16
  58.7 0.6 collective-permute-start.18
  59.2 1.1 collective-permute-start.20
  60.4 1.3 %collective-permute-start.22 = (bf16[4,128,128]{2,1,0:T(8,128)(2,1)S(1)}, bf16[4,128,128]{2,1,0:T(8,128)(2,1)S(1)}, u32[]{:S(2)}, u32[]{:S(2)}) collective-permute-start(bf16[4,128,128]{2,1,0:T(8,128)(2,1)S(1)} %get-tuple-element.85), channel_id=1, source_target_pairs={{0,7},{1,6},{2,5},{3,4},{4,3},{5,2},{6,1},{7,0},{8,15},{9,14},{10,... | collective-permute-start | bytes 393224 | tf_op jit(solution)/shard_map/ppermute | solution.py:372
  61.6 0.8 collective-permute-start.17
  62.4 0.0 collective-permute-done.16.rest_1_
  62.4 1.5 %collective-permute-start.19 = (bf16[4,128,128]{2,1,0:T(8,128)(2,1)S(1)}, bf16[4,128,128]{2,1,0:T(8,128)(2,1)S(1)}, u32[]{:S(2)}, u32[]{:S(2)}) collective-permute-start(bf16[4,128,128]{2,1,0:T(8,128)(2,1)S(1)} %get-tuple-element.82), channel_id=1, source_target_pairs={{0,4},{1,5},{2,6},{3,7},{4,0},{5,1},{6,2},{7,3},{8,12},{9,13},{10,... | collective-permute-start | bytes 393224 | tf_op jit(solution)/shard_map/ppermute | solution.py:372
  63.9 0.2 collective-permute-done.18.rest_3_
  64.2 1.1 %collective-permute-start.21 = (bf16[4,128,128]{2,1,0:T(8,128)(2,1)S(1)}, bf16[4,128,128]{2,1,0:T(8,128)(2,1)S(1)}, u32[]{:S(2)}, u32[]{:S(2)}) collective-permute-start(bf16[4,128,128]{2,1,0:T(8,128)(2,1)S(1)} %get-tuple-element.84), channel_id=1, source_target_pairs={{0,6},{1,7},{2,4},{3,5},{4,2},{5,3},{6,0},{7,1},{8,14},{9,15},{10,... | collective-permute-start | bytes 393224 | tf_op jit(solution)/shard_map/ppermute | solution.py:372
  65.3 0.0 collective-permute-done.20.rest_5_
  65.3 2.8 %collective-permute-done.22.rest_7_ = bf16[4,128,128]{2,1,0:T(8,128)(2,1)S(1)} collective-permute-done((bf16[4,128,128]{2,1,0:T(8,128)(2,1)S(1)}, bf16[4,128,128]{2,1,0:T(8,128)(2,1)S(1)}, u32[]{:S(2)}, u32[]{:S(2)}) %collective-permute-start.22) | collective-permute-done | bytes 131104 | tf_op jit(solution)/shard_map/ppermute | solution.py:372
  68.1 2.1 %collective-permute-done.17.rest_2_ = bf16[4,128,128]{2,1,0:T(8,128)(2,1)S(1)} collective-permute-done((bf16[4,128,128]{2,1,0:T(8,128)(2,1)S(1)}, bf16[4,128,128]{2,1,0:T(8,128)(2,1)S(1)}, u32[]{:S(2)}, u32[]{:S(2)}) %collective-permute-start.17) | collective-permute-done | bytes 131104 | tf_op jit(solution)/shard_map/ppermute | solution.py:372
  70.2 0.7 collective-permute-done.19.rest_4_
  70.9 3.2 %collective-permute-done.21.rest_6_ = bf16[4,128,128]{2,1,0:T(8,128)(2,1)S(1)} collective-permute-done((bf16[4,128,128]{2,1,0:T(8,128)(2,1)S(1)}, bf16[4,128,128]{2,1,0:T(8,128)(2,1)S(1)}, u32[]{:S(2)}, u32[]{:S(2)}) %collective-permute-start.21) | collective-permute-done | bytes 131104 | tf_op jit(solution)/shard_map/ppermute | solution.py:372
  74.2 0.9 future_total.1
  75.0 1.3 %collective-permute-start.24 = (bf16[4,128,128]{2,1,0:T(8,128)(2,1)S(1)}, bf16[4,128,128]{2,1,0:T(8,128)(2,1)S(1)}, u32[]{:S(2)}, u32[]{:S(2)}) collective-permute-start(bf16[4,128,128]{2,1,0:T(8,128)(2,1)S(1)} %future_total.1), channel_id=1, source_target_pairs={{16,0},{24,8},{17,1},{25,9},{18,2},{26,10},{19,3},{27,11},{20,4},{... | collective-permute-start | bytes 393224 | tf_op jit(solution)/shard_map/ppermute | solution.py:398
  76.3 1.3 %collective-permute-start.23 = (bf16[4,128,128]{2,1,0:T(8,128)(2,1)S(1)}, bf16[4,128,128]{2,1,0:T(8,128)(2,1)S(1)}, u32[]{:S(2)}, u32[]{:S(2)}) collective-permute-start(bf16[4,128,128]{2,1,0:T(8,128)(2,1)S(1)} %future_total.1), channel_id=1, source_target_pairs={{8,0},{16,8},{24,16},{9,1},{17,9},{25,17},{10,2},{18,10},{26,18},{... | collective-permute-start | bytes 393224 | tf_op jit(solution)/shard_map/ppermute | solution.py:398
  77.6 12.3 %collective-permute-done.24.rest_9_ = bf16[4,128,128]{2,1,0:T(8,128)(2,1)S(1)} collective-permute-done((bf16[4,128,128]{2,1,0:T(8,128)(2,1)S(1)}, bf16[4,128,128]{2,1,0:T(8,128)(2,1)S(1)}, u32[]{:S(2)}, u32[]{:S(2)}) %collective-permute-start.24) | collective-permute-done | bytes 131104 | tf_op jit(solution)/shard_map/ppermute | solution.py:398
  90.0 1.1 future_prefix.1
  91.1 1.5 %collective-permute-start.29 = (bf16[4,128,128]{2,1,0:T(8,128)(2,1)S(1)}, bf16[4,128,128]{2,1,0:T(8,128)(2,1)S(1)}, u32[]{:S(2)}, u32[]{:S(2)}) collective-permute-start(bf16[4,128,128]{2,1,0:T(8,128)(2,1)S(1)} %get-tuple-element.90), channel_id=1, source_target_pairs={{0,6},{1,7},{2,4},{3,5},{4,2},{5,3},{6,0},{7,1},{8,14},{9,15},{10,... | collective-permute-start | bytes 393224 | tf_op jit(solution)/shard_map/ppermute | solution.py:372
  92.6 1.6 %collective-permute-start.30 = (bf16[4,128,128]{2,1,0:T(8,128)(2,1)S(1)}, bf16[4,128,128]{2,1,0:T(8,128)(2,1)S(1)}, u32[]{:S(2)}, u32[]{:S(2)}) collective-permute-start(bf16[4,128,128]{2,1,0:T(8,128)(2,1)S(1)} %get-tuple-element.91), channel_id=1, source_target_pairs={{0,4},{1,5},{2,6},{3,7},{4,0},{5,1},{6,2},{7,3},{8,12},{9,13},{10,... | collective-permute-start | bytes 393224 | tf_op jit(solution)/shard_map/ppermute | solution.py:372
  94.2 0.5 collective-permute-start.31
  94.6 2.7 %collective-permute-start.26 = (bf16[4,128,128]{2,1,0:T(8,128)(2,1)S(1)}, bf16[4,128,128]{2,1,0:T(8,128)(2,1)S(1)}, u32[]{:S(2)}, u32[]{:S(2)}) collective-permute-start(bf16[4,128,128]{2,1,0:T(8,128)(2,1)S(1)} %get-tuple-element.87), channel_id=1, source_target_pairs={{0,5},{1,4},{2,7},{3,6},{4,1},{5,0},{6,3},{7,2},{8,13},{9,12},{10,... | collective-permute-start | bytes 393224 | tf_op jit(solution)/shard_map/ppermute | solution.py:372
  97.4 1.3 %collective-permute-done.30.rest_1_ = bf16[4,128,128]{2,1,0:T(8,128)(2,1)S(1)} collective-permute-done((bf16[4,128,128]{2,1,0:T(8,128)(2,1)S(1)}, bf16[4,128,128]{2,1,0:T(8,128)(2,1)S(1)}, u32[]{:S(2)}, u32[]{:S(2)}) %collective-permute-start.30) | collective-permute-done | bytes 131104 | tf_op jit(solution)/shard_map/ppermute | solution.py:372
  98.7 0.2 collective-permute-start.28
  98.9 7.1 %grads_within.1 = (bf16[128,4096]{1,0:T(8,128)(2,1)}, f32[128,4096]{1,0:T(8,128)}, f32[128,4096]{1,0:T(8,128)}) custom-call(s32[8]{0:T(128)S(1)} %copy-done.2, s32[3]{0:T(128)S(1)} %copy-done.1, bf16[128,4096]{1,0:T(8,128)(2,1)} %q.3, bf16[128,4096]{1,0:T(8,128)(2,1)} %k.11, bf16[128,4096]{1,0:T(8,128)(2,1)} %v.11, ...), custom_call_target="tpu_custom_call" | custom-call | flops 671088640 | bytes 11534336 | tf_op jit(solution)/shard_map/grads_within/pallas_call | solution.py:346
  106.0 3.7 %grads_last_0.1 = (bf16[128,4096]{1,0:T(8,128)(2,1)}, bf16[128,4096]{1,0:T(8,128)(2,1)}) custom-call(s32[8]{0:T(128)S(1)} %copy-done.2, s32[3]{0:T(128)S(1)} %copy-done.1, bf16[128,4096]{1,0:T(8,128)(2,1)} %k.11, bf16[128,4096]{1,0:T(8,128)(2,1)} %v.11, f32[128,4096]{1,0:T(8,128)} %get-tuple-element.76.gk_part, f32[128,4096]{1,0:T(8,128)} %get-tuple-element.77.gv_part, ...), custom_call_target="tpu_custom_call" | custom-call | flops 134217728 | bytes 4718592 | tf_op jit(solution)/shard_map/grads_last_0/pallas_call | solution.py:346
  109.7 3.7 %grads_last_1.1 = (bf16[128,4096]{1,0:T(8,128)(2,1)}, bf16[128,4096]{1,0:T(8,128)(2,1)}) custom-call(s32[8]{0:T(128)S(1)} %copy-done.2, s32[3]{0:T(128)S(1)} %copy-done.1, bf16[128,4096]{1,0:T(8,128)(2,1)} %k.11, bf16[128,4096]{1,0:T(8,128)(2,1)} %v.11, f32[128,4096]{1,0:T(8,128)} %get-tuple-element.76.gk_part, ...), custom_call_target="tpu_custom_call", output_to_operand_aliasing={{0}: (10, {}), {1}: (11, {})} | custom-call | flops 134217728 | bytes 4718592 | tf_op jit(solution)/shard_map/grads_last_1/pallas_call | solution.py:346
  (19 shorter events, 0.0 us)
Async XLA Ops:
  1.3 21.2 %copy-start.1 = (s32[3]{0:T(128)S(1)}, s32[3]{0:T(128)}, u32[]{:S(2)}) copy-start(s32[3]{0:T(128)} %pad_add_fusion.place) | copy-start | bytes 40
  1.3 21.2 %copy-start.2 = (s32[8]{0:T(128)S(1)}, s32[8]{0:T(128)}, u32[]{:S(2)}) copy-start(s32[8]{0:T(128)} %lens.23) | copy-start | bytes 100
  4.8 9.7 %collective-permute-start = (bf16[4,128,128]{2,1,0:T(8,128)(2,1)}, bf16[4,128,128]{2,1,0:T(8,128)(2,1)S(1)}, u32[]{:S(2)}, u32[]{:S(2)}) collective-permute-start(bf16[4,128,128]{2,1,0:T(8,128)(2,1)} %get-tuple-element.55), channel_id=1, source_target_pairs={{0,1},{1,0},{2,3},{3,2},{4,5},{5,4},{6,7},{7,6},{8,9},{9,8},{10,11... | collective-permute-start | bytes 393224 | tf_op jit(solution)/shard_map/ppermute | solution.py:372
  5.3 10.7 %collective-permute-start.2 = (bf16[4,128,128]{2,1,0:T(8,128)(2,1)}, bf16[4,128,128]{2,1,0:T(8,128)(2,1)S(1)}, u32[]{:S(2)}, u32[]{:S(2)}) collective-permute-start(bf16[4,128,128]{2,1,0:T(8,128)(2,1)} %get-tuple-element.57), channel_id=1, source_target_pairs={{0,3},{1,2},{2,1},{3,0},{4,7},{5,6},{6,5},{7,4},{8,11},{9,10},{10,... | collective-permute-start | bytes 393224 | tf_op jit(solution)/shard_map/ppermute | solution.py:372
  7.9 8.1 %collective-permute-start.4 = (bf16[4,128,128]{2,1,0:T(8,128)(2,1)}, bf16[4,128,128]{2,1,0:T(8,128)(2,1)S(1)}, u32[]{:S(2)}, u32[]{:S(2)}) collective-permute-start(bf16[4,128,128]{2,1,0:T(8,128)(2,1)} %get-tuple-element.59), channel_id=1, source_target_pairs={{0,5},{1,4},{2,7},{3,6},{4,1},{5,0},{6,3},{7,2},{8,13},{9,12},{10,... | collective-permute-start | bytes 393224 | tf_op jit(solution)/shard_map/ppermute | solution.py:372
  9.0 7.0 %collective-permute-start.6 = (bf16[4,128,128]{2,1,0:T(8,128)(2,1)}, bf16[4,128,128]{2,1,0:T(8,128)(2,1)S(1)}, u32[]{:S(2)}, u32[]{:S(2)}) collective-permute-start(bf16[4,128,128]{2,1,0:T(8,128)(2,1)} %get-tuple-element.61), channel_id=1, source_target_pairs={{0,7},{1,6},{2,5},{3,4},{4,3},{5,2},{6,1},{7,0},{8,15},{9,14},{10,... | collective-permute-start | bytes 393224 | tf_op jit(solution)/shard_map/ppermute | solution.py:372
  12.5 7.0 %collective-permute-start.1 = (bf16[4,128,128]{2,1,0:T(8,128)(2,1)}, bf16[4,128,128]{2,1,0:T(8,128)(2,1)S(1)}, u32[]{:S(2)}, u32[]{:S(2)}) collective-permute-start(bf16[4,128,128]{2,1,0:T(8,128)(2,1)} %get-tuple-element.56), channel_id=1, source_target_pairs={{0,2},{1,3},{2,0},{3,1},{4,6},{5,7},{6,4},{7,5},{8,10},{9,11},{10,... | collective-permute-start | bytes 393224 | tf_op jit(solution)/shard_map/ppermute | solution.py:372
  14.5 6.6 %collective-permute-start.3 = (bf16[4,128,128]{2,1,0:T(8,128)(2,1)}, bf16[4,128,128]{2,1,0:T(8,128)(2,1)S(1)}, u32[]{:S(2)}, u32[]{:S(2)}) collective-permute-start(bf16[4,128,128]{2,1,0:T(8,128)(2,1)} %get-tuple-element.58), channel_id=1, source_target_pairs={{0,4},{1,5},{2,6},{3,7},{4,0},{5,1},{6,2},{7,3},{8,12},{9,13},{10,... | collective-permute-start | bytes 393224 | tf_op jit(solution)/shard_map/ppermute | solution.py:372
  16.0 6.5 %collective-permute-start.5 = (bf16[4,128,128]{2,1,0:T(8,128)(2,1)}, bf16[4,128,128]{2,1,0:T(8,128)(2,1)S(1)}, u32[]{:S(2)}, u32[]{:S(2)}) collective-permute-start(bf16[4,128,128]{2,1,0:T(8,128)(2,1)} %get-tuple-element.60), channel_id=1, source_target_pairs={{0,6},{1,7},{2,4},{3,5},{4,2},{5,3},{6,0},{7,1},{8,14},{9,15},{10,... | collective-permute-start | bytes 393224 | tf_op jit(solution)/shard_map/ppermute | solution.py:372
  22.5 0.9 copy-start
  24.3 8.1 %collective-permute-start.8 = (bf16[4,128,128]{2,1,0:T(8,128)(2,1)S(1)}, bf16[4,128,128]{2,1,0:T(8,128)(2,1)S(1)}, u32[]{:S(2)}, u32[]{:S(2)}) collective-permute-start(bf16[4,128,128]{2,1,0:T(8,128)(2,1)S(1)} %carried_total.1), channel_id=1, source_target_pairs={{0,16},{8,24},{1,17},{9,25},{2,18},{10,26},{3,19},{11,27},{4,20},{... | collective-permute-start | bytes 393224 | tf_op jit(solution)/shard_map/ppermute | solution.py:398
  28.9 6.0 %collective-permute-start.7 = (bf16[4,128,128]{2,1,0:T(8,128)(2,1)S(1)}, bf16[4,128,128]{2,1,0:T(8,128)(2,1)S(1)}, u32[]{:S(2)}, u32[]{:S(2)}) collective-permute-start(bf16[4,128,128]{2,1,0:T(8,128)(2,1)S(1)} %carried_total.1), channel_id=1, source_target_pairs={{0,8},{8,16},{16,24},{1,9},{9,17},{17,25},{2,10},{10,18},{18,26},{... | collective-permute-start | bytes 393224 | tf_op jit(solution)/shard_map/ppermute | solution.py:398
  36.0 6.3 %collective-permute-start.13 = (bf16[4,128,128]{2,1,0:T(8,128)(2,1)S(1)}, bf16[4,128,128]{2,1,0:T(8,128)(2,1)S(1)}, u32[]{:S(2)}, u32[]{:S(2)}) collective-permute-start(bf16[4,128,128]{2,1,0:T(8,128)(2,1)S(1)} %get-tuple-element.66), channel_id=1, source_target_pairs={{0,6},{1,7},{2,4},{3,5},{4,2},{5,3},{6,0},{7,1},{8,14},{9,15},{10,... | collective-permute-start | bytes 393224 | tf_op jit(solution)/shard_map/ppermute | solution.py:372
  38.5 5.0 %collective-permute-start.14 = (bf16[4,128,128]{2,1,0:T(8,128)(2,1)S(1)}, bf16[4,128,128]{2,1,0:T(8,128)(2,1)S(1)}, u32[]{:S(2)}, u32[]{:S(2)}) collective-permute-start(bf16[4,128,128]{2,1,0:T(8,128)(2,1)S(1)} %get-tuple-element.67), channel_id=1, source_target_pairs={{0,4},{1,5},{2,6},{3,7},{4,0},{5,1},{6,2},{7,3},{8,12},{9,13},{10,... | collective-permute-start | bytes 393224 | tf_op jit(solution)/shard_map/ppermute | solution.py:372
  39.0 10.6 %collective-permute-start.15 = (bf16[4,128,128]{2,1,0:T(8,128)(2,1)S(1)}, bf16[4,128,128]{2,1,0:T(8,128)(2,1)S(1)}, u32[]{:S(2)}, u32[]{:S(2)}) collective-permute-start(bf16[4,128,128]{2,1,0:T(8,128)(2,1)S(1)} %get-tuple-element.68), channel_id=1, source_target_pairs={{0,2},{1,3},{2,0},{3,1},{4,6},{5,7},{6,4},{7,5},{8,10},{9,11},{10,... | collective-permute-start | bytes 393224 | tf_op jit(solution)/shard_map/ppermute | solution.py:372
  39.6 14.4 %collective-permute-start.9 = (bf16[4,128,128]{2,1,0:T(8,128)(2,1)S(1)}, bf16[4,128,128]{2,1,0:T(8,128)(2,1)S(1)}, u32[]{:S(2)}, u32[]{:S(2)}) collective-permute-start(bf16[4,128,128]{2,1,0:T(8,128)(2,1)S(1)} %get-tuple-element.62), channel_id=1, source_target_pairs={{0,7},{1,6},{2,5},{3,4},{4,3},{5,2},{6,1},{7,0},{8,15},{9,14},{10,... | collective-permute-start | bytes 393224 | tf_op jit(solution)/shard_map/ppermute | solution.py:372
  39.6 14.4 %collective-permute-start.10 = (bf16[4,128,128]{2,1,0:T(8,128)(2,1)S(1)}, bf16[4,128,128]{2,1,0:T(8,128)(2,1)S(1)}, u32[]{:S(2)}, u32[]{:S(2)}) collective-permute-start(bf16[4,128,128]{2,1,0:T(8,128)(2,1)S(1)} %get-tuple-element.63), channel_id=1, source_target_pairs={{0,5},{1,4},{2,7},{3,6},{4,1},{5,0},{6,3},{7,2},{8,13},{9,12},{10,... | collective-permute-start | bytes 393224 | tf_op jit(solution)/shard_map/ppermute | solution.py:372
  42.3 11.7 %collective-permute-start.11 = (bf16[4,128,128]{2,1,0:T(8,128)(2,1)S(1)}, bf16[4,128,128]{2,1,0:T(8,128)(2,1)S(1)}, u32[]{:S(2)}, u32[]{:S(2)}) collective-permute-start(bf16[4,128,128]{2,1,0:T(8,128)(2,1)S(1)} %get-tuple-element.64), channel_id=1, source_target_pairs={{0,3},{1,2},{2,1},{3,0},{4,7},{5,6},{6,5},{7,4},{8,11},{9,10},{10,... | collective-permute-start | bytes 393224 | tf_op jit(solution)/shard_map/ppermute | solution.py:372
  43.5 10.5 %collective-permute-start.12 = (bf16[4,128,128]{2,1,0:T(8,128)(2,1)S(1)}, bf16[4,128,128]{2,1,0:T(8,128)(2,1)S(1)}, u32[]{:S(2)}, u32[]{:S(2)}) collective-permute-start(bf16[4,128,128]{2,1,0:T(8,128)(2,1)S(1)} %get-tuple-element.65), channel_id=1, source_target_pairs={{0,1},{1,0},{2,3},{3,2},{4,5},{5,4},{6,7},{7,6},{8,9},{9,8},{10,11... | collective-permute-start | bytes 393224 | tf_op jit(solution)/shard_map/ppermute | solution.py:372
  58.3 4.1 %collective-permute-start.16 = (bf16[4,128,128]{2,1,0:T(8,128)(2,1)S(1)}, bf16[4,128,128]{2,1,0:T(8,128)(2,1)S(1)}, u32[]{:S(2)}, u32[]{:S(2)}) collective-permute-start(bf16[4,128,128]{2,1,0:T(8,128)(2,1)S(1)} %get-tuple-element.79), channel_id=1, source_target_pairs={{0,1},{1,0},{2,3},{3,2},{4,5},{5,4},{6,7},{7,6},{8,9},{9,8},{10,11... | collective-permute-start | bytes 393224 | tf_op jit(solution)/shard_map/ppermute | solution.py:372
  58.7 5.5 %collective-permute-start.18 = (bf16[4,128,128]{2,1,0:T(8,128)(2,1)S(1)}, bf16[4,128,128]{2,1,0:T(8,128)(2,1)S(1)}, u32[]{:S(2)}, u32[]{:S(2)}) collective-permute-start(bf16[4,128,128]{2,1,0:T(8,128)(2,1)S(1)} %get-tuple-element.81), channel_id=1, source_target_pairs={{0,3},{1,2},{2,1},{3,0},{4,7},{5,6},{6,5},{7,4},{8,11},{9,10},{10,... | collective-permute-start | bytes 393224 | tf_op jit(solution)/shard_map/ppermute | solution.py:372
  59.2 6.1 %collective-permute-start.20 = (bf16[4,128,128]{2,1,0:T(8,128)(2,1)S(1)}, bf16[4,128,128]{2,1,0:T(8,128)(2,1)S(1)}, u32[]{:S(2)}, u32[]{:S(2)}) collective-permute-start(bf16[4,128,128]{2,1,0:T(8,128)(2,1)S(1)} %get-tuple-element.83), channel_id=1, source_target_pairs={{0,5},{1,4},{2,7},{3,6},{4,1},{5,0},{6,3},{7,2},{8,13},{9,12},{10,... | collective-permute-start | bytes 393224 | tf_op jit(solution)/shard_map/ppermute | solution.py:372
  60.4 7.8 %collective-permute-start.22 = (bf16[4,128,128]{2,1,0:T(8,128)(2,1)S(1)}, bf16[4,128,128]{2,1,0:T(8,128)(2,1)S(1)}, u32[]{:S(2)}, u32[]{:S(2)}) collective-permute-start(bf16[4,128,128]{2,1,0:T(8,128)(2,1)S(1)} %get-tuple-element.85), channel_id=1, source_target_pairs={{0,7},{1,6},{2,5},{3,4},{4,3},{5,2},{6,1},{7,0},{8,15},{9,14},{10,... | collective-permute-start | bytes 393224 | tf_op jit(solution)/shard_map/ppermute | solution.py:372
  61.6 8.6 %collective-permute-start.17 = (bf16[4,128,128]{2,1,0:T(8,128)(2,1)S(1)}, bf16[4,128,128]{2,1,0:T(8,128)(2,1)S(1)}, u32[]{:S(2)}, u32[]{:S(2)}) collective-permute-start(bf16[4,128,128]{2,1,0:T(8,128)(2,1)S(1)} %get-tuple-element.80), channel_id=1, source_target_pairs={{0,2},{1,3},{2,0},{3,1},{4,6},{5,7},{6,4},{7,5},{8,10},{9,11},{10,... | collective-permute-start | bytes 393224 | tf_op jit(solution)/shard_map/ppermute | solution.py:372
  62.4 8.5 %collective-permute-start.19 = (bf16[4,128,128]{2,1,0:T(8,128)(2,1)S(1)}, bf16[4,128,128]{2,1,0:T(8,128)(2,1)S(1)}, u32[]{:S(2)}, u32[]{:S(2)}) collective-permute-start(bf16[4,128,128]{2,1,0:T(8,128)(2,1)S(1)} %get-tuple-element.82), channel_id=1, source_target_pairs={{0,4},{1,5},{2,6},{3,7},{4,0},{5,1},{6,2},{7,3},{8,12},{9,13},{10,... | collective-permute-start | bytes 393224 | tf_op jit(solution)/shard_map/ppermute | solution.py:372
  64.2 10.0 %collective-permute-start.21 = (bf16[4,128,128]{2,1,0:T(8,128)(2,1)S(1)}, bf16[4,128,128]{2,1,0:T(8,128)(2,1)S(1)}, u32[]{:S(2)}, u32[]{:S(2)}) collective-permute-start(bf16[4,128,128]{2,1,0:T(8,128)(2,1)S(1)} %get-tuple-element.84), channel_id=1, source_target_pairs={{0,6},{1,7},{2,4},{3,5},{4,2},{5,3},{6,0},{7,1},{8,14},{9,15},{10,... | collective-permute-start | bytes 393224 | tf_op jit(solution)/shard_map/ppermute | solution.py:372
  75.0 14.9 %collective-permute-start.24 = (bf16[4,128,128]{2,1,0:T(8,128)(2,1)S(1)}, bf16[4,128,128]{2,1,0:T(8,128)(2,1)S(1)}, u32[]{:S(2)}, u32[]{:S(2)}) collective-permute-start(bf16[4,128,128]{2,1,0:T(8,128)(2,1)S(1)} %future_total.1), channel_id=1, source_target_pairs={{16,0},{24,8},{17,1},{25,9},{18,2},{26,10},{19,3},{27,11},{20,4},{... | collective-permute-start | bytes 393224 | tf_op jit(solution)/shard_map/ppermute | solution.py:398
  76.3 13.6 %collective-permute-start.23 = (bf16[4,128,128]{2,1,0:T(8,128)(2,1)S(1)}, bf16[4,128,128]{2,1,0:T(8,128)(2,1)S(1)}, u32[]{:S(2)}, u32[]{:S(2)}) collective-permute-start(bf16[4,128,128]{2,1,0:T(8,128)(2,1)S(1)} %future_total.1), channel_id=1, source_target_pairs={{8,0},{16,8},{24,16},{9,1},{17,9},{25,17},{10,2},{18,10},{26,18},{... | collective-permute-start | bytes 393224 | tf_op jit(solution)/shard_map/ppermute | solution.py:398
  91.1 6.3 %collective-permute-start.29 = (bf16[4,128,128]{2,1,0:T(8,128)(2,1)S(1)}, bf16[4,128,128]{2,1,0:T(8,128)(2,1)S(1)}, u32[]{:S(2)}, u32[]{:S(2)}) collective-permute-start(bf16[4,128,128]{2,1,0:T(8,128)(2,1)S(1)} %get-tuple-element.90), channel_id=1, source_target_pairs={{0,6},{1,7},{2,4},{3,5},{4,2},{5,3},{6,0},{7,1},{8,14},{9,15},{10,... | collective-permute-start | bytes 393224 | tf_op jit(solution)/shard_map/ppermute | solution.py:372
  92.6 6.1 %collective-permute-start.30 = (bf16[4,128,128]{2,1,0:T(8,128)(2,1)S(1)}, bf16[4,128,128]{2,1,0:T(8,128)(2,1)S(1)}, u32[]{:S(2)}, u32[]{:S(2)}) collective-permute-start(bf16[4,128,128]{2,1,0:T(8,128)(2,1)S(1)} %get-tuple-element.91), channel_id=1, source_target_pairs={{0,4},{1,5},{2,6},{3,7},{4,0},{5,1},{6,2},{7,3},{8,12},{9,13},{10,... | collective-permute-start | bytes 393224 | tf_op jit(solution)/shard_map/ppermute | solution.py:372
  94.2 11.8 %collective-permute-start.31 = (bf16[4,128,128]{2,1,0:T(8,128)(2,1)S(1)}, bf16[4,128,128]{2,1,0:T(8,128)(2,1)S(1)}, u32[]{:S(2)}, u32[]{:S(2)}) collective-permute-start(bf16[4,128,128]{2,1,0:T(8,128)(2,1)S(1)} %get-tuple-element.92), channel_id=1, source_target_pairs={{0,2},{1,3},{2,0},{3,1},{4,6},{5,7},{6,4},{7,5},{8,10},{9,11},{10,... | collective-permute-start | bytes 393224 | tf_op jit(solution)/shard_map/ppermute | solution.py:372
  94.6 15.0 %collective-permute-start.25 = (bf16[4,128,128]{2,1,0:T(8,128)(2,1)S(1)}, bf16[4,128,128]{2,1,0:T(8,128)(2,1)S(1)}, u32[]{:S(2)}, u32[]{:S(2)}) collective-permute-start(bf16[4,128,128]{2,1,0:T(8,128)(2,1)S(1)} %get-tuple-element.86), channel_id=1, source_target_pairs={{0,7},{1,6},{2,5},{3,4},{4,3},{5,2},{6,1},{7,0},{8,15},{9,14},{10,... | collective-permute-start | bytes 393224 | tf_op jit(solution)/shard_map/ppermute | solution.py:372
  94.6 15.0 %collective-permute-start.26 = (bf16[4,128,128]{2,1,0:T(8,128)(2,1)S(1)}, bf16[4,128,128]{2,1,0:T(8,128)(2,1)S(1)}, u32[]{:S(2)}, u32[]{:S(2)}) collective-permute-start(bf16[4,128,128]{2,1,0:T(8,128)(2,1)S(1)} %get-tuple-element.87), channel_id=1, source_target_pairs={{0,5},{1,4},{2,7},{3,6},{4,1},{5,0},{6,3},{7,2},{8,13},{9,12},{10,... | collective-permute-start | bytes 393224 | tf_op jit(solution)/shard_map/ppermute | solution.py:372
  97.4 12.3 %collective-permute-start.27 = (bf16[4,128,128]{2,1,0:T(8,128)(2,1)S(1)}, bf16[4,128,128]{2,1,0:T(8,128)(2,1)S(1)}, u32[]{:S(2)}, u32[]{:S(2)}) collective-permute-start(bf16[4,128,128]{2,1,0:T(8,128)(2,1)S(1)} %get-tuple-element.88), channel_id=1, source_target_pairs={{0,3},{1,2},{2,1},{3,0},{4,7},{5,6},{6,5},{7,4},{8,11},{9,10},{10,... | collective-permute-start | bytes 393224 | tf_op jit(solution)/shard_map/ppermute | solution.py:372
  98.7 11.0 %collective-permute-start.28 = (bf16[4,128,128]{2,1,0:T(8,128)(2,1)S(1)}, bf16[4,128,128]{2,1,0:T(8,128)(2,1)S(1)}, u32[]{:S(2)}, u32[]{:S(2)}) collective-permute-start(bf16[4,128,128]{2,1,0:T(8,128)(2,1)S(1)} %get-tuple-element.89), channel_id=1, source_target_pairs={{0,1},{1,0},{2,3},{3,2},{4,5},{5,4},{6,7},{7,6},{8,9},{9,8},{10,11... | collective-permute-start | bytes 393224 | tf_op jit(solution)/shard_map/ppermute | solution.py:372

commit v6 on v5

--- a/solution.py
+++ b/solution.py
@@ -12,7 +12,6 @@
 BF16 = jnp.bfloat16
 NN = (((1,), (0,)), ((), ()))
 NT = (((1,), (1,)), ((), ()))
-TN = (((0,), (0,)), ((), ()))
 LAYER = ("x", "head")
 
 
@@ -54,11 +53,20 @@
 
 
 def visible(ends, first, count):
-    later = lax.broadcasted_iota(jnp.int32, (count, count), 0)
-    earlier = lax.broadcasted_iota(jnp.int32, (count, count), 1)
-    return (later >= earlier) & (
-        rows_of(ends, first, count) == columns_of(ends, first, count)
-    )
+    row = lax.broadcasted_iota(jnp.int32, (count, count), 0)
+    column = lax.broadcasted_iota(jnp.int32, (count, count), 1)
+    together = rows_of(ends, first, count) == columns_of(ends, first, count)
+    return (row >= column) & together, (row <= column) & together
+
+
+def identity(count):
+    row = lax.broadcasted_iota(jnp.int32, (count, count), 0)
+    column = lax.broadcasted_iota(jnp.int32, (count, count), 1)
+    return jnp.where(row == column, 1.0, 0.0).astype(BF16)
+
+
+def turn(array, eye):
+    return mul(eye, array, NT).astype(BF16)
 
 
 def head_mask(ends, first, count):
@@ -92,11 +100,13 @@
     heads = k.shape[1] // DH
     step = pl.program_id(0)
     tail = tail_mask(doc_ends(lens), place[0] * count, count)
+    eye = identity(DH)
     for hs in bunches(heads):
         fks = [
             jnp.where(tail, feature(k[:, cols(h)].astype(F32)), 0.0).astype(BF16) for h in hs
         ]
-        sums = [mul(fk, v[:, cols(h)], TN).astype(BF16) for h, fk in zip(hs, fks)]
+        turned = [turn(fk, eye) for fk in fks]
+        sums = [mul(fk, v[:, cols(h)], NN).astype(BF16) for h, fk in zip(hs, turned)]
         for h, value in zip(hs, sums):
             kept[step * heads + h] = value
 
@@ -110,22 +120,27 @@
     count = q.shape[0]
     ends = doc_ends(lens)
     first = place[0] * count
-    seen = visible(ends, first, count)
+    seen, seeing = visible(ends, first, count)
     head = head_mask(ends, first, count)
+    eye = identity(DH)
     for hs in bunches(scores.shape[0]):
         wides = [feature(q[:, cols(h)].astype(F32)) for h in hs]
+        fqs = [wide.astype(BF16) for wide in wides]
         fks = [feature(k[:, cols(h)].astype(F32)).astype(BF16) for h in hs]
         kept = [
-            jnp.where(seen, mul(wide.astype(BF16), fk, NT), 0.0).astype(BF16)
-            for wide, fk in zip(wides, fks)
+            jnp.where(seen, mul(fq, fk, NT), 0.0).astype(BF16) for fq, fk in zip(fqs, fks)
+        ]
+        flipped = [
+            jnp.where(seeing, mul(fk, fq, NT), 0.0).astype(BF16) for fq, fk in zip(fqs, fks)
         ]
         parts = [mul(s, v[:, cols(h)], NN) for h, s in zip(hs, kept)]
-        heads = [jnp.where(head, wide, 0.0) for wide in wides]
-        for h, s, p, f in zip(hs, kept, parts, heads):
+        heads = [jnp.where(head, wide, 0.0).astype(BF16) for wide in wides]
+        turns = [turn(f, eye) for f in heads]
+        for h, s, p, f, t in zip(hs, flipped, parts, heads, turns):
             scores[h] = s
             part[:, cols(h)] = p
-            head_fq[:, cols(h)] = f.astype(BF16)
-            turned[h] = f.T.astype(BF16)
+            head_fq[:, cols(h)] = f
+            turned[h] = t
 
 
 def norm_kernel(ns, filled, lens, place, head_fq, turned, g, part, *rest):
@@ -185,7 +200,7 @@
 
     ends = doc_ends(lens)
     first = place[0] * count
-    seen = visible(ends, first, count)
+    seen, seeing = visible(ends, first, count)
     head = head_mask(ends, first, count)
     for hs in bunches(scores.shape[0]):
         wides = [q[:, cols(h)].astype(F32) for h in hs]
@@ -200,8 +215,12 @@
             mul(gs, fk, NN) + jnp.where(head, mul(ga, came[step * heads + h], NT), 0.0)
             for h, gs, fk, ga in zip(hs, gss, fks, gas)
         ]
-        gks = [mul(gs, fq, TN) for gs, fq in zip(gss, fqs)]
-        gvs = [mul(scores[h], ga, TN) for h, ga in zip(hs, gas)]
+        flipped = [
+            jnp.where(seeing, mul(v[:, cols(h)], ga, NT), 0.0).astype(BF16)
+            for h, ga in zip(hs, gas)
+        ]
+        gks = [mul(gs, fq, NN) for gs, fq in zip(flipped, fqs)]
+        gvs = [mul(scores[h], ga, NN) for h, ga in zip(hs, gas)]
         for h, total, wide, a, b in zip(hs, totals, wides, gks, gvs):
             gq[:, cols(h)] = (total * slope(wide)).astype(BF16)
             gk[:, cols(h)] = a
@@ -257,7 +276,7 @@
 
 def prefix_kernel(forward, count, members, lens, place, *rest):
     states, outs, (held, sums) = rest[:members], rest[-members - 2 : -2], rest[-2:]
-    others = rest[members : -members - 2]
+    others = rest[members + 1 : -members - 2]
     for n, state in enumerate(states):
         held[place[2] ^ n] = state[...]
     span = members * count
@@ -293,10 +312,6 @@
 SMALL = pltpu.CompilerParams(
     dimension_semantics=("arbitrary",), vmem_limit_bytes=24 * 1024 * 1024
 )
-LARGE = pltpu.CompilerParams(
-    dimension_semantics=("arbitrary",), vmem_limit_bytes=60 * 1024 * 1024
-)
-
 
 def local(queries, keys, values, out_grad, doc_lengths):
     count, width = queries.shape
@@ -373,13 +388,9 @@
             for n, state in states.items()
         }
 
-    def scan(states, forward, name):
-        block = 2 if owned % 2 == 0 else 1
-        single = pl.BlockSpec((block, DH, DH), lambda i, *a: (i, 0, 0))
-        buffer = pltpu.VMEM((members, block, DH, DH), BF16)
+    def gather(states, forward, name):
         came = exchange(states)
         came = [came[n] for n in range(members)]
-        cost = (4 * heads * DH * DH, 4 * heads * DH * DH, 0)
         others = []
         if layers > 1:
             (total,) = run(
@@ -390,26 +401,33 @@
                 [owned_bf],
                 [buffer],
                 came,
-                cost,
+                combining,
                 name + "_total",
             )
             for s in reach:
                 pairs = [(i, i + s) if forward else (i + s, i) for i in range(layers - s)]
                 others.append(lax.ppermute(total, "z", pairs))
+        return came, others
+
+    def spread(came, others, after, forward, name):
         sums = run(
             functools.partial(prefix_kernel, forward, count, members),
             owned // block,
-            [single] * (members + len(others)),
+            [single] * members + [untouched] + [single] * len(others),
             [single] * members,
             [owned_bf] * members,
             [buffer, buffer],
-            came + others,
-            cost,
+            [*came, after, *others],
+            combining,
             name + "_prefix",
         )
-        return exchange({n: sums[n] for n in same_core + other_core})
-
-    groups = ((0, same_core), (1, other_core))
+        return exchange({n: sums[n] for n in other_core + same_core})
+
+    block = 2 if owned % 2 == 0 else 1
+    single = pl.BlockSpec((block, DH, DH), lambda i, *a: (i, 0, 0))
+    buffer = pltpu.VMEM((members, block, DH, DH), BF16)
+    combining = (4 * heads * DH * DH, 4 * heads * DH * DH, 0)
+    groups = ((1, other_core), (0, same_core))
     tail = {}
     for parity, ns in groups:
         outs = run(
@@ -422,10 +440,9 @@
             (keys, values),
             (product, 3 * array, half * count * DH),
             f"tail_{parity}",
-            LARGE,
         )
         tail.update(zip(ns, outs))
-    incoming = scan(tail, True, "carried")
+    came, others = gather(tail, True, "carried")
     scores, part, head_fq, turned = run(
         local_kernel,
         2 * steps,
@@ -437,6 +454,7 @@
         (4 * product, 16 * array, 4 * half * count * DH),
         "within",
     )
+    incoming = spread(came, others, part, True, "carried")
     head_state, made = {}, ()
     for parity, ns in groups:
         outs = run(
@@ -456,7 +474,7 @@
         made = tuple(outs[:2])
         head_state.update(zip(ns, outs[2:]))
     attn_out, grad_att = made
-    outgoing = scan(head_state, False, "future")
+    came, others = gather(head_state, False, "future")
     grad_queries, gk_part, gv_part = run(
         inner_kernel,
         2 * steps,
@@ -468,6 +486,7 @@
         (10 * product, 22 * array, 4 * half * count * DH),
         "grads_within",
     )
+    outgoing = spread(came, others, gk_part, False, "future")
     made = ()
     for parity, ns in groups:
         made = tuple(

time: 116 us -> 105 us (0.905); the launches traced: 113 us -> 105 us
  waiting for transfers between devices: 32.9 us -> 25.8 us
    ppermute x4, waiting for transfers between devices: 14.8 us -> 2 us  [gather(): others.append(lax.ppermute(total, 'z', pairs))]
    ppermute x28, waiting for transfers between devices: 18.1 us -> 23.8 us  [exchange(): lax.ppermute(state, LAYER, pairs[n])]
  transfers between devices with their start and end apart: 32 -> 32, of which waited for: 12 -> 18; matrix products, arithmetic and copies ran while one was open for 0% -> 0% of each run, Pallas kernels for 22% -> 24%
where the time goes in v6:
time: 105 us
  Pallas kernels  39.2 us (37%)
  starting transfers between devices  38.2 us (36%)
  waiting for transfers between devices  25.8 us (25%)
    pallas_call x12, Pallas kernels, run(): pl.pallas_call(kernel, grid_spec=pltpu.PrefetchScalarGridSpec(num_scalar_...  39.2 us
    ppermute x28, starting transfers between devices, exchange(): lax.ppermute(state, LAYER, pairs[n])  27.2 us
    ppermute x28, waiting for transfers between devices, exchange(): lax.ppermute(state, LAYER, pairs[n])  23.8 us
    ppermute x4, starting transfers between devices, gather(): others.append(lax.ppermute(total, 'z', pairs))  11 us
  transfers between devices with their start and end apart: 32, of which 18 were waited for; matrix products, arithmetic and copies ran while one was open for 0% of the time, Pallas kernels for 24%

profile of v6, /device:TPU:0, one launch (start us, length us, event | category | flops | bytes accessed | tf_op | source)
XLA Modules:
  0.0 104.6 jit_solution(9474096181306355068)
XLA Ops:
  0.6 0.1 pad_add_fusion.place
  0.7 0.7 copy-done
  1.4 2.6 %tail_1.1 = (bf16[4,128,128]{2,1,0:T(8,128)(2,1)S(1)}, bf16[4,128,128]{2,1,0:T(8,128)(2,1)S(1)}, bf16[4,128,128]{2,1,0:T(8,128)(2,1)S(1)}, bf16[4,128,128]{2,1,0:T(8,128)(2,1)S(1)}) custom-call(s32[8]{0:T(128)S(1)} %copy-done, s32[3]{0:T(128)S(1)} %pad_add_fusion.place, bf16[128,4096]{1,0:T(8,128)(2,1)} %k.11, bf16[128,4096]{1,0:T(8,128)(2,1)} %v.11), custom_call_target="tpu_custom_call" | custom-call | flops 67108864 | bytes 1572864 | tf_op jit(solution)/shard_map/tail_1/pallas_call | solution.py:361
  4.0 0.5 collective-permute-start
  4.5 2.6 %collective-permute-start.2 = (bf16[4,128,128]{2,1,0:T(8,128)(2,1)S(1)}, bf16[4,128,128]{2,1,0:T(8,128)(2,1)S(1)}, u32[]{:S(2)}, u32[]{:S(2)}) collective-permute-start(bf16[4,128,128]{2,1,0:T(8,128)(2,1)S(1)} %get-tuple-element.57), channel_id=1, source_target_pairs={{0,3},{1,2},{2,1},{3,0},{4,7},{5,6},{6,5},{7,4},{8,11},{9,10},{10,... | collective-permute-start | bytes 393224 | tf_op jit(solution)/shard_map/ppermute | solution.py:387
  7.2 1.2 %collective-permute-start.4 = (bf16[4,128,128]{2,1,0:T(8,128)(2,1)S(1)}, bf16[4,128,128]{2,1,0:T(8,128)(2,1)S(1)}, u32[]{:S(2)}, u32[]{:S(2)}) collective-permute-start(bf16[4,128,128]{2,1,0:T(8,128)(2,1)S(1)} %get-tuple-element.59), channel_id=1, source_target_pairs={{0,5},{1,4},{2,7},{3,6},{4,1},{5,0},{6,3},{7,2},{8,13},{9,12},{10,... | collective-permute-start | bytes 393224 | tf_op jit(solution)/shard_map/ppermute | solution.py:387
  8.3 0.1 collective-permute-start.6
  8.4 2.6 %tail_0.1 = (bf16[4,128,128]{2,1,0:T(8,128)(2,1)S(1)}, bf16[4,128,128]{2,1,0:T(8,128)(2,1)S(1)}, bf16[4,128,128]{2,1,0:T(8,128)(2,1)S(1)}, bf16[4,128,128]{2,1,0:T(8,128)(2,1)S(1)}) custom-call(s32[8]{0:T(128)S(1)} %copy-done, s32[3]{0:T(128)S(1)} %pad_add_fusion.place, bf16[128,4096]{1,0:T(8,128)(2,1)} %k.11, bf16[128,4096]{1,0:T(8,128)(2,1)} %v.11), custom_call_target="tpu_custom_call" | custom-call | flops 67108864 | bytes 1572864 | tf_op jit(solution)/shard_map/tail_0/pallas_call | solution.py:361
  11.0 2.1 %collective-permute-start.1 = (bf16[4,128,128]{2,1,0:T(8,128)(2,1)S(1)}, bf16[4,128,128]{2,1,0:T(8,128)(2,1)S(1)}, u32[]{:S(2)}, u32[]{:S(2)}) collective-permute-start(bf16[4,128,128]{2,1,0:T(8,128)(2,1)S(1)} %get-tuple-element.56), channel_id=1, source_target_pairs={{0,2},{1,3},{2,0},{3,1},{4,6},{5,7},{6,4},{7,5},{8,10},{9,11},{10,... | collective-permute-start | bytes 393224 | tf_op jit(solution)/shard_map/ppermute | solution.py:387
  13.1 1.5 %collective-permute-start.3 = (bf16[4,128,128]{2,1,0:T(8,128)(2,1)S(1)}, bf16[4,128,128]{2,1,0:T(8,128)(2,1)S(1)}, u32[]{:S(2)}, u32[]{:S(2)}) collective-permute-start(bf16[4,128,128]{2,1,0:T(8,128)(2,1)S(1)} %get-tuple-element.58), channel_id=1, source_target_pairs={{0,4},{1,5},{2,6},{3,7},{4,0},{5,1},{6,2},{7,3},{8,12},{9,13},{10,... | collective-permute-start | bytes 393224 | tf_op jit(solution)/shard_map/ppermute | solution.py:387
  14.6 0.0 collective-permute-done.2.rest_3_
  14.6 0.1 collective-permute-start.5
  14.6 0.0 collective-permute-done.4.rest_5_
  14.6 0.4 collective-permute-done.6.rest_7_
  15.0 3.4 %collective-permute-done.1.rest_2_ = bf16[4,128,128]{2,1,0:T(8,128)(2,1)S(1)} collective-permute-done((bf16[4,128,128]{2,1,0:T(8,128)(2,1)S(1)}, bf16[4,128,128]{2,1,0:T(8,128)(2,1)S(1)}, u32[]{:S(2)}, u32[]{:S(2)}) %collective-permute-start.1) | collective-permute-done | bytes 131104 | tf_op jit(solution)/shard_map/ppermute | solution.py:387
  18.5 1.1 %collective-permute-done.3.rest_4_ = bf16[4,128,128]{2,1,0:T(8,128)(2,1)S(1)} collective-permute-done((bf16[4,128,128]{2,1,0:T(8,128)(2,1)S(1)}, bf16[4,128,128]{2,1,0:T(8,128)(2,1)S(1)}, u32[]{:S(2)}, u32[]{:S(2)}) %collective-permute-start.3) | collective-permute-done | bytes 131104 | tf_op jit(solution)/shard_map/ppermute | solution.py:387
  19.5 1.4 %collective-permute-done.5.rest_6_ = bf16[4,128,128]{2,1,0:T(8,128)(2,1)S(1)} collective-permute-done((bf16[4,128,128]{2,1,0:T(8,128)(2,1)S(1)}, bf16[4,128,128]{2,1,0:T(8,128)(2,1)S(1)}, u32[]{:S(2)}, u32[]{:S(2)}) %collective-permute-start.5) | collective-permute-done | bytes 131104 | tf_op jit(solution)/shard_map/ppermute | solution.py:387
  20.9 0.9 carried_total.1
  21.8 4.9 %collective-permute-start.8 = (bf16[4,128,128]{2,1,0:T(8,128)(2,1)S(1)}, bf16[4,128,128]{2,1,0:T(8,128)(2,1)S(1)}, u32[]{:S(2)}, u32[]{:S(2)}) collective-permute-start(bf16[4,128,128]{2,1,0:T(8,128)(2,1)S(1)} %carried_total.1), channel_id=1, source_target_pairs={{0,16},{8,24},{1,17},{9,25},{2,18},{10,26},{3,19},{11,27},{4,20},{... | collective-permute-start | bytes 393224 | tf_op jit(solution)/shard_map/ppermute | solution.py:409
  26.7 3.5 %collective-permute-start.7 = (bf16[4,128,128]{2,1,0:T(8,128)(2,1)S(1)}, bf16[4,128,128]{2,1,0:T(8,128)(2,1)S(1)}, u32[]{:S(2)}, u32[]{:S(2)}) collective-permute-start(bf16[4,128,128]{2,1,0:T(8,128)(2,1)S(1)} %carried_total.1), channel_id=1, source_target_pairs={{0,8},{8,16},{16,24},{1,9},{9,17},{17,25},{2,10},{10,18},{18,26},{... | collective-permute-start | bytes 393224 | tf_op jit(solution)/shard_map/ppermute | solution.py:409
  30.2 6.6 %within.1 = (bf16[32,128,128]{2,1,0:T(8,128)(2,1)}, f32[128,4096]{1,0:T(8,128)}, bf16[128,4096]{1,0:T(8,128)(2,1)}, bf16[32,128,128]{2,1,0:T(8,128)(2,1)}) custom-call(s32[8]{0:T(128)S(1)} %copy-done, s32[3]{0:T(128)S(1)} %pad_add_fusion.place, bf16[128,4096]{1,0:T(8,128)(2,1)} %q.3, bf16[128,4096]{1,0:T(8,128)(2,1)} %k.11, bf16[128,4096]{1,0:T(8,128)(2,1)} %v.11), custom_call_target="tpu_custom_call" | custom-call | flops 268435456 | bytes 8388608 | tf_op jit(solution)/shard_map/within/pallas_call | solution.py:361
  36.9 1.1 %carried_prefix.1 = (bf16[4,128,128]{2,1,0:T(8,128)(2,1)S(1)}, bf16[4,128,128]{2,1,0:T(8,128)(2,1)S(1)}, bf16[4,128,128]{2,1,0:T(8,128)(2,1)S(1)}, bf16[4,128,12...) custom-call(s32[8]{0:T(128)S(1)} %copy-done, ...), custom_call_target="tpu_custom_call" | custom-call | flops 2097152 | bytes 2097152 | tf_op jit(solution)/shard_map/carried_prefix/pallas_call | solution.py:361
  38.0 0.7 collective-permute-start.12
  38.7 2.0 %collective-permute-start.13 = (bf16[4,128,128]{2,1,0:T(8,128)(2,1)S(1)}, bf16[4,128,128]{2,1,0:T(8,128)(2,1)S(1)}, u32[]{:S(2)}, u32[]{:S(2)}) collective-permute-start(bf16[4,128,128]{2,1,0:T(8,128)(2,1)S(1)} %get-tuple-element.67), channel_id=1, source_target_pairs={{0,5},{1,4},{2,7},{3,6},{4,1},{5,0},{6,3},{7,2},{8,13},{9,12},{10,... | collective-permute-start | bytes 393224 | tf_op jit(solution)/shard_map/ppermute | solution.py:387
  40.8 0.1 collective-permute-start.14
  40.9 0.5 collective-permute-start.15
  41.4 2.4 %collective-permute-start.9 = (bf16[4,128,128]{2,1,0:T(8,128)(2,1)S(1)}, bf16[4,128,128]{2,1,0:T(8,128)(2,1)S(1)}, u32[]{:S(2)}, u32[]{:S(2)}) collective-permute-start(bf16[4,128,128]{2,1,0:T(8,128)(2,1)S(1)} %get-tuple-element.62), channel_id=1, source_target_pairs={{0,6},{1,7},{2,4},{3,5},{4,2},{5,3},{6,0},{7,1},{8,14},{9,15},{10,... | collective-permute-start | bytes 393224 | tf_op jit(solution)/shard_map/ppermute | solution.py:387
  43.8 0.9 collective-permute-done.12.rest_0_.rest_7_
  44.8 1.5 %collective-permute-start.10 = (bf16[4,128,128]{2,1,0:T(8,128)(2,1)S(1)}, bf16[4,128,128]{2,1,0:T(8,128)(2,1)S(1)}, u32[]{:S(2)}, u32[]{:S(2)}) collective-permute-start(bf16[4,128,128]{2,1,0:T(8,128)(2,1)S(1)} %get-tuple-element.63), channel_id=1, source_target_pairs={{0,4},{1,5},{2,6},{3,7},{4,0},{5,1},{6,2},{7,3},{8,12},{9,13},{10,... | collective-permute-start | bytes 393224 | tf_op jit(solution)/shard_map/ppermute | solution.py:387
  46.2 0.5 collective-permute-done.13.rest_1_.rest_5_
  46.8 1.3 %collective-permute-start.11 = (bf16[4,128,128]{2,1,0:T(8,128)(2,1)S(1)}, bf16[4,128,128]{2,1,0:T(8,128)(2,1)S(1)}, u32[]{:S(2)}, u32[]{:S(2)}) collective-permute-start(bf16[4,128,128]{2,1,0:T(8,128)(2,1)S(1)} %get-tuple-element.64), channel_id=1, source_target_pairs={{0,2},{1,3},{2,0},{3,1},{4,6},{5,7},{6,4},{7,5},{8,10},{9,11},{10,... | collective-permute-start | bytes 393224 | tf_op jit(solution)/shard_map/ppermute | solution.py:387
  48.0 4.3 %normed_1.1 = (bf16[128,4096]{1,0:T(8,128)(2,1)}, bf16[128,4096]{1,0:T(8,128)(2,1)}, bf16[4,128,128]{2,1,0:T(8,128)(2,1)S(1)}, bf16[4,128,128]{2,1,0:T(8,128)(2,...) custom-call(s32[8]{0:T(128)S(1)} %copy-done, s32[3]{0:T(128)S(1)} %pad_add_fusion.place, ...), custom_call_target="tpu_custom_call" | custom-call | flops 268435456 | bytes 4718592 | tf_op jit(solution)/shard_map/normed_1/pallas_call | solution.py:361
  52.3 0.8 collective-permute-done.11.rest_2_
  53.2 4.3 %normed_0.1 = (bf16[128,4096]{1,0:T(8,128)(2,1)}, bf16[128,4096]{1,0:T(8,128)(2,1)}, bf16[4,128,128]{2,1,0:T(8,128)(2,1)S(1)}, bf16[4,128,128]{2,1,0:T(8,128)(2,...) custom-call(s32[8]{0:T(128)S(1)} %copy-done, ...), custom_call_target="tpu_custom_call", output_to_operand_aliasing={{0}: (10, {}), {1}: (11, {})} | custom-call | flops 268435456 | bytes 4718592 | tf_op jit(solution)/shard_map/normed_0/pallas_call | solution.py:361
  57.5 0.6 collective-permute-start.17
  58.1 1.2 %collective-permute-start.19 = (bf16[4,128,128]{2,1,0:T(8,128)(2,1)S(1)}, bf16[4,128,128]{2,1,0:T(8,128)(2,1)S(1)}, u32[]{:S(2)}, u32[]{:S(2)}) collective-permute-start(bf16[4,128,128]{2,1,0:T(8,128)(2,1)S(1)} %get-tuple-element.82), channel_id=1, source_target_pairs={{0,4},{1,5},{2,6},{3,7},{4,0},{5,1},{6,2},{7,3},{8,12},{9,13},{10,... | collective-permute-start | bytes 393224 | tf_op jit(solution)/shard_map/ppermute | solution.py:387
  59.3 1.7 %collective-permute-start.21 = (bf16[4,128,128]{2,1,0:T(8,128)(2,1)S(1)}, bf16[4,128,128]{2,1,0:T(8,128)(2,1)S(1)}, u32[]{:S(2)}, u32[]{:S(2)}) collective-permute-start(bf16[4,128,128]{2,1,0:T(8,128)(2,1)S(1)} %get-tuple-element.84), channel_id=1, source_target_pairs={{0,6},{1,7},{2,4},{3,5},{4,2},{5,3},{6,0},{7,1},{8,14},{9,15},{10,... | collective-permute-start | bytes 393224 | tf_op jit(solution)/shard_map/ppermute | solution.py:387
  61.0 0.7 collective-permute-start.18
  61.7 1.3 %collective-permute-done.17.rest_2_ = bf16[4,128,128]{2,1,0:T(8,128)(2,1)S(1)} collective-permute-done((bf16[4,128,128]{2,1,0:T(8,128)(2,1)S(1)}, bf16[4,128,128]{2,1,0:T(8,128)(2,1)S(1)}, u32[]{:S(2)}, u32[]{:S(2)}) %collective-permute-start.17) | collective-permute-done | bytes 131104 | tf_op jit(solution)/shard_map/ppermute | solution.py:387
  63.0 1.5 %collective-permute-done.19.rest_4_ = bf16[4,128,128]{2,1,0:T(8,128)(2,1)S(1)} collective-permute-done((bf16[4,128,128]{2,1,0:T(8,128)(2,1)S(1)}, bf16[4,128,128]{2,1,0:T(8,128)(2,1)S(1)}, u32[]{:S(2)}, u32[]{:S(2)}) %collective-permute-start.19) | collective-permute-done | bytes 131104 | tf_op jit(solution)/shard_map/ppermute | solution.py:387
  64.5 0.3 collective-permute-start.22
  64.8 2.9 %collective-permute-done.21.rest_6_ = bf16[4,128,128]{2,1,0:T(8,128)(2,1)S(1)} collective-permute-done((bf16[4,128,128]{2,1,0:T(8,128)(2,1)S(1)}, bf16[4,128,128]{2,1,0:T(8,128)(2,1)S(1)}, u32[]{:S(2)}, u32[]{:S(2)}) %collective-permute-start.21) | collective-permute-done | bytes 131104 | tf_op jit(solution)/shard_map/ppermute | solution.py:387
  67.7 1.0 collective-permute-done.18.rest_3_
  68.7 0.1 collective-permute-done.20.rest_5_
  68.8 2.9 %collective-permute-done.22.rest_7_ = bf16[4,128,128]{2,1,0:T(8,128)(2,1)S(1)} collective-permute-done((bf16[4,128,128]{2,1,0:T(8,128)(2,1)S(1)}, bf16[4,128,128]{2,1,0:T(8,128)(2,1)S(1)}, u32[]{:S(2)}, u32[]{:S(2)}) %collective-permute-start.22) | collective-permute-done | bytes 131104 | tf_op jit(solution)/shard_map/ppermute | solution.py:387
  71.7 0.9 future_total.1
  72.6 1.3 %collective-permute-start.24 = (bf16[4,128,128]{2,1,0:T(8,128)(2,1)S(1)}, bf16[4,128,128]{2,1,0:T(8,128)(2,1)S(1)}, u32[]{:S(2)}, u32[]{:S(2)}) collective-permute-start(bf16[4,128,128]{2,1,0:T(8,128)(2,1)S(1)} %future_total.1), channel_id=1, source_target_pairs={{16,0},{24,8},{17,1},{25,9},{18,2},{26,10},{19,3},{27,11},{20,4},{... | collective-permute-start | bytes 393224 | tf_op jit(solution)/shard_map/ppermute | solution.py:409
  73.9 1.3 %collective-permute-start.23 = (bf16[4,128,128]{2,1,0:T(8,128)(2,1)S(1)}, bf16[4,128,128]{2,1,0:T(8,128)(2,1)S(1)}, u32[]{:S(2)}, u32[]{:S(2)}) collective-permute-start(bf16[4,128,128]{2,1,0:T(8,128)(2,1)S(1)} %future_total.1), channel_id=1, source_target_pairs={{8,0},{16,8},{24,16},{9,1},{17,9},{25,17},{10,2},{18,10},{26,18},{... | collective-permute-start | bytes 393224 | tf_op jit(solution)/shard_map/ppermute | solution.py:409
  75.2 7.4 %grads_within.1 = (bf16[128,4096]{1,0:T(8,128)(2,1)}, f32[128,4096]{1,0:T(8,128)}, f32[128,4096]{1,0:T(8,128)}) custom-call(s32[8]{0:T(128)S(1)} %copy-done, s32[3]{0:T(128)S(1)} %pad_add_fusion.place, bf16[128,4096]{1,0:T(8,128)(2,1)} %q.3, bf16[128,4096]{1,0:T(8,128)(2,1)} %k.11, bf16[128,4096]{1,0:T(8,128)(2,1)} %v.11, ...), custom_call_target="tpu_custom_call" | custom-call | flops 671088640 | bytes 11534336 | tf_op jit(solution)/shard_map/grads_within/pallas_call | solution.py:361
  82.6 1.2 %collective-permute-done.24.rest_10_ = bf16[4,128,128]{2,1,0:T(8,128)(2,1)S(1)} collective-permute-done((bf16[4,128,128]{2,1,0:T(8,128)(2,1)S(1)}, bf16[4,128,128]{2,1,0:T(8,128)(2,1)S(1)}, u32[]{:S(2)}, u32[]{:S(2)}) %collective-permute-start.24) | collective-permute-done | bytes 131104 | tf_op jit(solution)/shard_map/ppermute | solution.py:409
  83.8 0.8 collective-permute-done.23.rest_9_
  84.6 1.1 %future_prefix.1 = (bf16[4,128,128]{2,1,0:T(8,128)(2,1)S(1)}, bf16[4,128,128]{2,1,0:T(8,128)(2,1)S(1)}, bf16[4,128,128]{2,1,0:T(8,128)(2,1)S(1)}, bf16[4,128,128...) custom-call(s32[8]{0:T(128)S(1)} %copy-done, ...), custom_call_target="tpu_custom_call" | custom-call | flops 2097152 | bytes 2097152 | tf_op jit(solution)/shard_map/future_prefix/pallas_call | solution.py:361
  85.7 0.1 collective-permute-start.28
  85.8 2.0 %collective-permute-start.29 = (bf16[4,128,128]{2,1,0:T(8,128)(2,1)S(1)}, bf16[4,128,128]{2,1,0:T(8,128)(2,1)S(1)}, u32[]{:S(2)}, u32[]{:S(2)}) collective-permute-start(bf16[4,128,128]{2,1,0:T(8,128)(2,1)S(1)} %get-tuple-element.91), channel_id=1, source_target_pairs={{0,5},{1,4},{2,7},{3,6},{4,1},{5,0},{6,3},{7,2},{8,13},{9,12},{10,... | collective-permute-start | bytes 393224 | tf_op jit(solution)/shard_map/ppermute | solution.py:387
  87.8 0.6 collective-permute-start.30
  88.4 0.7 collective-permute-start.31
  89.1 1.1 %collective-permute-start.25 = (bf16[4,128,128]{2,1,0:T(8,128)(2,1)S(1)}, bf16[4,128,128]{2,1,0:T(8,128)(2,1)S(1)}, u32[]{:S(2)}, u32[]{:S(2)}) collective-permute-start(bf16[4,128,128]{2,1,0:T(8,128)(2,1)S(1)} %get-tuple-element.86), channel_id=1, source_target_pairs={{0,6},{1,7},{2,4},{3,5},{4,2},{5,3},{6,0},{7,1},{8,14},{9,15},{10,... | collective-permute-start | bytes 393224 | tf_op jit(solution)/shard_map/ppermute | solution.py:387
  90.2 2.4 %collective-permute-done.28.rest_0_ = bf16[4,128,128]{2,1,0:T(8,128)(2,1)S(1)} collective-permute-done((bf16[4,128,128]{2,1,0:T(8,128)(2,1)S(1)}, bf16[4,128,128]{2,1,0:T(8,128)(2,1)S(1)}, u32[]{:S(2)}, u32[]{:S(2)}) %collective-permute-start.28) | collective-permute-done | bytes 131104 | tf_op jit(solution)/shard_map/ppermute | solution.py:387
  92.6 0.3 collective-permute-start.26
  92.9 1.7 %collective-permute-done.29.rest_1_ = bf16[4,128,128]{2,1,0:T(8,128)(2,1)S(1)} collective-permute-done((bf16[4,128,128]{2,1,0:T(8,128)(2,1)S(1)}, bf16[4,128,128]{2,1,0:T(8,128)(2,1)S(1)}, u32[]{:S(2)}, u32[]{:S(2)}) %collective-permute-start.29) | collective-permute-done | bytes 131104 | tf_op jit(solution)/shard_map/ppermute | solution.py:387
  94.6 1.3 %collective-permute-start.27 = (bf16[4,128,128]{2,1,0:T(8,128)(2,1)S(1)}, bf16[4,128,128]{2,1,0:T(8,128)(2,1)S(1)}, u32[]{:S(2)}, u32[]{:S(2)}) collective-permute-start(bf16[4,128,128]{2,1,0:T(8,128)(2,1)S(1)} %get-tuple-element.88), channel_id=1, source_target_pairs={{0,2},{1,3},{2,0},{3,1},{4,6},{5,7},{6,4},{7,5},{8,10},{9,11},{10,... | collective-permute-start | bytes 393224 | tf_op jit(solution)/shard_map/ppermute | solution.py:387
  95.9 3.7 %grads_last_1.1 = (bf16[128,4096]{1,0:T(8,128)(2,1)}, bf16[128,4096]{1,0:T(8,128)(2,1)}) custom-call(s32[8]{0:T(128)S(1)} %copy-done, s32[3]{0:T(128)S(1)} %pad_add_fusion.place, bf16[128,4096]{1,0:T(8,128)(2,1)} %k.11, bf16[128,4096]{1,0:T(8,128)(2,1)} %v.11, f32[128,4096]{1,0:T(8,128)} %get-tuple-element.76.rest_8_.gk_part, ...), custom_call_target="tpu_custom_call" | custom-call | flops 134217728 | bytes 4718592 | tf_op jit(solution)/shard_map/grads_last_1/pallas_call | solution.py:361
  99.5 1.4 %collective-permute-done.27.rest_2_ = bf16[4,128,128]{2,1,0:T(8,128)(2,1)S(1)} collective-permute-done((bf16[4,128,128]{2,1,0:T(8,128)(2,1)S(1)}, bf16[4,128,128]{2,1,0:T(8,128)(2,1)S(1)}, u32[]{:S(2)}, u32[]{:S(2)}) %collective-permute-start.27) | collective-permute-done | bytes 131104 | tf_op jit(solution)/shard_map/ppermute | solution.py:387
  100.9 3.6 %grads_last_0.1 = (bf16[128,4096]{1,0:T(8,128)(2,1)}, bf16[128,4096]{1,0:T(8,128)(2,1)}) custom-call(s32[8]{0:T(128)S(1)} %copy-done, s32[3]{0:T(128)S(1)} %pad_add_fusion.place, bf16[128,4096]{1,0:T(8,128)(2,1)} %k.11, bf16[128,4096]{1,0:T(8,128)(2,1)} %v.11, ...), custom_call_target="tpu_custom_call", output_to_operand_aliasing={{0}: (10, {}), {1}: (11, {})} | custom-call | flops 134217728 | bytes 4718592 | tf_op jit(solution)/shard_map/grads_last_0/pallas_call | solution.py:361
  (15 shorter events, 0.0 us)
Async XLA Ops:
  0.7 0.7 copy-start
  4.0 9.1 %collective-permute-start = (bf16[4,128,128]{2,1,0:T(8,128)(2,1)S(1)}, bf16[4,128,128]{2,1,0:T(8,128)(2,1)S(1)}, u32[]{:S(2)}, u32[]{:S(2)}) collective-permute-start(bf16[4,128,128]{2,1,0:T(8,128)(2,1)S(1)} %get-tuple-element.55), channel_id=1, source_target_pairs={{0,1},{1,0},{2,3},{3,2},{4,5},{5,4},{6,7},{7,6},{8,9},{9,8},{10,11... | collective-permute-start | bytes 393224 | tf_op jit(solution)/shard_map/ppermute | solution.py:387
  4.5 10.0 %collective-permute-start.2 = (bf16[4,128,128]{2,1,0:T(8,128)(2,1)S(1)}, bf16[4,128,128]{2,1,0:T(8,128)(2,1)S(1)}, u32[]{:S(2)}, u32[]{:S(2)}) collective-permute-start(bf16[4,128,128]{2,1,0:T(8,128)(2,1)S(1)} %get-tuple-element.57), channel_id=1, source_target_pairs={{0,3},{1,2},{2,1},{3,0},{4,7},{5,6},{6,5},{7,4},{8,11},{9,10},{10,... | collective-permute-start | bytes 393224 | tf_op jit(solution)/shard_map/ppermute | solution.py:387
  7.2 7.5 %collective-permute-start.4 = (bf16[4,128,128]{2,1,0:T(8,128)(2,1)S(1)}, bf16[4,128,128]{2,1,0:T(8,128)(2,1)S(1)}, u32[]{:S(2)}, u32[]{:S(2)}) collective-permute-start(bf16[4,128,128]{2,1,0:T(8,128)(2,1)S(1)} %get-tuple-element.59), channel_id=1, source_target_pairs={{0,5},{1,4},{2,7},{3,6},{4,1},{5,0},{6,3},{7,2},{8,13},{9,12},{10,... | collective-permute-start | bytes 393224 | tf_op jit(solution)/shard_map/ppermute | solution.py:387
  8.3 6.7 %collective-permute-start.6 = (bf16[4,128,128]{2,1,0:T(8,128)(2,1)S(1)}, bf16[4,128,128]{2,1,0:T(8,128)(2,1)S(1)}, u32[]{:S(2)}, u32[]{:S(2)}) collective-permute-start(bf16[4,128,128]{2,1,0:T(8,128)(2,1)S(1)} %get-tuple-element.61), channel_id=1, source_target_pairs={{0,7},{1,6},{2,5},{3,4},{4,3},{5,2},{6,1},{7,0},{8,15},{9,14},{10,... | collective-permute-start | bytes 393224 | tf_op jit(solution)/shard_map/ppermute | solution.py:387
  11.0 7.5 %collective-permute-start.1 = (bf16[4,128,128]{2,1,0:T(8,128)(2,1)S(1)}, bf16[4,128,128]{2,1,0:T(8,128)(2,1)S(1)}, u32[]{:S(2)}, u32[]{:S(2)}) collective-permute-start(bf16[4,128,128]{2,1,0:T(8,128)(2,1)S(1)} %get-tuple-element.56), channel_id=1, source_target_pairs={{0,2},{1,3},{2,0},{3,1},{4,6},{5,7},{6,4},{7,5},{8,10},{9,11},{10,... | collective-permute-start | bytes 393224 | tf_op jit(solution)/shard_map/ppermute | solution.py:387
  13.1 6.4 %collective-permute-start.3 = (bf16[4,128,128]{2,1,0:T(8,128)(2,1)S(1)}, bf16[4,128,128]{2,1,0:T(8,128)(2,1)S(1)}, u32[]{:S(2)}, u32[]{:S(2)}) collective-permute-start(bf16[4,128,128]{2,1,0:T(8,128)(2,1)S(1)} %get-tuple-element.58), channel_id=1, source_target_pairs={{0,4},{1,5},{2,6},{3,7},{4,0},{5,1},{6,2},{7,3},{8,12},{9,13},{10,... | collective-permute-start | bytes 393224 | tf_op jit(solution)/shard_map/ppermute | solution.py:387
  14.6 6.3 %collective-permute-start.5 = (bf16[4,128,128]{2,1,0:T(8,128)(2,1)S(1)}, bf16[4,128,128]{2,1,0:T(8,128)(2,1)S(1)}, u32[]{:S(2)}, u32[]{:S(2)}) collective-permute-start(bf16[4,128,128]{2,1,0:T(8,128)(2,1)S(1)} %get-tuple-element.60), channel_id=1, source_target_pairs={{0,6},{1,7},{2,4},{3,5},{4,2},{5,3},{6,0},{7,1},{8,14},{9,15},{10,... | collective-permute-start | bytes 393224 | tf_op jit(solution)/shard_map/ppermute | solution.py:387
  21.8 15.1 %collective-permute-start.8 = (bf16[4,128,128]{2,1,0:T(8,128)(2,1)S(1)}, bf16[4,128,128]{2,1,0:T(8,128)(2,1)S(1)}, u32[]{:S(2)}, u32[]{:S(2)}) collective-permute-start(bf16[4,128,128]{2,1,0:T(8,128)(2,1)S(1)} %carried_total.1), channel_id=1, source_target_pairs={{0,16},{8,24},{1,17},{9,25},{2,18},{10,26},{3,19},{11,27},{4,20},{... | collective-permute-start | bytes 393224 | tf_op jit(solution)/shard_map/ppermute | solution.py:409
  26.7 10.1 %collective-permute-start.7 = (bf16[4,128,128]{2,1,0:T(8,128)(2,1)S(1)}, bf16[4,128,128]{2,1,0:T(8,128)(2,1)S(1)}, u32[]{:S(2)}, u32[]{:S(2)}) collective-permute-start(bf16[4,128,128]{2,1,0:T(8,128)(2,1)S(1)} %carried_total.1), channel_id=1, source_target_pairs={{0,8},{8,16},{16,24},{1,9},{9,17},{17,25},{2,10},{10,18},{18,26},{... | collective-permute-start | bytes 393224 | tf_op jit(solution)/shard_map/ppermute | solution.py:409
  38.0 6.8 %collective-permute-start.12 = (bf16[4,128,128]{2,1,0:T(8,128)(2,1)S(1)}, bf16[4,128,128]{2,1,0:T(8,128)(2,1)S(1)}, u32[]{:S(2)}, u32[]{:S(2)}) collective-permute-start(bf16[4,128,128]{2,1,0:T(8,128)(2,1)S(1)} %get-tuple-element.66), channel_id=1, source_target_pairs={{0,7},{1,6},{2,5},{3,4},{4,3},{5,2},{6,1},{7,0},{8,15},{9,14},{10,... | collective-permute-start | bytes 393224 | tf_op jit(solution)/shard_map/ppermute | solution.py:387
  38.7 8.1 %collective-permute-start.13 = (bf16[4,128,128]{2,1,0:T(8,128)(2,1)S(1)}, bf16[4,128,128]{2,1,0:T(8,128)(2,1)S(1)}, u32[]{:S(2)}, u32[]{:S(2)}) collective-permute-start(bf16[4,128,128]{2,1,0:T(8,128)(2,1)S(1)} %get-tuple-element.67), channel_id=1, source_target_pairs={{0,5},{1,4},{2,7},{3,6},{4,1},{5,0},{6,3},{7,2},{8,13},{9,12},{10,... | collective-permute-start | bytes 393224 | tf_op jit(solution)/shard_map/ppermute | solution.py:387
  40.8 7.3 %collective-permute-start.14 = (bf16[4,128,128]{2,1,0:T(8,128)(2,1)S(1)}, bf16[4,128,128]{2,1,0:T(8,128)(2,1)S(1)}, u32[]{:S(2)}, u32[]{:S(2)}) collective-permute-start(bf16[4,128,128]{2,1,0:T(8,128)(2,1)S(1)} %get-tuple-element.68), channel_id=1, source_target_pairs={{0,3},{1,2},{2,1},{3,0},{4,7},{5,6},{6,5},{7,4},{8,11},{9,10},{10,... | collective-permute-start | bytes 393224 | tf_op jit(solution)/shard_map/ppermute | solution.py:387
  40.9 7.2 %collective-permute-start.15 = (bf16[4,128,128]{2,1,0:T(8,128)(2,1)S(1)}, bf16[4,128,128]{2,1,0:T(8,128)(2,1)S(1)}, u32[]{:S(2)}, u32[]{:S(2)}) collective-permute-start(bf16[4,128,128]{2,1,0:T(8,128)(2,1)S(1)} %get-tuple-element.69), channel_id=1, source_target_pairs={{0,1},{1,0},{2,3},{3,2},{4,5},{5,4},{6,7},{7,6},{8,9},{9,8},{10,11... | collective-permute-start | bytes 393224 | tf_op jit(solution)/shard_map/ppermute | solution.py:387
  41.4 11.0 %collective-permute-start.9 = (bf16[4,128,128]{2,1,0:T(8,128)(2,1)S(1)}, bf16[4,128,128]{2,1,0:T(8,128)(2,1)S(1)}, u32[]{:S(2)}, u32[]{:S(2)}) collective-permute-start(bf16[4,128,128]{2,1,0:T(8,128)(2,1)S(1)} %get-tuple-element.62), channel_id=1, source_target_pairs={{0,6},{1,7},{2,4},{3,5},{4,2},{5,3},{6,0},{7,1},{8,14},{9,15},{10,... | collective-permute-start | bytes 393224 | tf_op jit(solution)/shard_map/ppermute | solution.py:387
  44.8 7.6 %collective-permute-start.10 = (bf16[4,128,128]{2,1,0:T(8,128)(2,1)S(1)}, bf16[4,128,128]{2,1,0:T(8,128)(2,1)S(1)}, u32[]{:S(2)}, u32[]{:S(2)}) collective-permute-start(bf16[4,128,128]{2,1,0:T(8,128)(2,1)S(1)} %get-tuple-element.63), channel_id=1, source_target_pairs={{0,4},{1,5},{2,6},{3,7},{4,0},{5,1},{6,2},{7,3},{8,12},{9,13},{10,... | collective-permute-start | bytes 393224 | tf_op jit(solution)/shard_map/ppermute | solution.py:387
  46.8 6.4 %collective-permute-start.11 = (bf16[4,128,128]{2,1,0:T(8,128)(2,1)S(1)}, bf16[4,128,128]{2,1,0:T(8,128)(2,1)S(1)}, u32[]{:S(2)}, u32[]{:S(2)}) collective-permute-start(bf16[4,128,128]{2,1,0:T(8,128)(2,1)S(1)} %get-tuple-element.64), channel_id=1, source_target_pairs={{0,2},{1,3},{2,0},{3,1},{4,6},{5,7},{6,4},{7,5},{8,10},{9,11},{10,... | collective-permute-start | bytes 393224 | tf_op jit(solution)/shard_map/ppermute | solution.py:387
  57.5 5.5 %collective-permute-start.17 = (bf16[4,128,128]{2,1,0:T(8,128)(2,1)S(1)}, bf16[4,128,128]{2,1,0:T(8,128)(2,1)S(1)}, u32[]{:S(2)}, u32[]{:S(2)}) collective-permute-start(bf16[4,128,128]{2,1,0:T(8,128)(2,1)S(1)} %get-tuple-element.80), channel_id=1, source_target_pairs={{0,2},{1,3},{2,0},{3,1},{4,6},{5,7},{6,4},{7,5},{8,10},{9,11},{10,... | collective-permute-start | bytes 393224 | tf_op jit(solution)/shard_map/ppermute | solution.py:387
  58.1 6.4 %collective-permute-start.19 = (bf16[4,128,128]{2,1,0:T(8,128)(2,1)S(1)}, bf16[4,128,128]{2,1,0:T(8,128)(2,1)S(1)}, u32[]{:S(2)}, u32[]{:S(2)}) collective-permute-start(bf16[4,128,128]{2,1,0:T(8,128)(2,1)S(1)} %get-tuple-element.82), channel_id=1, source_target_pairs={{0,4},{1,5},{2,6},{3,7},{4,0},{5,1},{6,2},{7,3},{8,12},{9,13},{10,... | collective-permute-start | bytes 393224 | tf_op jit(solution)/shard_map/ppermute | solution.py:387
  59.3 8.5 %collective-permute-start.21 = (bf16[4,128,128]{2,1,0:T(8,128)(2,1)S(1)}, bf16[4,128,128]{2,1,0:T(8,128)(2,1)S(1)}, u32[]{:S(2)}, u32[]{:S(2)}) collective-permute-start(bf16[4,128,128]{2,1,0:T(8,128)(2,1)S(1)} %get-tuple-element.84), channel_id=1, source_target_pairs={{0,6},{1,7},{2,4},{3,5},{4,2},{5,3},{6,0},{7,1},{8,14},{9,15},{10,... | collective-permute-start | bytes 393224 | tf_op jit(solution)/shard_map/ppermute | solution.py:387
  61.0 6.8 %collective-permute-start.16 = (bf16[4,128,128]{2,1,0:T(8,128)(2,1)S(1)}, bf16[4,128,128]{2,1,0:T(8,128)(2,1)S(1)}, u32[]{:S(2)}, u32[]{:S(2)}) collective-permute-start(bf16[4,128,128]{2,1,0:T(8,128)(2,1)S(1)} %get-tuple-element.79), channel_id=1, source_target_pairs={{0,1},{1,0},{2,3},{3,2},{4,5},{5,4},{6,7},{7,6},{8,9},{9,8},{10,11... | collective-permute-start | bytes 393224 | tf_op jit(solution)/shard_map/ppermute | solution.py:387
  61.0 7.7 %collective-permute-start.18 = (bf16[4,128,128]{2,1,0:T(8,128)(2,1)S(1)}, bf16[4,128,128]{2,1,0:T(8,128)(2,1)S(1)}, u32[]{:S(2)}, u32[]{:S(2)}) collective-permute-start(bf16[4,128,128]{2,1,0:T(8,128)(2,1)S(1)} %get-tuple-element.81), channel_id=1, source_target_pairs={{0,3},{1,2},{2,1},{3,0},{4,7},{5,6},{6,5},{7,4},{8,11},{9,10},{10,... | collective-permute-start | bytes 393224 | tf_op jit(solution)/shard_map/ppermute | solution.py:387
  63.0 5.9 %collective-permute-start.20 = (bf16[4,128,128]{2,1,0:T(8,128)(2,1)S(1)}, bf16[4,128,128]{2,1,0:T(8,128)(2,1)S(1)}, u32[]{:S(2)}, u32[]{:S(2)}) collective-permute-start(bf16[4,128,128]{2,1,0:T(8,128)(2,1)S(1)} %get-tuple-element.83), channel_id=1, source_target_pairs={{0,5},{1,4},{2,7},{3,6},{4,1},{5,0},{6,3},{7,2},{8,13},{9,12},{10,... | collective-permute-start | bytes 393224 | tf_op jit(solution)/shard_map/ppermute | solution.py:387
  64.5 7.2 %collective-permute-start.22 = (bf16[4,128,128]{2,1,0:T(8,128)(2,1)S(1)}, bf16[4,128,128]{2,1,0:T(8,128)(2,1)S(1)}, u32[]{:S(2)}, u32[]{:S(2)}) collective-permute-start(bf16[4,128,128]{2,1,0:T(8,128)(2,1)S(1)} %get-tuple-element.85), channel_id=1, source_target_pairs={{0,7},{1,6},{2,5},{3,4},{4,3},{5,2},{6,1},{7,0},{8,15},{9,14},{10,... | collective-permute-start | bytes 393224 | tf_op jit(solution)/shard_map/ppermute | solution.py:387
  72.6 11.2 %collective-permute-start.24 = (bf16[4,128,128]{2,1,0:T(8,128)(2,1)S(1)}, bf16[4,128,128]{2,1,0:T(8,128)(2,1)S(1)}, u32[]{:S(2)}, u32[]{:S(2)}) collective-permute-start(bf16[4,128,128]{2,1,0:T(8,128)(2,1)S(1)} %future_total.1), channel_id=1, source_target_pairs={{16,0},{24,8},{17,1},{25,9},{18,2},{26,10},{19,3},{27,11},{20,4},{... | collective-permute-start | bytes 393224 | tf_op jit(solution)/shard_map/ppermute | solution.py:409
  73.9 10.7 %collective-permute-start.23 = (bf16[4,128,128]{2,1,0:T(8,128)(2,1)S(1)}, bf16[4,128,128]{2,1,0:T(8,128)(2,1)S(1)}, u32[]{:S(2)}, u32[]{:S(2)}) collective-permute-start(bf16[4,128,128]{2,1,0:T(8,128)(2,1)S(1)} %future_total.1), channel_id=1, source_target_pairs={{8,0},{16,8},{24,16},{9,1},{17,9},{25,17},{10,2},{18,10},{26,18},{... | collective-permute-start | bytes 393224 | tf_op jit(solution)/shard_map/ppermute | solution.py:409
  85.7 6.9 %collective-permute-start.28 = (bf16[4,128,128]{2,1,0:T(8,128)(2,1)S(1)}, bf16[4,128,128]{2,1,0:T(8,128)(2,1)S(1)}, u32[]{:S(2)}, u32[]{:S(2)}) collective-permute-start(bf16[4,128,128]{2,1,0:T(8,128)(2,1)S(1)} %get-tuple-element.90), channel_id=1, source_target_pairs={{0,7},{1,6},{2,5},{3,4},{4,3},{5,2},{6,1},{7,0},{8,15},{9,14},{10,... | collective-permute-start | bytes 393224 | tf_op jit(solution)/shard_map/ppermute | solution.py:387
  85.8 8.8 %collective-permute-start.29 = (bf16[4,128,128]{2,1,0:T(8,128)(2,1)S(1)}, bf16[4,128,128]{2,1,0:T(8,128)(2,1)S(1)}, u32[]{:S(2)}, u32[]{:S(2)}) collective-permute-start(bf16[4,128,128]{2,1,0:T(8,128)(2,1)S(1)} %get-tuple-element.91), channel_id=1, source_target_pairs={{0,5},{1,4},{2,7},{3,6},{4,1},{5,0},{6,3},{7,2},{8,13},{9,12},{10,... | collective-permute-start | bytes 393224 | tf_op jit(solution)/shard_map/ppermute | solution.py:387
  87.8 8.1 %collective-permute-start.30 = (bf16[4,128,128]{2,1,0:T(8,128)(2,1)S(1)}, bf16[4,128,128]{2,1,0:T(8,128)(2,1)S(1)}, u32[]{:S(2)}, u32[]{:S(2)}) collective-permute-start(bf16[4,128,128]{2,1,0:T(8,128)(2,1)S(1)} %get-tuple-element.92), channel_id=1, source_target_pairs={{0,3},{1,2},{2,1},{3,0},{4,7},{5,6},{6,5},{7,4},{8,11},{9,10},{10,... | collective-permute-start | bytes 393224 | tf_op jit(solution)/shard_map/ppermute | solution.py:387
  88.4 7.5 %collective-permute-start.31 = (bf16[4,128,128]{2,1,0:T(8,128)(2,1)S(1)}, bf16[4,128,128]{2,1,0:T(8,128)(2,1)S(1)}, u32[]{:S(2)}, u32[]{:S(2)}) collective-permute-start(bf16[4,128,128]{2,1,0:T(8,128)(2,1)S(1)} %get-tuple-element.93), channel_id=1, source_target_pairs={{0,1},{1,0},{2,3},{3,2},{4,5},{5,4},{6,7},{7,6},{8,9},{9,8},{10,11... | collective-permute-start | bytes 393224 | tf_op jit(solution)/shard_map/ppermute | solution.py:387
  89.1 10.4 %collective-permute-start.25 = (bf16[4,128,128]{2,1,0:T(8,128)(2,1)S(1)}, bf16[4,128,128]{2,1,0:T(8,128)(2,1)S(1)}, u32[]{:S(2)}, u32[]{:S(2)}) collective-permute-start(bf16[4,128,128]{2,1,0:T(8,128)(2,1)S(1)} %get-tuple-element.86), channel_id=1, source_target_pairs={{0,6},{1,7},{2,4},{3,5},{4,2},{5,3},{6,0},{7,1},{8,14},{9,15},{10,... | collective-permute-start | bytes 393224 | tf_op jit(solution)/shard_map/ppermute | solution.py:387
  92.6 7.0 %collective-permute-start.26 = (bf16[4,128,128]{2,1,0:T(8,128)(2,1)S(1)}, bf16[4,128,128]{2,1,0:T(8,128)(2,1)S(1)}, u32[]{:S(2)}, u32[]{:S(2)}) collective-permute-start(bf16[4,128,128]{2,1,0:T(8,128)(2,1)S(1)} %get-tuple-element.87), channel_id=1, source_target_pairs={{0,4},{1,5},{2,6},{3,7},{4,0},{5,1},{6,2},{7,3},{8,12},{9,13},{10,... | collective-permute-start | bytes 393224 | tf_op jit(solution)/shard_map/ppermute | solution.py:387
  94.6 6.3 %collective-permute-start.27 = (bf16[4,128,128]{2,1,0:T(8,128)(2,1)S(1)}, bf16[4,128,128]{2,1,0:T(8,128)(2,1)S(1)}, u32[]{:S(2)}, u32[]{:S(2)}) collective-permute-start(bf16[4,128,128]{2,1,0:T(8,128)(2,1)S(1)} %get-tuple-element.88), channel_id=1, source_target_pairs={{0,2},{1,3},{2,0},{3,1},{4,6},{5,7},{6,4},{7,5},{8,10},{9,11},{10,... | collective-permute-start | bytes 393224 | tf_op jit(solution)/shard_map/ppermute | solution.py:387

commit v7 on v6

--- a/solution.py
+++ b/solution.py
@@ -90,30 +90,18 @@
     return jnp.concatenate([high, (wide - high.astype(F32)).astype(BF16)], axis=1)
 
 
-def slot(place, n, owned):
-    return pl.ds(((place[2] ^ n) >> 1) * owned, owned)
-
-
-def tail_kernel(ns, lens, place, k, v, *rest):
-    outs, kept = rest[:-1], rest[-1]
+def tail_kernel(lens, place, k, v, out):
     count = k.shape[0]
-    heads = k.shape[1] // DH
-    step = pl.program_id(0)
     tail = tail_mask(doc_ends(lens), place[0] * count, count)
     eye = identity(DH)
-    for hs in bunches(heads):
+    for hs in bunches(out.shape[0]):
         fks = [
             jnp.where(tail, feature(k[:, cols(h)].astype(F32)), 0.0).astype(BF16) for h in hs
         ]
         turned = [turn(fk, eye) for fk in fks]
         sums = [mul(fk, v[:, cols(h)], NN).astype(BF16) for h, fk in zip(hs, turned)]
         for h, value in zip(hs, sums):
-            kept[step * heads + h] = value
-
-    @pl.when(step == pl.num_programs(0) - 1)
-    def _():
-        for n, out in zip(ns, outs):
-            out[...] = kept[slot(place, n, out.shape[0])]
+            out[h] = value
 
 
 def local_kernel(lens, place, q, k, v, scores, part, head_fq, turned):
@@ -143,24 +131,12 @@
             turned[h] = t
 
 
-def norm_kernel(ns, filled, lens, place, head_fq, turned, g, part, *rest):
-    size = len(ns)
-    incoming, rest = rest[:size], rest[size + filled :]
-    out, grad_att, outs, (came, kept) = rest[0], rest[1], rest[2:-2], rest[-2:]
+def norm_kernel(lens, place, head_fq, turned, g, part, incoming, *rest):
+    out, grad_att, state = rest[-3:]
     count = g.shape[0]
-    heads = turned.shape[0]
-    step = pl.program_id(0)
-
-    @pl.when(step == 0)
-    def _():
-        for n, state in zip(ns, incoming):
-            came[slot(place, n, state.shape[0])] = state[...]
-
     weights = jnp.full((2 * DH, DH), 1.0 / DH, BF16)
-    for hs in bunches(heads):
-        atts = [
-            part[:, cols(h)] + mul(head_fq[:, cols(h)], came[step * heads + h], NN) for h in hs
-        ]
+    for hs in bunches(state.shape[0]):
+        atts = [part[:, cols(h)] + mul(head_fq[:, cols(h)], incoming[h], NN) for h in hs]
         gos = [g[:, cols(h)].astype(F32) for h in hs]
         means = [
             mul(jnp.concatenate([halves(att * att), halves(go * att)], axis=0), weights, NN)
@@ -176,27 +152,20 @@
         for h, normed, ga, value in zip(hs, norms, gas, sums):
             out[:, cols(h)] = normed.astype(BF16)
             grad_att[:, cols(h)] = ga
-            kept[step * heads + h] = value
-
-    @pl.when(step == pl.num_programs(0) - 1)
-    def _():
-        for n, state in zip(ns, outs):
-            state[...] = kept[slot(place, n, state.shape[0])]
-
-
-def inner_kernel(lens, place, q, k, v, grad_att, scores, *rest):
-    states, (gq, gk, gv, came) = rest[:-4], rest[-4:]
+            state[h] = value
+
+
+def inner_kernel(lens, place, q, k, v, grad_att, scores, mine, other, gq, gk, gv, came):
     count = q.shape[0]
     heads = scores.shape[0]
     step = pl.program_id(0)
 
     @pl.when(step == 0)
     def _():
-        for n, state in enumerate(states):
-            owned = state.shape[0]
-            owner = place[2] ^ n
-            turn = (owner & 1) * (len(states) // 2) + (owner >> 1)
-            came[pl.ds(turn * owned, owned)] = state[...]
+        half = mine.shape[0]
+        core = place[2] & 1
+        came[pl.ds(core * half, half)] = mine[...]
+        came[pl.ds((1 - core) * half, half)] = other[...]
 
     ends = doc_ends(lens)
     first = place[0] * count
@@ -227,25 +196,16 @@
             gv[:, cols(h)] = b
 
 
-def last_kernel(ns, filled, lens, place, k, v, gk_part, gv_part, *rest):
-    size = len(ns)
-    outgoing, (gk, gv, came) = rest[:size], rest[size + filled :]
+def last_kernel(lens, place, k, v, gk_part, gv_part, outgoing, *rest):
+    gk, gv = rest[-2:]
     count = k.shape[0]
-    heads = k.shape[1] // DH
-    step = pl.program_id(0)
-
-    @pl.when(step == 0)
-    def _():
-        for n, state in zip(ns, outgoing):
-            came[slot(place, n, state.shape[0])] = state[...]
-
     tail = tail_mask(doc_ends(lens), place[0] * count, count)
-    for hs in bunches(heads):
+    for hs in bunches(outgoing.shape[0]):
         wides = [k[:, cols(h)].astype(F32) for h in hs]
         fks = [jnp.where(tail, feature(wide), 0.0).astype(BF16) for wide in wides]
         vts = [jnp.where(tail, v[:, cols(h)].astype(F32), 0.0).astype(BF16) for h in hs]
-        gks = [gk_part[:, cols(h)] + mul(vt, came[step * heads + h], NT) for h, vt in zip(hs, vts)]
-        gvs = [gv_part[:, cols(h)] + mul(fk, came[step * heads + h], NN) for h, fk in zip(hs, fks)]
+        gks = [gk_part[:, cols(h)] + mul(vt, outgoing[h], NT) for h, vt in zip(hs, vts)]
+        gvs = [gv_part[:, cols(h)] + mul(fk, outgoing[h], NN) for h, fk in zip(hs, fks)]
         for h, a, wide, b in zip(hs, gks, wides, gvs):
             gk[:, cols(h)] = (a * slope(wide)).astype(BF16)
             gv[:, cols(h)] = b.astype(BF16)
@@ -255,18 +215,58 @@
     return jnp.where(a == b, 1.0, 0.0).astype(F32)
 
 
-def total_kernel(forward, count, lens, place, *rest):
+def chip_docs(lens, place, count):
+    ends = doc_ends(lens)
+    core = place[2] & 1
+    start = (place[0] - core) * count
+    marks = (start, start + count - 1, start + count, start + 2 * count - 1)
+    return core, [doc_at(ends, mark) for mark in marks]
+
+
+def merge_kernel(forward, count, lens, place, mine, other, *outs):
+    core, (early_b, early_e, late_b, late_e) = chip_docs(lens, place, count)
+    far = same(early_e, late_e) if forward else same(early_b, late_b)
+    i_am_far = (core == 0) if forward else (core == 1)
+    mine_by = jnp.where(i_am_far, far, 1.0)
+    other_by = jnp.where(i_am_far, 1.0, far)
+    chip = place[2] >> 1
+    for n, out in enumerate(outs):
+        at = chip ^ n
+        out[...] = (mine[at].astype(F32) * mine_by + other[at].astype(F32) * other_by).astype(
+            BF16
+        )
+
+
+def form_kernel(forward, count, lens, place, *rest):
+    came, (mine, other, own_in, mate_in) = rest[:-4], rest[-4:]
+    core, (early_b, early_e, late_b, late_e) = chip_docs(lens, place, count)
+    if forward:
+        by_came, by_near, i_am_near = same(late_b, early_b), same(late_b, early_e), core == 1
+    else:
+        by_came, by_near, i_am_near = same(early_e, late_e), same(early_e, late_b), core == 0
+    chip = place[2] >> 1
+    for n, state in enumerate(came):
+        at = chip ^ n
+        total = state[...].astype(F32)
+        near = jnp.where(i_am_near, other[at].astype(F32), mine[at].astype(F32))
+        both = total * by_came + near * by_near
+        own_in[at] = jnp.where(i_am_near, both, total).astype(BF16)
+        mate_in[at] = jnp.where(i_am_near, total, both).astype(BF16)
+
+
+def total_kernel(forward, unit, lens, place, *rest):
     states, total, held = rest[:-2], rest[-2], rest[-1]
     members = len(states)
+    chip = place[2] >> 1
     for n, state in enumerate(states):
-        held[place[2] ^ n] = state[...]
+        held[chip ^ n] = state[...]
     ends = doc_ends(lens)
-    layer = place[1] * (members * count)
+    layer = place[1] * (members * unit)
     carry = None
     for step in range(members):
         i = step if forward else members - 1 - step
         mine = held[i].astype(F32)
-        edge = layer + ((i + 1) * count - 1 if forward else i * count)
+        edge = layer + ((i + 1) * unit - 1 if forward else i * unit)
         here = doc_at(ends, edge)
         if carry is not None:
             mine = mine + carry * same(here, previous)
@@ -274,12 +274,13 @@
     total[...] = carry.astype(BF16)
 
 
-def prefix_kernel(forward, count, members, lens, place, *rest):
+def prefix_kernel(forward, unit, members, lens, place, *rest):
     states, outs, (held, sums) = rest[:members], rest[-members - 2 : -2], rest[-2:]
     others = rest[members + 1 : -members - 2]
+    chip = place[2] >> 1
     for n, state in enumerate(states):
-        held[place[2] ^ n] = state[...]
-    span = members * count
+        held[chip ^ n] = state[...]
+    span = members * unit
     ends = doc_ends(lens)
     layer = place[1] * span
     sign = -1 if forward else 1
@@ -292,7 +293,7 @@
         carry = term if carry is None else carry + term
     for step in range(members):
         i = step if forward else members - 1 - step
-        near, far = layer + i * count, layer + (i + 1) * count - 1
+        near, far = layer + i * unit, layer + (i + 1) * unit - 1
         if not forward:
             near, far = far, near
         if carry is None:
@@ -306,7 +307,7 @@
                 mine = mine + carry * same(here, previous)
             carry, previous = mine, here
     for n, out in enumerate(outs):
-        out[...] = sums[place[2] ^ n]
+        out[...] = sums[chip ^ n]
 
 
 SMALL = pltpu.CompilerParams(
@@ -324,8 +325,7 @@
     place = jnp.stack(
         [lax.axis_index(("z", "x", "head")), lax.axis_index("z"), lax.axis_index(LAYER)]
     ).astype(jnp.int32)
-    same_core = [n for n in reversed(range(members)) if n % 2 == 0]
-    other_core = [n for n in reversed(range(members)) if n % 2 == 1]
+    chips = members // 2
     step_heads = max(n for n in (8, 4, 2, 1) if half % n == 0)
     steps = half // step_heads
 
@@ -345,17 +345,21 @@
         block = at(parity)
         return pl.BlockSpec((step_heads, rows, columns), lambda *a: (block(*a), 0, 0))
 
-    whole = pl.BlockSpec((owned, DH, DH), lambda *a: (0, 0, 0))
+    whole = pl.BlockSpec((half, DH, DH), lambda *a: (0, 0, 0))
+    halved = pl.BlockSpec((step_heads, DH, DH), lambda i, *a: (i, 0, 0))
     untouched = pl.BlockSpec(memory_space=pl.ANY)
     token_bf = pltpu.HBM((count, width), BF16)
     token_f32 = pltpu.HBM((count, width), F32)
     tile_bf = pltpu.HBM((heads, count, count), BF16)
     turned_bf = pltpu.HBM((heads, DH, count), BF16)
     owned_bf = jax.ShapeDtypeStruct((owned, DH, DH), BF16)
+    half_bf = jax.ShapeDtypeStruct((half, DH, DH), BF16)
+    chips_bf = jax.ShapeDtypeStruct((chips, owned, DH, DH), BF16)
 
     def run(kernel, grid, ins, outs, shapes, scratch, args, cost, name, params=SMALL, aliases={}):
         args = [
-            arg if arg.shape == (owned, DH, DH) else held_in_hbm(arg) for arg in args
+            arg if arg.shape[-2:] == (DH, DH) and arg.size <= half * DH * DH else held_in_hbm(arg)
+            for arg in args
         ]
         flops, moved, exps = cost
         return pl.pallas_call(
@@ -378,25 +382,45 @@
 
     product = 2 * half * count * DH * DH
     array = half * count * DH * 2
-    half_states = pltpu.VMEM((half, DH, DH), BF16)
     all_states = pltpu.VMEM((heads, DH, DH), BF16)
+    block = 2 if owned % 2 == 0 else 1
+    single = pl.BlockSpec((block, DH, DH), lambda i, *a: (i, 0, 0))
+    grouped = pl.BlockSpec((chips, block, DH, DH), lambda i, *a: (0, i, 0, 0))
+    buffer = pltpu.VMEM((chips, block, DH, DH), BF16)
+    combining = (4 * half * DH * DH, 4 * half * DH * DH, 0)
+    moves = owned // block
+
+    def swap(state):
+        return lax.ppermute(state, LAYER, [(i, i ^ 1) for i in range(members)])
 
     def exchange(states):
-        pairs = {n: [(i, i ^ n) for i in range(members)] for n in states}
-        return {
-            n: state if n == 0 else lax.ppermute(state, LAYER, pairs[n])
-            for n, state in states.items()
-        }
-
-    def gather(states, forward, name):
-        came = exchange(states)
-        came = [came[n] for n in range(members)]
+        pairs = [[(i, i ^ (2 * n)) for i in range(members)] for n in range(chips)]
+        return [
+            state if n == 0 else lax.ppermute(state, LAYER, pairs[n])
+            for n, state in enumerate(states)
+        ]
+
+    def gather(mine, theirs, forward, name):
+        mine = mine.reshape(chips, owned, DH, DH)
+        other = swap(theirs).reshape(chips, owned, DH, DH)
+        merged = run(
+            functools.partial(merge_kernel, forward, count),
+            moves,
+            [grouped] * 2,
+            [single] * chips,
+            [owned_bf] * chips,
+            [],
+            (mine, other),
+            combining,
+            name + "_chip",
+        )
+        came = exchange(merged)
         others = []
         if layers > 1:
             (total,) = run(
-                functools.partial(total_kernel, forward, count),
-                owned // block,
-                [single] * members,
+                functools.partial(total_kernel, forward, 2 * count),
+                moves,
+                [single] * chips,
                 [single],
                 [owned_bf],
                 [buffer],
@@ -407,42 +431,47 @@
             for s in reach:
                 pairs = [(i, i + s) if forward else (i + s, i) for i in range(layers - s)]
                 others.append(lax.ppermute(total, "z", pairs))
-        return came, others
-
-    def spread(came, others, after, forward, name):
+        return mine, other, came, others
+
+    def spread(mine, other, came, others, after, forward, name):
         sums = run(
-            functools.partial(prefix_kernel, forward, count, members),
-            owned // block,
-            [single] * members + [untouched] + [single] * len(others),
-            [single] * members,
-            [owned_bf] * members,
+            functools.partial(prefix_kernel, forward, 2 * count, chips),
+            moves,
+            [single] * chips + [untouched] + [single] * len(others),
+            [single] * chips,
+            [owned_bf] * chips,
             [buffer, buffer],
             [*came, after, *others],
             combining,
             name + "_prefix",
         )
-        return exchange({n: sums[n] for n in other_core + same_core})
-
-    block = 2 if owned % 2 == 0 else 1
-    single = pl.BlockSpec((block, DH, DH), lambda i, *a: (i, 0, 0))
-    buffer = pltpu.VMEM((members, block, DH, DH), BF16)
-    combining = (4 * heads * DH * DH, 4 * heads * DH * DH, 0)
-    groups = ((1, other_core), (0, same_core))
-    tail = {}
-    for parity, ns in groups:
-        outs = run(
-            functools.partial(tail_kernel, ns),
+        own_in, mate_in = run(
+            functools.partial(form_kernel, forward, count),
+            moves,
+            [single] * chips + [grouped] * 2,
+            [grouped] * 2,
+            [chips_bf] * 2,
+            [],
+            [*exchange(sums), mine, other],
+            combining,
+            name + "_device",
+        )
+        return own_in.reshape(half, DH, DH), swap(mate_in.reshape(half, DH, DH))
+
+    tail = [None, None]
+    for parity in (1, 0):
+        (tail[parity],) = run(
+            tail_kernel,
             steps,
             [tokens(parity)] * 2,
-            [whole] * len(ns),
-            [owned_bf] * len(ns),
-            [half_states],
+            [halved],
+            [half_bf],
+            [],
             (keys, values),
             (product, 3 * array, half * count * DH),
             f"tail_{parity}",
         )
-        tail.update(zip(ns, outs))
-    came, others = gather(tail, True, "carried")
+    scan = gather(*tail, True, "carried")
     scores, part, head_fq, turned = run(
         local_kernel,
         2 * steps,
@@ -454,53 +483,51 @@
         (4 * product, 16 * array, 4 * half * count * DH),
         "within",
     )
-    incoming = spread(came, others, part, True, "carried")
-    head_state, made = {}, ()
-    for parity, ns in groups:
-        outs = run(
-            functools.partial(norm_kernel, ns, len(made)),
+    incoming = spread(*scan, part, True, "carried")
+    head_state, made = [None, None], ()
+    for parity in (0, 1):
+        *made_now, head_state[parity] = run(
+            norm_kernel,
             steps,
-            [tokens(parity), tiles(parity, DH, count), tokens(parity), tokens(parity)]
-            + [whole] * len(ns)
+            [tokens(parity), tiles(parity, DH, count), tokens(parity), tokens(parity), halved]
             + [untouched] * len(made),
-            [tokens(parity)] * 2 + [whole] * len(ns),
-            [token_bf] * 2 + [owned_bf] * len(ns),
-            [half_states, half_states],
-            (head_fq, turned, out_grad, part, *[incoming[n] for n in ns], *made),
+            [tokens(parity)] * 2 + [halved],
+            [token_bf] * 2 + [half_bf],
+            [],
+            (head_fq, turned, out_grad, part, incoming[parity], *made),
             (4 * product, 9 * array, half * count * DH),
             f"normed_{parity}",
-            aliases={6 + len(ns) + j: j for j in range(len(made))},
-        )
-        made = tuple(outs[:2])
-        head_state.update(zip(ns, outs[2:]))
+            aliases={7 + j: j for j in range(len(made))},
+        )
+        made = tuple(made_now)
     attn_out, grad_att = made
-    came, others = gather(head_state, False, "future")
+    scan = gather(*head_state, False, "future")
     grad_queries, gk_part, gv_part = run(
         inner_kernel,
         2 * steps,
-        [tokens(None)] * 4 + [tiles(None, count, count)] + [whole] * members,
+        [tokens(None)] * 4 + [tiles(None, count, count)] + [whole] * 2,
         [tokens(None)] * 3,
         [token_bf, token_f32, token_f32],
         [all_states],
-        (queries, keys, values, grad_att, scores, *[incoming[n] for n in range(members)]),
+        (queries, keys, values, grad_att, scores, *incoming),
         (10 * product, 22 * array, 4 * half * count * DH),
         "grads_within",
     )
-    outgoing = spread(came, others, gk_part, False, "future")
+    outgoing = spread(*scan, gk_part, False, "future")
     made = ()
-    for parity, ns in groups:
+    for parity in (0, 1):
         made = tuple(
             run(
-                functools.partial(last_kernel, ns, len(made)),
+                last_kernel,
                 steps,
-                [tokens(parity)] * 4 + [whole] * len(ns) + [untouched] * len(made),
+                [tokens(parity)] * 4 + [halved] + [untouched] * len(made),
                 [tokens(parity)] * 2,
                 [token_bf] * 2,
-                [half_states],
-                (keys, values, gk_part, gv_part, *[outgoing[n] for n in ns], *made),
+                [],
+                (keys, values, gk_part, gv_part, outgoing[parity], *made),
                 (2 * product, 9 * array, half * count * DH),
                 f"grads_last_{parity}",
-                aliases={6 + len(ns) + j: j for j in range(len(made))},
+                aliases={7 + j: j for j in range(len(made))},
             )
         )
     return attn_out, grad_queries, *made

time: 105 us -> 97.8 us (0.931)
  starting transfers between devices: 38.2 us -> 26.7 us
  Pallas kernels: 39.2 us -> 42.4 us
    ppermute x28 -> x12, starting transfers between devices: 27.2 us -> 14.8 us  [exchange(): lax.ppermute(state, LAYER, pairs[n])]
    pallas_call x12 -> x16, Pallas kernels: 39.2 us -> 42.4 us  [run(): pl.pallas_call(kernel, grid_spec=pltpu.PrefetchScalarGridSpec(num_scalar_...]
    ppermute x0 -> x4, waiting for transfers between devices: none -> 1.54 us  [swap(): return lax.ppermute(state, LAYER, [(i, i ^ 1) for i in range(members)])]
    ppermute x4, waiting for transfers between devices: 2 us -> 0.61 us  [gather(): others.append(lax.ppermute(total, 'z', pairs))]
    ppermute x0 -> x4, starting transfers between devices: none -> 1.14 us  [swap(): return lax.ppermute(state, LAYER, [(i, i ^ 1) for i in range(members)])]
    ppermute x28 -> x12, waiting for transfers between devices: 23.8 us -> 23.6 us  [exchange(): lax.ppermute(state, LAYER, pairs[n])]
  transfers between devices with their start and end apart: 32 -> 20, of which waited for: 18 -> 15; matrix products, arithmetic and copies ran while one was open for 0% -> 0% of each run, Pallas kernels for 24% -> 25%
where the time goes in v7:
time: 97.8 us; the launch traced here: 96.3 us
  Pallas kernels  42.4 us (43%)
  starting transfers between devices  26.7 us (27%)
  waiting for transfers between devices  25.8 us (26%)
    pallas_call x16, Pallas kernels, run(): pl.pallas_call(kernel, grid_spec=pltpu.PrefetchScalarGridSpec(num_scalar_...  42.4 us
    ppermute x12, waiting for transfers between devices, exchange(): lax.ppermute(state, LAYER, pairs[n])  23.6 us
    ppermute x12, starting transfers between devices, exchange(): lax.ppermute(state, LAYER, pairs[n])  14.8 us
    ppermute x4, starting transfers between devices, gather(): others.append(lax.ppermute(total, 'z', pairs))  10.7 us
  transfers between devices with their start and end apart: 20, of which 15 were waited for; matrix products, arithmetic and copies ran while one was open for 0% of the time, Pallas kernels for 25%

profile of v7, /device:TPU:0, one launch (start us, length us, event | category | flops | bytes accessed | tf_op | source)
XLA Modules:
  0.0 96.3 jit_solution(12446955351227370268)
XLA Ops:
  0.6 0.1 pad_add_fusion.place
  0.7 0.0 copy-start
  0.7 0.7 copy-done
  1.4 2.6 %tail_1.1 = bf16[16,128,128]{2,1,0:T(8,128)(2,1)S(1)} custom-call(s32[8]{0:T(128)S(1)} %copy-done, s32[3]{0:T(128)S(1)} %pad_add_fusion.place, bf16[128,4096]{1,0:T(8,128)(2,1)} %k.11, bf16[128,4096]{1,0:T(8,128)(2,1)} %v.11), custom_call_target="tpu_custom_call" | custom-call | flops 67108864 | bytes 1572864 | tf_op jit(solution)/shard_map/tail_1/pallas_call | solution.py:365
  4.0 0.5 collective-permute-start
  4.5 2.6 %tail_0.1 = bf16[16,128,128]{2,1,0:T(8,128)(2,1)S(1)} custom-call(s32[8]{0:T(128)S(1)} %copy-done, s32[3]{0:T(128)S(1)} %pad_add_fusion.place, bf16[128,4096]{1,0:T(8,128)(2,1)} %k.11, bf16[128,4096]{1,0:T(8,128)(2,1)} %v.11), custom_call_target="tpu_custom_call" | custom-call | flops 67108864 | bytes 1572864 | tf_op jit(solution)/shard_map/tail_0/pallas_call | solution.py:365
  7.1 0.0 collective-permute-done
  7.1 0.9 carried_chip.1
  8.0 2.6 %collective-permute-start.1 = (bf16[4,128,128]{2,1,0:T(8,128)(2,1)S(1)}, bf16[4,128,128]{2,1,0:T(8,128)(2,1)S(1)}, u32[]{:S(2)}, u32[]{:S(2)}) collective-permute-start(bf16[4,128,128]{2,1,0:T(8,128)(2,1)S(1)} %get-tuple-element.45), channel_id=1, source_target_pairs={{0,2},{1,3},{2,0},{3,1},{4,6},{5,7},{6,4},{7,5},{8,10},{9,11},{10,... | collective-permute-start | bytes 393224 | tf_op jit(solution)/shard_map/ppermute | solution.py:399
  10.6 1.5 %collective-permute-start.2 = (bf16[4,128,128]{2,1,0:T(8,128)(2,1)S(1)}, bf16[4,128,128]{2,1,0:T(8,128)(2,1)S(1)}, u32[]{:S(2)}, u32[]{:S(2)}) collective-permute-start(bf16[4,128,128]{2,1,0:T(8,128)(2,1)S(1)} %get-tuple-element.46), channel_id=1, source_target_pairs={{0,4},{1,5},{2,6},{3,7},{4,0},{5,1},{6,2},{7,3},{8,12},{9,13},{10,... | collective-permute-start | bytes 393224 | tf_op jit(solution)/shard_map/ppermute | solution.py:399
  12.1 0.0 collective-permute-start.3
  12.2 2.6 %collective-permute-done.1.rest_1_ = bf16[4,128,128]{2,1,0:T(8,128)(2,1)S(1)} collective-permute-done((bf16[4,128,128]{2,1,0:T(8,128)(2,1)S(1)}, bf16[4,128,128]{2,1,0:T(8,128)(2,1)S(1)}, u32[]{:S(2)}, u32[]{:S(2)}) %collective-permute-start.1) | collective-permute-done | bytes 131104 | tf_op jit(solution)/shard_map/ppermute | solution.py:399
  14.8 2.2 %collective-permute-done.2.rest_2_ = bf16[4,128,128]{2,1,0:T(8,128)(2,1)S(1)} collective-permute-done((bf16[4,128,128]{2,1,0:T(8,128)(2,1)S(1)}, bf16[4,128,128]{2,1,0:T(8,128)(2,1)S(1)}, u32[]{:S(2)}, u32[]{:S(2)}) %collective-permute-start.2) | collective-permute-done | bytes 131104 | tf_op jit(solution)/shard_map/ppermute | solution.py:399
  17.0 1.9 %collective-permute-done.3.rest_3_ = bf16[4,128,128]{2,1,0:T(8,128)(2,1)S(1)} collective-permute-done((bf16[4,128,128]{2,1,0:T(8,128)(2,1)S(1)}, bf16[4,128,128]{2,1,0:T(8,128)(2,1)S(1)}, u32[]{:S(2)}, u32[]{:S(2)}) %collective-permute-start.3) | collective-permute-done | bytes 131104 | tf_op jit(solution)/shard_map/ppermute | solution.py:399
  18.8 0.7 carried_total.1
  19.6 4.6 %collective-permute-start.5 = (bf16[4,128,128]{2,1,0:T(8,128)(2,1)S(1)}, bf16[4,128,128]{2,1,0:T(8,128)(2,1)S(1)}, u32[]{:S(2)}, u32[]{:S(2)}) collective-permute-start(bf16[4,128,128]{2,1,0:T(8,128)(2,1)S(1)} %carried_total.1), channel_id=1, source_target_pairs={{0,16},{8,24},{1,17},{9,25},{2,18},{10,26},{3,19},{11,27},{4,20},{... | collective-permute-start | bytes 393224 | tf_op jit(solution)/shard_map/ppermute | solution.py:433
  24.3 3.5 %collective-permute-start.4 = (bf16[4,128,128]{2,1,0:T(8,128)(2,1)S(1)}, bf16[4,128,128]{2,1,0:T(8,128)(2,1)S(1)}, u32[]{:S(2)}, u32[]{:S(2)}) collective-permute-start(bf16[4,128,128]{2,1,0:T(8,128)(2,1)S(1)} %carried_total.1), channel_id=1, source_target_pairs={{0,8},{8,16},{16,24},{1,9},{9,17},{17,25},{2,10},{10,18},{18,26},{... | collective-permute-start | bytes 393224 | tf_op jit(solution)/shard_map/ppermute | solution.py:433
  27.7 6.6 %within.1 = (bf16[32,128,128]{2,1,0:T(8,128)(2,1)}, f32[128,4096]{1,0:T(8,128)}, bf16[128,4096]{1,0:T(8,128)(2,1)}, bf16[32,128,128]{2,1,0:T(8,128)(2,1)}) custom-call(s32[8]{0:T(128)S(1)} %copy-done, s32[3]{0:T(128)S(1)} %pad_add_fusion.place, bf16[128,4096]{1,0:T(8,128)(2,1)} %q.3, bf16[128,4096]{1,0:T(8,128)(2,1)} %k.11, bf16[128,4096]{1,0:T(8,128)(2,1)} %v.11), custom_call_target="tpu_custom_call" | custom-call | flops 268435456 | bytes 8388608 | tf_op jit(solution)/shard_map/within/pallas_call | solution.py:365
  34.4 0.0 collective-permute-done.5.rest_6_
  34.4 0.0 collective-permute-done.4.rest_5_
  34.4 0.9 carried_prefix.1
  35.3 1.6 %collective-permute-start.6 = (bf16[4,128,128]{2,1,0:T(8,128)(2,1)S(1)}, bf16[4,128,128]{2,1,0:T(8,128)(2,1)S(1)}, u32[]{:S(2)}, u32[]{:S(2)}) collective-permute-start(bf16[4,128,128]{2,1,0:T(8,128)(2,1)S(1)} %get-tuple-element.49), channel_id=1, source_target_pairs={{0,2},{1,3},{2,0},{3,1},{4,6},{5,7},{6,4},{7,5},{8,10},{9,11},{10,... | collective-permute-start | bytes 393224 | tf_op jit(solution)/shard_map/ppermute | solution.py:399
  36.9 1.5 %collective-permute-start.7 = (bf16[4,128,128]{2,1,0:T(8,128)(2,1)S(1)}, bf16[4,128,128]{2,1,0:T(8,128)(2,1)S(1)}, u32[]{:S(2)}, u32[]{:S(2)}) collective-permute-start(bf16[4,128,128]{2,1,0:T(8,128)(2,1)S(1)} %get-tuple-element.50), channel_id=1, source_target_pairs={{0,4},{1,5},{2,6},{3,7},{4,0},{5,1},{6,2},{7,3},{8,12},{9,13},{10,... | collective-permute-start | bytes 393224 | tf_op jit(solution)/shard_map/ppermute | solution.py:399
  38.4 0.5 collective-permute-start.8
  38.8 2.0 %collective-permute-done.6.rest_1_ = bf16[4,128,128]{2,1,0:T(8,128)(2,1)S(1)} collective-permute-done((bf16[4,128,128]{2,1,0:T(8,128)(2,1)S(1)}, bf16[4,128,128]{2,1,0:T(8,128)(2,1)S(1)}, u32[]{:S(2)}, u32[]{:S(2)}) %collective-permute-start.6) | collective-permute-done | bytes 131104 | tf_op jit(solution)/shard_map/ppermute | solution.py:399
  40.8 1.5 %collective-permute-done.7.rest_2_ = bf16[4,128,128]{2,1,0:T(8,128)(2,1)S(1)} collective-permute-done((bf16[4,128,128]{2,1,0:T(8,128)(2,1)S(1)}, bf16[4,128,128]{2,1,0:T(8,128)(2,1)S(1)}, u32[]{:S(2)}, u32[]{:S(2)}) %collective-permute-start.7) | collective-permute-done | bytes 131104 | tf_op jit(solution)/shard_map/ppermute | solution.py:399
  42.3 2.1 %collective-permute-done.8.rest_3_ = bf16[4,128,128]{2,1,0:T(8,128)(2,1)S(1)} collective-permute-done((bf16[4,128,128]{2,1,0:T(8,128)(2,1)S(1)}, bf16[4,128,128]{2,1,0:T(8,128)(2,1)S(1)}, u32[]{:S(2)}, u32[]{:S(2)}) %collective-permute-start.8) | collective-permute-done | bytes 131104 | tf_op jit(solution)/shard_map/ppermute | solution.py:399
  44.3 1.3 %carried_device.1 = (bf16[4,4,128,128]{3,2,1,0:T(8,128)(2,1)S(1)}, bf16[4,4,128,128]{3,2,1,0:T(8,128)(2,1)S(1)}) custom-call(s32[8]{0:T(128)S(1)} %copy-done, s32[3]{0:T(128)S(1)} %pad_add_fusion.place, bf16[4,128,128]{2,1,0:T(8,128)(2,1)S(1)} %get-tuple-element.48.rest_0_, bf16[4,128,128]{2,1,0:T(8,128)(2,1)S(1)} %collective-permute-done.6.rest_1_, ...), custom_call_target="tpu_custom_call" | custom-call | flops 1048576 | bytes 1048576 | tf_op jit(solution)/shard_map/carried_device/pallas_call | solution.py:365
  45.6 0.1 collective-permute-start.9
  45.7 4.1 %normed_0.1 = (bf16[128,4096]{1,0:T(8,128)(2,1)}, bf16[128,4096]{1,0:T(8,128)(2,1)}, bf16[16,128,128]{2,1,0:T(8,128)(2,1)S(1)}) custom-call(s32[8]{0:T(128)S(1)} %copy-done, s32[3]{0:T(128)S(1)} %pad_add_fusion.place, bf16[128,4096]{1,0:T(8,128)(2,1)} %get-tuple-element.41.head_fq, bf16[32,128,128]{2,1,0:T(8,128)(2,1)} %get-tuple-element.42.turned, ...), custom_call_target="tpu_custom_call" | custom-call | flops 268435456 | bytes 4718592 | tf_op jit(solution)/shard_map/normed_0/pallas_call | solution.py:365
  49.8 0.0 collective-permute-done.9.incoming.other
  49.8 4.1 %normed_1.1 = (bf16[128,4096]{1,0:T(8,128)(2,1)}, bf16[128,4096]{1,0:T(8,128)(2,1)}, bf16[16,128,128]{2,1,0:T(8,128)(2,1)S(1)}) custom-call(s32[8]{0:T(128)S(1)} %copy-done, s32[3]{0:T(128)S(1)} %pad_add_fusion.place, bf16[128,4096]{1,0:T(8,128)(2,1)} %get-tuple-element.41.head_fq, ...), custom_call_target="tpu_custom_call", output_to_operand_aliasing={{0}: (7, {}), {1}: (8, {})} | custom-call | flops 268435456 | bytes 4718592 | tf_op jit(solution)/shard_map/normed_1/pallas_call | solution.py:365
  53.9 0.5 collective-permute-start.10
  54.3 1.5 %collective-permute-done.10 = bf16[16,128,128]{2,1,0:T(8,128)(2,1)S(1)} collective-permute-done((bf16[16,128,128]{2,1,0:T(8,128)(2,1)S(1)}, bf16[16,128,128]{2,1,0:T(8,128)(2,1)S(1)}, u32[]{:S(2)}, u32[]{:S(2)}) %collective-permute-start.10) | collective-permute-done | bytes 524320 | tf_op jit(solution)/shard_map/ppermute | solution.py:394
  55.9 0.9 future_chip.1
  56.8 0.9 collective-permute-start.11
  57.7 1.5 %collective-permute-start.12 = (bf16[4,128,128]{2,1,0:T(8,128)(2,1)S(1)}, bf16[4,128,128]{2,1,0:T(8,128)(2,1)S(1)}, u32[]{:S(2)}, u32[]{:S(2)}) collective-permute-start(bf16[4,128,128]{2,1,0:T(8,128)(2,1)S(1)} %get-tuple-element.66), channel_id=1, source_target_pairs={{0,4},{1,5},{2,6},{3,7},{4,0},{5,1},{6,2},{7,3},{8,12},{9,13},{10,... | collective-permute-start | bytes 393224 | tf_op jit(solution)/shard_map/ppermute | solution.py:399
  59.2 1.2 %collective-permute-start.13 = (bf16[4,128,128]{2,1,0:T(8,128)(2,1)S(1)}, bf16[4,128,128]{2,1,0:T(8,128)(2,1)S(1)}, u32[]{:S(2)}, u32[]{:S(2)}) collective-permute-start(bf16[4,128,128]{2,1,0:T(8,128)(2,1)S(1)} %get-tuple-element.67), channel_id=1, source_target_pairs={{0,6},{1,7},{2,4},{3,5},{4,2},{5,3},{6,0},{7,1},{8,14},{9,15},{10,... | collective-permute-start | bytes 393224 | tf_op jit(solution)/shard_map/ppermute | solution.py:399
  60.4 2.3 %collective-permute-done.11.rest_1_ = bf16[4,128,128]{2,1,0:T(8,128)(2,1)S(1)} collective-permute-done((bf16[4,128,128]{2,1,0:T(8,128)(2,1)S(1)}, bf16[4,128,128]{2,1,0:T(8,128)(2,1)S(1)}, u32[]{:S(2)}, u32[]{:S(2)}) %collective-permute-start.11) | collective-permute-done | bytes 131104 | tf_op jit(solution)/shard_map/ppermute | solution.py:399
  62.7 1.4 %collective-permute-done.12.rest_2_ = bf16[4,128,128]{2,1,0:T(8,128)(2,1)S(1)} collective-permute-done((bf16[4,128,128]{2,1,0:T(8,128)(2,1)S(1)}, bf16[4,128,128]{2,1,0:T(8,128)(2,1)S(1)}, u32[]{:S(2)}, u32[]{:S(2)}) %collective-permute-start.12) | collective-permute-done | bytes 131104 | tf_op jit(solution)/shard_map/ppermute | solution.py:399
  64.0 2.6 %collective-permute-done.13.rest_3_ = bf16[4,128,128]{2,1,0:T(8,128)(2,1)S(1)} collective-permute-done((bf16[4,128,128]{2,1,0:T(8,128)(2,1)S(1)}, bf16[4,128,128]{2,1,0:T(8,128)(2,1)S(1)}, u32[]{:S(2)}, u32[]{:S(2)}) %collective-permute-start.13) | collective-permute-done | bytes 131104 | tf_op jit(solution)/shard_map/ppermute | solution.py:399
  66.6 0.7 future_total.1
  67.4 1.3 %collective-permute-start.15 = (bf16[4,128,128]{2,1,0:T(8,128)(2,1)S(1)}, bf16[4,128,128]{2,1,0:T(8,128)(2,1)S(1)}, u32[]{:S(2)}, u32[]{:S(2)}) collective-permute-start(bf16[4,128,128]{2,1,0:T(8,128)(2,1)S(1)} %future_total.1), channel_id=1, source_target_pairs={{16,0},{24,8},{17,1},{25,9},{18,2},{26,10},{19,3},{27,11},{20,4},{... | collective-permute-start | bytes 393224 | tf_op jit(solution)/shard_map/ppermute | solution.py:433
  68.7 1.3 %collective-permute-start.14 = (bf16[4,128,128]{2,1,0:T(8,128)(2,1)S(1)}, bf16[4,128,128]{2,1,0:T(8,128)(2,1)S(1)}, u32[]{:S(2)}, u32[]{:S(2)}) collective-permute-start(bf16[4,128,128]{2,1,0:T(8,128)(2,1)S(1)} %future_total.1), channel_id=1, source_target_pairs={{8,0},{16,8},{24,16},{9,1},{17,9},{25,17},{10,2},{18,10},{26,18},{... | collective-permute-start | bytes 393224 | tf_op jit(solution)/shard_map/ppermute | solution.py:433
  70.0 7.4 %grads_within.1 = (bf16[128,4096]{1,0:T(8,128)(2,1)}, f32[128,4096]{1,0:T(8,128)}, f32[128,4096]{1,0:T(8,128)}) custom-call(s32[8]{0:T(128)S(1)} %copy-done, s32[3]{0:T(128)S(1)} %pad_add_fusion.place, bf16[128,4096]{1,0:T(8,128)(2,1)} %q.3, bf16[128,4096]{1,0:T(8,128)(2,1)} %k.11, bf16[128,4096]{1,0:T(8,128)(2,1)} %v.11, ...), custom_call_target="tpu_custom_call" | custom-call | flops 671088640 | bytes 11534336 | tf_op jit(solution)/shard_map/grads_within/pallas_call | solution.py:365
  77.4 0.3 collective-permute-done.15.rest_6_
  77.7 0.3 collective-permute-done.14.rest_5_
  78.0 0.9 future_prefix.1
  78.9 0.9 collective-permute-start.16
  79.8 1.5 %collective-permute-start.17 = (bf16[4,128,128]{2,1,0:T(8,128)(2,1)S(1)}, bf16[4,128,128]{2,1,0:T(8,128)(2,1)S(1)}, u32[]{:S(2)}, u32[]{:S(2)}) collective-permute-start(bf16[4,128,128]{2,1,0:T(8,128)(2,1)S(1)} %get-tuple-element.70), channel_id=1, source_target_pairs={{0,4},{1,5},{2,6},{3,7},{4,0},{5,1},{6,2},{7,3},{8,12},{9,13},{10,... | collective-permute-start | bytes 393224 | tf_op jit(solution)/shard_map/ppermute | solution.py:399
  81.3 1.2 %collective-permute-start.18 = (bf16[4,128,128]{2,1,0:T(8,128)(2,1)S(1)}, bf16[4,128,128]{2,1,0:T(8,128)(2,1)S(1)}, u32[]{:S(2)}, u32[]{:S(2)}) collective-permute-start(bf16[4,128,128]{2,1,0:T(8,128)(2,1)S(1)} %get-tuple-element.71), channel_id=1, source_target_pairs={{0,6},{1,7},{2,4},{3,5},{4,2},{5,3},{6,0},{7,1},{8,14},{9,15},{10,... | collective-permute-start | bytes 393224 | tf_op jit(solution)/shard_map/ppermute | solution.py:399
  82.5 2.5 %collective-permute-done.16.rest_1_ = bf16[4,128,128]{2,1,0:T(8,128)(2,1)S(1)} collective-permute-done((bf16[4,128,128]{2,1,0:T(8,128)(2,1)S(1)}, bf16[4,128,128]{2,1,0:T(8,128)(2,1)S(1)}, u32[]{:S(2)}, u32[]{:S(2)}) %collective-permute-start.16) | collective-permute-done | bytes 131104 | tf_op jit(solution)/shard_map/ppermute | solution.py:399
  85.0 0.5 collective-permute-done.17.rest_2_
  85.5 2.1 %collective-permute-done.18.rest_3_ = bf16[4,128,128]{2,1,0:T(8,128)(2,1)S(1)} collective-permute-done((bf16[4,128,128]{2,1,0:T(8,128)(2,1)S(1)}, bf16[4,128,128]{2,1,0:T(8,128)(2,1)S(1)}, u32[]{:S(2)}, u32[]{:S(2)}) %collective-permute-start.18) | collective-permute-done | bytes 131104 | tf_op jit(solution)/shard_map/ppermute | solution.py:399
  87.6 1.3 %future_device.1 = (bf16[4,4,128,128]{3,2,1,0:T(8,128)(2,1)S(1)}, bf16[4,4,128,128]{3,2,1,0:T(8,128)(2,1)S(1)}) custom-call(s32[8]{0:T(128)S(1)} %copy-done, s32[3]{0:T(128)S(1)} %pad_add_fusion.place, bf16[4,128,128]{2,1,0:T(8,128)(2,1)S(1)} %get-tuple-element.68.rest_0_, bf16[4,128,128]{2,1,0:T(8,128)(2,1)S(1)} %collective-permute-done.16.rest_1_, ...), custom_call_target="tpu_custom_call" | custom-call | flops 1048576 | bytes 1048576 | tf_op jit(solution)/shard_map/future_device/pallas_call | solution.py:365
  88.9 0.1 collective-permute-start.19
  89.0 3.7 %grads_last_0.1 = (bf16[128,4096]{1,0:T(8,128)(2,1)}, bf16[128,4096]{1,0:T(8,128)(2,1)}) custom-call(s32[8]{0:T(128)S(1)} %copy-done, s32[3]{0:T(128)S(1)} %pad_add_fusion.place, bf16[128,4096]{1,0:T(8,128)(2,1)} %k.11, bf16[128,4096]{1,0:T(8,128)(2,1)} %v.11, f32[128,4096]{1,0:T(8,128)} %get-tuple-element.60.rest_4_.gk_part, ...), custom_call_target="tpu_custom_call" | custom-call | flops 134217728 | bytes 4718592 | tf_op jit(solution)/shard_map/grads_last_0/pallas_call | solution.py:365
  92.7 0.0 collective-permute-done.19.outgoing
  92.7 3.7 %grads_last_1.1 = (bf16[128,4096]{1,0:T(8,128)(2,1)}, bf16[128,4096]{1,0:T(8,128)(2,1)}) custom-call(s32[8]{0:T(128)S(1)} %copy-done, s32[3]{0:T(128)S(1)} %pad_add_fusion.place, bf16[128,4096]{1,0:T(8,128)(2,1)} %k.11, bf16[128,4096]{1,0:T(8,128)(2,1)} %v.11, ...), custom_call_target="tpu_custom_call", output_to_operand_aliasing={{0}: (7, {}), {1}: (8, {})} | custom-call | flops 134217728 | bytes 4718592 | tf_op jit(solution)/shard_map/grads_last_1/pallas_call | solution.py:365
Async XLA Ops:
  0.7 0.7 copy-start
  4.0 3.1 %collective-permute-start = (bf16[16,128,128]{2,1,0:T(8,128)(2,1)S(1)}, bf16[16,128,128]{2,1,0:T(8,128)(2,1)S(1)}, u32[]{:S(2)}, u32[]{:S(2)}) collective-permute-start(bf16[16,128,128]{2,1,0:T(8,128)(2,1)S(1)} %tail_1.1), channel_id=1, source_target_pairs={{0,1},{1,0},{2,3},{3,2},{4,5},{5,4},{6,7},{7,6},{8,9},{9,8},{10,11... | collective-permute-start | bytes 1572872 | tf_op jit(solution)/shard_map/ppermute | solution.py:394
  8.0 6.8 %collective-permute-start.1 = (bf16[4,128,128]{2,1,0:T(8,128)(2,1)S(1)}, bf16[4,128,128]{2,1,0:T(8,128)(2,1)S(1)}, u32[]{:S(2)}, u32[]{:S(2)}) collective-permute-start(bf16[4,128,128]{2,1,0:T(8,128)(2,1)S(1)} %get-tuple-element.45), channel_id=1, source_target_pairs={{0,2},{1,3},{2,0},{3,1},{4,6},{5,7},{6,4},{7,5},{8,10},{9,11},{10,... | collective-permute-start | bytes 393224 | tf_op jit(solution)/shard_map/ppermute | solution.py:399
  10.6 6.3 %collective-permute-start.2 = (bf16[4,128,128]{2,1,0:T(8,128)(2,1)S(1)}, bf16[4,128,128]{2,1,0:T(8,128)(2,1)S(1)}, u32[]{:S(2)}, u32[]{:S(2)}) collective-permute-start(bf16[4,128,128]{2,1,0:T(8,128)(2,1)S(1)} %get-tuple-element.46), channel_id=1, source_target_pairs={{0,4},{1,5},{2,6},{3,7},{4,0},{5,1},{6,2},{7,3},{8,12},{9,13},{10,... | collective-permute-start | bytes 393224 | tf_op jit(solution)/shard_map/ppermute | solution.py:399
  12.1 6.7 %collective-permute-start.3 = (bf16[4,128,128]{2,1,0:T(8,128)(2,1)S(1)}, bf16[4,128,128]{2,1,0:T(8,128)(2,1)S(1)}, u32[]{:S(2)}, u32[]{:S(2)}) collective-permute-start(bf16[4,128,128]{2,1,0:T(8,128)(2,1)S(1)} %get-tuple-element.47), channel_id=1, source_target_pairs={{0,6},{1,7},{2,4},{3,5},{4,2},{5,3},{6,0},{7,1},{8,14},{9,15},{10,... | collective-permute-start | bytes 393224 | tf_op jit(solution)/shard_map/ppermute | solution.py:399
  19.6 14.8 %collective-permute-start.5 = (bf16[4,128,128]{2,1,0:T(8,128)(2,1)S(1)}, bf16[4,128,128]{2,1,0:T(8,128)(2,1)S(1)}, u32[]{:S(2)}, u32[]{:S(2)}) collective-permute-start(bf16[4,128,128]{2,1,0:T(8,128)(2,1)S(1)} %carried_total.1), channel_id=1, source_target_pairs={{0,16},{8,24},{1,17},{9,25},{2,18},{10,26},{3,19},{11,27},{4,20},{... | collective-permute-start | bytes 393224 | tf_op jit(solution)/shard_map/ppermute | solution.py:433
  24.3 10.1 %collective-permute-start.4 = (bf16[4,128,128]{2,1,0:T(8,128)(2,1)S(1)}, bf16[4,128,128]{2,1,0:T(8,128)(2,1)S(1)}, u32[]{:S(2)}, u32[]{:S(2)}) collective-permute-start(bf16[4,128,128]{2,1,0:T(8,128)(2,1)S(1)} %carried_total.1), channel_id=1, source_target_pairs={{0,8},{8,16},{16,24},{1,9},{9,17},{17,25},{2,10},{10,18},{18,26},{... | collective-permute-start | bytes 393224 | tf_op jit(solution)/shard_map/ppermute | solution.py:433
  35.3 5.5 %collective-permute-start.6 = (bf16[4,128,128]{2,1,0:T(8,128)(2,1)S(1)}, bf16[4,128,128]{2,1,0:T(8,128)(2,1)S(1)}, u32[]{:S(2)}, u32[]{:S(2)}) collective-permute-start(bf16[4,128,128]{2,1,0:T(8,128)(2,1)S(1)} %get-tuple-element.49), channel_id=1, source_target_pairs={{0,2},{1,3},{2,0},{3,1},{4,6},{5,7},{6,4},{7,5},{8,10},{9,11},{10,... | collective-permute-start | bytes 393224 | tf_op jit(solution)/shard_map/ppermute | solution.py:399
  36.9 5.4 %collective-permute-start.7 = (bf16[4,128,128]{2,1,0:T(8,128)(2,1)S(1)}, bf16[4,128,128]{2,1,0:T(8,128)(2,1)S(1)}, u32[]{:S(2)}, u32[]{:S(2)}) collective-permute-start(bf16[4,128,128]{2,1,0:T(8,128)(2,1)S(1)} %get-tuple-element.50), channel_id=1, source_target_pairs={{0,4},{1,5},{2,6},{3,7},{4,0},{5,1},{6,2},{7,3},{8,12},{9,13},{10,... | collective-permute-start | bytes 393224 | tf_op jit(solution)/shard_map/ppermute | solution.py:399
  38.4 6.0 %collective-permute-start.8 = (bf16[4,128,128]{2,1,0:T(8,128)(2,1)S(1)}, bf16[4,128,128]{2,1,0:T(8,128)(2,1)S(1)}, u32[]{:S(2)}, u32[]{:S(2)}) collective-permute-start(bf16[4,128,128]{2,1,0:T(8,128)(2,1)S(1)} %get-tuple-element.51), channel_id=1, source_target_pairs={{0,6},{1,7},{2,4},{3,5},{4,2},{5,3},{6,0},{7,1},{8,14},{9,15},{10,... | collective-permute-start | bytes 393224 | tf_op jit(solution)/shard_map/ppermute | solution.py:399
  45.6 4.1 %collective-permute-start.9 = (bf16[16,128,128]{2,1,0:T(8,128)(2,1)S(1)}, bf16[16,128,128]{2,1,0:T(8,128)(2,1)S(1)}, u32[]{:S(2)}, u32[]{:S(2)}) collective-permute-start(bf16[16,128,128]{2,1,0:T(8,128)(2,1)S(1)} %bitcast.22), channel_id=1, source_target_pairs={{0,1},{1,0},{2,3},{3,2},{4,5},{5,4},{6,7},{7,6},{8,9},{9,8},{10,11... | collective-permute-start | bytes 1572872 | tf_op jit(solution)/shard_map/ppermute | solution.py:394
  53.9 2.0 %collective-permute-start.10 = (bf16[16,128,128]{2,1,0:T(8,128)(2,1)S(1)}, bf16[16,128,128]{2,1,0:T(8,128)(2,1)S(1)}, u32[]{:S(2)}, u32[]{:S(2)}) collective-permute-start(bf16[16,128,128]{2,1,0:T(8,128)(2,1)S(1)} %get-tuple-element.63), channel_id=1, source_target_pairs={{0,1},{1,0},{2,3},{3,2},{4,5},{5,4},{6,7},{7,6},{8,9},{9,8},{10,11... | collective-permute-start | bytes 1572872 | tf_op jit(solution)/shard_map/ppermute | solution.py:394
  56.8 5.8 %collective-permute-start.11 = (bf16[4,128,128]{2,1,0:T(8,128)(2,1)S(1)}, bf16[4,128,128]{2,1,0:T(8,128)(2,1)S(1)}, u32[]{:S(2)}, u32[]{:S(2)}) collective-permute-start(bf16[4,128,128]{2,1,0:T(8,128)(2,1)S(1)} %get-tuple-element.65), channel_id=1, source_target_pairs={{0,2},{1,3},{2,0},{3,1},{4,6},{5,7},{6,4},{7,5},{8,10},{9,11},{10,... | collective-permute-start | bytes 393224 | tf_op jit(solution)/shard_map/ppermute | solution.py:399
  57.7 6.4 %collective-permute-start.12 = (bf16[4,128,128]{2,1,0:T(8,128)(2,1)S(1)}, bf16[4,128,128]{2,1,0:T(8,128)(2,1)S(1)}, u32[]{:S(2)}, u32[]{:S(2)}) collective-permute-start(bf16[4,128,128]{2,1,0:T(8,128)(2,1)S(1)} %get-tuple-element.66), channel_id=1, source_target_pairs={{0,4},{1,5},{2,6},{3,7},{4,0},{5,1},{6,2},{7,3},{8,12},{9,13},{10,... | collective-permute-start | bytes 393224 | tf_op jit(solution)/shard_map/ppermute | solution.py:399
  59.2 7.5 %collective-permute-start.13 = (bf16[4,128,128]{2,1,0:T(8,128)(2,1)S(1)}, bf16[4,128,128]{2,1,0:T(8,128)(2,1)S(1)}, u32[]{:S(2)}, u32[]{:S(2)}) collective-permute-start(bf16[4,128,128]{2,1,0:T(8,128)(2,1)S(1)} %get-tuple-element.67), channel_id=1, source_target_pairs={{0,6},{1,7},{2,4},{3,5},{4,2},{5,3},{6,0},{7,1},{8,14},{9,15},{10,... | collective-permute-start | bytes 393224 | tf_op jit(solution)/shard_map/ppermute | solution.py:399
  67.4 10.3 %collective-permute-start.15 = (bf16[4,128,128]{2,1,0:T(8,128)(2,1)S(1)}, bf16[4,128,128]{2,1,0:T(8,128)(2,1)S(1)}, u32[]{:S(2)}, u32[]{:S(2)}) collective-permute-start(bf16[4,128,128]{2,1,0:T(8,128)(2,1)S(1)} %future_total.1), channel_id=1, source_target_pairs={{16,0},{24,8},{17,1},{25,9},{18,2},{26,10},{19,3},{27,11},{20,4},{... | collective-permute-start | bytes 393224 | tf_op jit(solution)/shard_map/ppermute | solution.py:433
  68.7 9.3 %collective-permute-start.14 = (bf16[4,128,128]{2,1,0:T(8,128)(2,1)S(1)}, bf16[4,128,128]{2,1,0:T(8,128)(2,1)S(1)}, u32[]{:S(2)}, u32[]{:S(2)}) collective-permute-start(bf16[4,128,128]{2,1,0:T(8,128)(2,1)S(1)} %future_total.1), channel_id=1, source_target_pairs={{8,0},{16,8},{24,16},{9,1},{17,9},{25,17},{10,2},{18,10},{26,18},{... | collective-permute-start | bytes 393224 | tf_op jit(solution)/shard_map/ppermute | solution.py:433
  78.9 6.1 %collective-permute-start.16 = (bf16[4,128,128]{2,1,0:T(8,128)(2,1)S(1)}, bf16[4,128,128]{2,1,0:T(8,128)(2,1)S(1)}, u32[]{:S(2)}, u32[]{:S(2)}) collective-permute-start(bf16[4,128,128]{2,1,0:T(8,128)(2,1)S(1)} %get-tuple-element.69), channel_id=1, source_target_pairs={{0,2},{1,3},{2,0},{3,1},{4,6},{5,7},{6,4},{7,5},{8,10},{9,11},{10,... | collective-permute-start | bytes 393224 | tf_op jit(solution)/shard_map/ppermute | solution.py:399
  79.8 5.7 %collective-permute-start.17 = (bf16[4,128,128]{2,1,0:T(8,128)(2,1)S(1)}, bf16[4,128,128]{2,1,0:T(8,128)(2,1)S(1)}, u32[]{:S(2)}, u32[]{:S(2)}) collective-permute-start(bf16[4,128,128]{2,1,0:T(8,128)(2,1)S(1)} %get-tuple-element.70), channel_id=1, source_target_pairs={{0,4},{1,5},{2,6},{3,7},{4,0},{5,1},{6,2},{7,3},{8,12},{9,13},{10,... | collective-permute-start | bytes 393224 | tf_op jit(solution)/shard_map/ppermute | solution.py:399
  81.3 6.4 %collective-permute-start.18 = (bf16[4,128,128]{2,1,0:T(8,128)(2,1)S(1)}, bf16[4,128,128]{2,1,0:T(8,128)(2,1)S(1)}, u32[]{:S(2)}, u32[]{:S(2)}) collective-permute-start(bf16[4,128,128]{2,1,0:T(8,128)(2,1)S(1)} %get-tuple-element.71), channel_id=1, source_target_pairs={{0,6},{1,7},{2,4},{3,5},{4,2},{5,3},{6,0},{7,1},{8,14},{9,15},{10,... | collective-permute-start | bytes 393224 | tf_op jit(solution)/shard_map/ppermute | solution.py:399
  88.9 3.7 %collective-permute-start.19 = (bf16[16,128,128]{2,1,0:T(8,128)(2,1)S(1)}, bf16[16,128,128]{2,1,0:T(8,128)(2,1)S(1)}, u32[]{:S(2)}, u32[]{:S(2)}) collective-permute-start(bf16[16,128,128]{2,1,0:T(8,128)(2,1)S(1)} %bitcast.23), channel_id=1, source_target_pairs={{0,1},{1,0},{2,3},{3,2},{4,5},{5,4},{6,7},{7,6},{8,9},{9,8},{10,11... | collective-permute-start | bytes 1572872 | tf_op jit(solution)/shard_map/ppermute | solution.py:394

commit v8 on v7

--- a/solution.py
+++ b/solution.py
@@ -311,7 +311,7 @@
 
 
 SMALL = pltpu.CompilerParams(
-    dimension_semantics=("arbitrary",), vmem_limit_bytes=24 * 1024 * 1024
+    dimension_semantics=("arbitrary",), vmem_limit_bytes=16 * 1024 * 1024
 )
 
 def local(queries, keys, values, out_grad, doc_lengths):
@@ -349,18 +349,15 @@
     halved = pl.BlockSpec((step_heads, DH, DH), lambda i, *a: (i, 0, 0))
     untouched = pl.BlockSpec(memory_space=pl.ANY)
     token_bf = pltpu.HBM((count, width), BF16)
-    token_f32 = pltpu.HBM((count, width), F32)
-    tile_bf = pltpu.HBM((heads, count, count), BF16)
-    turned_bf = pltpu.HBM((heads, DH, count), BF16)
+    inner_bf = jax.ShapeDtypeStruct((count, width), BF16)
+    token_f32 = jax.ShapeDtypeStruct((count, width), F32)
+    tile_bf = jax.ShapeDtypeStruct((heads, count, count), BF16)
+    turned_bf = jax.ShapeDtypeStruct((heads, DH, count), BF16)
     owned_bf = jax.ShapeDtypeStruct((owned, DH, DH), BF16)
     half_bf = jax.ShapeDtypeStruct((half, DH, DH), BF16)
     chips_bf = jax.ShapeDtypeStruct((chips, owned, DH, DH), BF16)
 
     def run(kernel, grid, ins, outs, shapes, scratch, args, cost, name, params=SMALL, aliases={}):
-        args = [
-            arg if arg.shape[-2:] == (DH, DH) and arg.size <= half * DH * DH else held_in_hbm(arg)
-            for arg in args
-        ]
         flops, moved, exps = cost
         return pl.pallas_call(
             kernel,
@@ -467,7 +464,7 @@
             [halved],
             [half_bf],
             [],
-            (keys, values),
+            (held_in_hbm(keys), held_in_hbm(values)),
             (product, 3 * array, half * count * DH),
             f"tail_{parity}",
         )
@@ -477,7 +474,7 @@
         2 * steps,
         [tokens(None)] * 3,
         [tiles(None, count, count), tokens(None), tokens(None), tiles(None, DH, count)],
-        [tile_bf, token_f32, token_bf, turned_bf],
+        [tile_bf, token_f32, inner_bf, turned_bf],
         [],
         (queries, keys, values),
         (4 * product, 16 * array, 4 * half * count * DH),
@@ -492,7 +489,7 @@
             [tokens(parity), tiles(parity, DH, count), tokens(parity), tokens(parity), halved]
             + [untouched] * len(made),
             [tokens(parity)] * 2 + [halved],
-            [token_bf] * 2 + [half_bf],
+            [token_bf, inner_bf, half_bf],
             [],
             (head_fq, turned, out_grad, part, incoming[parity], *made),
             (4 * product, 9 * array, half * count * DH),

time: 97.8 us -> 90.8 us (0.928)
  Pallas kernels: 42.4 us -> 33.6 us
  waiting for transfers between devices: 25.8 us -> 27.8 us
    pallas_call x16, Pallas kernels: 42.4 us -> 33.6 us  [run(): pl.pallas_call(kernel, grid_spec=pltpu.PrefetchScalarGridSpec(num_scalar_...]
    ppermute x4, waiting for transfers between devices: 0.61 us -> 3.52 us  [gather(): others.append(lax.ppermute(total, 'z', pairs))]
  transfers between devices with their start and end apart: 20 -> 20, of which waited for: 15 -> 13; matrix products, arithmetic and copies ran while one was open for 0% -> 0% of each run, Pallas kernels for 25% -> 20%
where the time goes in v8:
time: 90.8 us; the launch traced here: 90 us
  Pallas kernels  33.6 us (37%)
  waiting for transfers between devices  27.8 us (31%)
  starting transfers between devices  26.9 us (30%)
    pallas_call x16, Pallas kernels, run(): pl.pallas_call(kernel, grid_spec=pltpu.PrefetchScalarGridSpec(num_scalar_...  33.6 us
    ppermute x12, waiting for transfers between devices, exchange(): lax.ppermute(state, LAYER, pairs[n])  22.7 us
    ppermute x12, starting transfers between devices, exchange(): lax.ppermute(state, LAYER, pairs[n])  15.1 us
    ppermute x4, starting transfers between devices, gather(): others.append(lax.ppermute(total, 'z', pairs))  10.7 us
    ppermute x4, waiting for transfers between devices, gather(): others.append(lax.ppermute(total, 'z', pairs))  3.52 us
  transfers between devices with their start and end apart: 20, of which 13 were waited for; matrix products, arithmetic and copies ran while one was open for 0% of the time, Pallas kernels for 20%

profile of v8, /device:TPU:0, one launch (start us, length us, event | category | flops | bytes accessed | tf_op | source)
XLA Modules:
  0.0 90.0 jit_solution(10348148465711757612)
XLA Ops:
  0.6 0.1 pad_add_fusion.place
  0.7 0.7 copy-done.4
  1.4 2.6 %tail_1.1 = bf16[16,128,128]{2,1,0:T(8,128)(2,1)S(1)} custom-call(s32[8]{0:T(128)S(1)} %copy-done.4, s32[3]{0:T(128)S(1)} %pad_add_fusion.place, bf16[128,4096]{1,0:T(8,128)(2,1)} %k.11, bf16[128,4096]{1,0:T(8,128)(2,1)} %v.11), custom_call_target="tpu_custom_call" | custom-call | flops 67108864 | bytes 1572864 | tf_op jit(solution)/shard_map/tail_1/pallas_call | solution.py:362
  4.0 0.0 copy-start
  4.0 0.0 copy-start.1
  4.0 0.0 copy-start.3
  4.0 0.5 collective-permute-start
  4.5 2.6 %tail_0.1 = bf16[16,128,128]{2,1,0:T(8,128)(2,1)S(1)} custom-call(s32[8]{0:T(128)S(1)} %copy-done.4, s32[3]{0:T(128)S(1)} %pad_add_fusion.place, bf16[128,4096]{1,0:T(8,128)(2,1)} %k.11, bf16[128,4096]{1,0:T(8,128)(2,1)} %v.11), custom_call_target="tpu_custom_call" | custom-call | flops 67108864 | bytes 1572864 | tf_op jit(solution)/shard_map/tail_0/pallas_call | solution.py:362
  7.1 0.0 collective-permute-done
  7.1 0.9 %carried_chip.1 = (bf16[4,128,128]{2,1,0:T(8,128)(2,1)S(1)}, bf16[4,128,128]{2,1,0:T(8,128)(2,1)S(1)}, bf16[4,128,128]{2,1,0:T(8,128)(2,1)S(1)}, bf16[4,128,128]{2,1,0:T(8,128)(2,1)S(1)}) custom-call(s32[8]{0:T(128)S(1)} %copy-done.4, s32[3]{0:T(128)S(1)} %pad_add_fusion.place, bf16[4,4,128,128]{3,2,1,0:T(8,128)(2,1)S(1)} %bitcast.11, ...), custom_call_target="tpu_custom_call" | custom-call | flops 1048576 | bytes 1048576 | tf_op jit(solution)/shard_map/carried_chip/pallas_call | solution.py:362
  8.1 2.9 %collective-permute-start.1 = (bf16[4,128,128]{2,1,0:T(8,128)(2,1)S(1)}, bf16[4,128,128]{2,1,0:T(8,128)(2,1)S(1)}, u32[]{:S(2)}, u32[]{:S(2)}) collective-permute-start(bf16[4,128,128]{2,1,0:T(8,128)(2,1)S(1)} %get-tuple-element.45), channel_id=1, source_target_pairs={{0,2},{1,3},{2,0},{3,1},{4,6},{5,7},{6,4},{7,5},{8,10},{9,11},{10,... | collective-permute-start | bytes 393224 | tf_op jit(solution)/shard_map/ppermute | solution.py:396
  10.9 1.5 %collective-permute-start.2 = (bf16[4,128,128]{2,1,0:T(8,128)(2,1)S(1)}, bf16[4,128,128]{2,1,0:T(8,128)(2,1)S(1)}, u32[]{:S(2)}, u32[]{:S(2)}) collective-permute-start(bf16[4,128,128]{2,1,0:T(8,128)(2,1)S(1)} %get-tuple-element.46), channel_id=1, source_target_pairs={{0,4},{1,5},{2,6},{3,7},{4,0},{5,1},{6,2},{7,3},{8,12},{9,13},{10,... | collective-permute-start | bytes 393224 | tf_op jit(solution)/shard_map/ppermute | solution.py:396
  12.4 0.0 collective-permute-start.3
  12.5 2.3 %collective-permute-done.1.rest_1_ = bf16[4,128,128]{2,1,0:T(8,128)(2,1)S(1)} collective-permute-done((bf16[4,128,128]{2,1,0:T(8,128)(2,1)S(1)}, bf16[4,128,128]{2,1,0:T(8,128)(2,1)S(1)}, u32[]{:S(2)}, u32[]{:S(2)}) %collective-permute-start.1) | collective-permute-done | bytes 131104 | tf_op jit(solution)/shard_map/ppermute | solution.py:396
  14.8 2.5 %collective-permute-done.2.rest_2_ = bf16[4,128,128]{2,1,0:T(8,128)(2,1)S(1)} collective-permute-done((bf16[4,128,128]{2,1,0:T(8,128)(2,1)S(1)}, bf16[4,128,128]{2,1,0:T(8,128)(2,1)S(1)}, u32[]{:S(2)}, u32[]{:S(2)}) %collective-permute-start.2) | collective-permute-done | bytes 131104 | tf_op jit(solution)/shard_map/ppermute | solution.py:396
  17.3 1.6 %collective-permute-done.3.rest_3_ = bf16[4,128,128]{2,1,0:T(8,128)(2,1)S(1)} collective-permute-done((bf16[4,128,128]{2,1,0:T(8,128)(2,1)S(1)}, bf16[4,128,128]{2,1,0:T(8,128)(2,1)S(1)}, u32[]{:S(2)}, u32[]{:S(2)}) %collective-permute-start.3) | collective-permute-done | bytes 131104 | tf_op jit(solution)/shard_map/ppermute | solution.py:396
  18.9 0.7 carried_total.1
  19.6 4.6 %collective-permute-start.5 = (bf16[4,128,128]{2,1,0:T(8,128)(2,1)S(1)}, bf16[4,128,128]{2,1,0:T(8,128)(2,1)S(1)}, u32[]{:S(2)}, u32[]{:S(2)}) collective-permute-start(bf16[4,128,128]{2,1,0:T(8,128)(2,1)S(1)} %carried_total.1), channel_id=1, source_target_pairs={{0,16},{8,24},{1,17},{9,25},{2,18},{10,26},{3,19},{11,27},{4,20},{... | collective-permute-start | bytes 393224 | tf_op jit(solution)/shard_map/ppermute | solution.py:430
  24.3 3.5 %collective-permute-start.4 = (bf16[4,128,128]{2,1,0:T(8,128)(2,1)S(1)}, bf16[4,128,128]{2,1,0:T(8,128)(2,1)S(1)}, u32[]{:S(2)}, u32[]{:S(2)}) collective-permute-start(bf16[4,128,128]{2,1,0:T(8,128)(2,1)S(1)} %carried_total.1), channel_id=1, source_target_pairs={{0,8},{8,16},{16,24},{1,9},{9,17},{17,25},{2,10},{10,18},{18,26},{... | collective-permute-start | bytes 393224 | tf_op jit(solution)/shard_map/ppermute | solution.py:430
  27.8 0.0 copy-done
  27.8 0.0 copy-done.1
  27.8 4.6 %within.1 = (bf16[32,128,128]{2,1,0:T(8,128)(2,1)S(1)}, f32[128,4096]{1,0:T(8,128)S(1)}, bf16[128,4096]{1,0:T(8,128)(2,1)S(1)}, bf16[32,128,128]{2,1,0:T(8,128)(2,1)S(1)}) custom-call(s32[8]{0:T(128)S(1)} %copy-done.4, s32[3]{0:T(128)S(1)} %pad_add_fusion.place, bf16[128,4096]{1,0:T(8,128)(2,1)S(1)} %copy-done.3, bf16[128,4096]{1,0:T(8,128)(2,1)S(1)} %copy-done, ...), custom_call_target="tpu_custom_call" | custom-call | flops 268435456 | bytes 8388608 | tf_op jit(solution)/shard_map/within/pallas_call | solution.py:362
  32.4 0.0 collective-permute-done.5.rest_6_
  32.4 0.0 collective-permute-done.4.rest_5_
  32.5 0.0 copy-start.2
  32.5 0.9 carried_prefix.1
  33.4 1.6 %collective-permute-start.6 = (bf16[4,128,128]{2,1,0:T(8,128)(2,1)S(1)}, bf16[4,128,128]{2,1,0:T(8,128)(2,1)S(1)}, u32[]{:S(2)}, u32[]{:S(2)}) collective-permute-start(bf16[4,128,128]{2,1,0:T(8,128)(2,1)S(1)} %get-tuple-element.49), channel_id=1, source_target_pairs={{0,2},{1,3},{2,0},{3,1},{4,6},{5,7},{6,4},{7,5},{8,10},{9,11},{10,... | collective-permute-start | bytes 393224 | tf_op jit(solution)/shard_map/ppermute | solution.py:396
  34.9 1.5 %collective-permute-start.7 = (bf16[4,128,128]{2,1,0:T(8,128)(2,1)S(1)}, bf16[4,128,128]{2,1,0:T(8,128)(2,1)S(1)}, u32[]{:S(2)}, u32[]{:S(2)}) collective-permute-start(bf16[4,128,128]{2,1,0:T(8,128)(2,1)S(1)} %get-tuple-element.50), channel_id=1, source_target_pairs={{0,4},{1,5},{2,6},{3,7},{4,0},{5,1},{6,2},{7,3},{8,12},{9,13},{10,... | collective-permute-start | bytes 393224 | tf_op jit(solution)/shard_map/ppermute | solution.py:396
  36.4 0.5 collective-permute-start.8
  36.9 2.5 %collective-permute-done.6.rest_1_ = bf16[4,128,128]{2,1,0:T(8,128)(2,1)S(1)} collective-permute-done((bf16[4,128,128]{2,1,0:T(8,128)(2,1)S(1)}, bf16[4,128,128]{2,1,0:T(8,128)(2,1)S(1)}, u32[]{:S(2)}, u32[]{:S(2)}) %collective-permute-start.6) | collective-permute-done | bytes 131104 | tf_op jit(solution)/shard_map/ppermute | solution.py:396
  39.4 0.7 collective-permute-done.7.rest_2_
  40.0 2.3 %collective-permute-done.8.rest_3_ = bf16[4,128,128]{2,1,0:T(8,128)(2,1)S(1)} collective-permute-done((bf16[4,128,128]{2,1,0:T(8,128)(2,1)S(1)}, bf16[4,128,128]{2,1,0:T(8,128)(2,1)S(1)}, u32[]{:S(2)}, u32[]{:S(2)}) %collective-permute-start.8) | collective-permute-done | bytes 131104 | tf_op jit(solution)/shard_map/ppermute | solution.py:396
  42.3 1.3 %carried_device.1 = (bf16[4,4,128,128]{3,2,1,0:T(8,128)(2,1)S(1)}, bf16[4,4,128,128]{3,2,1,0:T(8,128)(2,1)S(1)}) custom-call(s32[8]{0:T(128)S(1)} %copy-done.4, s32[3]{0:T(128)S(1)} %pad_add_fusion.place, bf16[4,128,128]{2,1,0:T(8,128)(2,1)S(1)} %get-tuple-element.48.rest_0_, bf16[4,128,128]{2,1,0:T(8,128)(2,1)S(1)} %collective-permute-done.6.rest_1_, ...), custom_call_target="tpu_custom_call" | custom-call | flops 1048576 | bytes 1048576 | tf_op jit(solution)/shard_map/carried_device/pallas_call | solution.py:362
  43.6 0.1 collective-permute-start.9
  43.7 2.9 %normed_0.1 = (bf16[128,4096]{1,0:T(8,128)(2,1)}, bf16[128,4096]{1,0:T(8,128)(2,1)S(1)}, bf16[16,128,128]{2,1,0:T(8,128)(2,1)S(1)}) custom-call(s32[8]{0:T(128)S(1)} %copy-done.4, s32[3]{0:T(128)S(1)} %pad_add_fusion.place, bf16[128,4096]{1,0:T(8,128)(2,1)S(1)} %get-tuple-element.41.head_fq, bf16[32,128,128]{2,1,0:T(8,128)(2,1)S(1)} %get-tuple-element.42.turned, ...), custom_call_target="tpu_custom_call" | custom-call | flops 268435456 | bytes 4718592 | tf_op jit(solution)/shard_map/normed_0/pallas_call | solution.py:362
  46.5 0.0 collective-permute-done.9.incoming.other
  46.5 2.8 %normed_1.1 = (bf16[128,4096]{1,0:T(8,128)(2,1)}, bf16[128,4096]{1,0:T(8,128)(2,1)S(1)}, bf16[16,128,128]{2,1,0:T(8,128)(2,1)S(1)}) custom-call(s32[8]{0:T(128)S(1)} %copy-done.4, s32[3]{0:T(128)S(1)} %pad_add_fusion.place, bf16[128,4096]{1,0:T(8,128)(2,1)S(1)} %get-tuple-element.41.head_fq, ...), custom_call_target="tpu_custom_call", output_to_operand_aliasing={{0}: (7, {}), {1}: (8, {})} | custom-call | flops 268435456 | bytes 4718592 | tf_op jit(solution)/shard_map/normed_1/pallas_call | solution.py:362
  49.4 0.5 collective-permute-start.10
  49.9 1.5 %collective-permute-done.10 = bf16[16,128,128]{2,1,0:T(8,128)(2,1)S(1)} collective-permute-done((bf16[16,128,128]{2,1,0:T(8,128)(2,1)S(1)}, bf16[16,128,128]{2,1,0:T(8,128)(2,1)S(1)}, u32[]{:S(2)}, u32[]{:S(2)}) %collective-permute-start.10) | collective-permute-done | bytes 524320 | tf_op jit(solution)/shard_map/ppermute | solution.py:391
  51.4 0.9 %future_chip.1 = (bf16[4,128,128]{2,1,0:T(8,128)(2,1)S(1)}, bf16[4,128,128]{2,1,0:T(8,128)(2,1)S(1)}, bf16[4,128,128]{2,1,0:T(8,128)(2,1)S(1)}, bf16[4,128,128]{2,1,0:T(8,128)(2,1)S(1)}) custom-call(s32[8]{0:T(128)S(1)} %copy-done.4, s32[3]{0:T(128)S(1)} %pad_add_fusion.place, bf16[4,4,128,128]{3,2,1,0:T(8,128)(2,1)S(1)} %bitcast.13, ...), custom_call_target="tpu_custom_call" | custom-call | flops 1048576 | bytes 1048576 | tf_op jit(solution)/shard_map/future_chip/pallas_call | solution.py:362
  52.3 0.7 collective-permute-start.11
  53.0 1.5 %collective-permute-start.12 = (bf16[4,128,128]{2,1,0:T(8,128)(2,1)S(1)}, bf16[4,128,128]{2,1,0:T(8,128)(2,1)S(1)}, u32[]{:S(2)}, u32[]{:S(2)}) collective-permute-start(bf16[4,128,128]{2,1,0:T(8,128)(2,1)S(1)} %get-tuple-element.66), channel_id=1, source_target_pairs={{0,4},{1,5},{2,6},{3,7},{4,0},{5,1},{6,2},{7,3},{8,12},{9,13},{10,... | collective-permute-start | bytes 393224 | tf_op jit(solution)/shard_map/ppermute | solution.py:396
  54.5 1.4 %collective-permute-start.13 = (bf16[4,128,128]{2,1,0:T(8,128)(2,1)S(1)}, bf16[4,128,128]{2,1,0:T(8,128)(2,1)S(1)}, u32[]{:S(2)}, u32[]{:S(2)}) collective-permute-start(bf16[4,128,128]{2,1,0:T(8,128)(2,1)S(1)} %get-tuple-element.67), channel_id=1, source_target_pairs={{0,6},{1,7},{2,4},{3,5},{4,2},{5,3},{6,0},{7,1},{8,14},{9,15},{10,... | collective-permute-start | bytes 393224 | tf_op jit(solution)/shard_map/ppermute | solution.py:396
  55.9 2.3 %collective-permute-done.11.rest_1_ = bf16[4,128,128]{2,1,0:T(8,128)(2,1)S(1)} collective-permute-done((bf16[4,128,128]{2,1,0:T(8,128)(2,1)S(1)}, bf16[4,128,128]{2,1,0:T(8,128)(2,1)S(1)}, u32[]{:S(2)}, u32[]{:S(2)}) %collective-permute-start.11) | collective-permute-done | bytes 131104 | tf_op jit(solution)/shard_map/ppermute | solution.py:396
  58.2 1.2 %collective-permute-done.12.rest_2_ = bf16[4,128,128]{2,1,0:T(8,128)(2,1)S(1)} collective-permute-done((bf16[4,128,128]{2,1,0:T(8,128)(2,1)S(1)}, bf16[4,128,128]{2,1,0:T(8,128)(2,1)S(1)}, u32[]{:S(2)}, u32[]{:S(2)}) %collective-permute-start.12) | collective-permute-done | bytes 131104 | tf_op jit(solution)/shard_map/ppermute | solution.py:396
  59.4 2.8 %collective-permute-done.13.rest_3_ = bf16[4,128,128]{2,1,0:T(8,128)(2,1)S(1)} collective-permute-done((bf16[4,128,128]{2,1,0:T(8,128)(2,1)S(1)}, bf16[4,128,128]{2,1,0:T(8,128)(2,1)S(1)}, u32[]{:S(2)}, u32[]{:S(2)}) %collective-permute-start.13) | collective-permute-done | bytes 131104 | tf_op jit(solution)/shard_map/ppermute | solution.py:396
  62.2 0.7 future_total.1
  62.9 1.3 %collective-permute-start.15 = (bf16[4,128,128]{2,1,0:T(8,128)(2,1)S(1)}, bf16[4,128,128]{2,1,0:T(8,128)(2,1)S(1)}, u32[]{:S(2)}, u32[]{:S(2)}) collective-permute-start(bf16[4,128,128]{2,1,0:T(8,128)(2,1)S(1)} %future_total.1), channel_id=1, source_target_pairs={{16,0},{24,8},{17,1},{25,9},{18,2},{26,10},{19,3},{27,11},{20,4},{... | collective-permute-start | bytes 393224 | tf_op jit(solution)/shard_map/ppermute | solution.py:430
  64.2 1.3 %collective-permute-start.14 = (bf16[4,128,128]{2,1,0:T(8,128)(2,1)S(1)}, bf16[4,128,128]{2,1,0:T(8,128)(2,1)S(1)}, u32[]{:S(2)}, u32[]{:S(2)}) collective-permute-start(bf16[4,128,128]{2,1,0:T(8,128)(2,1)S(1)} %future_total.1), channel_id=1, source_target_pairs={{8,0},{16,8},{24,16},{9,1},{17,9},{25,17},{10,2},{18,10},{26,18},{... | collective-permute-start | bytes 393224 | tf_op jit(solution)/shard_map/ppermute | solution.py:430
  65.5 5.4 %grads_within.1 = (bf16[128,4096]{1,0:T(8,128)(2,1)}, f32[128,4096]{1,0:T(8,128)S(1)}, f32[128,4096]{1,0:T(8,128)S(1)}) custom-call(s32[8]{0:T(128)S(1)} %copy-done.4, s32[3]{0:T(128)S(1)} %pad_add_fusion.place, bf16[128,4096]{1,0:T(8,128)(2,1)S(1)} %copy-done.3, bf16[128,4096]{1,0:T(8,128)(2,1)S(1)} %copy-done, bf16[128,4096]{1,0:T(8,128)(2,1)S(1)} %copy-done.1, ...), custom_call_target="tpu_custom_call" | custom-call | flops 671088640 | bytes 11534336 | tf_op jit(solution)/shard_map/grads_within/pallas_call | solution.py:362
  70.9 3.5 %collective-permute-done.15.rest_6_ = bf16[4,128,128]{2,1,0:T(8,128)(2,1)S(1)} collective-permute-done((bf16[4,128,128]{2,1,0:T(8,128)(2,1)S(1)}, bf16[4,128,128]{2,1,0:T(8,128)(2,1)S(1)}, u32[]{:S(2)}, u32[]{:S(2)}) %collective-permute-start.15) | collective-permute-done | bytes 131104 | tf_op jit(solution)/shard_map/ppermute | solution.py:430
  74.4 0.0 collective-permute-done.14.rest_5_
  74.4 0.9 future_prefix.1
  75.3 0.9 collective-permute-start.16
  76.2 1.5 %collective-permute-start.17 = (bf16[4,128,128]{2,1,0:T(8,128)(2,1)S(1)}, bf16[4,128,128]{2,1,0:T(8,128)(2,1)S(1)}, u32[]{:S(2)}, u32[]{:S(2)}) collective-permute-start(bf16[4,128,128]{2,1,0:T(8,128)(2,1)S(1)} %get-tuple-element.70), channel_id=1, source_target_pairs={{0,4},{1,5},{2,6},{3,7},{4,0},{5,1},{6,2},{7,3},{8,12},{9,13},{10,... | collective-permute-start | bytes 393224 | tf_op jit(solution)/shard_map/ppermute | solution.py:396
  77.7 1.2 %collective-permute-start.18 = (bf16[4,128,128]{2,1,0:T(8,128)(2,1)S(1)}, bf16[4,128,128]{2,1,0:T(8,128)(2,1)S(1)}, u32[]{:S(2)}, u32[]{:S(2)}) collective-permute-start(bf16[4,128,128]{2,1,0:T(8,128)(2,1)S(1)} %get-tuple-element.71), channel_id=1, source_target_pairs={{0,6},{1,7},{2,4},{3,5},{4,2},{5,3},{6,0},{7,1},{8,14},{9,15},{10,... | collective-permute-start | bytes 393224 | tf_op jit(solution)/shard_map/ppermute | solution.py:396
  78.9 2.8 %collective-permute-done.16.rest_1_ = bf16[4,128,128]{2,1,0:T(8,128)(2,1)S(1)} collective-permute-done((bf16[4,128,128]{2,1,0:T(8,128)(2,1)S(1)}, bf16[4,128,128]{2,1,0:T(8,128)(2,1)S(1)}, u32[]{:S(2)}, u32[]{:S(2)}) %collective-permute-start.16) | collective-permute-done | bytes 131104 | tf_op jit(solution)/shard_map/ppermute | solution.py:396
  81.6 0.0 collective-permute-done.17.rest_2_
  81.6 1.9 %collective-permute-done.18.rest_3_ = bf16[4,128,128]{2,1,0:T(8,128)(2,1)S(1)} collective-permute-done((bf16[4,128,128]{2,1,0:T(8,128)(2,1)S(1)}, bf16[4,128,128]{2,1,0:T(8,128)(2,1)S(1)}, u32[]{:S(2)}, u32[]{:S(2)}) %collective-permute-start.18) | collective-permute-done | bytes 131104 | tf_op jit(solution)/shard_map/ppermute | solution.py:396
  83.6 1.3 %future_device.1 = (bf16[4,4,128,128]{3,2,1,0:T(8,128)(2,1)S(1)}, bf16[4,4,128,128]{3,2,1,0:T(8,128)(2,1)S(1)}) custom-call(s32[8]{0:T(128)S(1)} %copy-done.4, s32[3]{0:T(128)S(1)} %pad_add_fusion.place, bf16[4,128,128]{2,1,0:T(8,128)(2,1)S(1)} %get-tuple-element.68.rest_0_, bf16[4,128,128]{2,1,0:T(8,128)(2,1)S(1)} %collective-permute-done.16.rest_1_, ...), custom_call_target="tpu_custom_call" | custom-call | flops 1048576 | bytes 1048576 | tf_op jit(solution)/shard_map/future_device/pallas_call | solution.py:362
  84.9 0.1 collective-permute-start.19
  84.9 2.5 %grads_last_0.1 = (bf16[128,4096]{1,0:T(8,128)(2,1)}, bf16[128,4096]{1,0:T(8,128)(2,1)}) custom-call(s32[8]{0:T(128)S(1)} %copy-done.4, s32[3]{0:T(128)S(1)} %pad_add_fusion.place, bf16[128,4096]{1,0:T(8,128)(2,1)S(1)} %copy-done, bf16[128,4096]{1,0:T(8,128)(2,1)S(1)} %copy-done.1, f32[128,4096]{1,0:T(8,128)S(1)} %get-tuple-element.60.rest_4_.gk_part, ...), custom_call_target="tpu_custom_call" | custom-call | flops 134217728 | bytes 4718592 | tf_op jit(solution)/shard_map/grads_last_0/pallas_call | solution.py:362
  87.5 0.0 collective-permute-done.19.outgoing
  87.5 2.5 %grads_last_1.1 = (bf16[128,4096]{1,0:T(8,128)(2,1)}, bf16[128,4096]{1,0:T(8,128)(2,1)}) custom-call(s32[8]{0:T(128)S(1)} %copy-done.4, s32[3]{0:T(128)S(1)} %pad_add_fusion.place, bf16[128,4096]{1,0:T(8,128)(2,1)S(1)} %copy-done, bf16[128,4096]{1,0:T(8,128)(2,1)S(1)} %copy-done.1, ...), custom_call_target="tpu_custom_call", output_to_operand_aliasing={{0}: (7, {}), {1}: (8, {})} | custom-call | flops 134217728 | bytes 4718592 | tf_op jit(solution)/shard_map/grads_last_1/pallas_call | solution.py:362
  (3 shorter events, 0.0 us)
Async XLA Ops:
  0.7 0.7 copy-start.4
  4.0 23.8 %copy-start = (bf16[128,4096]{1,0:T(8,128)(2,1)S(1)}, bf16[128,4096]{1,0:T(8,128)(2,1)}, u32[]{:S(2)}) copy-start(bf16[128,4096]{1,0:T(8,128)(2,1)} %k.11) | copy-start | bytes 3145732
  4.0 23.8 %copy-start.1 = (bf16[128,4096]{1,0:T(8,128)(2,1)S(1)}, bf16[128,4096]{1,0:T(8,128)(2,1)}, u32[]{:S(2)}) copy-start(bf16[128,4096]{1,0:T(8,128)(2,1)} %v.11) | copy-start | bytes 3145732
  4.0 23.8 %copy-start.3 = (bf16[128,4096]{1,0:T(8,128)(2,1)S(1)}, bf16[128,4096]{1,0:T(8,128)(2,1)}, u32[]{:S(2)}) copy-start(bf16[128,4096]{1,0:T(8,128)(2,1)} %q.3) | copy-start | bytes 3145732
  4.0 3.1 %collective-permute-start = (bf16[16,128,128]{2,1,0:T(8,128)(2,1)S(1)}, bf16[16,128,128]{2,1,0:T(8,128)(2,1)S(1)}, u32[]{:S(2)}, u32[]{:S(2)}) collective-permute-start(bf16[16,128,128]{2,1,0:T(8,128)(2,1)S(1)} %tail_1.1), channel_id=1, source_target_pairs={{0,1},{1,0},{2,3},{3,2},{4,5},{5,4},{6,7},{7,6},{8,9},{9,8},{10,11... | collective-permute-start | bytes 1572872 | tf_op jit(solution)/shard_map/ppermute | solution.py:391
  8.1 6.8 %collective-permute-start.1 = (bf16[4,128,128]{2,1,0:T(8,128)(2,1)S(1)}, bf16[4,128,128]{2,1,0:T(8,128)(2,1)S(1)}, u32[]{:S(2)}, u32[]{:S(2)}) collective-permute-start(bf16[4,128,128]{2,1,0:T(8,128)(2,1)S(1)} %get-tuple-element.45), channel_id=1, source_target_pairs={{0,2},{1,3},{2,0},{3,1},{4,6},{5,7},{6,4},{7,5},{8,10},{9,11},{10,... | collective-permute-start | bytes 393224 | tf_op jit(solution)/shard_map/ppermute | solution.py:396
  10.9 6.4 %collective-permute-start.2 = (bf16[4,128,128]{2,1,0:T(8,128)(2,1)S(1)}, bf16[4,128,128]{2,1,0:T(8,128)(2,1)S(1)}, u32[]{:S(2)}, u32[]{:S(2)}) collective-permute-start(bf16[4,128,128]{2,1,0:T(8,128)(2,1)S(1)} %get-tuple-element.46), channel_id=1, source_target_pairs={{0,4},{1,5},{2,6},{3,7},{4,0},{5,1},{6,2},{7,3},{8,12},{9,13},{10,... | collective-permute-start | bytes 393224 | tf_op jit(solution)/shard_map/ppermute | solution.py:396
  12.4 6.4 %collective-permute-start.3 = (bf16[4,128,128]{2,1,0:T(8,128)(2,1)S(1)}, bf16[4,128,128]{2,1,0:T(8,128)(2,1)S(1)}, u32[]{:S(2)}, u32[]{:S(2)}) collective-permute-start(bf16[4,128,128]{2,1,0:T(8,128)(2,1)S(1)} %get-tuple-element.47), channel_id=1, source_target_pairs={{0,6},{1,7},{2,4},{3,5},{4,2},{5,3},{6,0},{7,1},{8,14},{9,15},{10,... | collective-permute-start | bytes 393224 | tf_op jit(solution)/shard_map/ppermute | solution.py:396
  19.6 12.8 %collective-permute-start.5 = (bf16[4,128,128]{2,1,0:T(8,128)(2,1)S(1)}, bf16[4,128,128]{2,1,0:T(8,128)(2,1)S(1)}, u32[]{:S(2)}, u32[]{:S(2)}) collective-permute-start(bf16[4,128,128]{2,1,0:T(8,128)(2,1)S(1)} %carried_total.1), channel_id=1, source_target_pairs={{0,16},{8,24},{1,17},{9,25},{2,18},{10,26},{3,19},{11,27},{4,20},{... | collective-permute-start | bytes 393224 | tf_op jit(solution)/shard_map/ppermute | solution.py:430
  24.3 8.2 %collective-permute-start.4 = (bf16[4,128,128]{2,1,0:T(8,128)(2,1)S(1)}, bf16[4,128,128]{2,1,0:T(8,128)(2,1)S(1)}, u32[]{:S(2)}, u32[]{:S(2)}) collective-permute-start(bf16[4,128,128]{2,1,0:T(8,128)(2,1)S(1)} %carried_total.1), channel_id=1, source_target_pairs={{0,8},{8,16},{16,24},{1,9},{9,17},{17,25},{2,10},{10,18},{18,26},{... | collective-permute-start | bytes 393224 | tf_op jit(solution)/shard_map/ppermute | solution.py:430
  32.5 11.2 %copy-start.2 = (bf16[128,4096]{1,0:T(8,128)(2,1)S(1)}, bf16[128,4096]{1,0:T(8,128)(2,1)}, u32[]{:S(2)}) copy-start(bf16[128,4096]{1,0:T(8,128)(2,1)} %g.3) | copy-start | bytes 3145732
  33.4 6.0 %collective-permute-start.6 = (bf16[4,128,128]{2,1,0:T(8,128)(2,1)S(1)}, bf16[4,128,128]{2,1,0:T(8,128)(2,1)S(1)}, u32[]{:S(2)}, u32[]{:S(2)}) collective-permute-start(bf16[4,128,128]{2,1,0:T(8,128)(2,1)S(1)} %get-tuple-element.49), channel_id=1, source_target_pairs={{0,2},{1,3},{2,0},{3,1},{4,6},{5,7},{6,4},{7,5},{8,10},{9,11},{10,... | collective-permute-start | bytes 393224 | tf_op jit(solution)/shard_map/ppermute | solution.py:396
  34.9 5.1 %collective-permute-start.7 = (bf16[4,128,128]{2,1,0:T(8,128)(2,1)S(1)}, bf16[4,128,128]{2,1,0:T(8,128)(2,1)S(1)}, u32[]{:S(2)}, u32[]{:S(2)}) collective-permute-start(bf16[4,128,128]{2,1,0:T(8,128)(2,1)S(1)} %get-tuple-element.50), channel_id=1, source_target_pairs={{0,4},{1,5},{2,6},{3,7},{4,0},{5,1},{6,2},{7,3},{8,12},{9,13},{10,... | collective-permute-start | bytes 393224 | tf_op jit(solution)/shard_map/ppermute | solution.py:396
  36.4 5.9 %collective-permute-start.8 = (bf16[4,128,128]{2,1,0:T(8,128)(2,1)S(1)}, bf16[4,128,128]{2,1,0:T(8,128)(2,1)S(1)}, u32[]{:S(2)}, u32[]{:S(2)}) collective-permute-start(bf16[4,128,128]{2,1,0:T(8,128)(2,1)S(1)} %get-tuple-element.51), channel_id=1, source_target_pairs={{0,6},{1,7},{2,4},{3,5},{4,2},{5,3},{6,0},{7,1},{8,14},{9,15},{10,... | collective-permute-start | bytes 393224 | tf_op jit(solution)/shard_map/ppermute | solution.py:396
  43.6 3.0 %collective-permute-start.9 = (bf16[16,128,128]{2,1,0:T(8,128)(2,1)S(1)}, bf16[16,128,128]{2,1,0:T(8,128)(2,1)S(1)}, u32[]{:S(2)}, u32[]{:S(2)}) collective-permute-start(bf16[16,128,128]{2,1,0:T(8,128)(2,1)S(1)} %bitcast.22), channel_id=1, source_target_pairs={{0,1},{1,0},{2,3},{3,2},{4,5},{5,4},{6,7},{7,6},{8,9},{9,8},{10,11... | collective-permute-start | bytes 1572872 | tf_op jit(solution)/shard_map/ppermute | solution.py:391
  49.4 2.0 %collective-permute-start.10 = (bf16[16,128,128]{2,1,0:T(8,128)(2,1)S(1)}, bf16[16,128,128]{2,1,0:T(8,128)(2,1)S(1)}, u32[]{:S(2)}, u32[]{:S(2)}) collective-permute-start(bf16[16,128,128]{2,1,0:T(8,128)(2,1)S(1)} %get-tuple-element.63), channel_id=1, source_target_pairs={{0,1},{1,0},{2,3},{3,2},{4,5},{5,4},{6,7},{7,6},{8,9},{9,8},{10,11... | collective-permute-start | bytes 1572872 | tf_op jit(solution)/shard_map/ppermute | solution.py:391
  52.3 5.8 %collective-permute-start.11 = (bf16[4,128,128]{2,1,0:T(8,128)(2,1)S(1)}, bf16[4,128,128]{2,1,0:T(8,128)(2,1)S(1)}, u32[]{:S(2)}, u32[]{:S(2)}) collective-permute-start(bf16[4,128,128]{2,1,0:T(8,128)(2,1)S(1)} %get-tuple-element.65), channel_id=1, source_target_pairs={{0,2},{1,3},{2,0},{3,1},{4,6},{5,7},{6,4},{7,5},{8,10},{9,11},{10,... | collective-permute-start | bytes 393224 | tf_op jit(solution)/shard_map/ppermute | solution.py:396
  53.0 6.4 %collective-permute-start.12 = (bf16[4,128,128]{2,1,0:T(8,128)(2,1)S(1)}, bf16[4,128,128]{2,1,0:T(8,128)(2,1)S(1)}, u32[]{:S(2)}, u32[]{:S(2)}) collective-permute-start(bf16[4,128,128]{2,1,0:T(8,128)(2,1)S(1)} %get-tuple-element.66), channel_id=1, source_target_pairs={{0,4},{1,5},{2,6},{3,7},{4,0},{5,1},{6,2},{7,3},{8,12},{9,13},{10,... | collective-permute-start | bytes 393224 | tf_op jit(solution)/shard_map/ppermute | solution.py:396
  54.5 7.7 %collective-permute-start.13 = (bf16[4,128,128]{2,1,0:T(8,128)(2,1)S(1)}, bf16[4,128,128]{2,1,0:T(8,128)(2,1)S(1)}, u32[]{:S(2)}, u32[]{:S(2)}) collective-permute-start(bf16[4,128,128]{2,1,0:T(8,128)(2,1)S(1)} %get-tuple-element.67), channel_id=1, source_target_pairs={{0,6},{1,7},{2,4},{3,5},{4,2},{5,3},{6,0},{7,1},{8,14},{9,15},{10,... | collective-permute-start | bytes 393224 | tf_op jit(solution)/shard_map/ppermute | solution.py:396
  62.9 11.5 %collective-permute-start.15 = (bf16[4,128,128]{2,1,0:T(8,128)(2,1)S(1)}, bf16[4,128,128]{2,1,0:T(8,128)(2,1)S(1)}, u32[]{:S(2)}, u32[]{:S(2)}) collective-permute-start(bf16[4,128,128]{2,1,0:T(8,128)(2,1)S(1)} %future_total.1), channel_id=1, source_target_pairs={{16,0},{24,8},{17,1},{25,9},{18,2},{26,10},{19,3},{27,11},{20,4},{... | collective-permute-start | bytes 393224 | tf_op jit(solution)/shard_map/ppermute | solution.py:430
  64.2 10.2 %collective-permute-start.14 = (bf16[4,128,128]{2,1,0:T(8,128)(2,1)S(1)}, bf16[4,128,128]{2,1,0:T(8,128)(2,1)S(1)}, u32[]{:S(2)}, u32[]{:S(2)}) collective-permute-start(bf16[4,128,128]{2,1,0:T(8,128)(2,1)S(1)} %future_total.1), channel_id=1, source_target_pairs={{8,0},{16,8},{24,16},{9,1},{17,9},{25,17},{10,2},{18,10},{26,18},{... | collective-permute-start | bytes 393224 | tf_op jit(solution)/shard_map/ppermute | solution.py:430
  75.3 6.3 %collective-permute-start.16 = (bf16[4,128,128]{2,1,0:T(8,128)(2,1)S(1)}, bf16[4,128,128]{2,1,0:T(8,128)(2,1)S(1)}, u32[]{:S(2)}, u32[]{:S(2)}) collective-permute-start(bf16[4,128,128]{2,1,0:T(8,128)(2,1)S(1)} %get-tuple-element.69), channel_id=1, source_target_pairs={{0,2},{1,3},{2,0},{3,1},{4,6},{5,7},{6,4},{7,5},{8,10},{9,11},{10,... | collective-permute-start | bytes 393224 | tf_op jit(solution)/shard_map/ppermute | solution.py:396
  76.2 5.4 %collective-permute-start.17 = (bf16[4,128,128]{2,1,0:T(8,128)(2,1)S(1)}, bf16[4,128,128]{2,1,0:T(8,128)(2,1)S(1)}, u32[]{:S(2)}, u32[]{:S(2)}) collective-permute-start(bf16[4,128,128]{2,1,0:T(8,128)(2,1)S(1)} %get-tuple-element.70), channel_id=1, source_target_pairs={{0,4},{1,5},{2,6},{3,7},{4,0},{5,1},{6,2},{7,3},{8,12},{9,13},{10,... | collective-permute-start | bytes 393224 | tf_op jit(solution)/shard_map/ppermute | solution.py:396
  77.7 5.9 %collective-permute-start.18 = (bf16[4,128,128]{2,1,0:T(8,128)(2,1)S(1)}, bf16[4,128,128]{2,1,0:T(8,128)(2,1)S(1)}, u32[]{:S(2)}, u32[]{:S(2)}) collective-permute-start(bf16[4,128,128]{2,1,0:T(8,128)(2,1)S(1)} %get-tuple-element.71), channel_id=1, source_target_pairs={{0,6},{1,7},{2,4},{3,5},{4,2},{5,3},{6,0},{7,1},{8,14},{9,15},{10,... | collective-permute-start | bytes 393224 | tf_op jit(solution)/shard_map/ppermute | solution.py:396
  84.9 2.6 %collective-permute-start.19 = (bf16[16,128,128]{2,1,0:T(8,128)(2,1)S(1)}, bf16[16,128,128]{2,1,0:T(8,128)(2,1)S(1)}, u32[]{:S(2)}, u32[]{:S(2)}) collective-permute-start(bf16[16,128,128]{2,1,0:T(8,128)(2,1)S(1)} %bitcast.23), channel_id=1, source_target_pairs={{0,1},{1,0},{2,3},{3,2},{4,5},{5,4},{6,7},{7,6},{8,9},{9,8},{10,11... | collective-permute-start | bytes 1572872 | tf_op jit(solution)/shard_map/ppermute | solution.py:391

commit v9 on v8

v9 whole, which is shorter than its diff:
```python
import functools

import jax
import jax.numpy as jnp
from jax import lax
from jax.experimental import pallas as pl
from jax.experimental.pallas import tpu as pltpu
from jax.sharding import Mesh, PartitionSpec as P

DH = 128
F32 = jnp.float32
BF16 = jnp.bfloat16
NN = (((1,), (0,)), ((), ()))
NT = (((1,), (1,)), ((), ()))
LAYER = ("x", "head")


def mul(a, b, dims):
    return lax.dot_general(a, b, dims, preferred_element_type=F32)


def feature(wide):
    return jnp.where(wide > 0, wide + 1.0, jnp.exp(jnp.minimum(wide, 0.0)))


def slope(wide):
    return jnp.where(wide > 0, 1.0, jnp.exp(jnp.minimum(wide, 0.0)))


def doc_ends(lens):
    ends, total = [], 0
    for j in range(lens.shape[0]):
        total = total + lens[j]
        ends.append(total)
    return ends


def doc_at(ends, where):
    found = 0
    for end in ends:
        found = found + jnp.where(where >= end, 1, 0)
    return found


def rows_of(ends, first, count):
    at = first + lax.broadcasted_iota(jnp.int32, (count, 1), 0)
    return doc_at(ends, at)


def columns_of(ends, first, count):
    at = first + lax.broadcasted_iota(jnp.int32, (1, count), 1)
    return doc_at(ends, at)


def visible(ends, first, count):
    row = lax.broadcasted_iota(jnp.int32, (count, count), 0)
    column = lax.broadcasted_iota(jnp.int32, (count, count), 1)
    together = rows_of(ends, first, count) == columns_of(ends, first, count)
    return (row >= column) & together, (row <= column) & together


def identity(count):
    row = lax.broadcasted_iota(jnp.int32, (count, count), 0)
    column = lax.broadcasted_iota(jnp.int32, (count, count), 1)
    return jnp.where(row == column, 1.0, 0.0).astype(BF16)


def turn(array, eye):
    return mul(eye, array, NT).astype(BF16)


def head_mask(ends, first, count):
    return rows_of(ends, first, count) == doc_at(ends, first)


def tail_mask(ends, first, count):
    return rows_of(ends, first, count) == doc_at(ends, first + count - 1)


def cols(h):
    return slice(h * DH, (h + 1) * DH)


def bunches(heads, size=8):
    return [range(h, min(h + size, heads)) for h in range(0, heads, size)]


def halves(wide):
    high = wide.astype(BF16)
    return jnp.concatenate([high, (wide - high.astype(F32)).astype(BF16)], axis=1)


def tail_kernel(lens, place, k, v, *rest):
    if len(rest) > 1:
        q, g, out, three, last = rest
        three[0], three[1], three[2] = q[...], k[...], v[...]
        last[...] = g[...]
    else:
        (out,) = rest
    count = k.shape[0]
    tail = tail_mask(doc_ends(lens), place[0] * count, count)
    eye = identity(DH)
    for hs in bunches(out.shape[0]):
        fks = [
            jnp.where(tail, feature(k[:, cols(h)].astype(F32)), 0.0).astype(BF16) for h in hs
        ]
        turned = [turn(fk, eye) for fk in fks]
        sums = [mul(fk, v[:, cols(h)], NN).astype(BF16) for h, fk in zip(hs, turned)]
        for h, value in zip(hs, sums):
            out[h] = value


def pair_docs(lens, place, count):
    ends = doc_ends(lens)
    core = place[2] & 1
    own, mate = place[0] * count, (place[0] + 1 - 2 * core) * count

    def along(axis):
        shape = (2 * count, 1) if axis == 0 else (1, 2 * count)
        at = lax.broadcasted_iota(jnp.int32, shape, axis)
        return jnp.where(at < count, own + at, mate + at - count)

    rows, columns = along(0), along(1)
    row_docs, column_docs = doc_at(ends, rows), doc_at(ends, columns)
    seen = (rows >= columns) & (row_docs == column_docs)
    first = (place[0] - core) * count
    late = columns >= first + count
    return (
        seen,
        row_docs == doc_at(ends, first),
        column_docs == doc_at(ends, first),
        late & (column_docs == doc_at(ends, first + count)),
    )


def fill_kernel(lens, place, array, held, after, out):
    out[...] = array[...]


def chip_kernel(lens, place, q, k, v, mate, part, head_fq, turned):
    count = q.shape[0]
    seen, head, _, _ = pair_docs(lens, place, count)
    eye = identity(DH)

    def both(mine, slot, h):
        return jnp.concatenate([mine[:, cols(h)], mate[slot, :, cols(h)]], axis=0)

    for hs in bunches(turned.shape[0], 4):
        wides = [feature(both(q, 0, h).astype(F32)) for h in hs]
        fks = [feature(both(k, 1, h).astype(F32)).astype(BF16) for h in hs]
        kept = [
            jnp.where(seen, mul(wide.astype(BF16), fk, NT), 0.0).astype(BF16)
            for wide, fk in zip(wides, fks)
        ]
        parts = [mul(s, both(v, 2, h), NN) for h, s in zip(hs, kept)]
        heads = [jnp.where(head, wide, 0.0).astype(BF16) for wide in wides]
        turns = [turn(wide.astype(BF16), eye) for wide in wides]
        for h, p, f, t in zip(hs, parts, heads, turns):
            part[:, cols(h)] = p
            head_fq[:, cols(h)] = f
            turned[h] = t


def norm_kernel(lens, place, head_fq, turned, g, mate_g, part, *rest):
    kept = rest[-1]
    chips = (len(rest) - 7) // 2
    incoming, (out, mate_out, ga_out, mate_ga, came, lates) = (
        rest[:chips],
        rest[chips : chips + 6],
    )
    states = rest[chips + 6 : -1]
    count = g.shape[0]
    _, _, head, late = pair_docs(lens, place, count)
    heads = turned.shape[0]
    step = pl.program_id(0)
    chip = place[2] >> 1

    @pl.when(step == 0)
    def _():
        for n, state in enumerate(incoming):
            owned = state.shape[0]
            came[pl.ds((chip ^ n) * owned, owned)] = state[...]

    weights = jnp.full((2 * DH, DH), 1.0 / DH, BF16)
    for hs in bunches(heads, 4):
        atts = [
            part[:, cols(h)] + mul(head_fq[:, cols(h)], came[step * heads + h], NN) for h in hs
        ]
        gos = [
            jnp.concatenate([g[:, cols(h)], mate_g[:, cols(h)]], axis=0).astype(F32) for h in hs
        ]
        means = [
            mul(jnp.concatenate([halves(att * att), halves(go * att)], axis=0), weights, NN)
            for att, go in zip(atts, gos)
        ]
        invs = [lax.rsqrt(m[: 2 * count] + 1e-05) for m in means]
        norms = [att * inv for att, inv in zip(atts, invs)]
        gas = [
            ((go - normed * (m[2 * count :] * inv)) * inv).astype(BF16)
            for go, normed, m, inv in zip(gos, norms, means, invs)
        ]
        sums = []
        for h, ga in zip(hs, gas):
            wide = turned[h].astype(F32)
            two = jnp.concatenate([jnp.where(head, wide, 0.0), jnp.where(late, wide, 0.0)], axis=0)
            sums.append(mul(two.astype(BF16), ga, NN).astype(BF16))
        for h, normed, ga, value in zip(hs, norms, gas, sums):
            normed = normed.astype(BF16)
            out[:, cols(h)], mate_out[:, cols(h)] = normed[:count], normed[count:]
            ga_out[:, cols(h)], mate_ga[:, cols(h)] = ga[:count], ga[count:]
            kept[step * heads + h] = value[:DH]
            lates[h] = value[DH:]

    @pl.when(step == pl.num_programs(0) - 1)
    def _():
        for n, state in enumerate(states):
            owned = state.shape[0]
            state[...] = kept[pl.ds((chip ^ n) * owned, owned)]


def inner_kernel(lens, place, q, k, v, mine_ga, other_ga, *rest):
    passed, earlier, (gq, gk, gv, came) = rest[:2], rest[2:4], rest[5:]
    count = q.shape[0]
    heads = q.shape[1] // DH
    step = pl.program_id(0)
    own = step < pl.num_programs(0) // 2

    @pl.when(step == 0)
    def _():
        half = came.shape[0] // 2
        core, (early_b, early_e, late_b, late_e) = chip_docs(lens, place, count)
        by_chip = jnp.where(core == 0, 1.0, same(late_b, early_b))
        by_mate = jnp.where(core == 0, 0.0, same(late_b, early_e))
        for j in range(2):
            came[pl.ds(j * half, half)] = (
                passed[j][...].astype(F32) * by_chip + earlier[j][...].astype(F32) * by_mate
            ).astype(BF16)

    ends = doc_ends(lens)
    first = place[0] * count
    seen, seeing = visible(ends, first, count)
    head = head_mask(ends, first, count)
    for hs in bunches(heads):
        wides = [q[:, cols(h)].astype(F32) for h in hs]
        fqs = [feature(wide).astype(BF16) for wide in wides]
        fks = [feature(k[:, cols(h)].astype(F32)).astype(BF16) for h in hs]
        gas = [jnp.where(own, mine_ga[:, cols(h)], other_ga[:, cols(h)]) for h in hs]
        gss = [
            jnp.where(seen, mul(ga, v[:, cols(h)], NT), 0.0).astype(BF16)
            for h, ga in zip(hs, gas)
        ]
        totals = [
            mul(gs, fk, NN) + jnp.where(head, mul(ga, came[step * heads + h], NT), 0.0)
            for h, gs, fk, ga in zip(hs, gss, fks, gas)
        ]
        flipped = [
            jnp.where(seeing, mul(v[:, cols(h)], ga, NT), 0.0).astype(BF16)
            for h, ga in zip(hs, gas)
        ]
        scores = [
            jnp.where(seeing, mul(fk, fq, NT), 0.0).astype(BF16) for fq, fk in zip(fqs, fks)
        ]
        gks = [mul(gs, fq, NN) for gs, fq in zip(flipped, fqs)]
        gvs = [mul(s, ga, NN) for s, ga in zip(scores, gas)]
        for h, total, wide, a, b in zip(hs, totals, wides, gks, gvs):
            gq[:, cols(h)] = (total * slope(wide)).astype(BF16)
            gk[:, cols(h)] = a
            gv[:, cols(h)] = b


def last_kernel(chips, lens, place, k, v, gk_part, gv_part, late, *rest):
    gk, gv, came = rest[-3:]
    outgoing = rest[:chips]
    count = k.shape[0]
    heads = k.shape[1] // DH
    step = pl.program_id(0)

    @pl.when(step == 0)
    def _():
        core, (early_b, early_e, late_b, late_e) = chip_docs(lens, place, count)
        chip = place[2] >> 1
        by_far = jnp.where(core == 0, same(early_e, late_e), 1.0)
        by_late = jnp.where(core == 0, same(early_e, late_b), 0.0)
        for n, state in enumerate(outgoing):
            owned = state.shape[0]
            at = pl.ds((chip ^ n) * owned, owned)
            came[at] = (
                state[...].astype(F32) * by_far + late[at].astype(F32) * by_late
            ).astype(BF16)

    tail = tail_mask(doc_ends(lens), place[0] * count, count)
    for hs in bunches(heads):
        wides = [k[:, cols(h)].astype(F32) for h in hs]
        fks = [jnp.where(tail, feature(wide), 0.0).astype(BF16) for wide in wides]
        vts = [jnp.where(tail, v[:, cols(h)].astype(F32), 0.0).astype(BF16) for h in hs]
        states = [came[step * heads + h] for h in hs]
        gks = [gk_part[:, cols(h)] + mul(vt, o, NT) for h, vt, o in zip(hs, vts, states)]
        gvs = [gv_part[:, cols(h)] + mul(fk, o, NN) for h, fk, o in zip(hs, fks, states)]
        for h, a, wide, b in zip(hs, gks, wides, gvs):
            gk[:, cols(h)] = (a * slope(wide)).astype(BF16)
            gv[:, cols(h)] = b.astype(BF16)


def same(a, b):
    return jnp.where(a == b, 1.0, 0.0).astype(F32)


def chip_docs(lens, place, count):
    ends = doc_ends(lens)
    core = place[2] & 1
    start = (place[0] - core) * count
    marks = (start, start + count - 1, start + count, start + 2 * count - 1)
    return core, [doc_at(ends, mark) for mark in marks]


def merge_kernel(count, chips, lens, place, mine, other, *rest):
    outs = rest[-chips - 2 : -2]
    core, (early_b, early_e, late_b, late_e) = chip_docs(lens, place, count)
    far = same(early_e, late_e)
    mine_by = jnp.where(core == 0, far, 1.0)
    other_by = jnp.where(core == 0, 1.0, far)
    chip = place[2] >> 1
    for n, out in enumerate(outs):
        at = chip ^ n
        out[...] = (mine[at].astype(F32) * mine_by + other[at].astype(F32) * other_by).astype(
            BF16
        )


def total_kernel(forward, unit, members, passed, lens, place, *rest):
    states, total, held = rest[:members], rest[members + passed], rest[-1]
    chip = place[2] >> 1
    for n, state in enumerate(states):
        held[chip ^ n] = state[...]
    ends = doc_ends(lens)
    layer = place[1] * (members * unit)
    carry = None
    for step in range(members):
        i = step if forward else members - 1 - step
        mine = held[i].astype(F32)
        edge = layer + ((i + 1) * unit - 1 if forward else i * unit)
        here = doc_at(ends, edge)
        if carry is not None:
            mine = mine + carry * same(here, previous)
        carry, previous = mine, here
    total[...] = carry.astype(BF16)


def prefix_kernel(forward, unit, members, unread, lens, place, *rest):
    states, outs, (held, sums) = rest[:members], rest[-members - 2 : -2], rest[-2:]
    others = rest[members + unread : -members - 2]
    chip = place[2] >> 1
    for n, state in enumerate(states):
        held[chip ^ n] = state[...]
    span = members * unit
    ends = doc_ends(lens)
    layer = place[1] * span
    sign = -1 if forward else 1
    previous = doc_at(ends, layer - 1 if forward else layer + span)
    carry = None
    for s, other in enumerate(others):
        far = layer + sign * s * span
        there = doc_at(ends, far - 1 if forward else far + span)
        term = other[...].astype(F32) * same(there, previous)
        carry = term if carry is None else carry + term
    for step in range(members):
        i = step if forward else members - 1 - step
        near, far = layer + i * unit, layer + (i + 1) * unit - 1
        if not forward:
            near, far = far, near
        if carry is None:
            sums[i] = jnp.zeros(sums.shape[1:], BF16)
        else:
            sums[i] = (carry * same(doc_at(ends, near), previous)).astype(BF16)
        if step < members - 1:
            here = doc_at(ends, far)
            mine = held[i].astype(F32)
            if carry is not None:
                mine = mine + carry * same(here, previous)
            carry, previous = mine, here
    for n, out in enumerate(outs):
        out[...] = sums[chip ^ n]


SMALL = pltpu.CompilerParams(
    dimension_semantics=("arbitrary",), vmem_limit_bytes=16 * 1024 * 1024
)

def local(queries, keys, values, out_grad, doc_lengths):
    count, width = queries.shape
    heads = width // DH
    layers = lax.axis_size("z")
    members = lax.axis_size("x") * lax.axis_size("head")
    owned = heads // members
    half = heads // 2
    reach = range(1, min(layers - 1, -(-layers // 2)) + 1)
    place = jnp.stack(
        [lax.axis_index(("z", "x", "head")), lax.axis_index("z"), lax.axis_index(LAYER)]
    ).astype(jnp.int32)
    chips = members // 2
    step_heads = max(n for n in (8, 4, 2, 1) if half % n == 0)
    steps = half // step_heads

    def held_in_hbm(arg):
        return pltpu.with_memory_space_constraint(arg, pltpu.HBM)

    def at(parity):
        if parity is None:
            return lambda i, lens, place: i
        return lambda i, lens, place: ((place[2] & 1) ^ parity) * steps + i

    def tokens(parity):
        block = at(parity)
        return pl.BlockSpec((count, step_heads * DH), lambda *a: (0, block(*a)))

    whole = pl.BlockSpec((half, DH, DH), lambda *a: (0, 0, 0))
    halved = pl.BlockSpec((step_heads, DH, DH), lambda i, *a: (i, 0, 0))
    untouched = pl.BlockSpec(memory_space=pl.ANY)
    token_bf = pltpu.HBM((count, width), BF16)
    token_f32 = jax.ShapeDtypeStruct((count, width), F32)
    owned_bf = jax.ShapeDtypeStruct((owned, DH, DH), BF16)
    half_bf = jax.ShapeDtypeStruct((half, DH, DH), BF16)

    def run(kernel, grid, ins, outs, shapes, scratch, args, cost, name, params=SMALL, aliases={}):
        flops, moved, exps = cost
        return pl.pallas_call(
            kernel,
            grid_spec=pltpu.PrefetchScalarGridSpec(
                num_scalar_prefetch=2,
                grid=(grid,),
                in_specs=ins,
                out_specs=outs,
                scratch_shapes=scratch,
            ),
            out_shape=shapes,
            input_output_aliases=aliases,
            compiler_params=params,
            cost_estimate=pl.CostEstimate(
                flops=flops, bytes_accessed=moved, transcendentals=exps
            ),
            name=name,
        )(doc_lengths, place, *args)

    product = 2 * half * count * DH * DH
    array = half * count * DH * 2
    all_states = pltpu.VMEM((heads, DH, DH), BF16)
    block = 2 if owned % 2 == 0 else 1
    single = pl.BlockSpec((block, DH, DH), lambda i, *a: (i, 0, 0))
    grouped = pl.BlockSpec((chips, block, DH, DH), lambda i, *a: (0, i, 0, 0))
    buffer = pltpu.VMEM((chips, block, DH, DH), BF16)
    combining = (4 * half * DH * DH, 4 * half * DH * DH, 0)
    moves = owned // block

    def swap(state):
        return lax.ppermute(state, LAYER, [(i, i ^ 1) for i in range(members)])

    def exchange(states):
        pairs = [[(i, i ^ (2 * n)) for i in range(members)] for n in range(chips)]
        return [
            state if n == 0 else lax.ppermute(state, LAYER, pairs[n])
            for n, state in enumerate(states)
        ]

    def reach_out(merged, along, forward, name):
        came = exchange(merged)
        total, *along = run(
            functools.partial(total_kernel, forward, 2 * count, chips, len(along)),
            moves,
            [single] * chips + [untouched] * len(along),
            [single] + [untouched] * len(along),
            [owned_bf] + [jax.ShapeDtypeStruct(array.shape, array.dtype) for array in along],
            [buffer],
            [*came, *along],
            combining,
            name + "_total",
            aliases={2 + chips + j: 1 + j for j in range(len(along))},
        )
        others = []
        for s in reach:
            pairs = [(i, i + s) if forward else (i + s, i) for i in range(layers - s)]
            others.append(lax.ppermute(total, "z", pairs))
        return came, others, total, along

    def spread(came, others, after, forward, name):
        sums = run(
            functools.partial(prefix_kernel, forward, 2 * count, chips, len(after)),
            moves,
            [single] * chips + [untouched] * len(after) + [single] * len(others),
            [single] * chips,
            [owned_bf] * chips,
            [buffer, buffer],
            [*came, *after, *others],
            combining,
            name + "_prefix",
        )
        return exchange(sums)

    narrow = (count, half * DH)
    lane = pl.BlockSpec((count, step_heads * DH), lambda i, *a: (0, i))
    pinned = [held_in_hbm(array) for array in (queries, keys, values, out_grad)]
    tail_work = (product, 3 * array, half * count * DH)
    copies = [
        jax.ShapeDtypeStruct((3, *narrow), BF16),
        jax.ShapeDtypeStruct(narrow, BF16),
    ]
    mate_tail, mate_three, mate_g = run(
        tail_kernel,
        steps,
        [tokens(1)] * 4,
        [halved, pl.BlockSpec((3, count, step_heads * DH), lambda i, *a: (0, 0, i)), lane],
        [half_bf, *copies],
        [],
        (pinned[1], pinned[2], pinned[0], pinned[3]),
        tail_work,
        "tail_mate",
    )
    (own_tail,) = run(
        tail_kernel,
        steps,
        [tokens(0)] * 2,
        [halved],
        [half_bf],
        [],
        pinned[1:3],
        tail_work,
        "tail_own",
    )
    mine = own_tail.reshape(chips, owned, DH, DH)
    other = swap(mate_tail).reshape(chips, owned, DH, DH)
    *merged, mate_three, mate_g = run(
        functools.partial(merge_kernel, count, chips),
        moves,
        [grouped] * 2 + [untouched] * 2,
        [single] * chips + [untouched] * 2,
        [owned_bf] * chips + copies,
        [],
        (mine, other, mate_three, mate_g),
        combining,
        "carried_chip",
        aliases={4: chips, 5: chips + 1},
    )
    came, others, _, _ = reach_out(merged, (), True, "carried")

    mate_three, mate_g = swap(mate_three), swap(mate_g)
    few = 4 if half % 4 == 0 else 1
    parts = half // few

    def own_few(i, lens, place):
        return 0, (place[2] & 1) * parts + i

    own_tokens = pl.BlockSpec((count, few * DH), own_few)
    pair_tokens = pl.BlockSpec((2 * count, few * DH), lambda i, *a: (0, i))
    lane_few = pl.BlockSpec((count, few * DH), lambda i, *a: (0, i))
    turns = pl.BlockSpec((few, DH, 2 * count), lambda i, *a: (i, 0, 0))
    part, head_fq, turned = run(
        chip_kernel,
        parts,
        [own_tokens] * 3 + [pl.BlockSpec((3, count, few * DH), lambda i, *a: (0, 0, i))],
        [pair_tokens, pair_tokens, turns],
        [
            jax.ShapeDtypeStruct((2 * count, half * DH), F32),
            jax.ShapeDtypeStruct((2 * count, half * DH), BF16),
            jax.ShapeDtypeStruct((half, DH, 2 * count), BF16),
        ],
        [],
        (queries, keys, values, mate_three),
        (10 * product, 14 * array, 4 * half * count * DH),
        "within_chip",
    )
    late_tail = swap(own_tail)
    chip_in = spread(came, others, (part, late_tail), True, "carried")
    few_states = pl.BlockSpec((few, DH, DH), lambda i, *a: (i, 0, 0))
    one_owner = pl.BlockSpec((owned, DH, DH), lambda *a: (0, 0, 0))
    half_states = pltpu.VMEM((half, DH, DH), BF16)
    narrow_bf = jax.ShapeDtypeStruct(narrow, BF16)
    attn_half, mate_out, mine_ga, mate_ga, mine_in, mine_late, *merged = run(
        norm_kernel,
        parts,
        [pair_tokens, turns, own_tokens, lane_few, pair_tokens] + [one_owner] * chips,
        [own_tokens] + [lane_few] * 3 + [whole, few_states] + [one_owner] * chips,
        [token_bf] + [narrow_bf] * 3 + [half_bf] * 2 + [owned_bf] * chips,
        [half_states],
        (head_fq, turned, out_grad, mate_g, part, *chip_in),
        (8 * product, 16 * array, 2 * half * count * DH),
        "normed",
    )
    came, others, total, (mate_out, mine_late) = reach_out(
        merged, (mate_out, mine_late), False, "future"
    )
    other_ga, other_in = swap(mate_ga), swap(mine_in)
    other_ga = swap(mate_ga)
    def both(i, lens, place):
        return ((place[2] & 1) ^ (i // steps)) * steps + i % steps

    spans = pl.BlockSpec((count, step_heads * DH), lambda *a: (0, both(*a)))
    lanes = pl.BlockSpec((count, step_heads * DH), lambda i, *a: (0, i % steps))
    grad_queries, gk_part, gv_part = run(
        inner_kernel,
        2 * steps,
        [spans] * 3 + [lanes] * 2 + [whole] * 4 + [untouched],
        [spans] * 3,
        [token_bf, token_f32, token_f32],
        [all_states],
        (
            queries,
            keys,
            values,
            mine_ga,
            other_ga,
            mine_in,
            other_in,
            other.reshape(half, DH, DH),
            late_tail,
            total,
        ),
        (16 * product, 22 * array, 4 * half * count * DH),
        "grads_within",
    )
    late = (mine_late, swap(mine_late))
    chip_out = spread(came, others, (gk_part,), False, "future")
    (attn_out,) = run(
        fill_kernel,
        steps,
        [lane, untouched, untouched],
        [tokens(1)],
        [token_bf],
        [],
        (swap(mate_out), held_in_hbm(attn_half), chip_out[0]),
        (0, 2 * array, 0),
        "attn_out",
        aliases={3: 0},
    )
    outgoing = (chip_out, [swap(state) for state in chip_out])
    made = ()
    for parity in (0, 1):
        after = (held_in_hbm(attn_out),) if parity == 0 else made
        made = tuple(
            run(
                functools.partial(last_kernel, chips),
                steps,
                [tokens(parity)] * 4
                + [whole]
                + [one_owner] * chips
                + [untouched] * len(after),
                [tokens(parity)] * 2,
                [token_bf] * 2,
                [half_states],
                (keys, values, gk_part, gv_part, late[parity], *outgoing[parity], *after),
                (2 * product, 9 * array, half * count * DH),
                f"grads_last_{parity}",
                aliases={7 + chips + j: j for j in range(2)} if parity else {},
            )
        )
    return attn_out, grad_queries, *made


def solution(mesh):
    n_seq, n_head = mesh.shape["seq"], mesh.shape["head"]
    inner = 2 if n_seq % 2 == 0 else 1
    fine = Mesh(mesh.devices.reshape(n_seq // inner, inner, n_head), ("z", "x", "head"))
    rows = P(("z", "x", "head"), None)
    return jax.shard_map(
        local,
        mesh=fine,
        in_specs=(rows, rows, rows, rows, P()),
        out_specs=(rows, rows, rows, rows),
        check_vma=False,
    )
```

time: 90.8 us -> 91.5 us (level)
  starting transfers between devices: 26.9 us -> 30.5 us
  waiting for transfers between devices: 27.8 us -> 25.9 us
    ppermute x12, starting transfers between devices: 15.1 us -> 17.4 us  [exchange(): lax.ppermute(state, LAYER, pairs[n])]
    ppermute x4 -> x12, waiting for transfers between devices: 1.54 us -> 0.03 us  [swap(): return lax.ppermute(state, LAYER, [(i, i ^ 1) for i in range(members)])]
    ppermute x4 -> x12, starting transfers between devices: 1.14 us -> 2.57 us  [swap(): return lax.ppermute(state, LAYER, [(i, i ^ 1) for i in range(members)])]
    pallas_call x16 -> x13, Pallas kernels: 33.6 us -> 33.2 us  [run(): pl.pallas_call(kernel, grid_spec=pltpu.PrefetchScalarGridSpec(num_scalar_...]
  transfers between devices with their start and end apart: 20 -> 28, of which waited for: 13 -> 12; matrix products, arithmetic and copies ran while one was open for 0% -> 0% of each run, Pallas kernels for 20% -> 23%
where the time goes in v9:
time: 91.5 us; the launch traced here: 91.2 us
  Pallas kernels  33.2 us (36%)
  starting transfers between devices  30.5 us (33%)
  waiting for transfers between devices  25.9 us (28%)
    pallas_call x13, Pallas kernels, run(): pl.pallas_call(kernel, grid_spec=pltpu.PrefetchScalarGridSpec(num_scalar_...  33.2 us
    ppermute x12, waiting for transfers between devices, exchange(): lax.ppermute(state, LAYER, pairs[n])  22.2 us
    ppermute x12, starting transfers between devices, exchange(): lax.ppermute(state, LAYER, pairs[n])  17.4 us
    ppermute x4, starting transfers between devices, reach_out(): others.append(lax.ppermute(total, 'z', pairs))  10.6 us
    ppermute x4, waiting for transfers between devices, reach_out(): others.append(lax.ppermute(total, 'z', pairs))  3.66 us
    ppermute x12, starting transfers between devices, swap(): return lax.ppermute(state, LAYER, [(i, i ^ 1) for i in range(members)])  2.57 us
  transfers between devices with their start and end apart: 28, of which 12 were waited for; matrix products, arithmetic and copies ran while one was open for 0% of the time, Pallas kernels for 23%

profile of v9, /device:TPU:0, one launch (start us, length us, event | category | flops | bytes accessed | tf_op | source)
XLA Modules:
  0.0 91.2 jit_solution(14708190775711400211)
XLA Ops:
  0.6 0.1 pad_add_fusion.place
  0.7 0.7 copy-done.4
  1.4 3.0 %tail_mate.1 = (bf16[16,128,128]{2,1,0:T(8,128)(2,1)S(1)}, bf16[3,128,2048]{2,1,0:T(8,128)(2,1)S(1)}, bf16[128,2048]{1,0:T(8,128)(2,1)S(1)}) custom-call(s32[8]{0:T(128)S(1)} %copy-done.4, s32[3]{0:T(128)S(1)} %pad_add_fusion.place, bf16[128,4096]{1,0:T(8,128)(2,1)} %k.11, bf16[128,4096]{1,0:T(8,128)(2,1)} %v.11, bf16[128,4096]{1,0:T(8,128)(2,1)} %q.3, ...), custom_call_target="tpu_custom_call" | custom-call | flops 67108864 | bytes 1572864 | tf_op jit(solution)/shard_map/tail_mate/pallas_call | solution.py:426
  4.4 0.5 collective-permute-start
  4.9 2.6 %tail_own.1 = bf16[16,128,128]{2,1,0:T(8,128)(2,1)S(1)} custom-call(s32[8]{0:T(128)S(1)} %copy-done.4, s32[3]{0:T(128)S(1)} %pad_add_fusion.place, bf16[128,4096]{1,0:T(8,128)(2,1)} %k.11, bf16[128,4096]{1,0:T(8,128)(2,1)} %v.11), custom_call_target="tpu_custom_call" | custom-call | flops 67108864 | bytes 1572864 | tf_op jit(solution)/shard_map/tail_own/pallas_call | solution.py:426
  7.5 0.0 copy-start
  7.5 0.0 copy-start.1
  7.5 0.0 copy-start.2
  7.5 0.9 %carried_chip.1 = (bf16[4,128,128]{2,1,0:T(8,128)(2,1)S(1)}, bf16[4,128,128]{2,1,0:T(8,128)(2,1)S(1)}, bf16[4,128,128]{2,1,0:T(8,128)(2,1)S(1)}, bf16[4,128,128]...) custom-call(s32[8]{0:T(128)S(1)} %copy-done.4, ...), custom_call_target="tpu_custom_call", output_to_operand_aliasing={{4}: (4, {}), {5}: (5, {})} | custom-call | flops 1048576 | bytes 1048576 | tf_op jit(solution)/shard_map/carried_chip/pallas_call | solution.py:426
  8.4 0.1 collective-permute-start.1
  8.6 0.4 collective-permute-start.6
  9.0 2.6 %collective-permute-start.3 = (bf16[4,128,128]{2,1,0:T(8,128)(2,1)S(1)}, bf16[4,128,128]{2,1,0:T(8,128)(2,1)S(1)}, u32[]{:S(2)}, u32[]{:S(2)}) collective-permute-start(bf16[4,128,128]{2,1,0:T(8,128)(2,1)S(1)} %get-tuple-element.53), channel_id=1, source_target_pairs={{0,2},{1,3},{2,0},{3,1},{4,6},{5,7},{6,4},{7,5},{8,10},{9,11},{10,... | collective-permute-start | bytes 393224 | tf_op jit(solution)/shard_map/ppermute | solution.py:460
  11.6 0.2 collective-permute-start.2
  11.8 1.5 %collective-permute-start.4 = (bf16[4,128,128]{2,1,0:T(8,128)(2,1)S(1)}, bf16[4,128,128]{2,1,0:T(8,128)(2,1)S(1)}, u32[]{:S(2)}, u32[]{:S(2)}) collective-permute-start(bf16[4,128,128]{2,1,0:T(8,128)(2,1)S(1)} %get-tuple-element.54), channel_id=1, source_target_pairs={{0,4},{1,5},{2,6},{3,7},{4,0},{5,1},{6,2},{7,3},{8,12},{9,13},{10,... | collective-permute-start | bytes 393224 | tf_op jit(solution)/shard_map/ppermute | solution.py:460
  13.3 2.4 %collective-permute-done.3.rest_1_ = bf16[4,128,128]{2,1,0:T(8,128)(2,1)S(1)} collective-permute-done((bf16[4,128,128]{2,1,0:T(8,128)(2,1)S(1)}, bf16[4,128,128]{2,1,0:T(8,128)(2,1)S(1)}, u32[]{:S(2)}, u32[]{:S(2)}) %collective-permute-start.3) | collective-permute-done | bytes 131104 | tf_op jit(solution)/shard_map/ppermute | solution.py:460
  15.7 2.7 %collective-permute-start.5 = (bf16[4,128,128]{2,1,0:T(8,128)(2,1)S(1)}, bf16[4,128,128]{2,1,0:T(8,128)(2,1)S(1)}, u32[]{:S(2)}, u32[]{:S(2)}) collective-permute-start(bf16[4,128,128]{2,1,0:T(8,128)(2,1)S(1)} %get-tuple-element.55), channel_id=1, source_target_pairs={{0,6},{1,7},{2,4},{3,5},{4,2},{5,3},{6,0},{7,1},{8,14},{9,15},{10,... | collective-permute-start | bytes 393224 | tf_op jit(solution)/shard_map/ppermute | solution.py:460
  18.4 0.0 collective-permute-done.4.rest_2_
  18.4 3.5 %collective-permute-done.5.rest_3_ = bf16[4,128,128]{2,1,0:T(8,128)(2,1)S(1)} collective-permute-done((bf16[4,128,128]{2,1,0:T(8,128)(2,1)S(1)}, bf16[4,128,128]{2,1,0:T(8,128)(2,1)S(1)}, u32[]{:S(2)}, u32[]{:S(2)}) %collective-permute-start.5) | collective-permute-done | bytes 131104 | tf_op jit(solution)/shard_map/ppermute | solution.py:460
  21.9 0.7 carried_total.1
  22.6 3.5 %collective-permute-start.7 = (bf16[4,128,128]{2,1,0:T(8,128)(2,1)S(1)}, bf16[4,128,128]{2,1,0:T(8,128)(2,1)S(1)}, u32[]{:S(2)}, u32[]{:S(2)}) collective-permute-start(bf16[4,128,128]{2,1,0:T(8,128)(2,1)S(1)} %carried_total.1), channel_id=1, source_target_pairs={{0,8},{8,16},{16,24},{1,9},{9,17},{17,25},{2,10},{10,18},{18,26},{... | collective-permute-start | bytes 393224 | tf_op jit(solution)/shard_map/ppermute | solution.py:481
  26.1 4.5 %collective-permute-start.8 = (bf16[4,128,128]{2,1,0:T(8,128)(2,1)S(1)}, bf16[4,128,128]{2,1,0:T(8,128)(2,1)S(1)}, u32[]{:S(2)}, u32[]{:S(2)}) collective-permute-start(bf16[4,128,128]{2,1,0:T(8,128)(2,1)S(1)} %carried_total.1), channel_id=1, source_target_pairs={{0,16},{8,24},{1,17},{9,25},{2,18},{10,26},{3,19},{11,27},{4,20},{... | collective-permute-start | bytes 393224 | tf_op jit(solution)/shard_map/ppermute | solution.py:481
  30.7 4.3 %within_chip.1 = (f32[256,2048]{1,0:T(8,128)S(1)}, bf16[256,2048]{1,0:T(8,128)(2,1)S(1)}, bf16[16,128,256]{2,1,0:T(8,128)(2,1)S(1)}) custom-call(s32[8]{0:T(128)S(1)} %copy-done.4, s32[3]{0:T(128)S(1)} %pad_add_fusion.place, bf16[128,4096]{1,0:T(8,128)(2,1)S(1)} %copy-done.2, bf16[128,4096]{1,0:T(8,128)(2,1)S(1)} %copy-done, ...), custom_call_target="tpu_custom_call" | custom-call | flops 671088640 | bytes 7340032 | tf_op jit(solution)/shard_map/within_chip/pallas_call | solution.py:426
  35.0 0.0 copy-start.3
  35.0 0.0 collective-permute-done.8.rest_7_
  35.0 0.9 carried_prefix.1
  35.9 1.6 %collective-permute-start.9 = (bf16[4,128,128]{2,1,0:T(8,128)(2,1)S(1)}, bf16[4,128,128]{2,1,0:T(8,128)(2,1)S(1)}, u32[]{:S(2)}, u32[]{:S(2)}) collective-permute-start(bf16[4,128,128]{2,1,0:T(8,128)(2,1)S(1)} %get-tuple-element.57), channel_id=1, source_target_pairs={{0,2},{1,3},{2,0},{3,1},{4,6},{5,7},{6,4},{7,5},{8,10},{9,11},{10,... | collective-permute-start | bytes 393224 | tf_op jit(solution)/shard_map/ppermute | solution.py:460
  37.5 1.5 %collective-permute-start.10 = (bf16[4,128,128]{2,1,0:T(8,128)(2,1)S(1)}, bf16[4,128,128]{2,1,0:T(8,128)(2,1)S(1)}, u32[]{:S(2)}, u32[]{:S(2)}) collective-permute-start(bf16[4,128,128]{2,1,0:T(8,128)(2,1)S(1)} %get-tuple-element.58), channel_id=1, source_target_pairs={{0,4},{1,5},{2,6},{3,7},{4,0},{5,1},{6,2},{7,3},{8,12},{9,13},{10,... | collective-permute-start | bytes 393224 | tf_op jit(solution)/shard_map/ppermute | solution.py:460
  39.0 0.5 collective-permute-start.11
  39.5 2.9 %collective-permute-done.9.rest_1_ = bf16[4,128,128]{2,1,0:T(8,128)(2,1)S(1)} collective-permute-done((bf16[4,128,128]{2,1,0:T(8,128)(2,1)S(1)}, bf16[4,128,128]{2,1,0:T(8,128)(2,1)S(1)}, u32[]{:S(2)}, u32[]{:S(2)}) %collective-permute-start.9) | collective-permute-done | bytes 131104 | tf_op jit(solution)/shard_map/ppermute | solution.py:460
  42.3 0.1 collective-permute-done.10.rest_2_
  42.5 2.4 %collective-permute-done.11.rest_3_ = bf16[4,128,128]{2,1,0:T(8,128)(2,1)S(1)} collective-permute-done((bf16[4,128,128]{2,1,0:T(8,128)(2,1)S(1)}, bf16[4,128,128]{2,1,0:T(8,128)(2,1)S(1)}, u32[]{:S(2)}, u32[]{:S(2)}) %collective-permute-start.11) | collective-permute-done | bytes 131104 | tf_op jit(solution)/shard_map/ppermute | solution.py:460
  44.9 5.3 %normed.1 = (bf16[128,4096]{1,0:T(8,128)(2,1)}, bf16[128,2048]{1,0:T(8,128)(2,1)S(1)}, bf16[128,2048]{1,0:T(8,128)(2,1)S(1)}, bf16[128,2048]{1,0:T(8,128)(2,1)S(...) custom-call(s32[8]{0:T(128)S(1)} %copy-done.4, ...), custom_call_target="tpu_custom_call" | custom-call | flops 536870912 | bytes 8388608 | tf_op jit(solution)/shard_map/normed/pallas_call | solution.py:426
  50.2 0.0 collective-permute-start.16
  50.2 0.5 collective-permute-start.17
  50.7 0.5 collective-permute-start.12
  51.2 1.5 %collective-permute-start.13 = (bf16[4,128,128]{2,1,0:T(8,128)(2,1)S(1)}, bf16[4,128,128]{2,1,0:T(8,128)(2,1)S(1)}, u32[]{:S(2)}, u32[]{:S(2)}) collective-permute-start(bf16[4,128,128]{2,1,0:T(8,128)(2,1)S(1)} %get-tuple-element.62), channel_id=1, source_target_pairs={{0,4},{1,5},{2,6},{3,7},{4,0},{5,1},{6,2},{7,3},{8,12},{9,13},{10,... | collective-permute-start | bytes 393224 | tf_op jit(solution)/shard_map/ppermute | solution.py:460
  52.6 1.5 %collective-permute-start.14 = (bf16[4,128,128]{2,1,0:T(8,128)(2,1)S(1)}, bf16[4,128,128]{2,1,0:T(8,128)(2,1)S(1)}, u32[]{:S(2)}, u32[]{:S(2)}) collective-permute-start(bf16[4,128,128]{2,1,0:T(8,128)(2,1)S(1)} %get-tuple-element.63), channel_id=1, source_target_pairs={{0,6},{1,7},{2,4},{3,5},{4,2},{5,3},{6,0},{7,1},{8,14},{9,15},{10,... | collective-permute-start | bytes 393224 | tf_op jit(solution)/shard_map/ppermute | solution.py:460
  54.2 2.0 %collective-permute-done.12.rest_1_ = bf16[4,128,128]{2,1,0:T(8,128)(2,1)S(1)} collective-permute-done((bf16[4,128,128]{2,1,0:T(8,128)(2,1)S(1)}, bf16[4,128,128]{2,1,0:T(8,128)(2,1)S(1)}, u32[]{:S(2)}, u32[]{:S(2)}) %collective-permute-start.12) | collective-permute-done | bytes 131104 | tf_op jit(solution)/shard_map/ppermute | solution.py:460
  56.2 1.4 %collective-permute-done.13.rest_2_ = bf16[4,128,128]{2,1,0:T(8,128)(2,1)S(1)} collective-permute-done((bf16[4,128,128]{2,1,0:T(8,128)(2,1)S(1)}, bf16[4,128,128]{2,1,0:T(8,128)(2,1)S(1)}, u32[]{:S(2)}, u32[]{:S(2)}) %collective-permute-start.13) | collective-permute-done | bytes 131104 | tf_op jit(solution)/shard_map/ppermute | solution.py:460
  57.6 2.5 %collective-permute-done.14.rest_3_ = bf16[4,128,128]{2,1,0:T(8,128)(2,1)S(1)} collective-permute-done((bf16[4,128,128]{2,1,0:T(8,128)(2,1)S(1)}, bf16[4,128,128]{2,1,0:T(8,128)(2,1)S(1)}, u32[]{:S(2)}, u32[]{:S(2)}) %collective-permute-start.14) | collective-permute-done | bytes 131104 | tf_op jit(solution)/shard_map/ppermute | solution.py:460
  60.1 0.7 future_total.1
  60.8 0.1 collective-permute-start.15
  60.9 0.5 collective-permute-start.20
  61.4 1.3 %collective-permute-start.18 = (bf16[4,128,128]{2,1,0:T(8,128)(2,1)S(1)}, bf16[4,128,128]{2,1,0:T(8,128)(2,1)S(1)}, u32[]{:S(2)}, u32[]{:S(2)}) collective-permute-start(bf16[4,128,128]{2,1,0:T(8,128)(2,1)S(1)} %get-tuple-element.71.rest_4_), channel_id=1, source_target_pairs={{8,0},{16,8},{24,16},{9,1},{17,9},{25,17},{10,2},{18,10},{26,18},{... | collective-permute-start | bytes 393224 | tf_op jit(solution)/shard_map/ppermute | solution.py:481
  62.7 0.0 collective-permute-done.16.other_ga
  62.7 1.3 %collective-permute-start.19 = (bf16[4,128,128]{2,1,0:T(8,128)(2,1)S(1)}, bf16[4,128,128]{2,1,0:T(8,128)(2,1)S(1)}, u32[]{:S(2)}, u32[]{:S(2)}) collective-permute-start(bf16[4,128,128]{2,1,0:T(8,128)(2,1)S(1)} %get-tuple-element.71.rest_4_), channel_id=1, source_target_pairs={{16,0},{24,8},{17,1},{25,9},{18,2},{26,10},{19,3},{27,11},{20,4},{... | collective-permute-start | bytes 393224 | tf_op jit(solution)/shard_map/ppermute | solution.py:481
  64.0 0.0 collective-permute-done.17.rest_1_
  64.0 6.9 %grads_within.1 = (bf16[128,4096]{1,0:T(8,128)(2,1)}, f32[128,4096]{1,0:T(8,128)S(1)}, f32[128,4096]{1,0:T(8,128)S(1)}) custom-call(s32[8]{0:T(128)S(1)} %copy-done.4, s32[3]{0:T(128)S(1)} %pad_add_fusion.place, bf16[128,4096]{1,0:T(8,128)(2,1)S(1)} %copy-done.2, bf16[128,4096]{1,0:T(8,128)(2,1)S(1)} %copy-done, bf16[128,4096]{1,0:T(8,128)(2,1)S(1)} %copy-done.1, ...), custom_call_target="tpu_custom_call" | custom-call | flops 1073741824 | bytes 11534336 | tf_op jit(solution)/shard_map/grads_within/pallas_call | solution.py:426
  71.0 3.7 %collective-permute-done.19.rest_6_ = bf16[4,128,128]{2,1,0:T(8,128)(2,1)S(1)} collective-permute-done((bf16[4,128,128]{2,1,0:T(8,128)(2,1)S(1)}, bf16[4,128,128]{2,1,0:T(8,128)(2,1)S(1)}, u32[]{:S(2)}, u32[]{:S(2)}) %collective-permute-start.19) | collective-permute-done | bytes 131104 | tf_op jit(solution)/shard_map/ppermute | solution.py:481
  74.6 0.9 future_prefix.1
  75.5 0.6 collective-permute-start.22
  76.1 1.5 %collective-permute-start.24 = (bf16[4,128,128]{2,1,0:T(8,128)(2,1)S(1)}, bf16[4,128,128]{2,1,0:T(8,128)(2,1)S(1)}, u32[]{:S(2)}, u32[]{:S(2)}) collective-permute-start(bf16[4,128,128]{2,1,0:T(8,128)(2,1)S(1)} %get-tuple-element.78), channel_id=1, source_target_pairs={{0,4},{1,5},{2,6},{3,7},{4,0},{5,1},{6,2},{7,3},{8,12},{9,13},{10,... | collective-permute-start | bytes 393224 | tf_op jit(solution)/shard_map/ppermute | solution.py:460
  77.5 1.5 %collective-permute-start.26 = (bf16[4,128,128]{2,1,0:T(8,128)(2,1)S(1)}, bf16[4,128,128]{2,1,0:T(8,128)(2,1)S(1)}, u32[]{:S(2)}, u32[]{:S(2)}) collective-permute-start(bf16[4,128,128]{2,1,0:T(8,128)(2,1)S(1)} %get-tuple-element.79), channel_id=1, source_target_pairs={{0,6},{1,7},{2,4},{3,5},{4,2},{5,3},{6,0},{7,1},{8,14},{9,15},{10,... | collective-permute-start | bytes 393224 | tf_op jit(solution)/shard_map/ppermute | solution.py:460
  79.0 0.0 collective-permute-done.15.array
  79.1 2.6 %collective-permute-done.22.rest_1_ = bf16[4,128,128]{2,1,0:T(8,128)(2,1)S(1)} collective-permute-done((bf16[4,128,128]{2,1,0:T(8,128)(2,1)S(1)}, bf16[4,128,128]{2,1,0:T(8,128)(2,1)S(1)}, u32[]{:S(2)}, u32[]{:S(2)}) %collective-permute-start.22) | collective-permute-done | bytes 131104 | tf_op jit(solution)/shard_map/ppermute | solution.py:460
  81.6 0.0 collective-permute-start.23
  81.6 0.3 collective-permute-done.24.rest_2_
  81.9 0.2 collective-permute-start.25
  82.1 2.1 %collective-permute-done.26.rest_3_ = bf16[4,128,128]{2,1,0:T(8,128)(2,1)S(1)} collective-permute-done((bf16[4,128,128]{2,1,0:T(8,128)(2,1)S(1)}, bf16[4,128,128]{2,1,0:T(8,128)(2,1)S(1)}, u32[]{:S(2)}, u32[]{:S(2)}) %collective-permute-start.26) | collective-permute-done | bytes 131104 | tf_op jit(solution)/shard_map/ppermute | solution.py:460
  84.3 1.4 %attn_out.1.rest_4_ = bf16[128,4096]{1,0:T(8,128)(2,1)} custom-call(s32[8]{0:T(128)S(1)} %copy-done.4, s32[3]{0:T(128)S(1)} %pad_add_fusion.place, bf16[128,2048]{1,0:T(8,128)(2,1)S(1)} %collective-permute-done.15.array, bf16[128,4096]{1,0:T(8,128)(2,1)} %get-tuple-element.67.held, ...), custom_call_target="tpu_custom_call", output_to_operand_aliasing={{}: (3, {})} | custom-call | bytes 1048576 | tf_op jit(solution)/shard_map/attn_out/pallas_call | solution.py:426
  85.7 2.8 %grads_last_0.1 = (bf16[128,4096]{1,0:T(8,128)(2,1)}, bf16[128,4096]{1,0:T(8,128)(2,1)}) custom-call(s32[8]{0:T(128)S(1)} %copy-done.4, s32[3]{0:T(128)S(1)} %pad_add_fusion.place, bf16[128,4096]{1,0:T(8,128)(2,1)S(1)} %copy-done, bf16[128,4096]{1,0:T(8,128)(2,1)S(1)} %copy-done.1, f32[128,4096]{1,0:T(8,128)S(1)} %get-tuple-element.72.rest_4_.gk_part, ...), custom_call_target="tpu_custom_call" | custom-call | flops 134217728 | bytes 4718592 | tf_op jit(solution)/shard_map/grads_last_0/pallas_call | solution.py:426
  88.4 0.0 collective-permute-done.25.rest_2_
  88.5 0.0 collective-permute-done.27.rest_3_
  88.5 2.8 %grads_last_1.1 = (bf16[128,4096]{1,0:T(8,128)(2,1)}, bf16[128,4096]{1,0:T(8,128)(2,1)}) custom-call(s32[8]{0:T(128)S(1)} %copy-done.4, s32[3]{0:T(128)S(1)} %pad_add_fusion.place, bf16[128,4096]{1,0:T(8,128)(2,1)S(1)} %copy-done, bf16[128,4096]{1,0:T(8,128)(2,1)S(1)} %copy-done.1, ...), custom_call_target="tpu_custom_call", output_to_operand_aliasing={{0}: (11, {}), {1}: (12, {})} | custom-call | flops 134217728 | bytes 4718592 | tf_op jit(solution)/shard_map/grads_last_1/pallas_call | solution.py:426
  (16 shorter events, 0.0 us)
Async XLA Ops:
  0.7 0.7 copy-start.4
  4.4 3.1 %collective-permute-start = (bf16[16,128,128]{2,1,0:T(8,128)(2,1)S(1)}, bf16[16,128,128]{2,1,0:T(8,128)(2,1)S(1)}, u32[]{:S(2)}, u32[]{:S(2)}) collective-permute-start(bf16[16,128,128]{2,1,0:T(8,128)(2,1)S(1)} %get-tuple-element.44), channel_id=1, source_target_pairs={{0,1},{1,0},{2,3},{3,2},{4,5},{5,4},{6,7},{7,6},{8,9},{9,8},{10,11... | collective-permute-start | bytes 1572872 | tf_op jit(solution)/shard_map/ppermute | solution.py:455
  7.5 23.2 %copy-start = (bf16[128,4096]{1,0:T(8,128)(2,1)S(1)}, bf16[128,4096]{1,0:T(8,128)(2,1)}, u32[]{:S(2)}) copy-start(bf16[128,4096]{1,0:T(8,128)(2,1)} %k.11) | copy-start | bytes 3145732
  7.5 23.2 %copy-start.1 = (bf16[128,4096]{1,0:T(8,128)(2,1)S(1)}, bf16[128,4096]{1,0:T(8,128)(2,1)}, u32[]{:S(2)}) copy-start(bf16[128,4096]{1,0:T(8,128)(2,1)} %v.11) | copy-start | bytes 3145732
  7.5 23.2 %copy-start.2 = (bf16[128,4096]{1,0:T(8,128)(2,1)S(1)}, bf16[128,4096]{1,0:T(8,128)(2,1)}, u32[]{:S(2)}) copy-start(bf16[128,4096]{1,0:T(8,128)(2,1)} %q.3) | copy-start | bytes 3145732
  8.4 22.2 %collective-permute-start.1 = (bf16[3,128,2048]{2,1,0:T(8,128)(2,1)S(1)}, bf16[3,128,2048]{2,1,0:T(8,128)(2,1)S(1)}, u32[]{:S(2)}, u32[]{:S(2)}) collective-permute-start(bf16[3,128,2048]{2,1,0:T(8,128)(2,1)S(1)} %get-tuple-element.47), channel_id=1, source_target_pairs={{0,1},{1,0},{2,3},{3,2},{4,5},{5,4},{6,7},{7,6},{8,9},{9,8},{10,11... | collective-permute-start | bytes 4718600 | tf_op jit(solution)/shard_map/ppermute | solution.py:455
  8.6 26.4 %collective-permute-start.6 = (bf16[16,128,128]{2,1,0:T(8,128)(2,1)S(1)}, bf16[16,128,128]{2,1,0:T(8,128)(2,1)S(1)}, u32[]{:S(2)}, u32[]{:S(2)}) collective-permute-start(bf16[16,128,128]{2,1,0:T(8,128)(2,1)S(1)} %tail_own.1), channel_id=1, source_target_pairs={{0,1},{1,0},{2,3},{3,2},{4,5},{5,4},{6,7},{7,6},{8,9},{9,8},{10,11... | collective-permute-start | bytes 1572872 | tf_op jit(solution)/shard_map/ppermute | solution.py:455
  9.0 6.7 %collective-permute-start.3 = (bf16[4,128,128]{2,1,0:T(8,128)(2,1)S(1)}, bf16[4,128,128]{2,1,0:T(8,128)(2,1)S(1)}, u32[]{:S(2)}, u32[]{:S(2)}) collective-permute-start(bf16[4,128,128]{2,1,0:T(8,128)(2,1)S(1)} %get-tuple-element.53), channel_id=1, source_target_pairs={{0,2},{1,3},{2,0},{3,1},{4,6},{5,7},{6,4},{7,5},{8,10},{9,11},{10,... | collective-permute-start | bytes 393224 | tf_op jit(solution)/shard_map/ppermute | solution.py:460
  11.6 27.8 %collective-permute-start.2 = (bf16[128,2048]{1,0:T(8,128)(2,1)S(1)}, bf16[128,2048]{1,0:T(8,128)(2,1)S(1)}, u32[]{:S(2)}, u32[]{:S(2)}) collective-permute-start(bf16[128,2048]{1,0:T(8,128)(2,1)S(1)} %get-tuple-element.50), channel_id=1, source_target_pairs={{0,1},{1,0},{2,3},{3,2},{4,5},{5,4},{6,7},{7,6},{8,9},{9,8},{10,11... | collective-permute-start | bytes 1572872 | tf_op jit(solution)/shard_map/ppermute | solution.py:455
  11.8 6.6 %collective-permute-start.4 = (bf16[4,128,128]{2,1,0:T(8,128)(2,1)S(1)}, bf16[4,128,128]{2,1,0:T(8,128)(2,1)S(1)}, u32[]{:S(2)}, u32[]{:S(2)}) collective-permute-start(bf16[4,128,128]{2,1,0:T(8,128)(2,1)S(1)} %get-tuple-element.54), channel_id=1, source_target_pairs={{0,4},{1,5},{2,6},{3,7},{4,0},{5,1},{6,2},{7,3},{8,12},{9,13},{10,... | collective-permute-start | bytes 393224 | tf_op jit(solution)/shard_map/ppermute | solution.py:460
  15.7 6.2 %collective-permute-start.5 = (bf16[4,128,128]{2,1,0:T(8,128)(2,1)S(1)}, bf16[4,128,128]{2,1,0:T(8,128)(2,1)S(1)}, u32[]{:S(2)}, u32[]{:S(2)}) collective-permute-start(bf16[4,128,128]{2,1,0:T(8,128)(2,1)S(1)} %get-tuple-element.55), channel_id=1, source_target_pairs={{0,6},{1,7},{2,4},{3,5},{4,2},{5,3},{6,0},{7,1},{8,14},{9,15},{10,... | collective-permute-start | bytes 393224 | tf_op jit(solution)/shard_map/ppermute | solution.py:460
  22.6 12.4 %collective-permute-start.7 = (bf16[4,128,128]{2,1,0:T(8,128)(2,1)S(1)}, bf16[4,128,128]{2,1,0:T(8,128)(2,1)S(1)}, u32[]{:S(2)}, u32[]{:S(2)}) collective-permute-start(bf16[4,128,128]{2,1,0:T(8,128)(2,1)S(1)} %carried_total.1), channel_id=1, source_target_pairs={{0,8},{8,16},{16,24},{1,9},{9,17},{17,25},{2,10},{10,18},{18,26},{... | collective-permute-start | bytes 393224 | tf_op jit(solution)/shard_map/ppermute | solution.py:481
  26.1 8.9 %collective-permute-start.8 = (bf16[4,128,128]{2,1,0:T(8,128)(2,1)S(1)}, bf16[4,128,128]{2,1,0:T(8,128)(2,1)S(1)}, u32[]{:S(2)}, u32[]{:S(2)}) collective-permute-start(bf16[4,128,128]{2,1,0:T(8,128)(2,1)S(1)} %carried_total.1), channel_id=1, source_target_pairs={{0,16},{8,24},{1,17},{9,25},{2,18},{10,26},{3,19},{11,27},{4,20},{... | collective-permute-start | bytes 393224 | tf_op jit(solution)/shard_map/ppermute | solution.py:481
  35.0 9.9 %copy-start.3 = (bf16[128,4096]{1,0:T(8,128)(2,1)S(1)}, bf16[128,4096]{1,0:T(8,128)(2,1)}, u32[]{:S(2)}) copy-start(bf16[128,4096]{1,0:T(8,128)(2,1)} %g.1) | copy-start | bytes 3145732
  35.9 6.4 %collective-permute-start.9 = (bf16[4,128,128]{2,1,0:T(8,128)(2,1)S(1)}, bf16[4,128,128]{2,1,0:T(8,128)(2,1)S(1)}, u32[]{:S(2)}, u32[]{:S(2)}) collective-permute-start(bf16[4,128,128]{2,1,0:T(8,128)(2,1)S(1)} %get-tuple-element.57), channel_id=1, source_target_pairs={{0,2},{1,3},{2,0},{3,1},{4,6},{5,7},{6,4},{7,5},{8,10},{9,11},{10,... | collective-permute-start | bytes 393224 | tf_op jit(solution)/shard_map/ppermute | solution.py:460
  37.5 5.0 %collective-permute-start.10 = (bf16[4,128,128]{2,1,0:T(8,128)(2,1)S(1)}, bf16[4,128,128]{2,1,0:T(8,128)(2,1)S(1)}, u32[]{:S(2)}, u32[]{:S(2)}) collective-permute-start(bf16[4,128,128]{2,1,0:T(8,128)(2,1)S(1)} %get-tuple-element.58), channel_id=1, source_target_pairs={{0,4},{1,5},{2,6},{3,7},{4,0},{5,1},{6,2},{7,3},{8,12},{9,13},{10,... | collective-permute-start | bytes 393224 | tf_op jit(solution)/shard_map/ppermute | solution.py:460
  39.0 5.9 %collective-permute-start.11 = (bf16[4,128,128]{2,1,0:T(8,128)(2,1)S(1)}, bf16[4,128,128]{2,1,0:T(8,128)(2,1)S(1)}, u32[]{:S(2)}, u32[]{:S(2)}) collective-permute-start(bf16[4,128,128]{2,1,0:T(8,128)(2,1)S(1)} %get-tuple-element.59), channel_id=1, source_target_pairs={{0,6},{1,7},{2,4},{3,5},{4,2},{5,3},{6,0},{7,1},{8,14},{9,15},{10,... | collective-permute-start | bytes 393224 | tf_op jit(solution)/shard_map/ppermute | solution.py:460
  50.2 12.5 %collective-permute-start.16 = (bf16[128,2048]{1,0:T(8,128)(2,1)S(1)}, bf16[128,2048]{1,0:T(8,128)(2,1)S(1)}, u32[]{:S(2)}, u32[]{:S(2)}) collective-permute-start(bf16[128,2048]{1,0:T(8,128)(2,1)S(1)} %get-tuple-element.69), channel_id=1, source_target_pairs={{0,1},{1,0},{2,3},{3,2},{4,5},{5,4},{6,7},{7,6},{8,9},{9,8},{10,11... | collective-permute-start | bytes 1572872 | tf_op jit(solution)/shard_map/ppermute | solution.py:455
  50.2 13.8 %collective-permute-start.17 = (bf16[16,128,128]{2,1,0:T(8,128)(2,1)S(1)}, bf16[16,128,128]{2,1,0:T(8,128)(2,1)S(1)}, u32[]{:S(2)}, u32[]{:S(2)}) collective-permute-start(bf16[16,128,128]{2,1,0:T(8,128)(2,1)S(1)} %get-tuple-element.70.rest_0_), channel_id=1, source_target_pairs={{0,1},{1,0},{2,3},{3,2},{4,5},{5,4},{6,7},{7,6},{8,9},{9,8},{10,11... | collective-permute-start | bytes 1572872 | tf_op jit(solution)/shard_map/ppermute | solution.py:455
  50.7 5.5 %collective-permute-start.12 = (bf16[4,128,128]{2,1,0:T(8,128)(2,1)S(1)}, bf16[4,128,128]{2,1,0:T(8,128)(2,1)S(1)}, u32[]{:S(2)}, u32[]{:S(2)}) collective-permute-start(bf16[4,128,128]{2,1,0:T(8,128)(2,1)S(1)} %get-tuple-element.61), channel_id=1, source_target_pairs={{0,2},{1,3},{2,0},{3,1},{4,6},{5,7},{6,4},{7,5},{8,10},{9,11},{10,... | collective-permute-start | bytes 393224 | tf_op jit(solution)/shard_map/ppermute | solution.py:460
  51.2 6.4 %collective-permute-start.13 = (bf16[4,128,128]{2,1,0:T(8,128)(2,1)S(1)}, bf16[4,128,128]{2,1,0:T(8,128)(2,1)S(1)}, u32[]{:S(2)}, u32[]{:S(2)}) collective-permute-start(bf16[4,128,128]{2,1,0:T(8,128)(2,1)S(1)} %get-tuple-element.62), channel_id=1, source_target_pairs={{0,4},{1,5},{2,6},{3,7},{4,0},{5,1},{6,2},{7,3},{8,12},{9,13},{10,... | collective-permute-start | bytes 393224 | tf_op jit(solution)/shard_map/ppermute | solution.py:460
  52.6 7.4 %collective-permute-start.14 = (bf16[4,128,128]{2,1,0:T(8,128)(2,1)S(1)}, bf16[4,128,128]{2,1,0:T(8,128)(2,1)S(1)}, u32[]{:S(2)}, u32[]{:S(2)}) collective-permute-start(bf16[4,128,128]{2,1,0:T(8,128)(2,1)S(1)} %get-tuple-element.63), channel_id=1, source_target_pairs={{0,6},{1,7},{2,4},{3,5},{4,2},{5,3},{6,0},{7,1},{8,14},{9,15},{10,... | collective-permute-start | bytes 393224 | tf_op jit(solution)/shard_map/ppermute | solution.py:460
  60.8 18.2 %collective-permute-start.15 = (bf16[128,2048]{1,0:T(8,128)(2,1)S(1)}, bf16[128,2048]{1,0:T(8,128)(2,1)S(1)}, u32[]{:S(2)}, u32[]{:S(2)}) collective-permute-start(bf16[128,2048]{1,0:T(8,128)(2,1)S(1)} %get-tuple-element.66), channel_id=1, source_target_pairs={{0,1},{1,0},{2,3},{3,2},{4,5},{5,4},{6,7},{7,6},{8,9},{9,8},{10,11... | collective-permute-start | bytes 1572872 | tf_op jit(solution)/shard_map/ppermute | solution.py:455
  60.9 27.5 %collective-permute-start.20 = (bf16[16,128,128]{2,1,0:T(8,128)(2,1)S(1)}, bf16[16,128,128]{2,1,0:T(8,128)(2,1)S(1)}, u32[]{:S(2)}, u32[]{:S(2)}) collective-permute-start(bf16[16,128,128]{2,1,0:T(8,128)(2,1)S(1)} %get-tuple-element.76.late), channel_id=1, source_target_pairs={{0,1},{1,0},{2,3},{3,2},{4,5},{5,4},{6,7},{7,6},{8,9},{9,8},{10,11... | collective-permute-start | bytes 1572872 | tf_op jit(solution)/shard_map/ppermute | solution.py:455
  61.4 9.5 %collective-permute-start.18 = (bf16[4,128,128]{2,1,0:T(8,128)(2,1)S(1)}, bf16[4,128,128]{2,1,0:T(8,128)(2,1)S(1)}, u32[]{:S(2)}, u32[]{:S(2)}) collective-permute-start(bf16[4,128,128]{2,1,0:T(8,128)(2,1)S(1)} %get-tuple-element.71.rest_4_), channel_id=1, source_target_pairs={{8,0},{16,8},{24,16},{9,1},{17,9},{25,17},{10,2},{18,10},{26,18},{... | collective-permute-start | bytes 393224 | tf_op jit(solution)/shard_map/ppermute | solution.py:481
  62.7 11.9 %collective-permute-start.19 = (bf16[4,128,128]{2,1,0:T(8,128)(2,1)S(1)}, bf16[4,128,128]{2,1,0:T(8,128)(2,1)S(1)}, u32[]{:S(2)}, u32[]{:S(2)}) collective-permute-start(bf16[4,128,128]{2,1,0:T(8,128)(2,1)S(1)} %get-tuple-element.71.rest_4_), channel_id=1, source_target_pairs={{16,0},{24,8},{17,1},{25,9},{18,2},{26,10},{19,3},{27,11},{20,4},{... | collective-permute-start | bytes 393224 | tf_op jit(solution)/shard_map/ppermute | solution.py:481
  75.5 6.1 %collective-permute-start.22 = (bf16[4,128,128]{2,1,0:T(8,128)(2,1)S(1)}, bf16[4,128,128]{2,1,0:T(8,128)(2,1)S(1)}, u32[]{:S(2)}, u32[]{:S(2)}) collective-permute-start(bf16[4,128,128]{2,1,0:T(8,128)(2,1)S(1)} %get-tuple-element.77), channel_id=1, source_target_pairs={{0,2},{1,3},{2,0},{3,1},{4,6},{5,7},{6,4},{7,5},{8,10},{9,11},{10,... | collective-permute-start | bytes 393224 | tf_op jit(solution)/shard_map/ppermute | solution.py:460
  76.1 5.8 %collective-permute-start.24 = (bf16[4,128,128]{2,1,0:T(8,128)(2,1)S(1)}, bf16[4,128,128]{2,1,0:T(8,128)(2,1)S(1)}, u32[]{:S(2)}, u32[]{:S(2)}) collective-permute-start(bf16[4,128,128]{2,1,0:T(8,128)(2,1)S(1)} %get-tuple-element.78), channel_id=1, source_target_pairs={{0,4},{1,5},{2,6},{3,7},{4,0},{5,1},{6,2},{7,3},{8,12},{9,13},{10,... | collective-permute-start | bytes 393224 | tf_op jit(solution)/shard_map/ppermute | solution.py:460
  77.5 6.7 %collective-permute-start.26 = (bf16[4,128,128]{2,1,0:T(8,128)(2,1)S(1)}, bf16[4,128,128]{2,1,0:T(8,128)(2,1)S(1)}, u32[]{:S(2)}, u32[]{:S(2)}) collective-permute-start(bf16[4,128,128]{2,1,0:T(8,128)(2,1)S(1)} %get-tuple-element.79), channel_id=1, source_target_pairs={{0,6},{1,7},{2,4},{3,5},{4,2},{5,3},{6,0},{7,1},{8,14},{9,15},{10,... | collective-permute-start | bytes 393224 | tf_op jit(solution)/shard_map/ppermute | solution.py:460
  79.0 9.4 %collective-permute-start.21 = (bf16[4,128,128]{2,1,0:T(8,128)(2,1)S(1)}, bf16[4,128,128]{2,1,0:T(8,128)(2,1)S(1)}, u32[]{:S(2)}, u32[]{:S(2)}) collective-permute-start(bf16[4,128,128]{2,1,0:T(8,128)(2,1)S(1)} %get-tuple-element.73.after.rest_0_), channel_id=1, source_target_pairs={{0,1},{1,0},{2,3},{3,2},{4,5},{5,4},{6,7},{7,6},{8,9},{9,8},{10,11... | collective-permute-start | bytes 393224 | tf_op jit(solution)/shard_map/ppermute | solution.py:455
  81.6 6.8 %collective-permute-start.23 = (bf16[4,128,128]{2,1,0:T(8,128)(2,1)S(1)}, bf16[4,128,128]{2,1,0:T(8,128)(2,1)S(1)}, u32[]{:S(2)}, u32[]{:S(2)}) collective-permute-start(bf16[4,128,128]{2,1,0:T(8,128)(2,1)S(1)} %collective-permute-done.22.rest_1_), channel_id=1, source_target_pairs={{0,1},{1,0},{2,3},{3,2},{4,5},{5,4},{6,7},{7,6},{8,9},{9,8},{10,11... | collective-permute-start | bytes 393224 | tf_op jit(solution)/shard_map/ppermute | solution.py:455
  81.9 6.6 %collective-permute-start.25 = (bf16[4,128,128]{2,1,0:T(8,128)(2,1)S(1)}, bf16[4,128,128]{2,1,0:T(8,128)(2,1)S(1)}, u32[]{:S(2)}, u32[]{:S(2)}) collective-permute-start(bf16[4,128,128]{2,1,0:T(8,128)(2,1)S(1)} %collective-permute-done.24.rest_2_), channel_id=1, source_target_pairs={{0,1},{1,0},{2,3},{3,2},{4,5},{5,4},{6,7},{7,6},{8,9},{9,8},{10,11... | collective-permute-start | bytes 393224 | tf_op jit(solution)/shard_map/ppermute | solution.py:455
  84.3 4.2 %collective-permute-start.27 = (bf16[4,128,128]{2,1,0:T(8,128)(2,1)S(1)}, bf16[4,128,128]{2,1,0:T(8,128)(2,1)S(1)}, u32[]{:S(2)}, u32[]{:S(2)}) collective-permute-start(bf16[4,128,128]{2,1,0:T(8,128)(2,1)S(1)} %collective-permute-done.26.rest_3_), channel_id=1, source_target_pairs={{0,1},{1,0},{2,3},{3,2},{4,5},{5,4},{6,7},{7,6},{8,9},{9,8},{10,11... | collective-permute-start | bytes 393224 | tf_op jit(solution)/shard_map/ppermute | solution.py:455

commit v10 on v9

--- a/solution.py
+++ b/solution.py
@@ -133,10 +133,6 @@
     )
 
 
-def fill_kernel(lens, place, array, held, after, out):
-    out[...] = array[...]
-
-
 def chip_kernel(lens, place, q, k, v, mate, part, head_fq, turned):
     count = q.shape[0]
     seen, head, _, _ = pair_docs(lens, place, count)
@@ -269,8 +265,11 @@
 
 
 def last_kernel(chips, lens, place, k, v, gk_part, gv_part, late, *rest):
-    gk, gv, came = rest[-3:]
-    outgoing = rest[:chips]
+    came = rest[-1]
+    outgoing, gk, gv = rest[:chips], rest[-3], rest[-2]
+    if len(rest) > chips + 3:
+        rest[-4][...] = rest[chips][...]
+        gk, gv = rest[-3], rest[-2]
     count = k.shape[0]
     heads = k.shape[1] // DH
     step = pl.program_id(0)
@@ -313,8 +312,7 @@
     return core, [doc_at(ends, mark) for mark in marks]
 
 
-def merge_kernel(count, chips, lens, place, mine, other, *rest):
-    outs = rest[-chips - 2 : -2]
+def merge_kernel(count, lens, place, mine, other, *outs):
     core, (early_b, early_e, late_b, late_e) = chip_docs(lens, place, count)
     far = same(early_e, late_e)
     mine_by = jnp.where(core == 0, far, 1.0)
@@ -444,7 +442,7 @@
     product = 2 * half * count * DH * DH
     array = half * count * DH * 2
     all_states = pltpu.VMEM((heads, DH, DH), BF16)
-    block = 2 if owned % 2 == 0 else 1
+    block = owned
     single = pl.BlockSpec((block, DH, DH), lambda i, *a: (i, 0, 0))
     grouped = pl.BlockSpec((chips, block, DH, DH), lambda i, *a: (0, i, 0, 0))
     buffer = pltpu.VMEM((chips, block, DH, DH), BF16)
@@ -527,20 +525,20 @@
     )
     mine = own_tail.reshape(chips, owned, DH, DH)
     other = swap(mate_tail).reshape(chips, owned, DH, DH)
-    *merged, mate_three, mate_g = run(
-        functools.partial(merge_kernel, count, chips),
+    merged = run(
+        functools.partial(merge_kernel, count),
         moves,
-        [grouped] * 2 + [untouched] * 2,
-        [single] * chips + [untouched] * 2,
-        [owned_bf] * chips + copies,
+        [grouped] * 2,
+        [single] * chips,
+        [owned_bf] * chips,
         [],
-        (mine, other, mate_three, mate_g),
+        (mine, other),
         combining,
         "carried_chip",
-        aliases={4: chips, 5: chips + 1},
-    )
-    came, others, _, _ = reach_out(merged, (), True, "carried")
-
+    )
+    came, others, _, (mate_three, mate_g, own_tail) = reach_out(
+        merged, (mate_three, mate_g, own_tail), True, "carried"
+    )
     mate_three, mate_g = swap(mate_three), swap(mate_g)
     few = 4 if half % 4 == 0 else 1
     parts = half // few
@@ -618,40 +616,31 @@
     )
     late = (mine_late, swap(mine_late))
     chip_out = spread(came, others, (gk_part,), False, "future")
-    (attn_out,) = run(
-        fill_kernel,
-        steps,
-        [lane, untouched, untouched],
+    outgoing = (chip_out, [swap(state) for state in chip_out])
+    def last(parity, extra_ins, extra_outs, shapes, args, aliases):
+        return run(
+            functools.partial(last_kernel, chips),
+            steps,
+            [tokens(parity)] * 4 + [whole] + [one_owner] * chips + extra_ins,
+            extra_outs + [tokens(parity)] * 2,
+            shapes,
+            [half_states],
+            (keys, values, gk_part, gv_part, late[parity], *outgoing[parity], *args),
+            (2 * product, 9 * array, half * count * DH),
+            f"grads_last_{parity}",
+            aliases=aliases,
+        )
+
+    grad_keys, grad_values = last(0, [], [], [token_bf] * 2, (), {})
+    attn_out, grad_keys, grad_values = last(
+        1,
+        [lane] + [untouched] * 3,
         [tokens(1)],
-        [token_bf],
-        [],
-        (swap(mate_out), held_in_hbm(attn_half), chip_out[0]),
-        (0, 2 * array, 0),
-        "attn_out",
-        aliases={3: 0},
-    )
-    outgoing = (chip_out, [swap(state) for state in chip_out])
-    made = ()
-    for parity in (0, 1):
-        after = (held_in_hbm(attn_out),) if parity == 0 else made
-        made = tuple(
-            run(
-                functools.partial(last_kernel, chips),
-                steps,
-                [tokens(parity)] * 4
-                + [whole]
-                + [one_owner] * chips
-                + [untouched] * len(after),
-                [tokens(parity)] * 2,
-                [token_bf] * 2,
-                [half_states],
-                (keys, values, gk_part, gv_part, late[parity], *outgoing[parity], *after),
-                (2 * product, 9 * array, half * count * DH),
-                f"grads_last_{parity}",
-                aliases={7 + chips + j: j for j in range(2)} if parity else {},
-            )
-        )
-    return attn_out, grad_queries, *made
+        [token_bf] * 3,
+        (swap(mate_out), held_in_hbm(attn_half), grad_keys, grad_values),
+        {8 + chips + j: j for j in range(3)},
+    )
+    return attn_out, grad_queries, grad_keys, grad_values
 
 
 def solution(mesh):

time: 91.5 us -> 89.4 us (0.977)
  starting transfers between devices: 30.5 us -> 27.7 us
  waiting for transfers between devices: 25.9 us -> 27.6 us
  Pallas kernels: 33.2 us -> 31.7 us
    ppermute x12, starting transfers between devices: 17.4 us -> 14.7 us  [exchange(): lax.ppermute(state, LAYER, pairs[n])]
    ppermute x12, waiting for transfers between devices: 22.2 us -> 24 us  [exchange(): lax.ppermute(state, LAYER, pairs[n])]
    pallas_call x13 -> x12, Pallas kernels: 33.2 us -> 31.7 us  [run(): pl.pallas_call(kernel, grid_spec=pltpu.PrefetchScalarGridSpec(num_scalar_...]
  transfers between devices with their start and end apart: 28 -> 28, of which waited for: 12 -> 13; matrix products, arithmetic and copies ran while one was open for 0% -> 0% of each run, Pallas kernels for 23% -> 21%
where the time goes in v10:
time: 89.4 us; the launch traced here: 88.6 us
  Pallas kernels  31.7 us (35%)
  starting transfers between devices  27.7 us (31%)
  waiting for transfers between devices  27.6 us (31%)
    pallas_call x12, Pallas kernels, run(): pl.pallas_call(kernel, grid_spec=pltpu.PrefetchScalarGridSpec(num_scalar_...  31.7 us
    ppermute x12, waiting for transfers between devices, exchange(): lax.ppermute(state, LAYER, pairs[n])  24 us
    ppermute x12, starting transfers between devices, exchange(): lax.ppermute(state, LAYER, pairs[n])  14.7 us
    ppermute x4, starting transfers between devices, reach_out(): others.append(lax.ppermute(total, 'z', pairs))  10.7 us
    ppermute x4, waiting for transfers between devices, reach_out(): others.append(lax.ppermute(total, 'z', pairs))  3.54 us
    ppermute x12, starting transfers between devices, swap(): return lax.ppermute(state, LAYER, [(i, i ^ 1) for i in range(members)])  2.25 us
  transfers between devices with their start and end apart: 28, of which 13 were waited for; matrix products, arithmetic and copies ran while one was open for 0% of the time, Pallas kernels for 21%

profile of v10, /device:TPU:0, one launch (start us, length us, event | category | flops | bytes accessed | tf_op | source)
XLA Modules:
  0.0 88.6 jit_solution(9436130992476821788)
XLA Ops:
  0.6 0.1 pad_add_fusion.place
  0.7 0.7 copy-done.4
  1.4 3.0 %tail_mate.1 = (bf16[16,128,128]{2,1,0:T(8,128)(2,1)S(1)}, bf16[3,128,2048]{2,1,0:T(8,128)(2,1)S(1)}, bf16[128,2048]{1,0:T(8,128)(2,1)S(1)}) custom-call(s32[8]{0:T(128)S(1)} %copy-done.4, s32[3]{0:T(128)S(1)} %pad_add_fusion.place, bf16[128,4096]{1,0:T(8,128)(2,1)} %k.11, bf16[128,4096]{1,0:T(8,128)(2,1)} %v.11, bf16[128,4096]{1,0:T(8,128)(2,1)} %q.3, ...), custom_call_target="tpu_custom_call" | custom-call | flops 67108864 | bytes 1572864 | tf_op jit(solution)/shard_map/tail_mate/pallas_call | solution.py:424
  4.4 0.5 collective-permute-start
  4.9 2.6 %tail_own.1.rest_6_ = bf16[16,128,128]{2,1,0:T(8,128)(2,1)S(1)} custom-call(s32[8]{0:T(128)S(1)} %copy-done.4, s32[3]{0:T(128)S(1)} %pad_add_fusion.place, bf16[128,4096]{1,0:T(8,128)(2,1)} %k.11, bf16[128,4096]{1,0:T(8,128)(2,1)} %v.11), custom_call_target="tpu_custom_call" | custom-call | flops 67108864 | bytes 1572864 | tf_op jit(solution)/shard_map/tail_own/pallas_call | solution.py:424
  7.5 0.0 copy-start
  7.5 0.0 copy-start.1
  7.5 0.0 copy-start.2
  7.5 0.8 carried_chip.1
  8.3 2.6 %collective-permute-start.1 = (bf16[4,128,128]{2,1,0:T(8,128)(2,1)S(1)}, bf16[4,128,128]{2,1,0:T(8,128)(2,1)S(1)}, u32[]{:S(2)}, u32[]{:S(2)}) collective-permute-start(bf16[4,128,128]{2,1,0:T(8,128)(2,1)S(1)} %get-tuple-element.49), channel_id=1, source_target_pairs={{0,2},{1,3},{2,0},{3,1},{4,6},{5,7},{6,4},{7,5},{8,10},{9,11},{10,... | collective-permute-start | bytes 393224 | tf_op jit(solution)/shard_map/ppermute | solution.py:458
  10.9 1.5 %collective-permute-start.2 = (bf16[4,128,128]{2,1,0:T(8,128)(2,1)S(1)}, bf16[4,128,128]{2,1,0:T(8,128)(2,1)S(1)}, u32[]{:S(2)}, u32[]{:S(2)}) collective-permute-start(bf16[4,128,128]{2,1,0:T(8,128)(2,1)S(1)} %get-tuple-element.50), channel_id=1, source_target_pairs={{0,4},{1,5},{2,6},{3,7},{4,0},{5,1},{6,2},{7,3},{8,12},{9,13},{10,... | collective-permute-start | bytes 393224 | tf_op jit(solution)/shard_map/ppermute | solution.py:458
  12.3 0.1 collective-permute-start.3
  12.4 2.6 %collective-permute-done.1.rest_1_ = bf16[4,128,128]{2,1,0:T(8,128)(2,1)S(1)} collective-permute-done((bf16[4,128,128]{2,1,0:T(8,128)(2,1)S(1)}, bf16[4,128,128]{2,1,0:T(8,128)(2,1)S(1)}, u32[]{:S(2)}, u32[]{:S(2)}) %collective-permute-start.1) | collective-permute-done | bytes 131104 | tf_op jit(solution)/shard_map/ppermute | solution.py:458
  15.0 2.2 %collective-permute-done.2.rest_2_ = bf16[4,128,128]{2,1,0:T(8,128)(2,1)S(1)} collective-permute-done((bf16[4,128,128]{2,1,0:T(8,128)(2,1)S(1)}, bf16[4,128,128]{2,1,0:T(8,128)(2,1)S(1)}, u32[]{:S(2)}, u32[]{:S(2)}) %collective-permute-start.2) | collective-permute-done | bytes 131104 | tf_op jit(solution)/shard_map/ppermute | solution.py:458
  17.2 1.9 %collective-permute-done.3.rest_3_ = bf16[4,128,128]{2,1,0:T(8,128)(2,1)S(1)} collective-permute-done((bf16[4,128,128]{2,1,0:T(8,128)(2,1)S(1)}, bf16[4,128,128]{2,1,0:T(8,128)(2,1)S(1)}, u32[]{:S(2)}, u32[]{:S(2)}) %collective-permute-start.3) | collective-permute-done | bytes 131104 | tf_op jit(solution)/shard_map/ppermute | solution.py:458
  19.1 0.7 carried_total.1
  19.8 0.1 collective-permute-start.4
  19.9 0.5 collective-permute-start.6
  20.4 0.1 collective-permute-start.5
  20.5 4.6 %collective-permute-start.8 = (bf16[4,128,128]{2,1,0:T(8,128)(2,1)S(1)}, bf16[4,128,128]{2,1,0:T(8,128)(2,1)S(1)}, u32[]{:S(2)}, u32[]{:S(2)}) collective-permute-start(bf16[4,128,128]{2,1,0:T(8,128)(2,1)S(1)} %get-tuple-element.60), channel_id=1, source_target_pairs={{0,16},{8,24},{1,17},{9,25},{2,18},{10,26},{3,19},{11,27},{4,20},{... | collective-permute-start | bytes 393224 | tf_op jit(solution)/shard_map/ppermute | solution.py:479
  25.1 3.5 %collective-permute-start.7 = (bf16[4,128,128]{2,1,0:T(8,128)(2,1)S(1)}, bf16[4,128,128]{2,1,0:T(8,128)(2,1)S(1)}, u32[]{:S(2)}, u32[]{:S(2)}) collective-permute-start(bf16[4,128,128]{2,1,0:T(8,128)(2,1)S(1)} %get-tuple-element.60), channel_id=1, source_target_pairs={{0,8},{8,16},{16,24},{1,9},{9,17},{17,25},{2,10},{10,18},{18,26},{... | collective-permute-start | bytes 393224 | tf_op jit(solution)/shard_map/ppermute | solution.py:479
  28.6 4.3 %within_chip.1 = (f32[256,2048]{1,0:T(8,128)S(1)}, bf16[256,2048]{1,0:T(8,128)(2,1)S(1)}, bf16[16,128,256]{2,1,0:T(8,128)(2,1)S(1)}) custom-call(s32[8]{0:T(128)S(1)} %copy-done.4, s32[3]{0:T(128)S(1)} %pad_add_fusion.place, bf16[128,4096]{1,0:T(8,128)(2,1)S(1)} %copy-done.2, bf16[128,4096]{1,0:T(8,128)(2,1)S(1)} %copy-done, ...), custom_call_target="tpu_custom_call" | custom-call | flops 671088640 | bytes 7340032 | tf_op jit(solution)/shard_map/within_chip/pallas_call | solution.py:424
  32.9 0.0 copy-start.3
  33.0 0.0 collective-permute-done.6.rest_5_.rest_3_
  33.0 0.9 carried_prefix.1
  33.8 1.6 %collective-permute-start.9 = (bf16[4,128,128]{2,1,0:T(8,128)(2,1)S(1)}, bf16[4,128,128]{2,1,0:T(8,128)(2,1)S(1)}, u32[]{:S(2)}, u32[]{:S(2)}) collective-permute-start(bf16[4,128,128]{2,1,0:T(8,128)(2,1)S(1)} %get-tuple-element.62), channel_id=1, source_target_pairs={{0,2},{1,3},{2,0},{3,1},{4,6},{5,7},{6,4},{7,5},{8,10},{9,11},{10,... | collective-permute-start | bytes 393224 | tf_op jit(solution)/shard_map/ppermute | solution.py:458
  35.4 1.5 %collective-permute-start.10 = (bf16[4,128,128]{2,1,0:T(8,128)(2,1)S(1)}, bf16[4,128,128]{2,1,0:T(8,128)(2,1)S(1)}, u32[]{:S(2)}, u32[]{:S(2)}) collective-permute-start(bf16[4,128,128]{2,1,0:T(8,128)(2,1)S(1)} %get-tuple-element.63), channel_id=1, source_target_pairs={{0,4},{1,5},{2,6},{3,7},{4,0},{5,1},{6,2},{7,3},{8,12},{9,13},{10,... | collective-permute-start | bytes 393224 | tf_op jit(solution)/shard_map/ppermute | solution.py:458
  36.9 0.5 collective-permute-start.11
  37.4 0.0 collective-permute-done.5.mate_g
  37.4 1.8 %collective-permute-done.9.rest_1_ = bf16[4,128,128]{2,1,0:T(8,128)(2,1)S(1)} collective-permute-done((bf16[4,128,128]{2,1,0:T(8,128)(2,1)S(1)}, bf16[4,128,128]{2,1,0:T(8,128)(2,1)S(1)}, u32[]{:S(2)}, u32[]{:S(2)}) %collective-permute-start.9) | collective-permute-done | bytes 131104 | tf_op jit(solution)/shard_map/ppermute | solution.py:458
  39.2 2.6 %collective-permute-done.10.rest_2_ = bf16[4,128,128]{2,1,0:T(8,128)(2,1)S(1)} collective-permute-done((bf16[4,128,128]{2,1,0:T(8,128)(2,1)S(1)}, bf16[4,128,128]{2,1,0:T(8,128)(2,1)S(1)}, u32[]{:S(2)}, u32[]{:S(2)}) %collective-permute-start.10) | collective-permute-done | bytes 131104 | tf_op jit(solution)/shard_map/ppermute | solution.py:458
  41.8 1.3 %collective-permute-done.11.rest_3_ = bf16[4,128,128]{2,1,0:T(8,128)(2,1)S(1)} collective-permute-done((bf16[4,128,128]{2,1,0:T(8,128)(2,1)S(1)}, bf16[4,128,128]{2,1,0:T(8,128)(2,1)S(1)}, u32[]{:S(2)}, u32[]{:S(2)}) %collective-permute-start.11) | collective-permute-done | bytes 131104 | tf_op jit(solution)/shard_map/ppermute | solution.py:458
  43.2 5.3 %normed.1 = (bf16[128,4096]{1,0:T(8,128)(2,1)}, bf16[128,2048]{1,0:T(8,128)(2,1)S(1)}, bf16[128,2048]{1,0:T(8,128)(2,1)S(1)}, bf16[128,2048]{1,0:T(8,128)(2,1)S(...) custom-call(s32[8]{0:T(128)S(1)} %copy-done.4, ...), custom_call_target="tpu_custom_call" | custom-call | flops 536870912 | bytes 8388608 | tf_op jit(solution)/shard_map/normed/pallas_call | solution.py:424
  48.5 0.5 collective-permute-start.13
  49.0 1.5 %collective-permute-start.14 = (bf16[4,128,128]{2,1,0:T(8,128)(2,1)S(1)}, bf16[4,128,128]{2,1,0:T(8,128)(2,1)S(1)}, u32[]{:S(2)}, u32[]{:S(2)}) collective-permute-start(bf16[4,128,128]{2,1,0:T(8,128)(2,1)S(1)} %get-tuple-element.69), channel_id=1, source_target_pairs={{0,2},{1,3},{2,0},{3,1},{4,6},{5,7},{6,4},{7,5},{8,10},{9,11},{10,... | collective-permute-start | bytes 393224 | tf_op jit(solution)/shard_map/ppermute | solution.py:458
  50.5 1.5 %collective-permute-start.15 = (bf16[4,128,128]{2,1,0:T(8,128)(2,1)S(1)}, bf16[4,128,128]{2,1,0:T(8,128)(2,1)S(1)}, u32[]{:S(2)}, u32[]{:S(2)}) collective-permute-start(bf16[4,128,128]{2,1,0:T(8,128)(2,1)S(1)} %get-tuple-element.70), channel_id=1, source_target_pairs={{0,4},{1,5},{2,6},{3,7},{4,0},{5,1},{6,2},{7,3},{8,12},{9,13},{10,... | collective-permute-start | bytes 393224 | tf_op jit(solution)/shard_map/ppermute | solution.py:458
  52.0 0.5 collective-permute-start.16
  52.5 1.9 %collective-permute-done.14.rest_1_ = bf16[4,128,128]{2,1,0:T(8,128)(2,1)S(1)} collective-permute-done((bf16[4,128,128]{2,1,0:T(8,128)(2,1)S(1)}, bf16[4,128,128]{2,1,0:T(8,128)(2,1)S(1)}, u32[]{:S(2)}, u32[]{:S(2)}) %collective-permute-start.14) | collective-permute-done | bytes 131104 | tf_op jit(solution)/shard_map/ppermute | solution.py:458
  54.4 2.5 %collective-permute-done.15.rest_2_ = bf16[4,128,128]{2,1,0:T(8,128)(2,1)S(1)} collective-permute-done((bf16[4,128,128]{2,1,0:T(8,128)(2,1)S(1)}, bf16[4,128,128]{2,1,0:T(8,128)(2,1)S(1)}, u32[]{:S(2)}, u32[]{:S(2)}) %collective-permute-start.15) | collective-permute-done | bytes 131104 | tf_op jit(solution)/shard_map/ppermute | solution.py:458
  56.9 1.5 %collective-permute-done.16.rest_3_ = bf16[4,128,128]{2,1,0:T(8,128)(2,1)S(1)} collective-permute-done((bf16[4,128,128]{2,1,0:T(8,128)(2,1)S(1)}, bf16[4,128,128]{2,1,0:T(8,128)(2,1)S(1)}, u32[]{:S(2)}, u32[]{:S(2)}) %collective-permute-start.16) | collective-permute-done | bytes 131104 | tf_op jit(solution)/shard_map/ppermute | solution.py:458
  58.4 0.7 future_total.1
  59.1 0.1 collective-permute-start.27
  59.2 0.5 collective-permute-start.17
  59.7 1.3 %collective-permute-start.19 = (bf16[4,128,128]{2,1,0:T(8,128)(2,1)S(1)}, bf16[4,128,128]{2,1,0:T(8,128)(2,1)S(1)}, u32[]{:S(2)}, u32[]{:S(2)}) collective-permute-start(bf16[4,128,128]{2,1,0:T(8,128)(2,1)S(1)} %get-tuple-element.74.rest_4_), channel_id=1, source_target_pairs={{16,0},{24,8},{17,1},{25,9},{18,2},{26,10},{19,3},{27,11},{20,4},{... | collective-permute-start | bytes 393224 | tf_op jit(solution)/shard_map/ppermute | solution.py:479
  61.0 1.3 %collective-permute-start.18 = (bf16[4,128,128]{2,1,0:T(8,128)(2,1)S(1)}, bf16[4,128,128]{2,1,0:T(8,128)(2,1)S(1)}, u32[]{:S(2)}, u32[]{:S(2)}) collective-permute-start(bf16[4,128,128]{2,1,0:T(8,128)(2,1)S(1)} %get-tuple-element.74.rest_4_), channel_id=1, source_target_pairs={{8,0},{16,8},{24,16},{9,1},{17,9},{25,17},{10,2},{18,10},{26,18},{... | collective-permute-start | bytes 393224 | tf_op jit(solution)/shard_map/ppermute | solution.py:479
  62.3 0.0 collective-permute-done.13.rest_1_
  62.3 6.9 %grads_within.1 = (bf16[128,4096]{1,0:T(8,128)(2,1)}, f32[128,4096]{1,0:T(8,128)S(1)}, f32[128,4096]{1,0:T(8,128)S(1)}) custom-call(s32[8]{0:T(128)S(1)} %copy-done.4, s32[3]{0:T(128)S(1)} %pad_add_fusion.place, bf16[128,4096]{1,0:T(8,128)(2,1)S(1)} %copy-done.2, bf16[128,4096]{1,0:T(8,128)(2,1)S(1)} %copy-done, bf16[128,4096]{1,0:T(8,128)(2,1)S(1)} %copy-done.1, ...), custom_call_target="tpu_custom_call" | custom-call | flops 1073741824 | bytes 11534336 | tf_op jit(solution)/shard_map/grads_within/pallas_call | solution.py:424
  69.3 3.5 %collective-permute-done.19.rest_6_ = bf16[4,128,128]{2,1,0:T(8,128)(2,1)S(1)} collective-permute-done((bf16[4,128,128]{2,1,0:T(8,128)(2,1)S(1)}, bf16[4,128,128]{2,1,0:T(8,128)(2,1)S(1)}, u32[]{:S(2)}, u32[]{:S(2)}) %collective-permute-start.19) | collective-permute-done | bytes 131104 | tf_op jit(solution)/shard_map/ppermute | solution.py:479
  72.8 0.0 collective-permute-done.18.rest_5_
  72.8 0.9 future_prefix.1
  73.7 1.6 %collective-permute-start.21 = (bf16[4,128,128]{2,1,0:T(8,128)(2,1)S(1)}, bf16[4,128,128]{2,1,0:T(8,128)(2,1)S(1)}, u32[]{:S(2)}, u32[]{:S(2)}) collective-permute-start(bf16[4,128,128]{2,1,0:T(8,128)(2,1)S(1)} %get-tuple-element.79), channel_id=1, source_target_pairs={{0,2},{1,3},{2,0},{3,1},{4,6},{5,7},{6,4},{7,5},{8,10},{9,11},{10,... | collective-permute-start | bytes 393224 | tf_op jit(solution)/shard_map/ppermute | solution.py:458
  75.2 1.5 %collective-permute-start.23 = (bf16[4,128,128]{2,1,0:T(8,128)(2,1)S(1)}, bf16[4,128,128]{2,1,0:T(8,128)(2,1)S(1)}, u32[]{:S(2)}, u32[]{:S(2)}) collective-permute-start(bf16[4,128,128]{2,1,0:T(8,128)(2,1)S(1)} %get-tuple-element.80), channel_id=1, source_target_pairs={{0,4},{1,5},{2,6},{3,7},{4,0},{5,1},{6,2},{7,3},{8,12},{9,13},{10,... | collective-permute-start | bytes 393224 | tf_op jit(solution)/shard_map/ppermute | solution.py:458
  76.8 0.5 collective-permute-start.25
  77.2 0.0 collective-permute-done.27.rest_4_
  77.2 0.0 collective-permute-start.20
  77.2 1.9 %collective-permute-done.21.rest_1_ = bf16[4,128,128]{2,1,0:T(8,128)(2,1)S(1)} collective-permute-done((bf16[4,128,128]{2,1,0:T(8,128)(2,1)S(1)}, bf16[4,128,128]{2,1,0:T(8,128)(2,1)S(1)}, u32[]{:S(2)}, u32[]{:S(2)}) %collective-permute-start.21) | collective-permute-done | bytes 131104 | tf_op jit(solution)/shard_map/ppermute | solution.py:458
  79.2 0.0 collective-permute-start.22
  79.2 1.6 %collective-permute-done.23.rest_2_ = bf16[4,128,128]{2,1,0:T(8,128)(2,1)S(1)} collective-permute-done((bf16[4,128,128]{2,1,0:T(8,128)(2,1)S(1)}, bf16[4,128,128]{2,1,0:T(8,128)(2,1)S(1)}, u32[]{:S(2)}, u32[]{:S(2)}) %collective-permute-start.23) | collective-permute-done | bytes 131104 | tf_op jit(solution)/shard_map/ppermute | solution.py:458
  80.8 0.0 collective-permute-start.24
  80.8 2.1 %collective-permute-done.25.rest_3_ = bf16[4,128,128]{2,1,0:T(8,128)(2,1)S(1)} collective-permute-done((bf16[4,128,128]{2,1,0:T(8,128)(2,1)S(1)}, bf16[4,128,128]{2,1,0:T(8,128)(2,1)S(1)}, u32[]{:S(2)}, u32[]{:S(2)}) %collective-permute-start.25) | collective-permute-done | bytes 131104 | tf_op jit(solution)/shard_map/ppermute | solution.py:458
  82.9 2.8 %grads_last_0.1 = (bf16[128,4096]{1,0:T(8,128)(2,1)}, bf16[128,4096]{1,0:T(8,128)(2,1)}) custom-call(s32[8]{0:T(128)S(1)} %copy-done.4, s32[3]{0:T(128)S(1)} %pad_add_fusion.place, bf16[128,4096]{1,0:T(8,128)(2,1)S(1)} %copy-done, bf16[128,4096]{1,0:T(8,128)(2,1)S(1)} %copy-done.1, f32[128,4096]{1,0:T(8,128)S(1)} %get-tuple-element.75.rest_4_.gk_part, ...), custom_call_target="tpu_custom_call" | custom-call | flops 134217728 | bytes 4718592 | tf_op jit(solution)/shard_map/grads_last_0/pallas_call | solution.py:424
  85.7 0.0 collective-permute-done.17.late
  85.7 0.0 collective-permute-done.20.rest_0_
  85.7 3.0 %grads_last_1.1 = (bf16[128,4096]{1,0:T(8,128)(2,1)}, bf16[128,4096]{1,0:T(8,128)(2,1)}, bf16[128,4096]{1,0:T(8,128)(2,1)}) custom-call(s32[8]{0:T(128)S(1)} %copy-done.4, s32[3]{0:T(128)S(1)} %pad_add_fusion.place, bf16[128,4096]{1,0:T(8,128)(2,1)S(1)} %copy-done, ...), custom_call_target="tpu_custom_call", output_to_operand_aliasing={{0}: (12, {}), {1}: (13, {}), {2}: (14, {})} | custom-call | flops 134217728 | bytes 4718592 | tf_op jit(solution)/shard_map/grads_last_1/pallas_call | solution.py:424
  (15 shorter events, 0.0 us)
Async XLA Ops:
  0.7 0.7 copy-start.4
  4.4 3.1 %collective-permute-start = (bf16[16,128,128]{2,1,0:T(8,128)(2,1)S(1)}, bf16[16,128,128]{2,1,0:T(8,128)(2,1)S(1)}, u32[]{:S(2)}, u32[]{:S(2)}) collective-permute-start(bf16[16,128,128]{2,1,0:T(8,128)(2,1)S(1)} %get-tuple-element.47), channel_id=1, source_target_pairs={{0,1},{1,0},{2,3},{3,2},{4,5},{5,4},{6,7},{7,6},{8,9},{9,8},{10,11... | collective-permute-start | bytes 1572872 | tf_op jit(solution)/shard_map/ppermute | solution.py:453
  7.5 21.1 %copy-start = (bf16[128,4096]{1,0:T(8,128)(2,1)S(1)}, bf16[128,4096]{1,0:T(8,128)(2,1)}, u32[]{:S(2)}) copy-start(bf16[128,4096]{1,0:T(8,128)(2,1)} %k.11) | copy-start | bytes 3145732
  7.5 21.1 %copy-start.1 = (bf16[128,4096]{1,0:T(8,128)(2,1)S(1)}, bf16[128,4096]{1,0:T(8,128)(2,1)}, u32[]{:S(2)}) copy-start(bf16[128,4096]{1,0:T(8,128)(2,1)} %v.11) | copy-start | bytes 3145732
  7.5 21.1 %copy-start.2 = (bf16[128,4096]{1,0:T(8,128)(2,1)S(1)}, bf16[128,4096]{1,0:T(8,128)(2,1)}, u32[]{:S(2)}) copy-start(bf16[128,4096]{1,0:T(8,128)(2,1)} %q.3) | copy-start | bytes 3145732
  8.3 6.8 %collective-permute-start.1 = (bf16[4,128,128]{2,1,0:T(8,128)(2,1)S(1)}, bf16[4,128,128]{2,1,0:T(8,128)(2,1)S(1)}, u32[]{:S(2)}, u32[]{:S(2)}) collective-permute-start(bf16[4,128,128]{2,1,0:T(8,128)(2,1)S(1)} %get-tuple-element.49), channel_id=1, source_target_pairs={{0,2},{1,3},{2,0},{3,1},{4,6},{5,7},{6,4},{7,5},{8,10},{9,11},{10,... | collective-permute-start | bytes 393224 | tf_op jit(solution)/shard_map/ppermute | solution.py:458
  10.9 6.3 %collective-permute-start.2 = (bf16[4,128,128]{2,1,0:T(8,128)(2,1)S(1)}, bf16[4,128,128]{2,1,0:T(8,128)(2,1)S(1)}, u32[]{:S(2)}, u32[]{:S(2)}) collective-permute-start(bf16[4,128,128]{2,1,0:T(8,128)(2,1)S(1)} %get-tuple-element.50), channel_id=1, source_target_pairs={{0,4},{1,5},{2,6},{3,7},{4,0},{5,1},{6,2},{7,3},{8,12},{9,13},{10,... | collective-permute-start | bytes 393224 | tf_op jit(solution)/shard_map/ppermute | solution.py:458
  12.3 6.7 %collective-permute-start.3 = (bf16[4,128,128]{2,1,0:T(8,128)(2,1)S(1)}, bf16[4,128,128]{2,1,0:T(8,128)(2,1)S(1)}, u32[]{:S(2)}, u32[]{:S(2)}) collective-permute-start(bf16[4,128,128]{2,1,0:T(8,128)(2,1)S(1)} %get-tuple-element.51), channel_id=1, source_target_pairs={{0,6},{1,7},{2,4},{3,5},{4,2},{5,3},{6,0},{7,1},{8,14},{9,15},{10,... | collective-permute-start | bytes 393224 | tf_op jit(solution)/shard_map/ppermute | solution.py:458
  19.8 8.8 %collective-permute-start.4 = (bf16[3,128,2048]{2,1,0:T(8,128)(2,1)S(1)}, bf16[3,128,2048]{2,1,0:T(8,128)(2,1)S(1)}, u32[]{:S(2)}, u32[]{:S(2)}) collective-permute-start(bf16[3,128,2048]{2,1,0:T(8,128)(2,1)S(1)} %get-tuple-element.54), channel_id=1, source_target_pairs={{0,1},{1,0},{2,3},{3,2},{4,5},{5,4},{6,7},{7,6},{8,9},{9,8},{10,11... | collective-permute-start | bytes 4718600 | tf_op jit(solution)/shard_map/ppermute | solution.py:453
  19.9 13.1 %collective-permute-start.6 = (bf16[16,128,128]{2,1,0:T(8,128)(2,1)S(1)}, bf16[16,128,128]{2,1,0:T(8,128)(2,1)S(1)}, u32[]{:S(2)}, u32[]{:S(2)}) collective-permute-start(bf16[16,128,128]{2,1,0:T(8,128)(2,1)S(1)} %get-tuple-element.59), channel_id=1, source_target_pairs={{0,1},{1,0},{2,3},{3,2},{4,5},{5,4},{6,7},{7,6},{8,9},{9,8},{10,11... | collective-permute-start | bytes 1572872 | tf_op jit(solution)/shard_map/ppermute | solution.py:453
  20.4 17.0 %collective-permute-start.5 = (bf16[128,2048]{1,0:T(8,128)(2,1)S(1)}, bf16[128,2048]{1,0:T(8,128)(2,1)S(1)}, u32[]{:S(2)}, u32[]{:S(2)}) collective-permute-start(bf16[128,2048]{1,0:T(8,128)(2,1)S(1)} %get-tuple-element.57), channel_id=1, source_target_pairs={{0,1},{1,0},{2,3},{3,2},{4,5},{5,4},{6,7},{7,6},{8,9},{9,8},{10,11... | collective-permute-start | bytes 1572872 | tf_op jit(solution)/shard_map/ppermute | solution.py:453
  20.5 12.5 %collective-permute-start.8 = (bf16[4,128,128]{2,1,0:T(8,128)(2,1)S(1)}, bf16[4,128,128]{2,1,0:T(8,128)(2,1)S(1)}, u32[]{:S(2)}, u32[]{:S(2)}) collective-permute-start(bf16[4,128,128]{2,1,0:T(8,128)(2,1)S(1)} %get-tuple-element.60), channel_id=1, source_target_pairs={{0,16},{8,24},{1,17},{9,25},{2,18},{10,26},{3,19},{11,27},{4,20},{... | collective-permute-start | bytes 393224 | tf_op jit(solution)/shard_map/ppermute | solution.py:479
  25.1 7.8 %collective-permute-start.7 = (bf16[4,128,128]{2,1,0:T(8,128)(2,1)S(1)}, bf16[4,128,128]{2,1,0:T(8,128)(2,1)S(1)}, u32[]{:S(2)}, u32[]{:S(2)}) collective-permute-start(bf16[4,128,128]{2,1,0:T(8,128)(2,1)S(1)} %get-tuple-element.60), channel_id=1, source_target_pairs={{0,8},{8,16},{16,24},{1,9},{9,17},{17,25},{2,10},{10,18},{18,26},{... | collective-permute-start | bytes 393224 | tf_op jit(solution)/shard_map/ppermute | solution.py:479
  32.9 10.3 %copy-start.3 = (bf16[128,4096]{1,0:T(8,128)(2,1)S(1)}, bf16[128,4096]{1,0:T(8,128)(2,1)}, u32[]{:S(2)}) copy-start(bf16[128,4096]{1,0:T(8,128)(2,1)} %g.1) | copy-start | bytes 3145732
  33.8 5.3 %collective-permute-start.9 = (bf16[4,128,128]{2,1,0:T(8,128)(2,1)S(1)}, bf16[4,128,128]{2,1,0:T(8,128)(2,1)S(1)}, u32[]{:S(2)}, u32[]{:S(2)}) collective-permute-start(bf16[4,128,128]{2,1,0:T(8,128)(2,1)S(1)} %get-tuple-element.62), channel_id=1, source_target_pairs={{0,2},{1,3},{2,0},{3,1},{4,6},{5,7},{6,4},{7,5},{8,10},{9,11},{10,... | collective-permute-start | bytes 393224 | tf_op jit(solution)/shard_map/ppermute | solution.py:458
  35.4 6.4 %collective-permute-start.10 = (bf16[4,128,128]{2,1,0:T(8,128)(2,1)S(1)}, bf16[4,128,128]{2,1,0:T(8,128)(2,1)S(1)}, u32[]{:S(2)}, u32[]{:S(2)}) collective-permute-start(bf16[4,128,128]{2,1,0:T(8,128)(2,1)S(1)} %get-tuple-element.63), channel_id=1, source_target_pairs={{0,4},{1,5},{2,6},{3,7},{4,0},{5,1},{6,2},{7,3},{8,12},{9,13},{10,... | collective-permute-start | bytes 393224 | tf_op jit(solution)/shard_map/ppermute | solution.py:458
  36.9 6.3 %collective-permute-start.11 = (bf16[4,128,128]{2,1,0:T(8,128)(2,1)S(1)}, bf16[4,128,128]{2,1,0:T(8,128)(2,1)S(1)}, u32[]{:S(2)}, u32[]{:S(2)}) collective-permute-start(bf16[4,128,128]{2,1,0:T(8,128)(2,1)S(1)} %get-tuple-element.64), channel_id=1, source_target_pairs={{0,6},{1,7},{2,4},{3,5},{4,2},{5,3},{6,0},{7,1},{8,14},{9,15},{10,... | collective-permute-start | bytes 393224 | tf_op jit(solution)/shard_map/ppermute | solution.py:458
  48.5 12.5 %collective-permute-start.12 = (bf16[128,2048]{1,0:T(8,128)(2,1)S(1)}, bf16[128,2048]{1,0:T(8,128)(2,1)S(1)}, u32[]{:S(2)}, u32[]{:S(2)}) collective-permute-start(bf16[128,2048]{1,0:T(8,128)(2,1)S(1)} %get-tuple-element.66), channel_id=1, source_target_pairs={{0,1},{1,0},{2,3},{3,2},{4,5},{5,4},{6,7},{7,6},{8,9},{9,8},{10,11... | collective-permute-start | bytes 1572872 | tf_op jit(solution)/shard_map/ppermute | solution.py:453
  48.5 13.8 %collective-permute-start.13 = (bf16[16,128,128]{2,1,0:T(8,128)(2,1)S(1)}, bf16[16,128,128]{2,1,0:T(8,128)(2,1)S(1)}, u32[]{:S(2)}, u32[]{:S(2)}) collective-permute-start(bf16[16,128,128]{2,1,0:T(8,128)(2,1)S(1)} %get-tuple-element.67.rest_0_), channel_id=1, source_target_pairs={{0,1},{1,0},{2,3},{3,2},{4,5},{5,4},{6,7},{7,6},{8,9},{9,8},{10,11... | collective-permute-start | bytes 1572872 | tf_op jit(solution)/shard_map/ppermute | solution.py:453
  49.0 5.4 %collective-permute-start.14 = (bf16[4,128,128]{2,1,0:T(8,128)(2,1)S(1)}, bf16[4,128,128]{2,1,0:T(8,128)(2,1)S(1)}, u32[]{:S(2)}, u32[]{:S(2)}) collective-permute-start(bf16[4,128,128]{2,1,0:T(8,128)(2,1)S(1)} %get-tuple-element.69), channel_id=1, source_target_pairs={{0,2},{1,3},{2,0},{3,1},{4,6},{5,7},{6,4},{7,5},{8,10},{9,11},{10,... | collective-permute-start | bytes 393224 | tf_op jit(solution)/shard_map/ppermute | solution.py:458
  50.5 6.4 %collective-permute-start.15 = (bf16[4,128,128]{2,1,0:T(8,128)(2,1)S(1)}, bf16[4,128,128]{2,1,0:T(8,128)(2,1)S(1)}, u32[]{:S(2)}, u32[]{:S(2)}) collective-permute-start(bf16[4,128,128]{2,1,0:T(8,128)(2,1)S(1)} %get-tuple-element.70), channel_id=1, source_target_pairs={{0,4},{1,5},{2,6},{3,7},{4,0},{5,1},{6,2},{7,3},{8,12},{9,13},{10,... | collective-permute-start | bytes 393224 | tf_op jit(solution)/shard_map/ppermute | solution.py:458
  52.0 6.4 %collective-permute-start.16 = (bf16[4,128,128]{2,1,0:T(8,128)(2,1)S(1)}, bf16[4,128,128]{2,1,0:T(8,128)(2,1)S(1)}, u32[]{:S(2)}, u32[]{:S(2)}) collective-permute-start(bf16[4,128,128]{2,1,0:T(8,128)(2,1)S(1)} %get-tuple-element.71), channel_id=1, source_target_pairs={{0,6},{1,7},{2,4},{3,5},{4,2},{5,3},{6,0},{7,1},{8,14},{9,15},{10,... | collective-permute-start | bytes 393224 | tf_op jit(solution)/shard_map/ppermute | solution.py:458
  59.1 18.1 %collective-permute-start.27 = (bf16[128,2048]{1,0:T(8,128)(2,1)S(1)}, bf16[128,2048]{1,0:T(8,128)(2,1)S(1)}, u32[]{:S(2)}, u32[]{:S(2)}) collective-permute-start(bf16[128,2048]{1,0:T(8,128)(2,1)S(1)} %get-tuple-element.82), channel_id=1, source_target_pairs={{0,1},{1,0},{2,3},{3,2},{4,5},{5,4},{6,7},{7,6},{8,9},{9,8},{10,11... | collective-permute-start | bytes 1572872 | tf_op jit(solution)/shard_map/ppermute | solution.py:453
  59.2 26.5 %collective-permute-start.17 = (bf16[16,128,128]{2,1,0:T(8,128)(2,1)S(1)}, bf16[16,128,128]{2,1,0:T(8,128)(2,1)S(1)}, u32[]{:S(2)}, u32[]{:S(2)}) collective-permute-start(bf16[16,128,128]{2,1,0:T(8,128)(2,1)S(1)} %get-tuple-element.77.late), channel_id=1, source_target_pairs={{0,1},{1,0},{2,3},{3,2},{4,5},{5,4},{6,7},{7,6},{8,9},{9,8},{10,11... | collective-permute-start | bytes 1572872 | tf_op jit(solution)/shard_map/ppermute | solution.py:453
  59.7 13.1 %collective-permute-start.19 = (bf16[4,128,128]{2,1,0:T(8,128)(2,1)S(1)}, bf16[4,128,128]{2,1,0:T(8,128)(2,1)S(1)}, u32[]{:S(2)}, u32[]{:S(2)}) collective-permute-start(bf16[4,128,128]{2,1,0:T(8,128)(2,1)S(1)} %get-tuple-element.74.rest_4_), channel_id=1, source_target_pairs={{16,0},{24,8},{17,1},{25,9},{18,2},{26,10},{19,3},{27,11},{20,4},{... | collective-permute-start | bytes 393224 | tf_op jit(solution)/shard_map/ppermute | solution.py:479
  61.0 11.8 %collective-permute-start.18 = (bf16[4,128,128]{2,1,0:T(8,128)(2,1)S(1)}, bf16[4,128,128]{2,1,0:T(8,128)(2,1)S(1)}, u32[]{:S(2)}, u32[]{:S(2)}) collective-permute-start(bf16[4,128,128]{2,1,0:T(8,128)(2,1)S(1)} %get-tuple-element.74.rest_4_), channel_id=1, source_target_pairs={{8,0},{16,8},{24,16},{9,1},{17,9},{25,17},{10,2},{18,10},{26,18},{... | collective-permute-start | bytes 393224 | tf_op jit(solution)/shard_map/ppermute | solution.py:479
  73.7 5.5 %collective-permute-start.21 = (bf16[4,128,128]{2,1,0:T(8,128)(2,1)S(1)}, bf16[4,128,128]{2,1,0:T(8,128)(2,1)S(1)}, u32[]{:S(2)}, u32[]{:S(2)}) collective-permute-start(bf16[4,128,128]{2,1,0:T(8,128)(2,1)S(1)} %get-tuple-element.79), channel_id=1, source_target_pairs={{0,2},{1,3},{2,0},{3,1},{4,6},{5,7},{6,4},{7,5},{8,10},{9,11},{10,... | collective-permute-start | bytes 393224 | tf_op jit(solution)/shard_map/ppermute | solution.py:458
  75.2 5.5 %collective-permute-start.23 = (bf16[4,128,128]{2,1,0:T(8,128)(2,1)S(1)}, bf16[4,128,128]{2,1,0:T(8,128)(2,1)S(1)}, u32[]{:S(2)}, u32[]{:S(2)}) collective-permute-start(bf16[4,128,128]{2,1,0:T(8,128)(2,1)S(1)} %get-tuple-element.80), channel_id=1, source_target_pairs={{0,4},{1,5},{2,6},{3,7},{4,0},{5,1},{6,2},{7,3},{8,12},{9,13},{10,... | collective-permute-start | bytes 393224 | tf_op jit(solution)/shard_map/ppermute | solution.py:458
  76.8 6.1 %collective-permute-start.25 = (bf16[4,128,128]{2,1,0:T(8,128)(2,1)S(1)}, bf16[4,128,128]{2,1,0:T(8,128)(2,1)S(1)}, u32[]{:S(2)}, u32[]{:S(2)}) collective-permute-start(bf16[4,128,128]{2,1,0:T(8,128)(2,1)S(1)} %get-tuple-element.81), channel_id=1, source_target_pairs={{0,6},{1,7},{2,4},{3,5},{4,2},{5,3},{6,0},{7,1},{8,14},{9,15},{10,... | collective-permute-start | bytes 393224 | tf_op jit(solution)/shard_map/ppermute | solution.py:458
  77.2 8.4 %collective-permute-start.20 = (bf16[4,128,128]{2,1,0:T(8,128)(2,1)S(1)}, bf16[4,128,128]{2,1,0:T(8,128)(2,1)S(1)}, u32[]{:S(2)}, u32[]{:S(2)}) collective-permute-start(bf16[4,128,128]{2,1,0:T(8,128)(2,1)S(1)} %get-tuple-element.78.rest_0_), channel_id=1, source_target_pairs={{0,1},{1,0},{2,3},{3,2},{4,5},{5,4},{6,7},{7,6},{8,9},{9,8},{10,11... | collective-permute-start | bytes 393224 | tf_op jit(solution)/shard_map/ppermute | solution.py:453
  79.2 6.5 %collective-permute-start.22 = (bf16[4,128,128]{2,1,0:T(8,128)(2,1)S(1)}, bf16[4,128,128]{2,1,0:T(8,128)(2,1)S(1)}, u32[]{:S(2)}, u32[]{:S(2)}) collective-permute-start(bf16[4,128,128]{2,1,0:T(8,128)(2,1)S(1)} %collective-permute-done.21.rest_1_), channel_id=1, source_target_pairs={{0,1},{1,0},{2,3},{3,2},{4,5},{5,4},{6,7},{7,6},{8,9},{9,8},{10,11... | collective-permute-start | bytes 393224 | tf_op jit(solution)/shard_map/ppermute | solution.py:453
  80.8 4.9 %collective-permute-start.24 = (bf16[4,128,128]{2,1,0:T(8,128)(2,1)S(1)}, bf16[4,128,128]{2,1,0:T(8,128)(2,1)S(1)}, u32[]{:S(2)}, u32[]{:S(2)}) collective-permute-start(bf16[4,128,128]{2,1,0:T(8,128)(2,1)S(1)} %collective-permute-done.23.rest_2_), channel_id=1, source_target_pairs={{0,1},{1,0},{2,3},{3,2},{4,5},{5,4},{6,7},{7,6},{8,9},{9,8},{10,11... | collective-permute-start | bytes 393224 | tf_op jit(solution)/shard_map/ppermute | solution.py:453
  82.9 2.8 %collective-permute-start.26 = (bf16[4,128,128]{2,1,0:T(8,128)(2,1)S(1)}, bf16[4,128,128]{2,1,0:T(8,128)(2,1)S(1)}, u32[]{:S(2)}, u32[]{:S(2)}) collective-permute-start(bf16[4,128,128]{2,1,0:T(8,128)(2,1)S(1)} %collective-permute-done.25.rest_3_), channel_id=1, source_target_pairs={{0,1},{1,0},{2,3},{3,2},{4,5},{5,4},{6,7},{7,6},{8,9},{9,8},{10,11... | collective-permute-start | bytes 393224 | tf_op jit(solution)/shard_map/ppermute | solution.py:453

commit v11 on v10

--- a/solution.py
+++ b/solution.py
@@ -353,14 +353,14 @@
     span = members * unit
     ends = doc_ends(lens)
     layer = place[1] * span
-    sign = -1 if forward else 1
     previous = doc_at(ends, layer - 1 if forward else layer + span)
     carry = None
-    for s, other in enumerate(others):
-        far = layer + sign * s * span
-        there = doc_at(ends, far - 1 if forward else far + span)
-        term = other[...].astype(F32) * same(there, previous)
-        carry = term if carry is None else carry + term
+    for other in others:
+        for z in range(other.shape[0]):
+            there = doc_at(ends, (z + 1) * span - 1 if forward else z * span)
+            beyond = z < place[1] if forward else z > place[1]
+            term = other[z].astype(F32) * jnp.where(beyond, same(there, previous), 0.0)
+            carry = term if carry is None else carry + term
     for step in range(members):
         i = step if forward else members - 1 - step
         near, far = layer + i * unit, layer + (i + 1) * unit - 1
@@ -391,7 +391,6 @@
     members = lax.axis_size("x") * lax.axis_size("head")
     owned = heads // members
     half = heads // 2
-    reach = range(1, min(layers - 1, -(-layers // 2)) + 1)
     place = jnp.stack(
         [lax.axis_index(("z", "x", "head")), lax.axis_index("z"), lax.axis_index(LAYER)]
     ).astype(jnp.int32)
@@ -444,6 +443,7 @@
     all_states = pltpu.VMEM((heads, DH, DH), BF16)
     block = owned
     single = pl.BlockSpec((block, DH, DH), lambda i, *a: (i, 0, 0))
+    stacked = pl.BlockSpec((layers, block, DH, DH), lambda i, *a: (0, i, 0, 0))
     grouped = pl.BlockSpec((chips, block, DH, DH), lambda i, *a: (0, i, 0, 0))
     buffer = pltpu.VMEM((chips, block, DH, DH), BF16)
     combining = (4 * half * DH * DH, 4 * half * DH * DH, 0)
@@ -473,17 +473,14 @@
             name + "_total",
             aliases={2 + chips + j: 1 + j for j in range(len(along))},
         )
-        others = []
-        for s in reach:
-            pairs = [(i, i + s) if forward else (i + s, i) for i in range(layers - s)]
-            others.append(lax.ppermute(total, "z", pairs))
+        others = [held_in_hbm(lax.all_gather(total, "z"))] if layers > 1 else []
         return came, others, total, along
 
     def spread(came, others, after, forward, name):
         sums = run(
             functools.partial(prefix_kernel, forward, 2 * count, chips, len(after)),
             moves,
-            [single] * chips + [untouched] * len(after) + [single] * len(others),
+            [single] * chips + [untouched] * len(after) + [stacked] * len(others),
             [single] * chips,
             [owned_bf] * chips,
             [buffer, buffer],

time: 89.4 us -> 109 us (1.22)
  blocking collectives: 0 us -> 33.3 us
  starting transfers between devices: 27.7 us -> 17.5 us
  waiting for transfers between devices: 27.6 us -> 22.2 us
  Pallas kernels: 31.7 us -> 33.9 us
    all_gather x0 -> x2, blocking collectives: none -> 33.3 us  [reach_out(): others = [held_in_hbm(lax.all_gather(total, 'z'))] if layers > 1 else []]
    ppermute x4 -> x0, starting transfers between devices: 10.7 us -> none  [reach_out(): others.append(lax.ppermute(total, 'z', pairs))]
    ppermute x4 -> x0, waiting for transfers between devices: 3.54 us -> none  [reach_out(): others.append(lax.ppermute(total, 'z', pairs))]
    pallas_call x12, Pallas kernels: 31.7 us -> 33.9 us  [run(): pl.pallas_call(kernel, grid_spec=pltpu.PrefetchScalarGridSpec(num_scalar_...]
    ppermute x12, waiting for transfers between devices: 24 us -> 22.2 us  [exchange(): lax.ppermute(state, LAYER, pairs[n])]
  transfers between devices with their start and end apart: 28 -> 24, of which waited for: 13 -> 11; matrix products, arithmetic and copies ran while one was open for 0% -> 0% of each run, Pallas kernels for 21% -> 20%
where the time goes in v11:
time: 109 us
  Pallas kernels  33.9 us (31%)
  blocking collectives  33.3 us (31%)
  waiting for transfers between devices  22.2 us (20%)
  starting transfers between devices  17.5 us (16%)
    pallas_call x12, Pallas kernels, run(): pl.pallas_call(kernel, grid_spec=pltpu.PrefetchScalarGridSpec(num_scalar_...  33.9 us
    all_gather x2, blocking collectives, reach_out(): others = [held_in_hbm(lax.all_gather(total, 'z'))] if layers > 1 else []  33.3 us
    ppermute x12, waiting for transfers between devices, exchange(): lax.ppermute(state, LAYER, pairs[n])  22.2 us
    ppermute x12, starting transfers between devices, exchange(): lax.ppermute(state, LAYER, pairs[n])  14.7 us
    ppermute x12, starting transfers between devices, swap(): return lax.ppermute(state, LAYER, [(i, i ^ 1) for i in range(members)])  2.76 us
  transfers between devices with their start and end apart: 24, of which 11 were waited for; matrix products, arithmetic and copies ran while one was open for 0% of the time, Pallas kernels for 20%

profile of v11, /device:TPU:0, one launch (start us, length us, event | category | flops | bytes accessed | tf_op | source)
XLA Modules:
  0.0 108.5 jit_solution(13668397743254500358)
XLA Ops:
  0.6 0.1 pad_add_fusion.place
  0.7 0.7 copy-done.4
  1.4 3.0 %tail_mate.1 = (bf16[16,128,128]{2,1,0:T(8,128)(2,1)S(1)}, bf16[3,128,2048]{2,1,0:T(8,128)(2,1)S(1)}, bf16[128,2048]{1,0:T(8,128)(2,1)S(1)}) custom-call(s32[8]{0:T(128)S(1)} %copy-done.4, s32[3]{0:T(128)S(1)} %pad_add_fusion.place, bf16[128,4096]{1,0:T(8,128)(2,1)} %k.11, bf16[128,4096]{1,0:T(8,128)(2,1)} %v.11, bf16[128,4096]{1,0:T(8,128)(2,1)} %q.3, ...), custom_call_target="tpu_custom_call" | custom-call | flops 67108864 | bytes 1572864 | tf_op jit(solution)/shard_map/tail_mate/pallas_call | solution.py:423
  4.4 0.5 collective-permute-start
  4.9 2.6 %tail_own.1.rest_6_ = bf16[16,128,128]{2,1,0:T(8,128)(2,1)S(1)} custom-call(s32[8]{0:T(128)S(1)} %copy-done.4, s32[3]{0:T(128)S(1)} %pad_add_fusion.place, bf16[128,4096]{1,0:T(8,128)(2,1)} %k.11, bf16[128,4096]{1,0:T(8,128)(2,1)} %v.11), custom_call_target="tpu_custom_call" | custom-call | flops 67108864 | bytes 1572864 | tf_op jit(solution)/shard_map/tail_own/pallas_call | solution.py:423
  7.5 0.0 collective-permute-done.rest_2_
  7.5 0.8 carried_chip.1
  8.2 0.0 copy-start
  8.3 0.0 copy-start.1
  8.3 0.0 copy-start.2
  8.3 2.6 %collective-permute-start.1 = (bf16[4,128,128]{2,1,0:T(8,128)(2,1)S(1)}, bf16[4,128,128]{2,1,0:T(8,128)(2,1)S(1)}, u32[]{:S(2)}, u32[]{:S(2)}) collective-permute-start(bf16[4,128,128]{2,1,0:T(8,128)(2,1)S(1)} %get-tuple-element.49), channel_id=1, source_target_pairs={{0,2},{1,3},{2,0},{3,1},{4,6},{5,7},{6,4},{7,5},{8,10},{9,11},{10,... | collective-permute-start | bytes 393224 | tf_op jit(solution)/shard_map/ppermute | solution.py:458
  10.9 1.5 %collective-permute-start.2 = (bf16[4,128,128]{2,1,0:T(8,128)(2,1)S(1)}, bf16[4,128,128]{2,1,0:T(8,128)(2,1)S(1)}, u32[]{:S(2)}, u32[]{:S(2)}) collective-permute-start(bf16[4,128,128]{2,1,0:T(8,128)(2,1)S(1)} %get-tuple-element.50), channel_id=1, source_target_pairs={{0,4},{1,5},{2,6},{3,7},{4,0},{5,1},{6,2},{7,3},{8,12},{9,13},{10,... | collective-permute-start | bytes 393224 | tf_op jit(solution)/shard_map/ppermute | solution.py:458
  12.3 0.1 collective-permute-start.3
  12.4 2.6 %collective-permute-done.1.rest_1_ = bf16[4,128,128]{2,1,0:T(8,128)(2,1)S(1)} collective-permute-done((bf16[4,128,128]{2,1,0:T(8,128)(2,1)S(1)}, bf16[4,128,128]{2,1,0:T(8,128)(2,1)S(1)}, u32[]{:S(2)}, u32[]{:S(2)}) %collective-permute-start.1) | collective-permute-done | bytes 131104 | tf_op jit(solution)/shard_map/ppermute | solution.py:458
  15.0 2.2 %collective-permute-done.2.rest_2_ = bf16[4,128,128]{2,1,0:T(8,128)(2,1)S(1)} collective-permute-done((bf16[4,128,128]{2,1,0:T(8,128)(2,1)S(1)}, bf16[4,128,128]{2,1,0:T(8,128)(2,1)S(1)}, u32[]{:S(2)}, u32[]{:S(2)}) %collective-permute-start.2) | collective-permute-done | bytes 131104 | tf_op jit(solution)/shard_map/ppermute | solution.py:458
  17.2 1.9 %collective-permute-done.3.rest_3_ = bf16[4,128,128]{2,1,0:T(8,128)(2,1)S(1)} collective-permute-done((bf16[4,128,128]{2,1,0:T(8,128)(2,1)S(1)}, bf16[4,128,128]{2,1,0:T(8,128)(2,1)S(1)}, u32[]{:S(2)}, u32[]{:S(2)}) %collective-permute-start.3) | collective-permute-done | bytes 131104 | tf_op jit(solution)/shard_map/ppermute | solution.py:458
  19.1 0.7 carried_total.1
  19.8 0.1 collective-permute-start.4
  19.9 0.5 collective-permute-start.6
  20.4 0.1 collective-permute-start.5
  20.5 17.0 %all-gather = bf16[16,128,128]{2,1,0:T(8,128)(2,1)} all-gather(bf16[4,128,128]{2,1,0:T(8,128)(2,1)S(1)} %get-tuple-element.60), channel_id=2, replica_groups=mesh['z'=4,'x'=2,'head'=4] {'z'}, dimensions={0}, use_global_device_ids=true | all-gather | bytes 655360 | tf_op jit(solution)/shard_map/all_gather | solution.py:476
  37.5 0.0 collective-permute-done.4.mate
  37.5 4.3 %within_chip.1 = (f32[256,2048]{1,0:T(8,128)S(1)}, bf16[256,2048]{1,0:T(8,128)(2,1)S(1)}, bf16[16,128,256]{2,1,0:T(8,128)(2,1)S(1)}) custom-call(s32[8]{0:T(128)S(1)} %copy-done.4, s32[3]{0:T(128)S(1)} %pad_add_fusion.place, bf16[128,4096]{1,0:T(8,128)(2,1)S(1)} %copy-done.2, bf16[128,4096]{1,0:T(8,128)(2,1)S(1)} %copy-done, ...), custom_call_target="tpu_custom_call" | custom-call | flops 671088640 | bytes 7340032 | tf_op jit(solution)/shard_map/within_chip/pallas_call | solution.py:423
  41.8 0.0 copy-start.3
  41.8 0.0 collective-permute-done.6.rest_5_.rest_3_
  41.8 2.0 %carried_prefix.1 = (bf16[4,128,128]{2,1,0:T(8,128)(2,1)S(1)}, bf16[4,128,128]{2,1,0:T(8,128)(2,1)S(1)}, bf16[4,128,128]{2,1,0:T(8,128)(2,1)S(1)}, bf16[4,128,128]{2,1,0:T(8,128)(2,1)S(1)}) custom-call(s32[8]{0:T(128)S(1)} %copy-done.4, s32[3]{0:T(128)S(1)} %pad_add_fusion.place, bf16[4,128,128]{2,1,0:T(8,128)(2,1)S(1)} %get-tuple-element.48.rest_0_, ...), custom_call_target="tpu_custom_call" | custom-call | flops 1048576 | bytes 1048576 | tf_op jit(solution)/shard_map/carried_prefix/pallas_call | solution.py:423
  43.8 1.6 %collective-permute-start.7 = (bf16[4,128,128]{2,1,0:T(8,128)(2,1)S(1)}, bf16[4,128,128]{2,1,0:T(8,128)(2,1)S(1)}, u32[]{:S(2)}, u32[]{:S(2)}) collective-permute-start(bf16[4,128,128]{2,1,0:T(8,128)(2,1)S(1)} %get-tuple-element.62), channel_id=1, source_target_pairs={{0,2},{1,3},{2,0},{3,1},{4,6},{5,7},{6,4},{7,5},{8,10},{9,11},{10,... | collective-permute-start | bytes 393224 | tf_op jit(solution)/shard_map/ppermute | solution.py:458
  45.4 1.5 %collective-permute-start.8 = (bf16[4,128,128]{2,1,0:T(8,128)(2,1)S(1)}, bf16[4,128,128]{2,1,0:T(8,128)(2,1)S(1)}, u32[]{:S(2)}, u32[]{:S(2)}) collective-permute-start(bf16[4,128,128]{2,1,0:T(8,128)(2,1)S(1)} %get-tuple-element.63), channel_id=1, source_target_pairs={{0,4},{1,5},{2,6},{3,7},{4,0},{5,1},{6,2},{7,3},{8,12},{9,13},{10,... | collective-permute-start | bytes 393224 | tf_op jit(solution)/shard_map/ppermute | solution.py:458
  46.9 0.5 collective-permute-start.9
  47.4 0.0 collective-permute-done.5.mate_g
  47.4 1.8 %collective-permute-done.7.rest_1_ = bf16[4,128,128]{2,1,0:T(8,128)(2,1)S(1)} collective-permute-done((bf16[4,128,128]{2,1,0:T(8,128)(2,1)S(1)}, bf16[4,128,128]{2,1,0:T(8,128)(2,1)S(1)}, u32[]{:S(2)}, u32[]{:S(2)}) %collective-permute-start.7) | collective-permute-done | bytes 131104 | tf_op jit(solution)/shard_map/ppermute | solution.py:458
  49.2 1.9 %collective-permute-done.8.rest_2_ = bf16[4,128,128]{2,1,0:T(8,128)(2,1)S(1)} collective-permute-done((bf16[4,128,128]{2,1,0:T(8,128)(2,1)S(1)}, bf16[4,128,128]{2,1,0:T(8,128)(2,1)S(1)}, u32[]{:S(2)}, u32[]{:S(2)}) %collective-permute-start.8) | collective-permute-done | bytes 131104 | tf_op jit(solution)/shard_map/ppermute | solution.py:458
  51.0 2.1 %collective-permute-done.9.rest_3_ = bf16[4,128,128]{2,1,0:T(8,128)(2,1)S(1)} collective-permute-done((bf16[4,128,128]{2,1,0:T(8,128)(2,1)S(1)}, bf16[4,128,128]{2,1,0:T(8,128)(2,1)S(1)}, u32[]{:S(2)}, u32[]{:S(2)}) %collective-permute-start.9) | collective-permute-done | bytes 131104 | tf_op jit(solution)/shard_map/ppermute | solution.py:458
  53.1 5.3 %normed.1 = (bf16[128,4096]{1,0:T(8,128)(2,1)}, bf16[128,2048]{1,0:T(8,128)(2,1)S(1)}, bf16[128,2048]{1,0:T(8,128)(2,1)S(1)}, bf16[128,2048]{1,0:T(8,128)(2,1)S(...) custom-call(s32[8]{0:T(128)S(1)} %copy-done.4, ...), custom_call_target="tpu_custom_call" | custom-call | flops 536870912 | bytes 8388608 | tf_op jit(solution)/shard_map/normed/pallas_call | solution.py:423
  58.4 0.0 collective-permute-start.10
  58.4 0.5 collective-permute-start.11
  58.9 0.8 collective-permute-start.12
  59.7 1.5 %collective-permute-start.13 = (bf16[4,128,128]{2,1,0:T(8,128)(2,1)S(1)}, bf16[4,128,128]{2,1,0:T(8,128)(2,1)S(1)}, u32[]{:S(2)}, u32[]{:S(2)}) collective-permute-start(bf16[4,128,128]{2,1,0:T(8,128)(2,1)S(1)} %get-tuple-element.70), channel_id=1, source_target_pairs={{0,4},{1,5},{2,6},{3,7},{4,0},{5,1},{6,2},{7,3},{8,12},{9,13},{10,... | collective-permute-start | bytes 393224 | tf_op jit(solution)/shard_map/ppermute | solution.py:458
  61.2 1.2 %collective-permute-start.14 = (bf16[4,128,128]{2,1,0:T(8,128)(2,1)S(1)}, bf16[4,128,128]{2,1,0:T(8,128)(2,1)S(1)}, u32[]{:S(2)}, u32[]{:S(2)}) collective-permute-start(bf16[4,128,128]{2,1,0:T(8,128)(2,1)S(1)} %get-tuple-element.71), channel_id=1, source_target_pairs={{0,6},{1,7},{2,4},{3,5},{4,2},{5,3},{6,0},{7,1},{8,14},{9,15},{10,... | collective-permute-start | bytes 393224 | tf_op jit(solution)/shard_map/ppermute | solution.py:458
  62.4 2.0 %collective-permute-done.12.rest_1_ = bf16[4,128,128]{2,1,0:T(8,128)(2,1)S(1)} collective-permute-done((bf16[4,128,128]{2,1,0:T(8,128)(2,1)S(1)}, bf16[4,128,128]{2,1,0:T(8,128)(2,1)S(1)}, u32[]{:S(2)}, u32[]{:S(2)}) %collective-permute-start.12) | collective-permute-done | bytes 131104 | tf_op jit(solution)/shard_map/ppermute | solution.py:458
  64.4 1.7 %collective-permute-done.13.rest_2_ = bf16[4,128,128]{2,1,0:T(8,128)(2,1)S(1)} collective-permute-done((bf16[4,128,128]{2,1,0:T(8,128)(2,1)S(1)}, bf16[4,128,128]{2,1,0:T(8,128)(2,1)S(1)}, u32[]{:S(2)}, u32[]{:S(2)}) %collective-permute-start.13) | collective-permute-done | bytes 131104 | tf_op jit(solution)/shard_map/ppermute | solution.py:458
  66.1 2.2 %collective-permute-done.14.rest_3_ = bf16[4,128,128]{2,1,0:T(8,128)(2,1)S(1)} collective-permute-done((bf16[4,128,128]{2,1,0:T(8,128)(2,1)S(1)}, bf16[4,128,128]{2,1,0:T(8,128)(2,1)S(1)}, u32[]{:S(2)}, u32[]{:S(2)}) %collective-permute-start.14) | collective-permute-done | bytes 131104 | tf_op jit(solution)/shard_map/ppermute | solution.py:458
  68.3 0.7 future_total.1
  69.1 0.1 collective-permute-start.23
  69.1 0.5 collective-permute-start.15
  69.6 16.3 %all-gather.1 = bf16[16,128,128]{2,1,0:T(8,128)(2,1)} all-gather(bf16[4,128,128]{2,1,0:T(8,128)(2,1)S(1)} %get-tuple-element.74.rest_4_), channel_id=3, replica_groups=mesh['z'=4,'x'=2,'head'=4] {'z'}, dimensions={0}, use_global_device_ids=true | all-gather | bytes 655360 | tf_op jit(solution)/shard_map/all_gather | solution.py:476
  85.9 0.0 collective-permute-done.10.other_ga
  85.9 0.0 collective-permute-done.11.rest_1_
  86.0 6.9 %grads_within.1 = (bf16[128,4096]{1,0:T(8,128)(2,1)}, f32[128,4096]{1,0:T(8,128)S(1)}, f32[128,4096]{1,0:T(8,128)S(1)}) custom-call(s32[8]{0:T(128)S(1)} %copy-done.4, s32[3]{0:T(128)S(1)} %pad_add_fusion.place, bf16[128,4096]{1,0:T(8,128)(2,1)S(1)} %copy-done.2, bf16[128,4096]{1,0:T(8,128)(2,1)S(1)} %copy-done, bf16[128,4096]{1,0:T(8,128)(2,1)S(1)} %copy-done.1, ...), custom_call_target="tpu_custom_call" | custom-call | flops 1073741824 | bytes 11534336 | tf_op jit(solution)/shard_map/grads_within/pallas_call | solution.py:423
  92.9 2.0 %future_prefix.1 = (bf16[4,128,128]{2,1,0:T(8,128)(2,1)S(1)}, bf16[4,128,128]{2,1,0:T(8,128)(2,1)S(1)}, bf16[4,128,128]{2,1,0:T(8,128)(2,1)S(1)}, bf16[4,128,128]{2,1,0:T(8,128)(2,1)S(1)}) custom-call(s32[8]{0:T(128)S(1)} %copy-done.4, s32[3]{0:T(128)S(1)} %pad_add_fusion.place, bf16[4,128,128]{2,1,0:T(8,128)(2,1)S(1)} %get-tuple-element.68.rest_0_, ...), custom_call_target="tpu_custom_call" | custom-call | flops 1048576 | bytes 1048576 | tf_op jit(solution)/shard_map/future_prefix/pallas_call | solution.py:423
  94.9 0.6 collective-permute-start.17
  95.4 1.5 %collective-permute-start.19 = (bf16[4,128,128]{2,1,0:T(8,128)(2,1)S(1)}, bf16[4,128,128]{2,1,0:T(8,128)(2,1)S(1)}, u32[]{:S(2)}, u32[]{:S(2)}) collective-permute-start(bf16[4,128,128]{2,1,0:T(8,128)(2,1)S(1)} %get-tuple-element.80), channel_id=1, source_target_pairs={{0,4},{1,5},{2,6},{3,7},{4,0},{5,1},{6,2},{7,3},{8,12},{9,13},{10,... | collective-permute-start | bytes 393224 | tf_op jit(solution)/shard_map/ppermute | solution.py:458
  96.9 1.5 %collective-permute-start.21 = (bf16[4,128,128]{2,1,0:T(8,128)(2,1)S(1)}, bf16[4,128,128]{2,1,0:T(8,128)(2,1)S(1)}, u32[]{:S(2)}, u32[]{:S(2)}) collective-permute-start(bf16[4,128,128]{2,1,0:T(8,128)(2,1)S(1)} %get-tuple-element.81), channel_id=1, source_target_pairs={{0,6},{1,7},{2,4},{3,5},{4,2},{5,3},{6,0},{7,1},{8,14},{9,15},{10,... | collective-permute-start | bytes 393224 | tf_op jit(solution)/shard_map/ppermute | solution.py:458
  98.4 2.7 %collective-permute-done.17.rest_1_ = bf16[4,128,128]{2,1,0:T(8,128)(2,1)S(1)} collective-permute-done((bf16[4,128,128]{2,1,0:T(8,128)(2,1)S(1)}, bf16[4,128,128]{2,1,0:T(8,128)(2,1)S(1)}, u32[]{:S(2)}, u32[]{:S(2)}) %collective-permute-start.17) | collective-permute-done | bytes 131104 | tf_op jit(solution)/shard_map/ppermute | solution.py:458
  101.1 0.0 collective-permute-done.19.rest_2_
  101.1 0.5 collective-permute-start.20
  101.7 1.1 %collective-permute-done.21.rest_3_ = bf16[4,128,128]{2,1,0:T(8,128)(2,1)S(1)} collective-permute-done((bf16[4,128,128]{2,1,0:T(8,128)(2,1)S(1)}, bf16[4,128,128]{2,1,0:T(8,128)(2,1)S(1)}, u32[]{:S(2)}, u32[]{:S(2)}) %collective-permute-start.21) | collective-permute-done | bytes 131104 | tf_op jit(solution)/shard_map/ppermute | solution.py:458
  102.8 0.0 collective-permute-start.22
  102.8 2.8 %grads_last_0.1 = (bf16[128,4096]{1,0:T(8,128)(2,1)}, bf16[128,4096]{1,0:T(8,128)(2,1)}) custom-call(s32[8]{0:T(128)S(1)} %copy-done.4, s32[3]{0:T(128)S(1)} %pad_add_fusion.place, bf16[128,4096]{1,0:T(8,128)(2,1)S(1)} %copy-done, bf16[128,4096]{1,0:T(8,128)(2,1)S(1)} %copy-done.1, f32[128,4096]{1,0:T(8,128)S(1)} %get-tuple-element.75.rest_4_.gk_part, ...), custom_call_target="tpu_custom_call" | custom-call | flops 134217728 | bytes 4718592 | tf_op jit(solution)/shard_map/grads_last_0/pallas_call | solution.py:423
  105.6 0.0 collective-permute-done.15.late
  105.6 0.0 collective-permute-done.16.rest_0_
  105.6 0.0 collective-permute-done.18.rest_1_
  105.6 0.0 collective-permute-done.20.rest_2_
  105.6 3.0 %grads_last_1.1 = (bf16[128,4096]{1,0:T(8,128)(2,1)}, bf16[128,4096]{1,0:T(8,128)(2,1)}, bf16[128,4096]{1,0:T(8,128)(2,1)}) custom-call(s32[8]{0:T(128)S(1)} %copy-done.4, s32[3]{0:T(128)S(1)} %pad_add_fusion.place, bf16[128,4096]{1,0:T(8,128)(2,1)S(1)} %copy-done, ...), custom_call_target="tpu_custom_call", output_to_operand_aliasing={{0}: (12, {}), {1}: (13, {}), {2}: (14, {})} | custom-call | flops 134217728 | bytes 4718592 | tf_op jit(solution)/shard_map/grads_last_1/pallas_call | solution.py:423
  (9 shorter events, 0.0 us)
Async XLA Ops:
  0.7 0.7 copy-start.4
  4.4 3.1 %collective-permute-start = (bf16[16,128,128]{2,1,0:T(8,128)(2,1)S(1)}, bf16[16,128,128]{2,1,0:T(8,128)(2,1)S(1)}, u32[]{:S(2)}, u32[]{:S(2)}) collective-permute-start(bf16[16,128,128]{2,1,0:T(8,128)(2,1)S(1)} %get-tuple-element.47), channel_id=1, source_target_pairs={{0,1},{1,0},{2,3},{3,2},{4,5},{5,4},{6,7},{7,6},{8,9},{9,8},{10,11... | collective-permute-start | bytes 1572872 | tf_op jit(solution)/shard_map/ppermute | solution.py:453
  8.2 29.3 %copy-start = (bf16[128,4096]{1,0:T(8,128)(2,1)S(1)}, bf16[128,4096]{1,0:T(8,128)(2,1)}, u32[]{:S(2)}) copy-start(bf16[128,4096]{1,0:T(8,128)(2,1)} %k.11) | copy-start | bytes 3145732
  8.3 29.2 %copy-start.1 = (bf16[128,4096]{1,0:T(8,128)(2,1)S(1)}, bf16[128,4096]{1,0:T(8,128)(2,1)}, u32[]{:S(2)}) copy-start(bf16[128,4096]{1,0:T(8,128)(2,1)} %v.11) | copy-start | bytes 3145732
  8.3 29.2 %copy-start.2 = (bf16[128,4096]{1,0:T(8,128)(2,1)S(1)}, bf16[128,4096]{1,0:T(8,128)(2,1)}, u32[]{:S(2)}) copy-start(bf16[128,4096]{1,0:T(8,128)(2,1)} %q.3) | copy-start | bytes 3145732
  8.3 6.8 %collective-permute-start.1 = (bf16[4,128,128]{2,1,0:T(8,128)(2,1)S(1)}, bf16[4,128,128]{2,1,0:T(8,128)(2,1)S(1)}, u32[]{:S(2)}, u32[]{:S(2)}) collective-permute-start(bf16[4,128,128]{2,1,0:T(8,128)(2,1)S(1)} %get-tuple-element.49), channel_id=1, source_target_pairs={{0,2},{1,3},{2,0},{3,1},{4,6},{5,7},{6,4},{7,5},{8,10},{9,11},{10,... | collective-permute-start | bytes 393224 | tf_op jit(solution)/shard_map/ppermute | solution.py:458
  10.9 6.3 %collective-permute-start.2 = (bf16[4,128,128]{2,1,0:T(8,128)(2,1)S(1)}, bf16[4,128,128]{2,1,0:T(8,128)(2,1)S(1)}, u32[]{:S(2)}, u32[]{:S(2)}) collective-permute-start(bf16[4,128,128]{2,1,0:T(8,128)(2,1)S(1)} %get-tuple-element.50), channel_id=1, source_target_pairs={{0,4},{1,5},{2,6},{3,7},{4,0},{5,1},{6,2},{7,3},{8,12},{9,13},{10,... | collective-permute-start | bytes 393224 | tf_op jit(solution)/shard_map/ppermute | solution.py:458
  12.3 6.7 %collective-permute-start.3 = (bf16[4,128,128]{2,1,0:T(8,128)(2,1)S(1)}, bf16[4,128,128]{2,1,0:T(8,128)(2,1)S(1)}, u32[]{:S(2)}, u32[]{:S(2)}) collective-permute-start(bf16[4,128,128]{2,1,0:T(8,128)(2,1)S(1)} %get-tuple-element.51), channel_id=1, source_target_pairs={{0,6},{1,7},{2,4},{3,5},{4,2},{5,3},{6,0},{7,1},{8,14},{9,15},{10,... | collective-permute-start | bytes 393224 | tf_op jit(solution)/shard_map/ppermute | solution.py:458
  19.8 17.7 %collective-permute-start.4 = (bf16[3,128,2048]{2,1,0:T(8,128)(2,1)S(1)}, bf16[3,128,2048]{2,1,0:T(8,128)(2,1)S(1)}, u32[]{:S(2)}, u32[]{:S(2)}) collective-permute-start(bf16[3,128,2048]{2,1,0:T(8,128)(2,1)S(1)} %get-tuple-element.54), channel_id=1, source_target_pairs={{0,1},{1,0},{2,3},{3,2},{4,5},{5,4},{6,7},{7,6},{8,9},{9,8},{10,11... | collective-permute-start | bytes 4718600 | tf_op jit(solution)/shard_map/ppermute | solution.py:453
  19.9 21.9 %collective-permute-start.6 = (bf16[16,128,128]{2,1,0:T(8,128)(2,1)S(1)}, bf16[16,128,128]{2,1,0:T(8,128)(2,1)S(1)}, u32[]{:S(2)}, u32[]{:S(2)}) collective-permute-start(bf16[16,128,128]{2,1,0:T(8,128)(2,1)S(1)} %get-tuple-element.59), channel_id=1, source_target_pairs={{0,1},{1,0},{2,3},{3,2},{4,5},{5,4},{6,7},{7,6},{8,9},{9,8},{10,11... | collective-permute-start | bytes 1572872 | tf_op jit(solution)/shard_map/ppermute | solution.py:453
  20.4 27.0 %collective-permute-start.5 = (bf16[128,2048]{1,0:T(8,128)(2,1)S(1)}, bf16[128,2048]{1,0:T(8,128)(2,1)S(1)}, u32[]{:S(2)}, u32[]{:S(2)}) collective-permute-start(bf16[128,2048]{1,0:T(8,128)(2,1)S(1)} %get-tuple-element.57), channel_id=1, source_target_pairs={{0,1},{1,0},{2,3},{3,2},{4,5},{5,4},{6,7},{7,6},{8,9},{9,8},{10,11... | collective-permute-start | bytes 1572872 | tf_op jit(solution)/shard_map/ppermute | solution.py:453
  41.8 11.3 %copy-start.3 = (bf16[128,4096]{1,0:T(8,128)(2,1)S(1)}, bf16[128,4096]{1,0:T(8,128)(2,1)}, u32[]{:S(2)}) copy-start(bf16[128,4096]{1,0:T(8,128)(2,1)} %g.1) | copy-start | bytes 3145732
  43.8 5.4 %collective-permute-start.7 = (bf16[4,128,128]{2,1,0:T(8,128)(2,1)S(1)}, bf16[4,128,128]{2,1,0:T(8,128)(2,1)S(1)}, u32[]{:S(2)}, u32[]{:S(2)}) collective-permute-start(bf16[4,128,128]{2,1,0:T(8,128)(2,1)S(1)} %get-tuple-element.62), channel_id=1, source_target_pairs={{0,2},{1,3},{2,0},{3,1},{4,6},{5,7},{6,4},{7,5},{8,10},{9,11},{10,... | collective-permute-start | bytes 393224 | tf_op jit(solution)/shard_map/ppermute | solution.py:458
  45.4 5.6 %collective-permute-start.8 = (bf16[4,128,128]{2,1,0:T(8,128)(2,1)S(1)}, bf16[4,128,128]{2,1,0:T(8,128)(2,1)S(1)}, u32[]{:S(2)}, u32[]{:S(2)}) collective-permute-start(bf16[4,128,128]{2,1,0:T(8,128)(2,1)S(1)} %get-tuple-element.63), channel_id=1, source_target_pairs={{0,4},{1,5},{2,6},{3,7},{4,0},{5,1},{6,2},{7,3},{8,12},{9,13},{10,... | collective-permute-start | bytes 393224 | tf_op jit(solution)/shard_map/ppermute | solution.py:458
  46.9 6.2 %collective-permute-start.9 = (bf16[4,128,128]{2,1,0:T(8,128)(2,1)S(1)}, bf16[4,128,128]{2,1,0:T(8,128)(2,1)S(1)}, u32[]{:S(2)}, u32[]{:S(2)}) collective-permute-start(bf16[4,128,128]{2,1,0:T(8,128)(2,1)S(1)} %get-tuple-element.64), channel_id=1, source_target_pairs={{0,6},{1,7},{2,4},{3,5},{4,2},{5,3},{6,0},{7,1},{8,14},{9,15},{10,... | collective-permute-start | bytes 393224 | tf_op jit(solution)/shard_map/ppermute | solution.py:458
  58.4 27.5 %collective-permute-start.10 = (bf16[128,2048]{1,0:T(8,128)(2,1)S(1)}, bf16[128,2048]{1,0:T(8,128)(2,1)S(1)}, u32[]{:S(2)}, u32[]{:S(2)}) collective-permute-start(bf16[128,2048]{1,0:T(8,128)(2,1)S(1)} %get-tuple-element.66), channel_id=1, source_target_pairs={{0,1},{1,0},{2,3},{3,2},{4,5},{5,4},{6,7},{7,6},{8,9},{9,8},{10,11... | collective-permute-start | bytes 1572872 | tf_op jit(solution)/shard_map/ppermute | solution.py:453
  58.4 27.5 %collective-permute-start.11 = (bf16[16,128,128]{2,1,0:T(8,128)(2,1)S(1)}, bf16[16,128,128]{2,1,0:T(8,128)(2,1)S(1)}, u32[]{:S(2)}, u32[]{:S(2)}) collective-permute-start(bf16[16,128,128]{2,1,0:T(8,128)(2,1)S(1)} %get-tuple-element.67.rest_0_), channel_id=1, source_target_pairs={{0,1},{1,0},{2,3},{3,2},{4,5},{5,4},{6,7},{7,6},{8,9},{9,8},{10,11... | collective-permute-start | bytes 1572872 | tf_op jit(solution)/shard_map/ppermute | solution.py:453
  58.9 5.5 %collective-permute-start.12 = (bf16[4,128,128]{2,1,0:T(8,128)(2,1)S(1)}, bf16[4,128,128]{2,1,0:T(8,128)(2,1)S(1)}, u32[]{:S(2)}, u32[]{:S(2)}) collective-permute-start(bf16[4,128,128]{2,1,0:T(8,128)(2,1)S(1)} %get-tuple-element.69), channel_id=1, source_target_pairs={{0,2},{1,3},{2,0},{3,1},{4,6},{5,7},{6,4},{7,5},{8,10},{9,11},{10,... | collective-permute-start | bytes 393224 | tf_op jit(solution)/shard_map/ppermute | solution.py:458
  59.7 6.4 %collective-permute-start.13 = (bf16[4,128,128]{2,1,0:T(8,128)(2,1)S(1)}, bf16[4,128,128]{2,1,0:T(8,128)(2,1)S(1)}, u32[]{:S(2)}, u32[]{:S(2)}) collective-permute-start(bf16[4,128,128]{2,1,0:T(8,128)(2,1)S(1)} %get-tuple-element.70), channel_id=1, source_target_pairs={{0,4},{1,5},{2,6},{3,7},{4,0},{5,1},{6,2},{7,3},{8,12},{9,13},{10,... | collective-permute-start | bytes 393224 | tf_op jit(solution)/shard_map/ppermute | solution.py:458
  61.2 7.1 %collective-permute-start.14 = (bf16[4,128,128]{2,1,0:T(8,128)(2,1)S(1)}, bf16[4,128,128]{2,1,0:T(8,128)(2,1)S(1)}, u32[]{:S(2)}, u32[]{:S(2)}) collective-permute-start(bf16[4,128,128]{2,1,0:T(8,128)(2,1)S(1)} %get-tuple-element.71), channel_id=1, source_target_pairs={{0,6},{1,7},{2,4},{3,5},{4,2},{5,3},{6,0},{7,1},{8,14},{9,15},{10,... | collective-permute-start | bytes 393224 | tf_op jit(solution)/shard_map/ppermute | solution.py:458
  69.1 29.4 %collective-permute-start.23 = (bf16[128,2048]{1,0:T(8,128)(2,1)S(1)}, bf16[128,2048]{1,0:T(8,128)(2,1)S(1)}, u32[]{:S(2)}, u32[]{:S(2)}) collective-permute-start(bf16[128,2048]{1,0:T(8,128)(2,1)S(1)} %get-tuple-element.82), channel_id=1, source_target_pairs={{0,1},{1,0},{2,3},{3,2},{4,5},{5,4},{6,7},{7,6},{8,9},{9,8},{10,11... | collective-permute-start | bytes 1572872 | tf_op jit(solution)/shard_map/ppermute | solution.py:453
  69.1 36.4 %collective-permute-start.15 = (bf16[16,128,128]{2,1,0:T(8,128)(2,1)S(1)}, bf16[16,128,128]{2,1,0:T(8,128)(2,1)S(1)}, u32[]{:S(2)}, u32[]{:S(2)}) collective-permute-start(bf16[16,128,128]{2,1,0:T(8,128)(2,1)S(1)} %get-tuple-element.77.late), channel_id=1, source_target_pairs={{0,1},{1,0},{2,3},{3,2},{4,5},{5,4},{6,7},{7,6},{8,9},{9,8},{10,11... | collective-permute-start | bytes 1572872 | tf_op jit(solution)/shard_map/ppermute | solution.py:453
  94.9 6.3 %collective-permute-start.17 = (bf16[4,128,128]{2,1,0:T(8,128)(2,1)S(1)}, bf16[4,128,128]{2,1,0:T(8,128)(2,1)S(1)}, u32[]{:S(2)}, u32[]{:S(2)}) collective-permute-start(bf16[4,128,128]{2,1,0:T(8,128)(2,1)S(1)} %get-tuple-element.79), channel_id=1, source_target_pairs={{0,2},{1,3},{2,0},{3,1},{4,6},{5,7},{6,4},{7,5},{8,10},{9,11},{10,... | collective-permute-start | bytes 393224 | tf_op jit(solution)/shard_map/ppermute | solution.py:458
  95.4 5.7 %collective-permute-start.19 = (bf16[4,128,128]{2,1,0:T(8,128)(2,1)S(1)}, bf16[4,128,128]{2,1,0:T(8,128)(2,1)S(1)}, u32[]{:S(2)}, u32[]{:S(2)}) collective-permute-start(bf16[4,128,128]{2,1,0:T(8,128)(2,1)S(1)} %get-tuple-element.80), channel_id=1, source_target_pairs={{0,4},{1,5},{2,6},{3,7},{4,0},{5,1},{6,2},{7,3},{8,12},{9,13},{10,... | collective-permute-start | bytes 393224 | tf_op jit(solution)/shard_map/ppermute | solution.py:458
  96.9 5.9 %collective-permute-start.21 = (bf16[4,128,128]{2,1,0:T(8,128)(2,1)S(1)}, bf16[4,128,128]{2,1,0:T(8,128)(2,1)S(1)}, u32[]{:S(2)}, u32[]{:S(2)}) collective-permute-start(bf16[4,128,128]{2,1,0:T(8,128)(2,1)S(1)} %get-tuple-element.81), channel_id=1, source_target_pairs={{0,6},{1,7},{2,4},{3,5},{4,2},{5,3},{6,0},{7,1},{8,14},{9,15},{10,... | collective-permute-start | bytes 393224 | tf_op jit(solution)/shard_map/ppermute | solution.py:458
  98.4 7.1 %collective-permute-start.16 = (bf16[4,128,128]{2,1,0:T(8,128)(2,1)S(1)}, bf16[4,128,128]{2,1,0:T(8,128)(2,1)S(1)}, u32[]{:S(2)}, u32[]{:S(2)}) collective-permute-start(bf16[4,128,128]{2,1,0:T(8,128)(2,1)S(1)} %get-tuple-element.78.rest_0_), channel_id=1, source_target_pairs={{0,1},{1,0},{2,3},{3,2},{4,5},{5,4},{6,7},{7,6},{8,9},{9,8},{10,11... | collective-permute-start | bytes 393224 | tf_op jit(solution)/shard_map/ppermute | solution.py:453
  101.1 4.4 %collective-permute-start.18 = (bf16[4,128,128]{2,1,0:T(8,128)(2,1)S(1)}, bf16[4,128,128]{2,1,0:T(8,128)(2,1)S(1)}, u32[]{:S(2)}, u32[]{:S(2)}) collective-permute-start(bf16[4,128,128]{2,1,0:T(8,128)(2,1)S(1)} %collective-permute-done.17.rest_1_), channel_id=1, source_target_pairs={{0,1},{1,0},{2,3},{3,2},{4,5},{5,4},{6,7},{7,6},{8,9},{9,8},{10,11... | collective-permute-start | bytes 393224 | tf_op jit(solution)/shard_map/ppermute | solution.py:453
  101.1 4.4 %collective-permute-start.20 = (bf16[4,128,128]{2,1,0:T(8,128)(2,1)S(1)}, bf16[4,128,128]{2,1,0:T(8,128)(2,1)S(1)}, u32[]{:S(2)}, u32[]{:S(2)}) collective-permute-start(bf16[4,128,128]{2,1,0:T(8,128)(2,1)S(1)} %collective-permute-done.19.rest_2_), channel_id=1, source_target_pairs={{0,1},{1,0},{2,3},{3,2},{4,5},{5,4},{6,7},{7,6},{8,9},{9,8},{10,11... | collective-permute-start | bytes 393224 | tf_op jit(solution)/shard_map/ppermute | solution.py:453
  102.8 2.8 %collective-permute-start.22 = (bf16[4,128,128]{2,1,0:T(8,128)(2,1)S(1)}, bf16[4,128,128]{2,1,0:T(8,128)(2,1)S(1)}, u32[]{:S(2)}, u32[]{:S(2)}) collective-permute-start(bf16[4,128,128]{2,1,0:T(8,128)(2,1)S(1)} %collective-permute-done.21.rest_3_), channel_id=1, source_target_pairs={{0,1},{1,0},{2,3},{3,2},{4,5},{5,4},{6,7},{7,6},{8,9},{9,8},{10,11... | collective-permute-start | bytes 393224 | tf_op jit(solution)/shard_map/ppermute | solution.py:453

commit v12 on v10

--- a/solution.py
+++ b/solution.py
@@ -411,7 +411,7 @@
         block = at(parity)
         return pl.BlockSpec((count, step_heads * DH), lambda *a: (0, block(*a)))
 
-    whole = pl.BlockSpec((half, DH, DH), lambda *a: (0, 0, 0))
+    whole = pl.BlockSpec(memory_space=pltpu.VMEM)
     halved = pl.BlockSpec((step_heads, DH, DH), lambda i, *a: (i, 0, 0))
     untouched = pl.BlockSpec(memory_space=pl.ANY)
     token_bf = pltpu.HBM((count, width), BF16)
@@ -419,7 +419,7 @@
     owned_bf = jax.ShapeDtypeStruct((owned, DH, DH), BF16)
     half_bf = jax.ShapeDtypeStruct((half, DH, DH), BF16)
 
-    def run(kernel, grid, ins, outs, shapes, scratch, args, cost, name, params=SMALL, aliases={}):
+    def run(kernel, grid, ins, outs, shapes, scratch, args, cost, name, aliases={}, lens=None):
         flops, moved, exps = cost
         return pl.pallas_call(
             kernel,
@@ -432,22 +432,21 @@
             ),
             out_shape=shapes,
             input_output_aliases=aliases,
-            compiler_params=params,
+            compiler_params=SMALL,
             cost_estimate=pl.CostEstimate(
                 flops=flops, bytes_accessed=moved, transcendentals=exps
             ),
             name=name,
-        )(doc_lengths, place, *args)
+        )(doc_lengths if lens is None else lens, place, *args)
 
     product = 2 * half * count * DH * DH
     array = half * count * DH * 2
     all_states = pltpu.VMEM((heads, DH, DH), BF16)
     block = owned
-    single = pl.BlockSpec((block, DH, DH), lambda i, *a: (i, 0, 0))
-    grouped = pl.BlockSpec((chips, block, DH, DH), lambda i, *a: (0, i, 0, 0))
+    single = grouped = whole
     buffer = pltpu.VMEM((chips, block, DH, DH), BF16)
     combining = (4 * half * DH * DH, 4 * half * DH * DH, 0)
-    moves = owned // block
+    moves = 1
 
     def swap(state):
         return lax.ppermute(state, LAYER, [(i, i ^ 1) for i in range(members)])
@@ -474,9 +473,9 @@
             aliases={2 + chips + j: 1 + j for j in range(len(along))},
         )
         others = []
-        for s in reach:
+        for s in reversed(reach):
             pairs = [(i, i + s) if forward else (i + s, i) for i in range(layers - s)]
-            others.append(lax.ppermute(total, "z", pairs))
+            others.insert(0, lax.ppermute(total, "z", pairs))
         return came, others, total, along
 
     def spread(came, others, after, forward, name):
@@ -511,6 +510,7 @@
         (pinned[1], pinned[2], pinned[0], pinned[3]),
         tail_work,
         "tail_mate",
+        lens=held_in_hbm(doc_lengths),
     )
     (own_tail,) = run(
         tail_kernel,
@@ -522,6 +522,7 @@
         pinned[1:3],
         tail_work,
         "tail_own",
+        lens=held_in_hbm(doc_lengths),
     )
     mine = own_tail.reshape(chips, owned, DH, DH)
     other = swap(mate_tail).reshape(chips, owned, DH, DH)
@@ -568,7 +569,7 @@
     late_tail = swap(own_tail)
     chip_in = spread(came, others, (part, late_tail), True, "carried")
     few_states = pl.BlockSpec((few, DH, DH), lambda i, *a: (i, 0, 0))
-    one_owner = pl.BlockSpec((owned, DH, DH), lambda *a: (0, 0, 0))
+    one_owner = whole
     half_states = pltpu.VMEM((half, DH, DH), BF16)
     narrow_bf = jax.ShapeDtypeStruct(narrow, BF16)
     attn_half, mate_out, mine_ga, mate_ga, mine_in, mine_late, *merged = run(

time: 89.4 us -> 89 us (level)
  transfers between devices with their start and end apart: 28 -> 28, of which waited for: 13 -> 13; matrix products, arithmetic and copies ran while one was open for 0% -> 0% of each run, Pallas kernels for 21% -> 22%
where the time goes in v12:
time: 89 us; the launch traced here: 88.2 us
  Pallas kernels  31.9 us (36%)
  starting transfers between devices  27.7 us (31%)
  waiting for transfers between devices  27.6 us (31%)
  between operations  0.91 us (1%)
    pallas_call x12, Pallas kernels, run(): pl.pallas_call(kernel, grid_spec=pltpu.PrefetchScalarGridSpec(num_scalar_...  31.9 us
    ppermute x12, waiting for transfers between devices, exchange(): lax.ppermute(state, LAYER, pairs[n])  24 us
    ppermute x12, starting transfers between devices, exchange(): lax.ppermute(state, LAYER, pairs[n])  14.7 us
    ppermute x4, starting transfers between devices, reach_out(): others.insert(0, lax.ppermute(total, 'z', pairs))  10.7 us
    ppermute x4, waiting for transfers between devices, reach_out(): others.insert(0, lax.ppermute(total, 'z', pairs))  3.53 us
    ppermute x12, starting transfers between devices, swap(): return lax.ppermute(state, LAYER, [(i, i ^ 1) for i in range(members)])  2.25 us
  transfers between devices with their start and end apart: 28, of which 13 were waited for; matrix products, arithmetic and copies ran while one was open for 0% of the time, Pallas kernels for 22%

profile of v12, /device:TPU:0, one launch (start us, length us, event | category | flops | bytes accessed | tf_op | source)
XLA Modules:
  0.0 88.2 jit_solution(361246096308234011)
XLA Ops:
  0.6 0.1 pad_add_fusion.place
  0.7 3.1 %tail_mate.1 = (bf16[16,128,128]{2,1,0:T(8,128)(2,1)S(1)}, bf16[3,128,2048]{2,1,0:T(8,128)(2,1)S(1)}, bf16[128,2048]{1,0:T(8,128)(2,1)S(1)}) custom-call(s32[8]{0:T(128)} %lens.23, s32[3]{0:T(128)S(1)} %pad_add_fusion.place, bf16[128,4096]{1,0:T(8,128)(2,1)} %k.11, bf16[128,4096]{1,0:T(8,128)(2,1)} %v.11, bf16[128,4096]{1,0:T(8,128)(2,1)} %q.3, ...), custom_call_target="tpu_custom_call" | custom-call | flops 67108864 | bytes 1572864 | tf_op jit(solution)/shard_map/tail_mate/pallas_call | solution.py:424
  3.8 0.0 copy-start.4
  3.8 0.5 collective-permute-start
  4.3 2.7 %tail_own.1.rest_6_ = bf16[16,128,128]{2,1,0:T(8,128)(2,1)S(1)} custom-call(s32[8]{0:T(128)} %lens.23, s32[3]{0:T(128)S(1)} %pad_add_fusion.place, bf16[128,4096]{1,0:T(8,128)(2,1)} %k.11, bf16[128,4096]{1,0:T(8,128)(2,1)} %v.11), custom_call_target="tpu_custom_call" | custom-call | flops 67108864 | bytes 1572864 | tf_op jit(solution)/shard_map/tail_own/pallas_call | solution.py:424
  7.1 0.0 collective-permute-done.rest_2_
  7.1 0.0 copy-start
  7.1 0.0 copy-start.1
  7.1 0.0 copy-start.2
  7.1 0.8 carried_chip.1
  7.9 2.6 %collective-permute-start.1 = (bf16[4,128,128]{2,1,0:T(8,128)(2,1)S(1)}, bf16[4,128,128]{2,1,0:T(8,128)(2,1)S(1)}, u32[]{:S(2)}, u32[]{:S(2)}) collective-permute-start(bf16[4,128,128]{2,1,0:T(8,128)(2,1)S(1)} %get-tuple-element.49), channel_id=1, source_target_pairs={{0,2},{1,3},{2,0},{3,1},{4,6},{5,7},{6,4},{7,5},{8,10},{9,11},{10,... | collective-permute-start | bytes 393224 | tf_op jit(solution)/shard_map/ppermute | solution.py:457
  10.5 1.5 %collective-permute-start.2 = (bf16[4,128,128]{2,1,0:T(8,128)(2,1)S(1)}, bf16[4,128,128]{2,1,0:T(8,128)(2,1)S(1)}, u32[]{:S(2)}, u32[]{:S(2)}) collective-permute-start(bf16[4,128,128]{2,1,0:T(8,128)(2,1)S(1)} %get-tuple-element.50), channel_id=1, source_target_pairs={{0,4},{1,5},{2,6},{3,7},{4,0},{5,1},{6,2},{7,3},{8,12},{9,13},{10,... | collective-permute-start | bytes 393224 | tf_op jit(solution)/shard_map/ppermute | solution.py:457
  12.0 0.0 collective-permute-start.3
  12.0 2.6 %collective-permute-done.1.rest_1_ = bf16[4,128,128]{2,1,0:T(8,128)(2,1)S(1)} collective-permute-done((bf16[4,128,128]{2,1,0:T(8,128)(2,1)S(1)}, bf16[4,128,128]{2,1,0:T(8,128)(2,1)S(1)}, u32[]{:S(2)}, u32[]{:S(2)}) %collective-permute-start.1) | collective-permute-done | bytes 131104 | tf_op jit(solution)/shard_map/ppermute | solution.py:457
  14.6 2.2 %collective-permute-done.2.rest_2_ = bf16[4,128,128]{2,1,0:T(8,128)(2,1)S(1)} collective-permute-done((bf16[4,128,128]{2,1,0:T(8,128)(2,1)S(1)}, bf16[4,128,128]{2,1,0:T(8,128)(2,1)S(1)}, u32[]{:S(2)}, u32[]{:S(2)}) %collective-permute-start.2) | collective-permute-done | bytes 131104 | tf_op jit(solution)/shard_map/ppermute | solution.py:457
  16.8 1.9 %collective-permute-done.3.rest_3_ = bf16[4,128,128]{2,1,0:T(8,128)(2,1)S(1)} collective-permute-done((bf16[4,128,128]{2,1,0:T(8,128)(2,1)S(1)}, bf16[4,128,128]{2,1,0:T(8,128)(2,1)S(1)}, u32[]{:S(2)}, u32[]{:S(2)}) %collective-permute-start.3) | collective-permute-done | bytes 131104 | tf_op jit(solution)/shard_map/ppermute | solution.py:457
  18.7 0.7 carried_total.1
  19.4 0.1 collective-permute-start.4
  19.5 0.5 collective-permute-start.6
  20.0 0.1 collective-permute-start.5
  20.1 4.6 %collective-permute-start.8 = (bf16[4,128,128]{2,1,0:T(8,128)(2,1)S(1)}, bf16[4,128,128]{2,1,0:T(8,128)(2,1)S(1)}, u32[]{:S(2)}, u32[]{:S(2)}) collective-permute-start(bf16[4,128,128]{2,1,0:T(8,128)(2,1)S(1)} %get-tuple-element.60), channel_id=1, source_target_pairs={{0,16},{8,24},{1,17},{9,25},{2,18},{10,26},{3,19},{11,27},{4,20},{... | collective-permute-start | bytes 393224 | tf_op jit(solution)/shard_map/ppermute | solution.py:478
  24.7 3.5 %collective-permute-start.7 = (bf16[4,128,128]{2,1,0:T(8,128)(2,1)S(1)}, bf16[4,128,128]{2,1,0:T(8,128)(2,1)S(1)}, u32[]{:S(2)}, u32[]{:S(2)}) collective-permute-start(bf16[4,128,128]{2,1,0:T(8,128)(2,1)S(1)} %get-tuple-element.60), channel_id=1, source_target_pairs={{0,8},{8,16},{16,24},{1,9},{9,17},{17,25},{2,10},{10,18},{18,26},{... | collective-permute-start | bytes 393224 | tf_op jit(solution)/shard_map/ppermute | solution.py:478
  28.2 0.0 collective-permute-done.4.mate
  28.3 4.3 %within_chip.1 = (f32[256,2048]{1,0:T(8,128)S(1)}, bf16[256,2048]{1,0:T(8,128)(2,1)S(1)}, bf16[16,128,256]{2,1,0:T(8,128)(2,1)S(1)}) custom-call(s32[8]{0:T(128)S(1)} %copy-done.4, s32[3]{0:T(128)S(1)} %pad_add_fusion.place, bf16[128,4096]{1,0:T(8,128)(2,1)S(1)} %copy-done.2, bf16[128,4096]{1,0:T(8,128)(2,1)S(1)} %copy-done, ...), custom_call_target="tpu_custom_call" | custom-call | flops 671088640 | bytes 7340032 | tf_op jit(solution)/shard_map/within_chip/pallas_call | solution.py:424
  32.5 0.0 copy-start.3
  32.5 0.0 collective-permute-done.8.rest_7_
  32.6 0.0 collective-permute-done.6.rest_5_.rest_3_
  32.6 0.9 carried_prefix.1
  33.5 1.6 %collective-permute-start.9 = (bf16[4,128,128]{2,1,0:T(8,128)(2,1)S(1)}, bf16[4,128,128]{2,1,0:T(8,128)(2,1)S(1)}, u32[]{:S(2)}, u32[]{:S(2)}) collective-permute-start(bf16[4,128,128]{2,1,0:T(8,128)(2,1)S(1)} %get-tuple-element.62), channel_id=1, source_target_pairs={{0,2},{1,3},{2,0},{3,1},{4,6},{5,7},{6,4},{7,5},{8,10},{9,11},{10,... | collective-permute-start | bytes 393224 | tf_op jit(solution)/shard_map/ppermute | solution.py:457
  35.0 1.5 %collective-permute-start.10 = (bf16[4,128,128]{2,1,0:T(8,128)(2,1)S(1)}, bf16[4,128,128]{2,1,0:T(8,128)(2,1)S(1)}, u32[]{:S(2)}, u32[]{:S(2)}) collective-permute-start(bf16[4,128,128]{2,1,0:T(8,128)(2,1)S(1)} %get-tuple-element.63), channel_id=1, source_target_pairs={{0,4},{1,5},{2,6},{3,7},{4,0},{5,1},{6,2},{7,3},{8,12},{9,13},{10,... | collective-permute-start | bytes 393224 | tf_op jit(solution)/shard_map/ppermute | solution.py:457
  36.5 0.5 collective-permute-start.11
  37.0 1.8 %collective-permute-done.9.rest_1_ = bf16[4,128,128]{2,1,0:T(8,128)(2,1)S(1)} collective-permute-done((bf16[4,128,128]{2,1,0:T(8,128)(2,1)S(1)}, bf16[4,128,128]{2,1,0:T(8,128)(2,1)S(1)}, u32[]{:S(2)}, u32[]{:S(2)}) %collective-permute-start.9) | collective-permute-done | bytes 131104 | tf_op jit(solution)/shard_map/ppermute | solution.py:457
  38.8 2.6 %collective-permute-done.10.rest_2_ = bf16[4,128,128]{2,1,0:T(8,128)(2,1)S(1)} collective-permute-done((bf16[4,128,128]{2,1,0:T(8,128)(2,1)S(1)}, bf16[4,128,128]{2,1,0:T(8,128)(2,1)S(1)}, u32[]{:S(2)}, u32[]{:S(2)}) %collective-permute-start.10) | collective-permute-done | bytes 131104 | tf_op jit(solution)/shard_map/ppermute | solution.py:457
  41.4 1.3 %collective-permute-done.11.rest_3_ = bf16[4,128,128]{2,1,0:T(8,128)(2,1)S(1)} collective-permute-done((bf16[4,128,128]{2,1,0:T(8,128)(2,1)S(1)}, bf16[4,128,128]{2,1,0:T(8,128)(2,1)S(1)}, u32[]{:S(2)}, u32[]{:S(2)}) %collective-permute-start.11) | collective-permute-done | bytes 131104 | tf_op jit(solution)/shard_map/ppermute | solution.py:457
  42.8 5.3 %normed.1 = (bf16[128,4096]{1,0:T(8,128)(2,1)}, bf16[128,2048]{1,0:T(8,128)(2,1)S(1)}, bf16[128,2048]{1,0:T(8,128)(2,1)S(1)}, bf16[128,2048]{1,0:T(8,128)(2,1)S(...) custom-call(s32[8]{0:T(128)S(1)} %copy-done.4, ...), custom_call_target="tpu_custom_call" | custom-call | flops 536870912 | bytes 8388608 | tf_op jit(solution)/shard_map/normed/pallas_call | solution.py:424
  48.1 0.0 collective-permute-start.12
  48.1 0.5 collective-permute-start.13
  48.6 1.5 %collective-permute-start.14 = (bf16[4,128,128]{2,1,0:T(8,128)(2,1)S(1)}, bf16[4,128,128]{2,1,0:T(8,128)(2,1)S(1)}, u32[]{:S(2)}, u32[]{:S(2)}) collective-permute-start(bf16[4,128,128]{2,1,0:T(8,128)(2,1)S(1)} %get-tuple-element.69), channel_id=1, source_target_pairs={{0,2},{1,3},{2,0},{3,1},{4,6},{5,7},{6,4},{7,5},{8,10},{9,11},{10,... | collective-permute-start | bytes 393224 | tf_op jit(solution)/shard_map/ppermute | solution.py:457
  50.1 1.5 %collective-permute-start.15 = (bf16[4,128,128]{2,1,0:T(8,128)(2,1)S(1)}, bf16[4,128,128]{2,1,0:T(8,128)(2,1)S(1)}, u32[]{:S(2)}, u32[]{:S(2)}) collective-permute-start(bf16[4,128,128]{2,1,0:T(8,128)(2,1)S(1)} %get-tuple-element.70), channel_id=1, source_target_pairs={{0,4},{1,5},{2,6},{3,7},{4,0},{5,1},{6,2},{7,3},{8,12},{9,13},{10,... | collective-permute-start | bytes 393224 | tf_op jit(solution)/shard_map/ppermute | solution.py:457
  51.6 0.5 collective-permute-start.16
  52.1 1.9 %collective-permute-done.14.rest_1_ = bf16[4,128,128]{2,1,0:T(8,128)(2,1)S(1)} collective-permute-done((bf16[4,128,128]{2,1,0:T(8,128)(2,1)S(1)}, bf16[4,128,128]{2,1,0:T(8,128)(2,1)S(1)}, u32[]{:S(2)}, u32[]{:S(2)}) %collective-permute-start.14) | collective-permute-done | bytes 131104 | tf_op jit(solution)/shard_map/ppermute | solution.py:457
  54.0 2.5 %collective-permute-done.15.rest_2_ = bf16[4,128,128]{2,1,0:T(8,128)(2,1)S(1)} collective-permute-done((bf16[4,128,128]{2,1,0:T(8,128)(2,1)S(1)}, bf16[4,128,128]{2,1,0:T(8,128)(2,1)S(1)}, u32[]{:S(2)}, u32[]{:S(2)}) %collective-permute-start.15) | collective-permute-done | bytes 131104 | tf_op jit(solution)/shard_map/ppermute | solution.py:457
  56.5 1.5 %collective-permute-done.16.rest_3_ = bf16[4,128,128]{2,1,0:T(8,128)(2,1)S(1)} collective-permute-done((bf16[4,128,128]{2,1,0:T(8,128)(2,1)S(1)}, bf16[4,128,128]{2,1,0:T(8,128)(2,1)S(1)}, u32[]{:S(2)}, u32[]{:S(2)}) %collective-permute-start.16) | collective-permute-done | bytes 131104 | tf_op jit(solution)/shard_map/ppermute | solution.py:457
  58.0 0.7 future_total.1
  58.7 0.1 collective-permute-start.27
  58.8 0.5 collective-permute-start.17
  59.3 1.3 %collective-permute-start.19 = (bf16[4,128,128]{2,1,0:T(8,128)(2,1)S(1)}, bf16[4,128,128]{2,1,0:T(8,128)(2,1)S(1)}, u32[]{:S(2)}, u32[]{:S(2)}) collective-permute-start(bf16[4,128,128]{2,1,0:T(8,128)(2,1)S(1)} %get-tuple-element.74.rest_4_), channel_id=1, source_target_pairs={{16,0},{24,8},{17,1},{25,9},{18,2},{26,10},{19,3},{27,11},{20,4},{... | collective-permute-start | bytes 393224 | tf_op jit(solution)/shard_map/ppermute | solution.py:478
  60.6 0.0 collective-permute-done.12.other_ga
  60.6 1.3 %collective-permute-start.18 = (bf16[4,128,128]{2,1,0:T(8,128)(2,1)S(1)}, bf16[4,128,128]{2,1,0:T(8,128)(2,1)S(1)}, u32[]{:S(2)}, u32[]{:S(2)}) collective-permute-start(bf16[4,128,128]{2,1,0:T(8,128)(2,1)S(1)} %get-tuple-element.74.rest_4_), channel_id=1, source_target_pairs={{8,0},{16,8},{24,16},{9,1},{17,9},{25,17},{10,2},{18,10},{26,18},{... | collective-permute-start | bytes 393224 | tf_op jit(solution)/shard_map/ppermute | solution.py:478
  61.9 6.9 %grads_within.1 = (bf16[128,4096]{1,0:T(8,128)(2,1)}, f32[128,4096]{1,0:T(8,128)S(1)}, f32[128,4096]{1,0:T(8,128)S(1)}) custom-call(s32[8]{0:T(128)S(1)} %copy-done.4, s32[3]{0:T(128)S(1)} %pad_add_fusion.place, bf16[128,4096]{1,0:T(8,128)(2,1)S(1)} %copy-done.2, bf16[128,4096]{1,0:T(8,128)(2,1)S(1)} %copy-done, bf16[128,4096]{1,0:T(8,128)(2,1)S(1)} %copy-done.1, ...), custom_call_target="tpu_custom_call" | custom-call | flops 1073741824 | bytes 11534336 | tf_op jit(solution)/shard_map/grads_within/pallas_call | solution.py:424
  68.9 3.5 %collective-permute-done.19.rest_6_ = bf16[4,128,128]{2,1,0:T(8,128)(2,1)S(1)} collective-permute-done((bf16[4,128,128]{2,1,0:T(8,128)(2,1)S(1)}, bf16[4,128,128]{2,1,0:T(8,128)(2,1)S(1)}, u32[]{:S(2)}, u32[]{:S(2)}) %collective-permute-start.19) | collective-permute-done | bytes 131104 | tf_op jit(solution)/shard_map/ppermute | solution.py:478
  72.4 0.0 collective-permute-done.18.rest_5_
  72.4 0.9 future_prefix.1
  73.3 1.6 %collective-permute-start.21 = (bf16[4,128,128]{2,1,0:T(8,128)(2,1)S(1)}, bf16[4,128,128]{2,1,0:T(8,128)(2,1)S(1)}, u32[]{:S(2)}, u32[]{:S(2)}) collective-permute-start(bf16[4,128,128]{2,1,0:T(8,128)(2,1)S(1)} %get-tuple-element.79), channel_id=1, source_target_pairs={{0,2},{1,3},{2,0},{3,1},{4,6},{5,7},{6,4},{7,5},{8,10},{9,11},{10,... | collective-permute-start | bytes 393224 | tf_op jit(solution)/shard_map/ppermute | solution.py:457
  74.8 1.5 %collective-permute-start.23 = (bf16[4,128,128]{2,1,0:T(8,128)(2,1)S(1)}, bf16[4,128,128]{2,1,0:T(8,128)(2,1)S(1)}, u32[]{:S(2)}, u32[]{:S(2)}) collective-permute-start(bf16[4,128,128]{2,1,0:T(8,128)(2,1)S(1)} %get-tuple-element.80), channel_id=1, source_target_pairs={{0,4},{1,5},{2,6},{3,7},{4,0},{5,1},{6,2},{7,3},{8,12},{9,13},{10,... | collective-permute-start | bytes 393224 | tf_op jit(solution)/shard_map/ppermute | solution.py:457
  76.3 0.5 collective-permute-start.25
  76.8 1.9 %collective-permute-done.21.rest_1_ = bf16[4,128,128]{2,1,0:T(8,128)(2,1)S(1)} collective-permute-done((bf16[4,128,128]{2,1,0:T(8,128)(2,1)S(1)}, bf16[4,128,128]{2,1,0:T(8,128)(2,1)S(1)}, u32[]{:S(2)}, u32[]{:S(2)}) %collective-permute-start.21) | collective-permute-done | bytes 131104 | tf_op jit(solution)/shard_map/ppermute | solution.py:457
  78.8 1.6 %collective-permute-done.23.rest_2_ = bf16[4,128,128]{2,1,0:T(8,128)(2,1)S(1)} collective-permute-done((bf16[4,128,128]{2,1,0:T(8,128)(2,1)S(1)}, bf16[4,128,128]{2,1,0:T(8,128)(2,1)S(1)}, u32[]{:S(2)}, u32[]{:S(2)}) %collective-permute-start.23) | collective-permute-done | bytes 131104 | tf_op jit(solution)/shard_map/ppermute | solution.py:457
  80.4 2.1 %collective-permute-done.25.rest_3_ = bf16[4,128,128]{2,1,0:T(8,128)(2,1)S(1)} collective-permute-done((bf16[4,128,128]{2,1,0:T(8,128)(2,1)S(1)}, bf16[4,128,128]{2,1,0:T(8,128)(2,1)S(1)}, u32[]{:S(2)}, u32[]{:S(2)}) %collective-permute-start.25) | collective-permute-done | bytes 131104 | tf_op jit(solution)/shard_map/ppermute | solution.py:457
  82.5 0.0 collective-permute-start.26
  82.5 2.8 %grads_last_0.1 = (bf16[128,4096]{1,0:T(8,128)(2,1)}, bf16[128,4096]{1,0:T(8,128)(2,1)}) custom-call(s32[8]{0:T(128)S(1)} %copy-done.4, s32[3]{0:T(128)S(1)} %pad_add_fusion.place, bf16[128,4096]{1,0:T(8,128)(2,1)S(1)} %copy-done, bf16[128,4096]{1,0:T(8,128)(2,1)S(1)} %copy-done.1, f32[128,4096]{1,0:T(8,128)S(1)} %get-tuple-element.75.rest_4_.gk_part, ...), custom_call_target="tpu_custom_call" | custom-call | flops 134217728 | bytes 4718592 | tf_op jit(solution)/shard_map/grads_last_0/pallas_call | solution.py:424
  85.3 0.0 collective-permute-done.24.rest_2_
  85.3 0.0 collective-permute-done.26.rest_3_
  85.3 3.0 %grads_last_1.1 = (bf16[128,4096]{1,0:T(8,128)(2,1)}, bf16[128,4096]{1,0:T(8,128)(2,1)}, bf16[128,4096]{1,0:T(8,128)(2,1)}) custom-call(s32[8]{0:T(128)S(1)} %copy-done.4, s32[3]{0:T(128)S(1)} %pad_add_fusion.place, bf16[128,4096]{1,0:T(8,128)(2,1)S(1)} %copy-done, ...), custom_call_target="tpu_custom_call", output_to_operand_aliasing={{0}: (12, {}), {1}: (13, {}), {2}: (14, {})} | custom-call | flops 134217728 | bytes 4718592 | tf_op jit(solution)/shard_map/grads_last_1/pallas_call | solution.py:424
  (15 shorter events, 0.0 us)
Async XLA Ops:
  3.8 3.3 %copy-start.4 = (s32[8]{0:T(128)S(1)}, s32[8]{0:T(128)}, u32[]{:S(2)}) copy-start(s32[8]{0:T(128)} %lens.23) | copy-start | bytes 100
  3.8 3.2 %collective-permute-start = (bf16[16,128,128]{2,1,0:T(8,128)(2,1)S(1)}, bf16[16,128,128]{2,1,0:T(8,128)(2,1)S(1)}, u32[]{:S(2)}, u32[]{:S(2)}) collective-permute-start(bf16[16,128,128]{2,1,0:T(8,128)(2,1)S(1)} %get-tuple-element.47), channel_id=1, source_target_pairs={{0,1},{1,0},{2,3},{3,2},{4,5},{5,4},{6,7},{7,6},{8,9},{9,8},{10,11... | collective-permute-start | bytes 1572872 | tf_op jit(solution)/shard_map/ppermute | solution.py:452
  7.1 21.2 %copy-start = (bf16[128,4096]{1,0:T(8,128)(2,1)S(1)}, bf16[128,4096]{1,0:T(8,128)(2,1)}, u32[]{:S(2)}) copy-start(bf16[128,4096]{1,0:T(8,128)(2,1)} %k.11) | copy-start | bytes 3145732
  7.1 21.2 %copy-start.1 = (bf16[128,4096]{1,0:T(8,128)(2,1)S(1)}, bf16[128,4096]{1,0:T(8,128)(2,1)}, u32[]{:S(2)}) copy-start(bf16[128,4096]{1,0:T(8,128)(2,1)} %v.11) | copy-start | bytes 3145732
  7.1 21.2 %copy-start.2 = (bf16[128,4096]{1,0:T(8,128)(2,1)S(1)}, bf16[128,4096]{1,0:T(8,128)(2,1)}, u32[]{:S(2)}) copy-start(bf16[128,4096]{1,0:T(8,128)(2,1)} %q.3) | copy-start | bytes 3145732
  7.9 6.8 %collective-permute-start.1 = (bf16[4,128,128]{2,1,0:T(8,128)(2,1)S(1)}, bf16[4,128,128]{2,1,0:T(8,128)(2,1)S(1)}, u32[]{:S(2)}, u32[]{:S(2)}) collective-permute-start(bf16[4,128,128]{2,1,0:T(8,128)(2,1)S(1)} %get-tuple-element.49), channel_id=1, source_target_pairs={{0,2},{1,3},{2,0},{3,1},{4,6},{5,7},{6,4},{7,5},{8,10},{9,11},{10,... | collective-permute-start | bytes 393224 | tf_op jit(solution)/shard_map/ppermute | solution.py:457
  10.5 6.3 %collective-permute-start.2 = (bf16[4,128,128]{2,1,0:T(8,128)(2,1)S(1)}, bf16[4,128,128]{2,1,0:T(8,128)(2,1)S(1)}, u32[]{:S(2)}, u32[]{:S(2)}) collective-permute-start(bf16[4,128,128]{2,1,0:T(8,128)(2,1)S(1)} %get-tuple-element.50), channel_id=1, source_target_pairs={{0,4},{1,5},{2,6},{3,7},{4,0},{5,1},{6,2},{7,3},{8,12},{9,13},{10,... | collective-permute-start | bytes 393224 | tf_op jit(solution)/shard_map/ppermute | solution.py:457
  12.0 6.7 %collective-permute-start.3 = (bf16[4,128,128]{2,1,0:T(8,128)(2,1)S(1)}, bf16[4,128,128]{2,1,0:T(8,128)(2,1)S(1)}, u32[]{:S(2)}, u32[]{:S(2)}) collective-permute-start(bf16[4,128,128]{2,1,0:T(8,128)(2,1)S(1)} %get-tuple-element.51), channel_id=1, source_target_pairs={{0,6},{1,7},{2,4},{3,5},{4,2},{5,3},{6,0},{7,1},{8,14},{9,15},{10,... | collective-permute-start | bytes 393224 | tf_op jit(solution)/shard_map/ppermute | solution.py:457
  19.4 8.8 %collective-permute-start.4 = (bf16[3,128,2048]{2,1,0:T(8,128)(2,1)S(1)}, bf16[3,128,2048]{2,1,0:T(8,128)(2,1)S(1)}, u32[]{:S(2)}, u32[]{:S(2)}) collective-permute-start(bf16[3,128,2048]{2,1,0:T(8,128)(2,1)S(1)} %get-tuple-element.54), channel_id=1, source_target_pairs={{0,1},{1,0},{2,3},{3,2},{4,5},{5,4},{6,7},{7,6},{8,9},{9,8},{10,11... | collective-permute-start | bytes 4718600 | tf_op jit(solution)/shard_map/ppermute | solution.py:452
  19.5 13.1 %collective-permute-start.6 = (bf16[16,128,128]{2,1,0:T(8,128)(2,1)S(1)}, bf16[16,128,128]{2,1,0:T(8,128)(2,1)S(1)}, u32[]{:S(2)}, u32[]{:S(2)}) collective-permute-start(bf16[16,128,128]{2,1,0:T(8,128)(2,1)S(1)} %get-tuple-element.59), channel_id=1, source_target_pairs={{0,1},{1,0},{2,3},{3,2},{4,5},{5,4},{6,7},{7,6},{8,9},{9,8},{10,11... | collective-permute-start | bytes 1572872 | tf_op jit(solution)/shard_map/ppermute | solution.py:452
  20.0 17.0 %collective-permute-start.5 = (bf16[128,2048]{1,0:T(8,128)(2,1)S(1)}, bf16[128,2048]{1,0:T(8,128)(2,1)S(1)}, u32[]{:S(2)}, u32[]{:S(2)}) collective-permute-start(bf16[128,2048]{1,0:T(8,128)(2,1)S(1)} %get-tuple-element.57), channel_id=1, source_target_pairs={{0,1},{1,0},{2,3},{3,2},{4,5},{5,4},{6,7},{7,6},{8,9},{9,8},{10,11... | collective-permute-start | bytes 1572872 | tf_op jit(solution)/shard_map/ppermute | solution.py:452
  20.1 12.5 %collective-permute-start.8 = (bf16[4,128,128]{2,1,0:T(8,128)(2,1)S(1)}, bf16[4,128,128]{2,1,0:T(8,128)(2,1)S(1)}, u32[]{:S(2)}, u32[]{:S(2)}) collective-permute-start(bf16[4,128,128]{2,1,0:T(8,128)(2,1)S(1)} %get-tuple-element.60), channel_id=1, source_target_pairs={{0,16},{8,24},{1,17},{9,25},{2,18},{10,26},{3,19},{11,27},{4,20},{... | collective-permute-start | bytes 393224 | tf_op jit(solution)/shard_map/ppermute | solution.py:478
  24.7 7.8 %collective-permute-start.7 = (bf16[4,128,128]{2,1,0:T(8,128)(2,1)S(1)}, bf16[4,128,128]{2,1,0:T(8,128)(2,1)S(1)}, u32[]{:S(2)}, u32[]{:S(2)}) collective-permute-start(bf16[4,128,128]{2,1,0:T(8,128)(2,1)S(1)} %get-tuple-element.60), channel_id=1, source_target_pairs={{0,8},{8,16},{16,24},{1,9},{9,17},{17,25},{2,10},{10,18},{18,26},{... | collective-permute-start | bytes 393224 | tf_op jit(solution)/shard_map/ppermute | solution.py:478
  32.5 10.3 %copy-start.3 = (bf16[128,4096]{1,0:T(8,128)(2,1)S(1)}, bf16[128,4096]{1,0:T(8,128)(2,1)}, u32[]{:S(2)}) copy-start(bf16[128,4096]{1,0:T(8,128)(2,1)} %g.1) | copy-start | bytes 3145732
  33.5 5.4 %collective-permute-start.9 = (bf16[4,128,128]{2,1,0:T(8,128)(2,1)S(1)}, bf16[4,128,128]{2,1,0:T(8,128)(2,1)S(1)}, u32[]{:S(2)}, u32[]{:S(2)}) collective-permute-start(bf16[4,128,128]{2,1,0:T(8,128)(2,1)S(1)} %get-tuple-element.62), channel_id=1, source_target_pairs={{0,2},{1,3},{2,0},{3,1},{4,6},{5,7},{6,4},{7,5},{8,10},{9,11},{10,... | collective-permute-start | bytes 393224 | tf_op jit(solution)/shard_map/ppermute | solution.py:457
  35.0 6.4 %collective-permute-start.10 = (bf16[4,128,128]{2,1,0:T(8,128)(2,1)S(1)}, bf16[4,128,128]{2,1,0:T(8,128)(2,1)S(1)}, u32[]{:S(2)}, u32[]{:S(2)}) collective-permute-start(bf16[4,128,128]{2,1,0:T(8,128)(2,1)S(1)} %get-tuple-element.63), channel_id=1, source_target_pairs={{0,4},{1,5},{2,6},{3,7},{4,0},{5,1},{6,2},{7,3},{8,12},{9,13},{10,... | collective-permute-start | bytes 393224 | tf_op jit(solution)/shard_map/ppermute | solution.py:457
  36.5 6.3 %collective-permute-start.11 = (bf16[4,128,128]{2,1,0:T(8,128)(2,1)S(1)}, bf16[4,128,128]{2,1,0:T(8,128)(2,1)S(1)}, u32[]{:S(2)}, u32[]{:S(2)}) collective-permute-start(bf16[4,128,128]{2,1,0:T(8,128)(2,1)S(1)} %get-tuple-element.64), channel_id=1, source_target_pairs={{0,6},{1,7},{2,4},{3,5},{4,2},{5,3},{6,0},{7,1},{8,14},{9,15},{10,... | collective-permute-start | bytes 393224 | tf_op jit(solution)/shard_map/ppermute | solution.py:457
  48.1 12.5 %collective-permute-start.12 = (bf16[128,2048]{1,0:T(8,128)(2,1)S(1)}, bf16[128,2048]{1,0:T(8,128)(2,1)S(1)}, u32[]{:S(2)}, u32[]{:S(2)}) collective-permute-start(bf16[128,2048]{1,0:T(8,128)(2,1)S(1)} %get-tuple-element.66), channel_id=1, source_target_pairs={{0,1},{1,0},{2,3},{3,2},{4,5},{5,4},{6,7},{7,6},{8,9},{9,8},{10,11... | collective-permute-start | bytes 1572872 | tf_op jit(solution)/shard_map/ppermute | solution.py:452
  48.1 13.8 %collective-permute-start.13 = (bf16[16,128,128]{2,1,0:T(8,128)(2,1)S(1)}, bf16[16,128,128]{2,1,0:T(8,128)(2,1)S(1)}, u32[]{:S(2)}, u32[]{:S(2)}) collective-permute-start(bf16[16,128,128]{2,1,0:T(8,128)(2,1)S(1)} %get-tuple-element.67.rest_0_), channel_id=1, source_target_pairs={{0,1},{1,0},{2,3},{3,2},{4,5},{5,4},{6,7},{7,6},{8,9},{9,8},{10,11... | collective-permute-start | bytes 1572872 | tf_op jit(solution)/shard_map/ppermute | solution.py:452
  48.6 5.4 %collective-permute-start.14 = (bf16[4,128,128]{2,1,0:T(8,128)(2,1)S(1)}, bf16[4,128,128]{2,1,0:T(8,128)(2,1)S(1)}, u32[]{:S(2)}, u32[]{:S(2)}) collective-permute-start(bf16[4,128,128]{2,1,0:T(8,128)(2,1)S(1)} %get-tuple-element.69), channel_id=1, source_target_pairs={{0,2},{1,3},{2,0},{3,1},{4,6},{5,7},{6,4},{7,5},{8,10},{9,11},{10,... | collective-permute-start | bytes 393224 | tf_op jit(solution)/shard_map/ppermute | solution.py:457
  50.1 6.4 %collective-permute-start.15 = (bf16[4,128,128]{2,1,0:T(8,128)(2,1)S(1)}, bf16[4,128,128]{2,1,0:T(8,128)(2,1)S(1)}, u32[]{:S(2)}, u32[]{:S(2)}) collective-permute-start(bf16[4,128,128]{2,1,0:T(8,128)(2,1)S(1)} %get-tuple-element.70), channel_id=1, source_target_pairs={{0,4},{1,5},{2,6},{3,7},{4,0},{5,1},{6,2},{7,3},{8,12},{9,13},{10,... | collective-permute-start | bytes 393224 | tf_op jit(solution)/shard_map/ppermute | solution.py:457
  51.6 6.4 %collective-permute-start.16 = (bf16[4,128,128]{2,1,0:T(8,128)(2,1)S(1)}, bf16[4,128,128]{2,1,0:T(8,128)(2,1)S(1)}, u32[]{:S(2)}, u32[]{:S(2)}) collective-permute-start(bf16[4,128,128]{2,1,0:T(8,128)(2,1)S(1)} %get-tuple-element.71), channel_id=1, source_target_pairs={{0,6},{1,7},{2,4},{3,5},{4,2},{5,3},{6,0},{7,1},{8,14},{9,15},{10,... | collective-permute-start | bytes 393224 | tf_op jit(solution)/shard_map/ppermute | solution.py:457
  58.7 18.1 %collective-permute-start.27 = (bf16[128,2048]{1,0:T(8,128)(2,1)S(1)}, bf16[128,2048]{1,0:T(8,128)(2,1)S(1)}, u32[]{:S(2)}, u32[]{:S(2)}) collective-permute-start(bf16[128,2048]{1,0:T(8,128)(2,1)S(1)} %get-tuple-element.82), channel_id=1, source_target_pairs={{0,1},{1,0},{2,3},{3,2},{4,5},{5,4},{6,7},{7,6},{8,9},{9,8},{10,11... | collective-permute-start | bytes 1572872 | tf_op jit(solution)/shard_map/ppermute | solution.py:452
  58.8 26.4 %collective-permute-start.17 = (bf16[16,128,128]{2,1,0:T(8,128)(2,1)S(1)}, bf16[16,128,128]{2,1,0:T(8,128)(2,1)S(1)}, u32[]{:S(2)}, u32[]{:S(2)}) collective-permute-start(bf16[16,128,128]{2,1,0:T(8,128)(2,1)S(1)} %get-tuple-element.77.late), channel_id=1, source_target_pairs={{0,1},{1,0},{2,3},{3,2},{4,5},{5,4},{6,7},{7,6},{8,9},{9,8},{10,11... | collective-permute-start | bytes 1572872 | tf_op jit(solution)/shard_map/ppermute | solution.py:452
  59.3 13.1 %collective-permute-start.19 = (bf16[4,128,128]{2,1,0:T(8,128)(2,1)S(1)}, bf16[4,128,128]{2,1,0:T(8,128)(2,1)S(1)}, u32[]{:S(2)}, u32[]{:S(2)}) collective-permute-start(bf16[4,128,128]{2,1,0:T(8,128)(2,1)S(1)} %get-tuple-element.74.rest_4_), channel_id=1, source_target_pairs={{16,0},{24,8},{17,1},{25,9},{18,2},{26,10},{19,3},{27,11},{20,4},{... | collective-permute-start | bytes 393224 | tf_op jit(solution)/shard_map/ppermute | solution.py:478
  60.6 11.8 %collective-permute-start.18 = (bf16[4,128,128]{2,1,0:T(8,128)(2,1)S(1)}, bf16[4,128,128]{2,1,0:T(8,128)(2,1)S(1)}, u32[]{:S(2)}, u32[]{:S(2)}) collective-permute-start(bf16[4,128,128]{2,1,0:T(8,128)(2,1)S(1)} %get-tuple-element.74.rest_4_), channel_id=1, source_target_pairs={{8,0},{16,8},{24,16},{9,1},{17,9},{25,17},{10,2},{18,10},{26,18},{... | collective-permute-start | bytes 393224 | tf_op jit(solution)/shard_map/ppermute | solution.py:478
  73.3 5.5 %collective-permute-start.21 = (bf16[4,128,128]{2,1,0:T(8,128)(2,1)S(1)}, bf16[4,128,128]{2,1,0:T(8,128)(2,1)S(1)}, u32[]{:S(2)}, u32[]{:S(2)}) collective-permute-start(bf16[4,128,128]{2,1,0:T(8,128)(2,1)S(1)} %get-tuple-element.79), channel_id=1, source_target_pairs={{0,2},{1,3},{2,0},{3,1},{4,6},{5,7},{6,4},{7,5},{8,10},{9,11},{10,... | collective-permute-start | bytes 393224 | tf_op jit(solution)/shard_map/ppermute | solution.py:457
  74.8 5.5 %collective-permute-start.23 = (bf16[4,128,128]{2,1,0:T(8,128)(2,1)S(1)}, bf16[4,128,128]{2,1,0:T(8,128)(2,1)S(1)}, u32[]{:S(2)}, u32[]{:S(2)}) collective-permute-start(bf16[4,128,128]{2,1,0:T(8,128)(2,1)S(1)} %get-tuple-element.80), channel_id=1, source_target_pairs={{0,4},{1,5},{2,6},{3,7},{4,0},{5,1},{6,2},{7,3},{8,12},{9,13},{10,... | collective-permute-start | bytes 393224 | tf_op jit(solution)/shard_map/ppermute | solution.py:457
  76.3 6.1 %collective-permute-start.25 = (bf16[4,128,128]{2,1,0:T(8,128)(2,1)S(1)}, bf16[4,128,128]{2,1,0:T(8,128)(2,1)S(1)}, u32[]{:S(2)}, u32[]{:S(2)}) collective-permute-start(bf16[4,128,128]{2,1,0:T(8,128)(2,1)S(1)} %get-tuple-element.81), channel_id=1, source_target_pairs={{0,6},{1,7},{2,4},{3,5},{4,2},{5,3},{6,0},{7,1},{8,14},{9,15},{10,... | collective-permute-start | bytes 393224 | tf_op jit(solution)/shard_map/ppermute | solution.py:457
  76.8 8.4 %collective-permute-start.20 = (bf16[4,128,128]{2,1,0:T(8,128)(2,1)S(1)}, bf16[4,128,128]{2,1,0:T(8,128)(2,1)S(1)}, u32[]{:S(2)}, u32[]{:S(2)}) collective-permute-start(bf16[4,128,128]{2,1,0:T(8,128)(2,1)S(1)} %get-tuple-element.78.rest_0_), channel_id=1, source_target_pairs={{0,1},{1,0},{2,3},{3,2},{4,5},{5,4},{6,7},{7,6},{8,9},{9,8},{10,11... | collective-permute-start | bytes 393224 | tf_op jit(solution)/shard_map/ppermute | solution.py:452
  78.8 6.5 %collective-permute-start.22 = (bf16[4,128,128]{2,1,0:T(8,128)(2,1)S(1)}, bf16[4,128,128]{2,1,0:T(8,128)(2,1)S(1)}, u32[]{:S(2)}, u32[]{:S(2)}) collective-permute-start(bf16[4,128,128]{2,1,0:T(8,128)(2,1)S(1)} %collective-permute-done.21.rest_1_), channel_id=1, source_target_pairs={{0,1},{1,0},{2,3},{3,2},{4,5},{5,4},{6,7},{7,6},{8,9},{9,8},{10,11... | collective-permute-start | bytes 393224 | tf_op jit(solution)/shard_map/ppermute | solution.py:452
  80.4 4.9 %collective-permute-start.24 = (bf16[4,128,128]{2,1,0:T(8,128)(2,1)S(1)}, bf16[4,128,128]{2,1,0:T(8,128)(2,1)S(1)}, u32[]{:S(2)}, u32[]{:S(2)}) collective-permute-start(bf16[4,128,128]{2,1,0:T(8,128)(2,1)S(1)} %collective-permute-done.23.rest_2_), channel_id=1, source_target_pairs={{0,1},{1,0},{2,3},{3,2},{4,5},{5,4},{6,7},{7,6},{8,9},{9,8},{10,11... | collective-permute-start | bytes 393224 | tf_op jit(solution)/shard_map/ppermute | solution.py:452
  82.5 2.8 %collective-permute-start.26 = (bf16[4,128,128]{2,1,0:T(8,128)(2,1)S(1)}, bf16[4,128,128]{2,1,0:T(8,128)(2,1)S(1)}, u32[]{:S(2)}, u32[]{:S(2)}) collective-permute-start(bf16[4,128,128]{2,1,0:T(8,128)(2,1)S(1)} %collective-permute-done.25.rest_3_), channel_id=1, source_target_pairs={{0,1},{1,0},{2,3},{3,2},{4,5},{5,4},{6,7},{7,6},{8,9},{9,8},{10,11... | collective-permute-start | bytes 393224 | tf_op jit(solution)/shard_map/ppermute | solution.py:452

commit v13 on v12

--- a/solution.py
+++ b/solution.py
@@ -159,12 +159,12 @@
 
 def norm_kernel(lens, place, head_fq, turned, g, mate_g, part, *rest):
     kept = rest[-1]
-    chips = (len(rest) - 7) // 2
-    incoming, (out, mate_out, ga_out, mate_ga, came, lates) = (
+    chips = (len(rest) - 9) // 2
+    incoming, (out, mate_out, ga_out, mate_ga, came, lates, sent_in, sent_late) = (
         rest[:chips],
-        rest[chips : chips + 6],
-    )
-    states = rest[chips + 6 : -1]
+        rest[chips : chips + 8],
+    )
+    states = rest[chips + 8 : -1]
     count = g.shape[0]
     _, _, head, late = pair_docs(lens, place, count)
     heads = turned.shape[0]
@@ -176,6 +176,7 @@
         for n, state in enumerate(incoming):
             owned = state.shape[0]
             came[pl.ds((chip ^ n) * owned, owned)] = state[...]
+            sent_in[pl.ds((chip ^ n) * owned, owned)] = state[...]
 
     weights = jnp.full((2 * DH, DH), 1.0 / DH, BF16)
     for hs in bunches(heads, 4):
@@ -206,6 +207,7 @@
             ga_out[:, cols(h)], mate_ga[:, cols(h)] = ga[:count], ga[count:]
             kept[step * heads + h] = value[:DH]
             lates[h] = value[DH:]
+            sent_late[h] = value[DH:]
 
     @pl.when(step == pl.num_programs(0) - 1)
     def _():
@@ -215,7 +217,7 @@
 
 
 def inner_kernel(lens, place, q, k, v, mine_ga, other_ga, *rest):
-    passed, earlier, (gq, gk, gv, came) = rest[:2], rest[2:4], rest[5:]
+    passed, earlier, (gq, gk, gv, _, _, came) = rest[:2], rest[2:4], rest[7:]
     count = q.shape[0]
     heads = q.shape[1] // DH
     step = pl.program_id(0)
@@ -312,7 +314,8 @@
     return core, [doc_at(ends, mark) for mark in marks]
 
 
-def merge_kernel(count, lens, place, mine, other, *outs):
+def merge_kernel(count, lens, place, mine, other, _, *outs):
+    outs = outs[:-1]
     core, (early_b, early_e, late_b, late_e) = chip_docs(lens, place, count)
     far = same(early_e, late_e)
     mine_by = jnp.where(core == 0, far, 1.0)
@@ -526,20 +529,19 @@
     )
     mine = own_tail.reshape(chips, owned, DH, DH)
     other = swap(mate_tail).reshape(chips, owned, DH, DH)
-    merged = run(
+    *merged, mate_three = run(
         functools.partial(merge_kernel, count),
         moves,
-        [grouped] * 2,
-        [single] * chips,
-        [owned_bf] * chips,
+        [grouped] * 2 + [untouched],
+        [single] * chips + [untouched],
+        [owned_bf] * chips + copies[:1],
         [],
-        (mine, other),
+        (mine, other, mate_three),
         combining,
         "carried_chip",
-    )
-    came, others, _, (mate_three, mate_g, own_tail) = reach_out(
-        merged, (mate_three, mate_g, own_tail), True, "carried"
-    )
+        aliases={4: chips},
+    )
+    came, others, _, (mate_g, own_tail) = reach_out(merged, (mate_g, own_tail), True, "carried")
     mate_three, mate_g = swap(mate_three), swap(mate_g)
     few = 4 if half % 4 == 0 else 1
     parts = half // few
@@ -572,33 +574,36 @@
     one_owner = whole
     half_states = pltpu.VMEM((half, DH, DH), BF16)
     narrow_bf = jax.ShapeDtypeStruct(narrow, BF16)
-    attn_half, mate_out, mine_ga, mate_ga, mine_in, mine_late, *merged = run(
+    attn_half, mate_out, mine_ga, mate_ga, mine_in, mine_late, sent_in, sent_late, *merged = run(
         norm_kernel,
         parts,
         [pair_tokens, turns, own_tokens, lane_few, pair_tokens] + [one_owner] * chips,
-        [own_tokens] + [lane_few] * 3 + [whole, few_states] + [one_owner] * chips,
-        [token_bf] + [narrow_bf] * 3 + [half_bf] * 2 + [owned_bf] * chips,
+        [own_tokens]
+        + [lane_few] * 3
+        + [whole, few_states, whole, few_states]
+        + [one_owner] * chips,
+        [token_bf] + [narrow_bf] * 3 + [half_bf] * 4 + [owned_bf] * chips,
         [half_states],
         (head_fq, turned, out_grad, mate_g, part, *chip_in),
         (8 * product, 16 * array, 2 * half * count * DH),
         "normed",
     )
-    came, others, total, (mate_out, mine_late) = reach_out(
-        merged, (mate_out, mine_late), False, "future"
-    )
-    other_ga, other_in = swap(mate_ga), swap(mine_in)
+    came, others, total, (mate_ga, sent_in) = reach_out(
+        merged, (mate_ga, sent_in), False, "future"
+    )
+    other_ga, other_in = swap(mate_ga), swap(sent_in)
     other_ga = swap(mate_ga)
     def both(i, lens, place):
         return ((place[2] & 1) ^ (i // steps)) * steps + i % steps
 
     spans = pl.BlockSpec((count, step_heads * DH), lambda *a: (0, both(*a)))
     lanes = pl.BlockSpec((count, step_heads * DH), lambda i, *a: (0, i % steps))
-    grad_queries, gk_part, gv_part = run(
+    grad_queries, gk_part, gv_part, mate_out, sent_late = run(
         inner_kernel,
         2 * steps,
-        [spans] * 3 + [lanes] * 2 + [whole] * 4 + [untouched],
-        [spans] * 3,
-        [token_bf, token_f32, token_f32],
+        [spans] * 3 + [lanes] * 2 + [whole] * 4 + [untouched] * 3,
+        [spans] * 3 + [untouched] * 2,
+        [token_bf, token_f32, token_f32, narrow_bf, half_bf],
         [all_states],
         (
             queries,
@@ -611,11 +616,14 @@
             other.reshape(half, DH, DH),
             late_tail,
             total,
+            mate_out,
+            sent_late,
         ),
         (16 * product, 22 * array, 4 * half * count * DH),
         "grads_within",
-    )
-    late = (mine_late, swap(mine_late))
+        aliases={12: 3, 13: 4},
+    )
+    late = (mine_late, swap(sent_late))
     chip_out = spread(came, others, (gk_part,), False, "future")
     outgoing = (chip_out, [swap(state) for state in chip_out])
     def last(parity, extra_ins, extra_outs, shapes, args, aliases):

time: 89 us -> 87.6 us (0.984)
  waiting for transfers between devices: 27.6 us -> 24.7 us
  starting transfers between devices: 27.7 us -> 29.1 us
    ppermute x12, waiting for transfers between devices: 24 us -> 21.6 us  [exchange(): lax.ppermute(state, LAYER, pairs[n])]
    ppermute x12, starting transfers between devices: 2.25 us -> 3.31 us  [swap(): return lax.ppermute(state, LAYER, [(i, i ^ 1) for i in range(members)])]
  transfers between devices with their start and end apart: 28 -> 28, of which waited for: 13 -> 11; matrix products, arithmetic and copies ran while one was open for 0% -> 0% of each run, Pallas kernels for 22% -> 22%
where the time goes in v13:
time: 87.6 us; the launch traced here: 86.8 us
  Pallas kernels  32 us (37%)
  starting transfers between devices  29.1 us (33%)
  waiting for transfers between devices  24.7 us (28%)
  between operations  0.91 us (1%)
    pallas_call x12, Pallas kernels, run(): pl.pallas_call(kernel, grid_spec=pltpu.PrefetchScalarGridSpec(num_scalar_...  32 us
    ppermute x12, waiting for transfers between devices, exchange(): lax.ppermute(state, LAYER, pairs[n])  21.6 us
    ppermute x12, starting transfers between devices, exchange(): lax.ppermute(state, LAYER, pairs[n])  15.1 us
    ppermute x4, starting transfers between devices, reach_out(): others.insert(0, lax.ppermute(total, 'z', pairs))  10.7 us
    ppermute x12, starting transfers between devices, swap(): return lax.ppermute(state, LAYER, [(i, i ^ 1) for i in range(members)])  3.31 us
    ppermute x4, waiting for transfers between devices, reach_out(): others.insert(0, lax.ppermute(total, 'z', pairs))  3.13 us
  transfers between devices with their start and end apart: 28, of which 11 were waited for; matrix products, arithmetic and copies ran while one was open for 0% of the time, Pallas kernels for 22%

profile of v13, /device:TPU:0, one launch (start us, length us, event | category | flops | bytes accessed | tf_op | source)
XLA Modules:
  0.0 86.8 jit_solution(6360943191019875306)
XLA Ops:
  0.6 0.1 pad_add_fusion.place
  0.7 3.1 %tail_mate.1 = (bf16[16,128,128]{2,1,0:T(8,128)(2,1)S(1)}, bf16[3,128,2048]{2,1,0:T(8,128)(2,1)S(1)}, bf16[128,2048]{1,0:T(8,128)(2,1)S(1)}) custom-call(s32[8]{0:T(128)} %lens.23, s32[3]{0:T(128)S(1)} %pad_add_fusion.place, bf16[128,4096]{1,0:T(8,128)(2,1)} %k.11, bf16[128,4096]{1,0:T(8,128)(2,1)} %v.11, bf16[128,4096]{1,0:T(8,128)(2,1)} %q.3, ...), custom_call_target="tpu_custom_call" | custom-call | flops 67108864 | bytes 1572864 | tf_op jit(solution)/shard_map/tail_mate/pallas_call | solution.py:427
  3.8 0.0 copy-start.4
  3.8 0.5 collective-permute-start
  4.3 2.7 %tail_own.1.rest_5_ = bf16[16,128,128]{2,1,0:T(8,128)(2,1)S(1)} custom-call(s32[8]{0:T(128)} %lens.23, s32[3]{0:T(128)S(1)} %pad_add_fusion.place, bf16[128,4096]{1,0:T(8,128)(2,1)} %k.11, bf16[128,4096]{1,0:T(8,128)(2,1)} %v.11), custom_call_target="tpu_custom_call" | custom-call | flops 67108864 | bytes 1572864 | tf_op jit(solution)/shard_map/tail_own/pallas_call | solution.py:427
  7.1 0.0 copy-start
  7.1 0.0 copy-start.1
  7.1 0.0 copy-start.2
  7.1 0.8 carried_chip.1
  7.9 0.1 collective-permute-start.1
  8.0 3.0 %collective-permute-start.2 = (bf16[4,128,128]{2,1,0:T(8,128)(2,1)S(1)}, bf16[4,128,128]{2,1,0:T(8,128)(2,1)S(1)}, u32[]{:S(2)}, u32[]{:S(2)}) collective-permute-start(bf16[4,128,128]{2,1,0:T(8,128)(2,1)S(1)} %get-tuple-element.57), channel_id=1, source_target_pairs={{0,2},{1,3},{2,0},{3,1},{4,6},{5,7},{6,4},{7,5},{8,10},{9,11},{10,... | collective-permute-start | bytes 393224 | tf_op jit(solution)/shard_map/ppermute | solution.py:460
  11.0 1.5 %collective-permute-start.3 = (bf16[4,128,128]{2,1,0:T(8,128)(2,1)S(1)}, bf16[4,128,128]{2,1,0:T(8,128)(2,1)S(1)}, u32[]{:S(2)}, u32[]{:S(2)}) collective-permute-start(bf16[4,128,128]{2,1,0:T(8,128)(2,1)S(1)} %get-tuple-element.58), channel_id=1, source_target_pairs={{0,4},{1,5},{2,6},{3,7},{4,0},{5,1},{6,2},{7,3},{8,12},{9,13},{10,... | collective-permute-start | bytes 393224 | tf_op jit(solution)/shard_map/ppermute | solution.py:460
  12.5 2.2 %collective-permute-done.2.rest_1_ = bf16[4,128,128]{2,1,0:T(8,128)(2,1)S(1)} collective-permute-done((bf16[4,128,128]{2,1,0:T(8,128)(2,1)S(1)}, bf16[4,128,128]{2,1,0:T(8,128)(2,1)S(1)}, u32[]{:S(2)}, u32[]{:S(2)}) %collective-permute-start.2) | collective-permute-done | bytes 131104 | tf_op jit(solution)/shard_map/ppermute | solution.py:460
  14.7 2.7 %collective-permute-done.3.rest_2_ = bf16[4,128,128]{2,1,0:T(8,128)(2,1)S(1)} collective-permute-done((bf16[4,128,128]{2,1,0:T(8,128)(2,1)S(1)}, bf16[4,128,128]{2,1,0:T(8,128)(2,1)S(1)}, u32[]{:S(2)}, u32[]{:S(2)}) %collective-permute-start.3) | collective-permute-done | bytes 131104 | tf_op jit(solution)/shard_map/ppermute | solution.py:460
  17.4 1.4 %collective-permute-done.4.rest_3_ = bf16[4,128,128]{2,1,0:T(8,128)(2,1)S(1)} collective-permute-done((bf16[4,128,128]{2,1,0:T(8,128)(2,1)S(1)}, bf16[4,128,128]{2,1,0:T(8,128)(2,1)S(1)}, u32[]{:S(2)}, u32[]{:S(2)}) %collective-permute-start.4) | collective-permute-done | bytes 131104 | tf_op jit(solution)/shard_map/ppermute | solution.py:460
  18.8 0.7 carried_total.1
  19.5 0.1 collective-permute-start.6
  19.6 0.5 collective-permute-start.5
  20.1 4.6 %collective-permute-start.8 = (bf16[4,128,128]{2,1,0:T(8,128)(2,1)S(1)}, bf16[4,128,128]{2,1,0:T(8,128)(2,1)S(1)}, u32[]{:S(2)}, u32[]{:S(2)}) collective-permute-start(bf16[4,128,128]{2,1,0:T(8,128)(2,1)S(1)} %get-tuple-element.64), channel_id=1, source_target_pairs={{0,16},{8,24},{1,17},{9,25},{2,18},{10,26},{3,19},{11,27},{4,20},{... | collective-permute-start | bytes 393224 | tf_op jit(solution)/shard_map/ppermute | solution.py:481
  24.7 3.5 %collective-permute-start.7 = (bf16[4,128,128]{2,1,0:T(8,128)(2,1)S(1)}, bf16[4,128,128]{2,1,0:T(8,128)(2,1)S(1)}, u32[]{:S(2)}, u32[]{:S(2)}) collective-permute-start(bf16[4,128,128]{2,1,0:T(8,128)(2,1)S(1)} %get-tuple-element.64), channel_id=1, source_target_pairs={{0,8},{8,16},{16,24},{1,9},{9,17},{17,25},{2,10},{10,18},{18,26},{... | collective-permute-start | bytes 393224 | tf_op jit(solution)/shard_map/ppermute | solution.py:481
  28.3 4.3 %within_chip.1 = (f32[256,2048]{1,0:T(8,128)S(1)}, bf16[256,2048]{1,0:T(8,128)(2,1)S(1)}, bf16[16,128,256]{2,1,0:T(8,128)(2,1)S(1)}) custom-call(s32[8]{0:T(128)S(1)} %copy-done.4, s32[3]{0:T(128)S(1)} %pad_add_fusion.place, bf16[128,4096]{1,0:T(8,128)(2,1)S(1)} %copy-done.2, bf16[128,4096]{1,0:T(8,128)(2,1)S(1)} %copy-done, ...), custom_call_target="tpu_custom_call" | custom-call | flops 671088640 | bytes 7340032 | tf_op jit(solution)/shard_map/within_chip/pallas_call | solution.py:427
  32.5 0.0 copy-start.3
  32.6 0.0 collective-permute-done.7.rest_6_
  32.6 0.0 collective-permute-done.6.rest_5_.rest_3_
  32.6 0.9 carried_prefix.1
  33.5 1.6 %collective-permute-start.9 = (bf16[4,128,128]{2,1,0:T(8,128)(2,1)S(1)}, bf16[4,128,128]{2,1,0:T(8,128)(2,1)S(1)}, u32[]{:S(2)}, u32[]{:S(2)}) collective-permute-start(bf16[4,128,128]{2,1,0:T(8,128)(2,1)S(1)} %get-tuple-element.66), channel_id=1, source_target_pairs={{0,2},{1,3},{2,0},{3,1},{4,6},{5,7},{6,4},{7,5},{8,10},{9,11},{10,... | collective-permute-start | bytes 393224 | tf_op jit(solution)/shard_map/ppermute | solution.py:460
  35.0 1.5 %collective-permute-start.10 = (bf16[4,128,128]{2,1,0:T(8,128)(2,1)S(1)}, bf16[4,128,128]{2,1,0:T(8,128)(2,1)S(1)}, u32[]{:S(2)}, u32[]{:S(2)}) collective-permute-start(bf16[4,128,128]{2,1,0:T(8,128)(2,1)S(1)} %get-tuple-element.67), channel_id=1, source_target_pairs={{0,4},{1,5},{2,6},{3,7},{4,0},{5,1},{6,2},{7,3},{8,12},{9,13},{10,... | collective-permute-start | bytes 393224 | tf_op jit(solution)/shard_map/ppermute | solution.py:460
  36.5 0.5 collective-permute-start.11
  37.0 0.0 collective-permute-done.5.mate_g
  37.0 1.5 %collective-permute-done.9.rest_1_ = bf16[4,128,128]{2,1,0:T(8,128)(2,1)S(1)} collective-permute-done((bf16[4,128,128]{2,1,0:T(8,128)(2,1)S(1)}, bf16[4,128,128]{2,1,0:T(8,128)(2,1)S(1)}, u32[]{:S(2)}, u32[]{:S(2)}) %collective-permute-start.9) | collective-permute-done | bytes 131104 | tf_op jit(solution)/shard_map/ppermute | solution.py:460
  38.5 2.6 %collective-permute-done.10.rest_2_ = bf16[4,128,128]{2,1,0:T(8,128)(2,1)S(1)} collective-permute-done((bf16[4,128,128]{2,1,0:T(8,128)(2,1)S(1)}, bf16[4,128,128]{2,1,0:T(8,128)(2,1)S(1)}, u32[]{:S(2)}, u32[]{:S(2)}) %collective-permute-start.10) | collective-permute-done | bytes 131104 | tf_op jit(solution)/shard_map/ppermute | solution.py:460
  41.1 1.7 %collective-permute-done.11.rest_3_ = bf16[4,128,128]{2,1,0:T(8,128)(2,1)S(1)} collective-permute-done((bf16[4,128,128]{2,1,0:T(8,128)(2,1)S(1)}, bf16[4,128,128]{2,1,0:T(8,128)(2,1)S(1)}, u32[]{:S(2)}, u32[]{:S(2)}) %collective-permute-start.11) | collective-permute-done | bytes 131104 | tf_op jit(solution)/shard_map/ppermute | solution.py:460
  42.8 5.4 %normed.1 = (bf16[128,4096]{1,0:T(8,128)(2,1)}, bf16[128,2048]{1,0:T(8,128)(2,1)S(1)}, bf16[128,2048]{1,0:T(8,128)(2,1)S(1)}, bf16[128,2048]{1,0:T(8,128)(2,1)S(...) custom-call(s32[8]{0:T(128)S(1)} %copy-done.4, ...), custom_call_target="tpu_custom_call" | custom-call | flops 536870912 | bytes 8388608 | tf_op jit(solution)/shard_map/normed/pallas_call | solution.py:427
  48.2 1.2 %collective-permute-start.12 = (bf16[4,128,128]{2,1,0:T(8,128)(2,1)S(1)}, bf16[4,128,128]{2,1,0:T(8,128)(2,1)S(1)}, u32[]{:S(2)}, u32[]{:S(2)}) collective-permute-start(bf16[4,128,128]{2,1,0:T(8,128)(2,1)S(1)} %get-tuple-element.71), channel_id=1, source_target_pairs={{0,2},{1,3},{2,0},{3,1},{4,6},{5,7},{6,4},{7,5},{8,10},{9,11},{10,... | collective-permute-start | bytes 393224 | tf_op jit(solution)/shard_map/ppermute | solution.py:460
  49.4 1.5 %collective-permute-start.13 = (bf16[4,128,128]{2,1,0:T(8,128)(2,1)S(1)}, bf16[4,128,128]{2,1,0:T(8,128)(2,1)S(1)}, u32[]{:S(2)}, u32[]{:S(2)}) collective-permute-start(bf16[4,128,128]{2,1,0:T(8,128)(2,1)S(1)} %get-tuple-element.72), channel_id=1, source_target_pairs={{0,4},{1,5},{2,6},{3,7},{4,0},{5,1},{6,2},{7,3},{8,12},{9,13},{10,... | collective-permute-start | bytes 393224 | tf_op jit(solution)/shard_map/ppermute | solution.py:460
  50.9 0.8 collective-permute-start.14
  51.7 2.9 %collective-permute-done.12.rest_1_ = bf16[4,128,128]{2,1,0:T(8,128)(2,1)S(1)} collective-permute-done((bf16[4,128,128]{2,1,0:T(8,128)(2,1)S(1)}, bf16[4,128,128]{2,1,0:T(8,128)(2,1)S(1)}, u32[]{:S(2)}, u32[]{:S(2)}) %collective-permute-start.12) | collective-permute-done | bytes 131104 | tf_op jit(solution)/shard_map/ppermute | solution.py:460
  54.5 0.0 collective-permute-done.13.rest_2_
  54.5 2.2 %collective-permute-done.14.rest_3_ = bf16[4,128,128]{2,1,0:T(8,128)(2,1)S(1)} collective-permute-done((bf16[4,128,128]{2,1,0:T(8,128)(2,1)S(1)}, bf16[4,128,128]{2,1,0:T(8,128)(2,1)S(1)}, u32[]{:S(2)}, u32[]{:S(2)}) %collective-permute-start.14) | collective-permute-done | bytes 131104 | tf_op jit(solution)/shard_map/ppermute | solution.py:460
  56.7 0.7 future_total.1
  57.4 0.1 collective-permute-start.15
  57.5 0.5 collective-permute-start.16
  58.0 1.3 %collective-permute-start.19 = (bf16[4,128,128]{2,1,0:T(8,128)(2,1)S(1)}, bf16[4,128,128]{2,1,0:T(8,128)(2,1)S(1)}, u32[]{:S(2)}, u32[]{:S(2)}) collective-permute-start(bf16[4,128,128]{2,1,0:T(8,128)(2,1)S(1)} %get-tuple-element.79.rest_4_), channel_id=1, source_target_pairs={{16,0},{24,8},{17,1},{25,9},{18,2},{26,10},{19,3},{27,11},{20,4},{... | collective-permute-start | bytes 393224 | tf_op jit(solution)/shard_map/ppermute | solution.py:481
  59.3 1.3 %collective-permute-start.18 = (bf16[4,128,128]{2,1,0:T(8,128)(2,1)S(1)}, bf16[4,128,128]{2,1,0:T(8,128)(2,1)S(1)}, u32[]{:S(2)}, u32[]{:S(2)}) collective-permute-start(bf16[4,128,128]{2,1,0:T(8,128)(2,1)S(1)} %get-tuple-element.79.rest_4_), channel_id=1, source_target_pairs={{8,0},{16,8},{24,16},{9,1},{17,9},{25,17},{10,2},{18,10},{26,18},{... | collective-permute-start | bytes 393224 | tf_op jit(solution)/shard_map/ppermute | solution.py:481
  60.6 0.0 collective-permute-done.15.other_ga
  60.6 0.0 collective-permute-done.16.rest_1_
  60.6 6.9 %grads_within.1 = (bf16[128,4096]{1,0:T(8,128)(2,1)}, f32[128,4096]{1,0:T(8,128)S(1)}, f32[128,4096]{1,0:T(8,128)S(1)}, bf16[128,2048]{1,0:T(8,128)(2,1)S(1)}, bf16[16,128,128]{2,1,0:T(8,128)(2,1)S(1)}) custom-call(s32[8]{0:T(128)S(1)} %copy-done.4, s32[3]{0:T(128)S(1)} %pad_add_fusion.place, ...), custom_call_target="tpu_custom_call", output_to_operand_aliasing={{3}: (12, {}), {4}: (13, {})} | custom-call | flops 1073741824 | bytes 11534336 | tf_op jit(solution)/shard_map/grads_within/pallas_call | solution.py:427
  67.6 0.1 collective-permute-start.17
  67.7 0.4 collective-permute-start.27
  68.1 3.1 %collective-permute-done.19.rest_6_ = bf16[4,128,128]{2,1,0:T(8,128)(2,1)S(1)} collective-permute-done((bf16[4,128,128]{2,1,0:T(8,128)(2,1)S(1)}, bf16[4,128,128]{2,1,0:T(8,128)(2,1)S(1)}, u32[]{:S(2)}, u32[]{:S(2)}) %collective-permute-start.19) | collective-permute-done | bytes 131104 | tf_op jit(solution)/shard_map/ppermute | solution.py:481
  71.2 0.0 collective-permute-done.18.rest_5_
  71.2 0.9 future_prefix.1
  72.1 0.9 collective-permute-start.21
  72.9 1.5 %collective-permute-start.23 = (bf16[4,128,128]{2,1,0:T(8,128)(2,1)S(1)}, bf16[4,128,128]{2,1,0:T(8,128)(2,1)S(1)}, u32[]{:S(2)}, u32[]{:S(2)}) collective-permute-start(bf16[4,128,128]{2,1,0:T(8,128)(2,1)S(1)} %get-tuple-element.87), channel_id=1, source_target_pairs={{0,4},{1,5},{2,6},{3,7},{4,0},{5,1},{6,2},{7,3},{8,12},{9,13},{10,... | collective-permute-start | bytes 393224 | tf_op jit(solution)/shard_map/ppermute | solution.py:460
  74.4 1.2 %collective-permute-start.25 = (bf16[4,128,128]{2,1,0:T(8,128)(2,1)S(1)}, bf16[4,128,128]{2,1,0:T(8,128)(2,1)S(1)}, u32[]{:S(2)}, u32[]{:S(2)}) collective-permute-start(bf16[4,128,128]{2,1,0:T(8,128)(2,1)S(1)} %get-tuple-element.88), channel_id=1, source_target_pairs={{0,6},{1,7},{2,4},{3,5},{4,2},{5,3},{6,0},{7,1},{8,14},{9,15},{10,... | collective-permute-start | bytes 393224 | tf_op jit(solution)/shard_map/ppermute | solution.py:460
  75.6 2.9 %collective-permute-done.21.rest_1_ = bf16[4,128,128]{2,1,0:T(8,128)(2,1)S(1)} collective-permute-done((bf16[4,128,128]{2,1,0:T(8,128)(2,1)S(1)}, bf16[4,128,128]{2,1,0:T(8,128)(2,1)S(1)}, u32[]{:S(2)}, u32[]{:S(2)}) %collective-permute-start.21) | collective-permute-done | bytes 131104 | tf_op jit(solution)/shard_map/ppermute | solution.py:460
  78.5 0.0 collective-permute-start.20
  78.5 0.0 collective-permute-done.23.rest_2_
  78.5 0.5 collective-permute-start.22
  79.0 1.6 %collective-permute-done.25.rest_3_ = bf16[4,128,128]{2,1,0:T(8,128)(2,1)S(1)} collective-permute-done((bf16[4,128,128]{2,1,0:T(8,128)(2,1)S(1)}, bf16[4,128,128]{2,1,0:T(8,128)(2,1)S(1)}, u32[]{:S(2)}, u32[]{:S(2)}) %collective-permute-start.25) | collective-permute-done | bytes 131104 | tf_op jit(solution)/shard_map/ppermute | solution.py:460
  80.6 0.5 collective-permute-start.26
  81.1 2.8 %grads_last_0.1 = (bf16[128,4096]{1,0:T(8,128)(2,1)}, bf16[128,4096]{1,0:T(8,128)(2,1)}) custom-call(s32[8]{0:T(128)S(1)} %copy-done.4, s32[3]{0:T(128)S(1)} %pad_add_fusion.place, bf16[128,4096]{1,0:T(8,128)(2,1)S(1)} %copy-done, bf16[128,4096]{1,0:T(8,128)(2,1)S(1)} %copy-done.1, f32[128,4096]{1,0:T(8,128)S(1)} %get-tuple-element.82.rest_4_.gk_part, ...), custom_call_target="tpu_custom_call" | custom-call | flops 134217728 | bytes 4718592 | tf_op jit(solution)/shard_map/grads_last_0/pallas_call | solution.py:427
  83.9 0.0 collective-permute-done.26.rest_3_
  83.9 3.0 %grads_last_1.1 = (bf16[128,4096]{1,0:T(8,128)(2,1)}, bf16[128,4096]{1,0:T(8,128)(2,1)}, bf16[128,4096]{1,0:T(8,128)(2,1)}) custom-call(s32[8]{0:T(128)S(1)} %copy-done.4, s32[3]{0:T(128)S(1)} %pad_add_fusion.place, bf16[128,4096]{1,0:T(8,128)(2,1)S(1)} %copy-done, ...), custom_call_target="tpu_custom_call", output_to_operand_aliasing={{0}: (12, {}), {1}: (13, {}), {2}: (14, {})} | custom-call | flops 134217728 | bytes 4718592 | tf_op jit(solution)/shard_map/grads_last_1/pallas_call | solution.py:427
  (15 shorter events, 0.0 us)
Async XLA Ops:
  3.8 3.3 %copy-start.4 = (s32[8]{0:T(128)S(1)}, s32[8]{0:T(128)}, u32[]{:S(2)}) copy-start(s32[8]{0:T(128)} %lens.23) | copy-start | bytes 100
  3.8 3.2 %collective-permute-start = (bf16[16,128,128]{2,1,0:T(8,128)(2,1)S(1)}, bf16[16,128,128]{2,1,0:T(8,128)(2,1)S(1)}, u32[]{:S(2)}, u32[]{:S(2)}) collective-permute-start(bf16[16,128,128]{2,1,0:T(8,128)(2,1)S(1)} %get-tuple-element.51), channel_id=1, source_target_pairs={{0,1},{1,0},{2,3},{3,2},{4,5},{5,4},{6,7},{7,6},{8,9},{9,8},{10,11... | collective-permute-start | bytes 1572872 | tf_op jit(solution)/shard_map/ppermute | solution.py:455
  7.1 21.2 %copy-start = (bf16[128,4096]{1,0:T(8,128)(2,1)S(1)}, bf16[128,4096]{1,0:T(8,128)(2,1)}, u32[]{:S(2)}) copy-start(bf16[128,4096]{1,0:T(8,128)(2,1)} %k.11) | copy-start | bytes 3145732
  7.1 21.2 %copy-start.1 = (bf16[128,4096]{1,0:T(8,128)(2,1)S(1)}, bf16[128,4096]{1,0:T(8,128)(2,1)}, u32[]{:S(2)}) copy-start(bf16[128,4096]{1,0:T(8,128)(2,1)} %v.11) | copy-start | bytes 3145732
  7.1 21.2 %copy-start.2 = (bf16[128,4096]{1,0:T(8,128)(2,1)S(1)}, bf16[128,4096]{1,0:T(8,128)(2,1)}, u32[]{:S(2)}) copy-start(bf16[128,4096]{1,0:T(8,128)(2,1)} %q.3) | copy-start | bytes 3145732
  7.9 20.4 %collective-permute-start.1 = (bf16[3,128,2048]{2,1,0:T(8,128)(2,1)S(1)}, bf16[3,128,2048]{2,1,0:T(8,128)(2,1)S(1)}, u32[]{:S(2)}, u32[]{:S(2)}) collective-permute-start(bf16[3,128,2048]{2,1,0:T(8,128)(2,1)S(1)} %get-tuple-element.53), channel_id=1, source_target_pairs={{0,1},{1,0},{2,3},{3,2},{4,5},{5,4},{6,7},{7,6},{8,9},{9,8},{10,11... | collective-permute-start | bytes 4718600 | tf_op jit(solution)/shard_map/ppermute | solution.py:455
  8.0 6.7 %collective-permute-start.2 = (bf16[4,128,128]{2,1,0:T(8,128)(2,1)S(1)}, bf16[4,128,128]{2,1,0:T(8,128)(2,1)S(1)}, u32[]{:S(2)}, u32[]{:S(2)}) collective-permute-start(bf16[4,128,128]{2,1,0:T(8,128)(2,1)S(1)} %get-tuple-element.57), channel_id=1, source_target_pairs={{0,2},{1,3},{2,0},{3,1},{4,6},{5,7},{6,4},{7,5},{8,10},{9,11},{10,... | collective-permute-start | bytes 393224 | tf_op jit(solution)/shard_map/ppermute | solution.py:460
  11.0 6.4 %collective-permute-start.3 = (bf16[4,128,128]{2,1,0:T(8,128)(2,1)S(1)}, bf16[4,128,128]{2,1,0:T(8,128)(2,1)S(1)}, u32[]{:S(2)}, u32[]{:S(2)}) collective-permute-start(bf16[4,128,128]{2,1,0:T(8,128)(2,1)S(1)} %get-tuple-element.58), channel_id=1, source_target_pairs={{0,4},{1,5},{2,6},{3,7},{4,0},{5,1},{6,2},{7,3},{8,12},{9,13},{10,... | collective-permute-start | bytes 393224 | tf_op jit(solution)/shard_map/ppermute | solution.py:460
  12.5 6.3 %collective-permute-start.4 = (bf16[4,128,128]{2,1,0:T(8,128)(2,1)S(1)}, bf16[4,128,128]{2,1,0:T(8,128)(2,1)S(1)}, u32[]{:S(2)}, u32[]{:S(2)}) collective-permute-start(bf16[4,128,128]{2,1,0:T(8,128)(2,1)S(1)} %get-tuple-element.59), channel_id=1, source_target_pairs={{0,6},{1,7},{2,4},{3,5},{4,2},{5,3},{6,0},{7,1},{8,14},{9,15},{10,... | collective-permute-start | bytes 393224 | tf_op jit(solution)/shard_map/ppermute | solution.py:460
  19.5 13.1 %collective-permute-start.6 = (bf16[16,128,128]{2,1,0:T(8,128)(2,1)S(1)}, bf16[16,128,128]{2,1,0:T(8,128)(2,1)S(1)}, u32[]{:S(2)}, u32[]{:S(2)}) collective-permute-start(bf16[16,128,128]{2,1,0:T(8,128)(2,1)S(1)} %get-tuple-element.63), channel_id=1, source_target_pairs={{0,1},{1,0},{2,3},{3,2},{4,5},{5,4},{6,7},{7,6},{8,9},{9,8},{10,11... | collective-permute-start | bytes 1572872 | tf_op jit(solution)/shard_map/ppermute | solution.py:455
  19.6 17.4 %collective-permute-start.5 = (bf16[128,2048]{1,0:T(8,128)(2,1)S(1)}, bf16[128,2048]{1,0:T(8,128)(2,1)S(1)}, u32[]{:S(2)}, u32[]{:S(2)}) collective-permute-start(bf16[128,2048]{1,0:T(8,128)(2,1)S(1)} %get-tuple-element.61), channel_id=1, source_target_pairs={{0,1},{1,0},{2,3},{3,2},{4,5},{5,4},{6,7},{7,6},{8,9},{9,8},{10,11... | collective-permute-start | bytes 1572872 | tf_op jit(solution)/shard_map/ppermute | solution.py:455
  20.1 12.5 %collective-permute-start.8 = (bf16[4,128,128]{2,1,0:T(8,128)(2,1)S(1)}, bf16[4,128,128]{2,1,0:T(8,128)(2,1)S(1)}, u32[]{:S(2)}, u32[]{:S(2)}) collective-permute-start(bf16[4,128,128]{2,1,0:T(8,128)(2,1)S(1)} %get-tuple-element.64), channel_id=1, source_target_pairs={{0,16},{8,24},{1,17},{9,25},{2,18},{10,26},{3,19},{11,27},{4,20},{... | collective-permute-start | bytes 393224 | tf_op jit(solution)/shard_map/ppermute | solution.py:481
  24.7 7.8 %collective-permute-start.7 = (bf16[4,128,128]{2,1,0:T(8,128)(2,1)S(1)}, bf16[4,128,128]{2,1,0:T(8,128)(2,1)S(1)}, u32[]{:S(2)}, u32[]{:S(2)}) collective-permute-start(bf16[4,128,128]{2,1,0:T(8,128)(2,1)S(1)} %get-tuple-element.64), channel_id=1, source_target_pairs={{0,8},{8,16},{16,24},{1,9},{9,17},{17,25},{2,10},{10,18},{18,26},{... | collective-permute-start | bytes 393224 | tf_op jit(solution)/shard_map/ppermute | solution.py:481
  32.5 10.2 %copy-start.3 = (bf16[128,4096]{1,0:T(8,128)(2,1)S(1)}, bf16[128,4096]{1,0:T(8,128)(2,1)}, u32[]{:S(2)}) copy-start(bf16[128,4096]{1,0:T(8,128)(2,1)} %g.1) | copy-start | bytes 3145732
  33.5 5.0 %collective-permute-start.9 = (bf16[4,128,128]{2,1,0:T(8,128)(2,1)S(1)}, bf16[4,128,128]{2,1,0:T(8,128)(2,1)S(1)}, u32[]{:S(2)}, u32[]{:S(2)}) collective-permute-start(bf16[4,128,128]{2,1,0:T(8,128)(2,1)S(1)} %get-tuple-element.66), channel_id=1, source_target_pairs={{0,2},{1,3},{2,0},{3,1},{4,6},{5,7},{6,4},{7,5},{8,10},{9,11},{10,... | collective-permute-start | bytes 393224 | tf_op jit(solution)/shard_map/ppermute | solution.py:460
  35.0 6.0 %collective-permute-start.10 = (bf16[4,128,128]{2,1,0:T(8,128)(2,1)S(1)}, bf16[4,128,128]{2,1,0:T(8,128)(2,1)S(1)}, u32[]{:S(2)}, u32[]{:S(2)}) collective-permute-start(bf16[4,128,128]{2,1,0:T(8,128)(2,1)S(1)} %get-tuple-element.67), channel_id=1, source_target_pairs={{0,4},{1,5},{2,6},{3,7},{4,0},{5,1},{6,2},{7,3},{8,12},{9,13},{10,... | collective-permute-start | bytes 393224 | tf_op jit(solution)/shard_map/ppermute | solution.py:460
  36.5 6.2 %collective-permute-start.11 = (bf16[4,128,128]{2,1,0:T(8,128)(2,1)S(1)}, bf16[4,128,128]{2,1,0:T(8,128)(2,1)S(1)}, u32[]{:S(2)}, u32[]{:S(2)}) collective-permute-start(bf16[4,128,128]{2,1,0:T(8,128)(2,1)S(1)} %get-tuple-element.68), channel_id=1, source_target_pairs={{0,6},{1,7},{2,4},{3,5},{4,2},{5,3},{6,0},{7,1},{8,14},{9,15},{10,... | collective-permute-start | bytes 393224 | tf_op jit(solution)/shard_map/ppermute | solution.py:460
  48.2 6.4 %collective-permute-start.12 = (bf16[4,128,128]{2,1,0:T(8,128)(2,1)S(1)}, bf16[4,128,128]{2,1,0:T(8,128)(2,1)S(1)}, u32[]{:S(2)}, u32[]{:S(2)}) collective-permute-start(bf16[4,128,128]{2,1,0:T(8,128)(2,1)S(1)} %get-tuple-element.71), channel_id=1, source_target_pairs={{0,2},{1,3},{2,0},{3,1},{4,6},{5,7},{6,4},{7,5},{8,10},{9,11},{10,... | collective-permute-start | bytes 393224 | tf_op jit(solution)/shard_map/ppermute | solution.py:460
  49.4 5.2 %collective-permute-start.13 = (bf16[4,128,128]{2,1,0:T(8,128)(2,1)S(1)}, bf16[4,128,128]{2,1,0:T(8,128)(2,1)S(1)}, u32[]{:S(2)}, u32[]{:S(2)}) collective-permute-start(bf16[4,128,128]{2,1,0:T(8,128)(2,1)S(1)} %get-tuple-element.72), channel_id=1, source_target_pairs={{0,4},{1,5},{2,6},{3,7},{4,0},{5,1},{6,2},{7,3},{8,12},{9,13},{10,... | collective-permute-start | bytes 393224 | tf_op jit(solution)/shard_map/ppermute | solution.py:460
  50.9 5.9 %collective-permute-start.14 = (bf16[4,128,128]{2,1,0:T(8,128)(2,1)S(1)}, bf16[4,128,128]{2,1,0:T(8,128)(2,1)S(1)}, u32[]{:S(2)}, u32[]{:S(2)}) collective-permute-start(bf16[4,128,128]{2,1,0:T(8,128)(2,1)S(1)} %get-tuple-element.73), channel_id=1, source_target_pairs={{0,6},{1,7},{2,4},{3,5},{4,2},{5,3},{6,0},{7,1},{8,14},{9,15},{10,... | collective-permute-start | bytes 393224 | tf_op jit(solution)/shard_map/ppermute | solution.py:460
  57.4 3.2 %collective-permute-start.15 = (bf16[128,2048]{1,0:T(8,128)(2,1)S(1)}, bf16[128,2048]{1,0:T(8,128)(2,1)S(1)}, u32[]{:S(2)}, u32[]{:S(2)}) collective-permute-start(bf16[128,2048]{1,0:T(8,128)(2,1)S(1)} %get-tuple-element.76), channel_id=1, source_target_pairs={{0,1},{1,0},{2,3},{3,2},{4,5},{5,4},{6,7},{7,6},{8,9},{9,8},{10,11... | collective-permute-start | bytes 1572872 | tf_op jit(solution)/shard_map/ppermute | solution.py:455
  57.5 3.1 %collective-permute-start.16 = (bf16[16,128,128]{2,1,0:T(8,128)(2,1)S(1)}, bf16[16,128,128]{2,1,0:T(8,128)(2,1)S(1)}, u32[]{:S(2)}, u32[]{:S(2)}) collective-permute-start(bf16[16,128,128]{2,1,0:T(8,128)(2,1)S(1)} %get-tuple-element.78), channel_id=1, source_target_pairs={{0,1},{1,0},{2,3},{3,2},{4,5},{5,4},{6,7},{7,6},{8,9},{9,8},{10,11... | collective-permute-start | bytes 1572872 | tf_op jit(solution)/shard_map/ppermute | solution.py:455
  58.0 13.2 %collective-permute-start.19 = (bf16[4,128,128]{2,1,0:T(8,128)(2,1)S(1)}, bf16[4,128,128]{2,1,0:T(8,128)(2,1)S(1)}, u32[]{:S(2)}, u32[]{:S(2)}) collective-permute-start(bf16[4,128,128]{2,1,0:T(8,128)(2,1)S(1)} %get-tuple-element.79.rest_4_), channel_id=1, source_target_pairs={{16,0},{24,8},{17,1},{25,9},{18,2},{26,10},{19,3},{27,11},{20,4},{... | collective-permute-start | bytes 393224 | tf_op jit(solution)/shard_map/ppermute | solution.py:481
  59.3 11.9 %collective-permute-start.18 = (bf16[4,128,128]{2,1,0:T(8,128)(2,1)S(1)}, bf16[4,128,128]{2,1,0:T(8,128)(2,1)S(1)}, u32[]{:S(2)}, u32[]{:S(2)}) collective-permute-start(bf16[4,128,128]{2,1,0:T(8,128)(2,1)S(1)} %get-tuple-element.79.rest_4_), channel_id=1, source_target_pairs={{8,0},{16,8},{24,16},{9,1},{17,9},{25,17},{10,2},{18,10},{26,18},{... | collective-permute-start | bytes 393224 | tf_op jit(solution)/shard_map/ppermute | solution.py:481
  67.6 16.3 %collective-permute-start.17 = (bf16[16,128,128]{2,1,0:T(8,128)(2,1)S(1)}, bf16[16,128,128]{2,1,0:T(8,128)(2,1)S(1)}, u32[]{:S(2)}, u32[]{:S(2)}) collective-permute-start(bf16[16,128,128]{2,1,0:T(8,128)(2,1)S(1)} %get-tuple-element.84), channel_id=1, source_target_pairs={{0,1},{1,0},{2,3},{3,2},{4,5},{5,4},{6,7},{7,6},{8,9},{9,8},{10,11... | collective-permute-start | bytes 1572872 | tf_op jit(solution)/shard_map/ppermute | solution.py:455
  67.7 16.2 %collective-permute-start.27 = (bf16[128,2048]{1,0:T(8,128)(2,1)S(1)}, bf16[128,2048]{1,0:T(8,128)(2,1)S(1)}, u32[]{:S(2)}, u32[]{:S(2)}) collective-permute-start(bf16[128,2048]{1,0:T(8,128)(2,1)S(1)} %get-tuple-element.89), channel_id=1, source_target_pairs={{0,1},{1,0},{2,3},{3,2},{4,5},{5,4},{6,7},{7,6},{8,9},{9,8},{10,11... | collective-permute-start | bytes 1572872 | tf_op jit(solution)/shard_map/ppermute | solution.py:455
  72.1 6.4 %collective-permute-start.21 = (bf16[4,128,128]{2,1,0:T(8,128)(2,1)S(1)}, bf16[4,128,128]{2,1,0:T(8,128)(2,1)S(1)}, u32[]{:S(2)}, u32[]{:S(2)}) collective-permute-start(bf16[4,128,128]{2,1,0:T(8,128)(2,1)S(1)} %get-tuple-element.86), channel_id=1, source_target_pairs={{0,2},{1,3},{2,0},{3,1},{4,6},{5,7},{6,4},{7,5},{8,10},{9,11},{10,... | collective-permute-start | bytes 393224 | tf_op jit(solution)/shard_map/ppermute | solution.py:460
  72.9 5.6 %collective-permute-start.23 = (bf16[4,128,128]{2,1,0:T(8,128)(2,1)S(1)}, bf16[4,128,128]{2,1,0:T(8,128)(2,1)S(1)}, u32[]{:S(2)}, u32[]{:S(2)}) collective-permute-start(bf16[4,128,128]{2,1,0:T(8,128)(2,1)S(1)} %get-tuple-element.87), channel_id=1, source_target_pairs={{0,4},{1,5},{2,6},{3,7},{4,0},{5,1},{6,2},{7,3},{8,12},{9,13},{10,... | collective-permute-start | bytes 393224 | tf_op jit(solution)/shard_map/ppermute | solution.py:460
  74.4 6.1 %collective-permute-start.25 = (bf16[4,128,128]{2,1,0:T(8,128)(2,1)S(1)}, bf16[4,128,128]{2,1,0:T(8,128)(2,1)S(1)}, u32[]{:S(2)}, u32[]{:S(2)}) collective-permute-start(bf16[4,128,128]{2,1,0:T(8,128)(2,1)S(1)} %get-tuple-element.88), channel_id=1, source_target_pairs={{0,6},{1,7},{2,4},{3,5},{4,2},{5,3},{6,0},{7,1},{8,14},{9,15},{10,... | collective-permute-start | bytes 393224 | tf_op jit(solution)/shard_map/ppermute | solution.py:460
  78.5 2.1 %collective-permute-start.20 = (bf16[4,128,128]{2,1,0:T(8,128)(2,1)S(1)}, bf16[4,128,128]{2,1,0:T(8,128)(2,1)S(1)}, u32[]{:S(2)}, u32[]{:S(2)}) collective-permute-start(bf16[4,128,128]{2,1,0:T(8,128)(2,1)S(1)} %get-tuple-element.85.rest_0_), channel_id=1, source_target_pairs={{0,1},{1,0},{2,3},{3,2},{4,5},{5,4},{6,7},{7,6},{8,9},{9,8},{10,11... | collective-permute-start | bytes 393224 | tf_op jit(solution)/shard_map/ppermute | solution.py:455
  78.5 5.3 %collective-permute-start.22 = (bf16[4,128,128]{2,1,0:T(8,128)(2,1)S(1)}, bf16[4,128,128]{2,1,0:T(8,128)(2,1)S(1)}, u32[]{:S(2)}, u32[]{:S(2)}) collective-permute-start(bf16[4,128,128]{2,1,0:T(8,128)(2,1)S(1)} %collective-permute-done.21.rest_1_), channel_id=1, source_target_pairs={{0,1},{1,0},{2,3},{3,2},{4,5},{5,4},{6,7},{7,6},{8,9},{9,8},{10,11... | collective-permute-start | bytes 393224 | tf_op jit(solution)/shard_map/ppermute | solution.py:455
  80.6 3.3 %collective-permute-start.24 = (bf16[4,128,128]{2,1,0:T(8,128)(2,1)S(1)}, bf16[4,128,128]{2,1,0:T(8,128)(2,1)S(1)}, u32[]{:S(2)}, u32[]{:S(2)}) collective-permute-start(bf16[4,128,128]{2,1,0:T(8,128)(2,1)S(1)} %collective-permute-done.23.rest_2_), channel_id=1, source_target_pairs={{0,1},{1,0},{2,3},{3,2},{4,5},{5,4},{6,7},{7,6},{8,9},{9,8},{10,11... | collective-permute-start | bytes 393224 | tf_op jit(solution)/shard_map/ppermute | solution.py:455
  80.6 3.3 %collective-permute-start.26 = (bf16[4,128,128]{2,1,0:T(8,128)(2,1)S(1)}, bf16[4,128,128]{2,1,0:T(8,128)(2,1)S(1)}, u32[]{:S(2)}, u32[]{:S(2)}) collective-permute-start(bf16[4,128,128]{2,1,0:T(8,128)(2,1)S(1)} %collective-permute-done.25.rest_3_), channel_id=1, source_target_pairs={{0,1},{1,0},{2,3},{3,2},{4,5},{5,4},{6,7},{7,6},{8,9},{9,8},{10,11... | collective-permute-start | bytes 393224 | tf_op jit(solution)/shard_map/ppermute | solution.py:455

commit v14 on v13

--- a/solution.py
+++ b/solution.py
@@ -135,7 +135,7 @@
 
 def chip_kernel(lens, place, q, k, v, mate, part, head_fq, turned):
     count = q.shape[0]
-    seen, head, _, _ = pair_docs(lens, place, count)
+    seen, head, chip_head, late_head = pair_docs(lens, place, count)
     eye = identity(DH)
 
     def both(mine, slot, h):
@@ -150,11 +150,12 @@
         ]
         parts = [mul(s, both(v, 2, h), NN) for h, s in zip(hs, kept)]
         heads = [jnp.where(head, wide, 0.0).astype(BF16) for wide in wides]
-        turns = [turn(wide.astype(BF16), eye) for wide in wides]
+        turns = [mul(eye, wide.astype(BF16), NT) for wide in wides]
         for h, p, f, t in zip(hs, parts, heads, turns):
             part[:, cols(h)] = p
             head_fq[:, cols(h)] = f
-            turned[h] = t
+            turned[h, :DH] = jnp.where(chip_head, t, 0.0).astype(BF16)
+            turned[h, DH:] = jnp.where(late_head, t, 0.0).astype(BF16)
 
 
 def norm_kernel(lens, place, head_fq, turned, g, mate_g, part, *rest):
@@ -166,7 +167,6 @@
     )
     states = rest[chips + 8 : -1]
     count = g.shape[0]
-    _, _, head, late = pair_docs(lens, place, count)
     heads = turned.shape[0]
     step = pl.program_id(0)
     chip = place[2] >> 1
@@ -196,11 +196,7 @@
             ((go - normed * (m[2 * count :] * inv)) * inv).astype(BF16)
             for go, normed, m, inv in zip(gos, norms, means, invs)
         ]
-        sums = []
-        for h, ga in zip(hs, gas):
-            wide = turned[h].astype(F32)
-            two = jnp.concatenate([jnp.where(head, wide, 0.0), jnp.where(late, wide, 0.0)], axis=0)
-            sums.append(mul(two.astype(BF16), ga, NN).astype(BF16))
+        sums = [mul(turned[h], ga, NN).astype(BF16) for h, ga in zip(hs, gas)]
         for h, normed, ga, value in zip(hs, norms, gas, sums):
             normed = normed.astype(BF16)
             out[:, cols(h)], mate_out[:, cols(h)] = normed[:count], normed[count:]
@@ -455,11 +451,11 @@
         return lax.ppermute(state, LAYER, [(i, i ^ 1) for i in range(members)])
 
     def exchange(states):
-        pairs = [[(i, i ^ (2 * n)) for i in range(members)] for n in range(chips)]
-        return [
-            state if n == 0 else lax.ppermute(state, LAYER, pairs[n])
-            for n, state in enumerate(states)
-        ]
+        came = list(states)
+        for n in reversed(range(1, chips)):
+            pairs = [(i, i ^ (2 * n)) for i in range(members)]
+            came[n] = lax.ppermute(states[n], LAYER, pairs)
+        return came
 
     def reach_out(merged, along, forward, name):
         came = exchange(merged)
@@ -552,7 +548,7 @@
     own_tokens = pl.BlockSpec((count, few * DH), own_few)
     pair_tokens = pl.BlockSpec((2 * count, few * DH), lambda i, *a: (0, i))
     lane_few = pl.BlockSpec((count, few * DH), lambda i, *a: (0, i))
-    turns = pl.BlockSpec((few, DH, 2 * count), lambda i, *a: (i, 0, 0))
+    turns = pl.BlockSpec((few, 2 * DH, 2 * count), lambda i, *a: (i, 0, 0))
     part, head_fq, turned = run(
         chip_kernel,
         parts,
@@ -561,7 +557,7 @@
         [
             jax.ShapeDtypeStruct((2 * count, half * DH), F32),
             jax.ShapeDtypeStruct((2 * count, half * DH), BF16),
-            jax.ShapeDtypeStruct((half, DH, 2 * count), BF16),
+            jax.ShapeDtypeStruct((half, 2 * DH, 2 * count), BF16),
         ],
         [],
         (queries, keys, values, mate_three),

time: 87.6 us -> 87.5 us (level)
  no operation moved by 1% of the time
where the time goes in v14:
time: 87.5 us; the launch traced here: 86.7 us
  Pallas kernels  32 us (37%)
  starting transfers between devices  29.1 us (33%)
  waiting for transfers between devices  24.7 us (28%)
  between operations  0.91 us (1%)
    pallas_call x12, Pallas kernels, run(): pl.pallas_call(kernel, grid_spec=pltpu.PrefetchScalarGridSpec(num_scalar_...  32 us
    ppermute x12, waiting for transfers between devices, exchange(): came[n] = lax.ppermute(states[n], LAYER, pairs)  21.5 us
    ppermute x12, starting transfers between devices, exchange(): came[n] = lax.ppermute(states[n], LAYER, pairs)  15.1 us
    ppermute x4, starting transfers between devices, reach_out(): others.insert(0, lax.ppermute(total, 'z', pairs))  10.7 us
    ppermute x12, starting transfers between devices, swap(): return lax.ppermute(state, LAYER, [(i, i ^ 1) for i in range(members)])  3.31 us
    ppermute x4, waiting for transfers between devices, reach_out(): others.insert(0, lax.ppermute(total, 'z', pairs))  3.09 us
  transfers between devices with their start and end apart: 28, of which 11 were waited for; matrix products, arithmetic and copies ran while one was open for 0% of the time, Pallas kernels for 22%

profile of v14, /device:TPU:0, one launch (start us, length us, event | category | flops | bytes accessed | tf_op | source)
XLA Modules:
  0.0 86.7 jit_solution(4573108086041309894)
XLA Ops:
  0.6 0.1 pad_add_fusion.place
  0.7 3.1 %tail_mate.1 = (bf16[16,128,128]{2,1,0:T(8,128)(2,1)S(1)}, bf16[3,128,2048]{2,1,0:T(8,128)(2,1)S(1)}, bf16[128,2048]{1,0:T(8,128)(2,1)S(1)}) custom-call(s32[8]{0:T(128)} %lens.23, s32[3]{0:T(128)S(1)} %pad_add_fusion.place, bf16[128,4096]{1,0:T(8,128)(2,1)} %k.11, bf16[128,4096]{1,0:T(8,128)(2,1)} %v.11, bf16[128,4096]{1,0:T(8,128)(2,1)} %q.3, ...), custom_call_target="tpu_custom_call" | custom-call | flops 67108864 | bytes 1572864 | tf_op jit(solution)/shard_map/tail_mate/pallas_call | solution.py:423
  3.8 0.0 copy-start.4
  3.8 0.5 collective-permute-start
  4.3 2.7 %tail_own.1.rest_5_ = bf16[16,128,128]{2,1,0:T(8,128)(2,1)S(1)} custom-call(s32[8]{0:T(128)} %lens.23, s32[3]{0:T(128)S(1)} %pad_add_fusion.place, bf16[128,4096]{1,0:T(8,128)(2,1)} %k.11, bf16[128,4096]{1,0:T(8,128)(2,1)} %v.11), custom_call_target="tpu_custom_call" | custom-call | flops 67108864 | bytes 1572864 | tf_op jit(solution)/shard_map/tail_own/pallas_call | solution.py:423
  7.1 0.0 copy-start
  7.1 0.0 copy-start.1
  7.1 0.0 copy-start.2
  7.1 0.8 carried_chip.1
  7.9 0.1 collective-permute-start.1
  8.0 3.0 %collective-permute-start.2 = (bf16[4,128,128]{2,1,0:T(8,128)(2,1)S(1)}, bf16[4,128,128]{2,1,0:T(8,128)(2,1)S(1)}, u32[]{:S(2)}, u32[]{:S(2)}) collective-permute-start(bf16[4,128,128]{2,1,0:T(8,128)(2,1)S(1)} %get-tuple-element.57), channel_id=1, source_target_pairs={{0,2},{1,3},{2,0},{3,1},{4,6},{5,7},{6,4},{7,5},{8,10},{9,11},{10,... | collective-permute-start | bytes 393224 | tf_op jit(solution)/shard_map/ppermute | solution.py:457
  11.0 1.5 %collective-permute-start.3 = (bf16[4,128,128]{2,1,0:T(8,128)(2,1)S(1)}, bf16[4,128,128]{2,1,0:T(8,128)(2,1)S(1)}, u32[]{:S(2)}, u32[]{:S(2)}) collective-permute-start(bf16[4,128,128]{2,1,0:T(8,128)(2,1)S(1)} %get-tuple-element.58), channel_id=1, source_target_pairs={{0,4},{1,5},{2,6},{3,7},{4,0},{5,1},{6,2},{7,3},{8,12},{9,13},{10,... | collective-permute-start | bytes 393224 | tf_op jit(solution)/shard_map/ppermute | solution.py:457
  12.5 2.2 %collective-permute-done.2.rest_1_ = bf16[4,128,128]{2,1,0:T(8,128)(2,1)S(1)} collective-permute-done((bf16[4,128,128]{2,1,0:T(8,128)(2,1)S(1)}, bf16[4,128,128]{2,1,0:T(8,128)(2,1)S(1)}, u32[]{:S(2)}, u32[]{:S(2)}) %collective-permute-start.2) | collective-permute-done | bytes 131104 | tf_op jit(solution)/shard_map/ppermute | solution.py:457
  14.7 2.7 %collective-permute-done.3.rest_2_ = bf16[4,128,128]{2,1,0:T(8,128)(2,1)S(1)} collective-permute-done((bf16[4,128,128]{2,1,0:T(8,128)(2,1)S(1)}, bf16[4,128,128]{2,1,0:T(8,128)(2,1)S(1)}, u32[]{:S(2)}, u32[]{:S(2)}) %collective-permute-start.3) | collective-permute-done | bytes 131104 | tf_op jit(solution)/shard_map/ppermute | solution.py:457
  17.4 1.4 %collective-permute-done.4.rest_3_ = bf16[4,128,128]{2,1,0:T(8,128)(2,1)S(1)} collective-permute-done((bf16[4,128,128]{2,1,0:T(8,128)(2,1)S(1)}, bf16[4,128,128]{2,1,0:T(8,128)(2,1)S(1)}, u32[]{:S(2)}, u32[]{:S(2)}) %collective-permute-start.4) | collective-permute-done | bytes 131104 | tf_op jit(solution)/shard_map/ppermute | solution.py:457
  18.8 0.7 carried_total.1
  19.5 0.1 collective-permute-start.6
  19.6 0.5 collective-permute-start.5
  20.1 4.6 %collective-permute-start.8 = (bf16[4,128,128]{2,1,0:T(8,128)(2,1)S(1)}, bf16[4,128,128]{2,1,0:T(8,128)(2,1)S(1)}, u32[]{:S(2)}, u32[]{:S(2)}) collective-permute-start(bf16[4,128,128]{2,1,0:T(8,128)(2,1)S(1)} %get-tuple-element.64), channel_id=1, source_target_pairs={{0,16},{8,24},{1,17},{9,25},{2,18},{10,26},{3,19},{11,27},{4,20},{... | collective-permute-start | bytes 393224 | tf_op jit(solution)/shard_map/ppermute | solution.py:477
  24.7 3.5 %collective-permute-start.7 = (bf16[4,128,128]{2,1,0:T(8,128)(2,1)S(1)}, bf16[4,128,128]{2,1,0:T(8,128)(2,1)S(1)}, u32[]{:S(2)}, u32[]{:S(2)}) collective-permute-start(bf16[4,128,128]{2,1,0:T(8,128)(2,1)S(1)} %get-tuple-element.64), channel_id=1, source_target_pairs={{0,8},{8,16},{16,24},{1,9},{9,17},{17,25},{2,10},{10,18},{18,26},{... | collective-permute-start | bytes 393224 | tf_op jit(solution)/shard_map/ppermute | solution.py:477
  28.3 4.3 %within_chip.1 = (f32[256,2048]{1,0:T(8,128)S(1)}, bf16[256,2048]{1,0:T(8,128)(2,1)S(1)}, bf16[16,256,256]{2,1,0:T(8,128)(2,1)S(1)}) custom-call(s32[8]{0:T(128)S(1)} %copy-done.4, s32[3]{0:T(128)S(1)} %pad_add_fusion.place, bf16[128,4096]{1,0:T(8,128)(2,1)S(1)} %copy-done.2, bf16[128,4096]{1,0:T(8,128)(2,1)S(1)} %copy-done, ...), custom_call_target="tpu_custom_call" | custom-call | flops 671088640 | bytes 7340032 | tf_op jit(solution)/shard_map/within_chip/pallas_call | solution.py:423
  32.6 0.0 copy-start.3
  32.6 0.0 collective-permute-done.8.rest_7_
  32.6 0.0 collective-permute-done.7.rest_6_
  32.6 0.9 %carried_prefix.1 = (bf16[4,128,128]{2,1,0:T(8,128)(2,1)S(1)}, bf16[4,128,128]{2,1,0:T(8,128)(2,1)S(1)}, bf16[4,128,128]{2,1,0:T(8,128)(2,1)S(1)}, bf16[4,128,128]{2,1,0:T(8,128)(2,1)S(1)}) custom-call(s32[8]{0:T(128)S(1)} %copy-done.4, s32[3]{0:T(128)S(1)} %pad_add_fusion.place, bf16[4,128,128]{2,1,0:T(8,128)(2,1)S(1)} %get-tuple-element.56.rest_0_, ...), custom_call_target="tpu_custom_call" | custom-call | flops 1048576 | bytes 1048576 | tf_op jit(solution)/shard_map/carried_prefix/pallas_call | solution.py:423
  33.5 1.6 %collective-permute-start.9 = (bf16[4,128,128]{2,1,0:T(8,128)(2,1)S(1)}, bf16[4,128,128]{2,1,0:T(8,128)(2,1)S(1)}, u32[]{:S(2)}, u32[]{:S(2)}) collective-permute-start(bf16[4,128,128]{2,1,0:T(8,128)(2,1)S(1)} %get-tuple-element.66), channel_id=1, source_target_pairs={{0,2},{1,3},{2,0},{3,1},{4,6},{5,7},{6,4},{7,5},{8,10},{9,11},{10,... | collective-permute-start | bytes 393224 | tf_op jit(solution)/shard_map/ppermute | solution.py:457
  35.1 1.5 %collective-permute-start.10 = (bf16[4,128,128]{2,1,0:T(8,128)(2,1)S(1)}, bf16[4,128,128]{2,1,0:T(8,128)(2,1)S(1)}, u32[]{:S(2)}, u32[]{:S(2)}) collective-permute-start(bf16[4,128,128]{2,1,0:T(8,128)(2,1)S(1)} %get-tuple-element.67), channel_id=1, source_target_pairs={{0,4},{1,5},{2,6},{3,7},{4,0},{5,1},{6,2},{7,3},{8,12},{9,13},{10,... | collective-permute-start | bytes 393224 | tf_op jit(solution)/shard_map/ppermute | solution.py:457
  36.6 0.5 collective-permute-start.11
  37.1 0.0 collective-permute-done.5.mate_g
  37.1 1.5 %collective-permute-done.9.rest_1_ = bf16[4,128,128]{2,1,0:T(8,128)(2,1)S(1)} collective-permute-done((bf16[4,128,128]{2,1,0:T(8,128)(2,1)S(1)}, bf16[4,128,128]{2,1,0:T(8,128)(2,1)S(1)}, u32[]{:S(2)}, u32[]{:S(2)}) %collective-permute-start.9) | collective-permute-done | bytes 131104 | tf_op jit(solution)/shard_map/ppermute | solution.py:457
  38.5 2.6 %collective-permute-done.10.rest_2_ = bf16[4,128,128]{2,1,0:T(8,128)(2,1)S(1)} collective-permute-done((bf16[4,128,128]{2,1,0:T(8,128)(2,1)S(1)}, bf16[4,128,128]{2,1,0:T(8,128)(2,1)S(1)}, u32[]{:S(2)}, u32[]{:S(2)}) %collective-permute-start.10) | collective-permute-done | bytes 131104 | tf_op jit(solution)/shard_map/ppermute | solution.py:457
  41.1 1.7 %collective-permute-done.11.rest_3_ = bf16[4,128,128]{2,1,0:T(8,128)(2,1)S(1)} collective-permute-done((bf16[4,128,128]{2,1,0:T(8,128)(2,1)S(1)}, bf16[4,128,128]{2,1,0:T(8,128)(2,1)S(1)}, u32[]{:S(2)}, u32[]{:S(2)}) %collective-permute-start.11) | collective-permute-done | bytes 131104 | tf_op jit(solution)/shard_map/ppermute | solution.py:457
  42.8 5.3 %normed.1 = (bf16[128,4096]{1,0:T(8,128)(2,1)}, bf16[128,2048]{1,0:T(8,128)(2,1)S(1)}, bf16[128,2048]{1,0:T(8,128)(2,1)S(1)}, bf16[128,2048]{1,0:T(8,128)(2,1)S(...) custom-call(s32[8]{0:T(128)S(1)} %copy-done.4, ...), custom_call_target="tpu_custom_call" | custom-call | flops 536870912 | bytes 8388608 | tf_op jit(solution)/shard_map/normed/pallas_call | solution.py:423
  48.1 1.2 %collective-permute-start.12 = (bf16[4,128,128]{2,1,0:T(8,128)(2,1)S(1)}, bf16[4,128,128]{2,1,0:T(8,128)(2,1)S(1)}, u32[]{:S(2)}, u32[]{:S(2)}) collective-permute-start(bf16[4,128,128]{2,1,0:T(8,128)(2,1)S(1)} %get-tuple-element.71), channel_id=1, source_target_pairs={{0,2},{1,3},{2,0},{3,1},{4,6},{5,7},{6,4},{7,5},{8,10},{9,11},{10,... | collective-permute-start | bytes 393224 | tf_op jit(solution)/shard_map/ppermute | solution.py:457
  49.3 1.5 %collective-permute-start.13 = (bf16[4,128,128]{2,1,0:T(8,128)(2,1)S(1)}, bf16[4,128,128]{2,1,0:T(8,128)(2,1)S(1)}, u32[]{:S(2)}, u32[]{:S(2)}) collective-permute-start(bf16[4,128,128]{2,1,0:T(8,128)(2,1)S(1)} %get-tuple-element.72), channel_id=1, source_target_pairs={{0,4},{1,5},{2,6},{3,7},{4,0},{5,1},{6,2},{7,3},{8,12},{9,13},{10,... | collective-permute-start | bytes 393224 | tf_op jit(solution)/shard_map/ppermute | solution.py:457
  50.8 0.8 collective-permute-start.14
  51.6 2.9 %collective-permute-done.12.rest_1_ = bf16[4,128,128]{2,1,0:T(8,128)(2,1)S(1)} collective-permute-done((bf16[4,128,128]{2,1,0:T(8,128)(2,1)S(1)}, bf16[4,128,128]{2,1,0:T(8,128)(2,1)S(1)}, u32[]{:S(2)}, u32[]{:S(2)}) %collective-permute-start.12) | collective-permute-done | bytes 131104 | tf_op jit(solution)/shard_map/ppermute | solution.py:457
  54.5 2.2 %collective-permute-done.14.rest_3_ = bf16[4,128,128]{2,1,0:T(8,128)(2,1)S(1)} collective-permute-done((bf16[4,128,128]{2,1,0:T(8,128)(2,1)S(1)}, bf16[4,128,128]{2,1,0:T(8,128)(2,1)S(1)}, u32[]{:S(2)}, u32[]{:S(2)}) %collective-permute-start.14) | collective-permute-done | bytes 131104 | tf_op jit(solution)/shard_map/ppermute | solution.py:457
  56.6 0.7 future_total.1
  57.4 0.1 collective-permute-start.15
  57.5 0.5 collective-permute-start.16
  58.0 1.3 %collective-permute-start.19 = (bf16[4,128,128]{2,1,0:T(8,128)(2,1)S(1)}, bf16[4,128,128]{2,1,0:T(8,128)(2,1)S(1)}, u32[]{:S(2)}, u32[]{:S(2)}) collective-permute-start(bf16[4,128,128]{2,1,0:T(8,128)(2,1)S(1)} %get-tuple-element.79.rest_4_), channel_id=1, source_target_pairs={{16,0},{24,8},{17,1},{25,9},{18,2},{26,10},{19,3},{27,11},{20,4},{... | collective-permute-start | bytes 393224 | tf_op jit(solution)/shard_map/ppermute | solution.py:477
  59.2 1.3 %collective-permute-start.18 = (bf16[4,128,128]{2,1,0:T(8,128)(2,1)S(1)}, bf16[4,128,128]{2,1,0:T(8,128)(2,1)S(1)}, u32[]{:S(2)}, u32[]{:S(2)}) collective-permute-start(bf16[4,128,128]{2,1,0:T(8,128)(2,1)S(1)} %get-tuple-element.79.rest_4_), channel_id=1, source_target_pairs={{8,0},{16,8},{24,16},{9,1},{17,9},{25,17},{10,2},{18,10},{26,18},{... | collective-permute-start | bytes 393224 | tf_op jit(solution)/shard_map/ppermute | solution.py:477
  60.5 0.0 collective-permute-done.16.rest_1_
  60.6 6.9 %grads_within.1 = (bf16[128,4096]{1,0:T(8,128)(2,1)}, f32[128,4096]{1,0:T(8,128)S(1)}, f32[128,4096]{1,0:T(8,128)S(1)}, bf16[128,2048]{1,0:T(8,128)(2,1)S(1)}, bf16[16,128,128]{2,1,0:T(8,128)(2,1)S(1)}) custom-call(s32[8]{0:T(128)S(1)} %copy-done.4, s32[3]{0:T(128)S(1)} %pad_add_fusion.place, ...), custom_call_target="tpu_custom_call", output_to_operand_aliasing={{3}: (12, {}), {4}: (13, {})} | custom-call | flops 1073741824 | bytes 11534336 | tf_op jit(solution)/shard_map/grads_within/pallas_call | solution.py:423
  67.5 0.1 collective-permute-start.17
  67.6 0.4 collective-permute-start.27
  68.0 3.1 %collective-permute-done.19.rest_6_ = bf16[4,128,128]{2,1,0:T(8,128)(2,1)S(1)} collective-permute-done((bf16[4,128,128]{2,1,0:T(8,128)(2,1)S(1)}, bf16[4,128,128]{2,1,0:T(8,128)(2,1)S(1)}, u32[]{:S(2)}, u32[]{:S(2)}) %collective-permute-start.19) | collective-permute-done | bytes 131104 | tf_op jit(solution)/shard_map/ppermute | solution.py:477
  71.1 0.9 future_prefix.1
  72.0 0.9 collective-permute-start.21
  72.8 1.5 %collective-permute-start.23 = (bf16[4,128,128]{2,1,0:T(8,128)(2,1)S(1)}, bf16[4,128,128]{2,1,0:T(8,128)(2,1)S(1)}, u32[]{:S(2)}, u32[]{:S(2)}) collective-permute-start(bf16[4,128,128]{2,1,0:T(8,128)(2,1)S(1)} %get-tuple-element.87), channel_id=1, source_target_pairs={{0,4},{1,5},{2,6},{3,7},{4,0},{5,1},{6,2},{7,3},{8,12},{9,13},{10,... | collective-permute-start | bytes 393224 | tf_op jit(solution)/shard_map/ppermute | solution.py:457
  74.3 1.2 %collective-permute-start.25 = (bf16[4,128,128]{2,1,0:T(8,128)(2,1)S(1)}, bf16[4,128,128]{2,1,0:T(8,128)(2,1)S(1)}, u32[]{:S(2)}, u32[]{:S(2)}) collective-permute-start(bf16[4,128,128]{2,1,0:T(8,128)(2,1)S(1)} %get-tuple-element.88), channel_id=1, source_target_pairs={{0,6},{1,7},{2,4},{3,5},{4,2},{5,3},{6,0},{7,1},{8,14},{9,15},{10,... | collective-permute-start | bytes 393224 | tf_op jit(solution)/shard_map/ppermute | solution.py:457
  75.5 2.9 %collective-permute-done.21.rest_1_ = bf16[4,128,128]{2,1,0:T(8,128)(2,1)S(1)} collective-permute-done((bf16[4,128,128]{2,1,0:T(8,128)(2,1)S(1)}, bf16[4,128,128]{2,1,0:T(8,128)(2,1)S(1)}, u32[]{:S(2)}, u32[]{:S(2)}) %collective-permute-start.21) | collective-permute-done | bytes 131104 | tf_op jit(solution)/shard_map/ppermute | solution.py:457
  78.4 0.0 collective-permute-start.20
  78.4 0.0 collective-permute-done.23.rest_2_
  78.4 0.5 collective-permute-start.22
  78.9 1.6 %collective-permute-done.25.rest_3_ = bf16[4,128,128]{2,1,0:T(8,128)(2,1)S(1)} collective-permute-done((bf16[4,128,128]{2,1,0:T(8,128)(2,1)S(1)}, bf16[4,128,128]{2,1,0:T(8,128)(2,1)S(1)}, u32[]{:S(2)}, u32[]{:S(2)}) %collective-permute-start.25) | collective-permute-done | bytes 131104 | tf_op jit(solution)/shard_map/ppermute | solution.py:457
  80.5 0.0 collective-permute-start.24
  80.5 0.0 collective-permute-done.20.rest_0_
  80.5 0.5 collective-permute-start.26
  81.0 2.8 %grads_last_0.1 = (bf16[128,4096]{1,0:T(8,128)(2,1)}, bf16[128,4096]{1,0:T(8,128)(2,1)}) custom-call(s32[8]{0:T(128)S(1)} %copy-done.4, s32[3]{0:T(128)S(1)} %pad_add_fusion.place, bf16[128,4096]{1,0:T(8,128)(2,1)S(1)} %copy-done, bf16[128,4096]{1,0:T(8,128)(2,1)S(1)} %copy-done.1, f32[128,4096]{1,0:T(8,128)S(1)} %get-tuple-element.82.rest_4_.gk_part, ...), custom_call_target="tpu_custom_call" | custom-call | flops 134217728 | bytes 4718592 | tf_op jit(solution)/shard_map/grads_last_0/pallas_call | solution.py:423
  83.7 0.0 collective-permute-done.22.rest_1_
  83.7 0.0 collective-permute-done.17.late
  83.8 3.0 %grads_last_1.1 = (bf16[128,4096]{1,0:T(8,128)(2,1)}, bf16[128,4096]{1,0:T(8,128)(2,1)}, bf16[128,4096]{1,0:T(8,128)(2,1)}) custom-call(s32[8]{0:T(128)S(1)} %copy-done.4, s32[3]{0:T(128)S(1)} %pad_add_fusion.place, bf16[128,4096]{1,0:T(8,128)(2,1)S(1)} %copy-done, ...), custom_call_target="tpu_custom_call", output_to_operand_aliasing={{0}: (12, {}), {1}: (13, {}), {2}: (14, {})} | custom-call | flops 134217728 | bytes 4718592 | tf_op jit(solution)/shard_map/grads_last_1/pallas_call | solution.py:423
  (15 shorter events, 0.0 us)
Async XLA Ops:
  3.8 3.3 %copy-start.4 = (s32[8]{0:T(128)S(1)}, s32[8]{0:T(128)}, u32[]{:S(2)}) copy-start(s32[8]{0:T(128)} %lens.23) | copy-start | bytes 100
  3.8 3.2 %collective-permute-start = (bf16[16,128,128]{2,1,0:T(8,128)(2,1)S(1)}, bf16[16,128,128]{2,1,0:T(8,128)(2,1)S(1)}, u32[]{:S(2)}, u32[]{:S(2)}) collective-permute-start(bf16[16,128,128]{2,1,0:T(8,128)(2,1)S(1)} %get-tuple-element.51), channel_id=1, source_target_pairs={{0,1},{1,0},{2,3},{3,2},{4,5},{5,4},{6,7},{7,6},{8,9},{9,8},{10,11... | collective-permute-start | bytes 1572872 | tf_op jit(solution)/shard_map/ppermute | solution.py:451
  7.1 21.2 %copy-start = (bf16[128,4096]{1,0:T(8,128)(2,1)S(1)}, bf16[128,4096]{1,0:T(8,128)(2,1)}, u32[]{:S(2)}) copy-start(bf16[128,4096]{1,0:T(8,128)(2,1)} %k.11) | copy-start | bytes 3145732
  7.1 21.2 %copy-start.1 = (bf16[128,4096]{1,0:T(8,128)(2,1)S(1)}, bf16[128,4096]{1,0:T(8,128)(2,1)}, u32[]{:S(2)}) copy-start(bf16[128,4096]{1,0:T(8,128)(2,1)} %v.11) | copy-start | bytes 3145732
  7.1 21.2 %copy-start.2 = (bf16[128,4096]{1,0:T(8,128)(2,1)S(1)}, bf16[128,4096]{1,0:T(8,128)(2,1)}, u32[]{:S(2)}) copy-start(bf16[128,4096]{1,0:T(8,128)(2,1)} %q.3) | copy-start | bytes 3145732
  7.9 20.4 %collective-permute-start.1 = (bf16[3,128,2048]{2,1,0:T(8,128)(2,1)S(1)}, bf16[3,128,2048]{2,1,0:T(8,128)(2,1)S(1)}, u32[]{:S(2)}, u32[]{:S(2)}) collective-permute-start(bf16[3,128,2048]{2,1,0:T(8,128)(2,1)S(1)} %get-tuple-element.53), channel_id=1, source_target_pairs={{0,1},{1,0},{2,3},{3,2},{4,5},{5,4},{6,7},{7,6},{8,9},{9,8},{10,11... | collective-permute-start | bytes 4718600 | tf_op jit(solution)/shard_map/ppermute | solution.py:451
  8.0 6.7 %collective-permute-start.2 = (bf16[4,128,128]{2,1,0:T(8,128)(2,1)S(1)}, bf16[4,128,128]{2,1,0:T(8,128)(2,1)S(1)}, u32[]{:S(2)}, u32[]{:S(2)}) collective-permute-start(bf16[4,128,128]{2,1,0:T(8,128)(2,1)S(1)} %get-tuple-element.57), channel_id=1, source_target_pairs={{0,2},{1,3},{2,0},{3,1},{4,6},{5,7},{6,4},{7,5},{8,10},{9,11},{10,... | collective-permute-start | bytes 393224 | tf_op jit(solution)/shard_map/ppermute | solution.py:457
  11.0 6.4 %collective-permute-start.3 = (bf16[4,128,128]{2,1,0:T(8,128)(2,1)S(1)}, bf16[4,128,128]{2,1,0:T(8,128)(2,1)S(1)}, u32[]{:S(2)}, u32[]{:S(2)}) collective-permute-start(bf16[4,128,128]{2,1,0:T(8,128)(2,1)S(1)} %get-tuple-element.58), channel_id=1, source_target_pairs={{0,4},{1,5},{2,6},{3,7},{4,0},{5,1},{6,2},{7,3},{8,12},{9,13},{10,... | collective-permute-start | bytes 393224 | tf_op jit(solution)/shard_map/ppermute | solution.py:457
  12.5 6.3 %collective-permute-start.4 = (bf16[4,128,128]{2,1,0:T(8,128)(2,1)S(1)}, bf16[4,128,128]{2,1,0:T(8,128)(2,1)S(1)}, u32[]{:S(2)}, u32[]{:S(2)}) collective-permute-start(bf16[4,128,128]{2,1,0:T(8,128)(2,1)S(1)} %get-tuple-element.59), channel_id=1, source_target_pairs={{0,6},{1,7},{2,4},{3,5},{4,2},{5,3},{6,0},{7,1},{8,14},{9,15},{10,... | collective-permute-start | bytes 393224 | tf_op jit(solution)/shard_map/ppermute | solution.py:457
  19.5 13.1 %collective-permute-start.6 = (bf16[16,128,128]{2,1,0:T(8,128)(2,1)S(1)}, bf16[16,128,128]{2,1,0:T(8,128)(2,1)S(1)}, u32[]{:S(2)}, u32[]{:S(2)}) collective-permute-start(bf16[16,128,128]{2,1,0:T(8,128)(2,1)S(1)} %get-tuple-element.63), channel_id=1, source_target_pairs={{0,1},{1,0},{2,3},{3,2},{4,5},{5,4},{6,7},{7,6},{8,9},{9,8},{10,11... | collective-permute-start | bytes 1572872 | tf_op jit(solution)/shard_map/ppermute | solution.py:451
  19.6 17.5 %collective-permute-start.5 = (bf16[128,2048]{1,0:T(8,128)(2,1)S(1)}, bf16[128,2048]{1,0:T(8,128)(2,1)S(1)}, u32[]{:S(2)}, u32[]{:S(2)}) collective-permute-start(bf16[128,2048]{1,0:T(8,128)(2,1)S(1)} %get-tuple-element.61), channel_id=1, source_target_pairs={{0,1},{1,0},{2,3},{3,2},{4,5},{5,4},{6,7},{7,6},{8,9},{9,8},{10,11... | collective-permute-start | bytes 1572872 | tf_op jit(solution)/shard_map/ppermute | solution.py:451
  20.1 12.5 %collective-permute-start.8 = (bf16[4,128,128]{2,1,0:T(8,128)(2,1)S(1)}, bf16[4,128,128]{2,1,0:T(8,128)(2,1)S(1)}, u32[]{:S(2)}, u32[]{:S(2)}) collective-permute-start(bf16[4,128,128]{2,1,0:T(8,128)(2,1)S(1)} %get-tuple-element.64), channel_id=1, source_target_pairs={{0,16},{8,24},{1,17},{9,25},{2,18},{10,26},{3,19},{11,27},{4,20},{... | collective-permute-start | bytes 393224 | tf_op jit(solution)/shard_map/ppermute | solution.py:477
  24.7 7.9 %collective-permute-start.7 = (bf16[4,128,128]{2,1,0:T(8,128)(2,1)S(1)}, bf16[4,128,128]{2,1,0:T(8,128)(2,1)S(1)}, u32[]{:S(2)}, u32[]{:S(2)}) collective-permute-start(bf16[4,128,128]{2,1,0:T(8,128)(2,1)S(1)} %get-tuple-element.64), channel_id=1, source_target_pairs={{0,8},{8,16},{16,24},{1,9},{9,17},{17,25},{2,10},{10,18},{18,26},{... | collective-permute-start | bytes 393224 | tf_op jit(solution)/shard_map/ppermute | solution.py:477
  32.6 10.2 %copy-start.3 = (bf16[128,4096]{1,0:T(8,128)(2,1)S(1)}, bf16[128,4096]{1,0:T(8,128)(2,1)}, u32[]{:S(2)}) copy-start(bf16[128,4096]{1,0:T(8,128)(2,1)} %g.1) | copy-start | bytes 3145732
  33.5 5.0 %collective-permute-start.9 = (bf16[4,128,128]{2,1,0:T(8,128)(2,1)S(1)}, bf16[4,128,128]{2,1,0:T(8,128)(2,1)S(1)}, u32[]{:S(2)}, u32[]{:S(2)}) collective-permute-start(bf16[4,128,128]{2,1,0:T(8,128)(2,1)S(1)} %get-tuple-element.66), channel_id=1, source_target_pairs={{0,2},{1,3},{2,0},{3,1},{4,6},{5,7},{6,4},{7,5},{8,10},{9,11},{10,... | collective-permute-start | bytes 393224 | tf_op jit(solution)/shard_map/ppermute | solution.py:457
  35.1 6.0 %collective-permute-start.10 = (bf16[4,128,128]{2,1,0:T(8,128)(2,1)S(1)}, bf16[4,128,128]{2,1,0:T(8,128)(2,1)S(1)}, u32[]{:S(2)}, u32[]{:S(2)}) collective-permute-start(bf16[4,128,128]{2,1,0:T(8,128)(2,1)S(1)} %get-tuple-element.67), channel_id=1, source_target_pairs={{0,4},{1,5},{2,6},{3,7},{4,0},{5,1},{6,2},{7,3},{8,12},{9,13},{10,... | collective-permute-start | bytes 393224 | tf_op jit(solution)/shard_map/ppermute | solution.py:457
  36.6 6.2 %collective-permute-start.11 = (bf16[4,128,128]{2,1,0:T(8,128)(2,1)S(1)}, bf16[4,128,128]{2,1,0:T(8,128)(2,1)S(1)}, u32[]{:S(2)}, u32[]{:S(2)}) collective-permute-start(bf16[4,128,128]{2,1,0:T(8,128)(2,1)S(1)} %get-tuple-element.68), channel_id=1, source_target_pairs={{0,6},{1,7},{2,4},{3,5},{4,2},{5,3},{6,0},{7,1},{8,14},{9,15},{10,... | collective-permute-start | bytes 393224 | tf_op jit(solution)/shard_map/ppermute | solution.py:457
  48.1 6.4 %collective-permute-start.12 = (bf16[4,128,128]{2,1,0:T(8,128)(2,1)S(1)}, bf16[4,128,128]{2,1,0:T(8,128)(2,1)S(1)}, u32[]{:S(2)}, u32[]{:S(2)}) collective-permute-start(bf16[4,128,128]{2,1,0:T(8,128)(2,1)S(1)} %get-tuple-element.71), channel_id=1, source_target_pairs={{0,2},{1,3},{2,0},{3,1},{4,6},{5,7},{6,4},{7,5},{8,10},{9,11},{10,... | collective-permute-start | bytes 393224 | tf_op jit(solution)/shard_map/ppermute | solution.py:457
  49.3 5.2 %collective-permute-start.13 = (bf16[4,128,128]{2,1,0:T(8,128)(2,1)S(1)}, bf16[4,128,128]{2,1,0:T(8,128)(2,1)S(1)}, u32[]{:S(2)}, u32[]{:S(2)}) collective-permute-start(bf16[4,128,128]{2,1,0:T(8,128)(2,1)S(1)} %get-tuple-element.72), channel_id=1, source_target_pairs={{0,4},{1,5},{2,6},{3,7},{4,0},{5,1},{6,2},{7,3},{8,12},{9,13},{10,... | collective-permute-start | bytes 393224 | tf_op jit(solution)/shard_map/ppermute | solution.py:457
  50.8 5.9 %collective-permute-start.14 = (bf16[4,128,128]{2,1,0:T(8,128)(2,1)S(1)}, bf16[4,128,128]{2,1,0:T(8,128)(2,1)S(1)}, u32[]{:S(2)}, u32[]{:S(2)}) collective-permute-start(bf16[4,128,128]{2,1,0:T(8,128)(2,1)S(1)} %get-tuple-element.73), channel_id=1, source_target_pairs={{0,6},{1,7},{2,4},{3,5},{4,2},{5,3},{6,0},{7,1},{8,14},{9,15},{10,... | collective-permute-start | bytes 393224 | tf_op jit(solution)/shard_map/ppermute | solution.py:457
  57.4 3.2 %collective-permute-start.15 = (bf16[128,2048]{1,0:T(8,128)(2,1)S(1)}, bf16[128,2048]{1,0:T(8,128)(2,1)S(1)}, u32[]{:S(2)}, u32[]{:S(2)}) collective-permute-start(bf16[128,2048]{1,0:T(8,128)(2,1)S(1)} %get-tuple-element.76), channel_id=1, source_target_pairs={{0,1},{1,0},{2,3},{3,2},{4,5},{5,4},{6,7},{7,6},{8,9},{9,8},{10,11... | collective-permute-start | bytes 1572872 | tf_op jit(solution)/shard_map/ppermute | solution.py:451
  57.5 3.1 %collective-permute-start.16 = (bf16[16,128,128]{2,1,0:T(8,128)(2,1)S(1)}, bf16[16,128,128]{2,1,0:T(8,128)(2,1)S(1)}, u32[]{:S(2)}, u32[]{:S(2)}) collective-permute-start(bf16[16,128,128]{2,1,0:T(8,128)(2,1)S(1)} %get-tuple-element.78), channel_id=1, source_target_pairs={{0,1},{1,0},{2,3},{3,2},{4,5},{5,4},{6,7},{7,6},{8,9},{9,8},{10,11... | collective-permute-start | bytes 1572872 | tf_op jit(solution)/shard_map/ppermute | solution.py:451
  58.0 13.1 %collective-permute-start.19 = (bf16[4,128,128]{2,1,0:T(8,128)(2,1)S(1)}, bf16[4,128,128]{2,1,0:T(8,128)(2,1)S(1)}, u32[]{:S(2)}, u32[]{:S(2)}) collective-permute-start(bf16[4,128,128]{2,1,0:T(8,128)(2,1)S(1)} %get-tuple-element.79.rest_4_), channel_id=1, source_target_pairs={{16,0},{24,8},{17,1},{25,9},{18,2},{26,10},{19,3},{27,11},{20,4},{... | collective-permute-start | bytes 393224 | tf_op jit(solution)/shard_map/ppermute | solution.py:477
  59.2 11.9 %collective-permute-start.18 = (bf16[4,128,128]{2,1,0:T(8,128)(2,1)S(1)}, bf16[4,128,128]{2,1,0:T(8,128)(2,1)S(1)}, u32[]{:S(2)}, u32[]{:S(2)}) collective-permute-start(bf16[4,128,128]{2,1,0:T(8,128)(2,1)S(1)} %get-tuple-element.79.rest_4_), channel_id=1, source_target_pairs={{8,0},{16,8},{24,16},{9,1},{17,9},{25,17},{10,2},{18,10},{26,18},{... | collective-permute-start | bytes 393224 | tf_op jit(solution)/shard_map/ppermute | solution.py:477
  67.5 16.3 %collective-permute-start.17 = (bf16[16,128,128]{2,1,0:T(8,128)(2,1)S(1)}, bf16[16,128,128]{2,1,0:T(8,128)(2,1)S(1)}, u32[]{:S(2)}, u32[]{:S(2)}) collective-permute-start(bf16[16,128,128]{2,1,0:T(8,128)(2,1)S(1)} %get-tuple-element.84), channel_id=1, source_target_pairs={{0,1},{1,0},{2,3},{3,2},{4,5},{5,4},{6,7},{7,6},{8,9},{9,8},{10,11... | collective-permute-start | bytes 1572872 | tf_op jit(solution)/shard_map/ppermute | solution.py:451
  67.6 16.2 %collective-permute-start.27 = (bf16[128,2048]{1,0:T(8,128)(2,1)S(1)}, bf16[128,2048]{1,0:T(8,128)(2,1)S(1)}, u32[]{:S(2)}, u32[]{:S(2)}) collective-permute-start(bf16[128,2048]{1,0:T(8,128)(2,1)S(1)} %get-tuple-element.89), channel_id=1, source_target_pairs={{0,1},{1,0},{2,3},{3,2},{4,5},{5,4},{6,7},{7,6},{8,9},{9,8},{10,11... | collective-permute-start | bytes 1572872 | tf_op jit(solution)/shard_map/ppermute | solution.py:451
  72.0 6.4 %collective-permute-start.21 = (bf16[4,128,128]{2,1,0:T(8,128)(2,1)S(1)}, bf16[4,128,128]{2,1,0:T(8,128)(2,1)S(1)}, u32[]{:S(2)}, u32[]{:S(2)}) collective-permute-start(bf16[4,128,128]{2,1,0:T(8,128)(2,1)S(1)} %get-tuple-element.86), channel_id=1, source_target_pairs={{0,2},{1,3},{2,0},{3,1},{4,6},{5,7},{6,4},{7,5},{8,10},{9,11},{10,... | collective-permute-start | bytes 393224 | tf_op jit(solution)/shard_map/ppermute | solution.py:457
  72.8 5.6 %collective-permute-start.23 = (bf16[4,128,128]{2,1,0:T(8,128)(2,1)S(1)}, bf16[4,128,128]{2,1,0:T(8,128)(2,1)S(1)}, u32[]{:S(2)}, u32[]{:S(2)}) collective-permute-start(bf16[4,128,128]{2,1,0:T(8,128)(2,1)S(1)} %get-tuple-element.87), channel_id=1, source_target_pairs={{0,4},{1,5},{2,6},{3,7},{4,0},{5,1},{6,2},{7,3},{8,12},{9,13},{10,... | collective-permute-start | bytes 393224 | tf_op jit(solution)/shard_map/ppermute | solution.py:457
  74.3 6.1 %collective-permute-start.25 = (bf16[4,128,128]{2,1,0:T(8,128)(2,1)S(1)}, bf16[4,128,128]{2,1,0:T(8,128)(2,1)S(1)}, u32[]{:S(2)}, u32[]{:S(2)}) collective-permute-start(bf16[4,128,128]{2,1,0:T(8,128)(2,1)S(1)} %get-tuple-element.88), channel_id=1, source_target_pairs={{0,6},{1,7},{2,4},{3,5},{4,2},{5,3},{6,0},{7,1},{8,14},{9,15},{10,... | collective-permute-start | bytes 393224 | tf_op jit(solution)/shard_map/ppermute | solution.py:457
  78.4 2.1 %collective-permute-start.20 = (bf16[4,128,128]{2,1,0:T(8,128)(2,1)S(1)}, bf16[4,128,128]{2,1,0:T(8,128)(2,1)S(1)}, u32[]{:S(2)}, u32[]{:S(2)}) collective-permute-start(bf16[4,128,128]{2,1,0:T(8,128)(2,1)S(1)} %get-tuple-element.85.rest_0_), channel_id=1, source_target_pairs={{0,1},{1,0},{2,3},{3,2},{4,5},{5,4},{6,7},{7,6},{8,9},{9,8},{10,11... | collective-permute-start | bytes 393224 | tf_op jit(solution)/shard_map/ppermute | solution.py:451
  78.4 5.3 %collective-permute-start.22 = (bf16[4,128,128]{2,1,0:T(8,128)(2,1)S(1)}, bf16[4,128,128]{2,1,0:T(8,128)(2,1)S(1)}, u32[]{:S(2)}, u32[]{:S(2)}) collective-permute-start(bf16[4,128,128]{2,1,0:T(8,128)(2,1)S(1)} %collective-permute-done.21.rest_1_), channel_id=1, source_target_pairs={{0,1},{1,0},{2,3},{3,2},{4,5},{5,4},{6,7},{7,6},{8,9},{9,8},{10,11... | collective-permute-start | bytes 393224 | tf_op jit(solution)/shard_map/ppermute | solution.py:451
  80.5 3.3 %collective-permute-start.24 = (bf16[4,128,128]{2,1,0:T(8,128)(2,1)S(1)}, bf16[4,128,128]{2,1,0:T(8,128)(2,1)S(1)}, u32[]{:S(2)}, u32[]{:S(2)}) collective-permute-start(bf16[4,128,128]{2,1,0:T(8,128)(2,1)S(1)} %collective-permute-done.23.rest_2_), channel_id=1, source_target_pairs={{0,1},{1,0},{2,3},{3,2},{4,5},{5,4},{6,7},{7,6},{8,9},{9,8},{10,11... | collective-permute-start | bytes 393224 | tf_op jit(solution)/shard_map/ppermute | solution.py:451
  80.5 3.3 %collective-permute-start.26 = (bf16[4,128,128]{2,1,0:T(8,128)(2,1)S(1)}, bf16[4,128,128]{2,1,0:T(8,128)(2,1)S(1)}, u32[]{:S(2)}, u32[]{:S(2)}) collective-permute-start(bf16[4,128,128]{2,1,0:T(8,128)(2,1)S(1)} %collective-permute-done.25.rest_3_), channel_id=1, source_target_pairs={{0,1},{1,0},{2,3},{3,2},{4,5},{5,4},{6,7},{7,6},{8,9},{9,8},{10,11... | collective-permute-start | bytes 393224 | tf_op jit(solution)/shard_map/ppermute | solution.py:451

commit v15 on v14

--- a/solution.py
+++ b/solution.py
@@ -173,7 +173,7 @@
 
     @pl.when(step == 0)
     def _():
-        for n, state in enumerate(incoming):
+        for n, state in enumerate(incoming[::-1]):
             owned = state.shape[0]
             came[pl.ds((chip ^ n) * owned, owned)] = state[...]
             sent_in[pl.ds((chip ^ n) * owned, owned)] = state[...]
@@ -278,7 +278,7 @@
         chip = place[2] >> 1
         by_far = jnp.where(core == 0, same(early_e, late_e), 1.0)
         by_late = jnp.where(core == 0, same(early_e, late_b), 0.0)
-        for n, state in enumerate(outgoing):
+        for n, state in enumerate(outgoing[::-1]):
             owned = state.shape[0]
             at = pl.ds((chip ^ n) * owned, owned)
             came[at] = (
@@ -325,7 +325,7 @@
 
 
 def total_kernel(forward, unit, members, passed, lens, place, *rest):
-    states, total, held = rest[:members], rest[members + passed], rest[-1]
+    states, total, held = rest[:members][::-1], rest[members + passed], rest[-1]
     chip = place[2] >> 1
     for n, state in enumerate(states):
         held[chip ^ n] = state[...]
@@ -344,7 +344,7 @@
 
 
 def prefix_kernel(forward, unit, members, unread, lens, place, *rest):
-    states, outs, (held, sums) = rest[:members], rest[-members - 2 : -2], rest[-2:]
+    states, outs, (held, sums) = rest[:members][::-1], rest[-members - 2 : -2], rest[-2:]
     others = rest[members + unread : -members - 2]
     chip = place[2] >> 1
     for n, state in enumerate(states):
@@ -466,7 +466,7 @@
             [single] + [untouched] * len(along),
             [owned_bf] + [jax.ShapeDtypeStruct(array.shape, array.dtype) for array in along],
             [buffer],
-            [*came, *along],
+            [*came[::-1], *along],
             combining,
             name + "_total",
             aliases={2 + chips + j: 1 + j for j in range(len(along))},
@@ -485,7 +485,7 @@
             [single] * chips,
             [owned_bf] * chips,
             [buffer, buffer],
-            [*came, *after, *others],
+            [*came[::-1], *after, *others],
             combining,
             name + "_prefix",
         )
@@ -580,7 +580,7 @@
         + [one_owner] * chips,
         [token_bf] + [narrow_bf] * 3 + [half_bf] * 4 + [owned_bf] * chips,
         [half_states],
-        (head_fq, turned, out_grad, mate_g, part, *chip_in),
+        (head_fq, turned, out_grad, mate_g, part, *chip_in[::-1]),
         (8 * product, 16 * array, 2 * half * count * DH),
         "normed",
     )
@@ -630,7 +630,7 @@
             extra_outs + [tokens(parity)] * 2,
             shapes,
             [half_states],
-            (keys, values, gk_part, gv_part, late[parity], *outgoing[parity], *args),
+            (keys, values, gk_part, gv_part, late[parity], *outgoing[parity][::-1], *args),
             (2 * product, 9 * array, half * count * DH),
             f"grads_last_{parity}",
             aliases=aliases,

time: 87.5 us -> 87.3 us (level)
  transfers between devices with their start and end apart: 28 -> 28, of which waited for: 11 -> 12; matrix products, arithmetic and copies ran while one was open for 0% -> 0% of each run, Pallas kernels for 22% -> 22%
where the time goes in v15:
time: 87.3 us; the launch traced here: 86.1 us
  Pallas kernels  32 us (37%)
  starting transfers between devices  28.4 us (33%)
  waiting for transfers between devices  24.6 us (28%)
  between operations  0.91 us (1%)
    pallas_call x12, Pallas kernels, run(): pl.pallas_call(kernel, grid_spec=pltpu.PrefetchScalarGridSpec(num_scalar_...  32 us
    ppermute x12, waiting for transfers between devices, exchange(): came[n] = lax.ppermute(states[n], LAYER, pairs)  21.1 us
    ppermute x12, starting transfers between devices, exchange(): came[n] = lax.ppermute(states[n], LAYER, pairs)  15.1 us
    ppermute x4, starting transfers between devices, reach_out(): others.insert(0, lax.ppermute(total, 'z', pairs))  10.6 us
    ppermute x4, waiting for transfers between devices, reach_out(): others.insert(0, lax.ppermute(total, 'z', pairs))  3.48 us
    ppermute x12, starting transfers between devices, swap(): return lax.ppermute(state, LAYER, [(i, i ^ 1) for i in range(members)])  2.81 us
  transfers between devices with their start and end apart: 28, of which 12 were waited for; matrix products, arithmetic and copies ran while one was open for 0% of the time, Pallas kernels for 22%

profile of v15, /device:TPU:0, one launch (start us, length us, event | category | flops | bytes accessed | tf_op | source)
XLA Modules:
  0.0 86.1 jit_solution(9838896490923882060)
XLA Ops:
  0.6 0.1 pad_add_fusion.place
  0.7 3.1 %tail_mate.1 = (bf16[16,128,128]{2,1,0:T(8,128)(2,1)S(1)}, bf16[3,128,2048]{2,1,0:T(8,128)(2,1)S(1)}, bf16[128,2048]{1,0:T(8,128)(2,1)S(1)}) custom-call(s32[8]{0:T(128)} %lens.23, s32[3]{0:T(128)S(1)} %pad_add_fusion.place, bf16[128,4096]{1,0:T(8,128)(2,1)} %k.11, bf16[128,4096]{1,0:T(8,128)(2,1)} %v.11, bf16[128,4096]{1,0:T(8,128)(2,1)} %q.3, ...), custom_call_target="tpu_custom_call" | custom-call | flops 67108864 | bytes 1572864 | tf_op jit(solution)/shard_map/tail_mate/pallas_call | solution.py:423
  3.8 0.0 copy-start.4
  3.8 0.5 collective-permute-start
  4.3 2.7 %tail_own.1.rest_5_ = bf16[16,128,128]{2,1,0:T(8,128)(2,1)S(1)} custom-call(s32[8]{0:T(128)} %lens.23, s32[3]{0:T(128)S(1)} %pad_add_fusion.place, bf16[128,4096]{1,0:T(8,128)(2,1)} %k.11, bf16[128,4096]{1,0:T(8,128)(2,1)} %v.11), custom_call_target="tpu_custom_call" | custom-call | flops 67108864 | bytes 1572864 | tf_op jit(solution)/shard_map/tail_own/pallas_call | solution.py:423
  7.1 0.0 copy-start
  7.1 0.0 copy-start.1
  7.1 0.0 copy-start.2
  7.1 0.8 carried_chip.1
  7.9 0.1 collective-permute-start.1
  8.0 3.9 %collective-permute-start.2 = (bf16[4,128,128]{2,1,0:T(8,128)(2,1)S(1)}, bf16[4,128,128]{2,1,0:T(8,128)(2,1)S(1)}, u32[]{:S(2)}, u32[]{:S(2)}) collective-permute-start(bf16[4,128,128]{2,1,0:T(8,128)(2,1)S(1)} %get-tuple-element.56), channel_id=1, source_target_pairs={{0,6},{1,7},{2,4},{3,5},{4,2},{5,3},{6,0},{7,1},{8,14},{9,15},{10,... | collective-permute-start | bytes 393224 | tf_op jit(solution)/shard_map/ppermute | solution.py:457
  11.9 0.5 collective-permute-start.3
  12.4 0.0 collective-permute-start.4
  12.5 3.7 %collective-permute-done.2.rest_0_ = bf16[4,128,128]{2,1,0:T(8,128)(2,1)S(1)} collective-permute-done((bf16[4,128,128]{2,1,0:T(8,128)(2,1)S(1)}, bf16[4,128,128]{2,1,0:T(8,128)(2,1)S(1)}, u32[]{:S(2)}, u32[]{:S(2)}) %collective-permute-start.2) | collective-permute-done | bytes 131104 | tf_op jit(solution)/shard_map/ppermute | solution.py:457
  16.2 2.5 %collective-permute-done.3.rest_1_ = bf16[4,128,128]{2,1,0:T(8,128)(2,1)S(1)} collective-permute-done((bf16[4,128,128]{2,1,0:T(8,128)(2,1)S(1)}, bf16[4,128,128]{2,1,0:T(8,128)(2,1)S(1)}, u32[]{:S(2)}, u32[]{:S(2)}) %collective-permute-start.3) | collective-permute-done | bytes 131104 | tf_op jit(solution)/shard_map/ppermute | solution.py:457
  18.7 0.7 carried_total.1
  19.4 0.1 collective-permute-start.6
  19.5 0.5 collective-permute-start.5
  20.0 4.5 %collective-permute-start.8 = (bf16[4,128,128]{2,1,0:T(8,128)(2,1)S(1)}, bf16[4,128,128]{2,1,0:T(8,128)(2,1)S(1)}, u32[]{:S(2)}, u32[]{:S(2)}) collective-permute-start(bf16[4,128,128]{2,1,0:T(8,128)(2,1)S(1)} %get-tuple-element.64), channel_id=1, source_target_pairs={{0,16},{8,24},{1,17},{9,25},{2,18},{10,26},{3,19},{11,27},{4,20},{... | collective-permute-start | bytes 393224 | tf_op jit(solution)/shard_map/ppermute | solution.py:477
  24.5 3.5 %collective-permute-start.7 = (bf16[4,128,128]{2,1,0:T(8,128)(2,1)S(1)}, bf16[4,128,128]{2,1,0:T(8,128)(2,1)S(1)}, u32[]{:S(2)}, u32[]{:S(2)}) collective-permute-start(bf16[4,128,128]{2,1,0:T(8,128)(2,1)S(1)} %get-tuple-element.64), channel_id=1, source_target_pairs={{0,8},{8,16},{16,24},{1,9},{9,17},{17,25},{2,10},{10,18},{18,26},{... | collective-permute-start | bytes 393224 | tf_op jit(solution)/shard_map/ppermute | solution.py:477
  28.0 0.0 collective-permute-done.1.mate
  28.0 4.3 %within_chip.1 = (f32[256,2048]{1,0:T(8,128)S(1)}, bf16[256,2048]{1,0:T(8,128)(2,1)S(1)}, bf16[16,256,256]{2,1,0:T(8,128)(2,1)S(1)}) custom-call(s32[8]{0:T(128)S(1)} %copy-done.4, s32[3]{0:T(128)S(1)} %pad_add_fusion.place, bf16[128,4096]{1,0:T(8,128)(2,1)S(1)} %copy-done.2, bf16[128,4096]{1,0:T(8,128)(2,1)S(1)} %copy-done, ...), custom_call_target="tpu_custom_call" | custom-call | flops 671088640 | bytes 7340032 | tf_op jit(solution)/shard_map/within_chip/pallas_call | solution.py:423
  32.4 0.0 copy-start.3
  32.4 0.0 collective-permute-done.6.rest_5_.rest_3_
  32.4 0.9 %carried_prefix.1 = (bf16[4,128,128]{2,1,0:T(8,128)(2,1)S(1)}, bf16[4,128,128]{2,1,0:T(8,128)(2,1)S(1)}, bf16[4,128,128]{2,1,0:T(8,128)(2,1)S(1)}, bf16[4,128,128]{2,1,0:T(8,128)(2,1)S(1)}) custom-call(s32[8]{0:T(128)S(1)} %copy-done.4, s32[3]{0:T(128)S(1)} %pad_add_fusion.place, bf16[4,128,128]{2,1,0:T(8,128)(2,1)S(1)} %collective-permute-done.2.rest_0_, ...), custom_call_target="tpu_custom_call" | custom-call | flops 1048576 | bytes 1048576 | tf_op jit(solution)/shard_map/carried_prefix/pallas_call | solution.py:423
  33.3 2.4 %collective-permute-start.9 = (bf16[4,128,128]{2,1,0:T(8,128)(2,1)S(1)}, bf16[4,128,128]{2,1,0:T(8,128)(2,1)S(1)}, u32[]{:S(2)}, u32[]{:S(2)}) collective-permute-start(bf16[4,128,128]{2,1,0:T(8,128)(2,1)S(1)} %get-tuple-element.65), channel_id=1, source_target_pairs={{0,6},{1,7},{2,4},{3,5},{4,2},{5,3},{6,0},{7,1},{8,14},{9,15},{10,... | collective-permute-start | bytes 393224 | tf_op jit(solution)/shard_map/ppermute | solution.py:457
  35.7 0.5 collective-permute-start.10
  36.3 0.6 collective-permute-start.11
  36.8 0.0 collective-permute-done.5.mate_g
  36.8 3.8 %collective-permute-done.9.rest_0_ = bf16[4,128,128]{2,1,0:T(8,128)(2,1)S(1)} collective-permute-done((bf16[4,128,128]{2,1,0:T(8,128)(2,1)S(1)}, bf16[4,128,128]{2,1,0:T(8,128)(2,1)S(1)}, u32[]{:S(2)}, u32[]{:S(2)}) %collective-permute-start.9) | collective-permute-done | bytes 131104 | tf_op jit(solution)/shard_map/ppermute | solution.py:457
  40.7 1.3 %collective-permute-done.10.rest_1_ = bf16[4,128,128]{2,1,0:T(8,128)(2,1)S(1)} collective-permute-done((bf16[4,128,128]{2,1,0:T(8,128)(2,1)S(1)}, bf16[4,128,128]{2,1,0:T(8,128)(2,1)S(1)}, u32[]{:S(2)}, u32[]{:S(2)}) %collective-permute-start.10) | collective-permute-done | bytes 131104 | tf_op jit(solution)/shard_map/ppermute | solution.py:457
  42.0 0.1 collective-permute-done.11.rest_2_
  42.0 5.3 %normed.1 = (bf16[128,4096]{1,0:T(8,128)(2,1)}, bf16[128,2048]{1,0:T(8,128)(2,1)S(1)}, bf16[128,2048]{1,0:T(8,128)(2,1)S(1)}, bf16[128,2048]{1,0:T(8,128)(2,1)S(...) custom-call(s32[8]{0:T(128)S(1)} %copy-done.4, ...), custom_call_target="tpu_custom_call" | custom-call | flops 536870912 | bytes 8388608 | tf_op jit(solution)/shard_map/normed/pallas_call | solution.py:423
  47.3 2.3 %collective-permute-start.12 = (bf16[4,128,128]{2,1,0:T(8,128)(2,1)S(1)}, bf16[4,128,128]{2,1,0:T(8,128)(2,1)S(1)}, u32[]{:S(2)}, u32[]{:S(2)}) collective-permute-start(bf16[4,128,128]{2,1,0:T(8,128)(2,1)S(1)} %get-tuple-element.70), channel_id=1, source_target_pairs={{0,6},{1,7},{2,4},{3,5},{4,2},{5,3},{6,0},{7,1},{8,14},{9,15},{10,... | collective-permute-start | bytes 393224 | tf_op jit(solution)/shard_map/ppermute | solution.py:457
  49.7 0.5 collective-permute-start.13
  50.2 0.6 collective-permute-start.14
  50.8 3.4 %collective-permute-done.12.rest_0_ = bf16[4,128,128]{2,1,0:T(8,128)(2,1)S(1)} collective-permute-done((bf16[4,128,128]{2,1,0:T(8,128)(2,1)S(1)}, bf16[4,128,128]{2,1,0:T(8,128)(2,1)S(1)}, u32[]{:S(2)}, u32[]{:S(2)}) %collective-permute-start.12) | collective-permute-done | bytes 131104 | tf_op jit(solution)/shard_map/ppermute | solution.py:457
  54.3 1.6 %collective-permute-done.13.rest_1_ = bf16[4,128,128]{2,1,0:T(8,128)(2,1)S(1)} collective-permute-done((bf16[4,128,128]{2,1,0:T(8,128)(2,1)S(1)}, bf16[4,128,128]{2,1,0:T(8,128)(2,1)S(1)}, u32[]{:S(2)}, u32[]{:S(2)}) %collective-permute-start.13) | collective-permute-done | bytes 131104 | tf_op jit(solution)/shard_map/ppermute | solution.py:457
  55.8 0.1 collective-permute-done.14.rest_2_
  55.9 0.7 future_total.1
  56.6 0.1 collective-permute-start.15
  56.7 0.5 collective-permute-start.16
  57.2 1.3 %collective-permute-start.19 = (bf16[4,128,128]{2,1,0:T(8,128)(2,1)S(1)}, bf16[4,128,128]{2,1,0:T(8,128)(2,1)S(1)}, u32[]{:S(2)}, u32[]{:S(2)}) collective-permute-start(bf16[4,128,128]{2,1,0:T(8,128)(2,1)S(1)} %get-tuple-element.79.rest_4_), channel_id=1, source_target_pairs={{16,0},{24,8},{17,1},{25,9},{18,2},{26,10},{19,3},{27,11},{20,4},{... | collective-permute-start | bytes 393224 | tf_op jit(solution)/shard_map/ppermute | solution.py:477
  58.5 1.3 %collective-permute-start.18 = (bf16[4,128,128]{2,1,0:T(8,128)(2,1)S(1)}, bf16[4,128,128]{2,1,0:T(8,128)(2,1)S(1)}, u32[]{:S(2)}, u32[]{:S(2)}) collective-permute-start(bf16[4,128,128]{2,1,0:T(8,128)(2,1)S(1)} %get-tuple-element.79.rest_4_), channel_id=1, source_target_pairs={{8,0},{16,8},{24,16},{9,1},{17,9},{25,17},{10,2},{18,10},{26,18},{... | collective-permute-start | bytes 393224 | tf_op jit(solution)/shard_map/ppermute | solution.py:477
  59.8 0.0 collective-permute-done.15.other_ga
  59.8 0.0 collective-permute-done.16.rest_1_
  59.8 6.9 %grads_within.1 = (bf16[128,4096]{1,0:T(8,128)(2,1)}, f32[128,4096]{1,0:T(8,128)S(1)}, f32[128,4096]{1,0:T(8,128)S(1)}, bf16[128,2048]{1,0:T(8,128)(2,1)S(1)}, bf16[16,128,128]{2,1,0:T(8,128)(2,1)S(1)}) custom-call(s32[8]{0:T(128)S(1)} %copy-done.4, s32[3]{0:T(128)S(1)} %pad_add_fusion.place, ...), custom_call_target="tpu_custom_call", output_to_operand_aliasing={{3}: (12, {}), {4}: (13, {})} | custom-call | flops 1073741824 | bytes 11534336 | tf_op jit(solution)/shard_map/grads_within/pallas_call | solution.py:423
  66.7 0.1 collective-permute-start.17
  66.8 0.4 collective-permute-start.27
  67.2 3.5 %collective-permute-done.19.rest_6_ = bf16[4,128,128]{2,1,0:T(8,128)(2,1)S(1)} collective-permute-done((bf16[4,128,128]{2,1,0:T(8,128)(2,1)S(1)}, bf16[4,128,128]{2,1,0:T(8,128)(2,1)S(1)}, u32[]{:S(2)}, u32[]{:S(2)}) %collective-permute-start.19) | collective-permute-done | bytes 131104 | tf_op jit(solution)/shard_map/ppermute | solution.py:477
  70.7 0.0 collective-permute-done.18.rest_5_
  70.7 0.9 %future_prefix.1 = (bf16[4,128,128]{2,1,0:T(8,128)(2,1)S(1)}, bf16[4,128,128]{2,1,0:T(8,128)(2,1)S(1)}, bf16[4,128,128]{2,1,0:T(8,128)(2,1)S(1)}, bf16[4,128,128]{2,1,0:T(8,128)(2,1)S(1)}) custom-call(s32[8]{0:T(128)S(1)} %copy-done.4, s32[3]{0:T(128)S(1)} %pad_add_fusion.place, bf16[4,128,128]{2,1,0:T(8,128)(2,1)S(1)} %collective-permute-done.12.rest_0_, ...), custom_call_target="tpu_custom_call" | custom-call | flops 1048576 | bytes 1048576 | tf_op jit(solution)/shard_map/future_prefix/pallas_call | solution.py:423
  71.6 2.4 %collective-permute-start.20 = (bf16[4,128,128]{2,1,0:T(8,128)(2,1)S(1)}, bf16[4,128,128]{2,1,0:T(8,128)(2,1)S(1)}, u32[]{:S(2)}, u32[]{:S(2)}) collective-permute-start(bf16[4,128,128]{2,1,0:T(8,128)(2,1)S(1)} %get-tuple-element.85), channel_id=1, source_target_pairs={{0,6},{1,7},{2,4},{3,5},{4,2},{5,3},{6,0},{7,1},{8,14},{9,15},{10,... | collective-permute-start | bytes 393224 | tf_op jit(solution)/shard_map/ppermute | solution.py:457
  74.0 0.5 collective-permute-start.22
  74.6 0.6 collective-permute-start.24
  75.1 3.3 %collective-permute-done.20.rest_0_ = bf16[4,128,128]{2,1,0:T(8,128)(2,1)S(1)} collective-permute-done((bf16[4,128,128]{2,1,0:T(8,128)(2,1)S(1)}, bf16[4,128,128]{2,1,0:T(8,128)(2,1)S(1)}, u32[]{:S(2)}, u32[]{:S(2)}) %collective-permute-start.20) | collective-permute-done | bytes 131104 | tf_op jit(solution)/shard_map/ppermute | solution.py:457
  78.4 1.3 %collective-permute-done.22.rest_1_ = bf16[4,128,128]{2,1,0:T(8,128)(2,1)S(1)} collective-permute-done((bf16[4,128,128]{2,1,0:T(8,128)(2,1)S(1)}, bf16[4,128,128]{2,1,0:T(8,128)(2,1)S(1)}, u32[]{:S(2)}, u32[]{:S(2)}) %collective-permute-start.22) | collective-permute-done | bytes 131104 | tf_op jit(solution)/shard_map/ppermute | solution.py:457
  79.7 0.1 collective-permute-done.24.rest_2_
  79.8 0.5 collective-permute-start.23
  80.3 0.0 collective-permute-done.26.rest_3_
  80.3 0.1 collective-permute-start.25
  80.3 2.8 %grads_last_0.1 = (bf16[128,4096]{1,0:T(8,128)(2,1)}, bf16[128,4096]{1,0:T(8,128)(2,1)}) custom-call(s32[8]{0:T(128)S(1)} %copy-done.4, s32[3]{0:T(128)S(1)} %pad_add_fusion.place, bf16[128,4096]{1,0:T(8,128)(2,1)S(1)} %copy-done, bf16[128,4096]{1,0:T(8,128)(2,1)S(1)} %copy-done.1, f32[128,4096]{1,0:T(8,128)S(1)} %get-tuple-element.82.rest_4_.gk_part, ...), custom_call_target="tpu_custom_call" | custom-call | flops 134217728 | bytes 4718592 | tf_op jit(solution)/shard_map/grads_last_0/pallas_call | solution.py:423
  83.1 0.0 collective-permute-done.17.late
  83.1 2.9 %grads_last_1.1 = (bf16[128,4096]{1,0:T(8,128)(2,1)}, bf16[128,4096]{1,0:T(8,128)(2,1)}, bf16[128,4096]{1,0:T(8,128)(2,1)}) custom-call(s32[8]{0:T(128)S(1)} %copy-done.4, s32[3]{0:T(128)S(1)} %pad_add_fusion.place, bf16[128,4096]{1,0:T(8,128)(2,1)S(1)} %copy-done, ...), custom_call_target="tpu_custom_call", output_to_operand_aliasing={{0}: (12, {}), {1}: (13, {}), {2}: (14, {})} | custom-call | flops 134217728 | bytes 4718592 | tf_op jit(solution)/shard_map/grads_last_1/pallas_call | solution.py:423
  (15 shorter events, 0.0 us)
Async XLA Ops:
  3.8 3.3 %copy-start.4 = (s32[8]{0:T(128)S(1)}, s32[8]{0:T(128)}, u32[]{:S(2)}) copy-start(s32[8]{0:T(128)} %lens.23) | copy-start | bytes 100
  3.8 3.2 %collective-permute-start = (bf16[16,128,128]{2,1,0:T(8,128)(2,1)S(1)}, bf16[16,128,128]{2,1,0:T(8,128)(2,1)S(1)}, u32[]{:S(2)}, u32[]{:S(2)}) collective-permute-start(bf16[16,128,128]{2,1,0:T(8,128)(2,1)S(1)} %get-tuple-element.51), channel_id=1, source_target_pairs={{0,1},{1,0},{2,3},{3,2},{4,5},{5,4},{6,7},{7,6},{8,9},{9,8},{10,11... | collective-permute-start | bytes 1572872 | tf_op jit(solution)/shard_map/ppermute | solution.py:451
  7.1 20.9 %copy-start = (bf16[128,4096]{1,0:T(8,128)(2,1)S(1)}, bf16[128,4096]{1,0:T(8,128)(2,1)}, u32[]{:S(2)}) copy-start(bf16[128,4096]{1,0:T(8,128)(2,1)} %k.11) | copy-start | bytes 3145732
  7.1 20.9 %copy-start.1 = (bf16[128,4096]{1,0:T(8,128)(2,1)S(1)}, bf16[128,4096]{1,0:T(8,128)(2,1)}, u32[]{:S(2)}) copy-start(bf16[128,4096]{1,0:T(8,128)(2,1)} %v.11) | copy-start | bytes 3145732
  7.1 20.9 %copy-start.2 = (bf16[128,4096]{1,0:T(8,128)(2,1)S(1)}, bf16[128,4096]{1,0:T(8,128)(2,1)}, u32[]{:S(2)}) copy-start(bf16[128,4096]{1,0:T(8,128)(2,1)} %q.3) | copy-start | bytes 3145732
  7.9 20.1 %collective-permute-start.1 = (bf16[3,128,2048]{2,1,0:T(8,128)(2,1)S(1)}, bf16[3,128,2048]{2,1,0:T(8,128)(2,1)S(1)}, u32[]{:S(2)}, u32[]{:S(2)}) collective-permute-start(bf16[3,128,2048]{2,1,0:T(8,128)(2,1)S(1)} %get-tuple-element.53), channel_id=1, source_target_pairs={{0,1},{1,0},{2,3},{3,2},{4,5},{5,4},{6,7},{7,6},{8,9},{9,8},{10,11... | collective-permute-start | bytes 4718600 | tf_op jit(solution)/shard_map/ppermute | solution.py:451
  8.0 8.2 %collective-permute-start.2 = (bf16[4,128,128]{2,1,0:T(8,128)(2,1)S(1)}, bf16[4,128,128]{2,1,0:T(8,128)(2,1)S(1)}, u32[]{:S(2)}, u32[]{:S(2)}) collective-permute-start(bf16[4,128,128]{2,1,0:T(8,128)(2,1)S(1)} %get-tuple-element.56), channel_id=1, source_target_pairs={{0,6},{1,7},{2,4},{3,5},{4,2},{5,3},{6,0},{7,1},{8,14},{9,15},{10,... | collective-permute-start | bytes 393224 | tf_op jit(solution)/shard_map/ppermute | solution.py:457
  11.9 6.8 %collective-permute-start.3 = (bf16[4,128,128]{2,1,0:T(8,128)(2,1)S(1)}, bf16[4,128,128]{2,1,0:T(8,128)(2,1)S(1)}, u32[]{:S(2)}, u32[]{:S(2)}) collective-permute-start(bf16[4,128,128]{2,1,0:T(8,128)(2,1)S(1)} %get-tuple-element.57), channel_id=1, source_target_pairs={{0,4},{1,5},{2,6},{3,7},{4,0},{5,1},{6,2},{7,3},{8,12},{9,13},{10,... | collective-permute-start | bytes 393224 | tf_op jit(solution)/shard_map/ppermute | solution.py:457
  12.4 6.3 %collective-permute-start.4 = (bf16[4,128,128]{2,1,0:T(8,128)(2,1)S(1)}, bf16[4,128,128]{2,1,0:T(8,128)(2,1)S(1)}, u32[]{:S(2)}, u32[]{:S(2)}) collective-permute-start(bf16[4,128,128]{2,1,0:T(8,128)(2,1)S(1)} %get-tuple-element.58), channel_id=1, source_target_pairs={{0,2},{1,3},{2,0},{3,1},{4,6},{5,7},{6,4},{7,5},{8,10},{9,11},{10,... | collective-permute-start | bytes 393224 | tf_op jit(solution)/shard_map/ppermute | solution.py:457
  19.4 13.0 %collective-permute-start.6 = (bf16[16,128,128]{2,1,0:T(8,128)(2,1)S(1)}, bf16[16,128,128]{2,1,0:T(8,128)(2,1)S(1)}, u32[]{:S(2)}, u32[]{:S(2)}) collective-permute-start(bf16[16,128,128]{2,1,0:T(8,128)(2,1)S(1)} %get-tuple-element.63), channel_id=1, source_target_pairs={{0,1},{1,0},{2,3},{3,2},{4,5},{5,4},{6,7},{7,6},{8,9},{9,8},{10,11... | collective-permute-start | bytes 1572872 | tf_op jit(solution)/shard_map/ppermute | solution.py:451
  19.5 17.3 %collective-permute-start.5 = (bf16[128,2048]{1,0:T(8,128)(2,1)S(1)}, bf16[128,2048]{1,0:T(8,128)(2,1)S(1)}, u32[]{:S(2)}, u32[]{:S(2)}) collective-permute-start(bf16[128,2048]{1,0:T(8,128)(2,1)S(1)} %get-tuple-element.61), channel_id=1, source_target_pairs={{0,1},{1,0},{2,3},{3,2},{4,5},{5,4},{6,7},{7,6},{8,9},{9,8},{10,11... | collective-permute-start | bytes 1572872 | tf_op jit(solution)/shard_map/ppermute | solution.py:451
  20.0 12.4 %collective-permute-start.8 = (bf16[4,128,128]{2,1,0:T(8,128)(2,1)S(1)}, bf16[4,128,128]{2,1,0:T(8,128)(2,1)S(1)}, u32[]{:S(2)}, u32[]{:S(2)}) collective-permute-start(bf16[4,128,128]{2,1,0:T(8,128)(2,1)S(1)} %get-tuple-element.64), channel_id=1, source_target_pairs={{0,16},{8,24},{1,17},{9,25},{2,18},{10,26},{3,19},{11,27},{4,20},{... | collective-permute-start | bytes 393224 | tf_op jit(solution)/shard_map/ppermute | solution.py:477
  24.5 7.9 %collective-permute-start.7 = (bf16[4,128,128]{2,1,0:T(8,128)(2,1)S(1)}, bf16[4,128,128]{2,1,0:T(8,128)(2,1)S(1)}, u32[]{:S(2)}, u32[]{:S(2)}) collective-permute-start(bf16[4,128,128]{2,1,0:T(8,128)(2,1)S(1)} %get-tuple-element.64), channel_id=1, source_target_pairs={{0,8},{8,16},{16,24},{1,9},{9,17},{17,25},{2,10},{10,18},{18,26},{... | collective-permute-start | bytes 393224 | tf_op jit(solution)/shard_map/ppermute | solution.py:477
  32.4 9.7 %copy-start.3 = (bf16[128,4096]{1,0:T(8,128)(2,1)S(1)}, bf16[128,4096]{1,0:T(8,128)(2,1)}, u32[]{:S(2)}) copy-start(bf16[128,4096]{1,0:T(8,128)(2,1)} %g.1) | copy-start | bytes 3145732
  33.3 7.4 %collective-permute-start.9 = (bf16[4,128,128]{2,1,0:T(8,128)(2,1)S(1)}, bf16[4,128,128]{2,1,0:T(8,128)(2,1)S(1)}, u32[]{:S(2)}, u32[]{:S(2)}) collective-permute-start(bf16[4,128,128]{2,1,0:T(8,128)(2,1)S(1)} %get-tuple-element.65), channel_id=1, source_target_pairs={{0,6},{1,7},{2,4},{3,5},{4,2},{5,3},{6,0},{7,1},{8,14},{9,15},{10,... | collective-permute-start | bytes 393224 | tf_op jit(solution)/shard_map/ppermute | solution.py:457
  35.7 6.3 %collective-permute-start.10 = (bf16[4,128,128]{2,1,0:T(8,128)(2,1)S(1)}, bf16[4,128,128]{2,1,0:T(8,128)(2,1)S(1)}, u32[]{:S(2)}, u32[]{:S(2)}) collective-permute-start(bf16[4,128,128]{2,1,0:T(8,128)(2,1)S(1)} %get-tuple-element.66), channel_id=1, source_target_pairs={{0,4},{1,5},{2,6},{3,7},{4,0},{5,1},{6,2},{7,3},{8,12},{9,13},{10,... | collective-permute-start | bytes 393224 | tf_op jit(solution)/shard_map/ppermute | solution.py:457
  36.3 5.8 %collective-permute-start.11 = (bf16[4,128,128]{2,1,0:T(8,128)(2,1)S(1)}, bf16[4,128,128]{2,1,0:T(8,128)(2,1)S(1)}, u32[]{:S(2)}, u32[]{:S(2)}) collective-permute-start(bf16[4,128,128]{2,1,0:T(8,128)(2,1)S(1)} %get-tuple-element.67), channel_id=1, source_target_pairs={{0,2},{1,3},{2,0},{3,1},{4,6},{5,7},{6,4},{7,5},{8,10},{9,11},{10,... | collective-permute-start | bytes 393224 | tf_op jit(solution)/shard_map/ppermute | solution.py:457
  47.3 6.9 %collective-permute-start.12 = (bf16[4,128,128]{2,1,0:T(8,128)(2,1)S(1)}, bf16[4,128,128]{2,1,0:T(8,128)(2,1)S(1)}, u32[]{:S(2)}, u32[]{:S(2)}) collective-permute-start(bf16[4,128,128]{2,1,0:T(8,128)(2,1)S(1)} %get-tuple-element.70), channel_id=1, source_target_pairs={{0,6},{1,7},{2,4},{3,5},{4,2},{5,3},{6,0},{7,1},{8,14},{9,15},{10,... | collective-permute-start | bytes 393224 | tf_op jit(solution)/shard_map/ppermute | solution.py:457
  49.7 6.1 %collective-permute-start.13 = (bf16[4,128,128]{2,1,0:T(8,128)(2,1)S(1)}, bf16[4,128,128]{2,1,0:T(8,128)(2,1)S(1)}, u32[]{:S(2)}, u32[]{:S(2)}) collective-permute-start(bf16[4,128,128]{2,1,0:T(8,128)(2,1)S(1)} %get-tuple-element.71), channel_id=1, source_target_pairs={{0,4},{1,5},{2,6},{3,7},{4,0},{5,1},{6,2},{7,3},{8,12},{9,13},{10,... | collective-permute-start | bytes 393224 | tf_op jit(solution)/shard_map/ppermute | solution.py:457
  50.2 5.7 %collective-permute-start.14 = (bf16[4,128,128]{2,1,0:T(8,128)(2,1)S(1)}, bf16[4,128,128]{2,1,0:T(8,128)(2,1)S(1)}, u32[]{:S(2)}, u32[]{:S(2)}) collective-permute-start(bf16[4,128,128]{2,1,0:T(8,128)(2,1)S(1)} %get-tuple-element.72), channel_id=1, source_target_pairs={{0,2},{1,3},{2,0},{3,1},{4,6},{5,7},{6,4},{7,5},{8,10},{9,11},{10,... | collective-permute-start | bytes 393224 | tf_op jit(solution)/shard_map/ppermute | solution.py:457
  56.6 3.2 %collective-permute-start.15 = (bf16[128,2048]{1,0:T(8,128)(2,1)S(1)}, bf16[128,2048]{1,0:T(8,128)(2,1)S(1)}, u32[]{:S(2)}, u32[]{:S(2)}) collective-permute-start(bf16[128,2048]{1,0:T(8,128)(2,1)S(1)} %get-tuple-element.76), channel_id=1, source_target_pairs={{0,1},{1,0},{2,3},{3,2},{4,5},{5,4},{6,7},{7,6},{8,9},{9,8},{10,11... | collective-permute-start | bytes 1572872 | tf_op jit(solution)/shard_map/ppermute | solution.py:451
  56.7 3.1 %collective-permute-start.16 = (bf16[16,128,128]{2,1,0:T(8,128)(2,1)S(1)}, bf16[16,128,128]{2,1,0:T(8,128)(2,1)S(1)}, u32[]{:S(2)}, u32[]{:S(2)}) collective-permute-start(bf16[16,128,128]{2,1,0:T(8,128)(2,1)S(1)} %get-tuple-element.78), channel_id=1, source_target_pairs={{0,1},{1,0},{2,3},{3,2},{4,5},{5,4},{6,7},{7,6},{8,9},{9,8},{10,11... | collective-permute-start | bytes 1572872 | tf_op jit(solution)/shard_map/ppermute | solution.py:451
  57.2 13.5 %collective-permute-start.19 = (bf16[4,128,128]{2,1,0:T(8,128)(2,1)S(1)}, bf16[4,128,128]{2,1,0:T(8,128)(2,1)S(1)}, u32[]{:S(2)}, u32[]{:S(2)}) collective-permute-start(bf16[4,128,128]{2,1,0:T(8,128)(2,1)S(1)} %get-tuple-element.79.rest_4_), channel_id=1, source_target_pairs={{16,0},{24,8},{17,1},{25,9},{18,2},{26,10},{19,3},{27,11},{20,4},{... | collective-permute-start | bytes 393224 | tf_op jit(solution)/shard_map/ppermute | solution.py:477
  58.5 12.3 %collective-permute-start.18 = (bf16[4,128,128]{2,1,0:T(8,128)(2,1)S(1)}, bf16[4,128,128]{2,1,0:T(8,128)(2,1)S(1)}, u32[]{:S(2)}, u32[]{:S(2)}) collective-permute-start(bf16[4,128,128]{2,1,0:T(8,128)(2,1)S(1)} %get-tuple-element.79.rest_4_), channel_id=1, source_target_pairs={{8,0},{16,8},{24,16},{9,1},{17,9},{25,17},{10,2},{18,10},{26,18},{... | collective-permute-start | bytes 393224 | tf_op jit(solution)/shard_map/ppermute | solution.py:477
  66.7 16.4 %collective-permute-start.17 = (bf16[16,128,128]{2,1,0:T(8,128)(2,1)S(1)}, bf16[16,128,128]{2,1,0:T(8,128)(2,1)S(1)}, u32[]{:S(2)}, u32[]{:S(2)}) collective-permute-start(bf16[16,128,128]{2,1,0:T(8,128)(2,1)S(1)} %get-tuple-element.84), channel_id=1, source_target_pairs={{0,1},{1,0},{2,3},{3,2},{4,5},{5,4},{6,7},{7,6},{8,9},{9,8},{10,11... | collective-permute-start | bytes 1572872 | tf_op jit(solution)/shard_map/ppermute | solution.py:451
  66.8 16.3 %collective-permute-start.27 = (bf16[128,2048]{1,0:T(8,128)(2,1)S(1)}, bf16[128,2048]{1,0:T(8,128)(2,1)S(1)}, u32[]{:S(2)}, u32[]{:S(2)}) collective-permute-start(bf16[128,2048]{1,0:T(8,128)(2,1)S(1)} %get-tuple-element.89), channel_id=1, source_target_pairs={{0,1},{1,0},{2,3},{3,2},{4,5},{5,4},{6,7},{7,6},{8,9},{9,8},{10,11... | collective-permute-start | bytes 1572872 | tf_op jit(solution)/shard_map/ppermute | solution.py:451
  71.6 6.8 %collective-permute-start.20 = (bf16[4,128,128]{2,1,0:T(8,128)(2,1)S(1)}, bf16[4,128,128]{2,1,0:T(8,128)(2,1)S(1)}, u32[]{:S(2)}, u32[]{:S(2)}) collective-permute-start(bf16[4,128,128]{2,1,0:T(8,128)(2,1)S(1)} %get-tuple-element.85), channel_id=1, source_target_pairs={{0,6},{1,7},{2,4},{3,5},{4,2},{5,3},{6,0},{7,1},{8,14},{9,15},{10,... | collective-permute-start | bytes 393224 | tf_op jit(solution)/shard_map/ppermute | solution.py:457
  74.0 5.7 %collective-permute-start.22 = (bf16[4,128,128]{2,1,0:T(8,128)(2,1)S(1)}, bf16[4,128,128]{2,1,0:T(8,128)(2,1)S(1)}, u32[]{:S(2)}, u32[]{:S(2)}) collective-permute-start(bf16[4,128,128]{2,1,0:T(8,128)(2,1)S(1)} %get-tuple-element.86), channel_id=1, source_target_pairs={{0,4},{1,5},{2,6},{3,7},{4,0},{5,1},{6,2},{7,3},{8,12},{9,13},{10,... | collective-permute-start | bytes 393224 | tf_op jit(solution)/shard_map/ppermute | solution.py:457
  74.6 5.2 %collective-permute-start.24 = (bf16[4,128,128]{2,1,0:T(8,128)(2,1)S(1)}, bf16[4,128,128]{2,1,0:T(8,128)(2,1)S(1)}, u32[]{:S(2)}, u32[]{:S(2)}) collective-permute-start(bf16[4,128,128]{2,1,0:T(8,128)(2,1)S(1)} %get-tuple-element.87), channel_id=1, source_target_pairs={{0,2},{1,3},{2,0},{3,1},{4,6},{5,7},{6,4},{7,5},{8,10},{9,11},{10,... | collective-permute-start | bytes 393224 | tf_op jit(solution)/shard_map/ppermute | solution.py:457
  78.4 1.8 %collective-permute-start.26 = (bf16[4,128,128]{2,1,0:T(8,128)(2,1)S(1)}, bf16[4,128,128]{2,1,0:T(8,128)(2,1)S(1)}, u32[]{:S(2)}, u32[]{:S(2)}) collective-permute-start(bf16[4,128,128]{2,1,0:T(8,128)(2,1)S(1)} %get-tuple-element.88.rest_3_), channel_id=1, source_target_pairs={{0,1},{1,0},{2,3},{3,2},{4,5},{5,4},{6,7},{7,6},{8,9},{9,8},{10,11... | collective-permute-start | bytes 393224 | tf_op jit(solution)/shard_map/ppermute | solution.py:451
  79.7 3.3 %collective-permute-start.21 = (bf16[4,128,128]{2,1,0:T(8,128)(2,1)S(1)}, bf16[4,128,128]{2,1,0:T(8,128)(2,1)S(1)}, u32[]{:S(2)}, u32[]{:S(2)}) collective-permute-start(bf16[4,128,128]{2,1,0:T(8,128)(2,1)S(1)} %collective-permute-done.20.rest_0_), channel_id=1, source_target_pairs={{0,1},{1,0},{2,3},{3,2},{4,5},{5,4},{6,7},{7,6},{8,9},{9,8},{10,11... | collective-permute-start | bytes 393224 | tf_op jit(solution)/shard_map/ppermute | solution.py:451
  79.8 3.3 %collective-permute-start.23 = (bf16[4,128,128]{2,1,0:T(8,128)(2,1)S(1)}, bf16[4,128,128]{2,1,0:T(8,128)(2,1)S(1)}, u32[]{:S(2)}, u32[]{:S(2)}) collective-permute-start(bf16[4,128,128]{2,1,0:T(8,128)(2,1)S(1)} %collective-permute-done.22.rest_1_), channel_id=1, source_target_pairs={{0,1},{1,0},{2,3},{3,2},{4,5},{5,4},{6,7},{7,6},{8,9},{9,8},{10,11... | collective-permute-start | bytes 393224 | tf_op jit(solution)/shard_map/ppermute | solution.py:451
  80.3 2.8 %collective-permute-start.25 = (bf16[4,128,128]{2,1,0:T(8,128)(2,1)S(1)}, bf16[4,128,128]{2,1,0:T(8,128)(2,1)S(1)}, u32[]{:S(2)}, u32[]{:S(2)}) collective-permute-start(bf16[4,128,128]{2,1,0:T(8,128)(2,1)S(1)} %collective-permute-done.24.rest_2_), channel_id=1, source_target_pairs={{0,1},{1,0},{2,3},{3,2},{4,5},{5,4},{6,7},{7,6},{8,9},{9,8},{10,11... | collective-permute-start | bytes 393224 | tf_op jit(solution)/shard_map/ppermute | solution.py:451

commit v16 on v15

--- a/solution.py
+++ b/solution.py
@@ -212,23 +212,20 @@
             state[...] = kept[pl.ds((chip ^ n) * owned, owned)]
 
 
-def inner_kernel(lens, place, q, k, v, mine_ga, other_ga, *rest):
-    passed, earlier, (gq, gk, gv, _, _, came) = rest[:2], rest[2:4], rest[7:]
+def inner_kernel(along, lens, place, q, k, v, grad_att, passed, earlier, *rest):
+    (gq, gk, gv), came = rest[-4 - along : -1 - along], rest[-1]
     count = q.shape[0]
     heads = q.shape[1] // DH
     step = pl.program_id(0)
-    own = step < pl.num_programs(0) // 2
 
     @pl.when(step == 0)
     def _():
-        half = came.shape[0] // 2
         core, (early_b, early_e, late_b, late_e) = chip_docs(lens, place, count)
         by_chip = jnp.where(core == 0, 1.0, same(late_b, early_b))
         by_mate = jnp.where(core == 0, 0.0, same(late_b, early_e))
-        for j in range(2):
-            came[pl.ds(j * half, half)] = (
-                passed[j][...].astype(F32) * by_chip + earlier[j][...].astype(F32) * by_mate
-            ).astype(BF16)
+        came[...] = (
+            passed[...].astype(F32) * by_chip + earlier[...].astype(F32) * by_mate
+        ).astype(BF16)
 
     ends = doc_ends(lens)
     first = place[0] * count
@@ -238,7 +235,7 @@
         wides = [q[:, cols(h)].astype(F32) for h in hs]
         fqs = [feature(wide).astype(BF16) for wide in wides]
         fks = [feature(k[:, cols(h)].astype(F32)).astype(BF16) for h in hs]
-        gas = [jnp.where(own, mine_ga[:, cols(h)], other_ga[:, cols(h)]) for h in hs]
+        gas = [grad_att[:, cols(h)] for h in hs]
         gss = [
             jnp.where(seen, mul(ga, v[:, cols(h)], NT), 0.0).astype(BF16)
             for h, ga in zip(hs, gas)
@@ -584,40 +581,31 @@
         (8 * product, 16 * array, 2 * half * count * DH),
         "normed",
     )
-    came, others, total, (mate_ga, sent_in) = reach_out(
-        merged, (mate_ga, sent_in), False, "future"
-    )
-    other_ga, other_in = swap(mate_ga), swap(sent_in)
-    other_ga = swap(mate_ga)
-    def both(i, lens, place):
-        return ((place[2] & 1) ^ (i // steps)) * steps + i % steps
-
-    spans = pl.BlockSpec((count, step_heads * DH), lambda *a: (0, both(*a)))
-    lanes = pl.BlockSpec((count, step_heads * DH), lambda i, *a: (0, i % steps))
-    grad_queries, gk_part, gv_part, mate_out, sent_late = run(
-        inner_kernel,
-        2 * steps,
-        [spans] * 3 + [lanes] * 2 + [whole] * 4 + [untouched] * 3,
-        [spans] * 3 + [untouched] * 2,
-        [token_bf, token_f32, token_f32, narrow_bf, half_bf],
-        [all_states],
-        (
-            queries,
-            keys,
-            values,
-            mine_ga,
-            other_ga,
-            mine_in,
-            other_in,
-            other.reshape(half, DH, DH),
-            late_tail,
-            total,
-            mate_out,
-            sent_late,
-        ),
-        (16 * product, 22 * array, 4 * half * count * DH),
-        "grads_within",
-        aliases={12: 3, 13: 4},
+    def inner(parity, grad_att, passed, earlier, after, made, along):
+        return run(
+            functools.partial(inner_kernel, len(along)),
+            steps,
+            [tokens(parity)] * 3
+            + [lane]
+            + [whole] * 2
+            + [untouched] * (len(after) + len(made) + len(along)),
+            [tokens(parity)] * 3 + [untouched] * len(along),
+            [token_bf, token_f32, token_f32]
+            + [jax.ShapeDtypeStruct(array.shape, array.dtype) for array in along],
+            [half_states],
+            (queries, keys, values, grad_att, passed, earlier, *after, *made, *along),
+            (7 * product, 11 * array, 2 * half * count * DH),
+            f"grads_within_{parity}",
+            aliases={8 + len(after) + j: j for j in range(len(made) + len(along))},
+        )
+
+    made = inner(0, mine_ga, mine_in, other.reshape(half, DH, DH), (), (), ())
+    came, others, total, (mate_ga, sent_in, gk_half) = reach_out(
+        merged, (mate_ga, sent_in, made[1]), False, "future"
+    )
+    made = (held_in_hbm(made[0]), gk_half, made[2])
+    grad_queries, gk_part, gv_part, mate_out, sent_late = inner(
+        1, swap(mate_ga), swap(sent_in), late_tail, (total,), made, (mate_out, sent_late)
     )
     late = (mine_late, swap(sent_late))
     chip_out = spread(came, others, (gk_part,), False, "future")

time: 87.3 us -> 86.4 us (0.990); the launches traced: 86.1 us -> 86.2 us
    ppermute x12, waiting for transfers between devices: 21.1 us -> 17.4 us  [exchange(): came[n] = lax.ppermute(states[n], LAYER, pairs)]
    ppermute x4, waiting for transfers between devices: 3.48 us -> 7.1 us  [reach_out(): others.insert(0, lax.ppermute(total, 'z', pairs))]
    pallas_call x12 -> x13, Pallas kernels: 32 us -> 32.2 us  [run(): pl.pallas_call(kernel, grid_spec=pltpu.PrefetchScalarGridSpec(num_scalar_...]
  transfers between devices with their start and end apart: 28 -> 28, of which waited for: 12 -> 10; matrix products, arithmetic and copies ran while one was open for 0% -> 0% of each run, Pallas kernels for 22% -> 22%
where the time goes in v16:
time: 86.4 us; the launch traced here: 86.2 us
  Pallas kernels  32.2 us (37%)
  starting transfers between devices  28.4 us (33%)
  waiting for transfers between devices  24.6 us (28%)
  between operations  0.91 us (1%)
    pallas_call x13, Pallas kernels, run(): pl.pallas_call(kernel, grid_spec=pltpu.PrefetchScalarGridSpec(num_scalar_...  32.2 us
    ppermute x12, waiting for transfers between devices, exchange(): came[n] = lax.ppermute(states[n], LAYER, pairs)  17.4 us
    ppermute x12, starting transfers between devices, exchange(): came[n] = lax.ppermute(states[n], LAYER, pairs)  15.1 us
    ppermute x4, starting transfers between devices, reach_out(): others.insert(0, lax.ppermute(total, 'z', pairs))  10.6 us
    ppermute x4, waiting for transfers between devices, reach_out(): others.insert(0, lax.ppermute(total, 'z', pairs))  7.1 us
    ppermute x12, starting transfers between devices, swap(): return lax.ppermute(state, LAYER, [(i, i ^ 1) for i in range(members)])  2.8 us
  transfers between devices with their start and end apart: 28, of which 10 were waited for; matrix products, arithmetic and copies ran while one was open for 0% of the time, Pallas kernels for 22%

profile of v16, /device:TPU:0, one launch (start us, length us, event | category | flops | bytes accessed | tf_op | source)
XLA Modules:
  0.0 86.2 jit_solution(8080393411399532345)
XLA Ops:
  0.6 0.1 pad_add_fusion.place
  0.7 3.1 %tail_mate.1 = (bf16[16,128,128]{2,1,0:T(8,128)(2,1)S(1)}, bf16[3,128,2048]{2,1,0:T(8,128)(2,1)S(1)}, bf16[128,2048]{1,0:T(8,128)(2,1)S(1)}) custom-call(s32[8]{0:T(128)} %lens.25, s32[3]{0:T(128)S(1)} %pad_add_fusion.place, bf16[128,4096]{1,0:T(8,128)(2,1)} %k.13, bf16[128,4096]{1,0:T(8,128)(2,1)} %v.13, bf16[128,4096]{1,0:T(8,128)(2,1)} %q.5, ...), custom_call_target="tpu_custom_call" | custom-call | flops 67108864 | bytes 1572864 | tf_op jit(solution)/shard_map/tail_mate/pallas_call | solution.py:420
  3.8 0.0 copy-start.4
  3.8 0.5 collective-permute-start
  4.3 2.7 %tail_own.1.rest_5_ = bf16[16,128,128]{2,1,0:T(8,128)(2,1)S(1)} custom-call(s32[8]{0:T(128)} %lens.25, s32[3]{0:T(128)S(1)} %pad_add_fusion.place, bf16[128,4096]{1,0:T(8,128)(2,1)} %k.13, bf16[128,4096]{1,0:T(8,128)(2,1)} %v.13), custom_call_target="tpu_custom_call" | custom-call | flops 67108864 | bytes 1572864 | tf_op jit(solution)/shard_map/tail_own/pallas_call | solution.py:420
  7.1 0.0 collective-permute-done.earlier
  7.1 0.0 copy-start
  7.1 0.0 copy-start.1
  7.1 0.0 copy-start.2
  7.1 0.8 carried_chip.1
  7.9 0.1 collective-permute-start.1
  8.0 3.9 %collective-permute-start.2 = (bf16[4,128,128]{2,1,0:T(8,128)(2,1)S(1)}, bf16[4,128,128]{2,1,0:T(8,128)(2,1)S(1)}, u32[]{:S(2)}, u32[]{:S(2)}) collective-permute-start(bf16[4,128,128]{2,1,0:T(8,128)(2,1)S(1)} %get-tuple-element.60), channel_id=1, source_target_pairs={{0,6},{1,7},{2,4},{3,5},{4,2},{5,3},{6,0},{7,1},{8,14},{9,15},{10,... | collective-permute-start | bytes 393224 | tf_op jit(solution)/shard_map/ppermute | solution.py:454
  11.9 0.5 collective-permute-start.3
  12.4 0.0 collective-permute-start.4
  12.5 3.7 %collective-permute-done.2.rest_0_ = bf16[4,128,128]{2,1,0:T(8,128)(2,1)S(1)} collective-permute-done((bf16[4,128,128]{2,1,0:T(8,128)(2,1)S(1)}, bf16[4,128,128]{2,1,0:T(8,128)(2,1)S(1)}, u32[]{:S(2)}, u32[]{:S(2)}) %collective-permute-start.2) | collective-permute-done | bytes 131104 | tf_op jit(solution)/shard_map/ppermute | solution.py:454
  16.2 2.5 %collective-permute-done.3.rest_1_ = bf16[4,128,128]{2,1,0:T(8,128)(2,1)S(1)} collective-permute-done((bf16[4,128,128]{2,1,0:T(8,128)(2,1)S(1)}, bf16[4,128,128]{2,1,0:T(8,128)(2,1)S(1)}, u32[]{:S(2)}, u32[]{:S(2)}) %collective-permute-start.3) | collective-permute-done | bytes 131104 | tf_op jit(solution)/shard_map/ppermute | solution.py:454
  18.7 0.0 collective-permute-done.4.rest_2_
  18.7 0.7 carried_total.1
  19.4 0.1 collective-permute-start.6
  19.5 0.5 collective-permute-start.5
  20.0 3.5 %collective-permute-start.7 = (bf16[4,128,128]{2,1,0:T(8,128)(2,1)S(1)}, bf16[4,128,128]{2,1,0:T(8,128)(2,1)S(1)}, u32[]{:S(2)}, u32[]{:S(2)}) collective-permute-start(bf16[4,128,128]{2,1,0:T(8,128)(2,1)S(1)} %get-tuple-element.68), channel_id=1, source_target_pairs={{0,8},{8,16},{16,24},{1,9},{9,17},{17,25},{2,10},{10,18},{18,26},{... | collective-permute-start | bytes 393224 | tf_op jit(solution)/shard_map/ppermute | solution.py:474
  23.5 4.5 %collective-permute-start.8 = (bf16[4,128,128]{2,1,0:T(8,128)(2,1)S(1)}, bf16[4,128,128]{2,1,0:T(8,128)(2,1)S(1)}, u32[]{:S(2)}, u32[]{:S(2)}) collective-permute-start(bf16[4,128,128]{2,1,0:T(8,128)(2,1)S(1)} %get-tuple-element.68), channel_id=1, source_target_pairs={{0,16},{8,24},{1,17},{9,25},{2,18},{10,26},{3,19},{11,27},{4,20},{... | collective-permute-start | bytes 393224 | tf_op jit(solution)/shard_map/ppermute | solution.py:474
  28.0 0.0 collective-permute-done.1.mate
  28.0 4.3 %within_chip.1 = (f32[256,2048]{1,0:T(8,128)S(1)}, bf16[256,2048]{1,0:T(8,128)(2,1)S(1)}, bf16[16,256,256]{2,1,0:T(8,128)(2,1)S(1)}) custom-call(s32[8]{0:T(128)S(1)} %copy-done.4, s32[3]{0:T(128)S(1)} %pad_add_fusion.place, bf16[128,4096]{1,0:T(8,128)(2,1)S(1)} %copy-done.2, bf16[128,4096]{1,0:T(8,128)(2,1)S(1)} %copy-done, ...), custom_call_target="tpu_custom_call" | custom-call | flops 671088640 | bytes 7340032 | tf_op jit(solution)/shard_map/within_chip/pallas_call | solution.py:420
  32.4 0.0 copy-start.3
  32.4 0.0 collective-permute-done.7.rest_6_
  32.4 0.9 %carried_prefix.1 = (bf16[4,128,128]{2,1,0:T(8,128)(2,1)S(1)}, bf16[4,128,128]{2,1,0:T(8,128)(2,1)S(1)}, bf16[4,128,128]{2,1,0:T(8,128)(2,1)S(1)}, bf16[4,128,128]{2,1,0:T(8,128)(2,1)S(1)}) custom-call(s32[8]{0:T(128)S(1)} %copy-done.4, s32[3]{0:T(128)S(1)} %pad_add_fusion.place, bf16[4,128,128]{2,1,0:T(8,128)(2,1)S(1)} %collective-permute-done.2.rest_0_, ...), custom_call_target="tpu_custom_call" | custom-call | flops 1048576 | bytes 1048576 | tf_op jit(solution)/shard_map/carried_prefix/pallas_call | solution.py:420
  33.3 1.5 %collective-permute-start.10 = (bf16[4,128,128]{2,1,0:T(8,128)(2,1)S(1)}, bf16[4,128,128]{2,1,0:T(8,128)(2,1)S(1)}, u32[]{:S(2)}, u32[]{:S(2)}) collective-permute-start(bf16[4,128,128]{2,1,0:T(8,128)(2,1)S(1)} %get-tuple-element.70), channel_id=1, source_target_pairs={{0,4},{1,5},{2,6},{3,7},{4,0},{5,1},{6,2},{7,3},{8,12},{9,13},{10,... | collective-permute-start | bytes 393224 | tf_op jit(solution)/shard_map/ppermute | solution.py:454
  34.8 1.5 %collective-permute-start.11 = (bf16[4,128,128]{2,1,0:T(8,128)(2,1)S(1)}, bf16[4,128,128]{2,1,0:T(8,128)(2,1)S(1)}, u32[]{:S(2)}, u32[]{:S(2)}) collective-permute-start(bf16[4,128,128]{2,1,0:T(8,128)(2,1)S(1)} %get-tuple-element.71), channel_id=1, source_target_pairs={{0,2},{1,3},{2,0},{3,1},{4,6},{5,7},{6,4},{7,5},{8,10},{9,11},{10,... | collective-permute-start | bytes 393224 | tf_op jit(solution)/shard_map/ppermute | solution.py:454
  36.3 0.6 collective-permute-start.9
  36.8 2.0 %collective-permute-done.10.rest_1_ = bf16[4,128,128]{2,1,0:T(8,128)(2,1)S(1)} collective-permute-done((bf16[4,128,128]{2,1,0:T(8,128)(2,1)S(1)}, bf16[4,128,128]{2,1,0:T(8,128)(2,1)S(1)}, u32[]{:S(2)}, u32[]{:S(2)}) %collective-permute-start.10) | collective-permute-done | bytes 131104 | tf_op jit(solution)/shard_map/ppermute | solution.py:454
  38.8 3.8 %collective-permute-done.11.rest_2_ = bf16[4,128,128]{2,1,0:T(8,128)(2,1)S(1)} collective-permute-done((bf16[4,128,128]{2,1,0:T(8,128)(2,1)S(1)}, bf16[4,128,128]{2,1,0:T(8,128)(2,1)S(1)}, u32[]{:S(2)}, u32[]{:S(2)}) %collective-permute-start.11) | collective-permute-done | bytes 131104 | tf_op jit(solution)/shard_map/ppermute | solution.py:454
  42.6 0.0 collective-permute-done.9.rest_0_
  42.6 5.3 %normed.1 = (bf16[128,4096]{1,0:T(8,128)(2,1)}, bf16[128,2048]{1,0:T(8,128)(2,1)S(1)}, bf16[128,2048]{1,0:T(8,128)(2,1)S(1)}, bf16[128,2048]{1,0:T(8,128)(2,1)S(...) custom-call(s32[8]{0:T(128)S(1)} %copy-done.4, ...), custom_call_target="tpu_custom_call" | custom-call | flops 536870912 | bytes 8388608 | tf_op jit(solution)/shard_map/normed/pallas_call | solution.py:420
  47.9 1.2 %collective-permute-start.12 = (bf16[4,128,128]{2,1,0:T(8,128)(2,1)S(1)}, bf16[4,128,128]{2,1,0:T(8,128)(2,1)S(1)}, u32[]{:S(2)}, u32[]{:S(2)}) collective-permute-start(bf16[4,128,128]{2,1,0:T(8,128)(2,1)S(1)} %get-tuple-element.73), channel_id=1, source_target_pairs={{0,6},{1,7},{2,4},{3,5},{4,2},{5,3},{6,0},{7,1},{8,14},{9,15},{10,... | collective-permute-start | bytes 393224 | tf_op jit(solution)/shard_map/ppermute | solution.py:454
  49.1 1.5 %collective-permute-start.13 = (bf16[4,128,128]{2,1,0:T(8,128)(2,1)S(1)}, bf16[4,128,128]{2,1,0:T(8,128)(2,1)S(1)}, u32[]{:S(2)}, u32[]{:S(2)}) collective-permute-start(bf16[4,128,128]{2,1,0:T(8,128)(2,1)S(1)} %get-tuple-element.74), channel_id=1, source_target_pairs={{0,4},{1,5},{2,6},{3,7},{4,0},{5,1},{6,2},{7,3},{8,12},{9,13},{10,... | collective-permute-start | bytes 393224 | tf_op jit(solution)/shard_map/ppermute | solution.py:454
  50.6 0.9 collective-permute-start.14
  51.4 3.5 %grads_within_0.1 = (bf16[128,4096]{1,0:T(8,128)(2,1)}, f32[128,4096]{1,0:T(8,128)S(1)}, f32[128,4096]{1,0:T(8,128)S(1)}) custom-call(s32[8]{0:T(128)S(1)} %copy-done.4, s32[3]{0:T(128)S(1)} %pad_add_fusion.place, bf16[128,4096]{1,0:T(8,128)(2,1)S(1)} %copy-done.2, bf16[128,4096]{1,0:T(8,128)(2,1)S(1)} %copy-done, bf16[128,4096]{1,0:T(8,128)(2,1)S(1)} %copy-done.1, ...), custom_call_target="tpu_custom_call" | custom-call | flops 469762048 | bytes 5767168 | tf_op jit(solution)/shard_map/grads_within_0/pallas_call | solution.py:420
  55.0 0.6 collective-permute-done.14.rest_2_
  55.5 0.7 future_total.1
  56.3 0.1 collective-permute-start.15
  56.3 0.5 collective-permute-start.16
  56.8 1.3 %collective-permute-start.18 = (bf16[4,128,128]{2,1,0:T(8,128)(2,1)S(1)}, bf16[4,128,128]{2,1,0:T(8,128)(2,1)S(1)}, u32[]{:S(2)}, u32[]{:S(2)}) collective-permute-start(bf16[4,128,128]{2,1,0:T(8,128)(2,1)S(1)} %get-tuple-element.84.rest_0_), channel_id=1, source_target_pairs={{8,0},{16,8},{24,16},{9,1},{17,9},{25,17},{10,2},{18,10},{26,18},{... | collective-permute-start | bytes 393224 | tf_op jit(solution)/shard_map/ppermute | solution.py:474
  58.1 1.3 %collective-permute-start.19 = (bf16[4,128,128]{2,1,0:T(8,128)(2,1)S(1)}, bf16[4,128,128]{2,1,0:T(8,128)(2,1)S(1)}, u32[]{:S(2)}, u32[]{:S(2)}) collective-permute-start(bf16[4,128,128]{2,1,0:T(8,128)(2,1)S(1)} %get-tuple-element.84.rest_0_), channel_id=1, source_target_pairs={{16,0},{24,8},{17,1},{25,9},{18,2},{26,10},{19,3},{27,11},{20,4},{... | collective-permute-start | bytes 393224 | tf_op jit(solution)/shard_map/ppermute | solution.py:474
  59.4 0.0 collective-permute-done.16.passed
  59.4 3.6 %grads_within_1.1 = (bf16[128,4096]{1,0:T(8,128)(2,1)}, f32[128,4096]{1,0:T(8,128)S(1)}, f32[128,4096]{1,0:T(8,128)S(1)}, bf16[128,2048]{1,0:T(8,128)(2,1)S(1)}, bf16[16,128,128]{2,1,0:T(8,128)(2,1)S(1)}) custom-call(s32[8]{0:T(128)S(1)} %copy-done.4, ...), custom_call_target="tpu_custom_call", output_to_operand_aliasing={{0}: (9, {}), {1}: (10, {}), {2}: (11, {}), {3}: (12, {}), ... | custom-call | flops 469762048 | bytes 5767168 | tf_op jit(solution)/shard_map/grads_within_1/pallas_call | solution.py:420
  63.0 0.1 collective-permute-start.17
  63.1 0.4 collective-permute-start.27
  63.5 0.7 collective-permute-done.18.rest_5_
  64.3 6.4 %collective-permute-done.19.rest_6_ = bf16[4,128,128]{2,1,0:T(8,128)(2,1)S(1)} collective-permute-done((bf16[4,128,128]{2,1,0:T(8,128)(2,1)S(1)}, bf16[4,128,128]{2,1,0:T(8,128)(2,1)S(1)}, u32[]{:S(2)}, u32[]{:S(2)}) %collective-permute-start.19) | collective-permute-done | bytes 131104 | tf_op jit(solution)/shard_map/ppermute | solution.py:474
  70.6 0.9 %future_prefix.1 = (bf16[4,128,128]{2,1,0:T(8,128)(2,1)S(1)}, bf16[4,128,128]{2,1,0:T(8,128)(2,1)S(1)}, bf16[4,128,128]{2,1,0:T(8,128)(2,1)S(1)}, bf16[4,128,128]{2,1,0:T(8,128)(2,1)S(1)}) custom-call(s32[8]{0:T(128)S(1)} %copy-done.4, s32[3]{0:T(128)S(1)} %pad_add_fusion.place, bf16[4,128,128]{2,1,0:T(8,128)(2,1)S(1)} %collective-permute-done.12.rest_0_, ...), custom_call_target="tpu_custom_call" | custom-call | flops 1048576 | bytes 1048576 | tf_op jit(solution)/shard_map/future_prefix/pallas_call | solution.py:420
  71.5 1.3 %collective-permute-start.20 = (bf16[4,128,128]{2,1,0:T(8,128)(2,1)S(1)}, bf16[4,128,128]{2,1,0:T(8,128)(2,1)S(1)}, u32[]{:S(2)}, u32[]{:S(2)}) collective-permute-start(bf16[4,128,128]{2,1,0:T(8,128)(2,1)S(1)} %get-tuple-element.93), channel_id=1, source_target_pairs={{0,6},{1,7},{2,4},{3,5},{4,2},{5,3},{6,0},{7,1},{8,14},{9,15},{10,... | collective-permute-start | bytes 393224 | tf_op jit(solution)/shard_map/ppermute | solution.py:454
  72.8 1.1 %collective-permute-start.22 = (bf16[4,128,128]{2,1,0:T(8,128)(2,1)S(1)}, bf16[4,128,128]{2,1,0:T(8,128)(2,1)S(1)}, u32[]{:S(2)}, u32[]{:S(2)}) collective-permute-start(bf16[4,128,128]{2,1,0:T(8,128)(2,1)S(1)} %get-tuple-element.94), channel_id=1, source_target_pairs={{0,4},{1,5},{2,6},{3,7},{4,0},{5,1},{6,2},{7,3},{8,12},{9,13},{10,... | collective-permute-start | bytes 393224 | tf_op jit(solution)/shard_map/ppermute | solution.py:454
  73.9 1.2 %collective-permute-start.24 = (bf16[4,128,128]{2,1,0:T(8,128)(2,1)S(1)}, bf16[4,128,128]{2,1,0:T(8,128)(2,1)S(1)}, u32[]{:S(2)}, u32[]{:S(2)}) collective-permute-start(bf16[4,128,128]{2,1,0:T(8,128)(2,1)S(1)} %get-tuple-element.95), channel_id=1, source_target_pairs={{0,2},{1,3},{2,0},{3,1},{4,6},{5,7},{6,4},{7,5},{8,10},{9,11},{10,... | collective-permute-start | bytes 393224 | tf_op jit(solution)/shard_map/ppermute | solution.py:454
  75.0 3.5 %collective-permute-done.20.rest_0_ = bf16[4,128,128]{2,1,0:T(8,128)(2,1)S(1)} collective-permute-done((bf16[4,128,128]{2,1,0:T(8,128)(2,1)S(1)}, bf16[4,128,128]{2,1,0:T(8,128)(2,1)S(1)}, u32[]{:S(2)}, u32[]{:S(2)}) %collective-permute-start.20) | collective-permute-done | bytes 131104 | tf_op jit(solution)/shard_map/ppermute | solution.py:454
  78.5 0.7 collective-permute-done.22.rest_1_
  79.3 0.6 collective-permute-done.24.rest_2_
  79.9 0.0 collective-permute-start.23
  79.9 0.0 collective-permute-done.26.rest_3_
  79.9 0.5 collective-permute-start.25
  80.4 2.8 %grads_last_0.1 = (bf16[128,4096]{1,0:T(8,128)(2,1)}, bf16[128,4096]{1,0:T(8,128)(2,1)}) custom-call(s32[8]{0:T(128)S(1)} %copy-done.4, s32[3]{0:T(128)S(1)} %pad_add_fusion.place, bf16[128,4096]{1,0:T(8,128)(2,1)S(1)} %copy-done, bf16[128,4096]{1,0:T(8,128)(2,1)S(1)} %copy-done.1, f32[128,4096]{1,0:T(8,128)S(1)} %get-tuple-element.90.rest_4_.gk_part, ...), custom_call_target="tpu_custom_call" | custom-call | flops 134217728 | bytes 4718592 | tf_op jit(solution)/shard_map/grads_last_0/pallas_call | solution.py:420
  83.2 0.0 collective-permute-done.17.late
  83.2 0.0 collective-permute-done.27.rest_4_
  83.2 2.9 %grads_last_1.1 = (bf16[128,4096]{1,0:T(8,128)(2,1)}, bf16[128,4096]{1,0:T(8,128)(2,1)}, bf16[128,4096]{1,0:T(8,128)(2,1)}) custom-call(s32[8]{0:T(128)S(1)} %copy-done.4, s32[3]{0:T(128)S(1)} %pad_add_fusion.place, bf16[128,4096]{1,0:T(8,128)(2,1)S(1)} %copy-done, ...), custom_call_target="tpu_custom_call", output_to_operand_aliasing={{0}: (12, {}), {1}: (13, {}), {2}: (14, {})} | custom-call | flops 134217728 | bytes 4718592 | tf_op jit(solution)/shard_map/grads_last_1/pallas_call | solution.py:420
  (16 shorter events, 0.0 us)
Async XLA Ops:
  3.8 3.3 %copy-start.4 = (s32[8]{0:T(128)S(1)}, s32[8]{0:T(128)}, u32[]{:S(2)}) copy-start(s32[8]{0:T(128)} %lens.25) | copy-start | bytes 100
  3.8 3.2 %collective-permute-start = (bf16[16,128,128]{2,1,0:T(8,128)(2,1)S(1)}, bf16[16,128,128]{2,1,0:T(8,128)(2,1)S(1)}, u32[]{:S(2)}, u32[]{:S(2)}) collective-permute-start(bf16[16,128,128]{2,1,0:T(8,128)(2,1)S(1)} %get-tuple-element.55), channel_id=1, source_target_pairs={{0,1},{1,0},{2,3},{3,2},{4,5},{5,4},{6,7},{7,6},{8,9},{9,8},{10,11... | collective-permute-start | bytes 1572872 | tf_op jit(solution)/shard_map/ppermute | solution.py:448
  7.1 20.9 %copy-start = (bf16[128,4096]{1,0:T(8,128)(2,1)S(1)}, bf16[128,4096]{1,0:T(8,128)(2,1)}, u32[]{:S(2)}) copy-start(bf16[128,4096]{1,0:T(8,128)(2,1)} %k.13) | copy-start | bytes 3145732
  7.1 20.9 %copy-start.1 = (bf16[128,4096]{1,0:T(8,128)(2,1)S(1)}, bf16[128,4096]{1,0:T(8,128)(2,1)}, u32[]{:S(2)}) copy-start(bf16[128,4096]{1,0:T(8,128)(2,1)} %v.13) | copy-start | bytes 3145732
  7.1 20.9 %copy-start.2 = (bf16[128,4096]{1,0:T(8,128)(2,1)S(1)}, bf16[128,4096]{1,0:T(8,128)(2,1)}, u32[]{:S(2)}) copy-start(bf16[128,4096]{1,0:T(8,128)(2,1)} %q.5) | copy-start | bytes 3145732
  7.9 20.1 %collective-permute-start.1 = (bf16[3,128,2048]{2,1,0:T(8,128)(2,1)S(1)}, bf16[3,128,2048]{2,1,0:T(8,128)(2,1)S(1)}, u32[]{:S(2)}, u32[]{:S(2)}) collective-permute-start(bf16[3,128,2048]{2,1,0:T(8,128)(2,1)S(1)} %get-tuple-element.57), channel_id=1, source_target_pairs={{0,1},{1,0},{2,3},{3,2},{4,5},{5,4},{6,7},{7,6},{8,9},{9,8},{10,11... | collective-permute-start | bytes 4718600 | tf_op jit(solution)/shard_map/ppermute | solution.py:448
  8.0 8.2 %collective-permute-start.2 = (bf16[4,128,128]{2,1,0:T(8,128)(2,1)S(1)}, bf16[4,128,128]{2,1,0:T(8,128)(2,1)S(1)}, u32[]{:S(2)}, u32[]{:S(2)}) collective-permute-start(bf16[4,128,128]{2,1,0:T(8,128)(2,1)S(1)} %get-tuple-element.60), channel_id=1, source_target_pairs={{0,6},{1,7},{2,4},{3,5},{4,2},{5,3},{6,0},{7,1},{8,14},{9,15},{10,... | collective-permute-start | bytes 393224 | tf_op jit(solution)/shard_map/ppermute | solution.py:454
  11.9 6.8 %collective-permute-start.3 = (bf16[4,128,128]{2,1,0:T(8,128)(2,1)S(1)}, bf16[4,128,128]{2,1,0:T(8,128)(2,1)S(1)}, u32[]{:S(2)}, u32[]{:S(2)}) collective-permute-start(bf16[4,128,128]{2,1,0:T(8,128)(2,1)S(1)} %get-tuple-element.61), channel_id=1, source_target_pairs={{0,4},{1,5},{2,6},{3,7},{4,0},{5,1},{6,2},{7,3},{8,12},{9,13},{10,... | collective-permute-start | bytes 393224 | tf_op jit(solution)/shard_map/ppermute | solution.py:454
  12.4 6.3 %collective-permute-start.4 = (bf16[4,128,128]{2,1,0:T(8,128)(2,1)S(1)}, bf16[4,128,128]{2,1,0:T(8,128)(2,1)S(1)}, u32[]{:S(2)}, u32[]{:S(2)}) collective-permute-start(bf16[4,128,128]{2,1,0:T(8,128)(2,1)S(1)} %get-tuple-element.62), channel_id=1, source_target_pairs={{0,2},{1,3},{2,0},{3,1},{4,6},{5,7},{6,4},{7,5},{8,10},{9,11},{10,... | collective-permute-start | bytes 393224 | tf_op jit(solution)/shard_map/ppermute | solution.py:454
  19.4 13.0 %collective-permute-start.6 = (bf16[16,128,128]{2,1,0:T(8,128)(2,1)S(1)}, bf16[16,128,128]{2,1,0:T(8,128)(2,1)S(1)}, u32[]{:S(2)}, u32[]{:S(2)}) collective-permute-start(bf16[16,128,128]{2,1,0:T(8,128)(2,1)S(1)} %get-tuple-element.67), channel_id=1, source_target_pairs={{0,1},{1,0},{2,3},{3,2},{4,5},{5,4},{6,7},{7,6},{8,9},{9,8},{10,11... | collective-permute-start | bytes 1572872 | tf_op jit(solution)/shard_map/ppermute | solution.py:448
  19.5 17.3 %collective-permute-start.5 = (bf16[128,2048]{1,0:T(8,128)(2,1)S(1)}, bf16[128,2048]{1,0:T(8,128)(2,1)S(1)}, u32[]{:S(2)}, u32[]{:S(2)}) collective-permute-start(bf16[128,2048]{1,0:T(8,128)(2,1)S(1)} %get-tuple-element.65), channel_id=1, source_target_pairs={{0,1},{1,0},{2,3},{3,2},{4,5},{5,4},{6,7},{7,6},{8,9},{9,8},{10,11... | collective-permute-start | bytes 1572872 | tf_op jit(solution)/shard_map/ppermute | solution.py:448
  20.0 12.4 %collective-permute-start.7 = (bf16[4,128,128]{2,1,0:T(8,128)(2,1)S(1)}, bf16[4,128,128]{2,1,0:T(8,128)(2,1)S(1)}, u32[]{:S(2)}, u32[]{:S(2)}) collective-permute-start(bf16[4,128,128]{2,1,0:T(8,128)(2,1)S(1)} %get-tuple-element.68), channel_id=1, source_target_pairs={{0,8},{8,16},{16,24},{1,9},{9,17},{17,25},{2,10},{10,18},{18,26},{... | collective-permute-start | bytes 393224 | tf_op jit(solution)/shard_map/ppermute | solution.py:474
  23.5 8.9 %collective-permute-start.8 = (bf16[4,128,128]{2,1,0:T(8,128)(2,1)S(1)}, bf16[4,128,128]{2,1,0:T(8,128)(2,1)S(1)}, u32[]{:S(2)}, u32[]{:S(2)}) collective-permute-start(bf16[4,128,128]{2,1,0:T(8,128)(2,1)S(1)} %get-tuple-element.68), channel_id=1, source_target_pairs={{0,16},{8,24},{1,17},{9,25},{2,18},{10,26},{3,19},{11,27},{4,20},{... | collective-permute-start | bytes 393224 | tf_op jit(solution)/shard_map/ppermute | solution.py:474
  32.4 10.2 %copy-start.3 = (bf16[128,4096]{1,0:T(8,128)(2,1)S(1)}, bf16[128,4096]{1,0:T(8,128)(2,1)}, u32[]{:S(2)}) copy-start(bf16[128,4096]{1,0:T(8,128)(2,1)} %g.1) | copy-start | bytes 3145732
  33.3 5.5 %collective-permute-start.10 = (bf16[4,128,128]{2,1,0:T(8,128)(2,1)S(1)}, bf16[4,128,128]{2,1,0:T(8,128)(2,1)S(1)}, u32[]{:S(2)}, u32[]{:S(2)}) collective-permute-start(bf16[4,128,128]{2,1,0:T(8,128)(2,1)S(1)} %get-tuple-element.70), channel_id=1, source_target_pairs={{0,4},{1,5},{2,6},{3,7},{4,0},{5,1},{6,2},{7,3},{8,12},{9,13},{10,... | collective-permute-start | bytes 393224 | tf_op jit(solution)/shard_map/ppermute | solution.py:454
  34.8 7.8 %collective-permute-start.11 = (bf16[4,128,128]{2,1,0:T(8,128)(2,1)S(1)}, bf16[4,128,128]{2,1,0:T(8,128)(2,1)S(1)}, u32[]{:S(2)}, u32[]{:S(2)}) collective-permute-start(bf16[4,128,128]{2,1,0:T(8,128)(2,1)S(1)} %get-tuple-element.71), channel_id=1, source_target_pairs={{0,2},{1,3},{2,0},{3,1},{4,6},{5,7},{6,4},{7,5},{8,10},{9,11},{10,... | collective-permute-start | bytes 393224 | tf_op jit(solution)/shard_map/ppermute | solution.py:454
  36.3 6.3 %collective-permute-start.9 = (bf16[4,128,128]{2,1,0:T(8,128)(2,1)S(1)}, bf16[4,128,128]{2,1,0:T(8,128)(2,1)S(1)}, u32[]{:S(2)}, u32[]{:S(2)}) collective-permute-start(bf16[4,128,128]{2,1,0:T(8,128)(2,1)S(1)} %get-tuple-element.69), channel_id=1, source_target_pairs={{0,6},{1,7},{2,4},{3,5},{4,2},{5,3},{6,0},{7,1},{8,14},{9,15},{10,... | collective-permute-start | bytes 393224 | tf_op jit(solution)/shard_map/ppermute | solution.py:454
  47.9 7.0 %collective-permute-start.12 = (bf16[4,128,128]{2,1,0:T(8,128)(2,1)S(1)}, bf16[4,128,128]{2,1,0:T(8,128)(2,1)S(1)}, u32[]{:S(2)}, u32[]{:S(2)}) collective-permute-start(bf16[4,128,128]{2,1,0:T(8,128)(2,1)S(1)} %get-tuple-element.73), channel_id=1, source_target_pairs={{0,6},{1,7},{2,4},{3,5},{4,2},{5,3},{6,0},{7,1},{8,14},{9,15},{10,... | collective-permute-start | bytes 393224 | tf_op jit(solution)/shard_map/ppermute | solution.py:454
  49.1 5.9 %collective-permute-start.13 = (bf16[4,128,128]{2,1,0:T(8,128)(2,1)S(1)}, bf16[4,128,128]{2,1,0:T(8,128)(2,1)S(1)}, u32[]{:S(2)}, u32[]{:S(2)}) collective-permute-start(bf16[4,128,128]{2,1,0:T(8,128)(2,1)S(1)} %get-tuple-element.74), channel_id=1, source_target_pairs={{0,4},{1,5},{2,6},{3,7},{4,0},{5,1},{6,2},{7,3},{8,12},{9,13},{10,... | collective-permute-start | bytes 393224 | tf_op jit(solution)/shard_map/ppermute | solution.py:454
  50.6 5.0 %collective-permute-start.14 = (bf16[4,128,128]{2,1,0:T(8,128)(2,1)S(1)}, bf16[4,128,128]{2,1,0:T(8,128)(2,1)S(1)}, u32[]{:S(2)}, u32[]{:S(2)}) collective-permute-start(bf16[4,128,128]{2,1,0:T(8,128)(2,1)S(1)} %get-tuple-element.75), channel_id=1, source_target_pairs={{0,2},{1,3},{2,0},{3,1},{4,6},{5,7},{6,4},{7,5},{8,10},{9,11},{10,... | collective-permute-start | bytes 393224 | tf_op jit(solution)/shard_map/ppermute | solution.py:454
  56.3 3.2 %collective-permute-start.15 = (bf16[128,2048]{1,0:T(8,128)(2,1)S(1)}, bf16[128,2048]{1,0:T(8,128)(2,1)S(1)}, u32[]{:S(2)}, u32[]{:S(2)}) collective-permute-start(bf16[128,2048]{1,0:T(8,128)(2,1)S(1)} %get-tuple-element.82), channel_id=1, source_target_pairs={{0,1},{1,0},{2,3},{3,2},{4,5},{5,4},{6,7},{7,6},{8,9},{9,8},{10,11... | collective-permute-start | bytes 1572872 | tf_op jit(solution)/shard_map/ppermute | solution.py:448
  56.3 3.1 %collective-permute-start.16 = (bf16[16,128,128]{2,1,0:T(8,128)(2,1)S(1)}, bf16[16,128,128]{2,1,0:T(8,128)(2,1)S(1)}, u32[]{:S(2)}, u32[]{:S(2)}) collective-permute-start(bf16[16,128,128]{2,1,0:T(8,128)(2,1)S(1)} %get-tuple-element.83), channel_id=1, source_target_pairs={{0,1},{1,0},{2,3},{3,2},{4,5},{5,4},{6,7},{7,6},{8,9},{9,8},{10,11... | collective-permute-start | bytes 1572872 | tf_op jit(solution)/shard_map/ppermute | solution.py:448
  56.8 7.4 %collective-permute-start.18 = (bf16[4,128,128]{2,1,0:T(8,128)(2,1)S(1)}, bf16[4,128,128]{2,1,0:T(8,128)(2,1)S(1)}, u32[]{:S(2)}, u32[]{:S(2)}) collective-permute-start(bf16[4,128,128]{2,1,0:T(8,128)(2,1)S(1)} %get-tuple-element.84.rest_0_), channel_id=1, source_target_pairs={{8,0},{16,8},{24,16},{9,1},{17,9},{25,17},{10,2},{18,10},{26,18},{... | collective-permute-start | bytes 393224 | tf_op jit(solution)/shard_map/ppermute | solution.py:474
  58.1 12.5 %collective-permute-start.19 = (bf16[4,128,128]{2,1,0:T(8,128)(2,1)S(1)}, bf16[4,128,128]{2,1,0:T(8,128)(2,1)S(1)}, u32[]{:S(2)}, u32[]{:S(2)}) collective-permute-start(bf16[4,128,128]{2,1,0:T(8,128)(2,1)S(1)} %get-tuple-element.84.rest_0_), channel_id=1, source_target_pairs={{16,0},{24,8},{17,1},{25,9},{18,2},{26,10},{19,3},{27,11},{20,4},{... | collective-permute-start | bytes 393224 | tf_op jit(solution)/shard_map/ppermute | solution.py:474
  63.0 20.2 %collective-permute-start.17 = (bf16[16,128,128]{2,1,0:T(8,128)(2,1)S(1)}, bf16[16,128,128]{2,1,0:T(8,128)(2,1)S(1)}, u32[]{:S(2)}, u32[]{:S(2)}) collective-permute-start(bf16[16,128,128]{2,1,0:T(8,128)(2,1)S(1)} %get-tuple-element.92), channel_id=1, source_target_pairs={{0,1},{1,0},{2,3},{3,2},{4,5},{5,4},{6,7},{7,6},{8,9},{9,8},{10,11... | collective-permute-start | bytes 1572872 | tf_op jit(solution)/shard_map/ppermute | solution.py:448
  63.1 20.1 %collective-permute-start.27 = (bf16[128,2048]{1,0:T(8,128)(2,1)S(1)}, bf16[128,2048]{1,0:T(8,128)(2,1)S(1)}, u32[]{:S(2)}, u32[]{:S(2)}) collective-permute-start(bf16[128,2048]{1,0:T(8,128)(2,1)S(1)} %get-tuple-element.97), channel_id=1, source_target_pairs={{0,1},{1,0},{2,3},{3,2},{4,5},{5,4},{6,7},{7,6},{8,9},{9,8},{10,11... | collective-permute-start | bytes 1572872 | tf_op jit(solution)/shard_map/ppermute | solution.py:448
  71.5 7.0 %collective-permute-start.20 = (bf16[4,128,128]{2,1,0:T(8,128)(2,1)S(1)}, bf16[4,128,128]{2,1,0:T(8,128)(2,1)S(1)}, u32[]{:S(2)}, u32[]{:S(2)}) collective-permute-start(bf16[4,128,128]{2,1,0:T(8,128)(2,1)S(1)} %get-tuple-element.93), channel_id=1, source_target_pairs={{0,6},{1,7},{2,4},{3,5},{4,2},{5,3},{6,0},{7,1},{8,14},{9,15},{10,... | collective-permute-start | bytes 393224 | tf_op jit(solution)/shard_map/ppermute | solution.py:454
  72.8 6.5 %collective-permute-start.22 = (bf16[4,128,128]{2,1,0:T(8,128)(2,1)S(1)}, bf16[4,128,128]{2,1,0:T(8,128)(2,1)S(1)}, u32[]{:S(2)}, u32[]{:S(2)}) collective-permute-start(bf16[4,128,128]{2,1,0:T(8,128)(2,1)S(1)} %get-tuple-element.94), channel_id=1, source_target_pairs={{0,4},{1,5},{2,6},{3,7},{4,0},{5,1},{6,2},{7,3},{8,12},{9,13},{10,... | collective-permute-start | bytes 393224 | tf_op jit(solution)/shard_map/ppermute | solution.py:454
  73.9 6.0 %collective-permute-start.24 = (bf16[4,128,128]{2,1,0:T(8,128)(2,1)S(1)}, bf16[4,128,128]{2,1,0:T(8,128)(2,1)S(1)}, u32[]{:S(2)}, u32[]{:S(2)}) collective-permute-start(bf16[4,128,128]{2,1,0:T(8,128)(2,1)S(1)} %get-tuple-element.95), channel_id=1, source_target_pairs={{0,2},{1,3},{2,0},{3,1},{4,6},{5,7},{6,4},{7,5},{8,10},{9,11},{10,... | collective-permute-start | bytes 393224 | tf_op jit(solution)/shard_map/ppermute | solution.py:454
  78.5 1.4 %collective-permute-start.26 = (bf16[4,128,128]{2,1,0:T(8,128)(2,1)S(1)}, bf16[4,128,128]{2,1,0:T(8,128)(2,1)S(1)}, u32[]{:S(2)}, u32[]{:S(2)}) collective-permute-start(bf16[4,128,128]{2,1,0:T(8,128)(2,1)S(1)} %get-tuple-element.96.rest_3_), channel_id=1, source_target_pairs={{0,1},{1,0},{2,3},{3,2},{4,5},{5,4},{6,7},{7,6},{8,9},{9,8},{10,11... | collective-permute-start | bytes 393224 | tf_op jit(solution)/shard_map/ppermute | solution.py:448
  79.3 3.9 %collective-permute-start.21 = (bf16[4,128,128]{2,1,0:T(8,128)(2,1)S(1)}, bf16[4,128,128]{2,1,0:T(8,128)(2,1)S(1)}, u32[]{:S(2)}, u32[]{:S(2)}) collective-permute-start(bf16[4,128,128]{2,1,0:T(8,128)(2,1)S(1)} %collective-permute-done.20.rest_0_), channel_id=1, source_target_pairs={{0,1},{1,0},{2,3},{3,2},{4,5},{5,4},{6,7},{7,6},{8,9},{9,8},{10,11... | collective-permute-start | bytes 393224 | tf_op jit(solution)/shard_map/ppermute | solution.py:448
  79.9 3.3 %collective-permute-start.23 = (bf16[4,128,128]{2,1,0:T(8,128)(2,1)S(1)}, bf16[4,128,128]{2,1,0:T(8,128)(2,1)S(1)}, u32[]{:S(2)}, u32[]{:S(2)}) collective-permute-start(bf16[4,128,128]{2,1,0:T(8,128)(2,1)S(1)} %collective-permute-done.22.rest_1_), channel_id=1, source_target_pairs={{0,1},{1,0},{2,3},{3,2},{4,5},{5,4},{6,7},{7,6},{8,9},{9,8},{10,11... | collective-permute-start | bytes 393224 | tf_op jit(solution)/shard_map/ppermute | solution.py:448
  79.9 3.3 %collective-permute-start.25 = (bf16[4,128,128]{2,1,0:T(8,128)(2,1)S(1)}, bf16[4,128,128]{2,1,0:T(8,128)(2,1)S(1)}, u32[]{:S(2)}, u32[]{:S(2)}) collective-permute-start(bf16[4,128,128]{2,1,0:T(8,128)(2,1)S(1)} %collective-permute-done.24.rest_2_), channel_id=1, source_target_pairs={{0,1},{1,0},{2,3},{3,2},{4,5},{5,4},{6,7},{7,6},{8,9},{9,8},{10,11... | collective-permute-start | bytes 393224 | tf_op jit(solution)/shard_map/ppermute | solution.py:448

commit v17 on v16

--- a/solution.py
+++ b/solution.py
@@ -158,6 +158,11 @@
             turned[h, DH:] = jnp.where(late_head, t, 0.0).astype(BF16)
 
 
+def norm_order(chips):
+    order = list(reversed(range(chips)))
+    return order[1:2] + order[:1] + order[2:]
+
+
 def norm_kernel(lens, place, head_fq, turned, g, mate_g, part, *rest):
     kept = rest[-1]
     chips = (len(rest) - 9) // 2
@@ -173,7 +178,7 @@
 
     @pl.when(step == 0)
     def _():
-        for n, state in enumerate(incoming[::-1]):
+        for n, state in zip(norm_order(chips), incoming):
             owned = state.shape[0]
             came[pl.ds((chip ^ n) * owned, owned)] = state[...]
             sent_in[pl.ds((chip ^ n) * owned, owned)] = state[...]
@@ -577,7 +582,7 @@
         + [one_owner] * chips,
         [token_bf] + [narrow_bf] * 3 + [half_bf] * 4 + [owned_bf] * chips,
         [half_states],
-        (head_fq, turned, out_grad, mate_g, part, *chip_in[::-1]),
+        (head_fq, turned, out_grad, mate_g, part, *[chip_in[n] for n in norm_order(chips)]),
         (8 * product, 16 * array, 2 * half * count * DH),
         "normed",
     )

time: 86.4 us -> 87.3 us (1.010)
  waiting for transfers between devices: 24.6 us -> 25.5 us
  transfers between devices with their start and end apart: 28 -> 28, of which waited for: 10 -> 11; matrix products, arithmetic and copies ran while one was open for 0% -> 0% of each run, Pallas kernels for 22% -> 22%
where the time goes in v17:
time: 87.3 us; the launch traced here: 87.1 us
  Pallas kernels  32.2 us (37%)
  starting transfers between devices  28.4 us (33%)
  waiting for transfers between devices  25.5 us (29%)
  between operations  0.91 us (1%)
    pallas_call x13, Pallas kernels, run(): pl.pallas_call(kernel, grid_spec=pltpu.PrefetchScalarGridSpec(num_scalar_...  32.2 us
    ppermute x12, waiting for transfers between devices, exchange(): came[n] = lax.ppermute(states[n], LAYER, pairs)  18.1 us
    ppermute x12, starting transfers between devices, exchange(): came[n] = lax.ppermute(states[n], LAYER, pairs)  15.1 us
    ppermute x4, starting transfers between devices, reach_out(): others.insert(0, lax.ppermute(total, 'z', pairs))  10.6 us
    ppermute x4, waiting for transfers between devices, reach_out(): others.insert(0, lax.ppermute(total, 'z', pairs))  7.28 us
    ppermute x12, starting transfers between devices, swap(): return lax.ppermute(state, LAYER, [(i, i ^ 1) for i in range(members)])  2.81 us
  transfers between devices with their start and end apart: 28, of which 11 were waited for; matrix products, arithmetic and copies ran while one was open for 0% of the time, Pallas kernels for 22%

profile of v17, /device:TPU:0, one launch (start us, length us, event | category | flops | bytes accessed | tf_op | source)
XLA Modules:
  0.0 87.1 jit_solution(6355187981491848089)
XLA Ops:
  0.6 0.1 pad_add_fusion.place
  0.7 3.1 %tail_mate.1 = (bf16[16,128,128]{2,1,0:T(8,128)(2,1)S(1)}, bf16[3,128,2048]{2,1,0:T(8,128)(2,1)S(1)}, bf16[128,2048]{1,0:T(8,128)(2,1)S(1)}) custom-call(s32[8]{0:T(128)} %lens.25, s32[3]{0:T(128)S(1)} %pad_add_fusion.place, bf16[128,4096]{1,0:T(8,128)(2,1)} %k.13, bf16[128,4096]{1,0:T(8,128)(2,1)} %v.13, bf16[128,4096]{1,0:T(8,128)(2,1)} %q.5, ...), custom_call_target="tpu_custom_call" | custom-call | flops 67108864 | bytes 1572864 | tf_op jit(solution)/shard_map/tail_mate/pallas_call | solution.py:425
  3.8 0.0 copy-start.4
  3.8 0.5 collective-permute-start
  4.3 2.7 %tail_own.1.rest_5_ = bf16[16,128,128]{2,1,0:T(8,128)(2,1)S(1)} custom-call(s32[8]{0:T(128)} %lens.25, s32[3]{0:T(128)S(1)} %pad_add_fusion.place, bf16[128,4096]{1,0:T(8,128)(2,1)} %k.13, bf16[128,4096]{1,0:T(8,128)(2,1)} %v.13), custom_call_target="tpu_custom_call" | custom-call | flops 67108864 | bytes 1572864 | tf_op jit(solution)/shard_map/tail_own/pallas_call | solution.py:425
  7.1 0.0 collective-permute-done.earlier
  7.1 0.0 copy-start
  7.1 0.0 copy-start.1
  7.1 0.0 copy-start.2
  7.1 0.8 carried_chip.1
  7.9 0.1 collective-permute-start.1
  8.0 3.9 %collective-permute-start.2 = (bf16[4,128,128]{2,1,0:T(8,128)(2,1)S(1)}, bf16[4,128,128]{2,1,0:T(8,128)(2,1)S(1)}, u32[]{:S(2)}, u32[]{:S(2)}) collective-permute-start(bf16[4,128,128]{2,1,0:T(8,128)(2,1)S(1)} %get-tuple-element.60), channel_id=1, source_target_pairs={{0,6},{1,7},{2,4},{3,5},{4,2},{5,3},{6,0},{7,1},{8,14},{9,15},{10,... | collective-permute-start | bytes 393224 | tf_op jit(solution)/shard_map/ppermute | solution.py:459
  11.9 0.5 collective-permute-start.3
  12.4 0.0 collective-permute-start.4
  12.5 3.7 %collective-permute-done.2.rest_0_ = bf16[4,128,128]{2,1,0:T(8,128)(2,1)S(1)} collective-permute-done((bf16[4,128,128]{2,1,0:T(8,128)(2,1)S(1)}, bf16[4,128,128]{2,1,0:T(8,128)(2,1)S(1)}, u32[]{:S(2)}, u32[]{:S(2)}) %collective-permute-start.2) | collective-permute-done | bytes 131104 | tf_op jit(solution)/shard_map/ppermute | solution.py:459
  16.2 2.5 %collective-permute-done.3.rest_1_ = bf16[4,128,128]{2,1,0:T(8,128)(2,1)S(1)} collective-permute-done((bf16[4,128,128]{2,1,0:T(8,128)(2,1)S(1)}, bf16[4,128,128]{2,1,0:T(8,128)(2,1)S(1)}, u32[]{:S(2)}, u32[]{:S(2)}) %collective-permute-start.3) | collective-permute-done | bytes 131104 | tf_op jit(solution)/shard_map/ppermute | solution.py:459
  18.7 0.7 carried_total.1
  19.4 0.1 collective-permute-start.6
  19.5 0.5 collective-permute-start.5
  20.0 3.5 %collective-permute-start.7 = (bf16[4,128,128]{2,1,0:T(8,128)(2,1)S(1)}, bf16[4,128,128]{2,1,0:T(8,128)(2,1)S(1)}, u32[]{:S(2)}, u32[]{:S(2)}) collective-permute-start(bf16[4,128,128]{2,1,0:T(8,128)(2,1)S(1)} %get-tuple-element.68), channel_id=1, source_target_pairs={{0,8},{8,16},{16,24},{1,9},{9,17},{17,25},{2,10},{10,18},{18,26},{... | collective-permute-start | bytes 393224 | tf_op jit(solution)/shard_map/ppermute | solution.py:479
  23.5 4.5 %collective-permute-start.8 = (bf16[4,128,128]{2,1,0:T(8,128)(2,1)S(1)}, bf16[4,128,128]{2,1,0:T(8,128)(2,1)S(1)}, u32[]{:S(2)}, u32[]{:S(2)}) collective-permute-start(bf16[4,128,128]{2,1,0:T(8,128)(2,1)S(1)} %get-tuple-element.68), channel_id=1, source_target_pairs={{0,16},{8,24},{1,17},{9,25},{2,18},{10,26},{3,19},{11,27},{4,20},{... | collective-permute-start | bytes 393224 | tf_op jit(solution)/shard_map/ppermute | solution.py:479
  28.0 4.3 %within_chip.1 = (f32[256,2048]{1,0:T(8,128)S(1)}, bf16[256,2048]{1,0:T(8,128)(2,1)S(1)}, bf16[16,256,256]{2,1,0:T(8,128)(2,1)S(1)}) custom-call(s32[8]{0:T(128)S(1)} %copy-done.4, s32[3]{0:T(128)S(1)} %pad_add_fusion.place, bf16[128,4096]{1,0:T(8,128)(2,1)S(1)} %copy-done.2, bf16[128,4096]{1,0:T(8,128)(2,1)S(1)} %copy-done, ...), custom_call_target="tpu_custom_call" | custom-call | flops 671088640 | bytes 7340032 | tf_op jit(solution)/shard_map/within_chip/pallas_call | solution.py:425
  32.4 0.0 copy-start.3
  32.4 0.0 collective-permute-done.8.rest_7_
  32.4 0.0 collective-permute-done.6.rest_5_.earlier
  32.4 0.9 carried_prefix.1
  33.3 2.4 %collective-permute-start.10 = (bf16[4,128,128]{2,1,0:T(8,128)(2,1)S(1)}, bf16[4,128,128]{2,1,0:T(8,128)(2,1)S(1)}, u32[]{:S(2)}, u32[]{:S(2)}) collective-permute-start(bf16[4,128,128]{2,1,0:T(8,128)(2,1)S(1)} %get-tuple-element.70), channel_id=1, source_target_pairs={{0,6},{1,7},{2,4},{3,5},{4,2},{5,3},{6,0},{7,1},{8,14},{9,15},{10,... | collective-permute-start | bytes 393224 | tf_op jit(solution)/shard_map/ppermute | solution.py:459
  35.7 0.6 collective-permute-start.11
  36.3 0.5 collective-permute-start.9
  36.8 0.0 collective-permute-done.5.mate_g
  36.8 2.9 %collective-permute-done.10.rest_1_ = bf16[4,128,128]{2,1,0:T(8,128)(2,1)S(1)} collective-permute-done((bf16[4,128,128]{2,1,0:T(8,128)(2,1)S(1)}, bf16[4,128,128]{2,1,0:T(8,128)(2,1)S(1)}, u32[]{:S(2)}, u32[]{:S(2)}) %collective-permute-start.10) | collective-permute-done | bytes 131104 | tf_op jit(solution)/shard_map/ppermute | solution.py:459
  39.7 2.3 %collective-permute-done.11.rest_2_ = bf16[4,128,128]{2,1,0:T(8,128)(2,1)S(1)} collective-permute-done((bf16[4,128,128]{2,1,0:T(8,128)(2,1)S(1)}, bf16[4,128,128]{2,1,0:T(8,128)(2,1)S(1)}, u32[]{:S(2)}, u32[]{:S(2)}) %collective-permute-start.11) | collective-permute-done | bytes 131104 | tf_op jit(solution)/shard_map/ppermute | solution.py:459
  42.0 0.0 collective-permute-done.9.rest_0_
  42.0 5.3 %normed.1 = (bf16[128,4096]{1,0:T(8,128)(2,1)}, bf16[128,2048]{1,0:T(8,128)(2,1)S(1)}, bf16[128,2048]{1,0:T(8,128)(2,1)S(1)}, bf16[128,2048]{1,0:T(8,128)(2,1)S(...) custom-call(s32[8]{0:T(128)S(1)} %copy-done.4, ...), custom_call_target="tpu_custom_call" | custom-call | flops 536870912 | bytes 8388608 | tf_op jit(solution)/shard_map/normed/pallas_call | solution.py:425
  47.3 1.7 %collective-permute-start.12 = (bf16[4,128,128]{2,1,0:T(8,128)(2,1)S(1)}, bf16[4,128,128]{2,1,0:T(8,128)(2,1)S(1)}, u32[]{:S(2)}, u32[]{:S(2)}) collective-permute-start(bf16[4,128,128]{2,1,0:T(8,128)(2,1)S(1)} %get-tuple-element.73), channel_id=1, source_target_pairs={{0,6},{1,7},{2,4},{3,5},{4,2},{5,3},{6,0},{7,1},{8,14},{9,15},{10,... | collective-permute-start | bytes 393224 | tf_op jit(solution)/shard_map/ppermute | solution.py:459
  49.0 1.2 %collective-permute-start.13 = (bf16[4,128,128]{2,1,0:T(8,128)(2,1)S(1)}, bf16[4,128,128]{2,1,0:T(8,128)(2,1)S(1)}, u32[]{:S(2)}, u32[]{:S(2)}) collective-permute-start(bf16[4,128,128]{2,1,0:T(8,128)(2,1)S(1)} %get-tuple-element.74), channel_id=1, source_target_pairs={{0,4},{1,5},{2,6},{3,7},{4,0},{5,1},{6,2},{7,3},{8,12},{9,13},{10,... | collective-permute-start | bytes 393224 | tf_op jit(solution)/shard_map/ppermute | solution.py:459
  50.2 0.6 collective-permute-start.14
  50.8 3.5 %grads_within_0.1 = (bf16[128,4096]{1,0:T(8,128)(2,1)}, f32[128,4096]{1,0:T(8,128)S(1)}, f32[128,4096]{1,0:T(8,128)S(1)}) custom-call(s32[8]{0:T(128)S(1)} %copy-done.4, s32[3]{0:T(128)S(1)} %pad_add_fusion.place, bf16[128,4096]{1,0:T(8,128)(2,1)S(1)} %copy-done.2, bf16[128,4096]{1,0:T(8,128)(2,1)S(1)} %copy-done, bf16[128,4096]{1,0:T(8,128)(2,1)S(1)} %copy-done.1, ...), custom_call_target="tpu_custom_call" | custom-call | flops 469762048 | bytes 5767168 | tf_op jit(solution)/shard_map/grads_within_0/pallas_call | solution.py:425
  54.4 0.3 collective-permute-done.12.rest_0_
  54.6 1.6 %collective-permute-done.13.rest_1_ = bf16[4,128,128]{2,1,0:T(8,128)(2,1)S(1)} collective-permute-done((bf16[4,128,128]{2,1,0:T(8,128)(2,1)S(1)}, bf16[4,128,128]{2,1,0:T(8,128)(2,1)S(1)}, u32[]{:S(2)}, u32[]{:S(2)}) %collective-permute-start.13) | collective-permute-done | bytes 131104 | tf_op jit(solution)/shard_map/ppermute | solution.py:459
  56.2 0.0 collective-permute-done.14.rest_2_
  56.2 0.7 future_total.1
  56.9 0.1 collective-permute-start.15
  57.0 0.5 collective-permute-start.16
  57.5 1.3 %collective-permute-start.18 = (bf16[4,128,128]{2,1,0:T(8,128)(2,1)S(1)}, bf16[4,128,128]{2,1,0:T(8,128)(2,1)S(1)}, u32[]{:S(2)}, u32[]{:S(2)}) collective-permute-start(bf16[4,128,128]{2,1,0:T(8,128)(2,1)S(1)} %get-tuple-element.84.rest_0_), channel_id=1, source_target_pairs={{8,0},{16,8},{24,16},{9,1},{17,9},{25,17},{10,2},{18,10},{26,18},{... | collective-permute-start | bytes 393224 | tf_op jit(solution)/shard_map/ppermute | solution.py:479
  58.8 1.3 %collective-permute-start.19 = (bf16[4,128,128]{2,1,0:T(8,128)(2,1)S(1)}, bf16[4,128,128]{2,1,0:T(8,128)(2,1)S(1)}, u32[]{:S(2)}, u32[]{:S(2)}) collective-permute-start(bf16[4,128,128]{2,1,0:T(8,128)(2,1)S(1)} %get-tuple-element.84.rest_0_), channel_id=1, source_target_pairs={{16,0},{24,8},{17,1},{25,9},{18,2},{26,10},{19,3},{27,11},{20,4},{... | collective-permute-start | bytes 393224 | tf_op jit(solution)/shard_map/ppermute | solution.py:479
  60.1 0.0 collective-permute-done.16.passed
  60.1 3.6 %grads_within_1.1 = (bf16[128,4096]{1,0:T(8,128)(2,1)}, f32[128,4096]{1,0:T(8,128)S(1)}, f32[128,4096]{1,0:T(8,128)S(1)}, bf16[128,2048]{1,0:T(8,128)(2,1)S(1)}, bf16[16,128,128]{2,1,0:T(8,128)(2,1)S(1)}) custom-call(s32[8]{0:T(128)S(1)} %copy-done.4, ...), custom_call_target="tpu_custom_call", output_to_operand_aliasing={{0}: (9, {}), {1}: (10, {}), {2}: (11, {}), {3}: (12, {}), ... | custom-call | flops 469762048 | bytes 5767168 | tf_op jit(solution)/shard_map/grads_within_1/pallas_call | solution.py:425
  63.7 0.1 collective-permute-start.17
  63.8 0.4 collective-permute-start.27
  64.2 0.7 collective-permute-done.18.rest_5_
  64.9 6.6 %collective-permute-done.19.rest_6_ = bf16[4,128,128]{2,1,0:T(8,128)(2,1)S(1)} collective-permute-done((bf16[4,128,128]{2,1,0:T(8,128)(2,1)S(1)}, bf16[4,128,128]{2,1,0:T(8,128)(2,1)S(1)}, u32[]{:S(2)}, u32[]{:S(2)}) %collective-permute-start.19) | collective-permute-done | bytes 131104 | tf_op jit(solution)/shard_map/ppermute | solution.py:479
  71.5 0.9 future_prefix.1
  72.3 1.6 %collective-permute-start.20 = (bf16[4,128,128]{2,1,0:T(8,128)(2,1)S(1)}, bf16[4,128,128]{2,1,0:T(8,128)(2,1)S(1)}, u32[]{:S(2)}, u32[]{:S(2)}) collective-permute-start(bf16[4,128,128]{2,1,0:T(8,128)(2,1)S(1)} %get-tuple-element.93), channel_id=1, source_target_pairs={{0,6},{1,7},{2,4},{3,5},{4,2},{5,3},{6,0},{7,1},{8,14},{9,15},{10,... | collective-permute-start | bytes 393224 | tf_op jit(solution)/shard_map/ppermute | solution.py:459
  73.9 1.4 %collective-permute-start.22 = (bf16[4,128,128]{2,1,0:T(8,128)(2,1)S(1)}, bf16[4,128,128]{2,1,0:T(8,128)(2,1)S(1)}, u32[]{:S(2)}, u32[]{:S(2)}) collective-permute-start(bf16[4,128,128]{2,1,0:T(8,128)(2,1)S(1)} %get-tuple-element.94), channel_id=1, source_target_pairs={{0,4},{1,5},{2,6},{3,7},{4,0},{5,1},{6,2},{7,3},{8,12},{9,13},{10,... | collective-permute-start | bytes 393224 | tf_op jit(solution)/shard_map/ppermute | solution.py:459
  75.3 0.6 collective-permute-start.24
  75.9 3.6 %collective-permute-done.20.rest_0_ = bf16[4,128,128]{2,1,0:T(8,128)(2,1)S(1)} collective-permute-done((bf16[4,128,128]{2,1,0:T(8,128)(2,1)S(1)}, bf16[4,128,128]{2,1,0:T(8,128)(2,1)S(1)}, u32[]{:S(2)}, u32[]{:S(2)}) %collective-permute-start.20) | collective-permute-done | bytes 131104 | tf_op jit(solution)/shard_map/ppermute | solution.py:459
  79.5 0.0 collective-permute-start.26
  79.5 1.3 %collective-permute-done.22.rest_1_ = bf16[4,128,128]{2,1,0:T(8,128)(2,1)S(1)} collective-permute-done((bf16[4,128,128]{2,1,0:T(8,128)(2,1)S(1)}, bf16[4,128,128]{2,1,0:T(8,128)(2,1)S(1)}, u32[]{:S(2)}, u32[]{:S(2)}) %collective-permute-start.22) | collective-permute-done | bytes 131104 | tf_op jit(solution)/shard_map/ppermute | solution.py:459
  80.7 0.1 collective-permute-done.24.rest_2_
  80.8 0.5 collective-permute-start.23
  81.3 0.1 collective-permute-start.25
  81.3 2.8 %grads_last_0.1 = (bf16[128,4096]{1,0:T(8,128)(2,1)}, bf16[128,4096]{1,0:T(8,128)(2,1)}) custom-call(s32[8]{0:T(128)S(1)} %copy-done.4, s32[3]{0:T(128)S(1)} %pad_add_fusion.place, bf16[128,4096]{1,0:T(8,128)(2,1)S(1)} %copy-done, bf16[128,4096]{1,0:T(8,128)(2,1)S(1)} %copy-done.1, f32[128,4096]{1,0:T(8,128)S(1)} %get-tuple-element.90.rest_4_.gk_part, ...), custom_call_target="tpu_custom_call" | custom-call | flops 134217728 | bytes 4718592 | tf_op jit(solution)/shard_map/grads_last_0/pallas_call | solution.py:425
  84.1 3.0 %grads_last_1.1 = (bf16[128,4096]{1,0:T(8,128)(2,1)}, bf16[128,4096]{1,0:T(8,128)(2,1)}, bf16[128,4096]{1,0:T(8,128)(2,1)}) custom-call(s32[8]{0:T(128)S(1)} %copy-done.4, s32[3]{0:T(128)S(1)} %pad_add_fusion.place, bf16[128,4096]{1,0:T(8,128)(2,1)S(1)} %copy-done, ...), custom_call_target="tpu_custom_call", output_to_operand_aliasing={{0}: (12, {}), {1}: (13, {}), {2}: (14, {})} | custom-call | flops 134217728 | bytes 4718592 | tf_op jit(solution)/shard_map/grads_last_1/pallas_call | solution.py:425
  (16 shorter events, 0.0 us)
Async XLA Ops:
  3.8 3.3 %copy-start.4 = (s32[8]{0:T(128)S(1)}, s32[8]{0:T(128)}, u32[]{:S(2)}) copy-start(s32[8]{0:T(128)} %lens.25) | copy-start | bytes 100
  3.8 3.2 %collective-permute-start = (bf16[16,128,128]{2,1,0:T(8,128)(2,1)S(1)}, bf16[16,128,128]{2,1,0:T(8,128)(2,1)S(1)}, u32[]{:S(2)}, u32[]{:S(2)}) collective-permute-start(bf16[16,128,128]{2,1,0:T(8,128)(2,1)S(1)} %get-tuple-element.55), channel_id=1, source_target_pairs={{0,1},{1,0},{2,3},{3,2},{4,5},{5,4},{6,7},{7,6},{8,9},{9,8},{10,11... | collective-permute-start | bytes 1572872 | tf_op jit(solution)/shard_map/ppermute | solution.py:453
  7.1 20.9 %copy-start = (bf16[128,4096]{1,0:T(8,128)(2,1)S(1)}, bf16[128,4096]{1,0:T(8,128)(2,1)}, u32[]{:S(2)}) copy-start(bf16[128,4096]{1,0:T(8,128)(2,1)} %k.13) | copy-start | bytes 3145732
  7.1 20.9 %copy-start.1 = (bf16[128,4096]{1,0:T(8,128)(2,1)S(1)}, bf16[128,4096]{1,0:T(8,128)(2,1)}, u32[]{:S(2)}) copy-start(bf16[128,4096]{1,0:T(8,128)(2,1)} %v.13) | copy-start | bytes 3145732
  7.1 20.9 %copy-start.2 = (bf16[128,4096]{1,0:T(8,128)(2,1)S(1)}, bf16[128,4096]{1,0:T(8,128)(2,1)}, u32[]{:S(2)}) copy-start(bf16[128,4096]{1,0:T(8,128)(2,1)} %q.5) | copy-start | bytes 3145732
  7.9 20.1 %collective-permute-start.1 = (bf16[3,128,2048]{2,1,0:T(8,128)(2,1)S(1)}, bf16[3,128,2048]{2,1,0:T(8,128)(2,1)S(1)}, u32[]{:S(2)}, u32[]{:S(2)}) collective-permute-start(bf16[3,128,2048]{2,1,0:T(8,128)(2,1)S(1)} %get-tuple-element.57), channel_id=1, source_target_pairs={{0,1},{1,0},{2,3},{3,2},{4,5},{5,4},{6,7},{7,6},{8,9},{9,8},{10,11... | collective-permute-start | bytes 4718600 | tf_op jit(solution)/shard_map/ppermute | solution.py:453
  8.0 8.2 %collective-permute-start.2 = (bf16[4,128,128]{2,1,0:T(8,128)(2,1)S(1)}, bf16[4,128,128]{2,1,0:T(8,128)(2,1)S(1)}, u32[]{:S(2)}, u32[]{:S(2)}) collective-permute-start(bf16[4,128,128]{2,1,0:T(8,128)(2,1)S(1)} %get-tuple-element.60), channel_id=1, source_target_pairs={{0,6},{1,7},{2,4},{3,5},{4,2},{5,3},{6,0},{7,1},{8,14},{9,15},{10,... | collective-permute-start | bytes 393224 | tf_op jit(solution)/shard_map/ppermute | solution.py:459
  11.9 6.8 %collective-permute-start.3 = (bf16[4,128,128]{2,1,0:T(8,128)(2,1)S(1)}, bf16[4,128,128]{2,1,0:T(8,128)(2,1)S(1)}, u32[]{:S(2)}, u32[]{:S(2)}) collective-permute-start(bf16[4,128,128]{2,1,0:T(8,128)(2,1)S(1)} %get-tuple-element.61), channel_id=1, source_target_pairs={{0,4},{1,5},{2,6},{3,7},{4,0},{5,1},{6,2},{7,3},{8,12},{9,13},{10,... | collective-permute-start | bytes 393224 | tf_op jit(solution)/shard_map/ppermute | solution.py:459
  12.4 6.3 %collective-permute-start.4 = (bf16[4,128,128]{2,1,0:T(8,128)(2,1)S(1)}, bf16[4,128,128]{2,1,0:T(8,128)(2,1)S(1)}, u32[]{:S(2)}, u32[]{:S(2)}) collective-permute-start(bf16[4,128,128]{2,1,0:T(8,128)(2,1)S(1)} %get-tuple-element.62), channel_id=1, source_target_pairs={{0,2},{1,3},{2,0},{3,1},{4,6},{5,7},{6,4},{7,5},{8,10},{9,11},{10,... | collective-permute-start | bytes 393224 | tf_op jit(solution)/shard_map/ppermute | solution.py:459
  19.4 13.0 %collective-permute-start.6 = (bf16[16,128,128]{2,1,0:T(8,128)(2,1)S(1)}, bf16[16,128,128]{2,1,0:T(8,128)(2,1)S(1)}, u32[]{:S(2)}, u32[]{:S(2)}) collective-permute-start(bf16[16,128,128]{2,1,0:T(8,128)(2,1)S(1)} %get-tuple-element.67), channel_id=1, source_target_pairs={{0,1},{1,0},{2,3},{3,2},{4,5},{5,4},{6,7},{7,6},{8,9},{9,8},{10,11... | collective-permute-start | bytes 1572872 | tf_op jit(solution)/shard_map/ppermute | solution.py:453
  19.5 17.3 %collective-permute-start.5 = (bf16[128,2048]{1,0:T(8,128)(2,1)S(1)}, bf16[128,2048]{1,0:T(8,128)(2,1)S(1)}, u32[]{:S(2)}, u32[]{:S(2)}) collective-permute-start(bf16[128,2048]{1,0:T(8,128)(2,1)S(1)} %get-tuple-element.65), channel_id=1, source_target_pairs={{0,1},{1,0},{2,3},{3,2},{4,5},{5,4},{6,7},{7,6},{8,9},{9,8},{10,11... | collective-permute-start | bytes 1572872 | tf_op jit(solution)/shard_map/ppermute | solution.py:453
  20.0 12.4 %collective-permute-start.7 = (bf16[4,128,128]{2,1,0:T(8,128)(2,1)S(1)}, bf16[4,128,128]{2,1,0:T(8,128)(2,1)S(1)}, u32[]{:S(2)}, u32[]{:S(2)}) collective-permute-start(bf16[4,128,128]{2,1,0:T(8,128)(2,1)S(1)} %get-tuple-element.68), channel_id=1, source_target_pairs={{0,8},{8,16},{16,24},{1,9},{9,17},{17,25},{2,10},{10,18},{18,26},{... | collective-permute-start | bytes 393224 | tf_op jit(solution)/shard_map/ppermute | solution.py:479
  23.5 8.9 %collective-permute-start.8 = (bf16[4,128,128]{2,1,0:T(8,128)(2,1)S(1)}, bf16[4,128,128]{2,1,0:T(8,128)(2,1)S(1)}, u32[]{:S(2)}, u32[]{:S(2)}) collective-permute-start(bf16[4,128,128]{2,1,0:T(8,128)(2,1)S(1)} %get-tuple-element.68), channel_id=1, source_target_pairs={{0,16},{8,24},{1,17},{9,25},{2,18},{10,26},{3,19},{11,27},{4,20},{... | collective-permute-start | bytes 393224 | tf_op jit(solution)/shard_map/ppermute | solution.py:479
  32.4 9.7 %copy-start.3 = (bf16[128,4096]{1,0:T(8,128)(2,1)S(1)}, bf16[128,4096]{1,0:T(8,128)(2,1)}, u32[]{:S(2)}) copy-start(bf16[128,4096]{1,0:T(8,128)(2,1)} %g.1) | copy-start | bytes 3145732
  33.3 6.4 %collective-permute-start.10 = (bf16[4,128,128]{2,1,0:T(8,128)(2,1)S(1)}, bf16[4,128,128]{2,1,0:T(8,128)(2,1)S(1)}, u32[]{:S(2)}, u32[]{:S(2)}) collective-permute-start(bf16[4,128,128]{2,1,0:T(8,128)(2,1)S(1)} %get-tuple-element.70), channel_id=1, source_target_pairs={{0,6},{1,7},{2,4},{3,5},{4,2},{5,3},{6,0},{7,1},{8,14},{9,15},{10,... | collective-permute-start | bytes 393224 | tf_op jit(solution)/shard_map/ppermute | solution.py:459
  35.7 6.3 %collective-permute-start.11 = (bf16[4,128,128]{2,1,0:T(8,128)(2,1)S(1)}, bf16[4,128,128]{2,1,0:T(8,128)(2,1)S(1)}, u32[]{:S(2)}, u32[]{:S(2)}) collective-permute-start(bf16[4,128,128]{2,1,0:T(8,128)(2,1)S(1)} %get-tuple-element.71), channel_id=1, source_target_pairs={{0,2},{1,3},{2,0},{3,1},{4,6},{5,7},{6,4},{7,5},{8,10},{9,11},{10,... | collective-permute-start | bytes 393224 | tf_op jit(solution)/shard_map/ppermute | solution.py:459
  36.3 5.7 %collective-permute-start.9 = (bf16[4,128,128]{2,1,0:T(8,128)(2,1)S(1)}, bf16[4,128,128]{2,1,0:T(8,128)(2,1)S(1)}, u32[]{:S(2)}, u32[]{:S(2)}) collective-permute-start(bf16[4,128,128]{2,1,0:T(8,128)(2,1)S(1)} %get-tuple-element.69), channel_id=1, source_target_pairs={{0,4},{1,5},{2,6},{3,7},{4,0},{5,1},{6,2},{7,3},{8,12},{9,13},{10,... | collective-permute-start | bytes 393224 | tf_op jit(solution)/shard_map/ppermute | solution.py:459
  47.3 7.3 %collective-permute-start.12 = (bf16[4,128,128]{2,1,0:T(8,128)(2,1)S(1)}, bf16[4,128,128]{2,1,0:T(8,128)(2,1)S(1)}, u32[]{:S(2)}, u32[]{:S(2)}) collective-permute-start(bf16[4,128,128]{2,1,0:T(8,128)(2,1)S(1)} %get-tuple-element.73), channel_id=1, source_target_pairs={{0,6},{1,7},{2,4},{3,5},{4,2},{5,3},{6,0},{7,1},{8,14},{9,15},{10,... | collective-permute-start | bytes 393224 | tf_op jit(solution)/shard_map/ppermute | solution.py:459
  49.0 7.2 %collective-permute-start.13 = (bf16[4,128,128]{2,1,0:T(8,128)(2,1)S(1)}, bf16[4,128,128]{2,1,0:T(8,128)(2,1)S(1)}, u32[]{:S(2)}, u32[]{:S(2)}) collective-permute-start(bf16[4,128,128]{2,1,0:T(8,128)(2,1)S(1)} %get-tuple-element.74), channel_id=1, source_target_pairs={{0,4},{1,5},{2,6},{3,7},{4,0},{5,1},{6,2},{7,3},{8,12},{9,13},{10,... | collective-permute-start | bytes 393224 | tf_op jit(solution)/shard_map/ppermute | solution.py:459
  50.2 6.0 %collective-permute-start.14 = (bf16[4,128,128]{2,1,0:T(8,128)(2,1)S(1)}, bf16[4,128,128]{2,1,0:T(8,128)(2,1)S(1)}, u32[]{:S(2)}, u32[]{:S(2)}) collective-permute-start(bf16[4,128,128]{2,1,0:T(8,128)(2,1)S(1)} %get-tuple-element.75), channel_id=1, source_target_pairs={{0,2},{1,3},{2,0},{3,1},{4,6},{5,7},{6,4},{7,5},{8,10},{9,11},{10,... | collective-permute-start | bytes 393224 | tf_op jit(solution)/shard_map/ppermute | solution.py:459
  56.9 3.2 %collective-permute-start.15 = (bf16[128,2048]{1,0:T(8,128)(2,1)S(1)}, bf16[128,2048]{1,0:T(8,128)(2,1)S(1)}, u32[]{:S(2)}, u32[]{:S(2)}) collective-permute-start(bf16[128,2048]{1,0:T(8,128)(2,1)S(1)} %get-tuple-element.82), channel_id=1, source_target_pairs={{0,1},{1,0},{2,3},{3,2},{4,5},{5,4},{6,7},{7,6},{8,9},{9,8},{10,11... | collective-permute-start | bytes 1572872 | tf_op jit(solution)/shard_map/ppermute | solution.py:453
  57.0 3.1 %collective-permute-start.16 = (bf16[16,128,128]{2,1,0:T(8,128)(2,1)S(1)}, bf16[16,128,128]{2,1,0:T(8,128)(2,1)S(1)}, u32[]{:S(2)}, u32[]{:S(2)}) collective-permute-start(bf16[16,128,128]{2,1,0:T(8,128)(2,1)S(1)} %get-tuple-element.83), channel_id=1, source_target_pairs={{0,1},{1,0},{2,3},{3,2},{4,5},{5,4},{6,7},{7,6},{8,9},{9,8},{10,11... | collective-permute-start | bytes 1572872 | tf_op jit(solution)/shard_map/ppermute | solution.py:453
  57.5 7.4 %collective-permute-start.18 = (bf16[4,128,128]{2,1,0:T(8,128)(2,1)S(1)}, bf16[4,128,128]{2,1,0:T(8,128)(2,1)S(1)}, u32[]{:S(2)}, u32[]{:S(2)}) collective-permute-start(bf16[4,128,128]{2,1,0:T(8,128)(2,1)S(1)} %get-tuple-element.84.rest_0_), channel_id=1, source_target_pairs={{8,0},{16,8},{24,16},{9,1},{17,9},{25,17},{10,2},{18,10},{26,18},{... | collective-permute-start | bytes 393224 | tf_op jit(solution)/shard_map/ppermute | solution.py:479
  58.8 12.7 %collective-permute-start.19 = (bf16[4,128,128]{2,1,0:T(8,128)(2,1)S(1)}, bf16[4,128,128]{2,1,0:T(8,128)(2,1)S(1)}, u32[]{:S(2)}, u32[]{:S(2)}) collective-permute-start(bf16[4,128,128]{2,1,0:T(8,128)(2,1)S(1)} %get-tuple-element.84.rest_0_), channel_id=1, source_target_pairs={{16,0},{24,8},{17,1},{25,9},{18,2},{26,10},{19,3},{27,11},{20,4},{... | collective-permute-start | bytes 393224 | tf_op jit(solution)/shard_map/ppermute | solution.py:479
  63.7 20.4 %collective-permute-start.17 = (bf16[16,128,128]{2,1,0:T(8,128)(2,1)S(1)}, bf16[16,128,128]{2,1,0:T(8,128)(2,1)S(1)}, u32[]{:S(2)}, u32[]{:S(2)}) collective-permute-start(bf16[16,128,128]{2,1,0:T(8,128)(2,1)S(1)} %get-tuple-element.92), channel_id=1, source_target_pairs={{0,1},{1,0},{2,3},{3,2},{4,5},{5,4},{6,7},{7,6},{8,9},{9,8},{10,11... | collective-permute-start | bytes 1572872 | tf_op jit(solution)/shard_map/ppermute | solution.py:453
  63.8 20.4 %collective-permute-start.27 = (bf16[128,2048]{1,0:T(8,128)(2,1)S(1)}, bf16[128,2048]{1,0:T(8,128)(2,1)S(1)}, u32[]{:S(2)}, u32[]{:S(2)}) collective-permute-start(bf16[128,2048]{1,0:T(8,128)(2,1)S(1)} %get-tuple-element.97), channel_id=1, source_target_pairs={{0,1},{1,0},{2,3},{3,2},{4,5},{5,4},{6,7},{7,6},{8,9},{9,8},{10,11... | collective-permute-start | bytes 1572872 | tf_op jit(solution)/shard_map/ppermute | solution.py:453
  72.3 7.1 %collective-permute-start.20 = (bf16[4,128,128]{2,1,0:T(8,128)(2,1)S(1)}, bf16[4,128,128]{2,1,0:T(8,128)(2,1)S(1)}, u32[]{:S(2)}, u32[]{:S(2)}) collective-permute-start(bf16[4,128,128]{2,1,0:T(8,128)(2,1)S(1)} %get-tuple-element.93), channel_id=1, source_target_pairs={{0,6},{1,7},{2,4},{3,5},{4,2},{5,3},{6,0},{7,1},{8,14},{9,15},{10,... | collective-permute-start | bytes 393224 | tf_op jit(solution)/shard_map/ppermute | solution.py:459
  73.9 6.8 %collective-permute-start.22 = (bf16[4,128,128]{2,1,0:T(8,128)(2,1)S(1)}, bf16[4,128,128]{2,1,0:T(8,128)(2,1)S(1)}, u32[]{:S(2)}, u32[]{:S(2)}) collective-permute-start(bf16[4,128,128]{2,1,0:T(8,128)(2,1)S(1)} %get-tuple-element.94), channel_id=1, source_target_pairs={{0,4},{1,5},{2,6},{3,7},{4,0},{5,1},{6,2},{7,3},{8,12},{9,13},{10,... | collective-permute-start | bytes 393224 | tf_op jit(solution)/shard_map/ppermute | solution.py:459
  75.3 5.5 %collective-permute-start.24 = (bf16[4,128,128]{2,1,0:T(8,128)(2,1)S(1)}, bf16[4,128,128]{2,1,0:T(8,128)(2,1)S(1)}, u32[]{:S(2)}, u32[]{:S(2)}) collective-permute-start(bf16[4,128,128]{2,1,0:T(8,128)(2,1)S(1)} %get-tuple-element.95), channel_id=1, source_target_pairs={{0,2},{1,3},{2,0},{3,1},{4,6},{5,7},{6,4},{7,5},{8,10},{9,11},{10,... | collective-permute-start | bytes 393224 | tf_op jit(solution)/shard_map/ppermute | solution.py:459
  79.5 1.8 %collective-permute-start.26 = (bf16[4,128,128]{2,1,0:T(8,128)(2,1)S(1)}, bf16[4,128,128]{2,1,0:T(8,128)(2,1)S(1)}, u32[]{:S(2)}, u32[]{:S(2)}) collective-permute-start(bf16[4,128,128]{2,1,0:T(8,128)(2,1)S(1)} %get-tuple-element.96.rest_3_), channel_id=1, source_target_pairs={{0,1},{1,0},{2,3},{3,2},{4,5},{5,4},{6,7},{7,6},{8,9},{9,8},{10,11... | collective-permute-start | bytes 393224 | tf_op jit(solution)/shard_map/ppermute | solution.py:453
  80.7 3.3 %collective-permute-start.21 = (bf16[4,128,128]{2,1,0:T(8,128)(2,1)S(1)}, bf16[4,128,128]{2,1,0:T(8,128)(2,1)S(1)}, u32[]{:S(2)}, u32[]{:S(2)}) collective-permute-start(bf16[4,128,128]{2,1,0:T(8,128)(2,1)S(1)} %collective-permute-done.20.rest_0_), channel_id=1, source_target_pairs={{0,1},{1,0},{2,3},{3,2},{4,5},{5,4},{6,7},{7,6},{8,9},{9,8},{10,11... | collective-permute-start | bytes 393224 | tf_op jit(solution)/shard_map/ppermute | solution.py:453
  80.8 3.3 %collective-permute-start.23 = (bf16[4,128,128]{2,1,0:T(8,128)(2,1)S(1)}, bf16[4,128,128]{2,1,0:T(8,128)(2,1)S(1)}, u32[]{:S(2)}, u32[]{:S(2)}) collective-permute-start(bf16[4,128,128]{2,1,0:T(8,128)(2,1)S(1)} %collective-permute-done.22.rest_1_), channel_id=1, source_target_pairs={{0,1},{1,0},{2,3},{3,2},{4,5},{5,4},{6,7},{7,6},{8,9},{9,8},{10,11... | collective-permute-start | bytes 393224 | tf_op jit(solution)/shard_map/ppermute | solution.py:453
  81.3 2.8 %collective-permute-start.25 = (bf16[4,128,128]{2,1,0:T(8,128)(2,1)S(1)}, bf16[4,128,128]{2,1,0:T(8,128)(2,1)S(1)}, u32[]{:S(2)}, u32[]{:S(2)}) collective-permute-start(bf16[4,128,128]{2,1,0:T(8,128)(2,1)S(1)} %collective-permute-done.24.rest_2_), channel_id=1, source_target_pairs={{0,1},{1,0},{2,3},{3,2},{4,5},{5,4},{6,7},{7,6},{8,9},{9,8},{10,11... | collective-permute-start | bytes 393224 | tf_op jit(solution)/shard_map/ppermute | solution.py:453

commit v18 on v16

--- a/solution.py
+++ b/solution.py
@@ -536,7 +536,7 @@
     )
     came, others, _, (mate_g, own_tail) = reach_out(merged, (mate_g, own_tail), True, "carried")
     mate_three, mate_g = swap(mate_three), swap(mate_g)
-    few = 4 if half % 4 == 0 else 1
+    few = max(n for n in (8, 4, 2, 1) if half % n == 0)
     parts = half // few
 
     def own_few(i, lens, place):

time: 86.4 us -> 86 us (level)
  Pallas kernels: 32.2 us -> 31.2 us
    pallas_call x13, Pallas kernels: 32.2 us -> 31.2 us  [run(): pl.pallas_call(kernel, grid_spec=pltpu.PrefetchScalarGridSpec(num_scalar_...]
where the time goes in v18:
time: 86 us; the launch traced here: 85.7 us
  Pallas kernels  31.2 us (36%)
  starting transfers between devices  28.6 us (33%)
  waiting for transfers between devices  24.9 us (29%)
  between operations  0.91 us (1%)
    pallas_call x13, Pallas kernels, run(): pl.pallas_call(kernel, grid_spec=pltpu.PrefetchScalarGridSpec(num_scalar_...  31.2 us
    ppermute x12, waiting for transfers between devices, exchange(): came[n] = lax.ppermute(states[n], LAYER, pairs)  17.4 us
    ppermute x12, starting transfers between devices, exchange(): came[n] = lax.ppermute(states[n], LAYER, pairs)  15.1 us
    ppermute x4, starting transfers between devices, reach_out(): others.insert(0, lax.ppermute(total, 'z', pairs))  10.7 us
    ppermute x4, waiting for transfers between devices, reach_out(): others.insert(0, lax.ppermute(total, 'z', pairs))  7.47 us
    ppermute x12, starting transfers between devices, swap(): return lax.ppermute(state, LAYER, [(i, i ^ 1) for i in range(members)])  2.8 us
  transfers between devices with their start and end apart: 28, of which 10 were waited for; matrix products, arithmetic and copies ran while one was open for 0% of the time, Pallas kernels for 22%

profile of v18, /device:TPU:0, one launch (start us, length us, event | category | flops | bytes accessed | tf_op | source)
XLA Modules:
  0.0 85.7 jit_solution(13676718419551951084)
XLA Ops:
  0.6 0.1 pad_add_fusion.place
  0.7 3.1 %tail_mate.1 = (bf16[16,128,128]{2,1,0:T(8,128)(2,1)S(1)}, bf16[3,128,2048]{2,1,0:T(8,128)(2,1)S(1)}, bf16[128,2048]{1,0:T(8,128)(2,1)S(1)}) custom-call(s32[8]{0:T(128)} %lens.25, s32[3]{0:T(128)S(1)} %pad_add_fusion.place, bf16[128,4096]{1,0:T(8,128)(2,1)} %k.13, bf16[128,4096]{1,0:T(8,128)(2,1)} %v.13, bf16[128,4096]{1,0:T(8,128)(2,1)} %q.5, ...), custom_call_target="tpu_custom_call" | custom-call | flops 67108864 | bytes 1572864 | tf_op jit(solution)/shard_map/tail_mate/pallas_call | solution.py:420
  3.8 0.0 copy-start.4
  3.8 0.5 collective-permute-start
  4.3 2.7 %tail_own.1.rest_5_ = bf16[16,128,128]{2,1,0:T(8,128)(2,1)S(1)} custom-call(s32[8]{0:T(128)} %lens.25, s32[3]{0:T(128)S(1)} %pad_add_fusion.place, bf16[128,4096]{1,0:T(8,128)(2,1)} %k.13, bf16[128,4096]{1,0:T(8,128)(2,1)} %v.13), custom_call_target="tpu_custom_call" | custom-call | flops 67108864 | bytes 1572864 | tf_op jit(solution)/shard_map/tail_own/pallas_call | solution.py:420
  7.1 0.0 collective-permute-done.earlier
  7.1 0.0 copy-start
  7.1 0.0 copy-start.1
  7.1 0.0 copy-start.2
  7.1 0.8 carried_chip.1
  7.9 0.1 collective-permute-start.1
  8.0 3.9 %collective-permute-start.2 = (bf16[4,128,128]{2,1,0:T(8,128)(2,1)S(1)}, bf16[4,128,128]{2,1,0:T(8,128)(2,1)S(1)}, u32[]{:S(2)}, u32[]{:S(2)}) collective-permute-start(bf16[4,128,128]{2,1,0:T(8,128)(2,1)S(1)} %get-tuple-element.60), channel_id=1, source_target_pairs={{0,6},{1,7},{2,4},{3,5},{4,2},{5,3},{6,0},{7,1},{8,14},{9,15},{10,... | collective-permute-start | bytes 393224 | tf_op jit(solution)/shard_map/ppermute | solution.py:454
  11.9 0.5 collective-permute-start.3
  12.4 0.0 collective-permute-start.4
  12.5 3.7 %collective-permute-done.2.rest_0_ = bf16[4,128,128]{2,1,0:T(8,128)(2,1)S(1)} collective-permute-done((bf16[4,128,128]{2,1,0:T(8,128)(2,1)S(1)}, bf16[4,128,128]{2,1,0:T(8,128)(2,1)S(1)}, u32[]{:S(2)}, u32[]{:S(2)}) %collective-permute-start.2) | collective-permute-done | bytes 131104 | tf_op jit(solution)/shard_map/ppermute | solution.py:454
  16.2 2.5 %collective-permute-done.3.rest_1_ = bf16[4,128,128]{2,1,0:T(8,128)(2,1)S(1)} collective-permute-done((bf16[4,128,128]{2,1,0:T(8,128)(2,1)S(1)}, bf16[4,128,128]{2,1,0:T(8,128)(2,1)S(1)}, u32[]{:S(2)}, u32[]{:S(2)}) %collective-permute-start.3) | collective-permute-done | bytes 131104 | tf_op jit(solution)/shard_map/ppermute | solution.py:454
  18.7 0.0 collective-permute-done.4.rest_2_
  18.7 0.7 carried_total.1
  19.4 0.1 collective-permute-start.6
  19.5 0.5 collective-permute-start.5
  20.0 3.5 %collective-permute-start.7 = (bf16[4,128,128]{2,1,0:T(8,128)(2,1)S(1)}, bf16[4,128,128]{2,1,0:T(8,128)(2,1)S(1)}, u32[]{:S(2)}, u32[]{:S(2)}) collective-permute-start(bf16[4,128,128]{2,1,0:T(8,128)(2,1)S(1)} %get-tuple-element.68), channel_id=1, source_target_pairs={{0,8},{8,16},{16,24},{1,9},{9,17},{17,25},{2,10},{10,18},{18,26},{... | collective-permute-start | bytes 393224 | tf_op jit(solution)/shard_map/ppermute | solution.py:474
  23.5 4.5 %collective-permute-start.8 = (bf16[4,128,128]{2,1,0:T(8,128)(2,1)S(1)}, bf16[4,128,128]{2,1,0:T(8,128)(2,1)S(1)}, u32[]{:S(2)}, u32[]{:S(2)}) collective-permute-start(bf16[4,128,128]{2,1,0:T(8,128)(2,1)S(1)} %get-tuple-element.68), channel_id=1, source_target_pairs={{0,16},{8,24},{1,17},{9,25},{2,18},{10,26},{3,19},{11,27},{4,20},{... | collective-permute-start | bytes 393224 | tf_op jit(solution)/shard_map/ppermute | solution.py:474
  28.0 0.0 collective-permute-done.1.mate
  28.0 3.7 %within_chip.1 = (f32[256,2048]{1,0:T(8,128)S(1)}, bf16[256,2048]{1,0:T(8,128)(2,1)S(1)}, bf16[16,256,256]{2,1,0:T(8,128)(2,1)S(1)}) custom-call(s32[8]{0:T(128)S(1)} %copy-done.4, s32[3]{0:T(128)S(1)} %pad_add_fusion.place, bf16[128,4096]{1,0:T(8,128)(2,1)S(1)} %copy-done.2, bf16[128,4096]{1,0:T(8,128)(2,1)S(1)} %copy-done, ...), custom_call_target="tpu_custom_call" | custom-call | flops 671088640 | bytes 7340032 | tf_op jit(solution)/shard_map/within_chip/pallas_call | solution.py:420
  31.8 0.0 copy-start.3
  31.8 0.0 collective-permute-done.8.rest_7_
  31.8 0.0 collective-permute-done.6.rest_5_.earlier
  31.8 0.9 %carried_prefix.1 = (bf16[4,128,128]{2,1,0:T(8,128)(2,1)S(1)}, bf16[4,128,128]{2,1,0:T(8,128)(2,1)S(1)}, bf16[4,128,128]{2,1,0:T(8,128)(2,1)S(1)}, bf16[4,128,128]{2,1,0:T(8,128)(2,1)S(1)}) custom-call(s32[8]{0:T(128)S(1)} %copy-done.4, s32[3]{0:T(128)S(1)} %pad_add_fusion.place, bf16[4,128,128]{2,1,0:T(8,128)(2,1)S(1)} %collective-permute-done.2.rest_0_, ...), custom_call_target="tpu_custom_call" | custom-call | flops 1048576 | bytes 1048576 | tf_op jit(solution)/shard_map/carried_prefix/pallas_call | solution.py:420
  32.7 1.6 %collective-permute-start.10 = (bf16[4,128,128]{2,1,0:T(8,128)(2,1)S(1)}, bf16[4,128,128]{2,1,0:T(8,128)(2,1)S(1)}, u32[]{:S(2)}, u32[]{:S(2)}) collective-permute-start(bf16[4,128,128]{2,1,0:T(8,128)(2,1)S(1)} %get-tuple-element.70), channel_id=1, source_target_pairs={{0,4},{1,5},{2,6},{3,7},{4,0},{5,1},{6,2},{7,3},{8,12},{9,13},{10,... | collective-permute-start | bytes 393224 | tf_op jit(solution)/shard_map/ppermute | solution.py:454
  34.3 1.5 %collective-permute-start.11 = (bf16[4,128,128]{2,1,0:T(8,128)(2,1)S(1)}, bf16[4,128,128]{2,1,0:T(8,128)(2,1)S(1)}, u32[]{:S(2)}, u32[]{:S(2)}) collective-permute-start(bf16[4,128,128]{2,1,0:T(8,128)(2,1)S(1)} %get-tuple-element.71), channel_id=1, source_target_pairs={{0,2},{1,3},{2,0},{3,1},{4,6},{5,7},{6,4},{7,5},{8,10},{9,11},{10,... | collective-permute-start | bytes 393224 | tf_op jit(solution)/shard_map/ppermute | solution.py:454
  35.7 0.5 collective-permute-start.9
  36.3 0.0 collective-permute-done.5.mate_g
  36.3 1.9 %collective-permute-done.10.rest_1_ = bf16[4,128,128]{2,1,0:T(8,128)(2,1)S(1)} collective-permute-done((bf16[4,128,128]{2,1,0:T(8,128)(2,1)S(1)}, bf16[4,128,128]{2,1,0:T(8,128)(2,1)S(1)}, u32[]{:S(2)}, u32[]{:S(2)}) %collective-permute-start.10) | collective-permute-done | bytes 131104 | tf_op jit(solution)/shard_map/ppermute | solution.py:454
  38.2 3.8 %collective-permute-done.11.rest_2_ = bf16[4,128,128]{2,1,0:T(8,128)(2,1)S(1)} collective-permute-done((bf16[4,128,128]{2,1,0:T(8,128)(2,1)S(1)}, bf16[4,128,128]{2,1,0:T(8,128)(2,1)S(1)}, u32[]{:S(2)}, u32[]{:S(2)}) %collective-permute-start.11) | collective-permute-done | bytes 131104 | tf_op jit(solution)/shard_map/ppermute | solution.py:454
  42.0 0.0 collective-permute-done.9.rest_0_
  42.0 4.9 %normed.1 = (bf16[128,4096]{1,0:T(8,128)(2,1)}, bf16[128,2048]{1,0:T(8,128)(2,1)S(1)}, bf16[128,2048]{1,0:T(8,128)(2,1)S(1)}, bf16[128,2048]{1,0:T(8,128)(2,1)S(...) custom-call(s32[8]{0:T(128)S(1)} %copy-done.4, ...), custom_call_target="tpu_custom_call" | custom-call | flops 536870912 | bytes 8388608 | tf_op jit(solution)/shard_map/normed/pallas_call | solution.py:420
  46.9 1.1 %collective-permute-start.12 = (bf16[4,128,128]{2,1,0:T(8,128)(2,1)S(1)}, bf16[4,128,128]{2,1,0:T(8,128)(2,1)S(1)}, u32[]{:S(2)}, u32[]{:S(2)}) collective-permute-start(bf16[4,128,128]{2,1,0:T(8,128)(2,1)S(1)} %get-tuple-element.73), channel_id=1, source_target_pairs={{0,6},{1,7},{2,4},{3,5},{4,2},{5,3},{6,0},{7,1},{8,14},{9,15},{10,... | collective-permute-start | bytes 393224 | tf_op jit(solution)/shard_map/ppermute | solution.py:454
  48.1 1.5 %collective-permute-start.13 = (bf16[4,128,128]{2,1,0:T(8,128)(2,1)S(1)}, bf16[4,128,128]{2,1,0:T(8,128)(2,1)S(1)}, u32[]{:S(2)}, u32[]{:S(2)}) collective-permute-start(bf16[4,128,128]{2,1,0:T(8,128)(2,1)S(1)} %get-tuple-element.74), channel_id=1, source_target_pairs={{0,4},{1,5},{2,6},{3,7},{4,0},{5,1},{6,2},{7,3},{8,12},{9,13},{10,... | collective-permute-start | bytes 393224 | tf_op jit(solution)/shard_map/ppermute | solution.py:454
  49.6 0.8 collective-permute-start.14
  50.4 3.5 %grads_within_0.1 = (bf16[128,4096]{1,0:T(8,128)(2,1)}, f32[128,4096]{1,0:T(8,128)S(1)}, f32[128,4096]{1,0:T(8,128)S(1)}) custom-call(s32[8]{0:T(128)S(1)} %copy-done.4, s32[3]{0:T(128)S(1)} %pad_add_fusion.place, bf16[128,4096]{1,0:T(8,128)(2,1)S(1)} %copy-done.2, bf16[128,4096]{1,0:T(8,128)(2,1)S(1)} %copy-done, bf16[128,4096]{1,0:T(8,128)(2,1)S(1)} %copy-done.1, ...), custom_call_target="tpu_custom_call" | custom-call | flops 469762048 | bytes 5767168 | tf_op jit(solution)/shard_map/grads_within_0/pallas_call | solution.py:420
  54.0 0.0 collective-permute-done.13.rest_1_
  54.0 0.6 collective-permute-done.14.rest_2_
  54.6 0.7 future_total.1
  55.3 0.1 collective-permute-start.15
  55.4 0.5 collective-permute-start.16
  55.9 1.3 %collective-permute-start.18 = (bf16[4,128,128]{2,1,0:T(8,128)(2,1)S(1)}, bf16[4,128,128]{2,1,0:T(8,128)(2,1)S(1)}, u32[]{:S(2)}, u32[]{:S(2)}) collective-permute-start(bf16[4,128,128]{2,1,0:T(8,128)(2,1)S(1)} %get-tuple-element.84.rest_0_), channel_id=1, source_target_pairs={{8,0},{16,8},{24,16},{9,1},{17,9},{25,17},{10,2},{18,10},{26,18},{... | collective-permute-start | bytes 393224 | tf_op jit(solution)/shard_map/ppermute | solution.py:474
  57.2 1.5 %collective-permute-start.19 = (bf16[4,128,128]{2,1,0:T(8,128)(2,1)S(1)}, bf16[4,128,128]{2,1,0:T(8,128)(2,1)S(1)}, u32[]{:S(2)}, u32[]{:S(2)}) collective-permute-start(bf16[4,128,128]{2,1,0:T(8,128)(2,1)S(1)} %get-tuple-element.84.rest_0_), channel_id=1, source_target_pairs={{16,0},{24,8},{17,1},{25,9},{18,2},{26,10},{19,3},{27,11},{20,4},{... | collective-permute-start | bytes 393224 | tf_op jit(solution)/shard_map/ppermute | solution.py:474
  58.6 0.0 collective-permute-done.15.grad_att
  58.6 0.0 collective-permute-done.16.passed
  58.7 3.6 %grads_within_1.1 = (bf16[128,4096]{1,0:T(8,128)(2,1)}, f32[128,4096]{1,0:T(8,128)S(1)}, f32[128,4096]{1,0:T(8,128)S(1)}, bf16[128,2048]{1,0:T(8,128)(2,1)S(1)}, bf16[16,128,128]{2,1,0:T(8,128)(2,1)S(1)}) custom-call(s32[8]{0:T(128)S(1)} %copy-done.4, ...), custom_call_target="tpu_custom_call", output_to_operand_aliasing={{0}: (9, {}), {1}: (10, {}), {2}: (11, {}), {3}: (12, {}), ... | custom-call | flops 469762048 | bytes 5767168 | tf_op jit(solution)/shard_map/grads_within_1/pallas_call | solution.py:420
  62.2 0.1 collective-permute-start.17
  62.3 0.4 collective-permute-start.27
  62.7 0.7 collective-permute-done.18.rest_5_
  63.4 6.8 %collective-permute-done.19.rest_6_ = bf16[4,128,128]{2,1,0:T(8,128)(2,1)S(1)} collective-permute-done((bf16[4,128,128]{2,1,0:T(8,128)(2,1)S(1)}, bf16[4,128,128]{2,1,0:T(8,128)(2,1)S(1)}, u32[]{:S(2)}, u32[]{:S(2)}) %collective-permute-start.19) | collective-permute-done | bytes 131104 | tf_op jit(solution)/shard_map/ppermute | solution.py:474
  70.2 0.9 %future_prefix.1 = (bf16[4,128,128]{2,1,0:T(8,128)(2,1)S(1)}, bf16[4,128,128]{2,1,0:T(8,128)(2,1)S(1)}, bf16[4,128,128]{2,1,0:T(8,128)(2,1)S(1)}, bf16[4,128,128]{2,1,0:T(8,128)(2,1)S(1)}) custom-call(s32[8]{0:T(128)S(1)} %copy-done.4, s32[3]{0:T(128)S(1)} %pad_add_fusion.place, bf16[4,128,128]{2,1,0:T(8,128)(2,1)S(1)} %collective-permute-done.12.rest_0_, ...), custom_call_target="tpu_custom_call" | custom-call | flops 1048576 | bytes 1048576 | tf_op jit(solution)/shard_map/future_prefix/pallas_call | solution.py:420
  71.1 1.3 %collective-permute-start.20 = (bf16[4,128,128]{2,1,0:T(8,128)(2,1)S(1)}, bf16[4,128,128]{2,1,0:T(8,128)(2,1)S(1)}, u32[]{:S(2)}, u32[]{:S(2)}) collective-permute-start(bf16[4,128,128]{2,1,0:T(8,128)(2,1)S(1)} %get-tuple-element.93), channel_id=1, source_target_pairs={{0,6},{1,7},{2,4},{3,5},{4,2},{5,3},{6,0},{7,1},{8,14},{9,15},{10,... | collective-permute-start | bytes 393224 | tf_op jit(solution)/shard_map/ppermute | solution.py:454
  72.4 1.1 %collective-permute-start.22 = (bf16[4,128,128]{2,1,0:T(8,128)(2,1)S(1)}, bf16[4,128,128]{2,1,0:T(8,128)(2,1)S(1)}, u32[]{:S(2)}, u32[]{:S(2)}) collective-permute-start(bf16[4,128,128]{2,1,0:T(8,128)(2,1)S(1)} %get-tuple-element.94), channel_id=1, source_target_pairs={{0,4},{1,5},{2,6},{3,7},{4,0},{5,1},{6,2},{7,3},{8,12},{9,13},{10,... | collective-permute-start | bytes 393224 | tf_op jit(solution)/shard_map/ppermute | solution.py:454
  73.4 1.2 %collective-permute-start.24 = (bf16[4,128,128]{2,1,0:T(8,128)(2,1)S(1)}, bf16[4,128,128]{2,1,0:T(8,128)(2,1)S(1)}, u32[]{:S(2)}, u32[]{:S(2)}) collective-permute-start(bf16[4,128,128]{2,1,0:T(8,128)(2,1)S(1)} %get-tuple-element.95), channel_id=1, source_target_pairs={{0,2},{1,3},{2,0},{3,1},{4,6},{5,7},{6,4},{7,5},{8,10},{9,11},{10,... | collective-permute-start | bytes 393224 | tf_op jit(solution)/shard_map/ppermute | solution.py:454
  74.6 3.5 %collective-permute-done.20.rest_0_ = bf16[4,128,128]{2,1,0:T(8,128)(2,1)S(1)} collective-permute-done((bf16[4,128,128]{2,1,0:T(8,128)(2,1)S(1)}, bf16[4,128,128]{2,1,0:T(8,128)(2,1)S(1)}, u32[]{:S(2)}, u32[]{:S(2)}) %collective-permute-start.20) | collective-permute-done | bytes 131104 | tf_op jit(solution)/shard_map/ppermute | solution.py:454
  78.1 0.7 collective-permute-done.22.rest_1_
  78.9 0.6 collective-permute-done.24.rest_2_
  79.5 0.5 collective-permute-start.25
  80.0 2.8 %grads_last_0.1 = (bf16[128,4096]{1,0:T(8,128)(2,1)}, bf16[128,4096]{1,0:T(8,128)(2,1)}) custom-call(s32[8]{0:T(128)S(1)} %copy-done.4, s32[3]{0:T(128)S(1)} %pad_add_fusion.place, bf16[128,4096]{1,0:T(8,128)(2,1)S(1)} %copy-done, bf16[128,4096]{1,0:T(8,128)(2,1)S(1)} %copy-done.1, f32[128,4096]{1,0:T(8,128)S(1)} %get-tuple-element.90.rest_4_.gk_part, ...), custom_call_target="tpu_custom_call" | custom-call | flops 134217728 | bytes 4718592 | tf_op jit(solution)/shard_map/grads_last_0/pallas_call | solution.py:420
  82.8 2.9 %grads_last_1.1 = (bf16[128,4096]{1,0:T(8,128)(2,1)}, bf16[128,4096]{1,0:T(8,128)(2,1)}, bf16[128,4096]{1,0:T(8,128)(2,1)}) custom-call(s32[8]{0:T(128)S(1)} %copy-done.4, s32[3]{0:T(128)S(1)} %pad_add_fusion.place, bf16[128,4096]{1,0:T(8,128)(2,1)S(1)} %copy-done, ...), custom_call_target="tpu_custom_call", output_to_operand_aliasing={{0}: (12, {}), {1}: (13, {}), {2}: (14, {})} | custom-call | flops 134217728 | bytes 4718592 | tf_op jit(solution)/shard_map/grads_last_1/pallas_call | solution.py:420
  (16 shorter events, 0.0 us)
Async XLA Ops:
  3.8 3.3 %copy-start.4 = (s32[8]{0:T(128)S(1)}, s32[8]{0:T(128)}, u32[]{:S(2)}) copy-start(s32[8]{0:T(128)} %lens.25) | copy-start | bytes 100
  3.8 3.2 %collective-permute-start = (bf16[16,128,128]{2,1,0:T(8,128)(2,1)S(1)}, bf16[16,128,128]{2,1,0:T(8,128)(2,1)S(1)}, u32[]{:S(2)}, u32[]{:S(2)}) collective-permute-start(bf16[16,128,128]{2,1,0:T(8,128)(2,1)S(1)} %get-tuple-element.55), channel_id=1, source_target_pairs={{0,1},{1,0},{2,3},{3,2},{4,5},{5,4},{6,7},{7,6},{8,9},{9,8},{10,11... | collective-permute-start | bytes 1572872 | tf_op jit(solution)/shard_map/ppermute | solution.py:448
  7.1 20.9 %copy-start = (bf16[128,4096]{1,0:T(8,128)(2,1)S(1)}, bf16[128,4096]{1,0:T(8,128)(2,1)}, u32[]{:S(2)}) copy-start(bf16[128,4096]{1,0:T(8,128)(2,1)} %k.13) | copy-start | bytes 3145732
  7.1 20.9 %copy-start.1 = (bf16[128,4096]{1,0:T(8,128)(2,1)S(1)}, bf16[128,4096]{1,0:T(8,128)(2,1)}, u32[]{:S(2)}) copy-start(bf16[128,4096]{1,0:T(8,128)(2,1)} %v.13) | copy-start | bytes 3145732
  7.1 20.9 %copy-start.2 = (bf16[128,4096]{1,0:T(8,128)(2,1)S(1)}, bf16[128,4096]{1,0:T(8,128)(2,1)}, u32[]{:S(2)}) copy-start(bf16[128,4096]{1,0:T(8,128)(2,1)} %q.5) | copy-start | bytes 3145732
  7.9 20.1 %collective-permute-start.1 = (bf16[3,128,2048]{2,1,0:T(8,128)(2,1)S(1)}, bf16[3,128,2048]{2,1,0:T(8,128)(2,1)S(1)}, u32[]{:S(2)}, u32[]{:S(2)}) collective-permute-start(bf16[3,128,2048]{2,1,0:T(8,128)(2,1)S(1)} %get-tuple-element.57), channel_id=1, source_target_pairs={{0,1},{1,0},{2,3},{3,2},{4,5},{5,4},{6,7},{7,6},{8,9},{9,8},{10,11... | collective-permute-start | bytes 4718600 | tf_op jit(solution)/shard_map/ppermute | solution.py:448
  8.0 8.2 %collective-permute-start.2 = (bf16[4,128,128]{2,1,0:T(8,128)(2,1)S(1)}, bf16[4,128,128]{2,1,0:T(8,128)(2,1)S(1)}, u32[]{:S(2)}, u32[]{:S(2)}) collective-permute-start(bf16[4,128,128]{2,1,0:T(8,128)(2,1)S(1)} %get-tuple-element.60), channel_id=1, source_target_pairs={{0,6},{1,7},{2,4},{3,5},{4,2},{5,3},{6,0},{7,1},{8,14},{9,15},{10,... | collective-permute-start | bytes 393224 | tf_op jit(solution)/shard_map/ppermute | solution.py:454
  11.9 6.8 %collective-permute-start.3 = (bf16[4,128,128]{2,1,0:T(8,128)(2,1)S(1)}, bf16[4,128,128]{2,1,0:T(8,128)(2,1)S(1)}, u32[]{:S(2)}, u32[]{:S(2)}) collective-permute-start(bf16[4,128,128]{2,1,0:T(8,128)(2,1)S(1)} %get-tuple-element.61), channel_id=1, source_target_pairs={{0,4},{1,5},{2,6},{3,7},{4,0},{5,1},{6,2},{7,3},{8,12},{9,13},{10,... | collective-permute-start | bytes 393224 | tf_op jit(solution)/shard_map/ppermute | solution.py:454
  12.4 6.3 %collective-permute-start.4 = (bf16[4,128,128]{2,1,0:T(8,128)(2,1)S(1)}, bf16[4,128,128]{2,1,0:T(8,128)(2,1)S(1)}, u32[]{:S(2)}, u32[]{:S(2)}) collective-permute-start(bf16[4,128,128]{2,1,0:T(8,128)(2,1)S(1)} %get-tuple-element.62), channel_id=1, source_target_pairs={{0,2},{1,3},{2,0},{3,1},{4,6},{5,7},{6,4},{7,5},{8,10},{9,11},{10,... | collective-permute-start | bytes 393224 | tf_op jit(solution)/shard_map/ppermute | solution.py:454
  19.4 12.4 %collective-permute-start.6 = (bf16[16,128,128]{2,1,0:T(8,128)(2,1)S(1)}, bf16[16,128,128]{2,1,0:T(8,128)(2,1)S(1)}, u32[]{:S(2)}, u32[]{:S(2)}) collective-permute-start(bf16[16,128,128]{2,1,0:T(8,128)(2,1)S(1)} %get-tuple-element.67), channel_id=1, source_target_pairs={{0,1},{1,0},{2,3},{3,2},{4,5},{5,4},{6,7},{7,6},{8,9},{9,8},{10,11... | collective-permute-start | bytes 1572872 | tf_op jit(solution)/shard_map/ppermute | solution.py:448
  19.5 16.7 %collective-permute-start.5 = (bf16[128,2048]{1,0:T(8,128)(2,1)S(1)}, bf16[128,2048]{1,0:T(8,128)(2,1)S(1)}, u32[]{:S(2)}, u32[]{:S(2)}) collective-permute-start(bf16[128,2048]{1,0:T(8,128)(2,1)S(1)} %get-tuple-element.65), channel_id=1, source_target_pairs={{0,1},{1,0},{2,3},{3,2},{4,5},{5,4},{6,7},{7,6},{8,9},{9,8},{10,11... | collective-permute-start | bytes 1572872 | tf_op jit(solution)/shard_map/ppermute | solution.py:448
  20.0 11.8 %collective-permute-start.7 = (bf16[4,128,128]{2,1,0:T(8,128)(2,1)S(1)}, bf16[4,128,128]{2,1,0:T(8,128)(2,1)S(1)}, u32[]{:S(2)}, u32[]{:S(2)}) collective-permute-start(bf16[4,128,128]{2,1,0:T(8,128)(2,1)S(1)} %get-tuple-element.68), channel_id=1, source_target_pairs={{0,8},{8,16},{16,24},{1,9},{9,17},{17,25},{2,10},{10,18},{18,26},{... | collective-permute-start | bytes 393224 | tf_op jit(solution)/shard_map/ppermute | solution.py:474
  23.5 8.3 %collective-permute-start.8 = (bf16[4,128,128]{2,1,0:T(8,128)(2,1)S(1)}, bf16[4,128,128]{2,1,0:T(8,128)(2,1)S(1)}, u32[]{:S(2)}, u32[]{:S(2)}) collective-permute-start(bf16[4,128,128]{2,1,0:T(8,128)(2,1)S(1)} %get-tuple-element.68), channel_id=1, source_target_pairs={{0,16},{8,24},{1,17},{9,25},{2,18},{10,26},{3,19},{11,27},{4,20},{... | collective-permute-start | bytes 393224 | tf_op jit(solution)/shard_map/ppermute | solution.py:474
  31.8 10.2 %copy-start.3 = (bf16[128,4096]{1,0:T(8,128)(2,1)S(1)}, bf16[128,4096]{1,0:T(8,128)(2,1)}, u32[]{:S(2)}) copy-start(bf16[128,4096]{1,0:T(8,128)(2,1)} %g.1) | copy-start | bytes 3145732
  32.7 5.5 %collective-permute-start.10 = (bf16[4,128,128]{2,1,0:T(8,128)(2,1)S(1)}, bf16[4,128,128]{2,1,0:T(8,128)(2,1)S(1)}, u32[]{:S(2)}, u32[]{:S(2)}) collective-permute-start(bf16[4,128,128]{2,1,0:T(8,128)(2,1)S(1)} %get-tuple-element.70), channel_id=1, source_target_pairs={{0,4},{1,5},{2,6},{3,7},{4,0},{5,1},{6,2},{7,3},{8,12},{9,13},{10,... | collective-permute-start | bytes 393224 | tf_op jit(solution)/shard_map/ppermute | solution.py:454
  34.3 7.8 %collective-permute-start.11 = (bf16[4,128,128]{2,1,0:T(8,128)(2,1)S(1)}, bf16[4,128,128]{2,1,0:T(8,128)(2,1)S(1)}, u32[]{:S(2)}, u32[]{:S(2)}) collective-permute-start(bf16[4,128,128]{2,1,0:T(8,128)(2,1)S(1)} %get-tuple-element.71), channel_id=1, source_target_pairs={{0,2},{1,3},{2,0},{3,1},{4,6},{5,7},{6,4},{7,5},{8,10},{9,11},{10,... | collective-permute-start | bytes 393224 | tf_op jit(solution)/shard_map/ppermute | solution.py:454
  35.7 6.3 %collective-permute-start.9 = (bf16[4,128,128]{2,1,0:T(8,128)(2,1)S(1)}, bf16[4,128,128]{2,1,0:T(8,128)(2,1)S(1)}, u32[]{:S(2)}, u32[]{:S(2)}) collective-permute-start(bf16[4,128,128]{2,1,0:T(8,128)(2,1)S(1)} %get-tuple-element.69), channel_id=1, source_target_pairs={{0,6},{1,7},{2,4},{3,5},{4,2},{5,3},{6,0},{7,1},{8,14},{9,15},{10,... | collective-permute-start | bytes 393224 | tf_op jit(solution)/shard_map/ppermute | solution.py:454
  46.9 7.0 %collective-permute-start.12 = (bf16[4,128,128]{2,1,0:T(8,128)(2,1)S(1)}, bf16[4,128,128]{2,1,0:T(8,128)(2,1)S(1)}, u32[]{:S(2)}, u32[]{:S(2)}) collective-permute-start(bf16[4,128,128]{2,1,0:T(8,128)(2,1)S(1)} %get-tuple-element.73), channel_id=1, source_target_pairs={{0,6},{1,7},{2,4},{3,5},{4,2},{5,3},{6,0},{7,1},{8,14},{9,15},{10,... | collective-permute-start | bytes 393224 | tf_op jit(solution)/shard_map/ppermute | solution.py:454
  48.1 5.9 %collective-permute-start.13 = (bf16[4,128,128]{2,1,0:T(8,128)(2,1)S(1)}, bf16[4,128,128]{2,1,0:T(8,128)(2,1)S(1)}, u32[]{:S(2)}, u32[]{:S(2)}) collective-permute-start(bf16[4,128,128]{2,1,0:T(8,128)(2,1)S(1)} %get-tuple-element.74), channel_id=1, source_target_pairs={{0,4},{1,5},{2,6},{3,7},{4,0},{5,1},{6,2},{7,3},{8,12},{9,13},{10,... | collective-permute-start | bytes 393224 | tf_op jit(solution)/shard_map/ppermute | solution.py:454
  49.6 5.0 %collective-permute-start.14 = (bf16[4,128,128]{2,1,0:T(8,128)(2,1)S(1)}, bf16[4,128,128]{2,1,0:T(8,128)(2,1)S(1)}, u32[]{:S(2)}, u32[]{:S(2)}) collective-permute-start(bf16[4,128,128]{2,1,0:T(8,128)(2,1)S(1)} %get-tuple-element.75), channel_id=1, source_target_pairs={{0,2},{1,3},{2,0},{3,1},{4,6},{5,7},{6,4},{7,5},{8,10},{9,11},{10,... | collective-permute-start | bytes 393224 | tf_op jit(solution)/shard_map/ppermute | solution.py:454
  55.3 3.3 %collective-permute-start.15 = (bf16[128,2048]{1,0:T(8,128)(2,1)S(1)}, bf16[128,2048]{1,0:T(8,128)(2,1)S(1)}, u32[]{:S(2)}, u32[]{:S(2)}) collective-permute-start(bf16[128,2048]{1,0:T(8,128)(2,1)S(1)} %get-tuple-element.82), channel_id=1, source_target_pairs={{0,1},{1,0},{2,3},{3,2},{4,5},{5,4},{6,7},{7,6},{8,9},{9,8},{10,11... | collective-permute-start | bytes 1572872 | tf_op jit(solution)/shard_map/ppermute | solution.py:448
  55.4 3.3 %collective-permute-start.16 = (bf16[16,128,128]{2,1,0:T(8,128)(2,1)S(1)}, bf16[16,128,128]{2,1,0:T(8,128)(2,1)S(1)}, u32[]{:S(2)}, u32[]{:S(2)}) collective-permute-start(bf16[16,128,128]{2,1,0:T(8,128)(2,1)S(1)} %get-tuple-element.83), channel_id=1, source_target_pairs={{0,1},{1,0},{2,3},{3,2},{4,5},{5,4},{6,7},{7,6},{8,9},{9,8},{10,11... | collective-permute-start | bytes 1572872 | tf_op jit(solution)/shard_map/ppermute | solution.py:448
  55.9 7.6 %collective-permute-start.18 = (bf16[4,128,128]{2,1,0:T(8,128)(2,1)S(1)}, bf16[4,128,128]{2,1,0:T(8,128)(2,1)S(1)}, u32[]{:S(2)}, u32[]{:S(2)}) collective-permute-start(bf16[4,128,128]{2,1,0:T(8,128)(2,1)S(1)} %get-tuple-element.84.rest_0_), channel_id=1, source_target_pairs={{8,0},{16,8},{24,16},{9,1},{17,9},{25,17},{10,2},{18,10},{26,18},{... | collective-permute-start | bytes 393224 | tf_op jit(solution)/shard_map/ppermute | solution.py:474
  57.2 13.1 %collective-permute-start.19 = (bf16[4,128,128]{2,1,0:T(8,128)(2,1)S(1)}, bf16[4,128,128]{2,1,0:T(8,128)(2,1)S(1)}, u32[]{:S(2)}, u32[]{:S(2)}) collective-permute-start(bf16[4,128,128]{2,1,0:T(8,128)(2,1)S(1)} %get-tuple-element.84.rest_0_), channel_id=1, source_target_pairs={{16,0},{24,8},{17,1},{25,9},{18,2},{26,10},{19,3},{27,11},{20,4},{... | collective-permute-start | bytes 393224 | tf_op jit(solution)/shard_map/ppermute | solution.py:474
  62.2 20.5 %collective-permute-start.17 = (bf16[16,128,128]{2,1,0:T(8,128)(2,1)S(1)}, bf16[16,128,128]{2,1,0:T(8,128)(2,1)S(1)}, u32[]{:S(2)}, u32[]{:S(2)}) collective-permute-start(bf16[16,128,128]{2,1,0:T(8,128)(2,1)S(1)} %get-tuple-element.92), channel_id=1, source_target_pairs={{0,1},{1,0},{2,3},{3,2},{4,5},{5,4},{6,7},{7,6},{8,9},{9,8},{10,11... | collective-permute-start | bytes 1572872 | tf_op jit(solution)/shard_map/ppermute | solution.py:448
  62.3 20.5 %collective-permute-start.27 = (bf16[128,2048]{1,0:T(8,128)(2,1)S(1)}, bf16[128,2048]{1,0:T(8,128)(2,1)S(1)}, u32[]{:S(2)}, u32[]{:S(2)}) collective-permute-start(bf16[128,2048]{1,0:T(8,128)(2,1)S(1)} %get-tuple-element.97), channel_id=1, source_target_pairs={{0,1},{1,0},{2,3},{3,2},{4,5},{5,4},{6,7},{7,6},{8,9},{9,8},{10,11... | collective-permute-start | bytes 1572872 | tf_op jit(solution)/shard_map/ppermute | solution.py:448
  71.1 7.0 %collective-permute-start.20 = (bf16[4,128,128]{2,1,0:T(8,128)(2,1)S(1)}, bf16[4,128,128]{2,1,0:T(8,128)(2,1)S(1)}, u32[]{:S(2)}, u32[]{:S(2)}) collective-permute-start(bf16[4,128,128]{2,1,0:T(8,128)(2,1)S(1)} %get-tuple-element.93), channel_id=1, source_target_pairs={{0,6},{1,7},{2,4},{3,5},{4,2},{5,3},{6,0},{7,1},{8,14},{9,15},{10,... | collective-permute-start | bytes 393224 | tf_op jit(solution)/shard_map/ppermute | solution.py:454
  72.4 6.5 %collective-permute-start.22 = (bf16[4,128,128]{2,1,0:T(8,128)(2,1)S(1)}, bf16[4,128,128]{2,1,0:T(8,128)(2,1)S(1)}, u32[]{:S(2)}, u32[]{:S(2)}) collective-permute-start(bf16[4,128,128]{2,1,0:T(8,128)(2,1)S(1)} %get-tuple-element.94), channel_id=1, source_target_pairs={{0,4},{1,5},{2,6},{3,7},{4,0},{5,1},{6,2},{7,3},{8,12},{9,13},{10,... | collective-permute-start | bytes 393224 | tf_op jit(solution)/shard_map/ppermute | solution.py:454
  73.4 6.0 %collective-permute-start.24 = (bf16[4,128,128]{2,1,0:T(8,128)(2,1)S(1)}, bf16[4,128,128]{2,1,0:T(8,128)(2,1)S(1)}, u32[]{:S(2)}, u32[]{:S(2)}) collective-permute-start(bf16[4,128,128]{2,1,0:T(8,128)(2,1)S(1)} %get-tuple-element.95), channel_id=1, source_target_pairs={{0,2},{1,3},{2,0},{3,1},{4,6},{5,7},{6,4},{7,5},{8,10},{9,11},{10,... | collective-permute-start | bytes 393224 | tf_op jit(solution)/shard_map/ppermute | solution.py:454
  78.1 1.4 %collective-permute-start.26 = (bf16[4,128,128]{2,1,0:T(8,128)(2,1)S(1)}, bf16[4,128,128]{2,1,0:T(8,128)(2,1)S(1)}, u32[]{:S(2)}, u32[]{:S(2)}) collective-permute-start(bf16[4,128,128]{2,1,0:T(8,128)(2,1)S(1)} %get-tuple-element.96.rest_3_), channel_id=1, source_target_pairs={{0,1},{1,0},{2,3},{3,2},{4,5},{5,4},{6,7},{7,6},{8,9},{9,8},{10,11... | collective-permute-start | bytes 393224 | tf_op jit(solution)/shard_map/ppermute | solution.py:448
  78.9 3.9 %collective-permute-start.21 = (bf16[4,128,128]{2,1,0:T(8,128)(2,1)S(1)}, bf16[4,128,128]{2,1,0:T(8,128)(2,1)S(1)}, u32[]{:S(2)}, u32[]{:S(2)}) collective-permute-start(bf16[4,128,128]{2,1,0:T(8,128)(2,1)S(1)} %collective-permute-done.20.rest_0_), channel_id=1, source_target_pairs={{0,1},{1,0},{2,3},{3,2},{4,5},{5,4},{6,7},{7,6},{8,9},{9,8},{10,11... | collective-permute-start | bytes 393224 | tf_op jit(solution)/shard_map/ppermute | solution.py:448
  79.5 3.3 %collective-permute-start.23 = (bf16[4,128,128]{2,1,0:T(8,128)(2,1)S(1)}, bf16[4,128,128]{2,1,0:T(8,128)(2,1)S(1)}, u32[]{:S(2)}, u32[]{:S(2)}) collective-permute-start(bf16[4,128,128]{2,1,0:T(8,128)(2,1)S(1)} %collective-permute-done.22.rest_1_), channel_id=1, source_target_pairs={{0,1},{1,0},{2,3},{3,2},{4,5},{5,4},{6,7},{7,6},{8,9},{9,8},{10,11... | collective-permute-start | bytes 393224 | tf_op jit(solution)/shard_map/ppermute | solution.py:448
  79.5 3.3 %collective-permute-start.25 = (bf16[4,128,128]{2,1,0:T(8,128)(2,1)S(1)}, bf16[4,128,128]{2,1,0:T(8,128)(2,1)S(1)}, u32[]{:S(2)}, u32[]{:S(2)}) collective-permute-start(bf16[4,128,128]{2,1,0:T(8,128)(2,1)S(1)} %collective-permute-done.24.rest_2_), channel_id=1, source_target_pairs={{0,1},{1,0},{2,3},{3,2},{4,5},{5,4},{6,7},{7,6},{8,9},{9,8},{10,11... | collective-permute-start | bytes 393224 | tf_op jit(solution)/shard_map/ppermute | solution.py:448

commit v19 on v18

--- a/solution.py
+++ b/solution.py
@@ -179,7 +179,7 @@
             sent_in[pl.ds((chip ^ n) * owned, owned)] = state[...]
 
     weights = jnp.full((2 * DH, DH), 1.0 / DH, BF16)
-    for hs in bunches(heads, 4):
+    for hs in bunches(heads, 8):
         atts = [
             part[:, cols(h)] + mul(head_fq[:, cols(h)], came[step * heads + h], NN) for h in hs
         ]

time: 86 us -> 85.6 us (level)
  no operation moved by 1% of the time
where the time goes in v19:
time: 85.6 us; the launch traced here: 85.3 us
  Pallas kernels  30.8 us (36%)
  starting transfers between devices  28.6 us (33%)
  waiting for transfers between devices  24.9 us (29%)
  between operations  0.91 us (1%)
    pallas_call x13, Pallas kernels, run(): pl.pallas_call(kernel, grid_spec=pltpu.PrefetchScalarGridSpec(num_scalar_...  30.8 us
    ppermute x12, waiting for transfers between devices, exchange(): came[n] = lax.ppermute(states[n], LAYER, pairs)  17.4 us
    ppermute x12, starting transfers between devices, exchange(): came[n] = lax.ppermute(states[n], LAYER, pairs)  15.1 us
    ppermute x4, starting transfers between devices, reach_out(): others.insert(0, lax.ppermute(total, 'z', pairs))  10.7 us
    ppermute x4, waiting for transfers between devices, reach_out(): others.insert(0, lax.ppermute(total, 'z', pairs))  7.47 us
    ppermute x12, starting transfers between devices, swap(): return lax.ppermute(state, LAYER, [(i, i ^ 1) for i in range(members)])  2.8 us
  transfers between devices with their start and end apart: 28, of which 10 were waited for; matrix products, arithmetic and copies ran while one was open for 0% of the time, Pallas kernels for 22%

profile of v19, /device:TPU:0, one launch (start us, length us, event | category | flops | bytes accessed | tf_op | source)
XLA Modules:
  0.0 85.3 jit_solution(17521338102550496019)
XLA Ops:
  0.6 0.1 pad_add_fusion.place
  0.7 3.1 %tail_mate.1 = (bf16[16,128,128]{2,1,0:T(8,128)(2,1)S(1)}, bf16[3,128,2048]{2,1,0:T(8,128)(2,1)S(1)}, bf16[128,2048]{1,0:T(8,128)(2,1)S(1)}) custom-call(s32[8]{0:T(128)} %lens.25, s32[3]{0:T(128)S(1)} %pad_add_fusion.place, bf16[128,4096]{1,0:T(8,128)(2,1)} %k.13, bf16[128,4096]{1,0:T(8,128)(2,1)} %v.13, bf16[128,4096]{1,0:T(8,128)(2,1)} %q.5, ...), custom_call_target="tpu_custom_call" | custom-call | flops 67108864 | bytes 1572864 | tf_op jit(solution)/shard_map/tail_mate/pallas_call | solution.py:420
  3.8 0.0 copy-start.4
  3.8 0.5 collective-permute-start
  4.3 2.7 %tail_own.1.rest_5_ = bf16[16,128,128]{2,1,0:T(8,128)(2,1)S(1)} custom-call(s32[8]{0:T(128)} %lens.25, s32[3]{0:T(128)S(1)} %pad_add_fusion.place, bf16[128,4096]{1,0:T(8,128)(2,1)} %k.13, bf16[128,4096]{1,0:T(8,128)(2,1)} %v.13), custom_call_target="tpu_custom_call" | custom-call | flops 67108864 | bytes 1572864 | tf_op jit(solution)/shard_map/tail_own/pallas_call | solution.py:420
  7.1 0.0 copy-start
  7.1 0.0 copy-start.1
  7.1 0.0 copy-start.2
  7.1 0.8 carried_chip.1
  7.9 0.1 collective-permute-start.1
  8.0 3.9 %collective-permute-start.2 = (bf16[4,128,128]{2,1,0:T(8,128)(2,1)S(1)}, bf16[4,128,128]{2,1,0:T(8,128)(2,1)S(1)}, u32[]{:S(2)}, u32[]{:S(2)}) collective-permute-start(bf16[4,128,128]{2,1,0:T(8,128)(2,1)S(1)} %get-tuple-element.60), channel_id=1, source_target_pairs={{0,6},{1,7},{2,4},{3,5},{4,2},{5,3},{6,0},{7,1},{8,14},{9,15},{10,... | collective-permute-start | bytes 393224 | tf_op jit(solution)/shard_map/ppermute | solution.py:454
  11.9 0.5 collective-permute-start.3
  12.4 0.0 collective-permute-start.4
  12.5 3.7 %collective-permute-done.2.rest_0_ = bf16[4,128,128]{2,1,0:T(8,128)(2,1)S(1)} collective-permute-done((bf16[4,128,128]{2,1,0:T(8,128)(2,1)S(1)}, bf16[4,128,128]{2,1,0:T(8,128)(2,1)S(1)}, u32[]{:S(2)}, u32[]{:S(2)}) %collective-permute-start.2) | collective-permute-done | bytes 131104 | tf_op jit(solution)/shard_map/ppermute | solution.py:454
  16.2 2.5 %collective-permute-done.3.rest_1_ = bf16[4,128,128]{2,1,0:T(8,128)(2,1)S(1)} collective-permute-done((bf16[4,128,128]{2,1,0:T(8,128)(2,1)S(1)}, bf16[4,128,128]{2,1,0:T(8,128)(2,1)S(1)}, u32[]{:S(2)}, u32[]{:S(2)}) %collective-permute-start.3) | collective-permute-done | bytes 131104 | tf_op jit(solution)/shard_map/ppermute | solution.py:454
  18.7 0.0 collective-permute-done.4.rest_2_
  18.7 0.7 carried_total.1
  19.4 0.1 collective-permute-start.6
  19.5 0.5 collective-permute-start.5
  20.0 3.5 %collective-permute-start.7 = (bf16[4,128,128]{2,1,0:T(8,128)(2,1)S(1)}, bf16[4,128,128]{2,1,0:T(8,128)(2,1)S(1)}, u32[]{:S(2)}, u32[]{:S(2)}) collective-permute-start(bf16[4,128,128]{2,1,0:T(8,128)(2,1)S(1)} %get-tuple-element.68), channel_id=1, source_target_pairs={{0,8},{8,16},{16,24},{1,9},{9,17},{17,25},{2,10},{10,18},{18,26},{... | collective-permute-start | bytes 393224 | tf_op jit(solution)/shard_map/ppermute | solution.py:474
  23.5 4.5 %collective-permute-start.8 = (bf16[4,128,128]{2,1,0:T(8,128)(2,1)S(1)}, bf16[4,128,128]{2,1,0:T(8,128)(2,1)S(1)}, u32[]{:S(2)}, u32[]{:S(2)}) collective-permute-start(bf16[4,128,128]{2,1,0:T(8,128)(2,1)S(1)} %get-tuple-element.68), channel_id=1, source_target_pairs={{0,16},{8,24},{1,17},{9,25},{2,18},{10,26},{3,19},{11,27},{4,20},{... | collective-permute-start | bytes 393224 | tf_op jit(solution)/shard_map/ppermute | solution.py:474
  28.0 3.7 %within_chip.1 = (f32[256,2048]{1,0:T(8,128)S(1)}, bf16[256,2048]{1,0:T(8,128)(2,1)S(1)}, bf16[16,256,256]{2,1,0:T(8,128)(2,1)S(1)}) custom-call(s32[8]{0:T(128)S(1)} %copy-done.4, s32[3]{0:T(128)S(1)} %pad_add_fusion.place, bf16[128,4096]{1,0:T(8,128)(2,1)S(1)} %copy-done.2, bf16[128,4096]{1,0:T(8,128)(2,1)S(1)} %copy-done, ...), custom_call_target="tpu_custom_call" | custom-call | flops 671088640 | bytes 7340032 | tf_op jit(solution)/shard_map/within_chip/pallas_call | solution.py:420
  31.8 0.0 copy-start.3
  31.8 0.0 collective-permute-done.7.rest_6_
  31.8 0.0 collective-permute-done.6.rest_5_.earlier
  31.8 0.9 %carried_prefix.1 = (bf16[4,128,128]{2,1,0:T(8,128)(2,1)S(1)}, bf16[4,128,128]{2,1,0:T(8,128)(2,1)S(1)}, bf16[4,128,128]{2,1,0:T(8,128)(2,1)S(1)}, bf16[4,128,128]{2,1,0:T(8,128)(2,1)S(1)}) custom-call(s32[8]{0:T(128)S(1)} %copy-done.4, s32[3]{0:T(128)S(1)} %pad_add_fusion.place, bf16[4,128,128]{2,1,0:T(8,128)(2,1)S(1)} %collective-permute-done.2.rest_0_, ...), custom_call_target="tpu_custom_call" | custom-call | flops 1048576 | bytes 1048576 | tf_op jit(solution)/shard_map/carried_prefix/pallas_call | solution.py:420
  32.7 1.6 %collective-permute-start.10 = (bf16[4,128,128]{2,1,0:T(8,128)(2,1)S(1)}, bf16[4,128,128]{2,1,0:T(8,128)(2,1)S(1)}, u32[]{:S(2)}, u32[]{:S(2)}) collective-permute-start(bf16[4,128,128]{2,1,0:T(8,128)(2,1)S(1)} %get-tuple-element.70), channel_id=1, source_target_pairs={{0,4},{1,5},{2,6},{3,7},{4,0},{5,1},{6,2},{7,3},{8,12},{9,13},{10,... | collective-permute-start | bytes 393224 | tf_op jit(solution)/shard_map/ppermute | solution.py:454
  34.3 1.5 %collective-permute-start.11 = (bf16[4,128,128]{2,1,0:T(8,128)(2,1)S(1)}, bf16[4,128,128]{2,1,0:T(8,128)(2,1)S(1)}, u32[]{:S(2)}, u32[]{:S(2)}) collective-permute-start(bf16[4,128,128]{2,1,0:T(8,128)(2,1)S(1)} %get-tuple-element.71), channel_id=1, source_target_pairs={{0,2},{1,3},{2,0},{3,1},{4,6},{5,7},{6,4},{7,5},{8,10},{9,11},{10,... | collective-permute-start | bytes 393224 | tf_op jit(solution)/shard_map/ppermute | solution.py:454
  35.7 0.5 collective-permute-start.9
  36.3 1.9 %collective-permute-done.10.rest_1_ = bf16[4,128,128]{2,1,0:T(8,128)(2,1)S(1)} collective-permute-done((bf16[4,128,128]{2,1,0:T(8,128)(2,1)S(1)}, bf16[4,128,128]{2,1,0:T(8,128)(2,1)S(1)}, u32[]{:S(2)}, u32[]{:S(2)}) %collective-permute-start.10) | collective-permute-done | bytes 131104 | tf_op jit(solution)/shard_map/ppermute | solution.py:454
  38.2 3.8 %collective-permute-done.11.rest_2_ = bf16[4,128,128]{2,1,0:T(8,128)(2,1)S(1)} collective-permute-done((bf16[4,128,128]{2,1,0:T(8,128)(2,1)S(1)}, bf16[4,128,128]{2,1,0:T(8,128)(2,1)S(1)}, u32[]{:S(2)}, u32[]{:S(2)}) %collective-permute-start.11) | collective-permute-done | bytes 131104 | tf_op jit(solution)/shard_map/ppermute | solution.py:454
  42.0 4.5 %normed.1 = (bf16[128,4096]{1,0:T(8,128)(2,1)}, bf16[128,2048]{1,0:T(8,128)(2,1)S(1)}, bf16[128,2048]{1,0:T(8,128)(2,1)S(1)}, bf16[128,2048]{1,0:T(8,128)(2,1)S(...) custom-call(s32[8]{0:T(128)S(1)} %copy-done.4, ...), custom_call_target="tpu_custom_call" | custom-call | flops 536870912 | bytes 8388608 | tf_op jit(solution)/shard_map/normed/pallas_call | solution.py:420
  46.5 1.2 %collective-permute-start.12 = (bf16[4,128,128]{2,1,0:T(8,128)(2,1)S(1)}, bf16[4,128,128]{2,1,0:T(8,128)(2,1)S(1)}, u32[]{:S(2)}, u32[]{:S(2)}) collective-permute-start(bf16[4,128,128]{2,1,0:T(8,128)(2,1)S(1)} %get-tuple-element.73), channel_id=1, source_target_pairs={{0,6},{1,7},{2,4},{3,5},{4,2},{5,3},{6,0},{7,1},{8,14},{9,15},{10,... | collective-permute-start | bytes 393224 | tf_op jit(solution)/shard_map/ppermute | solution.py:454
  47.7 1.5 %collective-permute-start.13 = (bf16[4,128,128]{2,1,0:T(8,128)(2,1)S(1)}, bf16[4,128,128]{2,1,0:T(8,128)(2,1)S(1)}, u32[]{:S(2)}, u32[]{:S(2)}) collective-permute-start(bf16[4,128,128]{2,1,0:T(8,128)(2,1)S(1)} %get-tuple-element.74), channel_id=1, source_target_pairs={{0,4},{1,5},{2,6},{3,7},{4,0},{5,1},{6,2},{7,3},{8,12},{9,13},{10,... | collective-permute-start | bytes 393224 | tf_op jit(solution)/shard_map/ppermute | solution.py:454
  49.2 0.8 collective-permute-start.14
  50.0 3.5 %grads_within_0.1 = (bf16[128,4096]{1,0:T(8,128)(2,1)}, f32[128,4096]{1,0:T(8,128)S(1)}, f32[128,4096]{1,0:T(8,128)S(1)}) custom-call(s32[8]{0:T(128)S(1)} %copy-done.4, s32[3]{0:T(128)S(1)} %pad_add_fusion.place, bf16[128,4096]{1,0:T(8,128)(2,1)S(1)} %copy-done.2, bf16[128,4096]{1,0:T(8,128)(2,1)S(1)} %copy-done, bf16[128,4096]{1,0:T(8,128)(2,1)S(1)} %copy-done.1, ...), custom_call_target="tpu_custom_call" | custom-call | flops 469762048 | bytes 5767168 | tf_op jit(solution)/shard_map/grads_within_0/pallas_call | solution.py:420
  53.6 0.0 collective-permute-done.12.rest_0_
  53.6 0.0 collective-permute-done.13.rest_1_
  53.6 0.6 collective-permute-done.14.rest_2_
  54.1 0.7 future_total.1
  54.9 0.1 collective-permute-start.15
  55.0 0.5 collective-permute-start.16
  55.5 1.3 %collective-permute-start.18 = (bf16[4,128,128]{2,1,0:T(8,128)(2,1)S(1)}, bf16[4,128,128]{2,1,0:T(8,128)(2,1)S(1)}, u32[]{:S(2)}, u32[]{:S(2)}) collective-permute-start(bf16[4,128,128]{2,1,0:T(8,128)(2,1)S(1)} %get-tuple-element.84.rest_0_), channel_id=1, source_target_pairs={{8,0},{16,8},{24,16},{9,1},{17,9},{25,17},{10,2},{18,10},{26,18},{... | collective-permute-start | bytes 393224 | tf_op jit(solution)/shard_map/ppermute | solution.py:474
  56.7 1.5 %collective-permute-start.19 = (bf16[4,128,128]{2,1,0:T(8,128)(2,1)S(1)}, bf16[4,128,128]{2,1,0:T(8,128)(2,1)S(1)}, u32[]{:S(2)}, u32[]{:S(2)}) collective-permute-start(bf16[4,128,128]{2,1,0:T(8,128)(2,1)S(1)} %get-tuple-element.84.rest_0_), channel_id=1, source_target_pairs={{16,0},{24,8},{17,1},{25,9},{18,2},{26,10},{19,3},{27,11},{20,4},{... | collective-permute-start | bytes 393224 | tf_op jit(solution)/shard_map/ppermute | solution.py:474
  58.2 0.0 collective-permute-done.15.grad_att
  58.2 3.6 %grads_within_1.1 = (bf16[128,4096]{1,0:T(8,128)(2,1)}, f32[128,4096]{1,0:T(8,128)S(1)}, f32[128,4096]{1,0:T(8,128)S(1)}, bf16[128,2048]{1,0:T(8,128)(2,1)S(1)}, bf16[16,128,128]{2,1,0:T(8,128)(2,1)S(1)}) custom-call(s32[8]{0:T(128)S(1)} %copy-done.4, ...), custom_call_target="tpu_custom_call", output_to_operand_aliasing={{0}: (9, {}), {1}: (10, {}), {2}: (11, {}), {3}: (12, {}), ... | custom-call | flops 469762048 | bytes 5767168 | tf_op jit(solution)/shard_map/grads_within_1/pallas_call | solution.py:420
  61.8 0.1 collective-permute-start.17
  61.9 0.4 collective-permute-start.27
  62.3 0.7 collective-permute-done.18.rest_5_
  63.0 6.8 %collective-permute-done.19.rest_6_ = bf16[4,128,128]{2,1,0:T(8,128)(2,1)S(1)} collective-permute-done((bf16[4,128,128]{2,1,0:T(8,128)(2,1)S(1)}, bf16[4,128,128]{2,1,0:T(8,128)(2,1)S(1)}, u32[]{:S(2)}, u32[]{:S(2)}) %collective-permute-start.19) | collective-permute-done | bytes 131104 | tf_op jit(solution)/shard_map/ppermute | solution.py:474
  69.8 0.9 %future_prefix.1 = (bf16[4,128,128]{2,1,0:T(8,128)(2,1)S(1)}, bf16[4,128,128]{2,1,0:T(8,128)(2,1)S(1)}, bf16[4,128,128]{2,1,0:T(8,128)(2,1)S(1)}, bf16[4,128,128]{2,1,0:T(8,128)(2,1)S(1)}) custom-call(s32[8]{0:T(128)S(1)} %copy-done.4, s32[3]{0:T(128)S(1)} %pad_add_fusion.place, bf16[4,128,128]{2,1,0:T(8,128)(2,1)S(1)} %collective-permute-done.12.rest_0_, ...), custom_call_target="tpu_custom_call" | custom-call | flops 1048576 | bytes 1048576 | tf_op jit(solution)/shard_map/future_prefix/pallas_call | solution.py:420
  70.7 1.3 %collective-permute-start.20 = (bf16[4,128,128]{2,1,0:T(8,128)(2,1)S(1)}, bf16[4,128,128]{2,1,0:T(8,128)(2,1)S(1)}, u32[]{:S(2)}, u32[]{:S(2)}) collective-permute-start(bf16[4,128,128]{2,1,0:T(8,128)(2,1)S(1)} %get-tuple-element.93), channel_id=1, source_target_pairs={{0,6},{1,7},{2,4},{3,5},{4,2},{5,3},{6,0},{7,1},{8,14},{9,15},{10,... | collective-permute-start | bytes 393224 | tf_op jit(solution)/shard_map/ppermute | solution.py:454
  71.9 1.1 %collective-permute-start.22 = (bf16[4,128,128]{2,1,0:T(8,128)(2,1)S(1)}, bf16[4,128,128]{2,1,0:T(8,128)(2,1)S(1)}, u32[]{:S(2)}, u32[]{:S(2)}) collective-permute-start(bf16[4,128,128]{2,1,0:T(8,128)(2,1)S(1)} %get-tuple-element.94), channel_id=1, source_target_pairs={{0,4},{1,5},{2,6},{3,7},{4,0},{5,1},{6,2},{7,3},{8,12},{9,13},{10,... | collective-permute-start | bytes 393224 | tf_op jit(solution)/shard_map/ppermute | solution.py:454
  73.0 1.2 %collective-permute-start.24 = (bf16[4,128,128]{2,1,0:T(8,128)(2,1)S(1)}, bf16[4,128,128]{2,1,0:T(8,128)(2,1)S(1)}, u32[]{:S(2)}, u32[]{:S(2)}) collective-permute-start(bf16[4,128,128]{2,1,0:T(8,128)(2,1)S(1)} %get-tuple-element.95), channel_id=1, source_target_pairs={{0,2},{1,3},{2,0},{3,1},{4,6},{5,7},{6,4},{7,5},{8,10},{9,11},{10,... | collective-permute-start | bytes 393224 | tf_op jit(solution)/shard_map/ppermute | solution.py:454
  74.2 3.5 %collective-permute-done.20.rest_0_ = bf16[4,128,128]{2,1,0:T(8,128)(2,1)S(1)} collective-permute-done((bf16[4,128,128]{2,1,0:T(8,128)(2,1)S(1)}, bf16[4,128,128]{2,1,0:T(8,128)(2,1)S(1)}, u32[]{:S(2)}, u32[]{:S(2)}) %collective-permute-start.20) | collective-permute-done | bytes 131104 | tf_op jit(solution)/shard_map/ppermute | solution.py:454
  77.7 0.0 collective-permute-start.26
  77.7 0.7 collective-permute-done.22.rest_1_
  78.5 0.0 collective-permute-start.21
  78.5 0.6 collective-permute-done.24.rest_2_
  79.1 0.5 collective-permute-start.25
  79.6 2.8 %grads_last_0.1 = (bf16[128,4096]{1,0:T(8,128)(2,1)}, bf16[128,4096]{1,0:T(8,128)(2,1)}) custom-call(s32[8]{0:T(128)S(1)} %copy-done.4, s32[3]{0:T(128)S(1)} %pad_add_fusion.place, bf16[128,4096]{1,0:T(8,128)(2,1)S(1)} %copy-done, bf16[128,4096]{1,0:T(8,128)(2,1)S(1)} %copy-done.1, f32[128,4096]{1,0:T(8,128)S(1)} %get-tuple-element.90.rest_4_.gk_part, ...), custom_call_target="tpu_custom_call" | custom-call | flops 134217728 | bytes 4718592 | tf_op jit(solution)/shard_map/grads_last_0/pallas_call | solution.py:420
  82.3 0.0 collective-permute-done.21.rest_0_
  82.3 0.0 collective-permute-done.23.rest_1_
  82.4 3.0 %grads_last_1.1 = (bf16[128,4096]{1,0:T(8,128)(2,1)}, bf16[128,4096]{1,0:T(8,128)(2,1)}, bf16[128,4096]{1,0:T(8,128)(2,1)}) custom-call(s32[8]{0:T(128)S(1)} %copy-done.4, s32[3]{0:T(128)S(1)} %pad_add_fusion.place, bf16[128,4096]{1,0:T(8,128)(2,1)S(1)} %copy-done, ...), custom_call_target="tpu_custom_call", output_to_operand_aliasing={{0}: (12, {}), {1}: (13, {}), {2}: (14, {})} | custom-call | flops 134217728 | bytes 4718592 | tf_op jit(solution)/shard_map/grads_last_1/pallas_call | solution.py:420
  (16 shorter events, 0.0 us)
Async XLA Ops:
  3.8 3.3 %copy-start.4 = (s32[8]{0:T(128)S(1)}, s32[8]{0:T(128)}, u32[]{:S(2)}) copy-start(s32[8]{0:T(128)} %lens.25) | copy-start | bytes 100
  3.8 3.2 %collective-permute-start = (bf16[16,128,128]{2,1,0:T(8,128)(2,1)S(1)}, bf16[16,128,128]{2,1,0:T(8,128)(2,1)S(1)}, u32[]{:S(2)}, u32[]{:S(2)}) collective-permute-start(bf16[16,128,128]{2,1,0:T(8,128)(2,1)S(1)} %get-tuple-element.55), channel_id=1, source_target_pairs={{0,1},{1,0},{2,3},{3,2},{4,5},{5,4},{6,7},{7,6},{8,9},{9,8},{10,11... | collective-permute-start | bytes 1572872 | tf_op jit(solution)/shard_map/ppermute | solution.py:448
  7.1 20.9 %copy-start = (bf16[128,4096]{1,0:T(8,128)(2,1)S(1)}, bf16[128,4096]{1,0:T(8,128)(2,1)}, u32[]{:S(2)}) copy-start(bf16[128,4096]{1,0:T(8,128)(2,1)} %k.13) | copy-start | bytes 3145732
  7.1 20.9 %copy-start.1 = (bf16[128,4096]{1,0:T(8,128)(2,1)S(1)}, bf16[128,4096]{1,0:T(8,128)(2,1)}, u32[]{:S(2)}) copy-start(bf16[128,4096]{1,0:T(8,128)(2,1)} %v.13) | copy-start | bytes 3145732
  7.1 20.9 %copy-start.2 = (bf16[128,4096]{1,0:T(8,128)(2,1)S(1)}, bf16[128,4096]{1,0:T(8,128)(2,1)}, u32[]{:S(2)}) copy-start(bf16[128,4096]{1,0:T(8,128)(2,1)} %q.5) | copy-start | bytes 3145732
  7.9 20.1 %collective-permute-start.1 = (bf16[3,128,2048]{2,1,0:T(8,128)(2,1)S(1)}, bf16[3,128,2048]{2,1,0:T(8,128)(2,1)S(1)}, u32[]{:S(2)}, u32[]{:S(2)}) collective-permute-start(bf16[3,128,2048]{2,1,0:T(8,128)(2,1)S(1)} %get-tuple-element.57), channel_id=1, source_target_pairs={{0,1},{1,0},{2,3},{3,2},{4,5},{5,4},{6,7},{7,6},{8,9},{9,8},{10,11... | collective-permute-start | bytes 4718600 | tf_op jit(solution)/shard_map/ppermute | solution.py:448
  8.0 8.2 %collective-permute-start.2 = (bf16[4,128,128]{2,1,0:T(8,128)(2,1)S(1)}, bf16[4,128,128]{2,1,0:T(8,128)(2,1)S(1)}, u32[]{:S(2)}, u32[]{:S(2)}) collective-permute-start(bf16[4,128,128]{2,1,0:T(8,128)(2,1)S(1)} %get-tuple-element.60), channel_id=1, source_target_pairs={{0,6},{1,7},{2,4},{3,5},{4,2},{5,3},{6,0},{7,1},{8,14},{9,15},{10,... | collective-permute-start | bytes 393224 | tf_op jit(solution)/shard_map/ppermute | solution.py:454
  11.9 6.8 %collective-permute-start.3 = (bf16[4,128,128]{2,1,0:T(8,128)(2,1)S(1)}, bf16[4,128,128]{2,1,0:T(8,128)(2,1)S(1)}, u32[]{:S(2)}, u32[]{:S(2)}) collective-permute-start(bf16[4,128,128]{2,1,0:T(8,128)(2,1)S(1)} %get-tuple-element.61), channel_id=1, source_target_pairs={{0,4},{1,5},{2,6},{3,7},{4,0},{5,1},{6,2},{7,3},{8,12},{9,13},{10,... | collective-permute-start | bytes 393224 | tf_op jit(solution)/shard_map/ppermute | solution.py:454
  12.4 6.3 %collective-permute-start.4 = (bf16[4,128,128]{2,1,0:T(8,128)(2,1)S(1)}, bf16[4,128,128]{2,1,0:T(8,128)(2,1)S(1)}, u32[]{:S(2)}, u32[]{:S(2)}) collective-permute-start(bf16[4,128,128]{2,1,0:T(8,128)(2,1)S(1)} %get-tuple-element.62), channel_id=1, source_target_pairs={{0,2},{1,3},{2,0},{3,1},{4,6},{5,7},{6,4},{7,5},{8,10},{9,11},{10,... | collective-permute-start | bytes 393224 | tf_op jit(solution)/shard_map/ppermute | solution.py:454
  19.4 12.4 %collective-permute-start.6 = (bf16[16,128,128]{2,1,0:T(8,128)(2,1)S(1)}, bf16[16,128,128]{2,1,0:T(8,128)(2,1)S(1)}, u32[]{:S(2)}, u32[]{:S(2)}) collective-permute-start(bf16[16,128,128]{2,1,0:T(8,128)(2,1)S(1)} %get-tuple-element.67), channel_id=1, source_target_pairs={{0,1},{1,0},{2,3},{3,2},{4,5},{5,4},{6,7},{7,6},{8,9},{9,8},{10,11... | collective-permute-start | bytes 1572872 | tf_op jit(solution)/shard_map/ppermute | solution.py:448
  19.5 16.7 %collective-permute-start.5 = (bf16[128,2048]{1,0:T(8,128)(2,1)S(1)}, bf16[128,2048]{1,0:T(8,128)(2,1)S(1)}, u32[]{:S(2)}, u32[]{:S(2)}) collective-permute-start(bf16[128,2048]{1,0:T(8,128)(2,1)S(1)} %get-tuple-element.65), channel_id=1, source_target_pairs={{0,1},{1,0},{2,3},{3,2},{4,5},{5,4},{6,7},{7,6},{8,9},{9,8},{10,11... | collective-permute-start | bytes 1572872 | tf_op jit(solution)/shard_map/ppermute | solution.py:448
  20.0 11.8 %collective-permute-start.7 = (bf16[4,128,128]{2,1,0:T(8,128)(2,1)S(1)}, bf16[4,128,128]{2,1,0:T(8,128)(2,1)S(1)}, u32[]{:S(2)}, u32[]{:S(2)}) collective-permute-start(bf16[4,128,128]{2,1,0:T(8,128)(2,1)S(1)} %get-tuple-element.68), channel_id=1, source_target_pairs={{0,8},{8,16},{16,24},{1,9},{9,17},{17,25},{2,10},{10,18},{18,26},{... | collective-permute-start | bytes 393224 | tf_op jit(solution)/shard_map/ppermute | solution.py:474
  23.5 8.3 %collective-permute-start.8 = (bf16[4,128,128]{2,1,0:T(8,128)(2,1)S(1)}, bf16[4,128,128]{2,1,0:T(8,128)(2,1)S(1)}, u32[]{:S(2)}, u32[]{:S(2)}) collective-permute-start(bf16[4,128,128]{2,1,0:T(8,128)(2,1)S(1)} %get-tuple-element.68), channel_id=1, source_target_pairs={{0,16},{8,24},{1,17},{9,25},{2,18},{10,26},{3,19},{11,27},{4,20},{... | collective-permute-start | bytes 393224 | tf_op jit(solution)/shard_map/ppermute | solution.py:474
  31.8 10.2 %copy-start.3 = (bf16[128,4096]{1,0:T(8,128)(2,1)S(1)}, bf16[128,4096]{1,0:T(8,128)(2,1)}, u32[]{:S(2)}) copy-start(bf16[128,4096]{1,0:T(8,128)(2,1)} %g.1) | copy-start | bytes 3145732
  32.7 5.5 %collective-permute-start.10 = (bf16[4,128,128]{2,1,0:T(8,128)(2,1)S(1)}, bf16[4,128,128]{2,1,0:T(8,128)(2,1)S(1)}, u32[]{:S(2)}, u32[]{:S(2)}) collective-permute-start(bf16[4,128,128]{2,1,0:T(8,128)(2,1)S(1)} %get-tuple-element.70), channel_id=1, source_target_pairs={{0,4},{1,5},{2,6},{3,7},{4,0},{5,1},{6,2},{7,3},{8,12},{9,13},{10,... | collective-permute-start | bytes 393224 | tf_op jit(solution)/shard_map/ppermute | solution.py:454
  34.3 7.8 %collective-permute-start.11 = (bf16[4,128,128]{2,1,0:T(8,128)(2,1)S(1)}, bf16[4,128,128]{2,1,0:T(8,128)(2,1)S(1)}, u32[]{:S(2)}, u32[]{:S(2)}) collective-permute-start(bf16[4,128,128]{2,1,0:T(8,128)(2,1)S(1)} %get-tuple-element.71), channel_id=1, source_target_pairs={{0,2},{1,3},{2,0},{3,1},{4,6},{5,7},{6,4},{7,5},{8,10},{9,11},{10,... | collective-permute-start | bytes 393224 | tf_op jit(solution)/shard_map/ppermute | solution.py:454
  35.7 6.3 %collective-permute-start.9 = (bf16[4,128,128]{2,1,0:T(8,128)(2,1)S(1)}, bf16[4,128,128]{2,1,0:T(8,128)(2,1)S(1)}, u32[]{:S(2)}, u32[]{:S(2)}) collective-permute-start(bf16[4,128,128]{2,1,0:T(8,128)(2,1)S(1)} %get-tuple-element.69), channel_id=1, source_target_pairs={{0,6},{1,7},{2,4},{3,5},{4,2},{5,3},{6,0},{7,1},{8,14},{9,15},{10,... | collective-permute-start | bytes 393224 | tf_op jit(solution)/shard_map/ppermute | solution.py:454
  46.5 7.0 %collective-permute-start.12 = (bf16[4,128,128]{2,1,0:T(8,128)(2,1)S(1)}, bf16[4,128,128]{2,1,0:T(8,128)(2,1)S(1)}, u32[]{:S(2)}, u32[]{:S(2)}) collective-permute-start(bf16[4,128,128]{2,1,0:T(8,128)(2,1)S(1)} %get-tuple-element.73), channel_id=1, source_target_pairs={{0,6},{1,7},{2,4},{3,5},{4,2},{5,3},{6,0},{7,1},{8,14},{9,15},{10,... | collective-permute-start | bytes 393224 | tf_op jit(solution)/shard_map/ppermute | solution.py:454
  47.7 5.9 %collective-permute-start.13 = (bf16[4,128,128]{2,1,0:T(8,128)(2,1)S(1)}, bf16[4,128,128]{2,1,0:T(8,128)(2,1)S(1)}, u32[]{:S(2)}, u32[]{:S(2)}) collective-permute-start(bf16[4,128,128]{2,1,0:T(8,128)(2,1)S(1)} %get-tuple-element.74), channel_id=1, source_target_pairs={{0,4},{1,5},{2,6},{3,7},{4,0},{5,1},{6,2},{7,3},{8,12},{9,13},{10,... | collective-permute-start | bytes 393224 | tf_op jit(solution)/shard_map/ppermute | solution.py:454
  49.2 5.0 %collective-permute-start.14 = (bf16[4,128,128]{2,1,0:T(8,128)(2,1)S(1)}, bf16[4,128,128]{2,1,0:T(8,128)(2,1)S(1)}, u32[]{:S(2)}, u32[]{:S(2)}) collective-permute-start(bf16[4,128,128]{2,1,0:T(8,128)(2,1)S(1)} %get-tuple-element.75), channel_id=1, source_target_pairs={{0,2},{1,3},{2,0},{3,1},{4,6},{5,7},{6,4},{7,5},{8,10},{9,11},{10,... | collective-permute-start | bytes 393224 | tf_op jit(solution)/shard_map/ppermute | solution.py:454
  54.9 3.3 %collective-permute-start.15 = (bf16[128,2048]{1,0:T(8,128)(2,1)S(1)}, bf16[128,2048]{1,0:T(8,128)(2,1)S(1)}, u32[]{:S(2)}, u32[]{:S(2)}) collective-permute-start(bf16[128,2048]{1,0:T(8,128)(2,1)S(1)} %get-tuple-element.82), channel_id=1, source_target_pairs={{0,1},{1,0},{2,3},{3,2},{4,5},{5,4},{6,7},{7,6},{8,9},{9,8},{10,11... | collective-permute-start | bytes 1572872 | tf_op jit(solution)/shard_map/ppermute | solution.py:448
  55.0 3.3 %collective-permute-start.16 = (bf16[16,128,128]{2,1,0:T(8,128)(2,1)S(1)}, bf16[16,128,128]{2,1,0:T(8,128)(2,1)S(1)}, u32[]{:S(2)}, u32[]{:S(2)}) collective-permute-start(bf16[16,128,128]{2,1,0:T(8,128)(2,1)S(1)} %get-tuple-element.83), channel_id=1, source_target_pairs={{0,1},{1,0},{2,3},{3,2},{4,5},{5,4},{6,7},{7,6},{8,9},{9,8},{10,11... | collective-permute-start | bytes 1572872 | tf_op jit(solution)/shard_map/ppermute | solution.py:448
  55.5 7.6 %collective-permute-start.18 = (bf16[4,128,128]{2,1,0:T(8,128)(2,1)S(1)}, bf16[4,128,128]{2,1,0:T(8,128)(2,1)S(1)}, u32[]{:S(2)}, u32[]{:S(2)}) collective-permute-start(bf16[4,128,128]{2,1,0:T(8,128)(2,1)S(1)} %get-tuple-element.84.rest_0_), channel_id=1, source_target_pairs={{8,0},{16,8},{24,16},{9,1},{17,9},{25,17},{10,2},{18,10},{26,18},{... | collective-permute-start | bytes 393224 | tf_op jit(solution)/shard_map/ppermute | solution.py:474
  56.7 13.1 %collective-permute-start.19 = (bf16[4,128,128]{2,1,0:T(8,128)(2,1)S(1)}, bf16[4,128,128]{2,1,0:T(8,128)(2,1)S(1)}, u32[]{:S(2)}, u32[]{:S(2)}) collective-permute-start(bf16[4,128,128]{2,1,0:T(8,128)(2,1)S(1)} %get-tuple-element.84.rest_0_), channel_id=1, source_target_pairs={{16,0},{24,8},{17,1},{25,9},{18,2},{26,10},{19,3},{27,11},{20,4},{... | collective-permute-start | bytes 393224 | tf_op jit(solution)/shard_map/ppermute | solution.py:474
  61.8 20.5 %collective-permute-start.17 = (bf16[16,128,128]{2,1,0:T(8,128)(2,1)S(1)}, bf16[16,128,128]{2,1,0:T(8,128)(2,1)S(1)}, u32[]{:S(2)}, u32[]{:S(2)}) collective-permute-start(bf16[16,128,128]{2,1,0:T(8,128)(2,1)S(1)} %get-tuple-element.92), channel_id=1, source_target_pairs={{0,1},{1,0},{2,3},{3,2},{4,5},{5,4},{6,7},{7,6},{8,9},{9,8},{10,11... | collective-permute-start | bytes 1572872 | tf_op jit(solution)/shard_map/ppermute | solution.py:448
  61.9 20.5 %collective-permute-start.27 = (bf16[128,2048]{1,0:T(8,128)(2,1)S(1)}, bf16[128,2048]{1,0:T(8,128)(2,1)S(1)}, u32[]{:S(2)}, u32[]{:S(2)}) collective-permute-start(bf16[128,2048]{1,0:T(8,128)(2,1)S(1)} %get-tuple-element.97), channel_id=1, source_target_pairs={{0,1},{1,0},{2,3},{3,2},{4,5},{5,4},{6,7},{7,6},{8,9},{9,8},{10,11... | collective-permute-start | bytes 1572872 | tf_op jit(solution)/shard_map/ppermute | solution.py:448
  70.7 7.0 %collective-permute-start.20 = (bf16[4,128,128]{2,1,0:T(8,128)(2,1)S(1)}, bf16[4,128,128]{2,1,0:T(8,128)(2,1)S(1)}, u32[]{:S(2)}, u32[]{:S(2)}) collective-permute-start(bf16[4,128,128]{2,1,0:T(8,128)(2,1)S(1)} %get-tuple-element.93), channel_id=1, source_target_pairs={{0,6},{1,7},{2,4},{3,5},{4,2},{5,3},{6,0},{7,1},{8,14},{9,15},{10,... | collective-permute-start | bytes 393224 | tf_op jit(solution)/shard_map/ppermute | solution.py:454
  71.9 6.5 %collective-permute-start.22 = (bf16[4,128,128]{2,1,0:T(8,128)(2,1)S(1)}, bf16[4,128,128]{2,1,0:T(8,128)(2,1)S(1)}, u32[]{:S(2)}, u32[]{:S(2)}) collective-permute-start(bf16[4,128,128]{2,1,0:T(8,128)(2,1)S(1)} %get-tuple-element.94), channel_id=1, source_target_pairs={{0,4},{1,5},{2,6},{3,7},{4,0},{5,1},{6,2},{7,3},{8,12},{9,13},{10,... | collective-permute-start | bytes 393224 | tf_op jit(solution)/shard_map/ppermute | solution.py:454
  73.0 6.0 %collective-permute-start.24 = (bf16[4,128,128]{2,1,0:T(8,128)(2,1)S(1)}, bf16[4,128,128]{2,1,0:T(8,128)(2,1)S(1)}, u32[]{:S(2)}, u32[]{:S(2)}) collective-permute-start(bf16[4,128,128]{2,1,0:T(8,128)(2,1)S(1)} %get-tuple-element.95), channel_id=1, source_target_pairs={{0,2},{1,3},{2,0},{3,1},{4,6},{5,7},{6,4},{7,5},{8,10},{9,11},{10,... | collective-permute-start | bytes 393224 | tf_op jit(solution)/shard_map/ppermute | solution.py:454
  77.7 1.4 %collective-permute-start.26 = (bf16[4,128,128]{2,1,0:T(8,128)(2,1)S(1)}, bf16[4,128,128]{2,1,0:T(8,128)(2,1)S(1)}, u32[]{:S(2)}, u32[]{:S(2)}) collective-permute-start(bf16[4,128,128]{2,1,0:T(8,128)(2,1)S(1)} %get-tuple-element.96.rest_3_), channel_id=1, source_target_pairs={{0,1},{1,0},{2,3},{3,2},{4,5},{5,4},{6,7},{7,6},{8,9},{9,8},{10,11... | collective-permute-start | bytes 393224 | tf_op jit(solution)/shard_map/ppermute | solution.py:448
  78.5 3.9 %collective-permute-start.21 = (bf16[4,128,128]{2,1,0:T(8,128)(2,1)S(1)}, bf16[4,128,128]{2,1,0:T(8,128)(2,1)S(1)}, u32[]{:S(2)}, u32[]{:S(2)}) collective-permute-start(bf16[4,128,128]{2,1,0:T(8,128)(2,1)S(1)} %collective-permute-done.20.rest_0_), channel_id=1, source_target_pairs={{0,1},{1,0},{2,3},{3,2},{4,5},{5,4},{6,7},{7,6},{8,9},{9,8},{10,11... | collective-permute-start | bytes 393224 | tf_op jit(solution)/shard_map/ppermute | solution.py:448
  79.1 3.3 %collective-permute-start.23 = (bf16[4,128,128]{2,1,0:T(8,128)(2,1)S(1)}, bf16[4,128,128]{2,1,0:T(8,128)(2,1)S(1)}, u32[]{:S(2)}, u32[]{:S(2)}) collective-permute-start(bf16[4,128,128]{2,1,0:T(8,128)(2,1)S(1)} %collective-permute-done.22.rest_1_), channel_id=1, source_target_pairs={{0,1},{1,0},{2,3},{3,2},{4,5},{5,4},{6,7},{7,6},{8,9},{9,8},{10,11... | collective-permute-start | bytes 393224 | tf_op jit(solution)/shard_map/ppermute | solution.py:448
  79.1 3.3 %collective-permute-start.25 = (bf16[4,128,128]{2,1,0:T(8,128)(2,1)S(1)}, bf16[4,128,128]{2,1,0:T(8,128)(2,1)S(1)}, u32[]{:S(2)}, u32[]{:S(2)}) collective-permute-start(bf16[4,128,128]{2,1,0:T(8,128)(2,1)S(1)} %collective-permute-done.24.rest_2_), channel_id=1, source_target_pairs={{0,1},{1,0},{2,3},{3,2},{4,5},{5,4},{6,7},{7,6},{8,9},{9,8},{10,11... | collective-permute-start | bytes 393224 | tf_op jit(solution)/shard_map/ppermute | solution.py:448
